TPU v7x, 32 devices: a whole 2x2x4 slice. The times are simulated.
32 devices in a mesh: img: 16 (over z, x, core), row: 2 (over y).
Axes of the slice: x: 2, y: 2, z: 4, core: 2. Of those that a mesh axis runs over, the one named last changes fastest.
Arguments:
- hidden: bfloat16 [16, 256, 2048], P('img', 'row'), may hold values from -6 to 6
- mask_index: int32 [16, 256], P('img'), may hold values from 0 to 255, as said below
- mask_count: int32 [16], P('img'), may hold values from 1 to 256, as said below
- mask_embed: float32 [2048], replicated, may hold values from -6 to 6
- norm_gains: float32 [3, 2048], replicated, may hold values from 0.1 to 1.9
- caption: bfloat16 [128, 4096], replicated, may hold values from -6 to 6
- w_qkv: bfloat16 [2048, 3, 2048], P(('img', 'row')), may hold values from -0.125 to 0.125
- w_out: bfloat16 [2048, 2048], P(('img', 'row')), may hold values from -0.5 to 0.5
- w_cross: bfloat16 [2048, 3, 2048], P(('img', 'row')), may hold values from -0.125 to 0.125
- w_cross_out: bfloat16 [2048, 2048], P(('img', 'row')), may hold values from -0.5 to 0.5
- w_text: bfloat16 [2048, 4096], P(('img', 'row')), may hold values from -0.09375 to 0.09375
- w_up: bfloat16 [2048, 8192], P(('img', 'row')), may hold values from -0.125 to 0.125
- w_down: bfloat16 [2048, 8192], P(('img', 'row')), may hold values from -0.09375 to 0.09375
- cotangent: bfloat16 [16, 256, 2048], P('img', 'row'), may hold values from -6 to 6
Outputs:
- output: bfloat16 [16, 256, 2048], P('img', 'row')
- grad_hidden: bfloat16 [16, 256, 2048], P('img', 'row')
- grad_caption: float32 [128, 4096], replicated
- grad_gains: float32 [3, 2048], replicated
- grad_mask: float32 [2048], replicated
- grad_qkv: float32 [2048, 3, 2048], P(('img', 'row'))
- grad_out: float32 [2048, 2048], P(('img', 'row'))
- grad_cross: float32 [2048, 3, 2048], P(('img', 'row'))
- grad_cross_out: float32 [2048, 2048], P(('img', 'row'))
- grad_text_w: float32 [2048, 4096], P(('img', 'row'))
- grad_up: float32 [2048, 8192], P(('img', 'row'))
- grad_down: float32 [2048, 8192], P(('img', 'row'))
Inputs may be any that keep to these rules, and one draw needn't show every extreme that they name: `mask_index`: each row lists every position 0 to 255 of its image once; the first mask_count entries are the masked positions. `mask_count`: masked tokens of each image, after a cosine plan; some image has all 256 masked and some image has one.
All inputs are finite; a program needn't handle non-finite values.
Results may differ from a plain program's by a relative error of at most 0.02.
Values may be sent and summed in bfloat16 or wider, within the bound.
No kernel may reach another device: no remote copies, remote signals or barrier semaphores. Data moves between devices by JAX's collectives and lax.ppermute only.
A program may use at most 832 MiB of HBM per device.

v0:
```python
import math

import jax
import jax.numpy as jnp
from jax import lax
from jax.sharding import PartitionSpec as P

H = 16
HD = 128


EPS = 1e-05


def normalize(values):
    centred = values - jnp.mean(values, axis=-1, keepdims=True)
    inv_std = lax.rsqrt(jnp.mean(centred * centred, axis=-1, keepdims=True) + EPS)
    return (centred * inv_std, inv_std)


def norm_back(grad_normed, normed, inv_std, gain):
    scaled = grad_normed * gain
    first_mean = jnp.mean(scaled, axis=-1, keepdims=True)
    second_mean = jnp.mean(scaled * normed, axis=-1, keepdims=True)
    return (
        inv_std * (scaled - first_mean - normed * second_mean),
        jnp.sum(grad_normed * normed, axis=(0, 1)),
    )


def split_heads(values):
    return values.reshape(values.shape[:-1] + (H, HD))


def merge_heads(values):
    return values.reshape(values.shape[:-2] + (H * HD,))


def attend_forward(queries, key_rows, value_rows, score_form, mix_form, score_scale):
    scores = (
        jnp.einsum(
            score_form,
            split_heads(queries),
            split_heads(key_rows),
            preferred_element_type=jnp.float32,
        )
        * score_scale
    )
    row_peak = jnp.max(scores, axis=-1, keepdims=True)
    exp_terms = jnp.exp(scores - row_peak)
    row_total = jnp.sum(exp_terms, axis=-1, keepdims=True)
    weights = (exp_terms / row_total).astype(jnp.bfloat16)
    mixed_heads = jnp.einsum(
        mix_form, weights, split_heads(value_rows), preferred_element_type=jnp.float32
    )
    return (row_peak + jnp.log(row_total), merge_heads(mixed_heads).astype(jnp.bfloat16))


def attend_back(
    queries,
    key_rows,
    value_rows,
    log_total,
    grad_mixed,
    score_form,
    mix_form,
    key_form,
    score_scale,
):
    heads_query = split_heads(queries)
    heads_key = split_heads(key_rows)
    heads_grad = split_heads(grad_mixed)
    scores = (
        jnp.einsum(score_form, heads_query, heads_key, preferred_element_type=jnp.float32)
        * score_scale
    )
    probs = jnp.exp(scores - log_total)
    grad_probs = jnp.einsum(
        score_form, heads_grad, split_heads(value_rows), preferred_element_type=jnp.float32
    )
    grad_scores = (
        probs * (grad_probs - jnp.sum(probs * grad_probs, axis=-1, keepdims=True))
    ).astype(jnp.bfloat16)
    grad_queries = (
        jnp.einsum(mix_form, grad_scores, heads_key, preferred_element_type=jnp.float32)
        * score_scale
    )
    grad_keys = (
        jnp.einsum(key_form, grad_scores, heads_query, preferred_element_type=jnp.float32)
        * score_scale
    )
    grad_values = jnp.einsum(
        key_form, probs.astype(jnp.bfloat16), heads_grad, preferred_element_type=jnp.float32
    )
    return (merge_heads(grad_queries), merge_heads(grad_keys), merge_heads(grad_values))


def own_columns(flat, row_index, group_count, shard_rows):
    shaped = flat.reshape(flat.shape[0], group_count, -1, shard_rows)
    picked = lax.dynamic_slice_in_dim(shaped, row_index, 1, 2)
    return picked.reshape(flat.shape[0], group_count * shard_rows)


def local(
    hidden,
    mask_index,
    mask_count,
    mask_embed,
    norm_gains,
    caption,
    w_qkv,
    w_out,
    w_cross,
    w_cross_out,
    w_text,
    w_up,
    w_down,
    cotangent,
):
    local_rows = hidden.shape[1]
    model_width = hidden.shape[2]
    full_length = mask_index.shape[1]
    score_scale = 1.0 / math.sqrt(HD)
    shard_rows = w_qkv.shape[0]
    row_index = lax.axis_index("row")
    first_row = (lax.axis_index("img") * lax.axis_size("row") + row_index) * shard_rows
    positions = row_index * local_rows + jnp.arange(local_rows, dtype=jnp.int32)
    ranks = jnp.arange(full_length, dtype=jnp.int32)
    matches = (mask_index[:, :, None] == positions[None, None, :]) & (
        ranks[None, :, None] < mask_count[:, None, None]
    )
    masked = jnp.any(matches, axis=1)[:, :, None]
    start_x = jnp.where(masked, mask_embed, hidden.astype(jnp.float32))
    qkv_full, out_full = (
        lax.all_gather(w_qkv, ("img", "row"), axis=0, tiled=True),
        lax.all_gather(w_out, ("img", "row"), axis=0, tiled=True),
    )
    normed_a, inv_a = normalize(start_x)
    attn_in = (normed_a * norm_gains[0]).astype(jnp.bfloat16)
    projected = jnp.einsum(
        "bsd,dje->bsje", attn_in, qkv_full, preferred_element_type=jnp.float32
    ).astype(jnp.bfloat16)
    queries = projected[:, :, 0]
    keys_all, values_all = (
        lax.all_gather(projected[:, :, 1], "row", axis=1, tiled=True),
        lax.all_gather(projected[:, :, 2], "row", axis=1, tiled=True),
    )
    self_lse, self_mixed = attend_forward(
        queries, keys_all, values_all, "bqhe,bkhe->bhqk", "bhqk,bkhe->bqhe", score_scale
    )
    after_attn = start_x + jnp.einsum(
        "bsd,ed->bse", self_mixed, out_full, preferred_element_type=jnp.float32
    )
    cross_full, cross_out_full, text_full = (
        lax.all_gather(w_cross, ("img", "row"), axis=0, tiled=True),
        lax.all_gather(w_cross_out, ("img", "row"), axis=0, tiled=True),
        lax.all_gather(w_text, ("img", "row"), axis=0, tiled=True),
    )
    text_hidden = jnp.einsum(
        "cf,df->cd", caption, text_full, preferred_element_type=jnp.float32
    ).astype(jnp.bfloat16)
    text_kv = jnp.einsum(
        "cd,dje->cje", text_hidden, cross_full[:, 1:], preferred_element_type=jnp.float32
    ).astype(jnp.bfloat16)
    text_keys = text_kv[:, 0]
    text_values = text_kv[:, 1]
    normed_b, inv_b = normalize(after_attn)
    cross_in = (normed_b * norm_gains[1]).astype(jnp.bfloat16)
    cross_queries = jnp.einsum(
        "bsd,de->bse", cross_in, cross_full[:, 0], preferred_element_type=jnp.float32
    ).astype(jnp.bfloat16)
    cross_lse, cross_mixed = attend_forward(
        cross_queries, text_keys, text_values, "bqhe,khe->bhqk", "bhqk,khe->bqhe", score_scale
    )
    after_cross = after_attn + jnp.einsum(
        "bsd,ed->bse", cross_mixed, cross_out_full, preferred_element_type=jnp.float32
    )
    up_full, down_full = (
        lax.all_gather(w_up, ("img", "row"), axis=0, tiled=True),
        lax.all_gather(w_down, ("img", "row"), axis=0, tiled=True),
    )
    normed_c, inv_c = normalize(after_cross)
    mlp_in = (normed_c * norm_gains[2]).astype(jnp.bfloat16)
    pre_act = jnp.einsum("bsd,df->bsf", mlp_in, up_full, preferred_element_type=jnp.float32)
    activated = jax.nn.gelu(pre_act).astype(jnp.bfloat16)
    result = after_cross + jnp.einsum(
        "bsf,df->bsd", activated, down_full, preferred_element_type=jnp.float32
    )
    output = result.astype(jnp.bfloat16)
    grad_top = cotangent.astype(jnp.float32) * masked.astype(jnp.float32)
    grad_y = grad_top.astype(jnp.bfloat16)
    up_back, down_back = (
        lax.all_gather(w_up, ("img", "row"), axis=0, tiled=True),
        lax.all_gather(w_down, ("img", "row"), axis=0, tiled=True),
    )
    grad_act = jnp.einsum("bsd,df->bsf", grad_y, down_back, preferred_element_type=jnp.float32)
    gelu_pull = jax.vjp(jax.nn.gelu, pre_act)[1]
    grad_pre = gelu_pull(grad_act)[0].astype(jnp.bfloat16)
    grad_mlp_in = jnp.einsum("bsf,df->bsd", grad_pre, up_back, preferred_element_type=jnp.float32)
    back_c, gain_grad_c = norm_back(grad_mlp_in, normed_c, inv_c, norm_gains[2])
    grad_after_cross = grad_top + back_c
    flat_mlp_in = mlp_in.reshape(-1, model_width)
    flat_grad_y = grad_y.reshape(-1, model_width)
    flat_grad_pre = grad_pre.reshape(-1, grad_pre.shape[-1])
    flat_act = activated.reshape(-1, activated.shape[-1])
    cross_back, cross_out_back, text_back = (
        lax.all_gather(w_cross, ("img", "row"), axis=0, tiled=True),
        lax.all_gather(w_cross_out, ("img", "row"), axis=0, tiled=True),
        lax.all_gather(w_text, ("img", "row"), axis=0, tiled=True),
    )
    grad_cross_branch = grad_after_cross.astype(jnp.bfloat16)
    grad_cross_mixed = jnp.einsum(
        "bse,ed->bsd", grad_cross_branch, cross_out_back, preferred_element_type=jnp.float32
    ).astype(jnp.bfloat16)
    grad_cq, grad_text_keys, grad_text_values = attend_back(
        cross_queries,
        text_keys,
        text_values,
        cross_lse,
        grad_cross_mixed,
        "bqhe,khe->bhqk",
        "bhqk,khe->bqhe",
        "bhqk,bqhe->khe",
        score_scale,
    )
    grad_cq = grad_cq.astype(jnp.bfloat16)
    grad_cross_in = jnp.einsum(
        "bse,de->bsd", grad_cq, cross_back[:, 0], preferred_element_type=jnp.float32
    )
    back_b, gain_grad_b = norm_back(grad_cross_in, normed_b, inv_b, norm_gains[1])
    grad_after_attn = grad_after_cross + back_b
    flat_cross_in = cross_in.reshape(-1, model_width)
    flat_grad_cq = grad_cq.reshape(-1, model_width)
    flat_cross_branch = grad_cross_branch.reshape(-1, model_width)
    flat_cross_mixed = cross_mixed.reshape(-1, model_width)
    qkv_back, out_back = (
        lax.all_gather(w_qkv, ("img", "row"), axis=0, tiled=True),
        lax.all_gather(w_out, ("img", "row"), axis=0, tiled=True),
    )
    grad_attn_branch = grad_after_attn.astype(jnp.bfloat16)
    grad_self_mixed = jnp.einsum(
        "bse,ed->bsd", grad_attn_branch, out_back, preferred_element_type=jnp.float32
    ).astype(jnp.bfloat16)
    grad_queries, grad_keys_all, grad_values_all = attend_back(
        queries,
        keys_all,
        values_all,
        self_lse,
        grad_self_mixed,
        "bqhe,bkhe->bhqk",
        "bhqk,bkhe->bqhe",
        "bhqk,bqhe->bkhe",
        score_scale,
    )
    grad_keys, grad_values = (
        lax.psum_scatter(
            grad_keys_all.astype(jnp.bfloat16), "row", scatter_dimension=1, tiled=True
        ).astype(jnp.float32),
        lax.psum_scatter(
            grad_values_all.astype(jnp.bfloat16), "row", scatter_dimension=1, tiled=True
        ).astype(jnp.float32),
    )
    grad_projected = jnp.stack([grad_queries, grad_keys, grad_values], axis=2).astype(jnp.bfloat16)
    grad_attn_in = jnp.einsum(
        "bsje,dje->bsd", grad_projected, qkv_back, preferred_element_type=jnp.float32
    )
    back_a, gain_grad_a = norm_back(grad_attn_in, normed_a, inv_a, norm_gains[0])
    grad_start = grad_after_attn + back_a
    flat_attn_in = attn_in.reshape(-1, model_width)
    flat_grad_proj = grad_projected.reshape(-1, 3 * model_width)
    flat_attn_branch = grad_attn_branch.reshape(-1, model_width)
    flat_self_mixed = self_mixed.reshape(-1, model_width)
    (
        pair_mlp_in,
        pair_grad_y,
        pair_grad_pre,
        pair_act,
        pair_cross_in,
        pair_grad_cq,
        pair_cross_branch,
        pair_cross_mixed,
        pair_attn_in,
        pair_grad_proj,
        pair_attn_branch,
        pair_self_mixed,
    ) = (
        lax.all_gather(flat_mlp_in, "row", axis=0, tiled=True),
        lax.all_gather(flat_grad_y, "row", axis=0, tiled=True),
        lax.all_gather(flat_grad_pre, "row", axis=0, tiled=True),
        lax.all_gather(flat_act, "row", axis=0, tiled=True),
        lax.all_gather(flat_cross_in, "row", axis=0, tiled=True),
        lax.all_gather(flat_grad_cq, "row", axis=0, tiled=True),
        lax.all_gather(flat_cross_branch, "row", axis=0, tiled=True),
        lax.all_gather(flat_cross_mixed, "row", axis=0, tiled=True),
        lax.all_gather(flat_attn_in, "row", axis=0, tiled=True),
        lax.all_gather(flat_grad_proj, "row", axis=0, tiled=True),
        lax.all_gather(flat_attn_branch, "row", axis=0, tiled=True),
        lax.all_gather(flat_self_mixed, "row", axis=0, tiled=True),
    )
    group_count = lax.axis_size("img")
    own_mlp_in = own_columns(pair_mlp_in, row_index, group_count, shard_rows)
    own_grad_y = own_columns(pair_grad_y, row_index, group_count, shard_rows)
    own_cross_in = own_columns(pair_cross_in, row_index, group_count, shard_rows)
    own_cross_branch = own_columns(pair_cross_branch, row_index, group_count, shard_rows)
    own_attn_in = own_columns(pair_attn_in, row_index, group_count, shard_rows)
    own_attn_branch = own_columns(pair_attn_branch, row_index, group_count, shard_rows)
    up_part = jnp.einsum("nd,nf->df", own_mlp_in, pair_grad_pre, preferred_element_type=jnp.float32)
    down_part = jnp.einsum("nd,nf->df", own_grad_y, pair_act, preferred_element_type=jnp.float32)
    query_part = jnp.einsum(
        "nd,ne->de", own_cross_in, pair_grad_cq, preferred_element_type=jnp.float32
    )
    cross_out_part = jnp.einsum(
        "nd,ne->de", own_cross_branch, pair_cross_mixed, preferred_element_type=jnp.float32
    )
    proj_part = jnp.einsum(
        "nd,ne->de", own_attn_in, pair_grad_proj, preferred_element_type=jnp.float32
    )
    out_part = jnp.einsum(
        "nd,ne->de", own_attn_branch, pair_self_mixed, preferred_element_type=jnp.float32
    )
    joint = lax.psum_scatter(
        jnp.concatenate(
            [up_part, down_part, query_part, cross_out_part, proj_part, out_part], axis=1
        ),
        "img",
        scatter_dimension=0,
        tiled=True,
    )
    hidden_units = flat_grad_pre.shape[-1]
    grad_up_rows = joint[:, :hidden_units]
    grad_down_rows = joint[:, hidden_units : 2 * hidden_units]
    offset = 2 * hidden_units
    grad_cq_rows = joint[:, offset : offset + model_width]
    grad_cross_out_rows = joint[:, offset + model_width : offset + 2 * model_width]
    grad_qkv_rows = joint[:, offset + 2 * model_width : offset + 5 * model_width].reshape(
        shard_rows, 3, model_width
    )
    grad_out_rows = joint[:, offset + 5 * model_width : offset + 6 * model_width]
    grad_hidden = jnp.where(masked, 0.0, grad_start).astype(jnp.bfloat16)
    mask_part = jnp.sum(jnp.where(masked, grad_start, 0.0), axis=(0, 1))
    gain_part = jnp.stack([gain_grad_a, gain_grad_b, gain_grad_c])
    grad_gains, grad_mask, key_sum, value_sum = lax.psum(
        (gain_part, mask_part, grad_text_keys, grad_text_values), ("img", "row")
    )
    key_grad = key_sum.astype(jnp.bfloat16)
    value_grad = value_sum.astype(jnp.bfloat16)
    hidden_cols = lax.dynamic_slice_in_dim(text_hidden, first_row, shard_rows, 1)
    key_weight_grad = jnp.einsum(
        "cd,ce->de", hidden_cols, key_grad, preferred_element_type=jnp.float32
    )
    value_weight_grad = jnp.einsum(
        "cd,ce->de", hidden_cols, value_grad, preferred_element_type=jnp.float32
    )
    grad_text_hidden = jnp.einsum(
        "ce,de->cd", key_grad, cross_back[:, 1], preferred_element_type=jnp.float32
    )
    grad_text_hidden = grad_text_hidden + jnp.einsum(
        "ce,de->cd", value_grad, cross_back[:, 2], preferred_element_type=jnp.float32
    )
    grad_text_hidden = grad_text_hidden.astype(jnp.bfloat16)
    grad_caption = jnp.einsum(
        "cd,df->cf", grad_text_hidden, text_back, preferred_element_type=jnp.float32
    )
    text_grad_cols = lax.dynamic_slice_in_dim(grad_text_hidden, first_row, shard_rows, 1)
    grad_text_w = jnp.einsum(
        "cd,cf->df", text_grad_cols, caption, preferred_element_type=jnp.float32
    )
    grad_cross = jnp.stack([grad_cq_rows, key_weight_grad, value_weight_grad], axis=1)
    return (
        output,
        grad_hidden,
        grad_caption,
        grad_gains,
        grad_mask,
        grad_qkv_rows,
        grad_out_rows,
        grad_cross,
        grad_cross_out_rows,
        grad_text_w,
        grad_up_rows,
        grad_down_rows,
    )


def solution(mesh):
    in_specs = (
        P("img", "row", None),
        P("img", None),
        P("img"),
        P(),
        P(),
        P(),
        P(("img", "row"), None, None),
        P(("img", "row"), None),
        P(("img", "row"), None, None),
        P(("img", "row"), None),
        P(("img", "row"), None),
        P(("img", "row"), None),
        P(("img", "row"), None),
        P("img", "row", None),
    )
    out_specs = (
        P("img", "row", None),
        P("img", "row", None),
        P(),
        P(),
        P(),
        P(("img", "row"), None, None),
        P(("img", "row"), None),
        P(("img", "row"), None, None),
        P(("img", "row"), None),
        P(("img", "row"), None),
        P(("img", "row"), None),
        P(("img", "row"), None),
    )
    return jax.shard_map(local, mesh=mesh, in_specs=in_specs, out_specs=out_specs, check_vma=False)
```

profile of v0, /device:TPU:0, one launch (start us, length us, event | category | flops | bytes accessed | tf_op | source)
XLA Modules:
  0.0 3463.4 jit_solution(13838896250400454699)
XLA Ops:
  16.0 152.3 %all-gather.30.cloned.1.call-done = bf16[2048,3,2048]{2,0,1:T(8,128)(2,1)} async-done(((bf16[64,3,2048]{2,0,1:T(8,128)(2,1)}), bf16[2048,3,2048]{2,0,1:T(8,128)(2,1)}) %all-gather.30.cloned.1.call-update) | async-done | bytes 25165840 | tf_op jit(solution)/shard_map/all_gather | solution.py:135
  185.6 98.6 %all-gather.34.cloned.1.call-done = bf16[2048,4096]{1,0:T(8,128)(2,1)} async-done(((bf16[64,4096]{1,0:T(8,128)(2,1)}), bf16[2048,4096]{1,0:T(8,128)(2,1)}) %all-gather.34.cloned.1.call-update) | async-done | bytes 16777232 | tf_op jit(solution)/shard_map/all_gather | solution.py:157
  296.7 143.3 %all-gather.36.cloned.1.call-done = bf16[2048,3,2048]{2,0,1:T(8,128)(2,1)} async-done(((bf16[64,3,2048]{2,0,1:T(8,128)(2,1)}), bf16[2048,3,2048]{2,0,1:T(8,128)(2,1)}) %all-gather.36.cloned.1.call-update) | async-done | bytes 25165840 | tf_op jit(solution)/shard_map/all_gather | solution.py:155
  463.9 20.9 all-gather.58.cloned.1.call-done
  492.6 72.6 %all-gather.32.cloned.1.call-done = bf16[2048,2048]{1,0:T(8,128)(2,1)} async-done(((bf16[64,2048]{1,0:T(8,128)(2,1)}), bf16[2048,2048]{1,0:T(8,128)(2,1)}) %all-gather.32.cloned.1.call-update) | async-done | bytes 8388624 | tf_op jit(solution)/shard_map/all_gather | solution.py:136
  586.6 57.8 %all-gather.38.cloned.1.call-done = bf16[2048,2048]{1,0:T(8,128)(2,1)} async-done(((bf16[64,2048]{1,0:T(8,128)(2,1)}), bf16[2048,2048]{1,0:T(8,128)(2,1)}) %all-gather.38.cloned.1.call-update) | async-done | bytes 8388624 | tf_op jit(solution)/shard_map/all_gather | solution.py:156
  653.1 187.8 %all-gather.40.cloned.1.call-done = bf16[2048,8192]{1,0:T(8,128)(2,1)} async-done(((bf16[64,8192]{1,0:T(8,128)(2,1)}), bf16[2048,8192]{1,0:T(8,128)(2,1)}) %all-gather.40.cloned.1.call-update) | async-done | bytes 33554448 | tf_op jit(solution)/shard_map/all_gather | solution.py:179
  840.9 20.2 multiply_convert_fusion
  861.1 176.0 %all-gather.42.cloned.1.call-done = bf16[2048,8192]{1,0:T(8,128)(2,1)} async-done(((bf16[64,8192]{1,0:T(8,128)(2,1)}), bf16[2048,8192]{1,0:T(8,128)(2,1)}) %all-gather.42.cloned.1.call-update) | async-done | bytes 33554448 | tf_op jit(solution)/shard_map/all_gather | solution.py:180
  1126.3 23.3 reduce-scatter.3.cloned.1.call-done
  1152.5 19.7 all-gather.62.cloned.1.call-done
  1173.7 21.4 all-gather.68.cloned.1.call-done
  1199.4 18.5 all-gather.60.cloned.1.call-done
  1220.2 21.0 all-gather.64.cloned.1.call-done
  1244.5 19.4 all-gather.66.cloned.1.call-done
  1267.3 19.4 all-gather.70.cloned.1.call-done
  1290.4 55.0 %all-gather.44.cloned.1.call-done = bf16[256,8192]{1,0:T(8,128)(2,1)} async-done(((bf16[128,8192]{1,0:T(8,128)(2,1)}), bf16[256,8192]{1,0:T(8,128)(2,1)}) %all-gather.44.cloned.1.call-update) | async-done | bytes 4194320 | tf_op jit(solution)/shard_map/all_gather | solution.py:289
  1345.4 20.1 convolution_dynamic-update-slice_fusion.1
  1365.5 38.8 %all-gather.46.cloned.1.call-done = bf16[256,8192]{1,0:T(8,128)(2,1)} async-done(((bf16[128,8192]{1,0:T(8,128)(2,1)}), bf16[256,8192]{1,0:T(8,128)(2,1)}) %all-gather.46.cloned.1.call-update) | async-done | bytes 4194320 | tf_op jit(solution)/shard_map/all_gather | solution.py:290
  1404.3 18.5 convolution_dynamic-update-slice_fusion
  1456.3 41.2 %all-gather.52.cloned.1.call-done = bf16[256,6144]{0,1:T(8,128)(2,1)} async-done(((bf16[128,6144]{0,1:T(8,128)(2,1)}), bf16[256,6144]{0,1:T(8,128)(2,1)}) %all-gather.52.cloned.1.call-update) | async-done | bytes 3145744 | tf_op jit(solution)/shard_map/all_gather | solution.py:296
  1536.4 17.1 fusion.21
  1569.4 83.1 %all-reduce.6 = (bf16[128,2048]{0,1:T(8,128)(2,1)S(1)}, bf16[128,2048]{0,1:T(8,128)(2,1)S(1)}, f32[3,2048]{1,0:T(4,128)}, f32[2048]{0:T(1024)}) all-reduce(f32[128,2048]{0,1:T(8,128)} %bitcast.290, f32[128,2048]{0,1:T(8,128)} %bitcast.291, f32[3,2048]{1,0:T(4,128)S(1)} %pad_maximum_fusion.2, ...), channel_id=1, replica_groups=mesh['img'=16,'row'=2] {'img','row'}, use_global_device_ids=true, to_apply=%region_22.23 | all-reduce | flops 532480 | bytes 3211264 | tf_op jit(solution)/shard_map/psum | solution.py:342
  1680.1 1764.1 %all-reduce.5.cloned.1.call-done = f32[1024,28672]{1,0:T(8,128)} async-done(((f32[1024,28672]{1,0:T(8,128)}), f32[1024,28672]{1,0:T(8,128)}) %all-reduce.5.cloned.1.call-update) | async-done | bytes 117440528
  (232 shorter events, 336.8 us)
Async XLA Ops:
  7.2 161.1 %all-gather.30.cloned.1.call-start = ((), (), s32[]{:S(2)}) async-start(), calls=%async_computation.2 | async-start | bytes 25952256 | tf_op jit(solution)/shard_map/all_gather | solution.py:135
  7.9 276.3 %all-gather.34.cloned.1.call-start = ((), (), s32[]{:S(2)}) async-start(), calls=%async_computation.4 | async-start | bytes 17301504 | tf_op jit(solution)/shard_map/all_gather | solution.py:157
  8.7 431.3 %all-gather.36.cloned.1.call-start = ((), (), s32[]{:S(2)}) async-start(), calls=%async_computation.5 | async-start | bytes 25952256 | tf_op jit(solution)/shard_map/all_gather | solution.py:155
  9.4 452.1 %all-gather.56.cloned.1.call-start = ((), (), s32[]{:S(2)}) async-start(), calls=%async_computation.17 | async-start | bytes 1572864 | tf_op jit(solution)/shard_map/all_gather | solution.py:146
  181.0 303.8 %all-gather.58.cloned.1.call-start = ((), (), s32[]{:S(2)}) async-start(), calls=%async_computation.18 | async-start | bytes 1572864 | tf_op jit(solution)/shard_map/all_gather | solution.py:145
  181.6 383.6 %all-gather.32.cloned.1.call-start = ((), (), s32[]{:S(2)}) async-start(), calls=%async_computation.3 | async-start | bytes 8650752 | tf_op jit(solution)/shard_map/all_gather | solution.py:136
  182.2 462.2 %all-gather.38.cloned.1.call-start = ((), (), s32[]{:S(2)}) async-start(), calls=%async_computation.6 | async-start | bytes 8650752 | tf_op jit(solution)/shard_map/all_gather | solution.py:156
  182.9 658.0 %all-gather.40.cloned.1.call-start = ((), (), s32[]{:S(2)}) async-start(), calls=%async_computation.7 | async-start | bytes 34603008 | tf_op jit(solution)/shard_map/all_gather | solution.py:179
  183.7 853.4 %all-gather.42.cloned.1.call-start = ((), (), s32[]{:S(2)}) async-start(), calls=%async_computation.8 | async-start | bytes 34603008 | tf_op jit(solution)/shard_map/all_gather | solution.py:180
  184.4 941.9 %reduce-scatter.5.cloned.1.call-start = ((), (), s32[]{:S(2)}) async-start(), calls=%async_computation.10 | async-start | bytes 1572864 | tf_op jit(solution)/shard_map/reduce_scatter | solution.py:259
  1107.6 41.9 %reduce-scatter.3.cloned.1.call-start = ((), (), s32[]{:S(2)}) async-start(), calls=%async_computation.9 | async-start | bytes 1572864 | tf_op jit(solution)/shard_map/reduce_scatter | solution.py:256
  1113.8 58.5 %all-gather.62.cloned.1.call-start = ((), (), s32[]{:S(2)}) async-start(), calls=%async_computation.20 | async-start | bytes 1572864 | tf_op jit(solution)/shard_map/all_gather | solution.py:288
  1114.4 80.8 %all-gather.68.cloned.1.call-start = ((), (), s32[]{:S(2)}) async-start(), calls=%async_computation.23 | async-start | bytes 1572864 | tf_op jit(solution)/shard_map/all_gather | solution.py:295
  1115.1 102.8 %all-gather.60.cloned.1.call-start = ((), (), s32[]{:S(2)}) async-start(), calls=%async_computation.19 | async-start | bytes 1572864 | tf_op jit(solution)/shard_map/all_gather | solution.py:287
  1115.7 125.5 %all-gather.64.cloned.1.call-start = ((), (), s32[]{:S(2)}) async-start(), calls=%async_computation.21 | async-start | bytes 1572864 | tf_op jit(solution)/shard_map/all_gather | solution.py:291
  1116.3 147.7 %all-gather.66.cloned.1.call-start = ((), (), s32[]{:S(2)}) async-start(), calls=%async_computation.22 | async-start | bytes 1572864 | tf_op jit(solution)/shard_map/all_gather | solution.py:293
  1116.9 169.8 %all-gather.70.cloned.1.call-start = ((), (), s32[]{:S(2)}) async-start(), calls=%async_computation.24 | async-start | bytes 1572864 | tf_op jit(solution)/shard_map/all_gather | solution.py:297
  1117.5 228.0 %all-gather.44.cloned.1.call-start = ((), (), s32[]{:S(2)}) async-start(), calls=%async_computation.11 | async-start | bytes 6291456 | tf_op jit(solution)/shard_map/all_gather | solution.py:289
  1118.0 286.3 %all-gather.46.cloned.1.call-start = ((), (), s32[]{:S(2)}) async-start(), calls=%async_computation.12 | async-start | bytes 6291456 | tf_op jit(solution)/shard_map/all_gather | solution.py:290
  1118.8 308.8 %all-gather.48.cloned.1.call-start = ((), (), s32[]{:S(2)}) async-start(), calls=%async_computation.13 | async-start | bytes 1572864 | tf_op jit(solution)/shard_map/all_gather | solution.py:292
  1119.4 331.1 %all-gather.50.cloned.1.call-start = ((), (), s32[]{:S(2)}) async-start(), calls=%async_computation.14 | async-start | bytes 1572864 | tf_op jit(solution)/shard_map/all_gather | solution.py:294
  1120.1 377.4 %all-gather.52.cloned.1.call-start = ((), (), s32[]{:S(2)}) async-start(), calls=%async_computation.15 | async-start | bytes 4718592 | tf_op jit(solution)/shard_map/all_gather | solution.py:296
  1152.5 368.4 %all-gather.54.cloned.1.call-start = ((), (), s32[]{:S(2)}) async-start(), calls=%async_computation.16 | async-start | bytes 1572864 | tf_op jit(solution)/shard_map/all_gather | solution.py:298
  1199.3 2244.9 %all-reduce.5.cloned.1.call-start = ((), (), s32[]{:S(2)}) async-start(), calls=%async_computation.25 | async-start | bytes 234881024
  (36 other events, 1916.5 us)
Sparse Core Ops, SparseCore 0:
  11.1 157.1 all-gather.29
  171.2 113.0 all-gather.33
  287.3 152.6 all-gather.35
  442.0 19.4 all-gather.55
  463.5 21.2 all-gather.57
  487.8 77.4 all-gather.31
  568.3 75.9 all-gather.37
  647.5 193.3 all-gather.39
  844.0 192.9 all-gather.41
  1107.8 18.4 reduce-scatter.4
  1129.2 20.3 reduce-scatter.2
  1150.9 21.2 all-gather.61
  1173.8 21.2 all-gather.67
  1196.5 21.2 all-gather.59
  1219.9 21.2 all-gather.63
  1242.6 21.2 all-gather.65
  1265.3 21.2 all-gather.69
  1288.6 56.7 all-gather.43
  1347.5 56.7 all-gather.45
  1406.3 21.2 all-gather.47
  1429.1 21.2 all-gather.49
  1452.6 44.8 all-gather.51
  1499.6 21.2 all-gather.53
  1527.1 1917.0 all-reduce.4
where the time goes:
time: 3470 us; the launch traced here: 3460 us
  waiting for transfers between devices  3010 us (87%)
  matrix products  273 us (8%)
  blocking collectives  83.1 us (2%)
  local copies, waits for them, and re-layouts  58.8 us (2%)
    unnamed x25, waiting for transfers between devices  1780 us
    all_gather x1, waiting for transfers between devices, local(): lax.all_gather(w_up, ('img', 'row'), axis=0, tiled=True)  188 us
    all_gather x1, waiting for transfers between devices, local(): lax.all_gather(w_down, ('img', 'row'), axis=0, tiled=True)  176 us
    all_gather x1, waiting for transfers between devices, local(): lax.all_gather(w_qkv, ('img', 'row'), axis=0, tiled=True)  152 us
    all_gather x1, waiting for transfers between devices, local(): lax.all_gather(w_cross, ('img', 'row'), axis=0, tiled=True)  143 us
    all_gather x1, waiting for transfers between devices, local(): lax.all_gather(w_text, ('img', 'row'), axis=0, tiled=True)  98.6 us
    psum x1, blocking collectives, local(): lax.psum((gain_part, mask_part, grad_text_keys, grad_text_values), ('img'...  83.1 us
    all_gather x1, waiting for transfers between devices, local(): lax.all_gather(w_out, ('img', 'row'), axis=0, tiled=True)  72.6 us
  transfers between devices with their start and end apart: 24, of which 24 were waited for; matrix products, arithmetic and copies ran while one was open for 8% of the time, Pallas kernels for 0%

commit v1 on v0

v1 whole, which is shorter than its diff:
```python
import math

import jax
import jax.numpy as jnp
from jax import lax
from jax.sharding import Mesh
from jax.sharding import PartitionSpec as P

HD = 128
EPS = 1e-05
BF = jnp.bfloat16
F32 = jnp.float32
PAIR = ((0, 1), (1, 0))
DIAG = ((0, 3), (1, 2), (2, 1), (3, 0))
DATA = ("z", "c")


def dot(a, b, dims):
    return lax.dot_general(a, b, (dims, ((), ())), preferred_element_type=F32)


def mm(a, b):
    return dot(a, b, ((1,), (0,)))


def mm_t(a, b):
    return dot(a, b, ((1,), (1,)))


def t_mm(a, b):
    return dot(a, b, ((0,), (0,)))


def normalize(values):
    centred = values - jnp.mean(values, axis=-1, keepdims=True)
    inv_std = lax.rsqrt(jnp.mean(centred * centred, axis=-1, keepdims=True) + EPS)
    return centred * inv_std, inv_std


def norm_back(grad_normed, normed, inv_std, gain):
    scaled = grad_normed * gain
    first_mean = jnp.mean(scaled, axis=-1, keepdims=True)
    second_mean = jnp.mean(scaled * normed, axis=-1, keepdims=True)
    return (
        inv_std * (scaled - first_mean - normed * second_mean),
        jnp.sum(grad_normed * normed, axis=0),
    )


def swap(values, axis):
    return lax.ppermute(values, axis, PAIR)


def swap_diag(values):
    return lax.ppermute(values, ("x", "y"), DIAG)


def gather_tokens(own):
    half = own.shape[0] // 2
    from_x = swap(own, "x")
    from_y = swap(own, "y")
    diag_low = swap(from_x[:half], "y")
    diag_high = swap(from_y[half:], "x")
    return jnp.concatenate([own, from_y, from_x, diag_low, diag_high], axis=0)


def scatter_tokens(partial):
    rows = partial.shape[0] // 4
    half = rows // 2
    own, for_y, for_x, for_diag = (partial[k * rows : (k + 1) * rows] for k in range(4))
    for_diag = for_diag.astype(BF)
    diag_low = swap(for_diag[:half], "y").astype(F32)
    diag_high = swap(for_diag[half:], "x").astype(F32)
    from_x = swap(
        jnp.concatenate([for_x[:half] + diag_low, for_x[half:]], axis=0).astype(BF), "x"
    )
    from_y = swap(
        jnp.concatenate([for_y[:half], for_y[half:] + diag_high], axis=0).astype(BF), "y"
    )
    return own + from_x.astype(F32) + from_y.astype(F32)


def exchange(blocks, rank):
    def pick(k):
        return lax.dynamic_index_in_dim(blocks, rank ^ k, 0, keepdims=True)

    parts = [pick(0), swap(pick(1), "y"), swap(pick(2), "x"), swap_diag(pick(3))]
    out = jnp.zeros_like(blocks)
    for k, part in enumerate(parts):
        out = lax.dynamic_update_slice_in_dim(out, part, rank ^ k, 0)
    return out


def column_blocks(weight, parts):
    rows = weight.shape[0]
    shaped = weight.reshape(rows, parts, 4, -1)
    return shaped.transpose(2, 0, 1, 3).reshape(4, rows, -1)


def weight_columns(blocks, rank):
    mine = exchange(blocks, rank)
    return lax.all_gather(mine.reshape(-1, mine.shape[-1]), DATA, axis=0, tiled=True)


def grad_rows(partial, rank):
    summed = lax.psum_scatter(partial, DATA, scatter_dimension=0, tiled=True)
    return exchange(summed.reshape(4, -1, summed.shape[-1]), rank)


def join_columns(blocks, parts):
    rows = blocks.shape[1]
    shaped = blocks.reshape(4, rows, parts, -1)
    return shaped.transpose(1, 2, 0, 3).reshape(rows, parts, -1)


def heads_of(values, images):
    return values.reshape(images, -1, values.shape[-1] // HD, HD)


def attend_forward(queries, keys, values, score_form, mix_form, scale):
    scores = jnp.einsum(score_form, queries, keys, preferred_element_type=F32) * scale
    row_peak = jnp.max(scores, axis=-1, keepdims=True)
    exp_terms = jnp.exp(scores - row_peak)
    probs = exp_terms / jnp.sum(exp_terms, axis=-1, keepdims=True)
    mixed = jnp.einsum(mix_form, probs.astype(BF), values, preferred_element_type=F32)
    return probs, mixed.astype(BF)


def attend_back(probs, queries, keys, values, grad_mixed, score_form, mix_form, key_form, scale):
    grad_probs = jnp.einsum(score_form, grad_mixed, values, preferred_element_type=F32)
    grad_scores = (
        probs * (grad_probs - jnp.sum(probs * grad_probs, axis=-1, keepdims=True))
    ).astype(BF)
    grad_queries = jnp.einsum(mix_form, grad_scores, keys, preferred_element_type=F32) * scale
    grad_keys = jnp.einsum(key_form, grad_scores, queries, preferred_element_type=F32) * scale
    grad_values = jnp.einsum(
        key_form, probs.astype(BF), grad_mixed, preferred_element_type=F32
    )
    return grad_queries, grad_keys, grad_values


def make_local(z_size):
    def sum_all(values):
        for axis in ("c", "x", "y"):
            values = values + swap(values, axis)
        step = 1
        while step < z_size:
            values = values + lax.ppermute(
                values, "z", tuple((k, k ^ step) for k in range(z_size))
            )
            step *= 2
        return values

    def feature_swap(values):
        lead = values.shape[:-1]
        shaped = values.reshape(lead + (z_size, 2, 2, -1))
        return jnp.swapaxes(shaped, -3, -2).reshape(values.shape)

    def local(
        hidden,
        mask_index,
        mask_count,
        mask_embed,
        norm_gains,
        caption,
        w_qkv,
        w_out,
        w_cross,
        w_cross_out,
        w_text,
        w_up,
        w_down,
        cotangent,
    ):
        images, local_rows, width = hidden.shape
        full_length = mask_index.shape[1]
        scale = 1.0 / math.sqrt(HD)
        shard_rows = w_qkv.shape[0]
        rank = lax.axis_index("x") * 2 + lax.axis_index("y")
        tokens = images * local_rows

        qkv = weight_columns(column_blocks(w_qkv.reshape(shard_rows, -1), 3), rank)
        mid = weight_columns(
            jnp.concatenate(
                [
                    column_blocks(w_out, 1),
                    column_blocks(w_cross[:, 0], 1),
                    column_blocks(w_cross_out, 1),
                ],
                axis=2,
            ),
            rank,
        )
        up = weight_columns(column_blocks(w_up, 1), rank)
        down = weight_columns(column_blocks(w_down, 1), rank)
        group = width // 4
        out_w, query_w, cross_out_w = (mid[:, k * group : (k + 1) * group] for k in range(3))

        own_text = mm_t(caption, w_text).astype(BF)
        kv_rows = w_cross[:, 1:].reshape(shard_rows, 2 * width)
        kv_part = mm(own_text, kv_rows)
        kv_part = exchange(column_blocks(kv_part, 2), rank).sum(axis=0)
        text_kv = lax.psum(kv_part, DATA).astype(BF)
        text_keys = text_kv[:, :group].reshape(-1, group // HD, HD)
        text_values = text_kv[:, group:].reshape(-1, group // HD, HD)

        positions = lax.axis_index("y") * local_rows + jnp.arange(local_rows, dtype=jnp.int32)
        ranks = jnp.arange(full_length, dtype=jnp.int32)
        matches = (mask_index[:, :, None] == positions[None, None, :]) & (
            ranks[None, :, None] < mask_count[:, None, None]
        )
        masked = jnp.any(matches, axis=1).reshape(tokens, 1)
        gains = feature_swap(norm_gains)
        start_x = jnp.where(
            masked,
            feature_swap(mask_embed),
            feature_swap(hidden.reshape(tokens, width)).astype(F32),
        )
        grad_top = feature_swap(cotangent.reshape(tokens, width)).astype(F32) * masked.astype(F32)
        grad_y = gather_tokens(grad_top.astype(BF))

        normed_a, inv_a = normalize(start_x)
        attn_in = gather_tokens((normed_a * gains[0]).astype(BF))
        projected = mm(attn_in, qkv).astype(BF)
        queries, keys, values = (
            heads_of(projected[:, k * group : (k + 1) * group], 2 * images) for k in range(3)
        )
        self_forms = ("bqhe,bkhe->bhqk", "bhqk,bkhe->bqhe")
        self_probs, self_mixed = attend_forward(queries, keys, values, *self_forms, scale)
        self_mixed = self_mixed.reshape(4 * tokens, group)
        after_attn = start_x + scatter_tokens(mm_t(self_mixed, out_w))

        normed_b, inv_b = normalize(after_attn)
        cross_in = gather_tokens((normed_b * gains[1]).astype(BF))
        cross_queries = heads_of(mm(cross_in, query_w).astype(BF), 2 * images)
        cross_forms = ("bqhe,khe->bhqk", "bhqk,khe->bqhe")
        cross_probs, cross_mixed = attend_forward(
            cross_queries, text_keys, text_values, *cross_forms, scale
        )
        cross_mixed = cross_mixed.reshape(4 * tokens, group)
        after_cross = after_attn + scatter_tokens(mm_t(cross_mixed, cross_out_w))

        normed_c, inv_c = normalize(after_cross)
        mlp_in = gather_tokens((normed_c * gains[2]).astype(BF))
        pre_act = mm(mlp_in, up)
        activated, gelu_pull = jax.vjp(jax.nn.gelu, pre_act)
        activated = activated.astype(BF)
        grad_pre = gelu_pull(mm(grad_y, down))[0].astype(BF)
        grad_mlp_in = scatter_tokens(mm_t(grad_pre, up))
        result = after_cross + scatter_tokens(mm_t(activated, down))
        output = feature_swap(result.astype(BF))
        down_grad = grad_rows(t_mm(grad_y, activated).astype(BF), rank)
        up_grad = grad_rows(t_mm(mlp_in, grad_pre).astype(BF), rank)
        back_c, gain_grad_c = norm_back(grad_mlp_in, normed_c, inv_c, gains[2])
        grad_after_cross = grad_top + back_c

        cross_branch = gather_tokens(grad_after_cross.astype(BF))
        grad_cross_mixed = heads_of(mm(cross_branch, cross_out_w).astype(BF), 2 * images)
        grad_cq, grad_tk, grad_tv = attend_back(
            cross_probs,
            cross_queries,
            text_keys,
            text_values,
            grad_cross_mixed,
            *cross_forms,
            "bhqk,bqhe->khe",
            scale,
        )
        grad_cq = grad_cq.astype(BF).reshape(4 * tokens, group)
        grad_cross_in = scatter_tokens(mm_t(grad_cq, query_w))
        back_b, gain_grad_b = norm_back(grad_cross_in, normed_b, inv_b, gains[1])
        grad_after_attn = grad_after_cross + back_b

        kv_grad = jnp.concatenate(
            [grad_tk.reshape(-1, group), grad_tv.reshape(-1, group)], axis=1
        )
        kv_grad = lax.psum(kv_grad, DATA).astype(BF)
        kv_grads = exchange(jnp.broadcast_to(kv_grad[None], (4,) + kv_grad.shape), rank)
        kv_grads = join_columns(kv_grads, 2).reshape(-1, 2 * width)
        kv_weight_grad = t_mm(own_text, kv_grads).reshape(shard_rows, 2, width)
        grad_text = mm_t(kv_grads, kv_rows).astype(BF)
        grad_text_w = t_mm(grad_text, caption)
        caption_part = mm(grad_text, w_text)
        caption_part = exchange(column_blocks(caption_part, 1), rank).sum(axis=0)
        caption_part = lax.psum(caption_part, DATA)
        caption_parts = exchange(
            jnp.broadcast_to(caption_part[None], (4,) + caption_part.shape), rank
        )
        grad_caption = join_columns(caption_parts, 1)[:, 0]

        attn_branch = gather_tokens(grad_after_attn.astype(BF))
        grad_self_mixed = heads_of(mm(attn_branch, out_w).astype(BF), 2 * images)
        grad_projected = attend_back(
            self_probs,
            queries,
            keys,
            values,
            grad_self_mixed,
            *self_forms,
            "bhqk,bqhe->bkhe",
            scale,
        )
        grad_projected = jnp.concatenate(
            [part.astype(BF).reshape(4 * tokens, group) for part in grad_projected], axis=1
        )
        mid_part = jnp.concatenate(
            [
                t_mm(attn_branch, self_mixed).astype(BF),
                t_mm(cross_in, grad_cq).astype(BF),
                t_mm(cross_branch, cross_mixed).astype(BF),
            ],
            axis=1,
        )
        mid_grad = join_columns(grad_rows(mid_part, rank), 3)
        qkv_grad = join_columns(
            grad_rows(t_mm(attn_in, grad_projected).astype(BF), rank), 3
        ).astype(F32)
        grad_attn_in = scatter_tokens(mm_t(grad_projected, qkv))
        back_a, gain_grad_a = norm_back(grad_attn_in, normed_a, inv_a, gains[0])
        grad_start = grad_after_attn + back_a

        grad_hidden = feature_swap(jnp.where(masked, 0.0, grad_start).astype(BF))
        mask_part = jnp.sum(jnp.where(masked, grad_start, 0.0), axis=0)
        sums = feature_swap(
            sum_all(jnp.stack([gain_grad_a, gain_grad_b, gain_grad_c, mask_part]))
        )
        mid_grad = mid_grad.astype(F32)
        grad_cross = jnp.concatenate([mid_grad[:, 1:2], kv_weight_grad], axis=1)
        return (
            output.reshape(hidden.shape),
            grad_hidden.reshape(hidden.shape),
            grad_caption,
            sums[:3],
            sums[3],
            qkv_grad,
            mid_grad[:, 0],
            grad_cross,
            mid_grad[:, 2],
            grad_text_w,
            join_columns(up_grad, 1)[:, 0].astype(F32),
            join_columns(down_grad, 1)[:, 0].astype(F32),
        )

    return local


def solution(mesh):
    z_size = mesh.shape["img"] // 4
    inner = Mesh(mesh.devices.reshape(z_size, 2, 2, 2), ("z", "x", "c", "y"))
    tokens = P(("z", "x", "c"), "y", None)
    rows = P(("z", "x", "c", "y"))
    in_specs = (
        tokens,
        P(("z", "x", "c"), None),
        P(("z", "x", "c")),
        P(),
        P(),
        P(),
        rows,
        rows,
        rows,
        rows,
        rows,
        rows,
        rows,
        tokens,
    )
    out_specs = (tokens, tokens, P(), P(), P()) + (rows,) * 7
    return jax.shard_map(
        make_local(z_size), mesh=inner, in_specs=in_specs, out_specs=out_specs, check_vma=False
    )
```

time: 3470 us -> 1020 us (0.29)
  waiting for transfers between devices: 3010 us -> 372 us
  local copies, waits for them, and re-layouts: 58.8 us -> 252 us
  matrix products: 273 us -> 136 us
  starting transfers between devices: 1.15 us -> 105 us
    unnamed x25 -> x9, waiting for transfers between devices: 1780 us -> 0.15 us
    all_gather x21 -> x4, waiting for transfers between devices: 1210 us -> 34.9 us  [weight_columns(): lax.all_gather(mine.reshape(-1, mine.shape[-1]), DATA, axis=0, tiled=True)]
    ppermute x0 -> x89, waiting for transfers between devices: none -> 177 us  [the longest x75 154 us: swap(): return lax.ppermute(values, axis, PAIR)]
    dot_general x38 -> x34, matrix products: 273 us -> 131 us  [the longest x24 114 us: dot(): return lax.dot_general(a, b, (dims, ((), ())), preferred_element_type=F32)]
    reduce_scatter x2 -> x4, waiting for transfers between devices: 26.9 us -> 160 us  [grad_rows(): summed = lax.psum_scatter(partial, DATA, scatter_dimension=0, tiled=True)]
    ppermute x0 -> x89, starting transfers between devices: none -> 103 us  [the longest x75 86.3 us: swap(): return lax.ppermute(values, axis, PAIR)]
    dynamic_update_slice x0 -> x44, local copies, waits for them, and re-layouts: none -> 86.9 us  [exchange(): out = lax.dynamic_update_slice_in_dim(out, part, rank ^ k, 0)]
    reshape x1 -> x36, local copies, waits for them, and re-layouts: 1.3 us -> 37.3 us  [the longest x12 17.3 us: join_columns(): shaped = blocks.reshape(4, rows, parts, -1)]
  transfers between devices with their start and end apart: 24 -> 98, of which waited for: 24 -> 52; matrix products, arithmetic and copies ran while one was open for 8% -> 37% of each run, Pallas kernels for 0% -> 0%
where the time goes in v1:
time: 1020 us; the launch traced here: 1000 us
  waiting for transfers between devices  372 us (36%)
  local copies, waits for them, and re-layouts  252 us (25%)
  matrix products  136 us (13%)
  starting transfers between devices  105 us (10%)
  blocking collectives  75.1 us (7%)
  other arithmetic  48.4 us (5%)
  between operations  16.7 us (2%)
    reduce_scatter x4, waiting for transfers between devices, grad_rows(): summed = lax.psum_scatter(partial, DATA, scatter_dimension=0, tiled=True)  160 us
    ppermute x75, waiting for transfers between devices, swap(): return lax.ppermute(values, axis, PAIR)  154 us
    dot_general x24, matrix products, dot(): return lax.dot_general(a, b, (dims, ((), ())), preferred_element_type=F32)  114 us
    dynamic_update_slice x44, local copies, waits for them, and re-layouts, exchange(): out = lax.dynamic_update_slice_in_dim(out, part, rank ^ k, 0)  86.9 us
    ppermute x75, starting transfers between devices, swap(): return lax.ppermute(values, axis, PAIR)  86.3 us
    psum x1, blocking collectives, local(): text_kv = lax.psum(kv_part, DATA).astype(BF)  39.4 us
    unnamed x200, local copies, waits for them, and re-layouts  37.8 us
    psum x1, blocking collectives, local(): kv_grad = lax.psum(kv_grad, DATA).astype(BF)  35.6 us
  transfers between devices with their start and end apart: 98, of which 52 were waited for; matrix products, arithmetic and copies ran while one was open for 37% of the time, Pallas kernels for 0%

profile of v1, /device:TPU:0, one launch (start us, length us, event | category | flops | bytes accessed | tf_op | source)
XLA Modules:
  0.0 1004.8 jit_solution(1668774046977958010)
XLA Ops:
  123.1 34.8 %all-gather.7.cloned.1.call-done = bf16[2048,1536]{1,0:T(8,128)(2,1)} async-done(((bf16[256,1536]{1,0:T(8,128)(2,1)}), bf16[2048,1536]{1,0:T(8,128)(2,1)}) %all-gather.7.cloned.1.call-update) | async-done | bytes 6291472 | tf_op jit(solution)/shard_map/all_gather | solution.py:102
  194.0 8.0 collective-permute-done.16
  216.3 39.4 %all-reduce.5 = bf16[128,1024]{0,1:T(8,128)(2,1)S(1)} all-reduce(f32[128,1024]{0,1:T(8,128)S(1)} %copy-done.35), channel_id=1, replica_groups=mesh['z'=4,'x'=2,'c'=2,'y'=2] {'z','c'}, use_global_device_ids=true, to_apply=%region_6.7 | all-reduce | flops 131072 | bytes 786432 | tf_op jit(solution)/shard_map/psum | solution.py:203
  290.9 8.9 collective-permute-done.40
  302.0 8.4 collective-permute-done.24
  316.7 8.3 collective-permute-done.26
  333.1 10.6 %fusion.123 = f32[512,2048]{1,0:T(8,128)} fusion(bf16[512,2048]{1,0:T(8,128)(2,1)} %constant_dynamic-update-slice_fusion.10, bf16[2048,2048]{1,0:T(8,128)(2,1)} %all-gather.9.cloned.1.call-done), kind=kOutput, calls=%fused_computation.344 | convolution fusion | flops 4294967296 | bytes 14680064 | tf_op jit(solution)/shard_map/dot_general | solution.py:19
  343.7 12.1 %fusion.8 = bf16[512,2048]{1,0:T(8,128)(2,1)S(1)} fusion(f32[512,2048]{1,0:T(8,128)} %fusion.123, bf16[512,2048]{1,0:T(8,128)(2,1)} %copy-done.57, bf16[2048,2048]{1,0:T(8,128)(2,1)} %all-gather.11.cloned.1.call-done), kind=kOutput, calls=%fused_computation.14 | convolution fusion | flops 4315938816 | bytes 16777216 | tf_op jit(solution)/shard_map/dot_general | solution.py:19
  362.7 8.9 fusion.120
  403.7 9.6 collective-permute-done.48
  432.9 35.6 %all-reduce.6 = bf16[128,1024]{0,1:T(8,128)(2,1)S(1)} all-reduce(f32[128,1024]{0,1:T(8,128)S(1)} %pad_maximum_fusion.15), channel_id=1, replica_groups=mesh['z'=4,'x'=2,'c'=2,'y'=2] {'z','c'}, use_global_device_ids=true, to_apply=%region_21.22 | all-reduce | flops 131072 | bytes 786432 | tf_op jit(solution)/shard_map/psum | solution.py:277
  554.8 11.4 %pad_maximum_fusion = bf16[2048,1536]{0,1:T(8,128)(2,1)} fusion(bf16[2048,512]{0,1:T(8,128)(2,1)S(1)} %copy-done.36, bf16[2048,512]{0,1:T(8,128)(2,1)S(1)} %copy-done.37, bf16[2048,512]{0,1:T(8,128)(2,1)S(1)} %convolution_convert_fusion.5), kind=kLoop, calls=%fused_computation.5 | loop fusion | flops 18874368 | bytes 12582912 | tf_op jit(solution)/shard_map/concatenate | solution.py:306
  596.3 10.2 %convolution_convert_fusion.1 = bf16[2048,2048]{1,0:T(8,128)(2,1)} fusion(bf16[512,2048]{1,0:T(8,128)(2,1)} %constant_dynamic-update-slice_fusion.10, bf16[512,2048]{1,0:T(8,128)(2,1)} %copy-done.82), kind=kOutput, calls=%fused_computation.3 | convolution fusion | flops 4299161600 | bytes 12582912 | tf_op jit(solution)/shard_map/dot_general | solution.py:19
  606.5 10.9 %convolution_convert_fusion = bf16[2048,2048]{1,0:T(8,128)(2,1)} fusion(bf16[512,2048]{1,0:T(8,128)(2,1)} %copy-done.57, f32[512,2048]{1,0:T(8,128)} %fusion.123), kind=kOutput, calls=%fused_computation.2 | convolution fusion | flops 4308598784 | bytes 14680064 | tf_op jit(solution)/shard_map/dot_general | solution.py:19
  658.5 20.4 %collective-permute-done.73 = f32[4,2048]{1,0:T(4,128)S(1)} collective-permute-done((f32[4,2048]{1,0:T(4,128)S(1)}, f32[4,2048]{1,0:T(4,128)S(1)}, u32[]{:S(2)}, u32[]{:S(2)}) %collective-permute-start.73) | collective-permute-done | bytes 32800 | tf_op jit(solution)/shard_map/ppermute | solution.py:51
  688.2 8.3 dynamic_update_slice.187
  712.8 28.8 %reduce-scatter.5.cloned.1.call-done = bf16[256,1536]{1,0:T(8,128)(2,1)} async-done(((bf16[2048,1536]{1,0:T(8,128)(2,1)}), bf16[256,1536]{1,0:T(8,128)(2,1)}) %reduce-scatter.5.cloned.1.call-update) | async-done | bytes 786448 | tf_op jit(solution)/shard_map/reduce_scatter | solution.py:106
  751.7 9.1 collective-permute-done.81
  775.7 56.3 %reduce-scatter.9.cloned.1.call-done = bf16[256,2048]{1,0:T(8,128)(2,1)} async-done(((bf16[2048,2048]{1,0:T(8,128)(2,1)}), bf16[256,2048]{1,0:T(8,128)(2,1)}) %reduce-scatter.9.cloned.1.call-update) | async-done | bytes 1048592 | tf_op jit(solution)/shard_map/reduce_scatter | solution.py:106
  847.3 75.0 %reduce-scatter.11.cloned.1.call-done = bf16[256,2048]{1,0:T(8,128)(2,1)} async-done(((bf16[2048,2048]{1,0:T(8,128)(2,1)}), bf16[256,2048]{1,0:T(8,128)(2,1)}) %reduce-scatter.11.cloned.1.call-update) | async-done | bytes 1048592 | tf_op jit(solution)/shard_map/reduce_scatter | solution.py:106
  935.1 7.9 dynamic_update_slice.200
  957.3 7.9 dynamic_update_slice.198
  965.2 8.1 dynamic_update_slice.199
  987.4 7.9 dynamic_update_slice.203
  (655 shorter events, 541.3 us)
Async XLA Ops:
  7.2 94.9 %all-gather.5.cloned.1.call-start = ((), (), s32[]{:S(2)}) async-start(), calls=%async_computation.4 | async-start | bytes 7077888 | tf_op jit(solution)/shard_map/all_gather | solution.py:102
  25.9 132.0 %all-gather.7.cloned.1.call-start = ((), (), s32[]{:S(2)}) async-start(), calls=%async_computation.5 | async-start | bytes 7077888 | tf_op jit(solution)/shard_map/all_gather | solution.py:102
  38.9 294.2 %all-gather.9.cloned.1.call-start = ((), (), s32[]{:S(2)}) async-start(), calls=%async_computation.6 | async-start | bytes 9437184 | tf_op jit(solution)/shard_map/all_gather | solution.py:102
  55.9 287.7 %all-gather.11.cloned.1.call-start = ((), (), s32[]{:S(2)}) async-start(), calls=%async_computation.7 | async-start | bytes 9437184 | tf_op jit(solution)/shard_map/all_gather | solution.py:102
  91.9 560.0 %all-reduce.4.cloned.1.call-start = ((), (), s32[]{:S(2)}) async-start(), calls=%async_computation.8 | async-start | bytes 1048576 | tf_op jit(solution)/shard_map/psum | solution.py:285
  180.0 30.8 %collective-permute-start.13 = (bf16[128,2048]{1,0:T(8,128)(2,1)}, bf16[128,2048]{1,0:T(8,128)(2,1)}, u32[]{:S(2)}, u32[]{:S(2)}) collective-permute-start(bf16[128,2048]{1,0:T(8,128)(2,1)} %pad_maximum_fusion.4), channel_id=1, source_target_pairs={{0,1},{1,0},{2,3},{3,2},{4,5},{5,4},{6,7},{7,6},{8,9},{9,8},{10,11... | collective-permute-start | bytes 1572872 | tf_op jit(solution)/shard_map/ppermute | solution.py:51
  181.4 29.4 %collective-permute-start.11 = (bf16[128,2048]{1,0:T(8,128)(2,1)}, bf16[128,2048]{1,0:T(8,128)(2,1)}, u32[]{:S(2)}, u32[]{:S(2)}) collective-permute-start(bf16[128,2048]{1,0:T(8,128)(2,1)} %pad_maximum_fusion.3), channel_id=1, source_target_pairs={{0,4},{4,0},{1,5},{5,1},{2,6},{6,2},{3,7},{7,3},{8,12},{12,8},{9,1... | collective-permute-start | bytes 1572872 | tf_op jit(solution)/shard_map/ppermute | solution.py:51
  214.2 45.6 %collective-permute-start.17 = (bf16[128,2048]{1,0:T(8,128)(2,1)}, bf16[128,2048]{1,0:T(8,128)(2,1)S(1)}, u32[]{:S(2)}, u32[]{:S(2)}) collective-permute-start(bf16[128,2048]{1,0:T(8,128)(2,1)} %get-tuple-element.39), channel_id=1, source_target_pairs={{0,1},{1,0},{2,3},{3,2},{4,5},{5,4},{6,7},{7,6},{8,9},{9,8},{10,11... | collective-permute-start | bytes 1572872 | tf_op jit(solution)/shard_map/ppermute | solution.py:51
  216.0 40.4 %collective-permute-start.18 = (bf16[128,2048]{1,0:T(8,128)(2,1)}, bf16[128,2048]{1,0:T(8,128)(2,1)}, u32[]{:S(2)}, u32[]{:S(2)}) collective-permute-start(bf16[128,2048]{1,0:T(8,128)(2,1)} %get-tuple-element.39), channel_id=1, source_target_pairs={{0,4},{4,0},{1,5},{5,1},{2,6},{6,2},{3,7},{7,3},{8,12},{12,8},{9,1... | collective-permute-start | bytes 1572872 | tf_op jit(solution)/shard_map/ppermute | solution.py:51
  540.9 167.7 %reduce-scatter.7.cloned.1.call-start = ((), (), s32[]{:S(2)}) async-start(), calls=%async_computation.10 | async-start | bytes 7077888 | tf_op jit(solution)/shard_map/reduce_scatter | solution.py:106
  566.2 175.4 %reduce-scatter.5.cloned.1.call-start = ((), (), s32[]{:S(2)}) async-start(), calls=%async_computation.9 | async-start | bytes 7077888 | tf_op jit(solution)/shard_map/reduce_scatter | solution.py:106
  596.0 236.0 %reduce-scatter.9.cloned.1.call-start = ((), (), s32[]{:S(2)}) async-start(), calls=%async_computation.11 | async-start | bytes 9437184 | tf_op jit(solution)/shard_map/reduce_scatter | solution.py:106
  606.5 315.9 %reduce-scatter.11.cloned.1.call-start = ((), (), s32[]{:S(2)}) async-start(), calls=%async_computation.12 | async-start | bytes 9437184 | tf_op jit(solution)/shard_map/reduce_scatter | solution.py:106
  651.9 28.3 %collective-permute-start.69 = (f32[1,128,1024]{1,2,0:T(8,128)}, f32[1,128,1024]{1,2,0:T(8,128)S(1)}, u32[]{:S(2)}, u32[]{:S(2)}) collective-permute-start(f32[1,128,1024]{1,2,0:T(8,128)} %bitcast.366), channel_id=1, source_target_pairs={{0,1},{1,0},{2,3},{3,2},{4,5},{5,4},{6,7},{7,6},{8,9},{9,8},{10,11... | collective-permute-start | bytes 1572872 | tf_op jit(solution)/shard_map/ppermute | solution.py:51
  652.7 30.3 %collective-permute-start.70 = (f32[1,128,1024]{1,2,0:T(8,128)}, f32[1,128,1024]{1,2,0:T(8,128)S(1)}, u32[]{:S(2)}, u32[]{:S(2)}) collective-permute-start(f32[1,128,1024]{1,2,0:T(8,128)} %bitcast.367), channel_id=1, source_target_pairs={{0,4},{4,0},{1,5},{5,1},{2,6},{6,2},{3,7},{7,3},{8,12},{12,8},{9,1... | collective-permute-start | bytes 1572872 | tf_op jit(solution)/shard_map/ppermute | solution.py:51
  654.0 32.2 %collective-permute-start.71 = (f32[1,128,1024]{1,2,0:T(8,128)}, f32[1,128,1024]{1,2,0:T(8,128)}, u32[]{:S(2)}, u32[]{:S(2)}) collective-permute-start(f32[1,128,1024]{1,2,0:T(8,128)} %bitcast.368), channel_id=1, source_target_pairs={{0,5},{1,4},{4,1},{5,0},{2,7},{3,6},{6,3},{7,2},{8,13},{9,12},{12,... | collective-permute-start | bytes 1572872 | tf_op jit(solution)/shard_map/ppermute | solution.py:55
  711.7 37.9 %collective-permute-start.80 = (bf16[1,64,1536]{2,1,0:T(8,128)(2,1)S(1)}, bf16[1,64,1536]{2,1,0:T(8,128)(2,1)S(1)}, u32[]{:S(2)}, u32[]{:S(2)}) collective-permute-start(bf16[1,64,1536]{2,1,0:T(8,128)(2,1)S(1)} %get-tuple-element.115), channel_id=1, source_target_pairs={{0,1},{1,0},{2,3},{3,2},{4,5},{5,4},{6,7},{7,6},{8,9},{9,8},{10,11... | collective-permute-start | bytes 589832 | tf_op jit(solution)/shard_map/ppermute | solution.py:51
  747.5 88.0 %collective-permute-start.79 = (bf16[1,64,1536]{2,1,0:T(8,128)(2,1)}, bf16[1,64,1536]{2,1,0:T(8,128)(2,1)}, u32[]{:S(2)}, u32[]{:S(2)}) collective-permute-start(bf16[1,64,1536]{2,1,0:T(8,128)(2,1)} %get-tuple-element.117), channel_id=1, source_target_pairs={{0,5},{1,4},{4,1},{5,0},{2,7},{3,6},{6,3},{7,2},{8,13},{9,12},{12,... | collective-permute-start | bytes 589832 | tf_op jit(solution)/shard_map/ppermute | solution.py:55
  834.1 93.4 %collective-permute-start.83 = (bf16[1,64,2048]{2,1,0:T(8,128)(2,1)}, bf16[1,64,2048]{2,1,0:T(8,128)(2,1)}, u32[]{:S(2)}, u32[]{:S(2)}) collective-permute-start(bf16[1,64,2048]{2,1,0:T(8,128)(2,1)} %get-tuple-element.102), channel_id=1, source_target_pairs={{0,1},{1,0},{2,3},{3,2},{4,5},{5,4},{6,7},{7,6},{8,9},{9,8},{10,11... | collective-permute-start | bytes 786440 | tf_op jit(solution)/shard_map/ppermute | solution.py:51
  845.4 99.8 %collective-permute-start.84 = (bf16[1,64,2048]{2,1,0:T(8,128)(2,1)}, bf16[1,64,2048]{2,1,0:T(8,128)(2,1)}, u32[]{:S(2)}, u32[]{:S(2)}) collective-permute-start(bf16[1,64,2048]{2,1,0:T(8,128)(2,1)} %get-tuple-element.101), channel_id=1, source_target_pairs={{0,4},{4,0},{1,5},{5,1},{2,6},{6,2},{3,7},{7,3},{8,12},{12,8},{9,1... | collective-permute-start | bytes 786440 | tf_op jit(solution)/shard_map/ppermute | solution.py:51
  846.9 100.4 %collective-permute-start.85 = (bf16[1,64,2048]{2,1,0:T(8,128)(2,1)}, bf16[1,64,2048]{2,1,0:T(8,128)(2,1)}, u32[]{:S(2)}, u32[]{:S(2)}) collective-permute-start(bf16[1,64,2048]{2,1,0:T(8,128)(2,1)} %get-tuple-element.100), channel_id=1, source_target_pairs={{0,5},{1,4},{4,1},{5,0},{2,7},{3,6},{6,3},{7,2},{8,13},{9,12},{12,... | collective-permute-start | bytes 786440 | tf_op jit(solution)/shard_map/ppermute | solution.py:55
  924.5 51.5 %collective-permute-start.86 = (bf16[1,64,2048]{2,1,0:T(8,128)(2,1)}, bf16[1,64,2048]{2,1,0:T(8,128)(2,1)}, u32[]{:S(2)}, u32[]{:S(2)}) collective-permute-start(bf16[1,64,2048]{2,1,0:T(8,128)(2,1)} %get-tuple-element.98), channel_id=1, source_target_pairs={{0,1},{1,0},{2,3},{3,2},{4,5},{5,4},{6,7},{7,6},{8,9},{9,8},{10,11... | collective-permute-start | bytes 786440 | tf_op jit(solution)/shard_map/ppermute | solution.py:51
  926.0 51.4 %collective-permute-start.87 = (bf16[1,64,2048]{2,1,0:T(8,128)(2,1)}, bf16[1,64,2048]{2,1,0:T(8,128)(2,1)}, u32[]{:S(2)}, u32[]{:S(2)}) collective-permute-start(bf16[1,64,2048]{2,1,0:T(8,128)(2,1)} %get-tuple-element.97), channel_id=1, source_target_pairs={{0,4},{4,0},{1,5},{5,1},{2,6},{6,2},{3,7},{7,3},{8,12},{12,8},{9,1... | collective-permute-start | bytes 786440 | tf_op jit(solution)/shard_map/ppermute | solution.py:51
  927.4 51.3 %collective-permute-start.88 = (bf16[1,64,2048]{2,1,0:T(8,128)(2,1)}, bf16[1,64,2048]{2,1,0:T(8,128)(2,1)}, u32[]{:S(2)}, u32[]{:S(2)}) collective-permute-start(bf16[1,64,2048]{2,1,0:T(8,128)(2,1)} %get-tuple-element.96), channel_id=1, source_target_pairs={{0,5},{1,4},{4,1},{5,0},{2,7},{3,6},{6,3},{7,2},{8,13},{9,12},{12,... | collective-permute-start | bytes 786440 | tf_op jit(solution)/shard_map/ppermute | solution.py:55
  (158 other events, 2236.6 us)
Sparse Core Ops, SparseCore 0:
  26.1 66.1 all-gather.4
  94.5 63.3 all-gather.6
  160.1 86.2 all-gather.8
  247.9 81.2 all-gather.10
  541.0 57.4 all-reduce.3
  600.8 68.7 reduce-scatter.6
  672.0 69.5 reduce-scatter.4
  744.0 87.9 reduce-scatter.8
  834.4 87.9 reduce-scatter.10

commit v2 on v1

v2 whole, which is shorter than its diff:
```python
import math

import jax
import jax.numpy as jnp
from jax import lax
from jax.experimental import pallas as pl
from jax.experimental.pallas import tpu as pltpu
from jax.sharding import Mesh
from jax.sharding import PartitionSpec as P

HD = 128
EPS = 1e-05
BF = jnp.bfloat16
F32 = jnp.float32
PAIR = ((0, 1), (1, 0))
DIAG = ((0, 3), (1, 2), (2, 1), (3, 0))
DATA = ("z", "c")
VMEM = 40 * 1024 * 1024


def dot(a, b, dims):
    return lax.dot_general(a, b, (dims, ((), ())), preferred_element_type=F32)


def mm(a, b):
    return dot(a, b, ((1,), (0,)))


def mm_t(a, b):
    return dot(a, b, ((1,), (1,)))


def t_mm(a, b):
    return dot(a, b, ((0,), (0,)))


def normalize(values):
    centred = values - jnp.mean(values, axis=-1, keepdims=True)
    inv_std = lax.rsqrt(jnp.mean(centred * centred, axis=-1, keepdims=True) + EPS)
    return centred * inv_std, inv_std


def norm_back(grad_normed, normed, inv_std, gain):
    scaled = grad_normed * gain
    first_mean = jnp.mean(scaled, axis=-1, keepdims=True)
    second_mean = jnp.mean(scaled * normed, axis=-1, keepdims=True)
    return (
        inv_std * (scaled - first_mean - normed * second_mean),
        jnp.sum(grad_normed * normed, axis=0),
    )


def swap(values, axis):
    return lax.ppermute(values, axis, PAIR)


def swap_diag(values):
    return lax.ppermute(values, ("x", "y"), DIAG)


def gather_tokens(own):
    half = own.shape[0] // 2
    from_x = swap(own, "x")
    from_y = swap(own, "y")
    diag_low = swap(from_x[:half], "y")
    diag_high = swap(from_y[half:], "x")
    return jnp.concatenate([own, from_y, from_x, diag_low, diag_high], axis=0)


def scatter_tokens(partial):
    rows = partial.shape[0] // 4
    half = rows // 2
    own, for_y, for_x, for_diag = (partial[k * rows : (k + 1) * rows] for k in range(4))
    for_diag = for_diag.astype(BF)
    diag_low = swap(for_diag[:half], "y").astype(F32)
    diag_high = swap(for_diag[half:], "x").astype(F32)
    from_x = swap(
        jnp.concatenate([for_x[:half] + diag_low, for_x[half:]], axis=0).astype(BF), "x"
    )
    from_y = swap(
        jnp.concatenate([for_y[:half], for_y[half:] + diag_high], axis=0).astype(BF), "y"
    )
    return own + from_x.astype(F32) + from_y.astype(F32)


def swap_all(parts):
    return [parts[0], swap(parts[1], "y"), swap(parts[2], "x"), swap_diag(parts[3])]


def pieces(values, rank, width):
    return [
        lax.dynamic_slice_in_dim(values, (rank ^ k) * width, width, 1) for k in range(4)
    ]


def grid_spec(in_specs, out_specs):
    return pltpu.PrefetchScalarGridSpec(
        num_scalar_prefetch=1, grid=(4,), in_specs=in_specs, out_specs=out_specs
    )


def pack(weights, rank):
    rows = weights[0].shape[0]
    widths = [w.shape[1] // 4 for w in weights]
    total = sum(widths)

    def kernel(rank_ref, *refs):
        step = pl.program_id(0)
        for k in range(4):

            @pl.when(step == k)
            def _():
                offset = 0
                for ref, width in zip(refs, widths):
                    refs[len(widths) + k][:, offset : offset + width] = ref[...]
                    offset += width

    return pl.pallas_call(
        kernel,
        out_shape=[jax.ShapeDtypeStruct((rows, total), BF)] * 4,
        grid_spec=grid_spec(
            [pl.BlockSpec((rows, w), lambda k, r: (0, k ^ r[0])) for w in widths],
            [pl.BlockSpec((rows, total), lambda k, r: (0, 0))] * 4,
        ),
        compiler_params=pltpu.CompilerParams(vmem_limit_bytes=VMEM),
        name="pack",
    )(rank.reshape(1), *weights)


def place(parts, rank, widths):
    rows, total = parts[0].shape

    def kernel(rank_ref, *refs):
        step = pl.program_id(0)
        for k in range(4):

            @pl.when(step == k)
            def _():
                offset = 0
                for ref, width in zip(refs[4:], widths):
                    ref[...] = refs[k][:, offset : offset + width]
                    offset += width

    return pl.pallas_call(
        kernel,
        out_shape=[jax.ShapeDtypeStruct((4 * rows, w), BF) for w in widths],
        grid_spec=grid_spec(
            [pl.BlockSpec((rows, total), lambda k, r: (0, 0))] * 4,
            [pl.BlockSpec((rows, w), lambda k, r: (k ^ r[0], 0)) for w in widths],
        ),
        compiler_params=pltpu.CompilerParams(vmem_limit_bytes=VMEM),
        name="place",
    )(rank.reshape(1), *parts)


def finish(parts, rank, widths):
    rows, total = parts[0].shape

    def kernel(rank_ref, *refs):
        step = pl.program_id(0)
        for k in range(4):

            @pl.when(step == k)
            def _():
                offset = 0
                for ref, width in zip(refs[4:], widths):
                    ref[...] = refs[k][:, offset : offset + width].astype(F32)
                    offset += width

    return pl.pallas_call(
        kernel,
        out_shape=[jax.ShapeDtypeStruct((rows, 4 * w), F32) for w in widths],
        grid_spec=grid_spec(
            [pl.BlockSpec((rows, total), lambda k, r: (0, 0))] * 4,
            [pl.BlockSpec((rows, w), lambda k, r: (0, k ^ r[0])) for w in widths],
        ),
        compiler_params=pltpu.CompilerParams(vmem_limit_bytes=VMEM),
        name="finish",
    )(rank.reshape(1), *parts)


def finish_three(parts, rank):
    rows, total = parts[0].shape
    width = total // 3

    def kernel(rank_ref, *refs):
        step = pl.program_id(0)
        for k in range(4):

            @pl.when(step == k)
            def _():
                for j in range(3):
                    refs[4][:, j, :] = refs[k][:, j * width : (j + 1) * width].astype(F32)

    return pl.pallas_call(
        kernel,
        out_shape=jax.ShapeDtypeStruct((rows, 3, 4 * width), F32),
        grid_spec=grid_spec(
            [pl.BlockSpec((rows, total), lambda k, r: (0, 0))] * 4,
            pl.BlockSpec((rows, 3, width), lambda k, r: (0, 0, k ^ r[0])),
        ),
        compiler_params=pltpu.CompilerParams(vmem_limit_bytes=VMEM),
        name="finish_three",
    )(rank.reshape(1), *parts)


def softmax(scores):
    exp_terms = jnp.exp(scores - jnp.max(scores, axis=-1, keepdims=True))
    return exp_terms / jnp.sum(exp_terms, axis=-1, keepdims=True)


def score_grad(probs, grad_probs):
    return (
        probs * (grad_probs - jnp.sum(probs * grad_probs, axis=-1, keepdims=True))
    ).astype(BF)


def head(ref, k):
    return ref[:, k * HD : (k + 1) * HD]


def kernel_call(kernel, out_shape, grid, in_specs, out_specs, flops, name):
    return pl.pallas_call(
        kernel,
        out_shape=out_shape,
        grid=grid,
        in_specs=in_specs,
        out_specs=out_specs,
        compiler_params=pltpu.CompilerParams(vmem_limit_bytes=VMEM),
        cost_estimate=pl.CostEstimate(flops=flops, bytes_accessed=1 << 22, transcendentals=0),
        name=name,
    )


def self_forward(projected, images):
    tokens, width = projected.shape
    rows, group = tokens // images, width // 3
    heads = group // HD
    scale = 1.0 / math.sqrt(HD)

    def kernel(proj, mixed):
        for k in range(heads):
            query, key, value = (head(proj, j * heads + k) for j in range(3))
            probs = softmax(mm_t(query, key) * scale).astype(BF)
            mixed[:, k * HD : (k + 1) * HD] = mm(probs, value).astype(BF)

    return kernel_call(
        kernel,
        jax.ShapeDtypeStruct((tokens, group), BF),
        (images,),
        [pl.BlockSpec((rows, width), lambda i: (i, 0))],
        pl.BlockSpec((rows, group), lambda i: (i, 0)),
        4 * tokens * rows * group,
        "self_forward",
    )(projected)


def self_back(projected, grad_mixed, images):
    tokens, width = projected.shape
    rows, group = tokens // images, width // 3
    heads = group // HD
    scale = 1.0 / math.sqrt(HD)

    def kernel(proj, grad, out):
        for k in range(heads):
            query, key, value = (head(proj, j * heads + k) for j in range(3))
            grad_head = head(grad, k)
            probs = softmax(mm_t(query, key) * scale)
            grad_scores = score_grad(probs, mm_t(grad_head, value))
            parts = (
                mm(grad_scores, key) * scale,
                t_mm(grad_scores, query) * scale,
                t_mm(probs.astype(BF), grad_head),
            )
            for j, part in enumerate(parts):
                at = (j * heads + k) * HD
                out[:, at : at + HD] = part.astype(BF)

    return kernel_call(
        kernel,
        jax.ShapeDtypeStruct((tokens, width), BF),
        (images,),
        [
            pl.BlockSpec((rows, width), lambda i: (i, 0)),
            pl.BlockSpec((rows, group), lambda i: (i, 0)),
        ],
        pl.BlockSpec((rows, width), lambda i: (i, 0)),
        10 * tokens * rows * group,
        "self_back",
    )(projected, grad_mixed)


def cross_forward(queries, text_kv):
    tokens, group = queries.shape
    context = text_kv.shape[0]
    heads = group // HD
    scale = 1.0 / math.sqrt(HD)

    def kernel(query, text, mixed):
        for k in range(heads):
            probs = softmax(mm_t(head(query, k), head(text, k)) * scale).astype(BF)
            mixed[:, k * HD : (k + 1) * HD] = mm(probs, head(text, heads + k)).astype(BF)

    return kernel_call(
        kernel,
        jax.ShapeDtypeStruct((tokens, group), BF),
        (1,),
        [
            pl.BlockSpec((tokens, group), lambda i: (0, 0)),
            pl.BlockSpec((context, 2 * group), lambda i: (0, 0)),
        ],
        pl.BlockSpec((tokens, group), lambda i: (0, 0)),
        4 * tokens * context * group,
        "cross_forward",
    )(queries, text_kv)


def cross_back(queries, text_kv, grad_mixed):
    tokens, group = queries.shape
    context = text_kv.shape[0]
    heads = group // HD
    scale = 1.0 / math.sqrt(HD)

    def kernel(query, text, grad, grad_query, grad_text):
        for k in range(heads):
            query_head, key, value = head(query, k), head(text, k), head(text, heads + k)
            grad_head = head(grad, k)
            probs = softmax(mm_t(query_head, key) * scale)
            grad_scores = score_grad(probs, mm_t(grad_head, value))
            grad_query[:, k * HD : (k + 1) * HD] = (mm(grad_scores, key) * scale).astype(BF)
            at = (heads + k) * HD
            grad_text[:, k * HD : (k + 1) * HD] = t_mm(grad_scores, query_head) * scale
            grad_text[:, at : at + HD] = t_mm(probs.astype(BF), grad_head)

    return kernel_call(
        kernel,
        [
            jax.ShapeDtypeStruct((tokens, group), BF),
            jax.ShapeDtypeStruct((context, 2 * group), F32),
        ],
        (1,),
        [
            pl.BlockSpec((tokens, group), lambda i: (0, 0)),
            pl.BlockSpec((context, 2 * group), lambda i: (0, 0)),
            pl.BlockSpec((tokens, group), lambda i: (0, 0)),
        ],
        [
            pl.BlockSpec((tokens, group), lambda i: (0, 0)),
            pl.BlockSpec((context, 2 * group), lambda i: (0, 0)),
        ],
        10 * tokens * context * group,
        "cross_back",
    )(queries, text_kv, grad_mixed)


def gather_rows(rows):
    return lax.all_gather(rows, DATA, axis=0, tiled=True)


def scatter_grad(partial):
    summed = lax.psum_scatter(partial, DATA, scatter_dimension=0, tiled=True)
    return summed.reshape(4, -1, summed.shape[-1])


def send_rows(blocks, rank):
    return swap_all(
        [lax.dynamic_index_in_dim(blocks, rank ^ k, 0, keepdims=False) for k in range(4)]
    )


def make_local(z_size):
    def sum_data(values):
        values = values + swap(values, "c")
        step = 1
        while step < z_size:
            sent = values.astype(BF)
            got = lax.ppermute(sent, "z", tuple((k, k ^ step) for k in range(z_size)))
            values = sent.astype(F32) + got.astype(F32)
            step *= 2
        return values

    def sum_all(values):
        for axis in ("c", "x", "y"):
            values = values + swap(values, axis)
        step = 1
        while step < z_size:
            values = values + lax.ppermute(
                values, "z", tuple((k, k ^ step) for k in range(z_size))
            )
            step *= 2
        return values

    def feature_swap(values):
        lead = values.shape[:-1]
        shaped = values.reshape(lead + (z_size, 2, 2, -1))
        return jnp.swapaxes(shaped, -3, -2).reshape(values.shape)

    def local(
        hidden,
        mask_index,
        mask_count,
        mask_embed,
        norm_gains,
        caption,
        w_qkv,
        w_out,
        w_cross,
        w_cross_out,
        w_text,
        w_up,
        w_down,
        cotangent,
    ):
        images, local_rows, width = hidden.shape
        full_length = mask_index.shape[1]
        shard_rows = w_qkv.shape[0]
        rank = lax.axis_index("x") * 2 + lax.axis_index("y")
        tokens = images * local_rows
        group = width // 4
        hidden_group = w_up.shape[1] // 4

        qkv_rows = w_qkv.reshape(shard_rows, 3 * width)
        qkv_parts = [
            pieces(qkv_rows[:, j * width : (j + 1) * width], rank, group) for j in range(3)
        ]
        qkv_parts = swap_all(
            [jnp.concatenate([part[k] for part in qkv_parts], axis=1) for k in range(4)]
        )
        qkv = gather_rows(place(qkv_parts, rank, [3 * group])[0])

        positions = lax.axis_index("y") * local_rows + jnp.arange(local_rows, dtype=jnp.int32)
        ranks = jnp.arange(full_length, dtype=jnp.int32)
        matches = (mask_index[:, :, None] == positions[None, None, :]) & (
            ranks[None, :, None] < mask_count[:, None, None]
        )
        masked = jnp.any(matches, axis=1).reshape(tokens, 1)
        gains = feature_swap(norm_gains)
        start_x = jnp.where(
            masked,
            feature_swap(mask_embed),
            feature_swap(hidden.reshape(tokens, width)).astype(F32),
        )
        grad_top = feature_swap(cotangent.reshape(tokens, width)).astype(F32) * masked.astype(F32)
        normed_a, inv_a = normalize(start_x)
        attn_in = gather_tokens((normed_a * gains[0]).astype(BF))

        rest = pack([w_out, w_cross[:, 0], w_cross_out, w_up, w_down], rank)
        mid, up, down = place(swap_all(rest), rank, [3 * group, hidden_group, hidden_group])
        mid = gather_rows(mid)
        up = gather_rows(up)
        down = gather_rows(down)
        out_w, query_w, cross_out_w = (mid[:, k * group : (k + 1) * group] for k in range(3))

        own_text = mm_t(caption, w_text).astype(BF)
        kv_rows = w_cross[:, 1:].reshape(shard_rows, 2 * width)
        kv_part = mm(own_text, kv_rows).astype(BF)
        kv_parts = [pieces(kv_part[:, j * width : (j + 1) * width], rank, group) for j in range(2)]
        kv_parts = swap_all(
            [jnp.concatenate([part[k] for part in kv_parts], axis=1) for k in range(4)]
        )
        text_kv = sum_data(sum(part.astype(F32) for part in kv_parts)).astype(BF)
        grad_y = gather_tokens(grad_top.astype(BF))

        projected = mm(attn_in, qkv).astype(BF)
        self_mixed = self_forward(projected, 2 * images)
        after_attn = start_x + scatter_tokens(mm_t(self_mixed, out_w))

        normed_b, inv_b = normalize(after_attn)
        cross_in = gather_tokens((normed_b * gains[1]).astype(BF))
        cross_queries = mm(cross_in, query_w).astype(BF)
        cross_mixed = cross_forward(cross_queries, text_kv)
        after_cross = after_attn + scatter_tokens(mm_t(cross_mixed, cross_out_w))

        normed_c, inv_c = normalize(after_cross)
        mlp_in = gather_tokens((normed_c * gains[2]).astype(BF))
        pre_act = mm(mlp_in, up)
        activated, gelu_pull = jax.vjp(jax.nn.gelu, pre_act)
        activated = activated.astype(BF)
        down_part = t_mm(grad_y, activated).astype(BF)
        grad_pre = gelu_pull(mm(grad_y, down))[0].astype(BF)
        grad_pre, down_part = lax.optimization_barrier((grad_pre, down_part))
        up_part = t_mm(mlp_in, grad_pre).astype(BF)
        back_part = mm_t(grad_pre, up)
        back_part, up_part = lax.optimization_barrier((back_part, up_part))
        down_rows = scatter_grad(down_part)
        up_rows = scatter_grad(up_part)
        grad_mlp_in = scatter_tokens(back_part)
        result = after_cross + scatter_tokens(mm_t(activated, down))
        output = feature_swap(result.astype(BF))
        back_c, gain_grad_c = norm_back(grad_mlp_in, normed_c, inv_c, gains[2])
        grad_after_cross = grad_top + back_c

        cross_branch = gather_tokens(grad_after_cross.astype(BF))
        grad_cross_mixed = mm(cross_branch, cross_out_w).astype(BF)
        grad_cq, kv_grad = cross_back(cross_queries, text_kv, grad_cross_mixed)
        grad_cross_in = scatter_tokens(mm_t(grad_cq, query_w))
        back_b, gain_grad_b = norm_back(grad_cross_in, normed_b, inv_b, gains[1])
        grad_after_attn = grad_after_cross + back_b

        attn_branch = gather_tokens(grad_after_attn.astype(BF))
        mid_part = jnp.concatenate(
            [
                t_mm(attn_branch, self_mixed).astype(BF),
                t_mm(cross_in, grad_cq).astype(BF),
                t_mm(cross_branch, cross_mixed).astype(BF),
            ],
            axis=1,
        )
        grad_self_mixed = mm(attn_branch, out_w).astype(BF)
        grad_self_mixed, mid_part = lax.optimization_barrier((grad_self_mixed, mid_part))
        mid_rows = scatter_grad(mid_part)
        grad_projected = self_back(projected, grad_self_mixed, 2 * images)
        qkv_part = t_mm(attn_in, grad_projected).astype(BF)
        grad_projected, qkv_part = lax.optimization_barrier((grad_projected, qkv_part))
        qkv_rows = scatter_grad(qkv_part)
        grad_attn_in = scatter_tokens(mm_t(grad_projected, qkv))
        back_a, gain_grad_a = norm_back(grad_attn_in, normed_a, inv_a, gains[0])
        grad_start = grad_after_attn + back_a

        kv_grad = sum_data(kv_grad).astype(BF)
        kv_grads = place(swap_all([kv_grad] * 4), rank, [group, group])
        kv_grads = [
            part.reshape(4, -1, group).transpose(1, 0, 2).reshape(-1, width) for part in kv_grads
        ]
        kv_grads = jnp.concatenate(kv_grads, axis=1)
        kv_weight_grad = t_mm(own_text, kv_grads).reshape(shard_rows, 2, width)
        grad_text = mm_t(kv_grads, kv_rows).astype(BF)
        grad_text_w = t_mm(grad_text, caption)
        caption_part = mm(grad_text, w_text).astype(BF)
        caption_parts = swap_all(pieces(caption_part, rank, caption.shape[1] // 4))
        caption_own = sum_data(sum(part.astype(F32) for part in caption_parts)).astype(BF)
        grad_caption = finish(swap_all([caption_own] * 4), rank, [caption_own.shape[1]])[0]

        down_grad, up_grad = (
            finish(send_rows(rows, rank), rank, [hidden_group])[0] for rows in (down_rows, up_rows)
        )
        out_grad, query_grad, cross_out_grad = finish(
            send_rows(mid_rows, rank), rank, [group] * 3
        )
        qkv_grad = finish_three(send_rows(qkv_rows, rank), rank)
        grad_hidden = feature_swap(jnp.where(masked, 0.0, grad_start).astype(BF))
        mask_part = jnp.sum(jnp.where(masked, grad_start, 0.0), axis=0)
        sums = feature_swap(
            sum_all(jnp.stack([gain_grad_a, gain_grad_b, gain_grad_c, mask_part]))
        )
        grad_cross = jnp.concatenate([query_grad[:, None], kv_weight_grad], axis=1)
        return (
            output.reshape(hidden.shape),
            grad_hidden.reshape(hidden.shape),
            grad_caption,
            sums[:3],
            sums[3],
            qkv_grad,
            out_grad,
            grad_cross,
            cross_out_grad,
            grad_text_w,
            up_grad,
            down_grad,
        )

    return local


def solution(mesh):
    z_size = mesh.shape["img"] // 4
    inner = Mesh(mesh.devices.reshape(z_size, 2, 2, 2), ("z", "x", "c", "y"))
    tokens = P(("z", "x", "c"), "y", None)
    rows = P(("z", "x", "c", "y"))
    in_specs = (
        tokens,
        P(("z", "x", "c"), None),
        P(("z", "x", "c")),
        P(),
        P(),
        P(),
        rows,
        rows,
        rows,
        rows,
        rows,
        rows,
        rows,
        tokens,
    )
    out_specs = (tokens, tokens, P(), P(), P()) + (rows,) * 7
    return jax.shard_map(
        make_local(z_size), mesh=inner, in_specs=in_specs, out_specs=out_specs, check_vma=False
    )
```

time: 1020 us -> 880 us (0.86)
  local copies, waits for them, and re-layouts: 252 us -> 66.6 us
  waiting for transfers between devices: 372 us -> 523 us
  blocking collectives: 75.1 us -> 0 us
  matrix products: 136 us -> 100 us
  Pallas kernels: 0 us -> 25 us
    ppermute x0 -> x6, waiting for transfers between devices: none -> 92.9 us  [sum_data(): got = lax.ppermute(sent, 'z', tuple(((k, k ^ step) for k in range(z_size))))]
    dynamic_update_slice x44 -> x0, local copies, waits for them, and re-layouts: 86.9 us -> none  [exchange(): out = lax.dynamic_update_slice_in_dim(out, part, rank ^ k, 0)]
    psum x2 -> x0, blocking collectives: 75.1 us -> none  [the longest x1 39.4 us: local(): text_kv = lax.psum(kv_part, DATA).astype(BF)]
    ppermute x75 -> x74, waiting for transfers between devices: 154 us -> 202 us  [swap(): return lax.ppermute(values, axis, PAIR)]
    reshape x30 -> x4, local copies, waits for them, and re-layouts: 35.6 us -> 5.5 us  [the longest x2 3.16 us: local(): part.reshape(4, -1, group).transpose(1, 0, 2).reshape(-1, width)]
    pallas_call x0 -> x13, Pallas kernels: none -> 25 us  [the longest x4 8.31 us: finish(): pl.pallas_call(kernel, out_shape=[jax.ShapeDtypeStruct((rows, 4 * w), F32...]
    convert_element_type x12 -> x0, local copies, waits for them, and re-layouts: 24 us -> none  [the longest x3 8.21 us: local(): qkv_grad = join_columns(grad_rows(t_mm(attn_in, grad_projected).astype(BF...]
    all_gather x4, waiting for transfers between devices: 34.9 us -> 56.2 us  [gather_rows(): return lax.all_gather(rows, DATA, axis=0, tiled=True)]
  transfers between devices with their start and end apart: 98 -> 100, of which waited for: 52 -> 64; matrix products, arithmetic and copies ran while one was open for 37% -> 19% of each run, Pallas kernels for 0% -> 2%
where the time goes in v2:
time: 880 us; the launch traced here: 871 us
  waiting for transfers between devices  523 us (59%)
  matrix products  100 us (11%)
  starting transfers between devices  98.4 us (11%)
  local copies, waits for them, and re-layouts  66.6 us (8%)
  other arithmetic  40.6 us (5%)
  Pallas kernels  25 us (3%)
  between operations  16.7 us (2%)
    ppermute x74, waiting for transfers between devices, swap(): return lax.ppermute(values, axis, PAIR)  202 us
    reduce_scatter x4, waiting for transfers between devices, scatter_grad(): summed = lax.psum_scatter(partial, DATA, scatter_dimension=0, tiled=True)  139 us
    dot_general x24, matrix products, dot(): return lax.dot_general(a, b, (dims, ((), ())), preferred_element_type=F32)  100 us
    ppermute x6, waiting for transfers between devices, sum_data(): got = lax.ppermute(sent, 'z', tuple(((k, k ^ step) for k in range(z_size))))  92.9 us
    ppermute x74, starting transfers between devices, swap(): return lax.ppermute(values, axis, PAIR)  73.5 us
    all_gather x4, waiting for transfers between devices, gather_rows(): return lax.all_gather(rows, DATA, axis=0, tiled=True)  56.2 us
    ppermute x10, waiting for transfers between devices, swap_diag(): return lax.ppermute(values, ('x', 'y'), DIAG)  25.1 us
    ppermute x10, starting transfers between devices, swap_diag(): return lax.ppermute(values, ('x', 'y'), DIAG)  17.8 us
  transfers between devices with their start and end apart: 100, of which 64 were waited for; matrix products, arithmetic and copies ran while one was open for 19% of the time, Pallas kernels for 2%

profile of v2, /device:TPU:0, one launch (start us, length us, event | category | flops | bytes accessed | tf_op | source)
XLA Modules:
  0.0 870.7 jit_solution(780320795880056362)
XLA Ops:
  30.0 14.7 %collective-permute-done.7.refs_1_ = bf16[64,5632]{1,0:T(8,128)(2,1)S(1)} collective-permute-done((bf16[64,5632]{1,0:T(8,128)(2,1)S(1)}, bf16[64,5632]{1,0:T(8,128)(2,1)S(1)}, u32[]{:S(2)}, u32[]{:S(2)}) %collective-permute-start.7) | collective-permute-done | bytes 720928 | tf_op jit(solution)/shard_map/ppermute | solution.py:54
  47.3 12.8 %collective-permute-done.9.refs_3_ = bf16[64,5632]{1,0:T(8,128)(2,1)S(1)} collective-permute-done((bf16[64,5632]{1,0:T(8,128)(2,1)S(1)}, bf16[64,5632]{1,0:T(8,128)(2,1)S(1)}, u32[]{:S(2)}, u32[]{:S(2)}) %collective-permute-start.9) | collective-permute-done | bytes 720928 | tf_op jit(solution)/shard_map/ppermute | solution.py:58
  92.6 9.8 %collective-permute-done.2 = bf16[64,2048]{1,0:T(8,128)(2,1)S(1)} collective-permute-done((bf16[64,2048]{1,0:T(8,128)(2,1)S(1)}, bf16[64,2048]{1,0:T(8,128)(2,1)S(1)}, u32[]{:S(2)}, u32[]{:S(2)}) %collective-permute-start.2) | collective-permute-done | bytes 262176 | tf_op jit(solution)/shard_map/ppermute | solution.py:54
  113.2 42.5 %all-gather.7.cloned.1.call-done = bf16[2048,1536]{1,0:T(8,128)(2,1)} async-done(((bf16[256,1536]{1,0:T(8,128)(2,1)}), bf16[2048,1536]{1,0:T(8,128)(2,1)}) %all-gather.7.cloned.1.call-update) | async-done | bytes 6291472 | tf_op jit(solution)/shard_map/all_gather | solution.py:357
  170.9 10.7 %collective-permute-done.13 = bf16[128,2048]{1,0:T(8,128)(2,1)S(1)} collective-permute-done((bf16[128,2048]{1,0:T(8,128)(2,1)S(1)}, bf16[128,2048]{1,0:T(8,128)(2,1)S(1)}, u32[]{:S(2)}, u32[]{:S(2)}) %collective-permute-start.13) | collective-permute-done | bytes 524320 | tf_op jit(solution)/shard_map/ppermute | solution.py:54
  187.5 12.9 %collective-permute-done.22 = bf16[128,1024]{1,0:T(8,128)(2,1)S(1)} collective-permute-done((bf16[128,1024]{1,0:T(8,128)(2,1)S(1)}, bf16[128,1024]{1,0:T(8,128)(2,1)S(1)}, u32[]{:S(2)}, u32[]{:S(2)}) %collective-permute-start.22) | collective-permute-done | bytes 262176 | tf_op jit(solution)/shard_map/ppermute | solution.py:377
  209.4 22.4 %collective-permute-done.23 = bf16[128,1024]{1,0:T(8,128)(2,1)} collective-permute-done((bf16[128,1024]{1,0:T(8,128)(2,1)S(1)}, bf16[128,1024]{1,0:T(8,128)(2,1)}, u32[]{:S(2)}, u32[]{:S(2)}) %collective-permute-start.23) | collective-permute-done | bytes 262176 | tf_op jit(solution)/shard_map/ppermute | solution.py:377
  264.0 9.2 %collective-permute-done.37 = bf16[128,2048]{1,0:T(8,128)(2,1)S(1)} collective-permute-done((bf16[128,2048]{1,0:T(8,128)(2,1)S(1)}, bf16[128,2048]{1,0:T(8,128)(2,1)S(1)}, u32[]{:S(2)}, u32[]{:S(2)}) %collective-permute-start.37) | collective-permute-done | bytes 524320 | tf_op jit(solution)/shard_map/ppermute | solution.py:54
  275.0 8.6 collective-permute-done.27
  290.0 8.9 %collective-permute-done.29 = bf16[128,2048]{1,0:T(8,128)(2,1)S(1)} collective-permute-done((bf16[128,2048]{1,0:T(8,128)(2,1)S(1)}, bf16[128,2048]{1,0:T(8,128)(2,1)S(1)}, u32[]{:S(2)}, u32[]{:S(2)}) %collective-permute-start.29) | collective-permute-done | bytes 524320 | tf_op jit(solution)/shard_map/ppermute | solution.py:54
  307.6 11.1 %fusion.73 = f32[512,2048]{1,0:T(8,128)} fusion(bf16[512,2048]{1,0:T(8,128)(2,1)} %constant_dynamic-update-slice_fusion.10, bf16[2048,2048]{1,0:T(8,128)(2,1)} %all-gather.9.cloned.1.call-done), kind=kOutput, calls=%fused_computation.244 | convolution fusion | flops 4294967296 | bytes 14680064 | tf_op jit(solution)/shard_map/dot_general | solution.py:22
  318.7 13.7 %all-gather.11.cloned.1.call-done = bf16[2048,2048]{1,0:T(8,128)(2,1)} async-done(((bf16[256,2048]{1,0:T(8,128)(2,1)}), bf16[2048,2048]{1,0:T(8,128)(2,1)}) %all-gather.11.cloned.1.call-update) | async-done | bytes 8388624 | tf_op jit(solution)/shard_map/all_gather | solution.py:357
  332.4 11.6 %fusion.70 = (bf16[512,2048]{1,0:T(8,128)(2,1)S(1)}, f32[512,2048]{1,0:T(8,128)}) fusion(bf16[2048,2048]{1,0:T(8,128)(2,1)} %all-gather.11.cloned.1.call-done, f32[512,2048]{1,0:T(8,128)} %fusion.73), kind=kOutput, calls=%fused_computation.241 | convolution fusion | flops 4305453056 | bytes 18874368 | tf_op jit(solution)/shard_map/dot_general | solution.py:22
  355.2 11.7 %fusion.6 = bf16[512,2048]{1,0:T(8,128)(2,1)S(1)} fusion(f32[512,2048]{1,0:T(8,128)} %fusion.73, bf16[512,2048]{1,0:T(8,128)(2,1)} %copy-done.44, bf16[2048,2048]{1,0:T(8,128)(2,1)} %all-gather.11.cloned.1.call-done), kind=kOutput, calls=%fused_computation.14 | convolution fusion | flops 4315938816 | bytes 16777216 | tf_op jit(solution)/shard_map/dot_general | solution.py:22
  368.3 8.4 convolution_convert_fusion.1
  406.1 9.3 %collective-permute-done.43 = bf16[128,2048]{1,0:T(8,128)(2,1)S(1)} collective-permute-done((bf16[128,2048]{1,0:T(8,128)(2,1)S(1)}, bf16[128,2048]{1,0:T(8,128)(2,1)S(1)}, u32[]{:S(2)}, u32[]{:S(2)}) %collective-permute-start.43) | collective-permute-done | bytes 524320 | tf_op jit(solution)/shard_map/ppermute | solution.py:54
  419.8 10.3 %collective-permute-done.45 = bf16[128,2048]{1,0:T(8,128)(2,1)S(1)} collective-permute-done((bf16[128,2048]{1,0:T(8,128)(2,1)S(1)}, bf16[128,2048]{1,0:T(8,128)(2,1)S(1)}, u32[]{:S(2)}, u32[]{:S(2)}) %collective-permute-start.45) | collective-permute-done | bytes 524320 | tf_op jit(solution)/shard_map/ppermute | solution.py:54
  488.7 11.2 %pad_maximum_fusion = bf16[2048,1536]{0,1:T(8,128)(2,1)} fusion(bf16[2048,512]{0,1:T(8,128)(2,1)S(1)} %convolution_convert_fusion.5, bf16[2048,512]{0,1:T(8,128)(2,1)S(1)} %convolution_convert_fusion.6, bf16[2048,512]{0,1:T(8,128)(2,1)S(1)} %convolution_convert_fusion.7), kind=kLoop, calls=%fused_computation.3 | loop fusion | flops 18874368 | bytes 12582912 | tf_op jit(solution)/shard_map/concatenate | solution.py:501
  518.7 14.6 %collective-permute-done.61 = bf16[128,1024]{1,0:T(8,128)(2,1)S(1)} collective-permute-done((bf16[128,1024]{1,0:T(8,128)(2,1)S(1)}, bf16[128,1024]{1,0:T(8,128)(2,1)S(1)}, u32[]{:S(2)}, u32[]{:S(2)}) %collective-permute-start.61) | collective-permute-done | bytes 262176 | tf_op jit(solution)/shard_map/ppermute | solution.py:377
  534.2 24.9 %collective-permute-done.62 = bf16[128,1024]{1,0:T(8,128)(2,1)S(1)} collective-permute-done((bf16[128,1024]{1,0:T(8,128)(2,1)S(1)}, bf16[128,1024]{1,0:T(8,128)(2,1)S(1)}, u32[]{:S(2)}, u32[]{:S(2)}) %collective-permute-start.62) | collective-permute-done | bytes 262176 | tf_op jit(solution)/shard_map/ppermute | solution.py:377
  608.9 11.4 %collective-permute-done.66 = bf16[128,1024]{1,0:T(8,128)(2,1)} collective-permute-done((bf16[128,1024]{1,0:T(8,128)(2,1)}, bf16[128,1024]{1,0:T(8,128)(2,1)}, u32[]{:S(2)}, u32[]{:S(2)}) %collective-permute-start.66) | collective-permute-done | bytes 262176 | tf_op jit(solution)/shard_map/ppermute | solution.py:54
  629.4 12.4 %collective-permute-done.70 = bf16[128,1024]{1,0:T(8,128)(2,1)S(1)} collective-permute-done((bf16[128,1024]{1,0:T(8,128)(2,1)S(1)}, bf16[128,1024]{1,0:T(8,128)(2,1)S(1)}, u32[]{:S(2)}, u32[]{:S(2)}) %collective-permute-start.70) | collective-permute-done | bytes 262176 | tf_op jit(solution)/shard_map/ppermute | solution.py:377
  677.8 79.9 %reduce-scatter.11.cloned.1.call-done = bf16[256,2048]{1,0:T(8,128)(2,1)} async-done(((bf16[2048,2048]{1,0:T(8,128)(2,1)}), bf16[256,2048]{1,0:T(8,128)(2,1)}) %reduce-scatter.11.cloned.1.call-update) | async-done | bytes 1048592 | tf_op jit(solution)/shard_map/reduce_scatter | solution.py:361
  788.8 59.1 %reduce-scatter.9.cloned.1.call-done = bf16[256,2048]{1,0:T(8,128)(2,1)} async-done(((bf16[2048,2048]{1,0:T(8,128)(2,1)}), bf16[256,2048]{1,0:T(8,128)(2,1)}) %reduce-scatter.9.cloned.1.call-update) | async-done | bytes 1048592 | tf_op jit(solution)/shard_map/reduce_scatter | solution.py:361
  (509 shorter events, 411.9 us)
Async XLA Ops:
  7.2 96.6 %all-gather.5.cloned.1.call-start = ((), (), s32[]{:S(2)}) async-start(), calls=%async_computation.4 | async-start | bytes 7077888 | tf_op jit(solution)/shard_map/all_gather | solution.py:357
  23.7 132.0 %all-gather.7.cloned.1.call-start = ((), (), s32[]{:S(2)}) async-start(), calls=%async_computation.5 | async-start | bytes 7077888 | tf_op jit(solution)/shard_map/all_gather | solution.py:357
  62.3 245.3 %all-gather.9.cloned.1.call-start = ((), (), s32[]{:S(2)}) async-start(), calls=%async_computation.6 | async-start | bytes 9437184 | tf_op jit(solution)/shard_map/all_gather | solution.py:357
  63.0 269.4 %all-gather.11.cloned.1.call-start = ((), (), s32[]{:S(2)}) async-start(), calls=%async_computation.7 | async-start | bytes 9437184 | tf_op jit(solution)/shard_map/all_gather | solution.py:357
  78.2 83.5 %collective-permute-start.18 = (bf16[128,1024]{1,0:T(8,128)(2,1)}, bf16[128,1024]{1,0:T(8,128)(2,1)}, u32[]{:S(2)}, u32[]{:S(2)}) collective-permute-start(bf16[128,1024]{1,0:T(8,128)(2,1)} %pad_maximum_fusion.17), channel_id=1, source_target_pairs={{0,1},{1,0},{2,3},{3,2},{4,5},{5,4},{6,7},{7,6},{8,9},{9,8},{10,11... | collective-permute-start | bytes 786440 | tf_op jit(solution)/shard_map/ppermute | solution.py:54
  79.5 82.2 %collective-permute-start.19 = (bf16[128,1024]{1,0:T(8,128)(2,1)}, bf16[128,1024]{1,0:T(8,128)(2,1)}, u32[]{:S(2)}, u32[]{:S(2)}) collective-permute-start(bf16[128,1024]{1,0:T(8,128)(2,1)} %pad_maximum_fusion.18), channel_id=1, source_target_pairs={{0,4},{4,0},{1,5},{5,1},{2,6},{6,2},{3,7},{7,3},{8,12},{12,8},{9,1... | collective-permute-start | bytes 786440 | tf_op jit(solution)/shard_map/ppermute | solution.py:54
  80.8 80.9 %collective-permute-start.20 = (bf16[128,1024]{1,0:T(8,128)(2,1)}, bf16[128,1024]{1,0:T(8,128)(2,1)}, u32[]{:S(2)}, u32[]{:S(2)}) collective-permute-start(bf16[128,1024]{1,0:T(8,128)(2,1)} %pad_maximum_fusion.19), channel_id=1, source_target_pairs={{0,5},{1,4},{4,1},{5,0},{2,7},{3,6},{6,3},{7,2},{8,13},{9,12},{12,... | collective-permute-start | bytes 786440 | tf_op jit(solution)/shard_map/ppermute | solution.py:58
  92.5 575.8 %reduce-scatter.7.cloned.1.call-start = ((), (), s32[]{:S(2)}) async-start(), calls=%async_computation.9 | async-start | bytes 7077888 | tf_op jit(solution)/shard_map/reduce_scatter | solution.py:361
  184.6 48.4 %collective-permute-start.15 = (bf16[128,2048]{1,0:T(8,128)(2,1)}, bf16[128,2048]{1,0:T(8,128)(2,1)S(1)}, u32[]{:S(2)}, u32[]{:S(2)}) collective-permute-start(bf16[128,2048]{1,0:T(8,128)(2,1)} %get-tuple-element.131), channel_id=1, source_target_pairs={{0,4},{4,0},{1,5},{5,1},{2,6},{6,2},{3,7},{7,3},{8,12},{12,8},{9,1... | collective-permute-start | bytes 1572872 | tf_op jit(solution)/shard_map/ppermute | solution.py:54
  186.1 48.4 %collective-permute-start.14 = (bf16[128,2048]{1,0:T(8,128)(2,1)}, bf16[128,2048]{1,0:T(8,128)(2,1)}, u32[]{:S(2)}, u32[]{:S(2)}) collective-permute-start(bf16[128,2048]{1,0:T(8,128)(2,1)} %get-tuple-element.131), channel_id=1, source_target_pairs={{0,1},{1,0},{2,3},{3,2},{4,5},{5,4},{6,7},{7,6},{8,9},{9,8},{10,11... | collective-permute-start | bytes 1572872 | tf_op jit(solution)/shard_map/ppermute | solution.py:54
  200.5 31.4 %collective-permute-start.23 = (bf16[128,1024]{1,0:T(8,128)(2,1)S(1)}, bf16[128,1024]{1,0:T(8,128)(2,1)}, u32[]{:S(2)}, u32[]{:S(2)}) collective-permute-start(bf16[128,1024]{1,0:T(8,128)(2,1)S(1)} %add_convert_fusion.9), channel_id=1, source_target_pairs={{0,16},{8,24},{16,0},{24,8},{1,17},{9,25},{17,1},{25,9},{2,18},{10... | collective-permute-start | bytes 786440 | tf_op jit(solution)/shard_map/ppermute | solution.py:377
  345.0 41.2 %collective-permute-start.32 = (bf16[64,2048]{1,0:T(8,128)(2,1)}, bf16[64,2048]{1,0:T(8,128)(2,1)}, u32[]{:S(2)}, u32[]{:S(2)}) collective-permute-start(bf16[64,2048]{1,0:T(8,128)(2,1)} %get-tuple-element.162), channel_id=1, source_target_pairs={{0,1},{1,0},{2,3},{3,2},{4,5},{5,4},{6,7},{7,6},{8,9},{9,8},{10,11... | collective-permute-start | bytes 786440 | tf_op jit(solution)/shard_map/ppermute | solution.py:54
  346.5 39.6 %collective-permute-start.34 = (bf16[64,2048]{1,0:T(8,128)(2,1)}, bf16[64,2048]{1,0:T(8,128)(2,1)}, u32[]{:S(2)}, u32[]{:S(2)}) collective-permute-start(bf16[64,2048]{1,0:T(8,128)(2,1)} %get-tuple-element.163), channel_id=1, source_target_pairs={{0,4},{4,0},{1,5},{5,1},{2,6},{6,2},{3,7},{7,3},{8,12},{12,8},{9,1... | collective-permute-start | bytes 786440 | tf_op jit(solution)/shard_map/ppermute | solution.py:54
  503.4 169.3 %reduce-scatter.5.cloned.1.call-start = ((), (), s32[]{:S(2)}) async-start(), calls=%async_computation.8 | async-start | bytes 7077888 | tf_op jit(solution)/shard_map/reduce_scatter | solution.py:361
  514.8 242.9 %reduce-scatter.11.cloned.1.call-start = ((), (), s32[]{:S(2)}) async-start(), calls=%async_computation.11 | async-start | bytes 9437184 | tf_op jit(solution)/shard_map/reduce_scatter | solution.py:361
  515.6 332.4 %reduce-scatter.9.cloned.1.call-start = ((), (), s32[]{:S(2)}) async-start(), calls=%async_computation.10 | async-start | bytes 9437184 | tf_op jit(solution)/shard_map/reduce_scatter | solution.py:361
  664.6 95.1 %collective-permute-start.74 = (bf16[128,1024]{1,0:T(8,128)(2,1)S(1)}, bf16[128,1024]{1,0:T(8,128)(2,1)S(1)}, u32[]{:S(2)}, u32[]{:S(2)}) collective-permute-start(bf16[128,1024]{1,0:T(8,128)(2,1)S(1)} %add_convert_fusion.refs_0_), channel_id=1, source_target_pairs={{0,5},{1,4},{4,1},{5,0},{2,7},{3,6},{6,3},{7,2},{8,13},{9,12},{12,... | collective-permute-start | bytes 786440 | tf_op jit(solution)/shard_map/ppermute | solution.py:58
  667.7 94.4 %collective-permute-start.73 = (bf16[128,1024]{1,0:T(8,128)(2,1)S(1)}, bf16[128,1024]{1,0:T(8,128)(2,1)S(1)}, u32[]{:S(2)}, u32[]{:S(2)}) collective-permute-start(bf16[128,1024]{1,0:T(8,128)(2,1)S(1)} %add_convert_fusion.refs_0_), channel_id=1, source_target_pairs={{0,4},{4,0},{1,5},{5,1},{2,6},{6,2},{3,7},{7,3},{8,12},{12,8},{9,1... | collective-permute-start | bytes 786440 | tf_op jit(solution)/shard_map/ppermute | solution.py:54
  667.7 95.0 %collective-permute-start.72 = (bf16[128,1024]{1,0:T(8,128)(2,1)S(1)}, bf16[128,1024]{1,0:T(8,128)(2,1)S(1)}, u32[]{:S(2)}, u32[]{:S(2)}) collective-permute-start(bf16[128,1024]{1,0:T(8,128)(2,1)S(1)} %add_convert_fusion.refs_0_), channel_id=1, source_target_pairs={{0,1},{1,0},{2,3},{3,2},{4,5},{5,4},{6,7},{7,6},{8,9},{9,8},{10,11... | collective-permute-start | bytes 786440 | tf_op jit(solution)/shard_map/ppermute | solution.py:54
  674.8 88.4 %collective-permute-start.82 = (bf16[64,1536]{1,0:T(8,128)(2,1)}, bf16[64,1536]{1,0:T(8,128)(2,1)S(1)}, u32[]{:S(2)}, u32[]{:S(2)}) collective-permute-start(bf16[64,1536]{1,0:T(8,128)(2,1)} %get-tuple-element.192), channel_id=1, source_target_pairs={{0,5},{1,4},{4,1},{5,0},{2,7},{3,6},{6,3},{7,2},{8,13},{9,12},{12,... | collective-permute-start | bytes 589832 | tf_op jit(solution)/shard_map/ppermute | solution.py:58
  677.8 86.9 %collective-permute-start.81 = (bf16[64,1536]{1,0:T(8,128)(2,1)S(1)}, bf16[64,1536]{1,0:T(8,128)(2,1)S(1)}, u32[]{:S(2)}, u32[]{:S(2)}) collective-permute-start(bf16[64,1536]{1,0:T(8,128)(2,1)S(1)} %get-tuple-element.193), channel_id=1, source_target_pairs={{0,4},{4,0},{1,5},{5,1},{2,6},{6,2},{3,7},{7,3},{8,12},{12,8},{9,1... | collective-permute-start | bytes 589832 | tf_op jit(solution)/shard_map/ppermute | solution.py:54
  764.7 87.6 %collective-permute-start.91 = (bf16[64,2048]{1,0:T(8,128)(2,1)}, bf16[64,2048]{1,0:T(8,128)(2,1)S(1)}, u32[]{:S(2)}, u32[]{:S(2)}) collective-permute-start(bf16[64,2048]{1,0:T(8,128)(2,1)} %get-tuple-element.174), channel_id=1, source_target_pairs={{0,5},{1,4},{4,1},{5,0},{2,7},{3,6},{6,3},{7,2},{8,13},{9,12},{12,... | collective-permute-start | bytes 786440 | tf_op jit(solution)/shard_map/ppermute | solution.py:58
  785.9 68.3 %collective-permute-start.90 = (bf16[64,2048]{1,0:T(8,128)(2,1)}, bf16[64,2048]{1,0:T(8,128)(2,1)S(1)}, u32[]{:S(2)}, u32[]{:S(2)}) collective-permute-start(bf16[64,2048]{1,0:T(8,128)(2,1)} %get-tuple-element.175), channel_id=1, source_target_pairs={{0,4},{4,0},{1,5},{5,1},{2,6},{6,2},{3,7},{7,3},{8,12},{12,8},{9,1... | collective-permute-start | bytes 786440 | tf_op jit(solution)/shard_map/ppermute | solution.py:54
  787.3 66.8 %collective-permute-start.89 = (bf16[64,2048]{1,0:T(8,128)(2,1)S(1)}, bf16[64,2048]{1,0:T(8,128)(2,1)S(1)}, u32[]{:S(2)}, u32[]{:S(2)}) collective-permute-start(bf16[64,2048]{1,0:T(8,128)(2,1)S(1)} %copy-done.39), channel_id=1, source_target_pairs={{0,1},{1,0},{2,3},{3,2},{4,5},{5,4},{6,7},{7,6},{8,9},{9,8},{10,11... | collective-permute-start | bytes 786440 | tf_op jit(solution)/shard_map/ppermute | solution.py:54
  (139 other events, 1658.1 us)
Sparse Core Ops, SparseCore 0:
  23.8 66.2 all-gather.4
  92.3 63.3 all-gather.6
  157.9 91.8 all-gather.8
  251.8 80.5 all-gather.10
  503.5 79.1 reduce-scatter.6
  584.9 82.0 reduce-scatter.4
  669.3 88.2 reduce-scatter.10
  759.9 87.9 reduce-scatter.8

commit v3 on v2

--- a/solution.py
+++ b/solution.py
@@ -153,8 +153,9 @@
     )(rank.reshape(1), *parts)
 
 
-def finish(parts, rank, widths):
+def finish(parts, rank, widths, lead=0):
     rows, total = parts[0].shape
+    first = widths[0]
 
     def kernel(rank_ref, *refs):
         step = pl.program_id(0)
@@ -162,45 +163,27 @@
 
             @pl.when(step == k)
             def _():
-                offset = 0
-                for ref, width in zip(refs[4:], widths):
+                outs = refs[4:]
+                offset = lead * first
+                if lead:
+                    for j in range(lead):
+                        outs[0][:, j, :] = refs[k][:, j * first : (j + 1) * first].astype(F32)
+                    outs = outs[1:]
+                for ref, width in zip(outs, widths):
                     ref[...] = refs[k][:, offset : offset + width].astype(F32)
                     offset += width
 
+    shapes = [jax.ShapeDtypeStruct((rows, 4 * w), F32) for w in widths]
+    specs = [pl.BlockSpec((rows, w), lambda k, r: (0, k ^ r[0])) for w in widths]
+    if lead:
+        shapes = [jax.ShapeDtypeStruct((rows, lead, 4 * first), F32)] + shapes
+        specs = [pl.BlockSpec((rows, lead, first), lambda k, r: (0, 0, k ^ r[0]))] + specs
     return pl.pallas_call(
         kernel,
-        out_shape=[jax.ShapeDtypeStruct((rows, 4 * w), F32) for w in widths],
-        grid_spec=grid_spec(
-            [pl.BlockSpec((rows, total), lambda k, r: (0, 0))] * 4,
-            [pl.BlockSpec((rows, w), lambda k, r: (0, k ^ r[0])) for w in widths],
-        ),
+        out_shape=shapes,
+        grid_spec=grid_spec([pl.BlockSpec((rows, total), lambda k, r: (0, 0))] * 4, specs),
         compiler_params=pltpu.CompilerParams(vmem_limit_bytes=VMEM),
         name="finish",
-    )(rank.reshape(1), *parts)
-
-
-def finish_three(parts, rank):
-    rows, total = parts[0].shape
-    width = total // 3
-
-    def kernel(rank_ref, *refs):
-        step = pl.program_id(0)
-        for k in range(4):
-
-            @pl.when(step == k)
-            def _():
-                for j in range(3):
-                    refs[4][:, j, :] = refs[k][:, j * width : (j + 1) * width].astype(F32)
-
-    return pl.pallas_call(
-        kernel,
-        out_shape=jax.ShapeDtypeStruct((rows, 3, 4 * width), F32),
-        grid_spec=grid_spec(
-            [pl.BlockSpec((rows, total), lambda k, r: (0, 0))] * 4,
-            pl.BlockSpec((rows, 3, width), lambda k, r: (0, 0, k ^ r[0])),
-        ),
-        compiler_params=pltpu.CompilerParams(vmem_limit_bytes=VMEM),
-        name="finish_three",
     )(rank.reshape(1), *parts)
 
 
@@ -351,6 +334,37 @@
         10 * tokens * context * group,
         "cross_back",
     )(queries, text_kv, grad_mixed)
+
+
+def grad_products(pairs):
+    tokens, width = pairs[0][0].shape
+    count = len(pairs)
+    widths = [y.shape[1] for _, y in pairs]
+    total = sum(widths)
+    rows = 256
+    step = 512
+
+    def kernel(*refs):
+        out = refs[2 * count]
+        offset = 0
+        for k, wide in enumerate(widths):
+            left = refs[k][...].T
+            for at in range(0, wide, step):
+                out[:, offset + at : offset + at + step] = mm(
+                    left, refs[count + k][:, at : at + step]
+                ).astype(BF)
+            offset += wide
+
+    return kernel_call(
+        kernel,
+        jax.ShapeDtypeStruct((width, total), BF),
+        (width // rows,),
+        [pl.BlockSpec((tokens, rows), lambda i: (0, i))] * count
+        + [pl.BlockSpec((tokens, w), lambda i: (0, 0)) for w in widths],
+        pl.BlockSpec((rows, total), lambda i: (i, 0)),
+        2 * tokens * width * total,
+        "grad_products",
+    )(*[x for x, _ in pairs], *[y for _, y in pairs])
 
 
 def gather_rows(rows):
@@ -419,14 +433,13 @@
         group = width // 4
         hidden_group = w_up.shape[1] // 4
 
-        qkv_rows = w_qkv.reshape(shard_rows, 3 * width)
-        qkv_parts = [
-            pieces(qkv_rows[:, j * width : (j + 1) * width], rank, group) for j in range(3)
-        ]
-        qkv_parts = swap_all(
-            [jnp.concatenate([part[k] for part in qkv_parts], axis=1) for k in range(4)]
-        )
-        qkv = gather_rows(place(qkv_parts, rank, [3 * group])[0])
+        first = [w_qkv.reshape(shard_rows, 3 * width)[:, j * width : (j + 1) * width] for j in range(3)]
+        first = [pieces(weight, rank, group) for weight in first + [w_out]]
+        first = swap_all(
+            [jnp.concatenate([part[k] for part in first], axis=1) for k in range(4)]
+        )
+        first = gather_rows(place(first, rank, [4 * group])[0])
+        qkv, out_w = first[:, : 3 * group], first[:, 3 * group :]
 
         positions = lax.axis_index("y") * local_rows + jnp.arange(local_rows, dtype=jnp.int32)
         ranks = jnp.arange(full_length, dtype=jnp.int32)
@@ -444,12 +457,12 @@
         normed_a, inv_a = normalize(start_x)
         attn_in = gather_tokens((normed_a * gains[0]).astype(BF))
 
-        rest = pack([w_out, w_cross[:, 0], w_cross_out, w_up, w_down], rank)
-        mid, up, down = place(swap_all(rest), rank, [3 * group, hidden_group, hidden_group])
+        rest = pack([w_cross[:, 0], w_cross_out, w_up, w_down], rank)
+        mid, up, down = place(swap_all(rest), rank, [2 * group, hidden_group, hidden_group])
         mid = gather_rows(mid)
         up = gather_rows(up)
         down = gather_rows(down)
-        out_w, query_w, cross_out_w = (mid[:, k * group : (k + 1) * group] for k in range(3))
+        query_w, cross_out_w = mid[:, :group], mid[:, group:]
 
         own_text = mm_t(caption, w_text).astype(BF)
         kv_rows = w_cross[:, 1:].reshape(shard_rows, 2 * width)
@@ -460,6 +473,7 @@
         )
         text_kv = sum_data(sum(part.astype(F32) for part in kv_parts)).astype(BF)
         grad_y = gather_tokens(grad_top.astype(BF))
+        attn_in, text_kv, grad_y = lax.optimization_barrier((attn_in, text_kv, grad_y))
 
         projected = mm(attn_in, qkv).astype(BF)
         self_mixed = self_forward(projected, 2 * images)
@@ -476,17 +490,12 @@
         pre_act = mm(mlp_in, up)
         activated, gelu_pull = jax.vjp(jax.nn.gelu, pre_act)
         activated = activated.astype(BF)
-        down_part = t_mm(grad_y, activated).astype(BF)
         grad_pre = gelu_pull(mm(grad_y, down))[0].astype(BF)
-        grad_pre, down_part = lax.optimization_barrier((grad_pre, down_part))
-        up_part = t_mm(mlp_in, grad_pre).astype(BF)
         back_part = mm_t(grad_pre, up)
-        back_part, up_part = lax.optimization_barrier((back_part, up_part))
-        down_rows = scatter_grad(down_part)
-        up_rows = scatter_grad(up_part)
+        grad_pre, back_part = lax.optimization_barrier((grad_pre, back_part))
+        mlp_part = grad_products([(grad_y, activated), (mlp_in, grad_pre)])
+        mlp_rows = scatter_grad(mlp_part)
         grad_mlp_in = scatter_tokens(back_part)
-        result = after_cross + scatter_tokens(mm_t(activated, down))
-        output = feature_swap(result.astype(BF))
         back_c, gain_grad_c = norm_back(grad_mlp_in, normed_c, inv_c, gains[2])
         grad_after_cross = grad_top + back_c
 
@@ -498,24 +507,26 @@
         grad_after_attn = grad_after_cross + back_b
 
         attn_branch = gather_tokens(grad_after_attn.astype(BF))
-        mid_part = jnp.concatenate(
+        grad_self_mixed = mm(attn_branch, out_w).astype(BF)
+        grad_projected = self_back(projected, grad_self_mixed, 2 * images)
+        attn_part = grad_products(
             [
-                t_mm(attn_branch, self_mixed).astype(BF),
-                t_mm(cross_in, grad_cq).astype(BF),
-                t_mm(cross_branch, cross_mixed).astype(BF),
-            ],
-            axis=1,
-        )
-        grad_self_mixed = mm(attn_branch, out_w).astype(BF)
-        grad_self_mixed, mid_part = lax.optimization_barrier((grad_self_mixed, mid_part))
-        mid_rows = scatter_grad(mid_part)
-        grad_projected = self_back(projected, grad_self_mixed, 2 * images)
-        qkv_part = t_mm(attn_in, grad_projected).astype(BF)
-        grad_projected, qkv_part = lax.optimization_barrier((grad_projected, qkv_part))
-        qkv_rows = scatter_grad(qkv_part)
+                (attn_in, grad_projected),
+                (attn_branch, self_mixed),
+                (cross_in, grad_cq),
+                (cross_branch, cross_mixed),
+            ]
+        )
+        attn_part, mlp_rows = lax.optimization_barrier((attn_part, mlp_rows))
+        attn_rows = scatter_grad(attn_part)
+        grad_projected, activated, kv_grad, attn_part = lax.optimization_barrier(
+            (grad_projected, activated, kv_grad, attn_part)
+        )
         grad_attn_in = scatter_tokens(mm_t(grad_projected, qkv))
         back_a, gain_grad_a = norm_back(grad_attn_in, normed_a, inv_a, gains[0])
         grad_start = grad_after_attn + back_a
+        result = after_cross + scatter_tokens(mm_t(activated, down))
+        output = feature_swap(result.astype(BF))
 
         kv_grad = sum_data(kv_grad).astype(BF)
         kv_grads = place(swap_all([kv_grad] * 4), rank, [group, group])
@@ -531,13 +542,10 @@
         caption_own = sum_data(sum(part.astype(F32) for part in caption_parts)).astype(BF)
         grad_caption = finish(swap_all([caption_own] * 4), rank, [caption_own.shape[1]])[0]
 
-        down_grad, up_grad = (
-            finish(send_rows(rows, rank), rank, [hidden_group])[0] for rows in (down_rows, up_rows)
-        )
-        out_grad, query_grad, cross_out_grad = finish(
-            send_rows(mid_rows, rank), rank, [group] * 3
-        )
-        qkv_grad = finish_three(send_rows(qkv_rows, rank), rank)
+        down_grad, up_grad = finish(send_rows(mlp_rows, rank), rank, [hidden_group] * 2)
+        qkv_grad, out_grad, query_grad, cross_out_grad = finish(
+            send_rows(attn_rows, rank), rank, [group] * 3, 3
+        )
         grad_hidden = feature_swap(jnp.where(masked, 0.0, grad_start).astype(BF))
         mask_part = jnp.sum(jnp.where(masked, grad_start, 0.0), axis=0)
         sums = feature_swap(

time: 880 us -> 748 us (0.85)
  waiting for transfers between devices: 523 us -> 418 us
  matrix products: 100 us -> 68.5 us
  Pallas kernels: 25 us -> 45.5 us
  other arithmetic: 40.6 us -> 30.2 us
  local copies, waits for them, and re-layouts: 66.6 us -> 56.6 us
    reduce_scatter x4 -> x2, waiting for transfers between devices: 139 us -> 48.9 us  [scatter_grad(): summed = lax.psum_scatter(partial, DATA, scatter_dimension=0, tiled=True)]
    dot_general x24 -> x18, matrix products: 100 us -> 68.5 us  [dot(): return lax.dot_general(a, b, (dims, ((), ())), preferred_element_type=F32)]
    pallas_call x5, Pallas kernels: 9.82 us -> 30.9 us  [the longest x2 24.4 us: grad_products(): kernel_call(kernel, jax.ShapeDtypeStruct((width, total), BF), (width // r...]
    concatenate x5 -> x4, other arithmetic: 11.2 us -> 0.08 us  [local(): jnp.concatenate([part[k] for part in first], axis=1)]
    ppermute x74 -> x70, starting transfers between devices: 73.5 us -> 83.1 us  [swap(): return lax.ppermute(values, axis, PAIR)]
    ppermute x10 -> x8, starting transfers between devices: 17.8 us -> 9.72 us  [swap_diag(): return lax.ppermute(values, ('x', 'y'), DIAG)]
    ppermute x74 -> x70, waiting for transfers between devices: 202 us -> 194 us  [swap(): return lax.ppermute(values, axis, PAIR)]
    ppermute x10 -> x8, waiting for transfers between devices: 25.1 us -> 29.3 us  [swap_diag(): return lax.ppermute(values, ('x', 'y'), DIAG)]
  transfers between devices with their start and end apart: 100 -> 92, of which waited for: 64 -> 61; matrix products, arithmetic and copies ran while one was open for 19% -> 17% of each run, Pallas kernels for 2% -> 4%
where the time goes in v3:
time: 748 us; the launch traced here: 738 us
  waiting for transfers between devices  418 us (56%)
  starting transfers between devices  102 us (14%)
  matrix products  68.5 us (9%)
  local copies, waits for them, and re-layouts  56.6 us (8%)
  Pallas kernels  45.5 us (6%)
  other arithmetic  30.2 us (4%)
  between operations  16.8 us (2%)
    ppermute x70, waiting for transfers between devices, swap(): return lax.ppermute(values, axis, PAIR)  194 us
    ppermute x6, waiting for transfers between devices, sum_data(): got = lax.ppermute(sent, 'z', tuple(((k, k ^ step) for k in range(z_size))))  88.9 us
    ppermute x70, starting transfers between devices, swap(): return lax.ppermute(values, axis, PAIR)  83.1 us
    dot_general x18, matrix products, dot(): return lax.dot_general(a, b, (dims, ((), ())), preferred_element_type=F32)  68.5 us
    all_gather x4, waiting for transfers between devices, gather_rows(): return lax.all_gather(rows, DATA, axis=0, tiled=True)  54.2 us
    reduce_scatter x2, waiting for transfers between devices, scatter_grad(): summed = lax.psum_scatter(partial, DATA, scatter_dimension=0, tiled=True)  48.9 us
    ppermute x8, waiting for transfers between devices, swap_diag(): return lax.ppermute(values, ('x', 'y'), DIAG)  29.3 us
    pallas_call x2, Pallas kernels, grad_products(): kernel_call(kernel, jax.ShapeDtypeStruct((width, total), BF), (width // r...  24.4 us
  transfers between devices with their start and end apart: 92, of which 61 were waited for; matrix products, arithmetic and copies ran while one was open for 17% of the time, Pallas kernels for 4%

profile of v3, /device:TPU:0, one launch (start us, length us, event | category | flops | bytes accessed | tf_op | source)
XLA Modules:
  0.0 737.5 jit_solution(3238379026812589067)
XLA Ops:
  31.9 13.3 %collective-permute-done.25.refs_1_ = bf16[64,5120]{1,0:T(8,128)(2,1)S(1)} collective-permute-done((bf16[64,5120]{1,0:T(8,128)(2,1)S(1)}, bf16[64,5120]{1,0:T(8,128)(2,1)S(1)}, u32[]{:S(2)}, u32[]{:S(2)}) %collective-permute-start.25) | collective-permute-done | bytes 655392 | tf_op jit(solution)/shard_map/ppermute | solution.py:54
  47.8 11.4 %collective-permute-done.27.refs_3_ = bf16[64,5120]{1,0:T(8,128)(2,1)S(1)} collective-permute-done((bf16[64,5120]{1,0:T(8,128)(2,1)S(1)}, bf16[64,5120]{1,0:T(8,128)(2,1)S(1)}, u32[]{:S(2)}, u32[]{:S(2)}) %collective-permute-start.27) | collective-permute-done | bytes 655392 | tf_op jit(solution)/shard_map/ppermute | solution.py:58
  101.2 9.1 %collective-permute-done.4 = bf16[128,1024]{1,0:T(8,128)(2,1)S(1)} collective-permute-done((bf16[128,1024]{1,0:T(8,128)(2,1)S(1)}, bf16[128,1024]{1,0:T(8,128)(2,1)S(1)}, u32[]{:S(2)}, u32[]{:S(2)}) %collective-permute-start.4) | collective-permute-done | bytes 262176 | tf_op jit(solution)/shard_map/ppermute | solution.py:54
  130.1 22.4 %collective-permute-done.8 = bf16[128,1024]{1,0:T(8,128)(2,1)S(1)} collective-permute-done((bf16[128,1024]{1,0:T(8,128)(2,1)S(1)}, bf16[128,1024]{1,0:T(8,128)(2,1)S(1)}, u32[]{:S(2)}, u32[]{:S(2)}) %collective-permute-start.8) | collective-permute-done | bytes 262176 | tf_op jit(solution)/shard_map/ppermute | solution.py:391
  157.4 12.9 %collective-permute-done.9 = bf16[128,1024]{1,0:T(8,128)(2,1)S(1)} collective-permute-done((bf16[128,1024]{1,0:T(8,128)(2,1)S(1)}, bf16[128,1024]{1,0:T(8,128)(2,1)S(1)}, u32[]{:S(2)}, u32[]{:S(2)}) %collective-permute-start.9) | collective-permute-done | bytes 262176 | tf_op jit(solution)/shard_map/ppermute | solution.py:391
  193.5 9.7 %collective-permute-done.20 = bf16[128,2048]{1,0:T(8,128)(2,1)S(1)} collective-permute-done((bf16[128,2048]{1,0:T(8,128)(2,1)S(1)}, bf16[128,2048]{1,0:T(8,128)(2,1)S(1)}, u32[]{:S(2)}, u32[]{:S(2)}) %collective-permute-start.20) | collective-permute-done | bytes 524320 | tf_op jit(solution)/shard_map/ppermute | solution.py:54
  208.5 9.3 %collective-permute-done.22 = bf16[128,2048]{1,0:T(8,128)(2,1)S(1)} collective-permute-done((bf16[128,2048]{1,0:T(8,128)(2,1)S(1)}, bf16[128,2048]{1,0:T(8,128)(2,1)S(1)}, u32[]{:S(2)}, u32[]{:S(2)}) %collective-permute-start.22) | collective-permute-done | bytes 524320 | tf_op jit(solution)/shard_map/ppermute | solution.py:54
  245.2 8.3 %collective-permute-done.31 = bf16[128,2048]{1,0:T(8,128)(2,1)S(1)} collective-permute-done((bf16[128,2048]{1,0:T(8,128)(2,1)S(1)}, bf16[128,2048]{1,0:T(8,128)(2,1)S(1)}, u32[]{:S(2)}, u32[]{:S(2)}) %collective-permute-start.31) | collective-permute-done | bytes 524320 | tf_op jit(solution)/shard_map/ppermute | solution.py:54
  258.6 11.6 %fusion.79 = f32[512,2048]{1,0:T(8,128)} fusion(bf16[512,2048]{1,0:T(8,128)(2,1)} %constant_dynamic-update-slice_fusion.5.refs_0_, bf16[2048,2048]{1,0:T(8,128)(2,1)} %all-gather.9.cloned.1.call-done), kind=kOutput, calls=%fused_computation.236 | convolution fusion | flops 4294967296 | bytes 14680064 | tf_op jit(solution)/shard_map/dot_general | solution.py:22
  279.6 54.2 %all-gather.11.cloned.1.call-done = bf16[2048,2048]{1,0:T(8,128)(2,1)} async-done(((bf16[256,2048]{1,0:T(8,128)(2,1)}), bf16[2048,2048]{1,0:T(8,128)(2,1)}) %all-gather.11.cloned.1.call-update) | async-done | bytes 8388624 | tf_op jit(solution)/shard_map/all_gather | solution.py:371
  333.8 12.8 %multiply_convert_fusion = (bf16[512,2048]{1,0:T(8,128)(2,1)S(1)}, bf16[512,2048]{1,0:T(8,128)(2,1)S(1)}) fusion(f32[512,2048]{1,0:T(8,128)} %fusion.79, bf16[512,2048]{1,0:T(8,128)(2,1)} %constant_dynamic-update-slice_fusion.15.refs_1_, bf16[2048,2048]{1,0:T(8,128)(2,1)} %all-gather.11.cloned.1.call-done), kind=kOutput, calls=%fused_computation.15 | convolution fusion | flops 4318035968 | bytes 18874368 | tf_op jit(solution)/shard_map/dot_general | solution.py:22
  352.9 13.2 %grad_products.3 = bf16[2048,4096]{1,0:T(8,128)(2,1)} custom-call(bf16[512,2048]{1,0:T(8,128)(2,1)} %constant_dynamic-update-slice_fusion.5.refs_0_, bf16[512,2048]{1,0:T(8,128)(2,1)} %constant_dynamic-update-slice_fusion.15.refs_1_, bf16[512,2048]{1,0:T(8,128)(2,1)S(1)} %get-tuple-element.54.refs_2_, bf16[512,2048]{1,0:T(8,128)(2,1)S(1)} %get-tuple-element.52.refs_3_), custom_call_target="tpu_custom_call" | custom-call | flops 8589934592 | bytes 4194304 | tf_op jit(solution)/shard_map/grad_products/pallas_call | solution.py:358
  381.2 10.9 %collective-permute-done.39 = bf16[128,2048]{1,0:T(8,128)(2,1)S(1)} collective-permute-done((bf16[128,2048]{1,0:T(8,128)(2,1)S(1)}, bf16[128,2048]{1,0:T(8,128)(2,1)S(1)}, u32[]{:S(2)}, u32[]{:S(2)}) %collective-permute-start.39) | collective-permute-done | bytes 524320 | tf_op jit(solution)/shard_map/ppermute | solution.py:54
  396.6 9.2 %collective-permute-done.41 = bf16[128,2048]{1,0:T(8,128)(2,1)S(1)} collective-permute-done((bf16[128,2048]{1,0:T(8,128)(2,1)S(1)}, bf16[128,2048]{1,0:T(8,128)(2,1)S(1)}, u32[]{:S(2)}, u32[]{:S(2)}) %collective-permute-start.41) | collective-permute-done | bytes 524320 | tf_op jit(solution)/shard_map/ppermute | solution.py:54
  430.0 9.6 %collective-permute-done.47 = bf16[128,2048]{1,0:T(8,128)(2,1)S(1)} collective-permute-done((bf16[128,2048]{1,0:T(8,128)(2,1)S(1)}, bf16[128,2048]{1,0:T(8,128)(2,1)S(1)}, u32[]{:S(2)}, u32[]{:S(2)}) %collective-permute-start.47) | collective-permute-done | bytes 524320 | tf_op jit(solution)/shard_map/ppermute | solution.py:54
  445.3 7.5 %collective-permute-done.49 = bf16[128,2048]{1,0:T(8,128)(2,1)S(1)} collective-permute-done((bf16[128,2048]{1,0:T(8,128)(2,1)S(1)}, bf16[128,2048]{1,0:T(8,128)(2,1)S(1)}, u32[]{:S(2)}, u32[]{:S(2)}) %collective-permute-start.49) | collective-permute-done | bytes 524320 | tf_op jit(solution)/shard_map/ppermute | solution.py:54
  471.8 11.2 %grad_products.2 = bf16[2048,3072]{1,0:T(8,128)(2,1)} custom-call(bf16[512,2048]{1,0:T(8,128)(2,1)S(1)} %copy-done.6, bf16[512,2048]{1,0:T(8,128)(2,1)S(1)} %constant_dynamic-update-slice_fusion.25.refs_1_, bf16[512,2048]{1,0:T(8,128)(2,1)} %constant_dynamic-update-slice_fusion.10.refs_2_, ...), custom_call_target="tpu_custom_call" | custom-call | flops 6442450944 | bytes 4194304 | tf_op jit(solution)/shard_map/grad_products/pallas_call | solution.py:358
  484.1 48.9 %reduce-scatter.3.cloned.1.call-done = bf16[256,4096]{1,0:T(8,128)(2,1)} async-done(((bf16[2048,4096]{1,0:T(8,128)(2,1)}), bf16[256,4096]{1,0:T(8,128)(2,1)}) %reduce-scatter.3.cloned.1.call-update) | async-done | bytes 2097168 | tf_op jit(solution)/shard_map/reduce_scatter | solution.py:375
  533.1 7.7 %fusion.77 = (bf16[512,2048]{1,0:T(8,128)(2,1)S(1)}, f32[512,2048]{1,0:T(8,128)S(1)}) fusion(bf16[512,2048]{1,0:T(8,128)(2,1)} %copy-done.12, bf16[2048,2048]{1,0:T(8,128)(2,1)} %all-gather.9.cloned.1.call-done), kind=kOutput, calls=%fused_computation.234 | convolution fusion | flops 4296015872 | bytes 16777216 | tf_op jit(solution)/shard_map/dot_general | solution.py:22
  563.5 11.3 %collective-permute-done.61 = bf16[128,1024]{1,0:T(8,128)(2,1)S(1)} collective-permute-done((bf16[128,1024]{1,0:T(8,128)(2,1)S(1)}, bf16[128,1024]{1,0:T(8,128)(2,1)S(1)}, u32[]{:S(2)}, u32[]{:S(2)}) %collective-permute-start.61) | collective-permute-done | bytes 262176 | tf_op jit(solution)/shard_map/ppermute | solution.py:391
  580.1 20.3 %collective-permute-done.62 = bf16[128,1024]{1,0:T(8,128)(2,1)S(1)} collective-permute-done((bf16[128,1024]{1,0:T(8,128)(2,1)S(1)}, bf16[128,1024]{1,0:T(8,128)(2,1)S(1)}, u32[]{:S(2)}, u32[]{:S(2)}) %collective-permute-start.62) | collective-permute-done | bytes 262176 | tf_op jit(solution)/shard_map/ppermute | solution.py:391
  661.4 12.2 %collective-permute-done.70 = bf16[128,1024]{1,0:T(8,128)(2,1)S(1)} collective-permute-done((bf16[128,1024]{1,0:T(8,128)(2,1)S(1)}, bf16[128,1024]{1,0:T(8,128)(2,1)S(1)}, u32[]{:S(2)}, u32[]{:S(2)}) %collective-permute-start.70) | collective-permute-done | bytes 262176 | tf_op jit(solution)/shard_map/ppermute | solution.py:391
  679.1 9.9 %collective-permute-done.71 = bf16[128,1024]{1,0:T(8,128)(2,1)S(1)} collective-permute-done((bf16[128,1024]{1,0:T(8,128)(2,1)S(1)}, bf16[128,1024]{1,0:T(8,128)(2,1)S(1)}, u32[]{:S(2)}, u32[]{:S(2)}) %collective-permute-start.71) | collective-permute-done | bytes 262176 | tf_op jit(solution)/shard_map/ppermute | solution.py:391
  701.7 17.1 %collective-permute-done.73.refs_2_ = bf16[128,1024]{1,0:T(8,128)(2,1)S(1)} collective-permute-done((bf16[128,1024]{1,0:T(8,128)(2,1)S(1)}, bf16[128,1024]{1,0:T(8,128)(2,1)S(1)}, u32[]{:S(2)}, u32[]{:S(2)}) %collective-permute-start.73) | collective-permute-done | bytes 262176 | tf_op jit(solution)/shard_map/ppermute | solution.py:54
  (469 shorter events, 356.9 us)
Async XLA Ops:
  7.2 163.1 %all-gather.5.cloned.1.call-start = ((), (), s32[]{:S(2)}) async-start(), calls=%async_computation.2 | async-start | bytes 9437184 | tf_op jit(solution)/shard_map/all_gather | solution.py:371
  26.6 199.5 %all-gather.7.cloned.1.call-start = ((), (), s32[]{:S(2)}) async-start(), calls=%async_computation.3 | async-start | bytes 4718592 | tf_op jit(solution)/shard_map/all_gather | solution.py:371
  31.6 27.6 %collective-permute-start.27 = (bf16[64,5120]{1,0:T(8,128)(2,1)S(1)}, bf16[64,5120]{1,0:T(8,128)(2,1)S(1)}, u32[]{:S(2)}, u32[]{:S(2)}) collective-permute-start(bf16[64,5120]{1,0:T(8,128)(2,1)S(1)} %get-tuple-element.43), channel_id=1, source_target_pairs={{0,5},{1,4},{4,1},{5,0},{2,7},{3,6},{6,3},{7,2},{8,13},{9,12},{12,... | collective-permute-start | bytes 1966088 | tf_op jit(solution)/shard_map/ppermute | solution.py:58
  62.0 196.6 %all-gather.9.cloned.1.call-start = ((), (), s32[]{:S(2)}) async-start(), calls=%async_computation.4 | async-start | bytes 9437184 | tf_op jit(solution)/shard_map/all_gather | solution.py:371
  62.8 271.0 %all-gather.11.cloned.1.call-start = ((), (), s32[]{:S(2)}) async-start(), calls=%async_computation.5 | async-start | bytes 9437184 | tf_op jit(solution)/shard_map/all_gather | solution.py:371
  72.8 42.7 %collective-permute-start = (bf16[128,2048]{1,0:T(8,128)(2,1)}, bf16[128,2048]{1,0:T(8,128)(2,1)}, u32[]{:S(2)}, u32[]{:S(2)}) collective-permute-start(bf16[128,2048]{1,0:T(8,128)(2,1)} %get-tuple-element.145), channel_id=1, source_target_pairs={{0,1},{1,0},{2,3},{3,2},{4,5},{5,4},{6,7},{7,6},{8,9},{9,8},{10,11... | collective-permute-start | bytes 1572872 | tf_op jit(solution)/shard_map/ppermute | solution.py:54
  74.1 38.2 %collective-permute-start.1 = (bf16[128,2048]{1,0:T(8,128)(2,1)}, bf16[128,2048]{1,0:T(8,128)(2,1)}, u32[]{:S(2)}, u32[]{:S(2)}) collective-permute-start(bf16[128,2048]{1,0:T(8,128)(2,1)} %get-tuple-element.145), channel_id=1, source_target_pairs={{0,4},{4,0},{1,5},{5,1},{2,6},{6,2},{3,7},{7,3},{8,12},{12,8},{9,1... | collective-permute-start | bytes 1572872 | tf_op jit(solution)/shard_map/ppermute | solution.py:54
  93.0 26.5 %collective-permute-start.10 = (bf16[128,2048]{1,0:T(8,128)(2,1)S(1)}, bf16[128,2048]{1,0:T(8,128)(2,1)S(1)}, u32[]{:S(2)}, u32[]{:S(2)}) collective-permute-start(bf16[128,2048]{1,0:T(8,128)(2,1)S(1)} %get-tuple-element.143), channel_id=1, source_target_pairs={{0,1},{1,0},{2,3},{3,2},{4,5},{5,4},{6,7},{7,6},{8,9},{9,8},{10,11... | collective-permute-start | bytes 1572872 | tf_op jit(solution)/shard_map/ppermute | solution.py:54
  95.0 23.1 %collective-permute-start.11 = (bf16[128,2048]{1,0:T(8,128)(2,1)S(1)}, bf16[128,2048]{1,0:T(8,128)(2,1)S(1)}, u32[]{:S(2)}, u32[]{:S(2)}) collective-permute-start(bf16[128,2048]{1,0:T(8,128)(2,1)S(1)} %get-tuple-element.143), channel_id=1, source_target_pairs={{0,4},{4,0},{1,5},{5,1},{2,6},{6,2},{3,7},{7,3},{8,12},{12,8},{9,1... | collective-permute-start | bytes 1572872 | tf_op jit(solution)/shard_map/ppermute | solution.py:54
  118.9 35.2 %collective-permute-start.12 = (bf16[64,2048]{1,0:T(8,128)(2,1)}, bf16[64,2048]{1,0:T(8,128)(2,1)}, u32[]{:S(2)}, u32[]{:S(2)}) collective-permute-start(bf16[64,2048]{1,0:T(8,128)(2,1)} %slice.368), channel_id=1, source_target_pairs={{0,1},{1,0},{2,3},{3,2},{4,5},{5,4},{6,7},{7,6},{8,9},{9,8},{10,11... | collective-permute-start | bytes 786440 | tf_op jit(solution)/shard_map/ppermute | solution.py:54
  120.3 35.4 %collective-permute-start.13 = (bf16[64,2048]{1,0:T(8,128)(2,1)}, bf16[64,2048]{1,0:T(8,128)(2,1)}, u32[]{:S(2)}, u32[]{:S(2)}) collective-permute-start(bf16[64,2048]{1,0:T(8,128)(2,1)} %slice.369), channel_id=1, source_target_pairs={{0,4},{4,0},{1,5},{5,1},{2,6},{6,2},{3,7},{7,3},{8,12},{12,8},{9,1... | collective-permute-start | bytes 786440 | tf_op jit(solution)/shard_map/ppermute | solution.py:54
  125.0 408.0 %reduce-scatter.3.cloned.1.call-start = ((), (), s32[]{:S(2)}) async-start(), calls=%async_computation.6 | async-start | bytes 18874368 | tf_op jit(solution)/shard_map/reduce_scatter | solution.py:375
  126.5 25.9 %collective-permute-start.8 = (bf16[128,1024]{1,0:T(8,128)(2,1)S(1)}, bf16[128,1024]{1,0:T(8,128)(2,1)S(1)}, u32[]{:S(2)}, u32[]{:S(2)}) collective-permute-start(bf16[128,1024]{1,0:T(8,128)(2,1)S(1)} %add_convert_fusion.10), channel_id=1, source_target_pairs={{0,8},{8,0},{16,24},{24,16},{1,9},{9,1},{17,25},{25,17},{2,10},{10... | collective-permute-start | bytes 786440 | tf_op jit(solution)/shard_map/ppermute | solution.py:391
  366.1 324.3 %reduce-scatter.5.cloned.1.call-start = ((), (), s32[]{:S(2)}) async-start(), calls=%async_computation.7 | async-start | bytes 14155776 | tf_op jit(solution)/shard_map/reduce_scatter | solution.py:375
  556.0 82.2 %collective-permute-start.83 = (bf16[64,4096]{1,0:T(8,128)(2,1)}, bf16[64,4096]{1,0:T(8,128)(2,1)S(1)}, u32[]{:S(2)}, u32[]{:S(2)}) collective-permute-start(bf16[64,4096]{1,0:T(8,128)(2,1)} %get-tuple-element.164), channel_id=1, source_target_pairs={{0,1},{1,0},{2,3},{3,2},{4,5},{5,4},{6,7},{7,6},{8,9},{9,8},{10,11... | collective-permute-start | bytes 1572872 | tf_op jit(solution)/shard_map/ppermute | solution.py:54
  557.0 89.9 %collective-permute-start.84 = (bf16[64,4096]{1,0:T(8,128)(2,1)}, bf16[64,4096]{1,0:T(8,128)(2,1)S(1)}, u32[]{:S(2)}, u32[]{:S(2)}) collective-permute-start(bf16[64,4096]{1,0:T(8,128)(2,1)} %get-tuple-element.163), channel_id=1, source_target_pairs={{0,4},{4,0},{1,5},{5,1},{2,6},{6,2},{3,7},{7,3},{8,12},{12,8},{9,1... | collective-permute-start | bytes 1572872 | tf_op jit(solution)/shard_map/ppermute | solution.py:54
  559.0 20.1 %collective-permute-start.59 = (bf16[128,2048]{1,0:T(8,128)(2,1)S(1)}, bf16[128,2048]{1,0:T(8,128)(2,1)S(1)}, u32[]{:S(2)}, u32[]{:S(2)}) collective-permute-start(bf16[128,2048]{1,0:T(8,128)(2,1)S(1)} %pad_maximum_fusion.15), channel_id=1, source_target_pairs={{0,1},{1,0},{2,3},{3,2},{4,5},{5,4},{6,7},{7,6},{8,9},{9,8},{10,11... | collective-permute-start | bytes 1572872 | tf_op jit(solution)/shard_map/ppermute | solution.py:54
  574.9 25.5 %collective-permute-start.62 = (bf16[128,1024]{1,0:T(8,128)(2,1)S(1)}, bf16[128,1024]{1,0:T(8,128)(2,1)S(1)}, u32[]{:S(2)}, u32[]{:S(2)}) collective-permute-start(bf16[128,1024]{1,0:T(8,128)(2,1)S(1)} %add_convert_fusion.4), channel_id=1, source_target_pairs={{0,16},{8,24},{16,0},{24,8},{1,17},{9,25},{17,1},{25,9},{2,18},{10... | collective-permute-start | bytes 786440 | tf_op jit(solution)/shard_map/ppermute | solution.py:391
  638.2 20.3 %collective-permute-start.55 = (bf16[128,2048]{1,0:T(8,128)(2,1)S(1)}, bf16[128,2048]{1,0:T(8,128)(2,1)S(1)}, u32[]{:S(2)}, u32[]{:S(2)}) collective-permute-start(bf16[128,2048]{1,0:T(8,128)(2,1)S(1)} %copy-done.38), channel_id=1, source_target_pairs={{0,1},{1,0},{2,3},{3,2},{4,5},{5,4},{6,7},{7,6},{8,9},{9,8},{10,11... | collective-permute-start | bytes 1572872 | tf_op jit(solution)/shard_map/ppermute | solution.py:54
  691.8 33.0 %collective-permute-start.80 = (bf16[64,3072]{1,0:T(8,128)(2,1)S(1)}, bf16[64,3072]{1,0:T(8,128)(2,1)S(1)}, u32[]{:S(2)}, u32[]{:S(2)}) collective-permute-start(bf16[64,3072]{1,0:T(8,128)(2,1)S(1)} %get-tuple-element.192), channel_id=1, source_target_pairs={{0,1},{1,0},{2,3},{3,2},{4,5},{5,4},{6,7},{7,6},{8,9},{9,8},{10,11... | collective-permute-start | bytes 1179656 | tf_op jit(solution)/shard_map/ppermute | solution.py:54
  692.6 32.2 %collective-permute-start.81 = (bf16[64,3072]{1,0:T(8,128)(2,1)S(1)}, bf16[64,3072]{1,0:T(8,128)(2,1)S(1)}, u32[]{:S(2)}, u32[]{:S(2)}) collective-permute-start(bf16[64,3072]{1,0:T(8,128)(2,1)S(1)} %get-tuple-element.191), channel_id=1, source_target_pairs={{0,4},{4,0},{1,5},{5,1},{2,6},{6,2},{3,7},{7,3},{8,12},{12,8},{9,1... | collective-permute-start | bytes 1179656 | tf_op jit(solution)/shard_map/ppermute | solution.py:54
  693.9 31.0 %collective-permute-start.82 = (bf16[64,3072]{1,0:T(8,128)(2,1)S(1)}, bf16[64,3072]{1,0:T(8,128)(2,1)S(1)}, u32[]{:S(2)}, u32[]{:S(2)}) collective-permute-start(bf16[64,3072]{1,0:T(8,128)(2,1)S(1)} %get-tuple-element.190), channel_id=1, source_target_pairs={{0,5},{1,4},{4,1},{5,0},{2,7},{3,6},{6,3},{7,2},{8,13},{9,12},{12,... | collective-permute-start | bytes 1179656 | tf_op jit(solution)/shard_map/ppermute | solution.py:58
  696.0 22.8 %collective-permute-start.73 = (bf16[128,1024]{1,0:T(8,128)(2,1)S(1)}, bf16[128,1024]{1,0:T(8,128)(2,1)S(1)}, u32[]{:S(2)}, u32[]{:S(2)}) collective-permute-start(bf16[128,1024]{1,0:T(8,128)(2,1)S(1)} %add_convert_fusion.refs_0_), channel_id=1, source_target_pairs={{0,4},{4,0},{1,5},{5,1},{2,6},{6,2},{3,7},{7,3},{8,12},{12,8},{9,1... | collective-permute-start | bytes 786440 | tf_op jit(solution)/shard_map/ppermute | solution.py:54
  698.3 24.7 %collective-permute-start.74 = (bf16[128,1024]{1,0:T(8,128)(2,1)S(1)}, bf16[128,1024]{1,0:T(8,128)(2,1)S(1)}, u32[]{:S(2)}, u32[]{:S(2)}) collective-permute-start(bf16[128,1024]{1,0:T(8,128)(2,1)S(1)} %add_convert_fusion.refs_0_), channel_id=1, source_target_pairs={{0,5},{1,4},{4,1},{5,0},{2,7},{3,6},{6,3},{7,2},{8,13},{9,12},{12,... | collective-permute-start | bytes 786440 | tf_op jit(solution)/shard_map/ppermute | solution.py:58
  (125 other events, 1458.3 us)
Sparse Core Ops, SparseCore 0:
  26.7 83.5 all-gather.4
  112.5 51.9 all-gather.6
  166.1 85.6 all-gather.8
  253.2 80.5 all-gather.10
  366.2 166.7 reduce-scatter.2
  535.2 149.1 reduce-scatter.4

commit v4 on v3

--- a/solution.py
+++ b/solution.py
@@ -14,7 +14,8 @@
 F32 = jnp.float32
 PAIR = ((0, 1), (1, 0))
 DIAG = ((0, 3), (1, 2), (2, 1), (3, 0))
-DATA = ("z", "c")
+DATA = ("w", "c", "z")
+PAIR_DATA = ("w", "c")
 VMEM = 40 * 1024 * 1024
 
 
@@ -83,6 +84,15 @@
     return own + from_x.astype(F32) + from_y.astype(F32)
 
 
+def gather_pair(own):
+    return gather_tokens(own), gather_tokens(swap(own, "z"))
+
+
+def scatter_pair(near, far):
+    far = scatter_tokens(far).astype(BF)
+    return scatter_tokens(near) + swap(far, "z").astype(F32)
+
+
 def swap_all(parts):
     return [parts[0], swap(parts[1], "y"), swap(parts[2], "x"), swap_diag(parts[3])]
 
@@ -93,16 +103,29 @@
     ]
 
 
-def grid_spec(in_specs, out_specs):
-    return pltpu.PrefetchScalarGridSpec(
-        num_scalar_prefetch=1, grid=(4,), in_specs=in_specs, out_specs=out_specs
-    )
-
-
-def pack(weights, rank):
-    rows = weights[0].shape[0]
-    widths = [w.shape[1] // 4 for w in weights]
-    total = sum(widths)
+def block_call(kernel, steps, out_shape, in_specs, out_specs, rank, operands, name):
+    return pl.pallas_call(
+        kernel,
+        out_shape=out_shape,
+        grid_spec=pltpu.PrefetchScalarGridSpec(
+            num_scalar_prefetch=1, grid=(steps,), in_specs=in_specs, out_specs=out_specs
+        ),
+        compiler_params=pltpu.CompilerParams(vmem_limit_bytes=VMEM),
+        name=name,
+    )(rank.reshape(1), *operands)
+
+
+def whole(array):
+    return pl.BlockSpec(array.shape, lambda k, r: (0,) * len(array.shape))
+
+
+def pack(cross, wide, rank):
+    rows = wide[0].shape[0]
+    cross_width, width = cross[0].shape[1] // 4, wide[0].shape[1] // 8
+    weights = cross + wide
+    widths = [cross_width] * len(cross) + [width] * len(wide)
+    total, far_total = sum(widths), width * len(wide)
+    count = len(weights)
 
     def kernel(rank_ref, *refs):
         step = pl.program_id(0)
@@ -111,80 +134,102 @@
             @pl.when(step == k)
             def _():
                 offset = 0
-                for ref, width in zip(refs, widths):
-                    refs[len(widths) + k][:, offset : offset + width] = ref[...]
-                    offset += width
-
-    return pl.pallas_call(
-        kernel,
-        out_shape=[jax.ShapeDtypeStruct((rows, total), BF)] * 4,
-        grid_spec=grid_spec(
-            [pl.BlockSpec((rows, w), lambda k, r: (0, k ^ r[0])) for w in widths],
-            [pl.BlockSpec((rows, total), lambda k, r: (0, 0))] * 4,
-        ),
-        compiler_params=pltpu.CompilerParams(vmem_limit_bytes=VMEM),
-        name="pack",
-    )(rank.reshape(1), *weights)
-
-
-def place(parts, rank, widths):
-    rows, total = parts[0].shape
+                for ref, w in zip(refs, widths):
+                    refs[count + k][:, offset : offset + w] = ref[...]
+                    offset += w
+
+            @pl.when(step == 4 + k)
+            def _():
+                for j in range(len(wide)):
+                    refs[count + 4][k * rows : (k + 1) * rows, j * width : (j + 1) * width] = refs[
+                        len(cross) + j
+                    ][...]
+
+    shapes = [jax.ShapeDtypeStruct((rows, total), BF)] * 4
+    shapes.append(jax.ShapeDtypeStruct((4 * rows, far_total), BF))
+    *near, far = block_call(
+        kernel,
+        8,
+        shapes,
+        [pl.BlockSpec((rows, cross_width), lambda k, r: (0, (k ^ r[0]) & 3))] * len(cross)
+        + [pl.BlockSpec((rows, width), lambda k, r: (0, k ^ r[0]))] * len(wide),
+        [whole(shape) for shape in shapes],
+        rank,
+        weights,
+        "pack",
+    )
+    return near, far
+
+
+def place(pieces, rank, widths):
+    rows, starts, arrays = block_rows(pieces)
+    count = len(arrays)
 
     def kernel(rank_ref, *refs):
         step = pl.program_id(0)
-        for k in range(4):
+        for k, (which, row, offset) in enumerate(starts):
 
             @pl.when(step == k)
             def _():
-                offset = 0
-                for ref, width in zip(refs[4:], widths):
-                    ref[...] = refs[k][:, offset : offset + width]
-                    offset += width
-
-    return pl.pallas_call(
-        kernel,
-        out_shape=[jax.ShapeDtypeStruct((4 * rows, w), BF) for w in widths],
-        grid_spec=grid_spec(
-            [pl.BlockSpec((rows, total), lambda k, r: (0, 0))] * 4,
-            [pl.BlockSpec((rows, w), lambda k, r: (k ^ r[0], 0)) for w in widths],
-        ),
-        compiler_params=pltpu.CompilerParams(vmem_limit_bytes=VMEM),
-        name="place",
-    )(rank.reshape(1), *parts)
-
-
-def finish(parts, rank, widths, lead=0):
-    rows, total = parts[0].shape
+                at = offset
+                for ref, width in zip(refs[count:], widths):
+                    ref[...] = refs[which][row : row + rows, at : at + width]
+                    at += width
+
+    return block_call(
+        kernel,
+        len(pieces),
+        [jax.ShapeDtypeStruct((len(pieces) * rows, w), BF) for w in widths],
+        [whole(array) for array in arrays],
+        [pl.BlockSpec((rows, w), lambda k, r: (k ^ r[0], 0)) for w in widths],
+        rank,
+        arrays,
+        "place",
+    )
+
+
+def block_rows(pieces):
+    arrays, starts = [], []
+    for array, row, column in pieces:
+        found = [k for k, other in enumerate(arrays) if other is array]
+        if not found:
+            arrays.append(array)
+        starts.append((found[0] if found else len(arrays) - 1, row, column))
+    rows = min([array.shape[0] for array in arrays] + [s[1] for s in starts if s[1]])
+    return rows, starts, arrays
+
+
+def finish(pieces, rank, widths, lead=0):
+    rows, starts, arrays = block_rows(pieces)
+    blocks = len(pieces)
     first = widths[0]
+    count = len(arrays)
 
     def kernel(rank_ref, *refs):
         step = pl.program_id(0)
-        for k in range(4):
+        for k, (which, row, offset) in enumerate(starts):
 
             @pl.when(step == k)
             def _():
-                outs = refs[4:]
-                offset = lead * first
+                outs = refs[count:]
+                at = offset
                 if lead:
                     for j in range(lead):
-                        outs[0][:, j, :] = refs[k][:, j * first : (j + 1) * first].astype(F32)
+                        outs[0][:, j, :] = refs[which][row : row + rows, at : at + first].astype(F32)
+                        at += first
                     outs = outs[1:]
                 for ref, width in zip(outs, widths):
-                    ref[...] = refs[k][:, offset : offset + width].astype(F32)
-                    offset += width
-
-    shapes = [jax.ShapeDtypeStruct((rows, 4 * w), F32) for w in widths]
+                    ref[...] = refs[which][row : row + rows, at : at + width].astype(F32)
+                    at += width
+
+    shapes = [jax.ShapeDtypeStruct((rows, blocks * w), F32) for w in widths]
     specs = [pl.BlockSpec((rows, w), lambda k, r: (0, k ^ r[0])) for w in widths]
     if lead:
-        shapes = [jax.ShapeDtypeStruct((rows, lead, 4 * first), F32)] + shapes
+        shapes = [jax.ShapeDtypeStruct((rows, lead, blocks * first), F32)] + shapes
         specs = [pl.BlockSpec((rows, lead, first), lambda k, r: (0, 0, k ^ r[0]))] + specs
-    return pl.pallas_call(
-        kernel,
-        out_shape=shapes,
-        grid_spec=grid_spec([pl.BlockSpec((rows, total), lambda k, r: (0, 0))] * 4, specs),
-        compiler_params=pltpu.CompilerParams(vmem_limit_bytes=VMEM),
-        name="finish",
-    )(rank.reshape(1), *parts)
+    return block_call(
+        kernel, blocks, shapes, [whole(a) for a in arrays], specs, rank, arrays, "finish"
+    )
 
 
 def softmax(scores):
@@ -337,21 +382,23 @@
 
 
 def grad_products(pairs):
-    tokens, width = pairs[0][0].shape
-    count = len(pairs)
-    widths = [y.shape[1] for _, y in pairs]
+    blocks = len(pairs[0][0])
+    tokens, width = pairs[0][0][0].shape
+    widths = [y[0].shape[1] for _, y in pairs]
     total = sum(widths)
     rows = 256
     step = 512
+    count = len(pairs) * blocks
 
     def kernel(*refs):
         out = refs[2 * count]
         offset = 0
         for k, wide in enumerate(widths):
-            left = refs[k][...].T
+            left = [refs[k * blocks + b][...].T for b in range(blocks)]
             for at in range(0, wide, step):
-                out[:, offset + at : offset + at + step] = mm(
-                    left, refs[count + k][:, at : at + step]
+                out[:, offset + at : offset + at + step] = sum(
+                    mm(left[b], refs[count + k * blocks + b][:, at : at + step])
+                    for b in range(blocks)
                 ).astype(BF)
             offset += wide
 
@@ -360,54 +407,72 @@
         jax.ShapeDtypeStruct((width, total), BF),
         (width // rows,),
         [pl.BlockSpec((tokens, rows), lambda i: (0, i))] * count
-        + [pl.BlockSpec((tokens, w), lambda i: (0, 0)) for w in widths],
+        + [pl.BlockSpec((tokens, w), lambda i: (0, 0)) for w in widths for _ in range(blocks)],
         pl.BlockSpec((rows, total), lambda i: (i, 0)),
-        2 * tokens * width * total,
+        2 * tokens * blocks * width * total,
         "grad_products",
-    )(*[x for x, _ in pairs], *[y for _, y in pairs])
-
-
-def gather_rows(rows):
-    return lax.all_gather(rows, DATA, axis=0, tiled=True)
-
-
-def scatter_grad(partial):
-    summed = lax.psum_scatter(partial, DATA, scatter_dimension=0, tiled=True)
-    return summed.reshape(4, -1, summed.shape[-1])
-
-
-def send_rows(blocks, rank):
-    return swap_all(
-        [lax.dynamic_index_in_dim(blocks, rank ^ k, 0, keepdims=False) for k in range(4)]
-    )
+    )(*[b for x, _ in pairs for b in x], *[b for _, y in pairs for b in y])
+
+
+def gather_rows(rows, axes):
+    return lax.all_gather(rows, axes, axis=0, tiled=True)
+
+
+def scatter_grad(partial, axes):
+    return lax.psum_scatter(partial, axes, scatter_dimension=0, tiled=True)
+
+
+def pick_rows(values, rank, count):
+    rows = values.shape[0] // count
+    return [
+        lax.dynamic_slice_in_dim(values, (rank ^ k) * rows, rows, 0) for k in range(count)
+    ]
 
 
 def make_local(z_size):
+    z_axes = ("w", "z")
+
+    def sum_z(values):
+        terms = [values] + [
+            lax.ppermute(values, z_axes, tuple((k, k ^ m) for k in range(z_size)))
+            for m in range(1, z_size)
+        ]
+        terms = [term.astype(F32) for term in terms]
+        while len(terms) > 1:
+            terms = [terms[k] + terms[k + 1] for k in range(0, len(terms), 2)]
+        return terms[0]
+
     def sum_data(values):
-        values = values + swap(values, "c")
-        step = 1
-        while step < z_size:
-            sent = values.astype(BF)
-            got = lax.ppermute(sent, "z", tuple((k, k ^ step) for k in range(z_size)))
-            values = sent.astype(F32) + got.astype(F32)
-            step *= 2
-        return values
+        core = lax.axis_index("c")
+        half = values.shape[0] // 2
+        keep = lax.dynamic_slice_in_dim(values, core * half, half, 0)
+        send = lax.dynamic_slice_in_dim(values, (1 - core) * half, half, 0)
+        mine = sum_z((keep + swap(send, "c")).astype(BF)).astype(BF)
+        other = swap(mine, "c")
+        return jnp.concatenate(
+            [jnp.where(core == 0, mine, other), jnp.where(core == 0, other, mine)], axis=0
+        )
 
     def sum_all(values):
-        for axis in ("c", "x", "y"):
+        for axis in ("c", "x", "y", "z"):
             values = values + swap(values, axis)
         step = 1
-        while step < z_size:
+        while 2 * step < z_size:
             values = values + lax.ppermute(
-                values, "z", tuple((k, k ^ step) for k in range(z_size))
+                values, "w", tuple((k, k ^ step) for k in range(z_size // 2))
             )
             step *= 2
         return values
 
-    def feature_swap(values):
+    def feature_order(values):
         lead = values.shape[:-1]
-        shaped = values.reshape(lead + (z_size, 2, 2, -1))
-        return jnp.swapaxes(shaped, -3, -2).reshape(values.shape)
+        shaped = values.reshape(lead + (z_size // 2, 2, 2, 2, -1))
+        return jnp.moveaxis(shaped, -2, -4).reshape(values.shape)
+
+    def natural_order(values):
+        lead = values.shape[:-1]
+        shaped = values.reshape(lead + (z_size // 2, 2, 2, 2, -1))
+        return jnp.moveaxis(shaped, -4, -2).reshape(values.shape)
 
     def local(
         hidden,
@@ -429,16 +494,17 @@
         full_length = mask_index.shape[1]
         shard_rows = w_qkv.shape[0]
         rank = lax.axis_index("x") * 2 + lax.axis_index("y")
+        pair_rank = lax.axis_index("z") * 4 + rank
         tokens = images * local_rows
         group = width // 4
-        hidden_group = w_up.shape[1] // 4
+        hidden_group = w_up.shape[1] // 8
 
         first = [w_qkv.reshape(shard_rows, 3 * width)[:, j * width : (j + 1) * width] for j in range(3)]
         first = [pieces(weight, rank, group) for weight in first + [w_out]]
         first = swap_all(
             [jnp.concatenate([part[k] for part in first], axis=1) for k in range(4)]
         )
-        first = gather_rows(place(first, rank, [4 * group])[0])
+        first = gather_rows(place([(p, 0, 0) for p in first], rank, [4 * group])[0], DATA)
         qkv, out_w = first[:, : 3 * group], first[:, 3 * group :]
 
         positions = lax.axis_index("y") * local_rows + jnp.arange(local_rows, dtype=jnp.int32)
@@ -447,22 +513,29 @@
             ranks[None, :, None] < mask_count[:, None, None]
         )
         masked = jnp.any(matches, axis=1).reshape(tokens, 1)
-        gains = feature_swap(norm_gains)
+        gains = feature_order(norm_gains)
         start_x = jnp.where(
             masked,
-            feature_swap(mask_embed),
-            feature_swap(hidden.reshape(tokens, width)).astype(F32),
-        )
-        grad_top = feature_swap(cotangent.reshape(tokens, width)).astype(F32) * masked.astype(F32)
+            feature_order(mask_embed),
+            feature_order(hidden.reshape(tokens, width)).astype(F32),
+        )
+        grad_top = feature_order(cotangent.reshape(tokens, width)).astype(F32) * masked.astype(F32)
         normed_a, inv_a = normalize(start_x)
         attn_in = gather_tokens((normed_a * gains[0]).astype(BF))
 
-        rest = pack([w_cross[:, 0], w_cross_out, w_up, w_down], rank)
-        mid, up, down = place(swap_all(rest), rank, [2 * group, hidden_group, hidden_group])
-        mid = gather_rows(mid)
-        up = gather_rows(up)
-        down = gather_rows(down)
+        near, far = pack([w_cross[:, 0], w_cross_out], [w_up, w_down], pair_rank)
+        far = swap(far, "z")
+        near = swap_all(near)
+        mid = gather_rows(place([(p, 0, 0) for p in near], rank, [2 * group])[0], DATA)
+        far = swap_all([far[k * shard_rows : (k + 1) * shard_rows] for k in range(4)])
+        mlp = place(
+            [(p, 0, 2 * group) for p in near] + [(p, 0, 0) for p in far],
+            pair_rank,
+            [2 * hidden_group],
+        )[0]
+        mlp = gather_rows(mlp, PAIR_DATA)
         query_w, cross_out_w = mid[:, :group], mid[:, group:]
+        up, down = mlp[:, :hidden_group], mlp[:, hidden_group:]
 
         own_text = mm_t(caption, w_text).astype(BF)
         kv_rows = w_cross[:, 1:].reshape(shard_rows, 2 * width)
@@ -471,12 +544,13 @@
         kv_parts = swap_all(
             [jnp.concatenate([part[k] for part in kv_parts], axis=1) for k in range(4)]
         )
-        text_kv = sum_data(sum(part.astype(F32) for part in kv_parts)).astype(BF)
-        grad_y = gather_tokens(grad_top.astype(BF))
-        attn_in, text_kv, grad_y = lax.optimization_barrier((attn_in, text_kv, grad_y))
+        text_kv = sum_data(sum(part.astype(F32) for part in kv_parts))
+        grad_y = gather_pair(grad_top.astype(BF))
+        attn_in, text_kv = lax.optimization_barrier((attn_in, text_kv))
 
         projected = mm(attn_in, qkv).astype(BF)
         self_mixed = self_forward(projected, 2 * images)
+        self_mixed, grad_y = lax.optimization_barrier((self_mixed, grad_y))
         after_attn = start_x + scatter_tokens(mm_t(self_mixed, out_w))
 
         normed_b, inv_b = normalize(after_attn)
@@ -486,22 +560,29 @@
         after_cross = after_attn + scatter_tokens(mm_t(cross_mixed, cross_out_w))
 
         normed_c, inv_c = normalize(after_cross)
-        mlp_in = gather_tokens((normed_c * gains[2]).astype(BF))
-        pre_act = mm(mlp_in, up)
-        activated, gelu_pull = jax.vjp(jax.nn.gelu, pre_act)
-        activated = activated.astype(BF)
-        grad_pre = gelu_pull(mm(grad_y, down))[0].astype(BF)
-        back_part = mm_t(grad_pre, up)
+        mlp_in = gather_pair((normed_c * gains[2]).astype(BF))
+        activated, grad_pre, back_part = [], [], []
+        for side in range(2):
+            pre_act = mm(mlp_in[side], up)
+            active, gelu_pull = jax.vjp(jax.nn.gelu, pre_act)
+            activated.append(active.astype(BF))
+            grad_pre.append(gelu_pull(mm(grad_y[side], down))[0].astype(BF))
+            back_part.append(mm_t(grad_pre[side], up))
         grad_pre, back_part = lax.optimization_barrier((grad_pre, back_part))
         mlp_part = grad_products([(grad_y, activated), (mlp_in, grad_pre)])
-        mlp_rows = scatter_grad(mlp_part)
-        grad_mlp_in = scatter_tokens(back_part)
+        mlp_rows = scatter_grad(mlp_part, PAIR_DATA)
+        grad_mlp_in = scatter_pair(*back_part)
         back_c, gain_grad_c = norm_back(grad_mlp_in, normed_c, inv_c, gains[2])
         grad_after_cross = grad_top + back_c
 
         cross_branch = gather_tokens(grad_after_cross.astype(BF))
         grad_cross_mixed = mm(cross_branch, cross_out_w).astype(BF)
         grad_cq, kv_grad = cross_back(cross_queries, text_kv, grad_cross_mixed)
+        cross_part = grad_products(
+            [([cross_in], [grad_cq]), ([cross_branch], [cross_mixed])]
+        )
+        cross_part, mlp_rows = lax.optimization_barrier((cross_part, mlp_rows))
+        cross_rows = scatter_grad(cross_part, DATA)
         grad_cross_in = scatter_tokens(mm_t(grad_cq, query_w))
         back_b, gain_grad_b = norm_back(grad_cross_in, normed_b, inv_b, gains[1])
         grad_after_attn = grad_after_cross + back_b
@@ -510,26 +591,21 @@
         grad_self_mixed = mm(attn_branch, out_w).astype(BF)
         grad_projected = self_back(projected, grad_self_mixed, 2 * images)
         attn_part = grad_products(
-            [
-                (attn_in, grad_projected),
-                (attn_branch, self_mixed),
-                (cross_in, grad_cq),
-                (cross_branch, cross_mixed),
-            ]
-        )
-        attn_part, mlp_rows = lax.optimization_barrier((attn_part, mlp_rows))
-        attn_rows = scatter_grad(attn_part)
+            [([attn_in], [grad_projected]), ([attn_branch], [self_mixed])]
+        )
+        attn_part, cross_rows = lax.optimization_barrier((attn_part, cross_rows))
+        attn_rows = scatter_grad(attn_part, DATA)
         grad_projected, activated, kv_grad, attn_part = lax.optimization_barrier(
             (grad_projected, activated, kv_grad, attn_part)
         )
         grad_attn_in = scatter_tokens(mm_t(grad_projected, qkv))
         back_a, gain_grad_a = norm_back(grad_attn_in, normed_a, inv_a, gains[0])
         grad_start = grad_after_attn + back_a
-        result = after_cross + scatter_tokens(mm_t(activated, down))
-        output = feature_swap(result.astype(BF))
-
-        kv_grad = sum_data(kv_grad).astype(BF)
-        kv_grads = place(swap_all([kv_grad] * 4), rank, [group, group])
+        result = after_cross + scatter_pair(*[mm_t(active, down) for active in activated])
+        output = natural_order(result.astype(BF))
+
+        kv_grad = sum_data(kv_grad)
+        kv_grads = place([(p, 0, 0) for p in swap_all([kv_grad] * 4)], rank, [group, group])
         kv_grads = [
             part.reshape(4, -1, group).transpose(1, 0, 2).reshape(-1, width) for part in kv_grads
         ]
@@ -539,16 +615,25 @@
         grad_text_w = t_mm(grad_text, caption)
         caption_part = mm(grad_text, w_text).astype(BF)
         caption_parts = swap_all(pieces(caption_part, rank, caption.shape[1] // 4))
-        caption_own = sum_data(sum(part.astype(F32) for part in caption_parts)).astype(BF)
-        grad_caption = finish(swap_all([caption_own] * 4), rank, [caption_own.shape[1]])[0]
-
-        down_grad, up_grad = finish(send_rows(mlp_rows, rank), rank, [hidden_group] * 2)
-        qkv_grad, out_grad, query_grad, cross_out_grad = finish(
-            send_rows(attn_rows, rank), rank, [group] * 3, 3
-        )
-        grad_hidden = feature_swap(jnp.where(masked, 0.0, grad_start).astype(BF))
+        caption_own = sum_data(sum(part.astype(F32) for part in caption_parts))
+        caption_parts = swap_all([caption_own] * 4)
+        grad_caption = finish([(p, 0, 0) for p in caption_parts], rank, [caption_own.shape[1]])[0]
+
+        picked = pick_rows(mlp_rows, pair_rank, 8)
+        parts = swap_all([jnp.concatenate([picked[k], picked[4 + k]], axis=0) for k in range(4)])
+        far = swap(jnp.concatenate([part[shard_rows:] for part in parts], axis=0), "z")
+        down_grad, up_grad = finish(
+            [(part, 0, 0) for part in parts] + [(far, k * shard_rows, 0) for k in range(4)],
+            pair_rank,
+            [hidden_group] * 2,
+        )
+        parts = swap_all(pick_rows(cross_rows, rank, 4))
+        query_grad, cross_out_grad = finish([(p, 0, 0) for p in parts], rank, [group] * 2)
+        parts = swap_all(pick_rows(attn_rows, rank, 4))
+        qkv_grad, out_grad = finish([(p, 0, 0) for p in parts], rank, [group], 3)
+        grad_hidden = natural_order(jnp.where(masked, 0.0, grad_start).astype(BF))
         mask_part = jnp.sum(jnp.where(masked, grad_start, 0.0), axis=0)
-        sums = feature_swap(
+        sums = natural_order(
             sum_all(jnp.stack([gain_grad_a, gain_grad_b, gain_grad_c, mask_part]))
         )
         grad_cross = jnp.concatenate([query_grad[:, None], kv_weight_grad], axis=1)
@@ -572,25 +657,11 @@
 
 def solution(mesh):
     z_size = mesh.shape["img"] // 4
-    inner = Mesh(mesh.devices.reshape(z_size, 2, 2, 2), ("z", "x", "c", "y"))
-    tokens = P(("z", "x", "c"), "y", None)
-    rows = P(("z", "x", "c", "y"))
-    in_specs = (
-        tokens,
-        P(("z", "x", "c"), None),
-        P(("z", "x", "c")),
-        P(),
-        P(),
-        P(),
-        rows,
-        rows,
-        rows,
-        rows,
-        rows,
-        rows,
-        rows,
-        tokens,
-    )
+    inner = Mesh(mesh.devices.reshape(z_size // 2, 2, 2, 2, 2), ("w", "z", "x", "c", "y"))
+    image = ("w", "z", "x", "c")
+    tokens = P(image, "y", None)
+    rows = P(image + ("y",))
+    in_specs = (tokens, P(image, None), P(image), P(), P(), P()) + (rows,) * 7 + (tokens,)
     out_specs = (tokens, tokens, P(), P(), P()) + (rows,) * 7
     return jax.shard_map(
         make_local(z_size), mesh=inner, in_specs=in_specs, out_specs=out_specs, check_vma=False

time: 748 us -> 948 us (1.27)
  waiting for transfers between devices: 418 us -> 544 us
  starting transfers between devices: 102 us -> 145 us
  local copies, waits for them, and re-layouts: 56.6 us -> 74 us
  Pallas kernels: 45.5 us -> 55.5 us
  other arithmetic: 30.2 us -> 40.1 us
    ppermute x70 -> x100, waiting for transfers between devices: 194 us -> 271 us  [swap(): return lax.ppermute(values, axis, PAIR)]
    all_gather x4 -> x3, waiting for transfers between devices: 54.2 us -> 97.6 us  [gather_rows(): return lax.all_gather(rows, axes, axis=0, tiled=True)]
    ppermute x70 -> x100, starting transfers between devices: 83.1 us -> 112 us  [swap(): return lax.ppermute(values, axis, PAIR)]
    ppermute x8 -> x10, waiting for transfers between devices: 29.3 us -> 52.5 us  [swap_diag(): return lax.ppermute(values, ('x', 'y'), DIAG)]
    ppermute x8 -> x10, waiting for transfers between devices: 90.2 us -> 70.3 us  [the longest x9 64.1 us: sum_z(): lax.ppermute(values, z_axes, tuple(((k, k ^ m) for k in range(z_size))))]
    ppermute x8 -> x10, starting transfers between devices: 8.64 us -> 19.2 us  [the longest x9 16.1 us: sum_z(): lax.ppermute(values, z_axes, tuple(((k, k ^ m) for k in range(z_size))))]
    unnamed x134 -> x142, local copies, waits for them, and re-layouts: 18.8 us -> 27.1 us
    reduce_scatter x2 -> x3, waiting for transfers between devices: 48.9 us -> 52.4 us  [scatter_grad(): return lax.psum_scatter(partial, axes, scatter_dimension=0, tiled=True)]
  transfers between devices with their start and end apart: 92 -> 126, of which waited for: 61 -> 82; matrix products, arithmetic and copies ran while one was open for 17% -> 17% of each run, Pallas kernels for 4% -> 4%
where the time goes in v4:
time: 948 us; the launch traced here: 944 us
  waiting for transfers between devices  544 us (57%)
  starting transfers between devices  145 us (15%)
  local copies, waits for them, and re-layouts  74 us (8%)
  matrix products  67.8 us (7%)
  Pallas kernels  55.5 us (6%)
  other arithmetic  40.1 us (4%)
  between operations  16.8 us (2%)
    ppermute x100, waiting for transfers between devices, swap(): return lax.ppermute(values, axis, PAIR)  271 us
    ppermute x100, starting transfers between devices, swap(): return lax.ppermute(values, axis, PAIR)  112 us
    all_gather x3, waiting for transfers between devices, gather_rows(): return lax.all_gather(rows, axes, axis=0, tiled=True)  97.6 us
    dot_general x22, matrix products, dot(): return lax.dot_general(a, b, (dims, ((), ())), preferred_element_type=F32)  67.8 us
    ppermute x9, waiting for transfers between devices, sum_z(): lax.ppermute(values, z_axes, tuple(((k, k ^ m) for k in range(z_size))))  64.1 us
    ppermute x10, waiting for transfers between devices, swap_diag(): return lax.ppermute(values, ('x', 'y'), DIAG)  52.5 us
    reduce_scatter x3, waiting for transfers between devices, scatter_grad(): return lax.psum_scatter(partial, axes, scatter_dimension=0, tiled=True)  52.4 us
    pallas_call x3, Pallas kernels, grad_products(): kernel_call(kernel, jax.ShapeDtypeStruct((width, total), BF), (width // r...  27.4 us
  transfers between devices with their start and end apart: 126, of which 82 were waited for; matrix products, arithmetic and copies ran while one was open for 17% of the time, Pallas kernels for 4%

profile of v4, /device:TPU:0, one launch (start us, length us, event | category | flops | bytes accessed | tf_op | source)
XLA Modules:
  0.0 943.6 jit_solution(8608112329883843530)
XLA Ops:
  99.2 15.3 %collective-permute-done.19 = bf16[128,2048]{1,0:T(8,128)(2,1)S(1)} collective-permute-done((bf16[128,2048]{1,0:T(8,128)(2,1)}, bf16[128,2048]{1,0:T(8,128)(2,1)S(1)}, u32[]{:S(2)}, u32[]{:S(2)}) %collective-permute-start.19) | collective-permute-done | bytes 524320 | tf_op jit(solution)/shard_map/ppermute | solution.py:55
  127.4 39.2 %collective-permute-done.10 = bf16[64,1024]{1,0:T(8,128)(2,1)S(1)} collective-permute-done((bf16[64,1024]{1,0:T(8,128)(2,1)S(1)}, bf16[64,1024]{1,0:T(8,128)(2,1)S(1)}, u32[]{:S(2)}, u32[]{:S(2)}) %collective-permute-start.10) | collective-permute-done | bytes 131104 | tf_op jit(solution)/shard_map/ppermute | solution.py:437
  184.6 8.5 collective-permute-done.21
  218.9 17.3 %all-gather.4.cloned.1.call-done = bf16[2048,2048]{1,0:T(8,128)(2,1)} async-done(((bf16[256,2048]{1,0:T(8,128)(2,1)}), bf16[2048,2048]{1,0:T(8,128)(2,1)}) %all-gather.4.cloned.1.call-update) | async-done | bytes 8388624 | tf_op jit(solution)/shard_map/all_gather | solution.py:418
  259.0 9.3 collective-permute-done.27
  273.3 7.8 collective-permute-done.29
  291.7 33.9 %all-gather.6.cloned.1.call-done = bf16[2048,1024]{1,0:T(8,128)(2,1)} async-done(((bf16[256,1024]{1,0:T(8,128)(2,1)}), bf16[2048,1024]{1,0:T(8,128)(2,1)}) %all-gather.6.cloned.1.call-update) | async-done | bytes 4194320 | tf_op jit(solution)/shard_map/all_gather | solution.py:418
  342.1 8.8 collective-permute-done.38
  356.8 6.9 collective-permute-done.44
  367.7 10.9 %collective-permute-done.47 = bf16[128,2048]{1,0:T(8,128)(2,1)} collective-permute-done((bf16[128,2048]{1,0:T(8,128)(2,1)S(1)}, bf16[128,2048]{1,0:T(8,128)(2,1)}, u32[]{:S(2)}, u32[]{:S(2)}) %collective-permute-start.47) | collective-permute-done | bytes 524320 | tf_op jit(solution)/shard_map/ppermute | solution.py:55
  384.8 46.4 %all-gather.8.cloned.1.call-done = bf16[2048,2048]{1,0:T(8,128)(2,1)} async-done(((bf16[512,2048]{1,0:T(8,128)(2,1)}), bf16[2048,2048]{1,0:T(8,128)(2,1)}) %all-gather.8.cloned.1.call-update) | async-done | bytes 8388624 | tf_op jit(solution)/shard_map/all_gather | solution.py:418
  467.2 13.0 %grad_products.5 = bf16[2048,2048]{1,0:T(8,128)(2,1)} custom-call(bf16[512,2048]{1,0:T(8,128)(2,1)S(1)} %copy-done.15, bf16[512,2048]{1,0:T(8,128)(2,1)S(1)} %copy-done.17, bf16[512,2048]{1,0:T(8,128)(2,1)} %constant_dynamic-update-slice_fusion.20.refs_2_, bf16[512,2048]{1,0:T(8,128)(2,1)S(1)} %constant_dynamic-update-slice_fusion.25.refs_3_, ...), custom_call_target="tpu_custom_call" | custom-call | flops 8589934592 | bytes 4194304 | tf_op jit(solution)/shard_map/grad_products/pallas_call | solution.py:405
  502.1 7.4 collective-permute-done.59
  510.3 8.5 collective-permute-done.55
  519.1 13.1 %collective-permute-done.60 = bf16[128,2048]{1,0:T(8,128)(2,1)S(1)} collective-permute-done((bf16[128,2048]{1,0:T(8,128)(2,1)S(1)}, bf16[128,2048]{1,0:T(8,128)(2,1)S(1)}, u32[]{:S(2)}, u32[]{:S(2)}) %collective-permute-start.60) | collective-permute-done | bytes 524320 | tf_op jit(solution)/shard_map/ppermute | solution.py:55
  537.3 7.7 collective-permute-done.62
  567.5 28.6 %reduce-scatter.4.cloned.1.call-done = bf16[512,2048]{1,0:T(8,128)(2,1)} async-done(((bf16[2048,2048]{1,0:T(8,128)(2,1)}), bf16[512,2048]{1,0:T(8,128)(2,1)}) %reduce-scatter.4.cloned.1.call-update) | async-done | bytes 2097168 | tf_op jit(solution)/shard_map/reduce_scatter | solution.py:422
  610.8 10.3 %collective-permute-done.68 = bf16[128,2048]{1,0:T(8,128)(2,1)S(1)} collective-permute-done((bf16[128,2048]{1,0:T(8,128)(2,1)S(1)}, bf16[128,2048]{1,0:T(8,128)(2,1)S(1)}, u32[]{:S(2)}, u32[]{:S(2)}) %collective-permute-start.68) | collective-permute-done | bytes 524320 | tf_op jit(solution)/shard_map/ppermute | solution.py:55
  626.4 8.5 collective-permute-done.70
  652.3 8.1 grad_products.3
  661.5 23.8 %reduce-scatter.6.cloned.1.call-done = bf16[256,1024]{1,0:T(8,128)(2,1)} async-done(((bf16[2048,1024]{1,0:T(8,128)(2,1)}), bf16[256,1024]{1,0:T(8,128)(2,1)}) %reduce-scatter.6.cloned.1.call-update) | async-done | bytes 524304 | tf_op jit(solution)/shard_map/reduce_scatter | solution.py:422
  690.9 20.6 %collective-permute-done.118.refs_3_ = bf16[128,2048]{1,0:T(8,128)(2,1)S(1)} collective-permute-done((bf16[128,2048]{1,0:T(8,128)(2,1)S(1)}, bf16[128,2048]{1,0:T(8,128)(2,1)S(1)}, u32[]{:S(2)}, u32[]{:S(2)}) %collective-permute-start.118) | collective-permute-done | bytes 524320 | tf_op jit(solution)/shard_map/ppermute | solution.py:59
  714.7 50.4 %collective-permute-done.119.refs_4_ = bf16[256,2048]{1,0:T(8,128)(2,1)} collective-permute-done((bf16[256,2048]{1,0:T(8,128)(2,1)}, bf16[256,2048]{1,0:T(8,128)(2,1)}, u32[]{:S(2)}, u32[]{:S(2)}) %collective-permute-start.119) | collective-permute-done | bytes 1048608 | tf_op jit(solution)/shard_map/ppermute | solution.py:55
  783.5 7.1 fusion.114
  (583 shorter events, 515.4 us)
Async XLA Ops:
  7.2 229.0 %all-gather.4.cloned.1.call-start = ((), (), s32[]{:S(2)}) async-start(), calls=%async_computation.3 | async-start | bytes 9437184 | tf_op jit(solution)/shard_map/all_gather | solution.py:418
  26.6 299.0 %all-gather.6.cloned.1.call-start = ((), (), s32[]{:S(2)}) async-start(), calls=%async_computation.4 | async-start | bytes 4718592 | tf_op jit(solution)/shard_map/all_gather | solution.py:418
  51.1 380.1 %all-gather.8.cloned.1.call-start = ((), (), s32[]{:S(2)}) async-start(), calls=%async_computation.5 | async-start | bytes 10485760 | tf_op jit(solution)/shard_map/all_gather | solution.py:418
  53.5 30.8 %collective-permute-start.6 = (bf16[128,1024]{1,0:T(8,128)(2,1)}, bf16[128,1024]{1,0:T(8,128)(2,1)}, u32[]{:S(2)}, u32[]{:S(2)}) collective-permute-start(bf16[128,1024]{1,0:T(8,128)(2,1)} %pad_maximum_fusion.27), channel_id=1, source_target_pairs={{0,5},{1,4},{4,1},{5,0},{2,7},{3,6},{6,3},{7,2},{8,13},{9,12},{12,... | collective-permute-start | bytes 786440 | tf_op jit(solution)/shard_map/ppermute | solution.py:59
  56.5 27.7 %collective-permute-start.5 = (bf16[128,1024]{1,0:T(8,128)(2,1)}, bf16[128,1024]{1,0:T(8,128)(2,1)}, u32[]{:S(2)}, u32[]{:S(2)}) collective-permute-start(bf16[128,1024]{1,0:T(8,128)(2,1)} %pad_maximum_fusion.26), channel_id=1, source_target_pairs={{0,4},{4,0},{1,5},{5,1},{2,6},{6,2},{3,7},{7,3},{8,12},{12,8},{9,1... | collective-permute-start | bytes 786440 | tf_op jit(solution)/shard_map/ppermute | solution.py:55
  57.8 26.4 %collective-permute-start.4 = (bf16[128,1024]{1,0:T(8,128)(2,1)}, bf16[128,1024]{1,0:T(8,128)(2,1)}, u32[]{:S(2)}, u32[]{:S(2)}) collective-permute-start(bf16[128,1024]{1,0:T(8,128)(2,1)} %pad_maximum_fusion.25), channel_id=1, source_target_pairs={{0,1},{1,0},{2,3},{3,2},{4,5},{5,4},{6,7},{7,6},{8,9},{9,8},{10,11... | collective-permute-start | bytes 786440 | tf_op jit(solution)/shard_map/ppermute | solution.py:55
  86.8 29.9 %collective-permute-start.15 = (bf16[128,2048]{1,0:T(8,128)(2,1)}, bf16[128,2048]{1,0:T(8,128)(2,1)}, u32[]{:S(2)}, u32[]{:S(2)}) collective-permute-start(bf16[128,2048]{1,0:T(8,128)(2,1)} %get-tuple-element.153), channel_id=1, source_target_pairs={{0,1},{1,0},{2,3},{3,2},{4,5},{5,4},{6,7},{7,6},{8,9},{9,8},{10,11... | collective-permute-start | bytes 1572872 | tf_op jit(solution)/shard_map/ppermute | solution.py:55
  87.3 33.7 %collective-permute-start.16 = (bf16[128,2048]{1,0:T(8,128)(2,1)}, bf16[128,2048]{1,0:T(8,128)(2,1)}, u32[]{:S(2)}, u32[]{:S(2)}) collective-permute-start(bf16[128,2048]{1,0:T(8,128)(2,1)} %get-tuple-element.153), channel_id=1, source_target_pairs={{0,4},{4,0},{1,5},{5,1},{2,6},{6,2},{3,7},{7,3},{8,12},{12,8},{9,1... | collective-permute-start | bytes 1572872 | tf_op jit(solution)/shard_map/ppermute | solution.py:55
  88.0 26.6 %collective-permute-start.19 = (bf16[128,2048]{1,0:T(8,128)(2,1)}, bf16[128,2048]{1,0:T(8,128)(2,1)S(1)}, u32[]{:S(2)}, u32[]{:S(2)}) collective-permute-start(bf16[128,2048]{1,0:T(8,128)(2,1)} %get-tuple-element.153), channel_id=1, source_target_pairs={{0,8},{8,0},{1,9},{9,1},{2,10},{10,2},{3,11},{11,3},{4,12},{12,4},... | collective-permute-start | bytes 1572872 | tf_op jit(solution)/shard_map/ppermute | solution.py:55
  91.3 105.7 %collective-permute-start.39 = (bf16[256,2048]{1,0:T(8,128)(2,1)}, bf16[256,2048]{1,0:T(8,128)(2,1)S(1)}, u32[]{:S(2)}, u32[]{:S(2)}) collective-permute-start(bf16[256,2048]{1,0:T(8,128)(2,1)} %copy-done.20), channel_id=1, source_target_pairs={{0,8},{8,0},{1,9},{9,1},{2,10},{10,2},{3,11},{11,3},{4,12},{12,4},... | collective-permute-start | bytes 3145736 | tf_op jit(solution)/shard_map/ppermute | solution.py:55
  92.9 73.8 %collective-permute-start.10 = (bf16[64,1024]{1,0:T(8,128)(2,1)S(1)}, bf16[64,1024]{1,0:T(8,128)(2,1)S(1)}, u32[]{:S(2)}, u32[]{:S(2)}) collective-permute-start(bf16[64,1024]{1,0:T(8,128)(2,1)S(1)} %add_convert_fusion.10), channel_id=1, source_target_pairs={{0,24},{8,16},{16,8},{24,0},{1,25},{9,17},{17,9},{25,1},{2,26},{10... | collective-permute-start | bytes 393224 | tf_op jit(solution)/shard_map/ppermute | solution.py:437
  114.5 54.8 %collective-permute-start.9 = (bf16[64,1024]{1,0:T(8,128)(2,1)S(1)}, bf16[64,1024]{1,0:T(8,128)(2,1)S(1)}, u32[]{:S(2)}, u32[]{:S(2)}) collective-permute-start(bf16[64,1024]{1,0:T(8,128)(2,1)S(1)} %add_convert_fusion.10), channel_id=1, source_target_pairs={{0,16},{8,24},{16,0},{24,8},{1,17},{9,25},{17,1},{25,9},{2,18},{10... | collective-permute-start | bytes 393224 | tf_op jit(solution)/shard_map/ppermute | solution.py:437
  116.7 57.9 %collective-permute-start.8 = (bf16[64,1024]{1,0:T(8,128)(2,1)S(1)}, bf16[64,1024]{1,0:T(8,128)(2,1)S(1)}, u32[]{:S(2)}, u32[]{:S(2)}) collective-permute-start(bf16[64,1024]{1,0:T(8,128)(2,1)S(1)} %add_convert_fusion.10), channel_id=1, source_target_pairs={{0,8},{8,0},{16,24},{24,16},{1,9},{9,1},{17,25},{25,17},{2,10},{10... | collective-permute-start | bytes 393224 | tf_op jit(solution)/shard_map/ppermute | solution.py:437
  121.0 55.2 %collective-permute-start.2 = (bf16[64,2048]{1,0:T(8,128)(2,1)S(1)}, bf16[64,2048]{1,0:T(8,128)(2,1)S(1)}, u32[]{:S(2)}, u32[]{:S(2)}) collective-permute-start(bf16[64,2048]{1,0:T(8,128)(2,1)S(1)} %slice.496), channel_id=1, source_target_pairs={{0,1},{1,0},{2,3},{3,2},{4,5},{5,4},{6,7},{7,6},{8,9},{9,8},{10,11... | collective-permute-start | bytes 786440 | tf_op jit(solution)/shard_map/ppermute | solution.py:55
  216.0 380.1 %reduce-scatter.4.cloned.1.call-start = ((), (), s32[]{:S(2)}) async-start(), calls=%async_computation.6 | async-start | bytes 10485760 | tf_op jit(solution)/shard_map/reduce_scatter | solution.py:422
  378.6 68.9 %collective-permute-start.48 = (bf16[128,2048]{1,0:T(8,128)(2,1)}, bf16[128,2048]{1,0:T(8,128)(2,1)}, u32[]{:S(2)}, u32[]{:S(2)}) collective-permute-start(bf16[128,2048]{1,0:T(8,128)(2,1)} %collective-permute-done.47), channel_id=1, source_target_pairs={{0,1},{1,0},{2,3},{3,2},{4,5},{5,4},{6,7},{7,6},{8,9},{9,8},{10,11... | collective-permute-start | bytes 1572872 | tf_op jit(solution)/shard_map/ppermute | solution.py:55
  379.2 65.8 %collective-permute-start.49 = (bf16[128,2048]{1,0:T(8,128)(2,1)}, bf16[128,2048]{1,0:T(8,128)(2,1)}, u32[]{:S(2)}, u32[]{:S(2)}) collective-permute-start(bf16[128,2048]{1,0:T(8,128)(2,1)} %collective-permute-done.47), channel_id=1, source_target_pairs={{0,4},{4,0},{1,5},{5,1},{2,6},{6,2},{3,7},{7,3},{8,12},{12,8},{9,1... | collective-permute-start | bytes 1572872 | tf_op jit(solution)/shard_map/ppermute | solution.py:55
  480.2 205.1 %reduce-scatter.6.cloned.1.call-start = ((), (), s32[]{:S(2)}) async-start(), calls=%async_computation.7 | async-start | bytes 4718592 | tf_op jit(solution)/shard_map/reduce_scatter | solution.py:422
  596.1 312.4 %reduce-scatter.8.cloned.1.call-start = ((), (), s32[]{:S(2)}) async-start(), calls=%async_computation.8 | async-start | bytes 9437184 | tf_op jit(solution)/shard_map/reduce_scatter | solution.py:422
  714.1 51.0 %collective-permute-start.119 = (bf16[256,2048]{1,0:T(8,128)(2,1)}, bf16[256,2048]{1,0:T(8,128)(2,1)}, u32[]{:S(2)}, u32[]{:S(2)}) collective-permute-start(bf16[256,2048]{1,0:T(8,128)(2,1)} %pad_maximum_fusion.2), channel_id=1, source_target_pairs={{0,8},{8,0},{1,9},{9,1},{2,10},{10,2},{3,11},{11,3},{4,12},{12,4},... | collective-permute-start | bytes 3145736 | tf_op jit(solution)/shard_map/ppermute | solution.py:55
  774.8 26.6 %collective-permute-start.79 = (bf16[64,2048]{1,0:T(8,128)(2,1)S(1)}, bf16[64,2048]{1,0:T(8,128)(2,1)S(1)}, u32[]{:S(2)}, u32[]{:S(2)}) collective-permute-start(bf16[64,2048]{1,0:T(8,128)(2,1)S(1)} %get-tuple-element.191), channel_id=1, source_target_pairs={{0,4},{4,0},{1,5},{5,1},{2,6},{6,2},{3,7},{7,3},{8,12},{12,8},{9,1... | collective-permute-start | bytes 786440 | tf_op jit(solution)/shard_map/ppermute | solution.py:55
  808.3 82.9 %collective-permute-start.80 = (bf16[128,2048]{1,0:T(8,128)(2,1)}, bf16[128,2048]{1,0:T(8,128)(2,1)}, u32[]{:S(2)}, u32[]{:S(2)}) collective-permute-start(bf16[128,2048]{1,0:T(8,128)(2,1)} %pad_maximum_fusion.18), channel_id=1, source_target_pairs={{0,1},{1,0},{2,3},{3,2},{4,5},{5,4},{6,7},{7,6},{8,9},{9,8},{10,11... | collective-permute-start | bytes 1572872 | tf_op jit(solution)/shard_map/ppermute | solution.py:55
  809.9 81.4 %collective-permute-start.78 = (bf16[128,2048]{1,0:T(8,128)(2,1)}, bf16[128,2048]{1,0:T(8,128)(2,1)}, u32[]{:S(2)}, u32[]{:S(2)}) collective-permute-start(bf16[128,2048]{1,0:T(8,128)(2,1)} %pad_maximum_fusion.17), channel_id=1, source_target_pairs={{0,4},{4,0},{1,5},{5,1},{2,6},{6,2},{3,7},{7,3},{8,12},{12,8},{9,1... | collective-permute-start | bytes 1572872 | tf_op jit(solution)/shard_map/ppermute | solution.py:55
  880.7 29.8 %collective-permute-start.76 = (bf16[128,2048]{1,0:T(8,128)(2,1)}, bf16[128,2048]{1,0:T(8,128)(2,1)}, u32[]{:S(2)}, u32[]{:S(2)}) collective-permute-start(bf16[128,2048]{1,0:T(8,128)(2,1)} %pad_maximum_fusion.16), channel_id=1, source_target_pairs={{0,1},{1,0},{2,3},{3,2},{4,5},{5,4},{6,7},{7,6},{8,9},{9,8},{10,11... | collective-permute-start | bytes 1572872 | tf_op jit(solution)/shard_map/ppermute | solution.py:55
  (159 other events, 1859.5 us)
Sparse Core Ops, SparseCore 0:
  26.7 209.3 all-gather.3
  238.3 87.3 all-gather.5
  327.2 103.9 all-gather.7
  480.4 115.6 reduce-scatter.3
  598.3 86.9 reduce-scatter.5
  687.6 206.0 reduce-scatter.7

commit v5 on v4

--- a/solution.py
+++ b/solution.py
@@ -14,7 +14,7 @@
 F32 = jnp.float32
 PAIR = ((0, 1), (1, 0))
 DIAG = ((0, 3), (1, 2), (2, 1), (3, 0))
-DATA = ("w", "c", "z")
+DATA = ("w", "z", "c")
 PAIR_DATA = ("w", "c")
 VMEM = 40 * 1024 * 1024
 
@@ -464,15 +464,16 @@
             step *= 2
         return values
 
-    def feature_order(values):
-        lead = values.shape[:-1]
-        shaped = values.reshape(lead + (z_size // 2, 2, 2, 2, -1))
-        return jnp.moveaxis(shaped, -2, -4).reshape(values.shape)
-
-    def natural_order(values):
-        lead = values.shape[:-1]
-        shaped = values.reshape(lead + (z_size // 2, 2, 2, 2, -1))
-        return jnp.moveaxis(shaped, -4, -2).reshape(values.shape)
+    def swap_dims(values, first):
+        shaped = values.reshape(values.shape[:-1] + (z_size // 2, 2, 2, 2, -1))
+        at = values.ndim - 1 + first
+        return jnp.swapaxes(shaped, at, at + 1).reshape(values.shape)
+
+    def layer_order(values):
+        return swap_dims(values, 2)
+
+    def pair_order(values):
+        return swap_dims(values, 1)
 
     def local(
         hidden,
@@ -513,13 +514,13 @@
             ranks[None, :, None] < mask_count[:, None, None]
         )
         masked = jnp.any(matches, axis=1).reshape(tokens, 1)
-        gains = feature_order(norm_gains)
+        gains = layer_order(norm_gains)
         start_x = jnp.where(
             masked,
-            feature_order(mask_embed),
-            feature_order(hidden.reshape(tokens, width)).astype(F32),
-        )
-        grad_top = feature_order(cotangent.reshape(tokens, width)).astype(F32) * masked.astype(F32)
+            layer_order(mask_embed),
+            layer_order(hidden.reshape(tokens, width)).astype(F32),
+        )
+        grad_top = layer_order(cotangent.reshape(tokens, width)).astype(F32) * masked.astype(F32)
         normed_a, inv_a = normalize(start_x)
         attn_in = gather_tokens((normed_a * gains[0]).astype(BF))
 
@@ -545,7 +546,7 @@
             [jnp.concatenate([part[k] for part in kv_parts], axis=1) for k in range(4)]
         )
         text_kv = sum_data(sum(part.astype(F32) for part in kv_parts))
-        grad_y = gather_pair(grad_top.astype(BF))
+        grad_y = gather_pair(pair_order(grad_top.astype(BF)))
         attn_in, text_kv = lax.optimization_barrier((attn_in, text_kv))
 
         projected = mm(attn_in, qkv).astype(BF)
@@ -560,7 +561,7 @@
         after_cross = after_attn + scatter_tokens(mm_t(cross_mixed, cross_out_w))
 
         normed_c, inv_c = normalize(after_cross)
-        mlp_in = gather_pair((normed_c * gains[2]).astype(BF))
+        mlp_in = gather_pair(pair_order((normed_c * gains[2]).astype(BF)))
         activated, grad_pre, back_part = [], [], []
         for side in range(2):
             pre_act = mm(mlp_in[side], up)
@@ -571,7 +572,7 @@
         grad_pre, back_part = lax.optimization_barrier((grad_pre, back_part))
         mlp_part = grad_products([(grad_y, activated), (mlp_in, grad_pre)])
         mlp_rows = scatter_grad(mlp_part, PAIR_DATA)
-        grad_mlp_in = scatter_pair(*back_part)
+        grad_mlp_in = pair_order(scatter_pair(*back_part))
         back_c, gain_grad_c = norm_back(grad_mlp_in, normed_c, inv_c, gains[2])
         grad_after_cross = grad_top + back_c
 
@@ -601,8 +602,10 @@
         grad_attn_in = scatter_tokens(mm_t(grad_projected, qkv))
         back_a, gain_grad_a = norm_back(grad_attn_in, normed_a, inv_a, gains[0])
         grad_start = grad_after_attn + back_a
-        result = after_cross + scatter_pair(*[mm_t(active, down) for active in activated])
-        output = natural_order(result.astype(BF))
+        result = after_cross + pair_order(
+            scatter_pair(*[mm_t(active, down) for active in activated])
+        )
+        output = layer_order(result.astype(BF))
 
         kv_grad = sum_data(kv_grad)
         kv_grads = place([(p, 0, 0) for p in swap_all([kv_grad] * 4)], rank, [group, group])
@@ -631,9 +634,9 @@
         query_grad, cross_out_grad = finish([(p, 0, 0) for p in parts], rank, [group] * 2)
         parts = swap_all(pick_rows(attn_rows, rank, 4))
         qkv_grad, out_grad = finish([(p, 0, 0) for p in parts], rank, [group], 3)
-        grad_hidden = natural_order(jnp.where(masked, 0.0, grad_start).astype(BF))
+        grad_hidden = layer_order(jnp.where(masked, 0.0, grad_start).astype(BF))
         mask_part = jnp.sum(jnp.where(masked, grad_start, 0.0), axis=0)
-        sums = natural_order(
+        sums = layer_order(
             sum_all(jnp.stack([gain_grad_a, gain_grad_b, gain_grad_c, mask_part]))
         )
         grad_cross = jnp.concatenate([query_grad[:, None], kv_weight_grad], axis=1)

time: 948 us -> 831 us (0.88)
  waiting for transfers between devices: 544 us -> 399 us
  local copies, waits for them, and re-layouts: 74 us -> 104 us
  starting transfers between devices: 145 us -> 128 us
  other arithmetic: 40.1 us -> 52.5 us
    all_gather x3, waiting for transfers between devices: 97.6 us -> 0.01 us  [gather_rows(): return lax.all_gather(rows, axes, axis=0, tiled=True)]
    reduce_scatter x3, waiting for transfers between devices: 52.4 us -> 12.8 us  [scatter_grad(): return lax.psum_scatter(partial, axes, scatter_dimension=0, tiled=True)]
    reshape x4 -> x14, local copies, waits for them, and re-layouts: 2.61 us -> 26.1 us  [the longest x10 16.8 us: swap_dims(): shaped = values.reshape(values.shape[:-1] + (z_size // 2, 2, 2, 2, -1))]
    ppermute x9, waiting for transfers between devices: 64.1 us -> 47.5 us  [sum_z(): lax.ppermute(values, z_axes, tuple(((k, k ^ m) for k in range(z_size))))]
    ppermute x100, starting transfers between devices: 112 us -> 99.4 us  [swap(): return lax.ppermute(values, axis, PAIR)]
    unnamed x142 -> x161, local copies, waits for them, and re-layouts: 27.1 us -> 33.8 us
  transfers between devices with their start and end apart: 126 -> 126, of which waited for: 82 -> 76; matrix products, arithmetic and copies ran while one was open for 17% -> 24% of each run, Pallas kernels for 4% -> 5%
where the time goes in v5:
time: 831 us; the launch traced here: 825 us
  waiting for transfers between devices  399 us (48%)
  starting transfers between devices  128 us (15%)
  local copies, waits for them, and re-layouts  104 us (13%)
  matrix products  67.3 us (8%)
  Pallas kernels  56.8 us (7%)
  other arithmetic  52.5 us (6%)
  between operations  16.9 us (2%)
    ppermute x100, waiting for transfers between devices, swap(): return lax.ppermute(values, axis, PAIR)  277 us
    ppermute x100, starting transfers between devices, swap(): return lax.ppermute(values, axis, PAIR)  99.4 us
    dot_general x22, matrix products, dot(): return lax.dot_general(a, b, (dims, ((), ())), preferred_element_type=F32)  67.3 us
    ppermute x10, waiting for transfers between devices, swap_diag(): return lax.ppermute(values, ('x', 'y'), DIAG)  53.9 us
    ppermute x9, waiting for transfers between devices, sum_z(): lax.ppermute(values, z_axes, tuple(((k, k ^ m) for k in range(z_size))))  47.5 us
    unnamed x161, local copies, waits for them, and re-layouts  33.8 us
    pallas_call x3, Pallas kernels, grad_products(): kernel_call(kernel, jax.ShapeDtypeStruct((width, total), BF), (width // r...  27.8 us
    pallas_call x9, Pallas kernels, block_call(): pl.pallas_call(kernel, out_shape=out_shape, grid_spec=pltpu.PrefetchScala...  18.5 us
  transfers between devices with their start and end apart: 126, of which 76 were waited for; matrix products, arithmetic and copies ran while one was open for 24% of the time, Pallas kernels for 5%

profile of v5, /device:TPU:0, one launch (start us, length us, event | category | flops | bytes accessed | tf_op | source)
XLA Modules:
  0.0 824.9 jit_solution(11275397629023835594)
XLA Ops:
  102.0 16.0 %collective-permute-done.19 = bf16[128,2048]{1,0:T(8,128)(2,1)S(1)} collective-permute-done((bf16[128,2048]{1,0:T(8,128)(2,1)}, bf16[128,2048]{1,0:T(8,128)(2,1)S(1)}, u32[]{:S(2)}, u32[]{:S(2)}) %collective-permute-start.19) | collective-permute-done | bytes 524320 | tf_op jit(solution)/shard_map/ppermute | solution.py:55
  129.1 25.1 %collective-permute-done.10 = bf16[64,1024]{1,0:T(8,128)(2,1)S(1)} collective-permute-done((bf16[64,1024]{1,0:T(8,128)(2,1)S(1)}, bf16[64,1024]{1,0:T(8,128)(2,1)S(1)}, u32[]{:S(2)}, u32[]{:S(2)}) %collective-permute-start.10) | collective-permute-done | bytes 131104 | tf_op jit(solution)/shard_map/ppermute | solution.py:437
  157.5 17.3 %collective-permute-done.8 = bf16[64,1024]{1,0:T(8,128)(2,1)S(1)} collective-permute-done((bf16[64,1024]{1,0:T(8,128)(2,1)S(1)}, bf16[64,1024]{1,0:T(8,128)(2,1)S(1)}, u32[]{:S(2)}, u32[]{:S(2)}) %collective-permute-start.8) | collective-permute-done | bytes 131104 | tf_op jit(solution)/shard_map/ppermute | solution.py:437
  184.9 9.2 %collective-permute-done.21 = bf16[128,2048]{1,0:T(8,128)(2,1)S(1)} collective-permute-done((bf16[128,2048]{1,0:T(8,128)(2,1)S(1)}, bf16[128,2048]{1,0:T(8,128)(2,1)S(1)}, u32[]{:S(2)}, u32[]{:S(2)}) %collective-permute-start.21) | collective-permute-done | bytes 524320 | tf_op jit(solution)/shard_map/ppermute | solution.py:55
  243.4 8.2 collective-permute-done.27
  257.0 8.0 collective-permute-done.29
  283.1 6.9 collective-permute-done.35
  293.1 8.1 collective-permute-done.38
  314.8 8.1 collective-permute-done.44
  325.2 8.1 collective-permute-done.47
  375.6 13.5 %grad_products.5 = bf16[2048,2048]{1,0:T(8,128)(2,1)} custom-call(bf16[512,2048]{1,0:T(8,128)(2,1)S(1)} %copy-done.17, bf16[512,2048]{1,0:T(8,128)(2,1)S(1)} %copy-done.16, bf16[512,2048]{1,0:T(8,128)(2,1)} %constant_dynamic-update-slice_fusion.20.refs_2_, bf16[512,2048]{1,0:T(8,128)(2,1)S(1)} %constant_dynamic-update-slice_fusion.25.refs_3_, ...), custom_call_target="tpu_custom_call" | custom-call | flops 8589934592 | bytes 4194304 | tf_op jit(solution)/shard_map/grad_products/pallas_call | solution.py:405
  411.2 6.9 collective-permute-done.59
  427.9 14.3 %collective-permute-done.60 = bf16[128,2048]{1,0:T(8,128)(2,1)} collective-permute-done((bf16[128,2048]{1,0:T(8,128)(2,1)}, bf16[128,2048]{1,0:T(8,128)(2,1)}, u32[]{:S(2)}, u32[]{:S(2)}) %collective-permute-start.60) | collective-permute-done | bytes 524320 | tf_op jit(solution)/shard_map/ppermute | solution.py:55
  461.0 10.9 %collective-permute-done.62 = bf16[128,2048]{1,0:T(8,128)(2,1)S(1)} collective-permute-done((bf16[128,2048]{1,0:T(8,128)(2,1)S(1)}, bf16[128,2048]{1,0:T(8,128)(2,1)S(1)}, u32[]{:S(2)}, u32[]{:S(2)}) %collective-permute-start.62) | collective-permute-done | bytes 524320 | tf_op jit(solution)/shard_map/ppermute | solution.py:55
  492.2 12.8 %reduce-scatter.4.cloned.1.call-done = bf16[512,2048]{1,0:T(8,128)(2,1)} async-done(((bf16[2048,2048]{1,0:T(8,128)(2,1)}), bf16[512,2048]{1,0:T(8,128)(2,1)}) %reduce-scatter.4.cloned.1.call-update) | async-done | bytes 2097168 | tf_op jit(solution)/shard_map/reduce_scatter | solution.py:422
  519.9 10.3 %collective-permute-done.68 = bf16[128,2048]{1,0:T(8,128)(2,1)S(1)} collective-permute-done((bf16[128,2048]{1,0:T(8,128)(2,1)S(1)}, bf16[128,2048]{1,0:T(8,128)(2,1)S(1)}, u32[]{:S(2)}, u32[]{:S(2)}) %collective-permute-start.68) | collective-permute-done | bytes 524320 | tf_op jit(solution)/shard_map/ppermute | solution.py:55
  535.5 8.5 %collective-permute-done.70 = bf16[128,2048]{1,0:T(8,128)(2,1)S(1)} collective-permute-done((bf16[128,2048]{1,0:T(8,128)(2,1)S(1)}, bf16[128,2048]{1,0:T(8,128)(2,1)S(1)}, u32[]{:S(2)}, u32[]{:S(2)}) %collective-permute-start.70) | collective-permute-done | bytes 524320 | tf_op jit(solution)/shard_map/ppermute | solution.py:55
  561.1 8.1 grad_products.3
  575.8 17.5 %collective-permute-done.118.refs_3_ = bf16[128,2048]{1,0:T(8,128)(2,1)S(1)} collective-permute-done((bf16[128,2048]{1,0:T(8,128)(2,1)S(1)}, bf16[128,2048]{1,0:T(8,128)(2,1)S(1)}, u32[]{:S(2)}, u32[]{:S(2)}) %collective-permute-start.118) | collective-permute-done | bytes 524320 | tf_op jit(solution)/shard_map/ppermute | solution.py:59
  596.0 46.2 %collective-permute-done.119.refs_4_ = bf16[256,2048]{1,0:T(8,128)(2,1)} collective-permute-done((bf16[256,2048]{1,0:T(8,128)(2,1)}, bf16[256,2048]{1,0:T(8,128)(2,1)}, u32[]{:S(2)}, u32[]{:S(2)}) %collective-permute-start.119) | collective-permute-done | bytes 1048608 | tf_op jit(solution)/shard_map/ppermute | solution.py:55
  660.7 7.1 fusion.112
  697.9 7.8 collective-permute-done.91.refs_1_
  744.2 9.8 %collective-permute-done.107 = f32[4,2048]{1,0:T(4,128)S(1)} collective-permute-done((f32[4,2048]{1,0:T(4,128)S(1)}, f32[4,2048]{1,0:T(4,128)S(1)}, u32[]{:S(2)}, u32[]{:S(2)}) %collective-permute-start.107) | collective-permute-done | bytes 32800 | tf_op jit(solution)/shard_map/ppermute | solution.py:55
  771.9 7.1 collective-permute-done.109
  (617 shorter events, 512.2 us)
Async XLA Ops:
  7.2 213.0 %all-gather.4.cloned.1.call-start = ((), (), s32[]{:S(2)}) async-start(), calls=%async_computation.3 | async-start | bytes 9437184 | tf_op jit(solution)/shard_map/all_gather | solution.py:418
  26.6 248.0 %all-gather.6.cloned.1.call-start = ((), (), s32[]{:S(2)}) async-start(), calls=%async_computation.4 | async-start | bytes 4718592 | tf_op jit(solution)/shard_map/all_gather | solution.py:418
  53.1 288.2 %all-gather.8.cloned.1.call-start = ((), (), s32[]{:S(2)}) async-start(), calls=%async_computation.5 | async-start | bytes 10485760 | tf_op jit(solution)/shard_map/all_gather | solution.py:418
  62.1 28.5 %collective-permute-start = (bf16[128,2048]{1,0:T(8,128)(2,1)}, bf16[128,2048]{1,0:T(8,128)(2,1)}, u32[]{:S(2)}, u32[]{:S(2)}) collective-permute-start(bf16[128,2048]{1,0:T(8,128)(2,1)} %get-tuple-element.173), channel_id=1, source_target_pairs={{0,1},{1,0},{2,3},{3,2},{4,5},{5,4},{6,7},{7,6},{8,9},{9,8},{10,11... | collective-permute-start | bytes 1572872 | tf_op jit(solution)/shard_map/ppermute | solution.py:55
  63.5 31.9 %collective-permute-start.1 = (bf16[128,2048]{1,0:T(8,128)(2,1)}, bf16[128,2048]{1,0:T(8,128)(2,1)}, u32[]{:S(2)}, u32[]{:S(2)}) collective-permute-start(bf16[128,2048]{1,0:T(8,128)(2,1)} %get-tuple-element.173), channel_id=1, source_target_pairs={{0,4},{4,0},{1,5},{5,1},{2,6},{6,2},{3,7},{7,3},{8,12},{12,8},{9,1... | collective-permute-start | bytes 1572872 | tf_op jit(solution)/shard_map/ppermute | solution.py:55
  83.8 35.7 %collective-permute-start.15 = (bf16[128,2048]{1,0:T(8,128)(2,1)}, bf16[128,2048]{1,0:T(8,128)(2,1)}, u32[]{:S(2)}, u32[]{:S(2)}) collective-permute-start(bf16[128,2048]{1,0:T(8,128)(2,1)} %reshape.325), channel_id=1, source_target_pairs={{0,1},{1,0},{2,3},{3,2},{4,5},{5,4},{6,7},{7,6},{8,9},{9,8},{10,11... | collective-permute-start | bytes 1572872 | tf_op jit(solution)/shard_map/ppermute | solution.py:55
  86.8 36.0 %collective-permute-start.16 = (bf16[128,2048]{1,0:T(8,128)(2,1)}, bf16[128,2048]{1,0:T(8,128)(2,1)}, u32[]{:S(2)}, u32[]{:S(2)}) collective-permute-start(bf16[128,2048]{1,0:T(8,128)(2,1)} %reshape.325), channel_id=1, source_target_pairs={{0,4},{4,0},{1,5},{5,1},{2,6},{6,2},{3,7},{7,3},{8,12},{12,8},{9,1... | collective-permute-start | bytes 1572872 | tf_op jit(solution)/shard_map/ppermute | solution.py:55
  90.5 27.5 %collective-permute-start.19 = (bf16[128,2048]{1,0:T(8,128)(2,1)}, bf16[128,2048]{1,0:T(8,128)(2,1)S(1)}, u32[]{:S(2)}, u32[]{:S(2)}) collective-permute-start(bf16[128,2048]{1,0:T(8,128)(2,1)} %reshape.325), channel_id=1, source_target_pairs={{0,8},{8,0},{1,9},{9,1},{2,10},{10,2},{3,11},{11,3},{4,12},{12,4},... | collective-permute-start | bytes 1572872 | tf_op jit(solution)/shard_map/ppermute | solution.py:55
  94.1 103.8 %collective-permute-start.39 = (bf16[256,2048]{1,0:T(8,128)(2,1)}, bf16[256,2048]{1,0:T(8,128)(2,1)S(1)}, u32[]{:S(2)}, u32[]{:S(2)}) collective-permute-start(bf16[256,2048]{1,0:T(8,128)(2,1)} %copy-done.20), channel_id=1, source_target_pairs={{0,8},{8,0},{1,9},{9,1},{2,10},{10,2},{3,11},{11,3},{4,12},{12,4},... | collective-permute-start | bytes 3145736 | tf_op jit(solution)/shard_map/ppermute | solution.py:55
  95.4 58.8 %collective-permute-start.10 = (bf16[64,1024]{1,0:T(8,128)(2,1)S(1)}, bf16[64,1024]{1,0:T(8,128)(2,1)S(1)}, u32[]{:S(2)}, u32[]{:S(2)}) collective-permute-start(bf16[64,1024]{1,0:T(8,128)(2,1)S(1)} %add_convert_fusion.11), channel_id=1, source_target_pairs={{0,24},{8,16},{16,8},{24,0},{1,25},{9,17},{17,9},{25,1},{2,26},{10... | collective-permute-start | bytes 393224 | tf_op jit(solution)/shard_map/ppermute | solution.py:437
  118.0 37.8 %collective-permute-start.9 = (bf16[64,1024]{1,0:T(8,128)(2,1)S(1)}, bf16[64,1024]{1,0:T(8,128)(2,1)S(1)}, u32[]{:S(2)}, u32[]{:S(2)}) collective-permute-start(bf16[64,1024]{1,0:T(8,128)(2,1)S(1)} %add_convert_fusion.11), channel_id=1, source_target_pairs={{0,16},{8,24},{16,0},{24,8},{1,17},{9,25},{17,1},{25,9},{2,18},{10... | collective-permute-start | bytes 393224 | tf_op jit(solution)/shard_map/ppermute | solution.py:437
  119.5 55.4 %collective-permute-start.8 = (bf16[64,1024]{1,0:T(8,128)(2,1)S(1)}, bf16[64,1024]{1,0:T(8,128)(2,1)S(1)}, u32[]{:S(2)}, u32[]{:S(2)}) collective-permute-start(bf16[64,1024]{1,0:T(8,128)(2,1)S(1)} %add_convert_fusion.11), channel_id=1, source_target_pairs={{0,8},{8,0},{16,24},{24,16},{1,9},{9,1},{17,25},{25,17},{2,10},{10... | collective-permute-start | bytes 393224 | tf_op jit(solution)/shard_map/ppermute | solution.py:437
  122.8 53.6 %collective-permute-start.2 = (bf16[64,2048]{1,0:T(8,128)(2,1)S(1)}, bf16[64,2048]{1,0:T(8,128)(2,1)S(1)}, u32[]{:S(2)}, u32[]{:S(2)}) collective-permute-start(bf16[64,2048]{1,0:T(8,128)(2,1)S(1)} %slice.496), channel_id=1, source_target_pairs={{0,1},{1,0},{2,3},{3,2},{4,5},{5,4},{6,7},{7,6},{8,9},{9,8},{10,11... | collective-permute-start | bytes 786440 | tf_op jit(solution)/shard_map/ppermute | solution.py:55
  154.2 24.5 %collective-permute-start.3 = (bf16[64,2048]{1,0:T(8,128)(2,1)S(1)}, bf16[64,2048]{1,0:T(8,128)(2,1)S(1)}, u32[]{:S(2)}, u32[]{:S(2)}) collective-permute-start(bf16[64,2048]{1,0:T(8,128)(2,1)S(1)} %slice.497), channel_id=1, source_target_pairs={{0,4},{4,0},{1,5},{5,1},{2,6},{6,2},{3,7},{7,3},{8,12},{12,8},{9,1... | collective-permute-start | bytes 786440 | tf_op jit(solution)/shard_map/ppermute | solution.py:55
  155.8 24.1 %collective-permute-start.17 = (bf16[64,2048]{1,0:T(8,128)(2,1)S(1)}, bf16[64,2048]{1,0:T(8,128)(2,1)S(1)}, u32[]{:S(2)}, u32[]{:S(2)}) collective-permute-start(bf16[64,2048]{1,0:T(8,128)(2,1)S(1)} %slice.504), channel_id=1, source_target_pairs={{0,1},{1,0},{2,3},{3,2},{4,5},{5,4},{6,7},{7,6},{8,9},{9,8},{10,11... | collective-permute-start | bytes 786440 | tf_op jit(solution)/shard_map/ppermute | solution.py:55
  217.7 287.3 %reduce-scatter.4.cloned.1.call-start = ((), (), s32[]{:S(2)}) async-start(), calls=%async_computation.6 | async-start | bytes 10485760 | tf_op jit(solution)/shard_map/reduce_scatter | solution.py:422
  389.1 181.2 %reduce-scatter.6.cloned.1.call-start = ((), (), s32[]{:S(2)}) async-start(), calls=%async_computation.7 | async-start | bytes 4718592 | tf_op jit(solution)/shard_map/reduce_scatter | solution.py:422
  505.0 286.0 %reduce-scatter.8.cloned.1.call-start = ((), (), s32[]{:S(2)}) async-start(), calls=%async_computation.8 | async-start | bytes 9437184 | tf_op jit(solution)/shard_map/reduce_scatter | solution.py:422
  596.0 46.3 %collective-permute-start.119 = (bf16[256,2048]{1,0:T(8,128)(2,1)}, bf16[256,2048]{1,0:T(8,128)(2,1)}, u32[]{:S(2)}, u32[]{:S(2)}) collective-permute-start(bf16[256,2048]{1,0:T(8,128)(2,1)} %pad_maximum_fusion.2), channel_id=1, source_target_pairs={{0,8},{8,0},{1,9},{9,1},{2,10},{10,2},{3,11},{11,3},{4,12},{12,4},... | collective-permute-start | bytes 3145736 | tf_op jit(solution)/shard_map/ppermute | solution.py:55
  651.8 25.6 %collective-permute-start.77 = (bf16[64,2048]{1,0:T(8,128)(2,1)S(1)}, bf16[64,2048]{1,0:T(8,128)(2,1)S(1)}, u32[]{:S(2)}, u32[]{:S(2)}) collective-permute-start(bf16[64,2048]{1,0:T(8,128)(2,1)S(1)} %get-tuple-element.208), channel_id=1, source_target_pairs={{0,1},{1,0},{2,3},{3,2},{4,5},{5,4},{6,7},{7,6},{8,9},{9,8},{10,11... | collective-permute-start | bytes 786440 | tf_op jit(solution)/shard_map/ppermute | solution.py:55
  652.5 26.2 %collective-permute-start.79 = (bf16[64,2048]{1,0:T(8,128)(2,1)S(1)}, bf16[64,2048]{1,0:T(8,128)(2,1)S(1)}, u32[]{:S(2)}, u32[]{:S(2)}) collective-permute-start(bf16[64,2048]{1,0:T(8,128)(2,1)S(1)} %get-tuple-element.209), channel_id=1, source_target_pairs={{0,4},{4,0},{1,5},{5,1},{2,6},{6,2},{3,7},{7,3},{8,12},{12,8},{9,1... | collective-permute-start | bytes 786440 | tf_op jit(solution)/shard_map/ppermute | solution.py:55
  685.5 71.7 %collective-permute-start.80 = (bf16[128,2048]{1,0:T(8,128)(2,1)}, bf16[128,2048]{1,0:T(8,128)(2,1)}, u32[]{:S(2)}, u32[]{:S(2)}) collective-permute-start(bf16[128,2048]{1,0:T(8,128)(2,1)} %pad_maximum_fusion.18), channel_id=1, source_target_pairs={{0,1},{1,0},{2,3},{3,2},{4,5},{5,4},{6,7},{7,6},{8,9},{9,8},{10,11... | collective-permute-start | bytes 1572872 | tf_op jit(solution)/shard_map/ppermute | solution.py:55
  687.5 70.3 %collective-permute-start.78 = (bf16[128,2048]{1,0:T(8,128)(2,1)}, bf16[128,2048]{1,0:T(8,128)(2,1)}, u32[]{:S(2)}, u32[]{:S(2)}) collective-permute-start(bf16[128,2048]{1,0:T(8,128)(2,1)} %pad_maximum_fusion.17), channel_id=1, source_target_pairs={{0,4},{4,0},{1,5},{5,1},{2,6},{6,2},{3,7},{7,3},{8,12},{12,8},{9,1... | collective-permute-start | bytes 1572872 | tf_op jit(solution)/shard_map/ppermute | solution.py:55
  737.1 43.9 %collective-permute-start.76 = (bf16[128,2048]{1,0:T(8,128)(2,1)}, bf16[128,2048]{1,0:T(8,128)(2,1)S(1)}, u32[]{:S(2)}, u32[]{:S(2)}) collective-permute-start(bf16[128,2048]{1,0:T(8,128)(2,1)} %pad_maximum_fusion.16), channel_id=1, source_target_pairs={{0,1},{1,0},{2,3},{3,2},{4,5},{5,4},{6,7},{7,6},{8,9},{9,8},{10,11... | collective-permute-start | bytes 1572872 | tf_op jit(solution)/shard_map/ppermute | solution.py:55
  (167 other events, 1860.4 us)
Sparse Core Ops, SparseCore 0:
  26.7 90.0 all-gather.3
  119.0 65.0 all-gather.5
  217.8 106.0 all-gather.7
  389.2 115.6 reduce-scatter.3
  507.2 48.9 reduce-scatter.5
  570.4 110.6 reduce-scatter.7

commit v6 on v5

v6 whole, which is shorter than its diff:
```python
import math

import jax
import jax.numpy as jnp
from jax import lax
from jax.experimental import pallas as pl
from jax.experimental.pallas import tpu as pltpu
from jax.sharding import Mesh
from jax.sharding import PartitionSpec as P

HD = 128
EPS = 1e-05
BF = jnp.bfloat16
F32 = jnp.float32
PAIR = ((0, 1), (1, 0))
GROUP = ("x", "y")
DATA = ("w", "z", "c")
PAIR_DATA = ("w", "c")
VMEM = 48 * 1024 * 1024
SCALE = 1.0 / math.sqrt(HD)
SLOPE = math.sqrt(2.0 / math.pi)
CUBIC = 0.044715


def dot(a, b, dims):
    return lax.dot_general(a, b, (dims, ((), ())), preferred_element_type=F32)


def mm(a, b):
    return dot(a, b, ((1,), (0,)))


def mm_t(a, b):
    return dot(a, b, ((1,), (1,)))


def t_mm(a, b):
    return dot(a, b, ((0,), (0,)))


def shape(dims, dtype=BF):
    return jax.ShapeDtypeStruct(dims, dtype)


def swap(values, axis):
    return lax.ppermute(values, axis, PAIR)


def trade(blocks, axes=GROUP):
    return lax.all_to_all(blocks, axes, 0, 0, tiled=True)


def spread(values, axes=GROUP, count=4):
    return trade(jnp.broadcast_to(values[None], (count,) + values.shape), axes)


def gather_tokens(own):
    half = own.shape[0] // 2
    from_x = swap(own, "x")
    from_y = swap(own, "y")
    return own, from_y, from_x, swap(from_x[:half], "y"), swap(from_y[half:], "x")


def scatter_tokens(parts):
    own, for_y, for_x, for_low, for_high = parts
    half = for_low.shape[0]
    low = swap(for_low, "y").astype(F32) + for_x[:half].astype(F32)
    high = swap(for_high, "x").astype(F32) + for_y[half:].astype(F32)
    from_x = swap(jnp.concatenate([low.astype(BF), for_x[half:]], axis=0), "x")
    from_y = swap(jnp.concatenate([for_y[:half], high.astype(BF)], axis=0), "y")
    return [own, from_x, from_y]


def gather_rows(rows, axes):
    return lax.all_gather(rows, axes, axis=0, tiled=True)


def scatter_grad(partial, axes):
    return lax.psum_scatter(partial, axes, scatter_dimension=0, tiled=True)


def call(kernel, grid, in_specs, out_specs, out_shape, operands, name, flops=0, size=1 << 22,
         rank=None, scratch=()):
    options = dict(
        out_shape=out_shape,
        compiler_params=pltpu.CompilerParams(vmem_limit_bytes=VMEM),
        cost_estimate=pl.CostEstimate(flops=flops, bytes_accessed=size, transcendentals=0),
        name=name,
    )
    if rank is None:
        return pl.pallas_call(
            kernel, grid=grid, in_specs=in_specs, out_specs=out_specs, scratch_shapes=scratch,
            **options,
        )(*operands)
    spec = pltpu.PrefetchScalarGridSpec(
        num_scalar_prefetch=1,
        grid=grid,
        in_specs=in_specs,
        out_specs=out_specs,
        scratch_shapes=scratch,
    )
    return pl.pallas_call(kernel, grid_spec=spec, **options)(rank.reshape(1), *operands)


def whole(array):
    return pl.BlockSpec(array.shape, lambda *_: (0,) * len(array.shape))


def reorder(values, unit, order):
    if order is None:
        return values
    return jnp.concatenate([values[:, k * unit : (k + 1) * unit] for k in order], axis=1)


def assemble(target, pieces, rank, unit, order):
    rows, half = pieces[0].shape[0], pieces[3].shape[0]
    for k in range(3):
        at = pl.multiple_of((rank ^ k) * rows, rows)
        target[pl.ds(at, rows), :] = reorder(pieces[k][...], unit, order)
    at = pl.multiple_of((rank ^ 3) * rows, rows)
    target[pl.ds(at, half), :] = reorder(pieces[3][...], unit, order)
    target[pl.ds(pl.multiple_of(at + half, half), half), :] = reorder(pieces[4][...], unit, order)


def gather_mm(pieces, rank, weight, first, columns, name):
    rows, width = pieces[0].shape
    step = 256

    def kernel(r, *refs):
        tokens, out = refs[6], refs[7]

        @pl.when(pl.program_id(0) == 0)
        def _():
            assemble(tokens, refs[:5], r[0], width, None)

        out[...] = mm(tokens[...], refs[5][...]).astype(BF)

    return call(
        kernel,
        (columns // step,),
        [whole(p) for p in pieces]
        + [pl.BlockSpec((width, step), lambda j, r: (0, first // step + j))],
        [
            pl.BlockSpec((4 * rows, width), lambda j, r: (0, 0)),
            pl.BlockSpec((4 * rows, step), lambda j, r: (0, j)),
        ],
        [shape((4 * rows, width)), shape((4 * rows, columns))],
        [*pieces, weight],
        name,
        flops=8 * rows * width * columns,
        size=2 * width * (columns + 8 * rows),
        rank=rank,
    )


def mm_scatter(values, rank, weight, first, name, unit=0, order=None):
    tokens, depth = values.shape
    rows = tokens // 4
    width = weight.shape[0]
    step = unit if order is not None else 512
    place = (lambda j: j) if order is None else (lambda j: pair_index(j))

    def kernel(r, x, w, own, for_y, for_x, low, high, total):
        total[...] = mm_t(x[...], w[...])

        def block(k):
            return total[pl.ds(pl.multiple_of((r[0] ^ k) * rows, rows), rows), :]

        own[...] = block(0)
        for_y[...] = block(1).astype(BF)
        for_x[...] = block(2).astype(BF)
        diagonal = block(3).astype(BF)
        low[...] = diagonal[: rows // 2]
        high[...] = diagonal[rows // 2 :]

    sizes = [rows, rows, rows, rows // 2, rows // 2]
    return call(
        kernel,
        (width // step,),
        [
            pl.BlockSpec((tokens, depth), lambda j, r: (0, 0)),
            pl.BlockSpec((step, depth), lambda j, r: (j, first // depth)),
        ],
        [pl.BlockSpec((n, step), lambda j, r: (0, place(j))) for n in sizes],
        [shape((n, width), F32 if k == 0 else BF) for k, n in enumerate(sizes)],
        [values, weight],
        name,
        flops=2 * tokens * depth * width,
        size=2 * width * (depth + 6 * rows),
        rank=rank,
        scratch=[pltpu.VMEM((tokens, step), F32)],
    )


def pair_index(j):
    return ((j >> 2) << 2) | ((j & 1) << 1) | ((j >> 1) & 1)


def normalize(values):
    centred = values - jnp.mean(values, axis=-1, keepdims=True)
    inv_std = lax.rsqrt(jnp.mean(centred * centred, axis=-1, keepdims=True) + EPS)
    return centred * inv_std, inv_std


NORM_ROWS = 32


def row_spec(array, at=None):
    width = array.shape[-1]
    if at is None:
        return pl.BlockSpec((NORM_ROWS, width), lambda i: (i, 0))
    return pl.BlockSpec((1, NORM_ROWS, width), lambda i, at=at: (at, i, 0))


def terms_of(terms):
    arrays, specs = [], []
    for term in terms:
        array, at = term if isinstance(term, tuple) else (term, None)
        arrays.append(array)
        specs.append(row_spec(array, at))
    return arrays, specs


def total_of(refs):
    values = [ref[0] if len(ref.shape) == 3 else ref[...] for ref in refs]
    return sum(value.astype(F32) for value in values)


def add_norm(terms, gain):
    arrays, specs = terms_of(terms)
    tokens, width = arrays[0].shape[-2], arrays[0].shape[-1]
    tokens = min(a.shape[-2] for a in arrays)

    def kernel(*refs):
        gain_ref, x, out = refs[-3:]
        values = total_of(refs[:-3])
        x[...] = values
        out[...] = (normalize(values)[0] * gain_ref[...]).astype(BF)

    return call(
        kernel,
        (tokens // NORM_ROWS,),
        specs + [whole(gain)],
        [row_spec(shape((tokens, width)))] * 2,
        [shape((tokens, width), F32), shape((tokens, width))],
        [*arrays, gain],
        "add_norm",
    )


def norm_grad(grad, values, gain):
    normed, inv_std = normalize(values)
    scaled = grad * gain
    first_mean = jnp.mean(scaled, axis=-1, keepdims=True)
    second_mean = jnp.mean(scaled * normed, axis=-1, keepdims=True)
    return (
        inv_std * (scaled - first_mean - normed * second_mean),
        jnp.sum(grad * normed, axis=0, keepdims=True),
    )


def accumulate(ref, value):
    @pl.when(pl.program_id(0) == 0)
    def _():
        ref[...] = jnp.zeros_like(ref)

    ref[...] += value


def norm_back(terms, upper, values, gain):
    arrays, specs = terms_of(terms)
    tokens, width = values.shape

    def kernel(*refs):
        upper_ref, x, gain_ref, out, out_low, gain_grad = refs[-6:]
        back, part = norm_grad(total_of(refs[:-6]), x[...], gain_ref[...])
        result = upper_ref[...].astype(F32) + back
        out[...] = result
        out_low[...] = result.astype(BF)
        accumulate(gain_grad, part)

    return call(
        kernel,
        (tokens // NORM_ROWS,),
        specs + [row_spec(upper), row_spec(values), whole(gain)],
        [row_spec(values)] * 2 + [pl.BlockSpec((1, width), lambda i: (0, 0))],
        [shape((tokens, width), F32), shape((tokens, width)), shape((1, width), F32)],
        [*arrays, upper, values, gain],
        "norm_back",
    )


def last_back(terms, upper, values, gain, masked, unit, order):
    arrays, specs = terms_of(terms)
    tokens, width = values.shape

    def kernel(*refs):
        upper_ref, x, gain_ref, mask, out, gain_grad, mask_grad = refs[-7:]
        back, part = norm_grad(total_of(refs[:-7]), x[...], gain_ref[...])
        result = upper_ref[...].astype(F32) + back
        hit = mask[...] > 0.5
        out[...] = reorder(jnp.where(hit, 0.0, result).astype(BF), unit, order)
        accumulate(gain_grad, part)
        accumulate(mask_grad, jnp.sum(jnp.where(hit, result, 0.0), axis=0, keepdims=True))

    line = pl.BlockSpec((1, width), lambda i: (0, 0))
    return call(
        kernel,
        (tokens // NORM_ROWS,),
        specs + [row_spec(upper), row_spec(values), whole(gain), row_spec(masked)],
        [row_spec(values), line, line],
        [shape((tokens, width)), shape((1, width), F32), shape((1, width), F32)],
        [*arrays, upper, values, gain, masked],
        "last_back",
    )


def start(hidden, cotangent, masked, embed, gain, unit, order):
    tokens, width = hidden.shape

    def kernel(hid, cot, mask, embed_ref, gain_ref, x, out, grad):
        hit = mask[...] > 0.5
        values = jnp.where(
            hit, embed_ref[...], reorder(hid[...], unit, order).astype(F32)
        )
        x[...] = values
        out[...] = (normalize(values)[0] * gain_ref[...]).astype(BF)
        grad[...] = jnp.where(hit, reorder(cot[...], unit, order).astype(F32), 0.0).astype(BF)

    rows = row_spec(hidden)
    return call(
        kernel,
        (tokens // NORM_ROWS,),
        [rows, rows, row_spec(masked), whole(embed), whole(gain)],
        [rows] * 3,
        [shape((tokens, width), F32), shape((tokens, width)), shape((tokens, width))],
        [hidden, cotangent, masked, embed, gain],
        "start",
    )


def layer_output(upper, terms, pair_unit, pair_order, unit, order):
    arrays, specs = terms_of(terms)
    tokens, width = upper.shape

    def kernel(*refs):
        values = refs[-2][...] + reorder(total_of(refs[:-2]), pair_unit, pair_order)
        refs[-1][...] = reorder(values.astype(BF), unit, order)

    return call(
        kernel,
        (tokens // NORM_ROWS,),
        specs + [row_spec(upper)],
        row_spec(upper),
        shape((tokens, width)),
        [*arrays, upper],
        "layer_output",
    )


def feed_forward(pieces, grad_y, side, rank, weight, unit, order):
    rows, width = pieces[0].shape
    hidden = weight.shape[1] // 2
    step = 256

    def kernel(r, *refs):
        dy, up, down, tokens, grads, act, pre = refs[5:]

        @pl.when(pl.program_id(0) == 0)
        def _():
            assemble(tokens, refs[:5], r[0], unit, order)
            for k in range(4):
                grads[k * rows : (k + 1) * rows, :] = reorder(dy[k], unit, order)

        u = mm(tokens[...], up[...])
        square = u * u
        bend = jnp.tanh(SLOPE * u * (1.0 + CUBIC * square))
        half = 0.5 * (1.0 + bend)
        act[...] = (u * half).astype(BF)
        slope = half + 0.5 * u * (1.0 - bend * bend) * SLOPE * (1.0 + 3.0 * CUBIC * square)
        pre[...] = (mm(grads[...], down[...]) * slope).astype(BF)

    full = pl.BlockSpec((4 * rows, width), lambda j, r: (0, 0))
    part = pl.BlockSpec((4 * rows, step), lambda j, r: (0, j))
    return call(
        kernel,
        (hidden // step,),
        [whole(p) for p in pieces]
        + [
            pl.BlockSpec((4, rows, width), lambda j, r: (0, side, 0)),
            pl.BlockSpec((width, step), lambda j, r: (0, j)),
            pl.BlockSpec((width, step), lambda j, r: (0, hidden // step + j)),
        ],
        [full, full, part, part],
        [shape((4 * rows, width))] * 2 + [shape((4 * rows, hidden))] * 2,
        [*pieces, grad_y, weight, weight],
        "feed_forward",
        flops=16 * rows * width * hidden,
        size=4 * width * (hidden + 8 * rows),
        rank=rank,
    )


def softmax(scores):
    exp_terms = jnp.exp(scores - jnp.max(scores, axis=-1, keepdims=True))
    return exp_terms / jnp.sum(exp_terms, axis=-1, keepdims=True)


def score_grad(probs, grad_probs):
    return (
        probs * (grad_probs - jnp.sum(probs * grad_probs, axis=-1, keepdims=True))
    ).astype(BF)


def head(ref, k):
    return ref[:, k * HD : (k + 1) * HD]


def self_forward(projected, images):
    tokens, width = projected.shape
    rows, group = tokens // images, width // 3
    heads = group // HD

    def kernel(proj, mixed):
        for k in range(heads):
            query, key, value = (head(proj, j * heads + k) for j in range(3))
            probs = softmax(mm_t(query, key) * SCALE).astype(BF)
            mixed[:, k * HD : (k + 1) * HD] = mm(probs, value).astype(BF)

    return call(
        kernel,
        (images,),
        [pl.BlockSpec((rows, width), lambda i: (i, 0))],
        pl.BlockSpec((rows, group), lambda i: (i, 0)),
        shape((tokens, group)),
        [projected],
        "self_forward",
        flops=4 * tokens * rows * group,
    )


def self_back(projected, grad_mixed, images):
    tokens, width = projected.shape
    rows, group = tokens // images, width // 3
    heads = group // HD

    def kernel(proj, grad, out):
        for k in range(heads):
            query, key, value = (head(proj, j * heads + k) for j in range(3))
            grad_head = head(grad, k)
            probs = softmax(mm_t(query, key) * SCALE)
            grad_scores = score_grad(probs, mm_t(grad_head, value))
            parts = (
                mm(grad_scores, key) * SCALE,
                t_mm(grad_scores, query) * SCALE,
                t_mm(probs.astype(BF), grad_head),
            )
            for j, part in enumerate(parts):
                at = (j * heads + k) * HD
                out[:, at : at + HD] = part.astype(BF)

    return call(
        kernel,
        (images,),
        [
            pl.BlockSpec((rows, width), lambda i: (i, 0)),
            pl.BlockSpec((rows, group), lambda i: (i, 0)),
        ],
        pl.BlockSpec((rows, width), lambda i: (i, 0)),
        shape((tokens, width)),
        [projected, grad_mixed],
        "self_back",
        flops=10 * tokens * rows * group,
    )


def cross_forward(queries, text_kv):
    tokens, group = queries.shape
    heads = group // HD

    def kernel(query, text, mixed):
        for k in range(heads):
            probs = softmax(mm_t(head(query, k), head(text, k)) * SCALE).astype(BF)
            mixed[:, k * HD : (k + 1) * HD] = mm(probs, head(text, heads + k)).astype(BF)

    return call(
        kernel,
        (1,),
        [whole(queries), whole(text_kv)],
        whole(queries),
        shape((tokens, group)),
        [queries, text_kv],
        "cross_forward",
        flops=4 * tokens * text_kv.shape[0] * group,
    )


def cross_back(queries, text_kv, grad_mixed):
    tokens, group = queries.shape
    context = text_kv.shape[0]
    heads = group // HD

    def kernel(query, text, grad, grad_query, grad_text):
        for k in range(heads):
            query_head, key, value = head(query, k), head(text, k), head(text, heads + k)
            grad_head = head(grad, k)
            probs = softmax(mm_t(query_head, key) * SCALE)
            grad_scores = score_grad(probs, mm_t(grad_head, value))
            grad_query[:, k * HD : (k + 1) * HD] = (mm(grad_scores, key) * SCALE).astype(BF)
            at = (heads + k) * HD
            grad_text[:, k * HD : (k + 1) * HD] = t_mm(grad_scores, query_head) * SCALE
            grad_text[:, at : at + HD] = t_mm(probs.astype(BF), grad_head)

    return call(
        kernel,
        (1,),
        [whole(queries), whole(text_kv), whole(grad_mixed)],
        [whole(queries), whole(text_kv)],
        [shape((tokens, group)), shape((context, 2 * group), F32)],
        [queries, text_kv, grad_mixed],
        "cross_back",
        flops=10 * tokens * context * group,
    )


def grad_products(pairs, name):
    blocks = len(pairs[0][0])
    tokens, width = pairs[0][0][0].shape
    widths = [y[0].shape[1] for _, y in pairs]
    total = sum(widths)
    rows = 256
    step = 512
    count = len(pairs) * blocks

    def kernel(*refs):
        out = refs[2 * count]
        offset = 0
        for k, wide in enumerate(widths):
            left = [refs[k * blocks + b][...].T for b in range(blocks)]
            for at in range(0, wide, step):
                out[:, offset + at : offset + at + step] = sum(
                    mm(left[b], refs[count + k * blocks + b][:, at : at + step])
                    for b in range(blocks)
                ).astype(BF)
            offset += wide

    return call(
        kernel,
        (width // rows,),
        [pl.BlockSpec((tokens, rows), lambda i: (0, i))] * count
        + [pl.BlockSpec((tokens, w), lambda i: (0, 0)) for w in widths for _ in range(blocks)],
        pl.BlockSpec((rows, total), lambda i: (i, 0)),
        shape((width, total)),
        [b for x, _ in pairs for b in x] + [b for _, y in pairs for b in y],
        name,
        flops=2 * tokens * blocks * width * total,
        size=4 * width * total,
    )


def finish_pair(near, far, z):
    count, rows, total = near.shape
    width = total // 2

    def kernel(r, near_ref, far_ref, first, second):
        step = pl.program_id(0)
        for side, ref in enumerate((near_ref, far_ref)):

            @pl.when(step // count == side)
            def _():
                block = ref[lax.rem(step, count)].astype(F32)
                first[...] = block[:, :width]
                second[...] = block[:, width:]

    out = pl.BlockSpec((rows, width), lambda k, r: (0, ((k // count) ^ r[0]) * count + k % count))
    return call(
        kernel,
        (2 * count,),
        [whole(near), whole(far)],
        [out, out],
        [shape((rows, 2 * count * width), F32)] * 2,
        [near, far],
        "finish_pair",
        rank=z,
    )


def finish_attention(blocks):
    count, rows, total = blocks.shape
    width = total // 4

    def kernel(ref, three, one):
        for j in range(3):
            three[:, j, :] = ref[0, :, j * width : (j + 1) * width].astype(F32)
        one[...] = ref[0, :, 3 * width :].astype(F32)

    return call(
        kernel,
        (count,),
        [pl.BlockSpec((1, rows, total), lambda k: (k, 0, 0))],
        [
            pl.BlockSpec((rows, 3, width), lambda k: (0, 0, k)),
            pl.BlockSpec((rows, width), lambda k: (0, k)),
        ],
        [shape((rows, 3, count * width), F32), shape((rows, count * width), F32)],
        [blocks],
        "finish_attention",
    )


def finish_cross(blocks, text_grad):
    count, rows, total = blocks.shape
    width = total // 2

    def kernel(ref, key, value, three, one):
        three[:, 0, :] = ref[0, :, :width].astype(F32)
        three[:, 1, :] = key[...]
        three[:, 2, :] = value[...]
        one[...] = ref[0, :, width:].astype(F32)

    return call(
        kernel,
        (count,),
        [
            pl.BlockSpec((1, rows, total), lambda k: (k, 0, 0)),
            pl.BlockSpec((rows, width), lambda k: (0, k)),
            pl.BlockSpec((rows, width), lambda k: (0, count + k)),
        ],
        [
            pl.BlockSpec((rows, 3, width), lambda k: (0, 0, k)),
            pl.BlockSpec((rows, width), lambda k: (0, k)),
        ],
        [shape((rows, 3, count * width), F32), shape((rows, count * width), F32)],
        [blocks, text_grad, text_grad],
        "finish_cross",
    )


def column_blocks(weight, count):
    rows = weight.shape[0]
    return weight.reshape(rows, count, -1).transpose(1, 0, 2)


def make_local(z_size):
    z_axes = ("w", "z")

    def sum_data(values):
        rows, columns = values.shape
        core = lax.axis_index("c")
        halves = values.reshape(2, rows // 2, columns)
        keep = lax.dynamic_index_in_dim(halves, core, 0, keepdims=False)
        send = lax.dynamic_index_in_dim(halves, 1 - core, 0, keepdims=False)
        mine = (keep + swap(send, "c")).astype(BF).reshape(z_size, -1, columns)
        mine = trade(mine, z_axes).astype(F32).sum(axis=0).astype(BF)
        mine = spread(mine, z_axes, z_size).reshape(rows // 2, columns)
        other = swap(mine, "c")
        return jnp.concatenate(
            [jnp.where(core == 0, mine, other), jnp.where(core == 0, other, mine)], axis=0
        )

    def sum_all(values):
        for axis in ("c", "x", "y", "z"):
            values = values + swap(values, axis)
        step = 1
        while 2 * step < z_size:
            values = values + lax.ppermute(
                values, "w", tuple((k, k ^ step) for k in range(z_size // 2))
            )
            step *= 2
        return values

    def swap_dims(values, first):
        shaped = values.reshape(values.shape[:-1] + (z_size // 2, 2, 2, 2, -1))
        at = values.ndim - 1 + first
        return jnp.swapaxes(shaped, at, at + 1).reshape(values.shape)

    def layer_order(values):
        return swap_dims(values, 2)

    def pair_order(values):
        return swap_dims(values, 1)

    def local(
        hidden,
        mask_index,
        mask_count,
        mask_embed,
        norm_gains,
        caption,
        w_qkv,
        w_out,
        w_cross,
        w_cross_out,
        w_text,
        w_up,
        w_down,
        cotangent,
    ):
        images, local_rows, width = hidden.shape
        full_length = mask_index.shape[1]
        shard_rows = w_qkv.shape[0]
        rank = lax.axis_index("x") * 2 + lax.axis_index("y")
        z = lax.axis_index("z")
        tokens = images * local_rows
        group = width // 4
        text_width = caption.shape[1]

        unit, pair_unit = width // (4 * z_size), width // (2 * z_size)
        inside = unit % 128 == 0
        order = [pair_index(k) for k in range(4 * z_size)] if inside else None
        pair = [pair_index(k) for k in range(2 * z_size)] if inside else None

        def outer(values, change):
            return values if inside else change(values)

        first = jnp.concatenate(
            [
                w_qkv.reshape(shard_rows, 3, 4, group)
                .transpose(2, 0, 1, 3)
                .reshape(4, shard_rows, 3 * group),
                column_blocks(w_out, 4),
            ],
            axis=2,
        )
        first = gather_rows(trade(first).reshape(4 * shard_rows, 4 * group), DATA)
        wide = jnp.concatenate([column_blocks(w_up, 8), column_blocks(w_down, 8)], axis=2)
        wide = wide.reshape(2, 4, shard_rows, -1)
        wide_near = lax.dynamic_index_in_dim(wide, z, 0, keepdims=False)
        wide_far = swap(lax.dynamic_index_in_dim(wide, 1 - z, 0, keepdims=False), "z")
        mid = jnp.concatenate([column_blocks(w_cross[:, 0], 4), column_blocks(w_cross_out, 4)], axis=2)
        mid = gather_rows(trade(mid).reshape(4 * shard_rows, 2 * group), DATA)
        wide_near, wide_far = trade(wide_near), trade(wide_far)
        mlp = jnp.concatenate(
            [jnp.where(z == 0, wide_near, wide_far), jnp.where(z == 0, wide_far, wide_near)],
            axis=0,
        )
        mlp = gather_rows(mlp.reshape(8 * shard_rows, -1), PAIR_DATA)

        positions = lax.axis_index("y") * local_rows + jnp.arange(local_rows, dtype=jnp.int32)
        ranks = jnp.arange(full_length, dtype=jnp.int32)
        matches = (mask_index[:, :, None] == positions[None, None, :]) & (
            ranks[None, :, None] < mask_count[:, None, None]
        )
        masked = jnp.any(matches, axis=1).reshape(tokens, 1).astype(F32)
        gains = layer_order(norm_gains)
        gain_a, gain_b, gain_c = gains[:1], gains[1:2], gains[2:]
        start_x, attn_in, grad_top = start(
            outer(hidden.reshape(tokens, width), layer_order),
            outer(cotangent.reshape(tokens, width), layer_order),
            masked,
            layer_order(mask_embed)[None],
            gain_a,
            unit,
            order,
        )
        attn_in = gather_tokens(attn_in)

        own_text = mm_t(caption, w_text).astype(BF)
        kv_rows = w_cross[:, 1:].reshape(shard_rows, 2 * width)
        kv_part = mm(own_text, kv_rows).astype(BF)
        kv_part = kv_part.reshape(-1, 2, 4, group).transpose(2, 0, 1, 3).reshape(4, -1, 2 * group)
        text_kv = sum_data(trade(kv_part).astype(F32).sum(axis=0))
        attn_in, text_kv = lax.optimization_barrier((attn_in, text_kv))

        grad_y = outer(grad_top, pair_order)
        grad_y = jnp.concatenate([grad_y, swap(grad_y, "z")], axis=0)
        grad_y = spread(grad_y)

        attn_in, projected = gather_mm(attn_in, rank, first, 0, 3 * group, "qkv_mm")
        self_mixed = self_forward(projected, 2 * images)
        self_mixed, grad_y = lax.optimization_barrier((self_mixed, grad_y))
        parts = scatter_tokens(mm_scatter(self_mixed, rank, first, 3 * group, "out_mm"))
        after_attn, cross_in = add_norm([start_x] + parts, gain_b)

        cross_in, cross_queries = gather_mm(gather_tokens(cross_in), rank, mid, 0, group, "query_mm")
        cross_mixed = cross_forward(cross_queries, text_kv)
        parts = scatter_tokens(mm_scatter(cross_mixed, rank, mid, group, "cross_out_mm"))
        after_cross, mlp_in = add_norm([after_attn] + parts, gain_c)

        mlp_in = outer(mlp_in, pair_order)
        mlp_in = [gather_tokens(mlp_in), gather_tokens(swap(mlp_in, "z"))]
        runs = [
            feed_forward(mlp_in[side], grad_y, side, rank, mlp, pair_unit, pair)
            for side in range(2)
        ]
        mlp_in, mlp_grad_y, activated, grad_pre = zip(*runs)
        back = [mm_scatter(grad_pre[s], rank, mlp, 0, "up_back", pair_unit, pair) for s in range(2)]
        back, grad_pre = lax.optimization_barrier((back, grad_pre))
        mlp_part = grad_products([(mlp_grad_y, activated), (mlp_in, grad_pre)], "mlp_grads")
        mlp_rows = scatter_grad(mlp_part, PAIR_DATA)
        near = scatter_tokens(back[0])
        far = sum(part.astype(F32) for part in scatter_tokens(back[1])).astype(BF)
        terms = near + [swap(far, "z")]
        if not inside:
            terms = [pair_order(sum(part.astype(F32) for part in terms))]
        grad_after_cross, cross_branch, gain_grad_c = norm_back(terms, grad_top, after_cross, gain_c)

        cross_branch, grad_cross_mixed = gather_mm(
            gather_tokens(cross_branch), rank, mid, group, group, "cross_out_back"
        )
        grad_cq, kv_grad = cross_back(cross_queries, text_kv, grad_cross_mixed)
        parts = scatter_tokens(mm_scatter(grad_cq, rank, mid, 0, "query_back"))
        grad_after_attn, attn_branch, gain_grad_b = norm_back(
            parts, grad_after_cross, after_attn, gain_b
        )
        cross_part = grad_products(
            [([cross_in], [grad_cq]), ([cross_branch], [cross_mixed])], "cross_grads"
        )
        cross_part, mlp_rows = lax.optimization_barrier((cross_part, mlp_rows))
        cross_rows = scatter_grad(cross_part, DATA)

        attn_branch, grad_self_mixed = gather_mm(
            gather_tokens(attn_branch), rank, first, 3 * group, group, "out_back"
        )
        grad_projected = self_back(projected, grad_self_mixed, 2 * images)
        attn_part = grad_products(
            [([attn_in], [grad_projected]), ([attn_branch], [self_mixed])], "attn_grads"
        )
        attn_part, cross_rows = lax.optimization_barrier((attn_part, cross_rows))
        attn_rows = scatter_grad(attn_part, DATA)
        grad_projected, activated, kv_grad, mlp_rows, attn_part = lax.optimization_barrier(
            (grad_projected, activated, kv_grad, mlp_rows, attn_part)
        )
        grad_attn = mm_t(grad_projected, first[:, : 3 * group]).astype(BF)
        grad_attn = trade(grad_attn.reshape(4, tokens, width))
        grad_hidden, gain_grad_a, mask_grad = last_back(
            [(grad_attn, k) for k in range(4)],
            grad_after_attn,
            start_x,
            gain_a,
            masked,
            unit,
            order,
        )
        sums = jnp.concatenate([gain_grad_a, gain_grad_b, gain_grad_c, mask_grad], axis=0)
        sums = layer_order(sum_all(sums))

        active = jnp.concatenate([a.reshape(4, tokens, -1) for a in activated], axis=1)
        result = mm_t(active.reshape(8 * tokens, -1), mlp[:, mlp.shape[1] // 2 :]).astype(BF)
        result = trade(result.reshape(4, 2 * tokens, width))
        far = swap(result[:, tokens:].astype(F32).sum(axis=0).astype(BF), "z")
        terms = [(result, k) for k in range(4)] + [far]
        if not inside:
            near = result[:, :tokens].astype(F32).sum(axis=0)
            terms = [pair_order(near + far.astype(F32))]
        output = layer_output(after_cross, terms, pair_unit, pair, unit, order)

        kv_grads = spread(sum_data(kv_grad)).reshape(4, -1, 2, group)
        kv_grads = kv_grads.transpose(1, 2, 0, 3).reshape(-1, 2 * width)
        kv_weight_grad = t_mm(own_text, kv_grads)
        grad_text = mm_t(kv_grads, kv_rows).astype(BF)
        grad_text_w = t_mm(grad_text, caption)
        caption_part = column_blocks(mm(grad_text, w_text).astype(BF), 4)
        caption_own = sum_data(trade(caption_part).astype(F32).sum(axis=0))
        grad_caption = spread(caption_own).transpose(1, 0, 2).reshape(-1, text_width).astype(F32)

        half_rows = 4 * shard_rows
        near = lax.dynamic_slice_in_dim(mlp_rows, z * half_rows, half_rows, 0)
        far = swap(lax.dynamic_slice_in_dim(mlp_rows, (1 - z) * half_rows, half_rows, 0), "z")
        near, far = (trade(part.reshape(4, shard_rows, -1)) for part in (near, far))
        down_grad, up_grad = finish_pair(near, far, z)
        grad_cross, cross_out_grad = finish_cross(
            trade(cross_rows.reshape(4, shard_rows, -1)), kv_weight_grad
        )
        qkv_grad, out_grad = finish_attention(trade(attn_rows.reshape(4, shard_rows, -1)))
        return (
            outer(output, layer_order).reshape(hidden.shape),
            outer(grad_hidden, layer_order).reshape(hidden.shape),
            grad_caption,
            sums[:3],
            sums[3],
            qkv_grad,
            out_grad,
            grad_cross,
            cross_out_grad,
            grad_text_w,
            up_grad,
            down_grad,
        )

    return local


def solution(mesh):
    z_size = mesh.shape["img"] // 4
    inner = Mesh(mesh.devices.reshape(z_size // 2, 2, 2, 2, 2), ("w", "z", "x", "c", "y"))
    image = ("w", "z", "x", "c")
    tokens = P(image, "y", None)
    rows = P(image + ("y",))
    in_specs = (tokens, P(image, None), P(image), P(), P(), P()) + (rows,) * 7 + (tokens,)
    out_specs = (tokens, tokens, P(), P(), P()) + (rows,) * 7
    return jax.shard_map(
        make_local(z_size), mesh=inner, in_specs=in_specs, out_specs=out_specs, check_vma=False
    )
```

time: 831 us -> 942 us (1.13)
  blocking collectives: 0 us -> 88.9 us
  Pallas kernels: 56.8 us -> 125 us
  waiting for transfers between devices: 399 us -> 457 us
  matrix products: 67.3 us -> 20.9 us
  other arithmetic: 52.5 us -> 18.2 us
  local copies, waits for them, and re-layouts: 104 us -> 78.8 us
    all_to_all x0 -> x15, waiting for transfers between devices: none -> 138 us  [trade(): return lax.all_to_all(blocks, axes, 0, 0, tiled=True)]
    ppermute x19 -> x0, waiting for transfers between devices: 101 us -> none  [the longest x10 53.9 us: swap_diag(): return lax.ppermute(values, ('x', 'y'), DIAG)]
    all_to_all x0 -> x6, blocking collectives: none -> 88.9 us  [trade(): return lax.all_to_all(blocks, axes, 0, 0, tiled=True)]
    pallas_call x16 -> x28, Pallas kernels: 56.8 us -> 125 us  [the longest x12 67 us: call(): pl.pallas_call(kernel, grid_spec=spec, **options)]
    all_to_all x0 -> x15, starting transfers between devices: none -> 58.2 us  [trade(): return lax.all_to_all(blocks, axes, 0, 0, tiled=True)]
    dot_general x22 -> x8, matrix products: 67.3 us -> 20.9 us  [dot(): return lax.dot_general(a, b, (dims, ((), ())), preferred_element_type=F32)]
    ppermute x100 -> x60, starting transfers between devices: 99.4 us -> 62.3 us  [swap(): return lax.ppermute(values, axis, PAIR)]
    ppermute x19 -> x0, starting transfers between devices: 28.1 us -> none  [the longest x10 14.5 us: swap_diag(): return lax.ppermute(values, ('x', 'y'), DIAG)]
  transfers between devices with their start and end apart: 126 -> 82, of which waited for: 76 -> 52; matrix products, arithmetic and copies ran while one was open for 24% -> 8% of each run, Pallas kernels for 5% -> 10%
where the time goes in v6:
time: 942 us; the launch traced here: 928 us
  waiting for transfers between devices  457 us (49%)
  Pallas kernels  125 us (13%)
  starting transfers between devices  124 us (13%)
  blocking collectives  88.9 us (9%)
  local copies, waits for them, and re-layouts  78.8 us (8%)
  matrix products  20.9 us (2%)
  other arithmetic  18.2 us (2%)
  between operations  16.9 us (2%)
    ppermute x60, waiting for transfers between devices, swap(): return lax.ppermute(values, axis, PAIR)  278 us
    all_to_all x15, waiting for transfers between devices, trade(): return lax.all_to_all(blocks, axes, 0, 0, tiled=True)  138 us
    all_to_all x6, blocking collectives, trade(): return lax.all_to_all(blocks, axes, 0, 0, tiled=True)  88.9 us
    pallas_call x12, Pallas kernels, call(): pl.pallas_call(kernel, grid_spec=spec, **options)  67 us
    ppermute x60, starting transfers between devices, swap(): return lax.ppermute(values, axis, PAIR)  62.3 us
    all_to_all x15, starting transfers between devices, trade(): return lax.all_to_all(blocks, axes, 0, 0, tiled=True)  58.2 us
    pallas_call x16, Pallas kernels, call(): pl.pallas_call(kernel, grid=grid, in_specs=in_specs, out_specs=out_specs,...  57.5 us
    unnamed x202, local copies, waits for them, and re-layouts  46.1 us
  transfers between devices with their start and end apart: 82, of which 52 were waited for; matrix products, arithmetic and copies ran while one was open for 8% of the time, Pallas kernels for 10%

profile of v6, /device:TPU:0, one launch (start us, length us, event | category | flops | bytes accessed | tf_op | source)
XLA Modules:
  0.0 928.5 jit_solution(17621371877042194635)
XLA Ops:
  12.5 19.3 %all_to_all.105 = bf16[4,64,2048]{2,1,0:T(8,128)(2,1)} all-to-all(bf16[4,64,2048]{2,1,0:T(8,128)(2,1)S(1)} %pad_maximum_fusion.3), channel_id=1, replica_groups=mesh['w'=2,'z'=2,'x'=2,'c'=2,'y'=2] {'x','y'}, dimensions={0} | all-to-all | bytes 2097152 | tf_op jit(solution)/shard_map/all_to_all | solution.py:50
  32.3 10.5 %all_to_all.106 = bf16[4,64,1024]{2,1,0:T(8,128)(2,1)} all-to-all(bf16[4,64,1024]{2,1,0:T(8,128)(2,1)S(1)} %pad_maximum_fusion.7), channel_id=1, replica_groups=mesh['w'=2,'z'=2,'x'=2,'c'=2,'y'=2] {'x','y'}, dimensions={0} | all-to-all | bytes 1048576 | tf_op jit(solution)/shard_map/all_to_all | solution.py:50
  47.2 13.8 %all_to_all.107 = bf16[4,64,2048]{2,1,0:T(8,128)(2,1)S(1)} all-to-all(bf16[4,64,2048]{2,1,0:T(8,128)(2,1)S(1)} %get-tuple-element.276), channel_id=1, replica_groups=mesh['w'=2,'z'=2,'x'=2,'c'=2,'y'=2] {'x','y'}, dimensions={0} | all-to-all | bytes 2097152 | tf_op jit(solution)/shard_map/all_to_all | solution.py:50
  61.0 64.1 %collective-permute-done.23 = bf16[4,64,2048]{2,1,0:T(8,128)(2,1)} collective-permute-done((bf16[4,64,2048]{2,1,0:T(8,128)(2,1)S(1)}, bf16[4,64,2048]{2,1,0:T(8,128)(2,1)}, u32[]{:S(2)}, u32[]{:S(2)}) %collective-permute-start.23) | collective-permute-done | bytes 1048608 | tf_op jit(solution)/shard_map/ppermute | solution.py:46
  128.7 11.8 %all-to-all-done.7 = bf16[4,64,2048]{2,1,0:T(8,128)(2,1)S(1)} async-done(((bf16[4,64,2048]{2,1,0:T(8,128)(2,1)}), bf16[4,64,2048]{2,1,0:T(8,128)(2,1)S(1)}, u32[]{:S(2)}, u32[]{:S(2)}) %all-to-all-start.7) | async-done | bytes 1048608 | tf_op jit(solution)/shard_map/all_to_all | solution.py:50
  152.7 12.4 %all-to-all-done = bf16[4,128,1024]{1,2,0:T(8,128)(2,1)} async-done(((bf16[4,128,1024]{1,2,0:T(8,128)(2,1)}), bf16[4,128,1024]{1,2,0:T(8,128)(2,1)}, u32[]{:S(2)}, u32[]{:S(2)}) %all-to-all-start) | async-done | bytes 1048608 | tf_op jit(solution)/shard_map/all_to_all | solution.py:50
  171.4 22.9 %all_to_all.108 = bf16[4,16,1024]{2,1,0:T(8,128)(2,1)S(1)} all-to-all(bf16[4,16,1024]{2,1,0:T(8,128)(2,1)S(1)} %bitcast.186), channel_id=1, replica_groups=mesh['w'=2,'z'=2,'x'=2,'c'=2,'y'=2] {'w','z'}, dimensions={0} | all-to-all | bytes 262144 | tf_op jit(solution)/shard_map/all_to_all | solution.py:50
  215.3 54.4 %collective-permute-done.1.refs_2_ = bf16[128,2048]{1,0:T(8,128)(2,1)S(1)} collective-permute-done((bf16[128,2048]{1,0:T(8,128)(2,1)}, bf16[128,2048]{1,0:T(8,128)(2,1)S(1)}, u32[]{:S(2)}, u32[]{:S(2)}) %collective-permute-start.1) | collective-permute-done | bytes 524320 | tf_op jit(solution)/shard_map/ppermute | solution.py:46
  407.3 9.6 %feed_forward.2 = (bf16[512,2048]{1,0:T(8,128)(2,1)}, bf16[512,2048]{1,0:T(8,128)(2,1)}, bf16[512,1024]{1,0:T(8,128)(2,1)S(1)}, bf16[512,1024]{1,0:T(8,128)(2,1)S(1)}) custom-call(s32[1]{0:T(128)} %bitcast.r, bf16[128,2048]{1,0:T(8,128)(2,1)S(1)} %copy-done.48, bf16[128,2048]{1,0:T(8,128)(2,1)S(1)} %copy-done.32, bf16[128,2048]{1,0:T(8,128)(2,1)S(1)} %copy-done.30, ...), custom_call_target="tpu_custom_call" | custom-call | flops 4294967296 | bytes 16777216 | tf_op jit(solution)/shard_map/feed_forward/pallas_call | solution.py:102
  428.6 9.7 %feed_forward.3 = (bf16[512,2048]{1,0:T(8,128)(2,1)}, bf16[512,2048]{1,0:T(8,128)(2,1)}, bf16[512,1024]{1,0:T(8,128)(2,1)S(1)}, bf16[512,1024]{1,0:T(8,128)(2,1)S(1)}) custom-call(s32[1]{0:T(128)} %bitcast.r, bf16[128,2048]{1,0:T(8,128)(2,1)S(1)} %copy-done.46, bf16[128,2048]{1,0:T(8,128)(2,1)S(1)} %copy-done.28, bf16[128,2048]{1,0:T(8,128)(2,1)S(1)} %copy-done.26, ...), custom_call_target="tpu_custom_call" | custom-call | flops 4294967296 | bytes 16777216 | tf_op jit(solution)/shard_map/feed_forward/pallas_call | solution.py:102
  449.7 13.5 %mlp_grads.1 = bf16[2048,2048]{1,0:T(8,128)(2,1)} custom-call(bf16[512,2048]{1,0:T(8,128)(2,1)} %get-tuple-element.171.refs_0_, bf16[512,2048]{1,0:T(8,128)(2,1)} %get-tuple-element.172.refs_1_, bf16[512,2048]{1,0:T(8,128)(2,1)} %get-tuple-element.173.refs_2_, bf16[512,2048]{1,0:T(8,128)(2,1)} %get-tuple-element.174.refs_3_, ...), custom_call_target="tpu_custom_call" | custom-call | flops 8589934592 | bytes 16777216 | tf_op jit(solution)/shard_map/mlp_grads/pallas_call | solution.py:91
  496.7 14.0 %collective-permute-done.37.refs_3_ = bf16[128,2048]{1,0:T(8,128)(2,1)S(1)} collective-permute-done((bf16[128,2048]{1,0:T(8,128)(2,1)S(1)}, bf16[128,2048]{1,0:T(8,128)(2,1)S(1)}, u32[]{:S(2)}, u32[]{:S(2)}) %collective-permute-start.37) | collective-permute-done | bytes 524320 | tf_op jit(solution)/shard_map/ppermute | solution.py:46
  540.8 39.6 %reduce-scatter.4.cloned.1.call-done = bf16[512,2048]{1,0:T(8,128)(2,1)} async-done(((bf16[2048,2048]{1,0:T(8,128)(2,1)}), bf16[512,2048]{1,0:T(8,128)(2,1)}) %reduce-scatter.4.cloned.1.call-update) | async-done | bytes 2097168 | tf_op jit(solution)/shard_map/reduce_scatter | solution.py:79
  595.7 9.7 %collective-permute-done.43.refs_1_ = bf16[128,2048]{1,0:T(8,128)(2,1)S(1)} collective-permute-done((bf16[128,2048]{1,0:T(8,128)(2,1)S(1)}, bf16[128,2048]{1,0:T(8,128)(2,1)S(1)}, u32[]{:S(2)}, u32[]{:S(2)}) %collective-permute-start.43) | collective-permute-done | bytes 524320 | tf_op jit(solution)/shard_map/ppermute | solution.py:46
  611.3 9.6 %collective-permute-done.47.refs_2_ = bf16[128,2048]{1,0:T(8,128)(2,1)S(1)} collective-permute-done((bf16[128,2048]{1,0:T(8,128)(2,1)S(1)}, bf16[128,2048]{1,0:T(8,128)(2,1)S(1)}, u32[]{:S(2)}, u32[]{:S(2)}) %collective-permute-start.47) | collective-permute-done | bytes 524320 | tf_op jit(solution)/shard_map/ppermute | solution.py:46
  637.1 9.5 %attn_grads.1 = bf16[2048,2048]{1,0:T(8,128)(2,1)} custom-call(bf16[512,2048]{1,0:T(8,128)(2,1)S(1)} %copy-done.78, bf16[512,2048]{1,0:T(8,128)(2,1)} %copy-done.65, bf16[512,1536]{1,0:T(8,128)(2,1)S(1)} %self_back.1.refs_2_, bf16[512,512]{1,0:T(8,128)(2,1)S(1)} %copy-done.17), custom_call_target="tpu_custom_call" | custom-call | flops 4294967296 | bytes 16777216 | tf_op jit(solution)/shard_map/attn_grads/pallas_call | solution.py:91
  650.5 11.4 %all_to_all.109 = bf16[4,16,1024]{2,1,0:T(8,128)(2,1)S(1)} all-to-all(bf16[4,16,1024]{2,1,0:T(8,128)(2,1)S(1)} %bitcast.187), channel_id=1, replica_groups=mesh['w'=2,'z'=2,'x'=2,'c'=2,'y'=2] {'w','z'}, dimensions={0} | all-to-all | bytes 262144 | tf_op jit(solution)/shard_map/all_to_all | solution.py:50
  661.9 11.0 %all_to_all.110 = bf16[4,16,1024]{2,1,0:T(8,128)(2,1)S(1)} all-to-all(bf16[4,16,1024]{2,1,0:T(8,128)(2,1)S(1)} %broadcast_in_dim.14), channel_id=1, replica_groups=mesh['w'=2,'z'=2,'x'=2,'c'=2,'y'=2] {'w','z'}, dimensions={0} | all-to-all | bytes 262144 | tf_op jit(solution)/shard_map/all_to_all | solution.py:50
  693.2 10.7 %all-to-all-done.12 = bf16[4,128,1024]{1,2,0:T(8,128)(2,1)S(1)} async-done(((bf16[4,128,1024]{1,2,0:T(8,128)(2,1)}), bf16[4,128,1024]{1,2,0:T(8,128)(2,1)S(1)}, u32[]{:S(2)}, u32[]{:S(2)}) %all-to-all-start.12) | async-done | bytes 1048608 | tf_op jit(solution)/shard_map/all_to_all | solution.py:50
  711.0 10.5 %all-to-all-done.19.near_ref = bf16[4,64,2048]{2,1,0:T(8,128)(2,1)S(1)} async-done(((bf16[4,64,2048]{2,1,0:T(8,128)(2,1)}), bf16[4,64,2048]{2,1,0:T(8,128)(2,1)S(1)}, u32[]{:S(2)}, u32[]{:S(2)}) %all-to-all-start.19) | async-done | bytes 1048608 | tf_op jit(solution)/shard_map/all_to_all | solution.py:50
  748.3 19.4 %all-to-all-done.9.refs_0_.refs_1_.refs_2_.refs_3_ = bf16[4,128,2048]{2,1,0:T(8,128)(2,1)S(1)} async-done(((bf16[4,128,2048]{2,1,0:T(8,128)(2,1)}), bf16[4,128,2048]{2,1,0:T(8,128)(2,1)S(1)}, u32[]{:S(2)}, u32[]{:S(2)}) %all-to-all-start.9) | async-done | bytes 2097184 | tf_op jit(solution)/shard_map/all_to_all | solution.py:50
  797.9 9.4 %fusion.4 = bf16[1024,2048]{1,0:T(8,128)(2,1)} fusion(bf16[1024,1024]{1,0:T(8,128)(2,1)} %bitcast.172, bf16[2048,2048]{1,0:T(8,128)(2,1)} %all-gather.8.cloned.1.call-done.refs_6_.refs_7_.w), kind=kOutput, calls=%fused_computation.6 | convolution fusion | flops 4297064448 | bytes 10485760 | tf_op jit(solution)/shard_map/dot_general | solution.py:26
  818.5 39.8 %all-to-all-done.8.refs_0_.refs_1_.refs_2_.refs_3_ = bf16[4,256,2048]{2,1,0:T(8,128)(2,1)} async-done(((bf16[4,256,2048]{2,1,0:T(8,128)(2,1)}), bf16[4,256,2048]{2,1,0:T(8,128)(2,1)}, u32[]{:S(2)}, u32[]{:S(2)}) %all-to-all-start.8) | async-done | bytes 4194336 | tf_op jit(solution)/shard_map/all_to_all | solution.py:50
  865.1 12.1 %collective-permute-done.56 = f32[4,2048]{1,0:T(4,128)S(1)} collective-permute-done((f32[4,2048]{1,0:T(4,128)S(1)}, f32[4,2048]{1,0:T(4,128)S(1)}, u32[]{:S(2)}, u32[]{:S(2)}) %collective-permute-start.56) | collective-permute-done | bytes 32800 | tf_op jit(solution)/shard_map/ppermute | solution.py:46
  (505 shorter events, 462.9 us)
Async XLA Ops:
  7.2 271.3 %all-gather.4.cloned.1.call-start = ((), (), s32[]{:S(2)}) async-start(), calls=%async_computation.24 | async-start | bytes 9437184 | tf_op jit(solution)/shard_map/all_gather | solution.py:75
  31.9 303.4 %all-gather.6.cloned.1.call-start = ((), (), s32[]{:S(2)}) async-start(), calls=%async_computation.25 | async-start | bytes 4718592 | tf_op jit(solution)/shard_map/all_gather | solution.py:75
  45.5 79.5 %collective-permute-start.23 = (bf16[4,64,2048]{2,1,0:T(8,128)(2,1)S(1)}, bf16[4,64,2048]{2,1,0:T(8,128)(2,1)}, u32[]{:S(2)}, u32[]{:S(2)}) collective-permute-start(bf16[4,64,2048]{2,1,0:T(8,128)(2,1)S(1)} %get-tuple-element.277), channel_id=1, source_target_pairs={{0,8},{8,0},{1,9},{9,1},{2,10},{10,2},{3,11},{11,3},{4,12},{12,4},... | collective-permute-start | bytes 3145736 | tf_op jit(solution)/shard_map/ppermute | solution.py:46
  128.6 275.5 %all-gather.8.cloned.1.call-start = ((), (), s32[]{:S(2)}) async-start(), calls=%async_computation.26 | async-start | bytes 10485760 | tf_op jit(solution)/shard_map/all_gather | solution.py:75
  147.3 17.8 %all-to-all-start = ((bf16[4,128,1024]{1,2,0:T(8,128)(2,1)}), bf16[4,128,1024]{1,2,0:T(8,128)(2,1)}, u32[]{:S(2)}, u32[]{:S(2)}) async-start(bf16[4,128,1024]{1,2,0:T(8,128)(2,1)} %bitcast.12), calls=%async_computation | async-start | bytes 2097152 | tf_op jit(solution)/shard_map/all_to_all | solution.py:50
  169.9 28.4 %collective-permute-start.6 = (bf16[128,2048]{1,0:T(8,128)(2,1)S(1)}, bf16[128,2048]{1,0:T(8,128)(2,1)}, u32[]{:S(2)}, u32[]{:S(2)}) collective-permute-start(bf16[128,2048]{1,0:T(8,128)(2,1)S(1)} %get-tuple-element.114.refs_4_), channel_id=1, source_target_pairs={{0,8},{8,0},{1,9},{9,1},{2,10},{10,2},{3,11},{11,3},{4,12},{12,4},... | collective-permute-start | bytes 1572872 | tf_op jit(solution)/shard_map/ppermute | solution.py:46
  207.0 86.5 %all-to-all-start.4 = ((bf16[4,256,2048]{2,1,0:T(8,128)(2,1)}), bf16[4,256,2048]{2,1,0:T(8,128)(2,1)}, u32[]{:S(2)}, u32[]{:S(2)}) async-start(bf16[4,256,2048]{2,1,0:T(8,128)(2,1)} %broadcast_in_dim.13), calls=%async_computation.4 | async-start | bytes 8388608 | tf_op jit(solution)/shard_map/all_to_all | solution.py:50
  211.9 368.5 %reduce-scatter.4.cloned.1.call-start = ((), (), s32[]{:S(2)}) async-start(), calls=%async_computation.27 | async-start | bytes 10485760 | tf_op jit(solution)/shard_map/reduce_scatter | solution.py:79
  211.9 57.8 %collective-permute-start.1 = (bf16[128,2048]{1,0:T(8,128)(2,1)}, bf16[128,2048]{1,0:T(8,128)(2,1)S(1)}, u32[]{:S(2)}, u32[]{:S(2)}) collective-permute-start(bf16[128,2048]{1,0:T(8,128)(2,1)} %copy-done.66), channel_id=1, source_target_pairs={{0,4},{4,0},{1,5},{5,1},{2,6},{6,2},{3,7},{7,3},{8,12},{12,8},{9,1... | collective-permute-start | bytes 1572872 | tf_op jit(solution)/shard_map/ppermute | solution.py:46
  213.8 57.4 %collective-permute-start = (bf16[128,2048]{1,0:T(8,128)(2,1)}, bf16[128,2048]{1,0:T(8,128)(2,1)S(1)}, u32[]{:S(2)}, u32[]{:S(2)}) collective-permute-start(bf16[128,2048]{1,0:T(8,128)(2,1)} %copy-done.66), channel_id=1, source_target_pairs={{0,1},{1,0},{2,3},{3,2},{4,5},{5,4},{6,7},{7,6},{8,9},{9,8},{10,11... | collective-permute-start | bytes 1572872 | tf_op jit(solution)/shard_map/ppermute | solution.py:46
  215.3 56.6 %collective-permute-start.5 = (bf16[64,1024]{1,0:T(8,128)(2,1)}, bf16[64,1024]{1,0:T(8,128)(2,1)S(1)}, u32[]{:S(2)}, u32[]{:S(2)}) collective-permute-start(bf16[64,1024]{1,0:T(8,128)(2,1)} %bitcast.183), channel_id=1, source_target_pairs={{0,2},{2,0},{1,3},{3,1},{4,6},{6,4},{5,7},{7,5},{8,10},{10,8},{9,1... | collective-permute-start | bytes 393224 | tf_op jit(solution)/shard_map/ppermute | solution.py:46
  400.8 27.8 %collective-permute-start.27 = (bf16[64,2048]{1,0:T(8,128)(2,1)}, bf16[64,2048]{1,0:T(8,128)(2,1)}, u32[]{:S(2)}, u32[]{:S(2)}) collective-permute-start(bf16[64,2048]{1,0:T(8,128)(2,1)} %slice.194), channel_id=1, source_target_pairs={{0,1},{1,0},{2,3},{3,2},{4,5},{5,4},{6,7},{7,6},{8,9},{9,8},{10,11... | collective-permute-start | bytes 786440 | tf_op jit(solution)/shard_map/ppermute | solution.py:46
  403.7 24.8 %collective-permute-start.28 = (bf16[64,2048]{1,0:T(8,128)(2,1)}, bf16[64,2048]{1,0:T(8,128)(2,1)}, u32[]{:S(2)}, u32[]{:S(2)}) collective-permute-start(bf16[64,2048]{1,0:T(8,128)(2,1)} %slice.195), channel_id=1, source_target_pairs={{0,4},{4,0},{1,5},{5,1},{2,6},{6,2},{3,7},{7,3},{8,12},{12,8},{9,1... | collective-permute-start | bytes 786440 | tf_op jit(solution)/shard_map/ppermute | solution.py:46
  463.2 184.6 %reduce-scatter.6.cloned.1.call-start = ((), (), s32[]{:S(2)}) async-start(), calls=%async_computation.28 | async-start | bytes 4718592 | tf_op jit(solution)/shard_map/reduce_scatter | solution.py:79
  473.1 19.7 %collective-permute-start.30 = (bf16[128,2048]{1,0:T(8,128)(2,1)S(1)}, bf16[128,2048]{1,0:T(8,128)(2,1)S(1)}, u32[]{:S(2)}, u32[]{:S(2)}) collective-permute-start(bf16[128,2048]{1,0:T(8,128)(2,1)S(1)} %pad_maximum_fusion.10), channel_id=1, source_target_pairs={{0,4},{4,0},{1,5},{5,1},{2,6},{6,2},{3,7},{7,3},{8,12},{12,8},{9,1... | collective-permute-start | bytes 1572872 | tf_op jit(solution)/shard_map/ppermute | solution.py:46
  491.5 19.2 %collective-permute-start.37 = (bf16[128,2048]{1,0:T(8,128)(2,1)S(1)}, bf16[128,2048]{1,0:T(8,128)(2,1)S(1)}, u32[]{:S(2)}, u32[]{:S(2)}) collective-permute-start(bf16[128,2048]{1,0:T(8,128)(2,1)S(1)} %add_convert_fusion), channel_id=1, source_target_pairs={{0,8},{8,0},{1,9},{9,1},{2,10},{10,2},{3,11},{11,3},{4,12},{12,4},... | collective-permute-start | bytes 1572872 | tf_op jit(solution)/shard_map/ppermute | solution.py:46
  580.4 302.6 %reduce-scatter.8.cloned.1.call-start = ((), (), s32[]{:S(2)}) async-start(), calls=%async_computation.29 | async-start | bytes 9437184 | tf_op jit(solution)/shard_map/reduce_scatter | solution.py:79
  703.9 17.5 %all-to-all-start.19 = ((bf16[4,64,2048]{2,1,0:T(8,128)(2,1)}), bf16[4,64,2048]{2,1,0:T(8,128)(2,1)S(1)}, u32[]{:S(2)}, u32[]{:S(2)}) async-start(bf16[4,64,2048]{2,1,0:T(8,128)(2,1)} %bitcast.59), calls=%async_computation.22 | async-start | bytes 2097152 | tf_op jit(solution)/shard_map/all_to_all | solution.py:50
  739.2 28.5 %all-to-all-start.9 = ((bf16[4,128,2048]{2,1,0:T(8,128)(2,1)}), bf16[4,128,2048]{2,1,0:T(8,128)(2,1)S(1)}, u32[]{:S(2)}, u32[]{:S(2)}) async-start(bf16[4,128,2048]{2,1,0:T(8,128)(2,1)} %bitcast.171), calls=%async_computation.11 | async-start | bytes 4194304 | tf_op jit(solution)/shard_map/all_to_all | solution.py:50
  742.8 28.2 %collective-permute-start.60 = (bf16[256,2048]{1,0:T(8,128)(2,1)}, bf16[256,2048]{1,0:T(8,128)(2,1)}, u32[]{:S(2)}, u32[]{:S(2)}) collective-permute-start(bf16[256,2048]{1,0:T(8,128)(2,1)} %get-tuple-element.272), channel_id=1, source_target_pairs={{0,8},{8,0},{1,9},{9,1},{2,10},{10,2},{3,11},{11,3},{4,12},{12,4},... | collective-permute-start | bytes 3145736 | tf_op jit(solution)/shard_map/ppermute | solution.py:46
  807.2 51.1 %all-to-all-start.8 = ((bf16[4,256,2048]{2,1,0:T(8,128)(2,1)}), bf16[4,256,2048]{2,1,0:T(8,128)(2,1)}, u32[]{:S(2)}, u32[]{:S(2)}) async-start(bf16[4,256,2048]{2,1,0:T(8,128)(2,1)} %bitcast.162), calls=%async_computation.10 | async-start | bytes 8388608 | tf_op jit(solution)/shard_map/all_to_all | solution.py:50
  817.2 45.8 %collective-permute-start.55 = (f32[4,2048]{1,0:T(4,128)S(1)}, f32[4,2048]{1,0:T(4,128)S(1)}, u32[]{:S(2)}, u32[]{:S(2)}) collective-permute-start(f32[4,2048]{1,0:T(4,128)S(1)} %pad_maximum_fusion.19), channel_id=1, source_target_pairs={{0,2},{2,0},{1,3},{3,1},{4,6},{6,4},{5,7},{7,5},{8,10},{10,8},{9,1... | collective-permute-start | bytes 98312 | tf_op jit(solution)/shard_map/ppermute | solution.py:46
  859.5 23.5 %all-to-all-start.16 = ((bf16[4,128,1024]{2,1,0:T(8,128)(2,1)}), bf16[4,128,1024]{2,1,0:T(8,128)(2,1)S(1)}, u32[]{:S(2)}, u32[]{:S(2)}) async-start(bf16[4,128,1024]{2,1,0:T(8,128)(2,1)} %broadcast_in_dim.17), calls=%async_computation.18 | async-start | bytes 2097152 | tf_op jit(solution)/shard_map/all_to_all | solution.py:50
  884.0 31.7 %all-to-all-start.17 = ((bf16[4,64,2048]{2,1,0:T(8,128)(2,1)}), bf16[4,64,2048]{2,1,0:T(8,128)(2,1)}, u32[]{:S(2)}, u32[]{:S(2)}) async-start(bf16[4,64,2048]{2,1,0:T(8,128)(2,1)} %bitcast.178), calls=%async_computation.20 | async-start | bytes 2097152 | tf_op jit(solution)/shard_map/all_to_all | solution.py:50
  (157 other events, 1471.6 us)
Sparse Core Ops, SparseCore 0:
  32.0 102.3 all-gather.3
  136.0 50.4 all-gather.5
  188.7 108.5 all-gather.7
  463.3 116.9 reduce-scatter.3
  582.6 48.9 reduce-scatter.5
  648.0 93.0 reduce-scatter.7

commit v7 on v6

--- a/solution.py
+++ b/solution.py
@@ -14,8 +14,7 @@
 F32 = jnp.float32
 PAIR = ((0, 1), (1, 0))
 GROUP = ("x", "y")
-DATA = ("w", "z", "c")
-PAIR_DATA = ("w", "c")
+DATA = ("z", "c")
 VMEM = 48 * 1024 * 1024
 SCALE = 1.0 / math.sqrt(HD)
 SLOPE = math.sqrt(2.0 / math.pi)
@@ -71,12 +70,23 @@
     return [own, from_x, from_y]
 
 
-def gather_rows(rows, axes):
-    return lax.all_gather(rows, axes, axis=0, tiled=True)
-
-
-def scatter_grad(partial, axes):
-    return lax.psum_scatter(partial, axes, scatter_dimension=0, tiled=True)
+def swap_blocks(blocks, rank):
+    parts = [lax.dynamic_index_in_dim(blocks, rank ^ k, 0, keepdims=False) for k in range(4)]
+    return [
+        parts[0],
+        swap(parts[1], "y"),
+        swap(parts[2], "x"),
+        lax.ppermute(parts[3], GROUP, ((0, 3), (1, 2), (2, 1), (3, 0))),
+    ]
+
+
+def gather_rows(rows):
+    return lax.all_gather(rows.reshape(-1, rows.shape[-1]), DATA, axis=0, tiled=True)
+
+
+def scatter_grad(partial):
+    summed = lax.psum_scatter(partial, DATA, scatter_dimension=0, tiled=True)
+    return summed.reshape(4, -1, summed.shape[-1])
 
 
 def call(kernel, grid, in_specs, out_specs, out_shape, operands, name, flops=0, size=1 << 22,
@@ -112,14 +122,13 @@
     return jnp.concatenate([values[:, k * unit : (k + 1) * unit] for k in order], axis=1)
 
 
-def assemble(target, pieces, rank, unit, order):
+def assemble(target, pieces, rank):
     rows, half = pieces[0].shape[0], pieces[3].shape[0]
     for k in range(3):
-        at = pl.multiple_of((rank ^ k) * rows, rows)
-        target[pl.ds(at, rows), :] = reorder(pieces[k][...], unit, order)
+        target[pl.ds(pl.multiple_of((rank ^ k) * rows, rows), rows), :] = pieces[k][...]
     at = pl.multiple_of((rank ^ 3) * rows, rows)
-    target[pl.ds(at, half), :] = reorder(pieces[3][...], unit, order)
-    target[pl.ds(pl.multiple_of(at + half, half), half), :] = reorder(pieces[4][...], unit, order)
+    target[pl.ds(at, half), :] = pieces[3][...]
+    target[pl.ds(pl.multiple_of(at + half, half), half), :] = pieces[4][...]
 
 
 def gather_mm(pieces, rank, weight, first, columns, name):
@@ -131,7 +140,7 @@
 
         @pl.when(pl.program_id(0) == 0)
         def _():
-            assemble(tokens, refs[:5], r[0], width, None)
+            assemble(tokens, refs[:5], r[0])
 
         out[...] = mm(tokens[...], refs[5][...]).astype(BF)
 
@@ -153,12 +162,11 @@
     )
 
 
-def mm_scatter(values, rank, weight, first, name, unit=0, order=None):
+def mm_scatter(values, rank, weight, first, name):
     tokens, depth = values.shape
     rows = tokens // 4
     width = weight.shape[0]
-    step = unit if order is not None else 512
-    place = (lambda j: j) if order is None else (lambda j: pair_index(j))
+    step = 512
 
     def kernel(r, x, w, own, for_y, for_x, low, high, total):
         total[...] = mm_t(x[...], w[...])
@@ -181,7 +189,7 @@
             pl.BlockSpec((tokens, depth), lambda j, r: (0, 0)),
             pl.BlockSpec((step, depth), lambda j, r: (j, first // depth)),
         ],
-        [pl.BlockSpec((n, step), lambda j, r: (0, place(j))) for n in sizes],
+        [pl.BlockSpec((n, step), lambda j, r: (0, j)) for n in sizes],
         [shape((n, width), F32 if k == 0 else BF) for k, n in enumerate(sizes)],
         [values, weight],
         name,
@@ -190,10 +198,6 @@
         rank=rank,
         scratch=[pltpu.VMEM((tokens, step), F32)],
     )
-
-
-def pair_index(j):
-    return ((j >> 2) << 2) | ((j & 1) << 1) | ((j >> 1) & 1)
 
 
 def normalize(values):
@@ -339,12 +343,12 @@
     )
 
 
-def layer_output(upper, terms, pair_unit, pair_order, unit, order):
+def layer_output(upper, terms, unit, order):
     arrays, specs = terms_of(terms)
     tokens, width = upper.shape
 
     def kernel(*refs):
-        values = refs[-2][...] + reorder(total_of(refs[:-2]), pair_unit, pair_order)
+        values = refs[-2][...] + total_of(refs[:-2])
         refs[-1][...] = reorder(values.astype(BF), unit, order)
 
     return call(
@@ -358,46 +362,59 @@
     )
 
 
-def feed_forward(pieces, grad_y, side, rank, weight, unit, order):
+def feed_up(pieces, rank, weight):
     rows, width = pieces[0].shape
-    hidden = weight.shape[1] // 2
+    hidden = weight.shape[1]
     step = 256
 
     def kernel(r, *refs):
-        dy, up, down, tokens, grads, act, pre = refs[5:]
+        up, tokens, act, slope = refs[5:]
 
         @pl.when(pl.program_id(0) == 0)
         def _():
-            assemble(tokens, refs[:5], r[0], unit, order)
-            for k in range(4):
-                grads[k * rows : (k + 1) * rows, :] = reorder(dy[k], unit, order)
+            assemble(tokens, refs[:5], r[0])
 
         u = mm(tokens[...], up[...])
         square = u * u
         bend = jnp.tanh(SLOPE * u * (1.0 + CUBIC * square))
         half = 0.5 * (1.0 + bend)
         act[...] = (u * half).astype(BF)
-        slope = half + 0.5 * u * (1.0 - bend * bend) * SLOPE * (1.0 + 3.0 * CUBIC * square)
-        pre[...] = (mm(grads[...], down[...]) * slope).astype(BF)
-
-    full = pl.BlockSpec((4 * rows, width), lambda j, r: (0, 0))
+        slope[...] = half + 0.5 * u * (1.0 - bend * bend) * SLOPE * (1.0 + 3.0 * CUBIC * square)
+
     part = pl.BlockSpec((4 * rows, step), lambda j, r: (0, j))
     return call(
         kernel,
         (hidden // step,),
-        [whole(p) for p in pieces]
-        + [
-            pl.BlockSpec((4, rows, width), lambda j, r: (0, side, 0)),
-            pl.BlockSpec((width, step), lambda j, r: (0, j)),
-            pl.BlockSpec((width, step), lambda j, r: (0, hidden // step + j)),
-        ],
-        [full, full, part, part],
-        [shape((4 * rows, width))] * 2 + [shape((4 * rows, hidden))] * 2,
-        [*pieces, grad_y, weight, weight],
-        "feed_forward",
-        flops=16 * rows * width * hidden,
-        size=4 * width * (hidden + 8 * rows),
+        [whole(p) for p in pieces] + [pl.BlockSpec((width, step), lambda j, r: (0, j))],
+        [pl.BlockSpec((4 * rows, width), lambda j, r: (0, 0)), part, part],
+        [shape((4 * rows, width)), shape((4 * rows, hidden)), shape((4 * rows, hidden), F32)],
+        [*pieces, weight],
+        "feed_up",
+        flops=8 * rows * width * hidden,
+        size=2 * width * (hidden + 8 * rows),
         rank=rank,
+    )
+
+
+def feed_down(grad_y, slope, weight):
+    tokens, width = grad_y.shape
+    hidden = weight.shape[1]
+    step = 256
+
+    def kernel(dy, slope_ref, down, out):
+        out[...] = (mm(dy[...], down[...]) * slope_ref[...]).astype(BF)
+
+    part = pl.BlockSpec((tokens, step), lambda j: (0, j))
+    return call(
+        kernel,
+        (hidden // step,),
+        [whole(grad_y), part, pl.BlockSpec((width, step), lambda j: (0, j))],
+        part,
+        shape((tokens, hidden)),
+        [grad_y, slope, weight],
+        "feed_down",
+        flops=2 * tokens * width * hidden,
+        size=2 * width * (hidden + 8 * tokens),
     )
 
 
@@ -558,81 +575,78 @@
     )
 
 
-def finish_pair(near, far, z):
-    count, rows, total = near.shape
-    width = total // 2
-
-    def kernel(r, near_ref, far_ref, first, second):
-        step = pl.program_id(0)
-        for side, ref in enumerate((near_ref, far_ref)):
-
-            @pl.when(step // count == side)
+def place(parts, rank):
+    def kernel(r, *refs):
+        for k in range(4):
+
+            @pl.when(pl.program_id(0) == k)
             def _():
-                block = ref[lax.rem(step, count)].astype(F32)
-                first[...] = block[:, :width]
-                second[...] = block[:, width:]
-
-    out = pl.BlockSpec((rows, width), lambda k, r: (0, ((k // count) ^ r[0]) * count + k % count))
-    return call(
-        kernel,
-        (2 * count,),
-        [whole(near), whole(far)],
-        [out, out],
-        [shape((rows, 2 * count * width), F32)] * 2,
-        [near, far],
-        "finish_pair",
-        rank=z,
-    )
-
-
-def finish_attention(blocks):
-    count, rows, total = blocks.shape
-    width = total // 4
-
-    def kernel(ref, three, one):
-        for j in range(3):
-            three[:, j, :] = ref[0, :, j * width : (j + 1) * width].astype(F32)
-        one[...] = ref[0, :, 3 * width :].astype(F32)
+                refs[4][0] = refs[k][...]
+
+    rows, columns = parts[0].shape
+    return call(
+        kernel,
+        (4,),
+        [whole(p) for p in parts],
+        pl.BlockSpec((1, rows, columns), lambda k, r: (k ^ r[0], 0, 0)),
+        shape((4, rows, columns)),
+        parts,
+        "place",
+        rank=rank,
+    )
+
+
+def finish_wide(blocks):
+    count, rows, width = blocks.shape
+
+    def kernel(ref, out):
+        out[...] = ref[0].astype(F32)
 
     return call(
         kernel,
         (count,),
-        [pl.BlockSpec((1, rows, total), lambda k: (k, 0, 0))],
-        [
-            pl.BlockSpec((rows, 3, width), lambda k: (0, 0, k)),
-            pl.BlockSpec((rows, width), lambda k: (0, k)),
-        ],
-        [shape((rows, 3, count * width), F32), shape((rows, count * width), F32)],
+        [pl.BlockSpec((1, rows, width), lambda k: (k, 0, 0))],
+        pl.BlockSpec((rows, width), lambda k: (0, k)),
+        shape((rows, count * width), F32),
         [blocks],
-        "finish_attention",
-    )
-
-
-def finish_cross(blocks, text_grad):
-    count, rows, total = blocks.shape
-    width = total // 2
-
-    def kernel(ref, key, value, three, one):
-        three[:, 0, :] = ref[0, :, :width].astype(F32)
-        three[:, 1, :] = key[...]
-        three[:, 2, :] = value[...]
-        one[...] = ref[0, :, width:].astype(F32)
-
-    return call(
-        kernel,
-        (count,),
-        [
-            pl.BlockSpec((1, rows, total), lambda k: (k, 0, 0)),
-            pl.BlockSpec((rows, width), lambda k: (0, k)),
-            pl.BlockSpec((rows, width), lambda k: (0, count + k)),
-        ],
-        [
-            pl.BlockSpec((rows, 3, width), lambda k: (0, 0, k)),
-            pl.BlockSpec((rows, width), lambda k: (0, k)),
-        ],
-        [shape((rows, 3, count * width), F32), shape((rows, count * width), F32)],
-        [blocks, text_grad, text_grad],
-        "finish_cross",
+        "finish_wide",
+    )
+
+
+def finish_all(parts, text_grad, rank):
+    rows, total = parts[0].shape
+    width = total // 6
+
+    def kernel(r, *refs):
+        key, value, three, out, cross, cross_out = refs[4:]
+        for k in range(4):
+
+            @pl.when(pl.program_id(0) == k)
+            def _():
+                def part(j):
+                    return refs[k][:, j * width : (j + 1) * width].astype(F32)
+
+                for j in range(3):
+                    three[:, j, :] = part(j)
+                out[...] = part(3)
+                cross[:, 0, :] = part(4)
+                cross_out[...] = part(5)
+
+        cross[:, 1, :] = key[...]
+        cross[:, 2, :] = value[...]
+
+    wide = pl.BlockSpec((rows, 3, width), lambda k, r: (0, 0, k ^ r[0]))
+    flat = pl.BlockSpec((rows, width), lambda k, r: (0, k ^ r[0]))
+    return call(
+        kernel,
+        (4,),
+        [whole(p) for p in parts]
+        + [flat, pl.BlockSpec((rows, width), lambda k, r: (0, 4 + (k ^ r[0])))],
+        [wide, flat, wide, flat],
+        [shape((rows, 3, 4 * width), F32), shape((rows, 4 * width), F32)] * 2,
+        [*parts, text_grad, text_grad],
+        "finish_all",
+        rank=rank,
     )
 
 
@@ -642,8 +656,6 @@
 
 
 def make_local(z_size):
-    z_axes = ("w", "z")
-
     def sum_data(values):
         rows, columns = values.shape
         core = lax.axis_index("c")
@@ -651,34 +663,27 @@
         keep = lax.dynamic_index_in_dim(halves, core, 0, keepdims=False)
         send = lax.dynamic_index_in_dim(halves, 1 - core, 0, keepdims=False)
         mine = (keep + swap(send, "c")).astype(BF).reshape(z_size, -1, columns)
-        mine = trade(mine, z_axes).astype(F32).sum(axis=0).astype(BF)
-        mine = spread(mine, z_axes, z_size).reshape(rows // 2, columns)
+        mine = trade(mine, "z").astype(F32).sum(axis=0).astype(BF)
+        mine = spread(mine, "z", z_size).reshape(rows // 2, columns)
         other = swap(mine, "c")
         return jnp.concatenate(
             [jnp.where(core == 0, mine, other), jnp.where(core == 0, other, mine)], axis=0
         )
 
     def sum_all(values):
-        for axis in ("c", "x", "y", "z"):
+        for axis in ("c", "x", "y"):
             values = values + swap(values, axis)
         step = 1
-        while 2 * step < z_size:
+        while step < z_size:
             values = values + lax.ppermute(
-                values, "w", tuple((k, k ^ step) for k in range(z_size // 2))
+                values, "z", tuple((k, k ^ step) for k in range(z_size))
             )
             step *= 2
         return values
 
-    def swap_dims(values, first):
-        shaped = values.reshape(values.shape[:-1] + (z_size // 2, 2, 2, 2, -1))
-        at = values.ndim - 1 + first
-        return jnp.swapaxes(shaped, at, at + 1).reshape(values.shape)
-
     def layer_order(values):
-        return swap_dims(values, 2)
-
-    def pair_order(values):
-        return swap_dims(values, 1)
+        shaped = values.reshape(values.shape[:-1] + (z_size, 2, 2, -1))
+        return jnp.swapaxes(shaped, -3, -2).reshape(values.shape)
 
     def local(
         hidden,
@@ -700,18 +705,16 @@
         full_length = mask_index.shape[1]
         shard_rows = w_qkv.shape[0]
         rank = lax.axis_index("x") * 2 + lax.axis_index("y")
-        z = lax.axis_index("z")
         tokens = images * local_rows
         group = width // 4
         text_width = caption.shape[1]
 
-        unit, pair_unit = width // (4 * z_size), width // (2 * z_size)
+        unit = width // (4 * z_size)
         inside = unit % 128 == 0
-        order = [pair_index(k) for k in range(4 * z_size)] if inside else None
-        pair = [pair_index(k) for k in range(2 * z_size)] if inside else None
-
-        def outer(values, change):
-            return values if inside else change(values)
+        order = [4 * k + j for k in range(z_size) for j in (0, 2, 1, 3)] if inside else None
+
+        def outer(values):
+            return values if inside else layer_order(values)
 
         first = jnp.concatenate(
             [
@@ -722,19 +725,11 @@
             ],
             axis=2,
         )
-        first = gather_rows(trade(first).reshape(4 * shard_rows, 4 * group), DATA)
-        wide = jnp.concatenate([column_blocks(w_up, 8), column_blocks(w_down, 8)], axis=2)
-        wide = wide.reshape(2, 4, shard_rows, -1)
-        wide_near = lax.dynamic_index_in_dim(wide, z, 0, keepdims=False)
-        wide_far = swap(lax.dynamic_index_in_dim(wide, 1 - z, 0, keepdims=False), "z")
+        first = gather_rows(place(swap_blocks(first, rank), rank))
         mid = jnp.concatenate([column_blocks(w_cross[:, 0], 4), column_blocks(w_cross_out, 4)], axis=2)
-        mid = gather_rows(trade(mid).reshape(4 * shard_rows, 2 * group), DATA)
-        wide_near, wide_far = trade(wide_near), trade(wide_far)
-        mlp = jnp.concatenate(
-            [jnp.where(z == 0, wide_near, wide_far), jnp.where(z == 0, wide_far, wide_near)],
-            axis=0,
-        )
-        mlp = gather_rows(mlp.reshape(8 * shard_rows, -1), PAIR_DATA)
+        mid = gather_rows(trade(mid))
+        up = gather_rows(trade(column_blocks(w_up, 4)))
+        down = gather_rows(trade(column_blocks(w_down, 4)))
 
         positions = lax.axis_index("y") * local_rows + jnp.arange(local_rows, dtype=jnp.int32)
         ranks = jnp.arange(full_length, dtype=jnp.int32)
@@ -745,8 +740,8 @@
         gains = layer_order(norm_gains)
         gain_a, gain_b, gain_c = gains[:1], gains[1:2], gains[2:]
         start_x, attn_in, grad_top = start(
-            outer(hidden.reshape(tokens, width), layer_order),
-            outer(cotangent.reshape(tokens, width), layer_order),
+            outer(hidden.reshape(tokens, width)),
+            outer(cotangent.reshape(tokens, width)),
             masked,
             layer_order(mask_embed)[None],
             gain_a,
@@ -762,9 +757,7 @@
         text_kv = sum_data(trade(kv_part).astype(F32).sum(axis=0))
         attn_in, text_kv = lax.optimization_barrier((attn_in, text_kv))
 
-        grad_y = outer(grad_top, pair_order)
-        grad_y = jnp.concatenate([grad_y, swap(grad_y, "z")], axis=0)
-        grad_y = spread(grad_y)
+        grad_y = spread(grad_top).reshape(4 * tokens, width)
 
         attn_in, projected = gather_mm(attn_in, rank, first, 0, 3 * group, "qkv_mm")
         self_mixed = self_forward(projected, 2 * images)
@@ -777,50 +770,47 @@
         parts = scatter_tokens(mm_scatter(cross_mixed, rank, mid, group, "cross_out_mm"))
         after_cross, mlp_in = add_norm([after_attn] + parts, gain_c)
 
-        mlp_in = outer(mlp_in, pair_order)
-        mlp_in = [gather_tokens(mlp_in), gather_tokens(swap(mlp_in, "z"))]
-        runs = [
-            feed_forward(mlp_in[side], grad_y, side, rank, mlp, pair_unit, pair)
-            for side in range(2)
-        ]
-        mlp_in, mlp_grad_y, activated, grad_pre = zip(*runs)
-        back = [mm_scatter(grad_pre[s], rank, mlp, 0, "up_back", pair_unit, pair) for s in range(2)]
-        back, grad_pre = lax.optimization_barrier((back, grad_pre))
-        mlp_part = grad_products([(mlp_grad_y, activated), (mlp_in, grad_pre)], "mlp_grads")
-        mlp_rows = scatter_grad(mlp_part, PAIR_DATA)
-        near = scatter_tokens(back[0])
-        far = sum(part.astype(F32) for part in scatter_tokens(back[1])).astype(BF)
-        terms = near + [swap(far, "z")]
-        if not inside:
-            terms = [pair_order(sum(part.astype(F32) for part in terms))]
-        grad_after_cross, cross_branch, gain_grad_c = norm_back(terms, grad_top, after_cross, gain_c)
+        mlp_in, activated, slope = feed_up(gather_tokens(mlp_in), rank, up)
+        down_part = grad_products([([grad_y], [activated])], "down_grads")
+        slope, down_part = lax.optimization_barrier((slope, down_part))
+        down_rows = scatter_grad(down_part)
+        grad_pre = feed_down(grad_y, slope, down)
+        parts = mm_scatter(grad_pre, rank, up, 0, "up_back")
+        parts, grad_pre = lax.optimization_barrier((parts, grad_pre))
+        up_part = grad_products([([mlp_in], [grad_pre])], "up_grads")
+        grad_after_cross, cross_branch, gain_grad_c = norm_back(
+            scatter_tokens(parts), grad_top, after_cross, gain_c
+        )
 
         cross_branch, grad_cross_mixed = gather_mm(
             gather_tokens(cross_branch), rank, mid, group, group, "cross_out_back"
         )
         grad_cq, kv_grad = cross_back(cross_queries, text_kv, grad_cross_mixed)
+        up_part, down_rows, kv_grad = lax.optimization_barrier((up_part, down_rows, kv_grad))
+        up_rows = scatter_grad(up_part)
         parts = scatter_tokens(mm_scatter(grad_cq, rank, mid, 0, "query_back"))
         grad_after_attn, attn_branch, gain_grad_b = norm_back(
             parts, grad_after_cross, after_attn, gain_b
         )
-        cross_part = grad_products(
-            [([cross_in], [grad_cq]), ([cross_branch], [cross_mixed])], "cross_grads"
-        )
-        cross_part, mlp_rows = lax.optimization_barrier((cross_part, mlp_rows))
-        cross_rows = scatter_grad(cross_part, DATA)
 
         attn_branch, grad_self_mixed = gather_mm(
             gather_tokens(attn_branch), rank, first, 3 * group, group, "out_back"
         )
         grad_projected = self_back(projected, grad_self_mixed, 2 * images)
-        attn_part = grad_products(
-            [([attn_in], [grad_projected]), ([attn_branch], [self_mixed])], "attn_grads"
-        )
-        attn_part, cross_rows = lax.optimization_barrier((attn_part, cross_rows))
-        attn_rows = scatter_grad(attn_part, DATA)
-        grad_projected, activated, kv_grad, mlp_rows, attn_part = lax.optimization_barrier(
-            (grad_projected, activated, kv_grad, mlp_rows, attn_part)
-        )
+        rest_part = grad_products(
+            [
+                ([attn_in], [grad_projected]),
+                ([attn_branch], [self_mixed]),
+                ([cross_in], [grad_cq]),
+                ([cross_branch], [cross_mixed]),
+            ],
+            "attention_grads",
+        )
+        grad_projected, activated, kv_grad, rest_part = lax.optimization_barrier(
+            (grad_projected, activated, kv_grad, rest_part)
+        )
+        rest_part, up_rows = lax.optimization_barrier((rest_part, up_rows))
+        rest_rows = scatter_grad(rest_part)
         grad_attn = mm_t(grad_projected, first[:, : 3 * group]).astype(BF)
         grad_attn = trade(grad_attn.reshape(4, tokens, width))
         grad_hidden, gain_grad_a, mask_grad = last_back(
@@ -835,15 +825,8 @@
         sums = jnp.concatenate([gain_grad_a, gain_grad_b, gain_grad_c, mask_grad], axis=0)
         sums = layer_order(sum_all(sums))
 
-        active = jnp.concatenate([a.reshape(4, tokens, -1) for a in activated], axis=1)
-        result = mm_t(active.reshape(8 * tokens, -1), mlp[:, mlp.shape[1] // 2 :]).astype(BF)
-        result = trade(result.reshape(4, 2 * tokens, width))
-        far = swap(result[:, tokens:].astype(F32).sum(axis=0).astype(BF), "z")
-        terms = [(result, k) for k in range(4)] + [far]
-        if not inside:
-            near = result[:, :tokens].astype(F32).sum(axis=0)
-            terms = [pair_order(near + far.astype(F32))]
-        output = layer_output(after_cross, terms, pair_unit, pair, unit, order)
+        result = trade(mm_t(activated, down).astype(BF).reshape(4, tokens, width))
+        output = layer_output(after_cross, [(result, k) for k in range(4)], unit, order)
 
         kv_grads = spread(sum_data(kv_grad)).reshape(4, -1, 2, group)
         kv_grads = kv_grads.transpose(1, 2, 0, 3).reshape(-1, 2 * width)
@@ -854,18 +837,14 @@
         caption_own = sum_data(trade(caption_part).astype(F32).sum(axis=0))
         grad_caption = spread(caption_own).transpose(1, 0, 2).reshape(-1, text_width).astype(F32)
 
-        half_rows = 4 * shard_rows
-        near = lax.dynamic_slice_in_dim(mlp_rows, z * half_rows, half_rows, 0)
-        far = swap(lax.dynamic_slice_in_dim(mlp_rows, (1 - z) * half_rows, half_rows, 0), "z")
-        near, far = (trade(part.reshape(4, shard_rows, -1)) for part in (near, far))
-        down_grad, up_grad = finish_pair(near, far, z)
-        grad_cross, cross_out_grad = finish_cross(
-            trade(cross_rows.reshape(4, shard_rows, -1)), kv_weight_grad
-        )
-        qkv_grad, out_grad = finish_attention(trade(attn_rows.reshape(4, shard_rows, -1)))
+        down_grad = finish_wide(trade(down_rows))
+        up_grad = finish_wide(trade(up_rows))
+        qkv_grad, out_grad, grad_cross, cross_out_grad = finish_all(
+            swap_blocks(rest_rows, rank), kv_weight_grad, rank
+        )
         return (
-            outer(output, layer_order).reshape(hidden.shape),
-            outer(grad_hidden, layer_order).reshape(hidden.shape),
+            outer(output).reshape(hidden.shape),
+            outer(grad_hidden).reshape(hidden.shape),
             grad_caption,
             sums[:3],
             sums[3],
@@ -883,8 +862,8 @@
 
 def solution(mesh):
     z_size = mesh.shape["img"] // 4
-    inner = Mesh(mesh.devices.reshape(z_size // 2, 2, 2, 2, 2), ("w", "z", "x", "c", "y"))
-    image = ("w", "z", "x", "c")
+    inner = Mesh(mesh.devices.reshape(z_size, 2, 2, 2), ("z", "x", "c", "y"))
+    image = ("z", "x", "c")
     tokens = P(image, "y", None)
     rows = P(image + ("y",))
     in_specs = (tokens, P(image, None), P(image), P(), P(), P()) + (rows,) * 7 + (tokens,)

time: 942 us -> 752 us (0.80)
  waiting for transfers between devices: 457 us -> 305 us
  starting transfers between devices: 124 us -> 103 us
  blocking collectives: 88.9 us -> 99.3 us
  other arithmetic: 18.2 us -> 8.59 us
    ppermute x60 -> x49, waiting for transfers between devices: 278 us -> 181 us  [swap(): return lax.ppermute(values, axis, PAIR)]
    all_to_all x15 -> x11, waiting for transfers between devices: 138 us -> 73.1 us  [trade(): return lax.all_to_all(blocks, axes, 0, 0, tiled=True)]
    ppermute x60 -> x49, starting transfers between devices: 62.3 us -> 47.3 us  [swap(): return lax.ppermute(values, axis, PAIR)]
    pallas_call x12 -> x11, Pallas kernels: 67 us -> 52.8 us  [call(): pl.pallas_call(kernel, grid_spec=spec, **options)]
    all_to_all x15 -> x11, starting transfers between devices: 58.2 us -> 44.6 us  [trade(): return lax.all_to_all(blocks, axes, 0, 0, tiled=True)]
    all_to_all x6 -> x7, blocking collectives: 88.9 us -> 99.3 us  [trade(): return lax.all_to_all(blocks, axes, 0, 0, tiled=True)]
    pallas_call x16 -> x17, Pallas kernels: 57.5 us -> 66.2 us  [call(): pl.pallas_call(kernel, grid=grid, in_specs=in_specs, out_specs=out_specs,...]
    unnamed x202 -> x152, local copies, waits for them, and re-layouts: 46.1 us -> 43.9 us
  transfers between devices with their start and end apart: 82 -> 71, of which waited for: 52 -> 49; matrix products, arithmetic and copies ran while one was open for 8% -> 7% of each run, Pallas kernels for 10% -> 15%
where the time goes in v7:
time: 752 us; the launch traced here: 743 us
  waiting for transfers between devices  305 us (41%)
  Pallas kernels  119 us (16%)
  starting transfers between devices  103 us (14%)
  blocking collectives  99.3 us (13%)
  local copies, waits for them, and re-layouts  69.5 us (9%)
  matrix products  21.8 us (3%)
  between operations  16.6 us (2%)
  other arithmetic  8.59 us (1%)
    ppermute x49, waiting for transfers between devices, swap(): return lax.ppermute(values, axis, PAIR)  181 us
    all_to_all x7, blocking collectives, trade(): return lax.all_to_all(blocks, axes, 0, 0, tiled=True)  99.3 us
    all_to_all x11, waiting for transfers between devices, trade(): return lax.all_to_all(blocks, axes, 0, 0, tiled=True)  73.1 us
    pallas_call x17, Pallas kernels, call(): pl.pallas_call(kernel, grid=grid, in_specs=in_specs, out_specs=out_specs,...  66.2 us
    pallas_call x11, Pallas kernels, call(): pl.pallas_call(kernel, grid_spec=spec, **options)  52.8 us
    ppermute x49, starting transfers between devices, swap(): return lax.ppermute(values, axis, PAIR)  47.3 us
    all_to_all x11, starting transfers between devices, trade(): return lax.all_to_all(blocks, axes, 0, 0, tiled=True)  44.6 us
    unnamed x152, local copies, waits for them, and re-layouts  43.9 us
  transfers between devices with their start and end apart: 71, of which 49 were waited for; matrix products, arithmetic and copies ran while one was open for 7% of the time, Pallas kernels for 15%

profile of v7, /device:TPU:0, one launch (start us, length us, event | category | flops | bytes accessed | tf_op | source)
XLA Modules:
  0.0 743.3 jit_solution(857456633556622417)
XLA Ops:
  30.7 11.8 %all_to_all.90 = bf16[4,64,1024]{2,1,0:T(8,128)(2,1)} all-to-all(bf16[4,64,1024]{2,1,0:T(8,128)(2,1)S(1)} %pad_maximum_fusion.2), channel_id=1, replica_groups=mesh['z'=4,'x'=2,'c'=2,'y'=2] {'x','y'}, dimensions={0} | all-to-all | bytes 1048576 | tf_op jit(solution)/shard_map/all_to_all | solution.py:49
  42.7 16.1 %all_to_all.91 = bf16[4,64,2048]{2,1,0:T(8,128)(2,1)} all-to-all(bf16[4,64,2048]{2,1,0:T(8,128)(2,1)S(1)} %bitcast.179), channel_id=1, replica_groups=mesh['z'=4,'x'=2,'c'=2,'y'=2] {'x','y'}, dimensions={0} | all-to-all | bytes 2097152 | tf_op jit(solution)/shard_map/all_to_all | solution.py:49
  59.1 14.9 %all_to_all.92 = bf16[4,64,2048]{2,1,0:T(8,128)(2,1)} all-to-all(bf16[4,64,2048]{2,1,0:T(8,128)(2,1)S(1)} %bitcast.180), channel_id=1, replica_groups=mesh['z'=4,'x'=2,'c'=2,'y'=2] {'x','y'}, dimensions={0} | all-to-all | bytes 2097152 | tf_op jit(solution)/shard_map/all_to_all | solution.py:49
  83.8 9.2 %all-to-all-done = bf16[4,128,1024]{1,2,0:T(8,128)(2,1)} async-done(((bf16[4,128,1024]{1,2,0:T(8,128)(2,1)}), bf16[4,128,1024]{1,2,0:T(8,128)(2,1)}, u32[]{:S(2)}, u32[]{:S(2)}) %all-to-all-start) | async-done | bytes 1048608 | tf_op jit(solution)/shard_map/all_to_all | solution.py:49
  102.7 10.3 %all-to-all-done.1 = bf16[4,16,1024]{2,1,0:T(8,128)(2,1)S(1)} async-done(((bf16[4,16,1024]{2,1,0:T(8,128)(2,1)}), bf16[4,16,1024]{2,1,0:T(8,128)(2,1)S(1)}, u32[]{:S(2)}, u32[]{:S(2)}) %all-to-all-start.1) | async-done | bytes 131104 | tf_op jit(solution)/shard_map/all_to_all | solution.py:49
  132.4 31.5 %collective-permute-done.1.refs_2_ = bf16[128,2048]{1,0:T(8,128)(2,1)} collective-permute-done((bf16[128,2048]{1,0:T(8,128)(2,1)}, bf16[128,2048]{1,0:T(8,128)(2,1)}, u32[]{:S(2)}, u32[]{:S(2)}) %collective-permute-start.1) | collective-permute-done | bytes 524320 | tf_op jit(solution)/shard_map/ppermute | solution.py:45
  217.7 9.3 %collective-permute-done.14.refs_2_ = bf16[128,2048]{1,0:T(8,128)(2,1)S(1)} collective-permute-done((bf16[128,2048]{1,0:T(8,128)(2,1)S(1)}, bf16[128,2048]{1,0:T(8,128)(2,1)S(1)}, u32[]{:S(2)}, u32[]{:S(2)}) %collective-permute-start.14) | collective-permute-done | bytes 524320 | tf_op jit(solution)/shard_map/ppermute | solution.py:45
  299.7 11.9 %feed_up.1 = (bf16[512,2048]{1,0:T(8,128)(2,1)S(1)}, bf16[512,2048]{1,0:T(8,128)(2,1)}, f32[512,2048]{1,0:T(8,128)}) custom-call(s32[1]{0:T(128)} %bitcast.r, bf16[128,2048]{1,0:T(8,128)(2,1)S(1)} %copy-done.50, bf16[128,2048]{1,0:T(8,128)(2,1)S(1)} %copy-done.46, bf16[128,2048]{1,0:T(8,128)(2,1)S(1)} %copy-done.44, ...), custom_call_target="tpu_custom_call" | custom-call | flops 4294967296 | bytes 12582912 | tf_op jit(solution)/shard_map/feed_up/pallas_call | solution.py:112
  327.5 9.6 %feed_down.1.x.refs_1_ = bf16[512,2048]{1,0:T(8,128)(2,1)S(1)} custom-call(bf16[512,2048]{1,0:T(8,128)(2,1)S(1)} %bitcast.157, f32[512,2048]{1,0:T(8,128)} %get-tuple-element.118.slope_ref, bf16[2048,2048]{1,0:T(8,128)(2,1)} %all-gather.11.cloned.1.call-done.down), custom_call_target="tpu_custom_call" | custom-call | flops 4294967296 | bytes 25165824 | tf_op jit(solution)/shard_map/feed_down/pallas_call | solution.py:101
  356.5 10.2 %collective-permute-done.28.refs_2_ = bf16[128,2048]{1,0:T(8,128)(2,1)S(1)} collective-permute-done((bf16[128,2048]{1,0:T(8,128)(2,1)S(1)}, bf16[128,2048]{1,0:T(8,128)(2,1)S(1)}, u32[]{:S(2)}, u32[]{:S(2)}) %collective-permute-start.28) | collective-permute-done | bytes 524320 | tf_op jit(solution)/shard_map/ppermute | solution.py:45
  372.7 10.3 %collective-permute-done.30.refs_2_ = bf16[128,2048]{1,0:T(8,128)(2,1)S(1)} collective-permute-done((bf16[128,2048]{1,0:T(8,128)(2,1)S(1)}, bf16[128,2048]{1,0:T(8,128)(2,1)S(1)}, u32[]{:S(2)}, u32[]{:S(2)}) %collective-permute-start.30) | collective-permute-done | bytes 524320 | tf_op jit(solution)/shard_map/ppermute | solution.py:45
  401.7 16.1 %reduce-scatter.4.cloned.1.call-done = bf16[256,2048]{1,0:T(8,128)(2,1)} async-done(((bf16[2048,2048]{1,0:T(8,128)(2,1)}), bf16[256,2048]{1,0:T(8,128)(2,1)}) %reduce-scatter.4.cloned.1.call-update) | async-done | bytes 1048592 | tf_op jit(solution)/shard_map/reduce_scatter | solution.py:88
  432.3 8.7 %collective-permute-done.36.refs_2_ = bf16[128,2048]{1,0:T(8,128)(2,1)S(1)} collective-permute-done((bf16[128,2048]{1,0:T(8,128)(2,1)S(1)}, bf16[128,2048]{1,0:T(8,128)(2,1)S(1)}, u32[]{:S(2)}, u32[]{:S(2)}) %collective-permute-start.36) | collective-permute-done | bytes 524320 | tf_op jit(solution)/shard_map/ppermute | solution.py:45
  445.5 9.7 %collective-permute-done.38.refs_2_ = bf16[128,2048]{1,0:T(8,128)(2,1)S(1)} collective-permute-done((bf16[128,2048]{1,0:T(8,128)(2,1)S(1)}, bf16[128,2048]{1,0:T(8,128)(2,1)S(1)}, u32[]{:S(2)}, u32[]{:S(2)}) %collective-permute-start.38) | collective-permute-done | bytes 524320 | tf_op jit(solution)/shard_map/ppermute | solution.py:45
  472.5 12.7 %attention_grads.1 = bf16[2048,3072]{1,0:T(8,128)(2,1)} custom-call(bf16[512,2048]{1,0:T(8,128)(2,1)S(1)} %copy-done.21, bf16[512,2048]{1,0:T(8,128)(2,1)} %copy-done.24, bf16[512,2048]{1,0:T(8,128)(2,1)} %copy-done.22, bf16[512,2048]{1,0:T(8,128)(2,1)} %copy-done.23, bf16[512,1536]{1,0:T(8,128)(2,1)S(1)} %self_back.1.refs_4_, ...), custom_call_target="tpu_custom_call" | custom-call | flops 6442450944 | bytes 25165824 | tf_op jit(solution)/shard_map/attention_grads/pallas_call | solution.py:101
  485.2 22.8 %reduce-scatter.6.cloned.1.call-done = bf16[256,2048]{1,0:T(8,128)(2,1)} async-done(((bf16[2048,2048]{1,0:T(8,128)(2,1)}), bf16[256,2048]{1,0:T(8,128)(2,1)}) %reduce-scatter.6.cloned.1.call-update) | async-done | bytes 1048592 | tf_op jit(solution)/shard_map/reduce_scatter | solution.py:88
  510.6 9.9 %all_to_all.93 = bf16[4,16,1024]{2,1,0:T(8,128)(2,1)S(1)} all-to-all(bf16[4,16,1024]{2,1,0:T(8,128)(2,1)S(1)} %bitcast.201), channel_id=1, replica_groups=mesh['z'=4,'x'=2,'c'=2,'y'=2] {'z'}, dimensions={0} | all-to-all | bytes 262144 | tf_op jit(solution)/shard_map/all_to_all | solution.py:49
  520.6 12.2 %all_to_all.94 = bf16[4,16,1024]{2,1,0:T(8,128)(2,1)S(1)} all-to-all(bf16[4,16,1024]{2,1,0:T(8,128)(2,1)S(1)} %broadcast_in_dim.14), channel_id=1, replica_groups=mesh['z'=4,'x'=2,'c'=2,'y'=2] {'z'}, dimensions={0} | all-to-all | bytes 262144 | tf_op jit(solution)/shard_map/all_to_all | solution.py:49
  534.5 18.0 %all_to_all.95 = bf16[4,128,1024]{1,2,0:T(8,128)(2,1)S(1)} all-to-all(bf16[4,128,1024]{1,2,0:T(8,128)(2,1)S(1)} %broadcast_in_dim.15), channel_id=1, replica_groups=mesh['z'=4,'x'=2,'c'=2,'y'=2] {'x','y'}, dimensions={0} | all-to-all | bytes 2097152 | tf_op jit(solution)/shard_map/all_to_all | solution.py:49
  554.3 16.4 %all_to_all.96 = bf16[4,128,1024]{2,1,0:T(8,128)(2,1)} all-to-all(bf16[4,128,1024]{2,1,0:T(8,128)(2,1)S(1)} %bitcast.178), channel_id=1, replica_groups=mesh['z'=4,'x'=2,'c'=2,'y'=2] {'x','y'}, dimensions={0} | all-to-all | bytes 2097152 | tf_op jit(solution)/shard_map/all_to_all | solution.py:49
  601.9 24.2 %all-to-all-done.8.refs_0_.refs_1_.refs_2_.refs_3_ = bf16[4,128,2048]{2,1,0:T(8,128)(2,1)S(1)} async-done(((bf16[4,128,2048]{2,1,0:T(8,128)(2,1)}), bf16[4,128,2048]{2,1,0:T(8,128)(2,1)S(1)}, u32[]{:S(2)}, u32[]{:S(2)}) %all-to-all-start.8) | async-done | bytes 2097184 | tf_op jit(solution)/shard_map/all_to_all | solution.py:49
  630.9 9.9 %convolution_convert_fusion.2 = bf16[512,2048]{1,0:T(8,128)(2,1)} fusion(bf16[512,2048]{1,0:T(8,128)(2,1)} %get-tuple-element.150.refs_1_, bf16[2048,2048]{1,0:T(8,128)(2,1)} %all-gather.11.cloned.1.call-done.down), kind=kOutput, calls=%fused_computation.5 | convolution fusion | flops 4296015872 | bytes 12582912 | tf_op jit(solution)/shard_map/dot_general | solution.py:25
  652.4 16.9 %all-to-all-done.7.refs_0_.refs_1_.refs_2_.refs_3_ = bf16[4,128,2048]{2,1,0:T(8,128)(2,1)S(1)} async-done(((bf16[4,128,2048]{2,1,0:T(8,128)(2,1)}), bf16[4,128,2048]{2,1,0:T(8,128)(2,1)S(1)}, u32[]{:S(2)}, u32[]{:S(2)}) %all-to-all-start.7) | async-done | bytes 2097184 | tf_op jit(solution)/shard_map/all_to_all | solution.py:49
  676.8 11.6 %collective-permute-done.46 = f32[4,2048]{1,0:T(4,128)S(1)} collective-permute-done((f32[4,2048]{1,0:T(4,128)S(1)}, f32[4,2048]{1,0:T(4,128)S(1)}, u32[]{:S(2)}, u32[]{:S(2)}) %collective-permute-start.46) | collective-permute-done | bytes 32800 | tf_op jit(solution)/shard_map/ppermute | solution.py:45
  (420 shorter events, 392.6 us)
Async XLA Ops:
  7.2 167.3 %all-gather.5.cloned.1.call-start = ((), (), s32[]{:S(2)}) async-start(), calls=%async_computation.21 | async-start | bytes 9437184 | tf_op jit(solution)/shard_map/all_gather | solution.py:84
  30.3 202.2 %all-gather.7.cloned.1.call-start = ((), (), s32[]{:S(2)}) async-start(), calls=%async_computation.22 | async-start | bytes 4718592 | tf_op jit(solution)/shard_map/all_gather | solution.py:84
  42.5 247.8 %all-gather.9.cloned.1.call-start = ((), (), s32[]{:S(2)}) async-start(), calls=%async_computation.23 | async-start | bytes 9437184 | tf_op jit(solution)/shard_map/all_gather | solution.py:84
  58.9 268.6 %all-gather.11.cloned.1.call-start = ((), (), s32[]{:S(2)}) async-start(), calls=%async_computation.24 | async-start | bytes 9437184 | tf_op jit(solution)/shard_map/all_gather | solution.py:84
  78.8 14.2 %all-to-all-start = ((bf16[4,128,1024]{1,2,0:T(8,128)(2,1)}), bf16[4,128,1024]{1,2,0:T(8,128)(2,1)}, u32[]{:S(2)}, u32[]{:S(2)}) async-start(bf16[4,128,1024]{1,2,0:T(8,128)(2,1)} %bitcast.12), calls=%async_computation | async-start | bytes 2097152 | tf_op jit(solution)/shard_map/all_to_all | solution.py:49
  96.9 16.2 %all-to-all-start.1 = ((bf16[4,16,1024]{2,1,0:T(8,128)(2,1)}), bf16[4,16,1024]{2,1,0:T(8,128)(2,1)S(1)}, u32[]{:S(2)}, u32[]{:S(2)}) async-start(bf16[4,16,1024]{2,1,0:T(8,128)(2,1)} %bitcast.16), calls=%async_computation.1 | async-start | bytes 262144 | tf_op jit(solution)/shard_map/all_to_all | solution.py:49
  125.1 65.1 %all-to-all-start.3 = ((bf16[4,128,2048]{2,1,0:T(8,128)(2,1)}), bf16[4,128,2048]{2,1,0:T(8,128)(2,1)S(1)}, u32[]{:S(2)}, u32[]{:S(2)}) async-start(bf16[4,128,2048]{2,1,0:T(8,128)(2,1)} %broadcast_in_dim.13), calls=%async_computation.3 | async-start | bytes 4194304 | tf_op jit(solution)/shard_map/all_to_all | solution.py:49
  128.7 289.1 %reduce-scatter.4.cloned.1.call-start = ((), (), s32[]{:S(2)}) async-start(), calls=%async_computation.25 | async-start | bytes 9437184 | tf_op jit(solution)/shard_map/reduce_scatter | solution.py:88
  128.9 34.9 %collective-permute-start.1 = (bf16[128,2048]{1,0:T(8,128)(2,1)}, bf16[128,2048]{1,0:T(8,128)(2,1)}, u32[]{:S(2)}, u32[]{:S(2)}) collective-permute-start(bf16[128,2048]{1,0:T(8,128)(2,1)} %copy-done.47), channel_id=1, source_target_pairs={{0,4},{4,0},{1,5},{5,1},{2,6},{6,2},{3,7},{7,3},{8,12},{12,8},{9,1... | collective-permute-start | bytes 1572872 | tf_op jit(solution)/shard_map/ppermute | solution.py:45
  130.9 35.4 %collective-permute-start = (bf16[128,2048]{1,0:T(8,128)(2,1)}, bf16[128,2048]{1,0:T(8,128)(2,1)}, u32[]{:S(2)}, u32[]{:S(2)}) collective-permute-start(bf16[128,2048]{1,0:T(8,128)(2,1)} %copy-done.47), channel_id=1, source_target_pairs={{0,1},{1,0},{2,3},{3,2},{4,5},{5,4},{6,7},{7,6},{8,9},{9,8},{10,11... | collective-permute-start | bytes 1572872 | tf_op jit(solution)/shard_map/ppermute | solution.py:45
  132.4 35.6 %collective-permute-start.5 = (bf16[64,1024]{1,0:T(8,128)(2,1)S(1)}, bf16[64,1024]{1,0:T(8,128)(2,1)S(1)}, u32[]{:S(2)}, u32[]{:S(2)}) collective-permute-start(bf16[64,1024]{1,0:T(8,128)(2,1)S(1)} %bitcast.198), channel_id=1, source_target_pairs={{0,2},{2,0},{1,3},{3,1},{4,6},{6,4},{5,7},{7,5},{8,10},{10,8},{9,1... | collective-permute-start | bytes 393224 | tf_op jit(solution)/shard_map/ppermute | solution.py:45
  322.4 185.6 %reduce-scatter.6.cloned.1.call-start = ((), (), s32[]{:S(2)}) async-start(), calls=%async_computation.26 | async-start | bytes 9437184 | tf_op jit(solution)/shard_map/reduce_scatter | solution.py:88
  417.8 282.1 %reduce-scatter.8.cloned.1.call-start = ((), (), s32[]{:S(2)}) async-start(), calls=%async_computation.27 | async-start | bytes 14155776 | tf_op jit(solution)/shard_map/reduce_scatter | solution.py:88
  570.8 15.8 %all-to-all-start.17 = ((bf16[4,64,2048]{2,1,0:T(8,128)(2,1)}), bf16[4,64,2048]{2,1,0:T(8,128)(2,1)}, u32[]{:S(2)}, u32[]{:S(2)}) async-start(bf16[4,64,2048]{2,1,0:T(8,128)(2,1)} %bitcast.194), calls=%async_computation.20 | async-start | bytes 2097152 | tf_op jit(solution)/shard_map/all_to_all | solution.py:49
  598.2 27.8 %all-to-all-start.8 = ((bf16[4,128,2048]{2,1,0:T(8,128)(2,1)}), bf16[4,128,2048]{2,1,0:T(8,128)(2,1)S(1)}, u32[]{:S(2)}, u32[]{:S(2)}) async-start(bf16[4,128,2048]{2,1,0:T(8,128)(2,1)} %bitcast.185), calls=%async_computation.9 | async-start | bytes 4194304 | tf_op jit(solution)/shard_map/all_to_all | solution.py:49
  626.7 14.0 %all-to-all-start.14 = ((bf16[4,16,1024]{2,1,0:T(8,128)(2,1)}), bf16[4,16,1024]{2,1,0:T(8,128)(2,1)S(1)}, u32[]{:S(2)}, u32[]{:S(2)}) async-start(bf16[4,16,1024]{2,1,0:T(8,128)(2,1)} %broadcast_in_dim.16), calls=%async_computation.15 | async-start | bytes 262144 | tf_op jit(solution)/shard_map/all_to_all | solution.py:49
  640.8 28.6 %all-to-all-start.7 = ((bf16[4,128,2048]{2,1,0:T(8,128)(2,1)}), bf16[4,128,2048]{2,1,0:T(8,128)(2,1)S(1)}, u32[]{:S(2)}, u32[]{:S(2)}) async-start(bf16[4,128,2048]{2,1,0:T(8,128)(2,1)} %bitcast.184), calls=%async_computation.8 | async-start | bytes 4194304 | tf_op jit(solution)/shard_map/all_to_all | solution.py:49
  651.1 23.6 %collective-permute-start.45 = (f32[4,2048]{1,0:T(4,128)S(1)}, f32[4,2048]{1,0:T(4,128)S(1)}, u32[]{:S(2)}, u32[]{:S(2)}) collective-permute-start(f32[4,2048]{1,0:T(4,128)S(1)} %pad_maximum_fusion.12), channel_id=1, source_target_pairs={{0,2},{2,0},{1,3},{3,1},{4,6},{6,4},{5,7},{7,5},{8,10},{10,8},{9,1... | collective-permute-start | bytes 98312 | tf_op jit(solution)/shard_map/ppermute | solution.py:45
  670.4 24.9 %all-to-all-start.15 = ((bf16[4,128,1024]{2,1,0:T(8,128)(2,1)}), bf16[4,128,1024]{2,1,0:T(8,128)(2,1)}, u32[]{:S(2)}, u32[]{:S(2)}) async-start(bf16[4,128,1024]{2,1,0:T(8,128)(2,1)} %broadcast_in_dim.17), calls=%async_computation.16 | async-start | bytes 2097152 | tf_op jit(solution)/shard_map/all_to_all | solution.py:49
  674.8 13.6 %collective-permute-start.46 = (f32[4,2048]{1,0:T(4,128)S(1)}, f32[4,2048]{1,0:T(4,128)S(1)}, u32[]{:S(2)}, u32[]{:S(2)}) collective-permute-start(f32[4,2048]{1,0:T(4,128)S(1)} %fusion.16), channel_id=1, source_target_pairs={{0,4},{4,0},{1,5},{5,1},{2,6},{6,2},{3,7},{7,3},{8,12},{12,8},{9,1... | collective-permute-start | bytes 98312 | tf_op jit(solution)/shard_map/ppermute | solution.py:45
  695.3 24.8 %all-to-all-start.16 = ((bf16[4,64,2048]{2,1,0:T(8,128)(2,1)}), bf16[4,64,2048]{2,1,0:T(8,128)(2,1)}, u32[]{:S(2)}, u32[]{:S(2)}) async-start(bf16[4,64,2048]{2,1,0:T(8,128)(2,1)} %bitcast.193), calls=%async_computation.19 | async-start | bytes 2097152 | tf_op jit(solution)/shard_map/all_to_all | solution.py:49
  702.4 21.9 %collective-permute-start.52 = (bf16[64,3072]{1,0:T(8,128)(2,1)}, bf16[64,3072]{1,0:T(8,128)(2,1)}, u32[]{:S(2)}, u32[]{:S(2)}) collective-permute-start(bf16[64,3072]{1,0:T(8,128)(2,1)} %get-tuple-element.240), channel_id=1, source_target_pairs={{0,5},{1,4},{4,1},{5,0},{2,7},{3,6},{6,3},{7,2},{8,13},{9,12},{12,... | collective-permute-start | bytes 1179656 | tf_op jit(solution)/shard_map/ppermute | solution.py:79
  705.3 22.7 %collective-permute-start.51 = (bf16[64,3072]{1,0:T(8,128)(2,1)}, bf16[64,3072]{1,0:T(8,128)(2,1)}, u32[]{:S(2)}, u32[]{:S(2)}) collective-permute-start(bf16[64,3072]{1,0:T(8,128)(2,1)} %get-tuple-element.241), channel_id=1, source_target_pairs={{0,4},{4,0},{1,5},{5,1},{2,6},{6,2},{3,7},{7,3},{8,12},{12,8},{9,1... | collective-permute-start | bytes 1179656 | tf_op jit(solution)/shard_map/ppermute | solution.py:45
  705.9 22.1 %collective-permute-start.50 = (bf16[64,3072]{1,0:T(8,128)(2,1)}, bf16[64,3072]{1,0:T(8,128)(2,1)}, u32[]{:S(2)}, u32[]{:S(2)}) collective-permute-start(bf16[64,3072]{1,0:T(8,128)(2,1)} %get-tuple-element.242), channel_id=1, source_target_pairs={{0,1},{1,0},{2,3},{3,2},{4,5},{5,4},{6,7},{7,6},{8,9},{9,8},{10,11... | collective-permute-start | bytes 1179656 | tf_op jit(solution)/shard_map/ppermute | solution.py:45
  (122 other events, 980.3 us)
Sparse Core Ops, SparseCore 0:
  30.4 85.3 all-gather.4
  117.4 45.5 all-gather.6
  164.6 80.7 all-gather.8
  246.8 80.5 all-gather.10
  329.6 88.1 reduce-scatter.3
  419.9 87.9 reduce-scatter.5
  510.2 135.5 reduce-scatter.7

commit v8 on v7

--- a/solution.py
+++ b/solution.py
@@ -15,6 +15,7 @@
 PAIR = ((0, 1), (1, 0))
 GROUP = ("x", "y")
 DATA = ("z", "c")
+PLANE = ("x", "c", "y")
 VMEM = 48 * 1024 * 1024
 SCALE = 1.0 / math.sqrt(HD)
 SLOPE = math.sqrt(2.0 / math.pi)
@@ -84,8 +85,8 @@
     return lax.all_gather(rows.reshape(-1, rows.shape[-1]), DATA, axis=0, tiled=True)
 
 
-def scatter_grad(partial):
-    summed = lax.psum_scatter(partial, DATA, scatter_dimension=0, tiled=True)
+def scatter_grad(partial, axes):
+    summed = lax.psum_scatter(partial, axes, scatter_dimension=0, tiled=True)
     return summed.reshape(4, -1, summed.shape[-1])
 
 
@@ -540,38 +541,41 @@
     )
 
 
-def grad_products(pairs, name):
-    blocks = len(pairs[0][0])
+def grad_products(pairs, name, core=None, blocks=0):
+    count_in = len(pairs[0][0])
     tokens, width = pairs[0][0][0].shape
     widths = [y[0].shape[1] for _, y in pairs]
     total = sum(widths)
-    rows = 256
+    rows = 256 if core is None else width // (2 * blocks)
+    steps = width // rows if core is None else blocks
     step = 512
-    count = len(pairs) * blocks
-
-    def kernel(*refs):
+    count = len(pairs) * count_in
+
+    def kernel(r, *refs):
         out = refs[2 * count]
         offset = 0
         for k, wide in enumerate(widths):
-            left = [refs[k * blocks + b][...].T for b in range(blocks)]
+            left = [refs[k * count_in + b][...].T for b in range(count_in)]
             for at in range(0, wide, step):
                 out[:, offset + at : offset + at + step] = sum(
-                    mm(left[b], refs[count + k * blocks + b][:, at : at + step])
-                    for b in range(blocks)
+                    mm(left[b], refs[count + k * count_in + b][:, at : at + step])
+                    for b in range(count_in)
                 ).astype(BF)
             offset += wide
 
-    return call(
-        kernel,
-        (width // rows,),
-        [pl.BlockSpec((tokens, rows), lambda i: (0, i))] * count
-        + [pl.BlockSpec((tokens, w), lambda i: (0, 0)) for w in widths for _ in range(blocks)],
-        pl.BlockSpec((rows, total), lambda i: (i, 0)),
-        shape((width, total)),
+    pick = (lambda i, r: (0, i)) if core is None else (lambda i, r: (0, 2 * i + r[0]))
+    return call(
+        kernel,
+        (steps,),
+        [pl.BlockSpec((tokens, rows), pick)] * count
+        + [pl.BlockSpec((tokens, w), lambda i, r: (0, 0)) for w in widths for _ in range(count_in)],
+        pl.BlockSpec((rows, total), lambda i, r: (i, 0)),
+        shape((steps * rows, total)),
         [b for x, _ in pairs for b in x] + [b for _, y in pairs for b in y],
         name,
-        flops=2 * tokens * blocks * width * total,
+        flops=2 * tokens * count_in * steps * rows * total,
         size=4 * width * total,
+        rank=jnp.zeros((), jnp.int32) if core is None else core,
     )
 
 
@@ -656,30 +660,21 @@
 
 
 def make_local(z_size):
-    def sum_data(values):
-        rows, columns = values.shape
-        core = lax.axis_index("c")
-        halves = values.reshape(2, rows // 2, columns)
-        keep = lax.dynamic_index_in_dim(halves, core, 0, keepdims=False)
-        send = lax.dynamic_index_in_dim(halves, 1 - core, 0, keepdims=False)
-        mine = (keep + swap(send, "c")).astype(BF).reshape(z_size, -1, columns)
-        mine = trade(mine, "z").astype(F32).sum(axis=0).astype(BF)
-        mine = spread(mine, "z", z_size).reshape(rows // 2, columns)
-        other = swap(mine, "c")
-        return jnp.concatenate(
-            [jnp.where(core == 0, mine, other), jnp.where(core == 0, other, mine)], axis=0
-        )
+    def sum_z(values):
+        return spread(values, "z", z_size).astype(F32).sum(axis=0)
+
+    def by_plane(values, parts):
+        rows = values.shape[0]
+        shaped = values.reshape(2, rows // 2, parts, 2, 2, -1)
+        return shaped.transpose(3, 0, 4, 1, 2, 5).reshape(8, rows // 2, -1)
+
+    def from_plane(blocks, parts):
+        rows = blocks.shape[1]
+        shaped = blocks.reshape(2, 2, 2, rows, parts, -1)
+        return shaped.transpose(1, 3, 4, 0, 2, 5).reshape(2 * rows, -1)
 
     def sum_all(values):
-        for axis in ("c", "x", "y"):
-            values = values + swap(values, axis)
-        step = 1
-        while step < z_size:
-            values = values + lax.ppermute(
-                values, "z", tuple((k, k ^ step) for k in range(z_size))
-            )
-            step *= 2
-        return values
+        return sum_z(spread(values, PLANE, 8).sum(axis=0))
 
     def layer_order(values):
         shaped = values.reshape(values.shape[:-1] + (z_size, 2, 2, -1))
@@ -705,6 +700,7 @@
         full_length = mask_index.shape[1]
         shard_rows = w_qkv.shape[0]
         rank = lax.axis_index("x") * 2 + lax.axis_index("y")
+        core = lax.axis_index("c")
         tokens = images * local_rows
         group = width // 4
         text_width = caption.shape[1]
@@ -726,11 +722,6 @@
             axis=2,
         )
         first = gather_rows(place(swap_blocks(first, rank), rank))
-        mid = jnp.concatenate([column_blocks(w_cross[:, 0], 4), column_blocks(w_cross_out, 4)], axis=2)
-        mid = gather_rows(trade(mid))
-        up = gather_rows(trade(column_blocks(w_up, 4)))
-        down = gather_rows(trade(column_blocks(w_down, 4)))
-
         positions = lax.axis_index("y") * local_rows + jnp.arange(local_rows, dtype=jnp.int32)
         ranks = jnp.arange(full_length, dtype=jnp.int32)
         matches = (mask_index[:, :, None] == positions[None, None, :]) & (
@@ -749,19 +740,29 @@
             order,
         )
         attn_in = gather_tokens(attn_in)
+        mid = jnp.concatenate([column_blocks(w_cross[:, 0], 4), column_blocks(w_cross_out, 4)], axis=2)
+        attn_in, mid = lax.optimization_barrier((attn_in, mid))
+        mid = gather_rows(trade(mid))
 
         own_text = mm_t(caption, w_text).astype(BF)
         kv_rows = w_cross[:, 1:].reshape(shard_rows, 2 * width)
-        kv_part = mm(own_text, kv_rows).astype(BF)
-        kv_part = kv_part.reshape(-1, 2, 4, group).transpose(2, 0, 1, 3).reshape(4, -1, 2 * group)
-        text_kv = sum_data(trade(kv_part).astype(F32).sum(axis=0))
-        attn_in, text_kv = lax.optimization_barrier((attn_in, text_kv))
-
+        kv_part = by_plane(mm(own_text, kv_rows).astype(BF), 2)
+        text_kv = trade(kv_part, PLANE).astype(F32).sum(axis=0).astype(BF)
+        text_kv = sum_z(text_kv).astype(BF)
+        other = swap(text_kv, "c")
+        text_kv = jnp.concatenate(
+            [jnp.where(core == 0, text_kv, other), jnp.where(core == 0, other, text_kv)], axis=0
+        )
+        up = column_blocks(w_up, 4)
+        attn_in, text_kv, up = lax.optimization_barrier((attn_in, text_kv, up))
+        up = gather_rows(trade(up))
+
+        attn_in, projected = gather_mm(attn_in, rank, first, 0, 3 * group, "qkv_mm")
+        down = column_blocks(w_down, 4)
+        projected, down, grad_top = lax.optimization_barrier((projected, down, grad_top))
+        down = gather_rows(trade(down))
         grad_y = spread(grad_top).reshape(4 * tokens, width)
-
-        attn_in, projected = gather_mm(attn_in, rank, first, 0, 3 * group, "qkv_mm")
         self_mixed = self_forward(projected, 2 * images)
-        self_mixed, grad_y = lax.optimization_barrier((self_mixed, grad_y))
         parts = scatter_tokens(mm_scatter(self_mixed, rank, first, 3 * group, "out_mm"))
         after_attn, cross_in = add_norm([start_x] + parts, gain_b)
 
@@ -771,13 +772,28 @@
         after_cross, mlp_in = add_norm([after_attn] + parts, gain_c)
 
         mlp_in, activated, slope = feed_up(gather_tokens(mlp_in), rank, up)
-        down_part = grad_products([([grad_y], [activated])], "down_grads")
-        slope, down_part = lax.optimization_barrier((slope, down_part))
-        down_rows = scatter_grad(down_part)
+        early = [attn_in, self_mixed, cross_in, cross_mixed]
+        if inside:
+            grad_axes, halves = "z", (core, z_size)
+
+            def both(values):
+                return [values, swap(values, "c")]
+
+        else:
+            grad_axes, halves = DATA, ()
+
+            def both(values):
+                return [values]
+
+        early = [both(values) for values in early]
+        down_part = grad_products([(both(grad_y), both(activated))], "down_grads", *halves)
+        mlp_in = both(mlp_in)
+        slope, down_part, early, mlp_in = lax.optimization_barrier((slope, down_part, early, mlp_in))
+        down_rows = scatter_grad(down_part, grad_axes)
         grad_pre = feed_down(grad_y, slope, down)
         parts = mm_scatter(grad_pre, rank, up, 0, "up_back")
         parts, grad_pre = lax.optimization_barrier((parts, grad_pre))
-        up_part = grad_products([([mlp_in], [grad_pre])], "up_grads")
+        up_part = grad_products([(mlp_in, both(grad_pre))], "up_grads", *halves)
         grad_after_cross, cross_branch, gain_grad_c = norm_back(
             scatter_tokens(parts), grad_top, after_cross, gain_c
         )
@@ -787,7 +803,8 @@
         )
         grad_cq, kv_grad = cross_back(cross_queries, text_kv, grad_cross_mixed)
         up_part, down_rows, kv_grad = lax.optimization_barrier((up_part, down_rows, kv_grad))
-        up_rows = scatter_grad(up_part)
+        up_rows = scatter_grad(up_part, grad_axes)
+        cross_branch, grad_cq_both = both(cross_branch), both(grad_cq)
         parts = scatter_tokens(mm_scatter(grad_cq, rank, mid, 0, "query_back"))
         grad_after_attn, attn_branch, gain_grad_b = norm_back(
             parts, grad_after_cross, after_attn, gain_b
@@ -797,20 +814,33 @@
             gather_tokens(attn_branch), rank, first, 3 * group, group, "out_back"
         )
         grad_projected = self_back(projected, grad_self_mixed, 2 * images)
+        kv_keep = lax.dynamic_index_in_dim(
+            kv_grad.reshape(2, -1, 2 * group), core, 0, keepdims=False
+        )
+        kv_send = lax.dynamic_index_in_dim(
+            kv_grad.reshape(2, -1, 2 * group), 1 - core, 0, keepdims=False
+        )
+        kv_sum = sum_z((kv_keep + swap(kv_send, "c")).astype(BF)).astype(BF)
+        kv_grads = spread(kv_sum, PLANE, 8)
+        down_rows = trade(down_rows)
+        grad_projected, kv_grads, down_rows = lax.optimization_barrier(
+            (grad_projected, kv_grads, down_rows)
+        )
         rest_part = grad_products(
             [
-                ([attn_in], [grad_projected]),
-                ([attn_branch], [self_mixed]),
-                ([cross_in], [grad_cq]),
-                ([cross_branch], [cross_mixed]),
+                (early[0], both(grad_projected)),
+                (both(attn_branch), early[1]),
+                (early[2], grad_cq_both),
+                (cross_branch, early[3]),
             ],
             "attention_grads",
-        )
-        grad_projected, activated, kv_grad, rest_part = lax.optimization_barrier(
-            (grad_projected, activated, kv_grad, rest_part)
+            *halves,
+        )
+        grad_projected, activated, kv_grads, rest_part = lax.optimization_barrier(
+            (grad_projected, activated, kv_grads, rest_part)
         )
         rest_part, up_rows = lax.optimization_barrier((rest_part, up_rows))
-        rest_rows = scatter_grad(rest_part)
+        rest_rows = scatter_grad(rest_part, grad_axes)
         grad_attn = mm_t(grad_projected, first[:, : 3 * group]).astype(BF)
         grad_attn = trade(grad_attn.reshape(4, tokens, width))
         grad_hidden, gain_grad_a, mask_grad = last_back(
@@ -828,16 +858,16 @@
         result = trade(mm_t(activated, down).astype(BF).reshape(4, tokens, width))
         output = layer_output(after_cross, [(result, k) for k in range(4)], unit, order)
 
-        kv_grads = spread(sum_data(kv_grad)).reshape(4, -1, 2, group)
-        kv_grads = kv_grads.transpose(1, 2, 0, 3).reshape(-1, 2 * width)
+        kv_grads = from_plane(kv_grads, 2)
         kv_weight_grad = t_mm(own_text, kv_grads)
         grad_text = mm_t(kv_grads, kv_rows).astype(BF)
         grad_text_w = t_mm(grad_text, caption)
-        caption_part = column_blocks(mm(grad_text, w_text).astype(BF), 4)
-        caption_own = sum_data(trade(caption_part).astype(F32).sum(axis=0))
-        grad_caption = spread(caption_own).transpose(1, 0, 2).reshape(-1, text_width).astype(F32)
-
-        down_grad = finish_wide(trade(down_rows))
+        caption_part = by_plane(mm(grad_text, w_text).astype(BF), 1)
+        caption_own = trade(caption_part, PLANE).astype(F32).sum(axis=0).astype(BF)
+        caption_own = sum_z(caption_own).astype(BF)
+        grad_caption = from_plane(spread(caption_own, PLANE, 8), 1).astype(F32)
+
+        down_grad = finish_wide(down_rows)
         up_grad = finish_wide(trade(up_rows))
         qkv_grad, out_grad, grad_cross, cross_out_grad = finish_all(
             swap_blocks(rest_rows, rank), kv_weight_grad, rank

time: 752 us -> 755 us (level)
  waiting for transfers between devices: 305 us -> 278 us
  local copies, waits for them, and re-layouts: 69.5 us -> 92.2 us
  Pallas kernels: 119 us -> 127 us
  blocking collectives: 99.3 us -> 91.3 us
    reduce_scatter x3, waiting for transfers between devices: 38.9 us -> 0.04 us  [scatter_grad(): summed = lax.psum_scatter(partial, axes, scatter_dimension=0, tiled=True)]
    pallas_call x11 -> x14, Pallas kernels: 52.8 us -> 86.9 us  [call(): pl.pallas_call(kernel, grid_spec=spec, **options)]
    all_to_all x11 -> x12, waiting for transfers between devices: 73.1 us -> 102 us  [trade(): return lax.all_to_all(blocks, axes, 0, 0, tiled=True)]
    pallas_call x17 -> x14, Pallas kernels: 66.2 us -> 40.3 us  [call(): pl.pallas_call(kernel, grid=grid, in_specs=in_specs, out_specs=out_specs,...]
    ppermute x49 -> x54, waiting for transfers between devices: 181 us -> 163 us  [swap(): return lax.ppermute(values, axis, PAIR)]
    reshape x2 -> x7, local copies, waits for them, and re-layouts: 2.49 us -> 15.8 us  [the longest x4 8.73 us: by_plane(): shaped = values.reshape(2, rows // 2, parts, 2, 2, -1)]
    all_to_all x7 -> x5, blocking collectives: 99.3 us -> 91.3 us  [trade(): return lax.all_to_all(blocks, axes, 0, 0, tiled=True)]
    unnamed x152 -> x147, local copies, waits for them, and re-layouts: 43.9 us -> 37.9 us
  transfers between devices with their start and end apart: 71 -> 75, of which waited for: 49 -> 44; matrix products, arithmetic and copies ran while one was open for 7% -> 12% of each run, Pallas kernels for 15% -> 16%
where the time goes in v8:
time: 755 us; the launch traced here: 745 us
  waiting for transfers between devices  278 us (37%)
  Pallas kernels  127 us (17%)
  starting transfers between devices  98.4 us (13%)
  local copies, waits for them, and re-layouts  92.2 us (12%)
  blocking collectives  91.3 us (12%)
  matrix products  27.1 us (4%)
  between operations  16.2 us (2%)
  other arithmetic  14.6 us (2%)
    ppermute x54, waiting for transfers between devices, swap(): return lax.ppermute(values, axis, PAIR)  163 us
    all_to_all x12, waiting for transfers between devices, trade(): return lax.all_to_all(blocks, axes, 0, 0, tiled=True)  102 us
    all_to_all x5, blocking collectives, trade(): return lax.all_to_all(blocks, axes, 0, 0, tiled=True)  91.3 us
    pallas_call x14, Pallas kernels, call(): pl.pallas_call(kernel, grid_spec=spec, **options)  86.9 us
    ppermute x54, starting transfers between devices, swap(): return lax.ppermute(values, axis, PAIR)  51.2 us
    all_to_all x12, starting transfers between devices, trade(): return lax.all_to_all(blocks, axes, 0, 0, tiled=True)  46.1 us
    pallas_call x14, Pallas kernels, call(): pl.pallas_call(kernel, grid=grid, in_specs=in_specs, out_specs=out_specs,...  40.3 us
    unnamed x147, local copies, waits for them, and re-layouts  37.9 us
  transfers between devices with their start and end apart: 75, of which 44 were waited for; matrix products, arithmetic and copies ran while one was open for 12% of the time, Pallas kernels for 16%

profile of v8, /device:TPU:0, one launch (start us, length us, event | category | flops | bytes accessed | tf_op | source)
XLA Modules:
  0.0 745.1 jit_solution(4455936070629528304)
XLA Ops:
  36.9 8.8 %collective-permute-done.1.refs_2_ = bf16[128,2048]{1,0:T(8,128)(2,1)S(1)} collective-permute-done((bf16[128,2048]{1,0:T(8,128)(2,1)S(1)}, bf16[128,2048]{1,0:T(8,128)(2,1)S(1)}, u32[]{:S(2)}, u32[]{:S(2)}) %collective-permute-start.1) | collective-permute-done | bytes 524320 | tf_op jit(solution)/shard_map/ppermute | solution.py:46
  55.2 10.2 %all_to_all.85 = bf16[4,64,1024]{2,1,0:T(8,128)(2,1)} all-to-all(bf16[4,64,1024]{2,1,0:T(8,128)(2,1)S(1)} %pad_maximum_fusion), channel_id=1, replica_groups=mesh['z'=4,'x'=2,'c'=2,'y'=2] {'x','y'}, dimensions={0} | all-to-all | bytes 1048576 | tf_op jit(solution)/shard_map/all_to_all | solution.py:50
  75.3 17.6 %all_to_all.86 = bf16[8,64,1024]{2,1,0:T(8,128)(2,1)} all-to-all(bf16[8,64,1024]{2,1,0:T(8,128)(2,1)S(1)} %reshape.271), channel_id=1, replica_groups=mesh['z'=4,'x'=2,'c'=2,'y'=2] {'x','c','y'}, dimensions={0} | all-to-all | bytes 2097152 | tf_op jit(solution)/shard_map/all_to_all | solution.py:50
  94.3 28.4 %all_to_all.87 = bf16[4,64,1024]{2,1,0:T(8,128)(2,1)S(1)} all-to-all(bf16[4,64,1024]{2,1,0:T(8,128)(2,1)S(1)} %broadcast_in_dim.16), channel_id=1, replica_groups=mesh['z'=4,'x'=2,'c'=2,'y'=2] {'z'}, dimensions={0} | all-to-all | bytes 1048576 | tf_op jit(solution)/shard_map/all_to_all | solution.py:50
  124.2 18.3 %all_to_all.88 = bf16[4,64,2048]{2,1,0:T(8,128)(2,1)} all-to-all(bf16[4,64,2048]{2,1,0:T(8,128)(2,1)S(1)} %bitcast.144), channel_id=1, replica_groups=mesh['z'=4,'x'=2,'c'=2,'y'=2] {'x','y'}, dimensions={0} | all-to-all | bytes 2097152 | tf_op jit(solution)/shard_map/all_to_all | solution.py:50
  157.9 16.8 %all_to_all.89 = bf16[4,64,2048]{2,1,0:T(8,128)(2,1)} all-to-all(bf16[4,64,2048]{2,1,0:T(8,128)(2,1)S(1)} %bitcast.145), channel_id=1, replica_groups=mesh['z'=4,'x'=2,'c'=2,'y'=2] {'x','y'}, dimensions={0} | all-to-all | bytes 2097152 | tf_op jit(solution)/shard_map/all_to_all | solution.py:50
  192.0 8.6 %collective-permute-done.11.refs_3_ = bf16[128,2048]{1,0:T(8,128)(2,1)S(1)} collective-permute-done((bf16[128,2048]{1,0:T(8,128)(2,1)S(1)}, bf16[128,2048]{1,0:T(8,128)(2,1)S(1)}, u32[]{:S(2)}, u32[]{:S(2)}) %collective-permute-start.11) | collective-permute-done | bytes 524320 | tf_op jit(solution)/shard_map/ppermute | solution.py:46
  204.7 9.2 %collective-permute-done.13.refs_2_ = bf16[128,2048]{1,0:T(8,128)(2,1)S(1)} collective-permute-done((bf16[128,2048]{1,0:T(8,128)(2,1)S(1)}, bf16[128,2048]{1,0:T(8,128)(2,1)S(1)}, u32[]{:S(2)}, u32[]{:S(2)}) %collective-permute-start.13) | collective-permute-done | bytes 524320 | tf_op jit(solution)/shard_map/ppermute | solution.py:46
  248.5 23.4 %collective-permute-done.16 = bf16[64,2048]{1,0:T(8,128)(2,1)S(1)} collective-permute-done((bf16[64,2048]{1,0:T(8,128)(2,1)}, bf16[64,2048]{1,0:T(8,128)(2,1)S(1)}, u32[]{:S(2)}, u32[]{:S(2)}) %collective-permute-start.16) | collective-permute-done | bytes 262176 | tf_op jit(solution)/shard_map/ppermute | solution.py:46
  285.4 8.5 %collective-permute-done.21.refs_2_ = bf16[128,2048]{1,0:T(8,128)(2,1)S(1)} collective-permute-done((bf16[128,2048]{1,0:T(8,128)(2,1)S(1)}, bf16[128,2048]{1,0:T(8,128)(2,1)S(1)}, u32[]{:S(2)}, u32[]{:S(2)}) %collective-permute-start.21) | collective-permute-done | bytes 524320 | tf_op jit(solution)/shard_map/ppermute | solution.py:46
  307.4 12.0 %feed_up.1 = (bf16[512,2048]{1,0:T(8,128)(2,1)}, bf16[512,2048]{1,0:T(8,128)(2,1)}, f32[512,2048]{1,0:T(8,128)}) custom-call(s32[1]{0:T(128)} %bitcast.r, bf16[128,2048]{1,0:T(8,128)(2,1)S(1)} %copy-done.50, bf16[128,2048]{1,0:T(8,128)(2,1)S(1)} %copy-done.46, bf16[128,2048]{1,0:T(8,128)(2,1)S(1)} %copy-done.44, ...), custom_call_target="tpu_custom_call" | custom-call | flops 4294967296 | bytes 12582912 | tf_op jit(solution)/shard_map/feed_up/pallas_call | solution.py:113
  328.0 8.6 %down_grads.1 = bf16[1024,2048]{1,0:T(8,128)(2,1)} custom-call(s32[1]{0:T(128)} %bitcast.28.r, bf16[512,2048]{1,0:T(8,128)(2,1)S(1)} %bitcast.126, bf16[512,2048]{1,0:T(8,128)(2,1)} %collective-permute-done.24.refs_1_, bf16[512,2048]{1,0:T(8,128)(2,1)} %get-tuple-element.192.refs_2_, bf16[512,2048]{1,0:T(8,128)(2,1)} %copy-done.71), custom_call_target="tpu_custom_call" | custom-call | flops 4294967296 | bytes 16777216 | tf_op jit(solution)/shard_map/down_grads/pallas_call | solution.py:113
  337.3 10.0 %feed_down.1.x.refs_2_ = bf16[512,2048]{1,0:T(8,128)(2,1)S(1)} custom-call(bf16[512,2048]{1,0:T(8,128)(2,1)S(1)} %bitcast.127, f32[512,2048]{1,0:T(8,128)} %get-tuple-element.149.slope_ref, bf16[2048,2048]{1,0:T(8,128)(2,1)} %all-gather.11.cloned.1.call-done.down), custom_call_target="tpu_custom_call" | custom-call | flops 4294967296 | bytes 25165824 | tf_op jit(solution)/shard_map/feed_down/pallas_call | solution.py:102
  367.5 9.9 %collective-permute-done.34.refs_2_ = bf16[128,2048]{1,0:T(8,128)(2,1)S(1)} collective-permute-done((bf16[128,2048]{1,0:T(8,128)(2,1)S(1)}, bf16[128,2048]{1,0:T(8,128)(2,1)S(1)}, u32[]{:S(2)}, u32[]{:S(2)}) %collective-permute-start.34) | collective-permute-done | bytes 524320 | tf_op jit(solution)/shard_map/ppermute | solution.py:46
  383.4 11.3 %collective-permute-done.36.refs_2_ = bf16[128,2048]{1,0:T(8,128)(2,1)S(1)} collective-permute-done((bf16[128,2048]{1,0:T(8,128)(2,1)S(1)}, bf16[128,2048]{1,0:T(8,128)(2,1)S(1)}, u32[]{:S(2)}, u32[]{:S(2)}) %collective-permute-start.36) | collective-permute-done | bytes 524320 | tf_op jit(solution)/shard_map/ppermute | solution.py:46
  410.2 8.7 %up_grads.1 = bf16[1024,2048]{1,0:T(8,128)(2,1)} custom-call(s32[1]{0:T(128)} %bitcast.28.r, bf16[512,2048]{1,0:T(8,128)(2,1)} %get-tuple-element.173.refs_0_, bf16[512,2048]{1,0:T(8,128)(2,1)} %collective-permute-done.30.refs_1_, bf16[512,2048]{1,0:T(8,128)(2,1)} %copy-done.24, bf16[512,2048]{1,0:T(8,128)(2,1)} %copy-done.70), custom_call_target="tpu_custom_call" | custom-call | flops 4294967296 | bytes 16777216 | tf_op jit(solution)/shard_map/up_grads/pallas_call | solution.py:113
  442.4 24.1 %all-to-all-done.6 = bf16[4,64,1024]{2,1,0:T(8,128)(2,1)S(1)} async-done(((bf16[4,64,1024]{2,1,0:T(8,128)(2,1)}), bf16[4,64,1024]{2,1,0:T(8,128)(2,1)S(1)}, u32[]{:S(2)}, u32[]{:S(2)}) %all-to-all-start.6) | async-done | bytes 524320 | tf_op jit(solution)/shard_map/all_to_all | solution.py:50
  494.6 15.7 %collective-permute-done.45.refs_3_ = bf16[64,2048]{1,0:T(8,128)(2,1)S(1)} collective-permute-done((bf16[64,2048]{1,0:T(8,128)(2,1)S(1)}, bf16[64,2048]{1,0:T(8,128)(2,1)S(1)}, u32[]{:S(2)}, u32[]{:S(2)}) %collective-permute-start.45) | collective-permute-done | bytes 262176 | tf_op jit(solution)/shard_map/ppermute | solution.py:46
  524.6 11.9 %attention_grads.1 = bf16[1024,3072]{1,0:T(8,128)(2,1)} custom-call(s32[1]{0:T(128)} %bitcast.28.r, bf16[512,2048]{1,0:T(8,128)(2,1)} %get-tuple-element.182.refs_0_, bf16[512,2048]{1,0:T(8,128)(2,1)} %collective-permute-done.26.refs_1_, bf16[512,2048]{1,0:T(8,128)(2,1)} %get-tuple-element.184.refs_2_, bf16[512,2048]{1,0:T(8,128)(2,1)} %collective-permute-done.49.refs_3_, ...), custom_call_target="tpu_custom_call" | custom-call | flops 6442450944 | bytes 25165824 | tf_op jit(solution)/shard_map/attention_grads/pallas_call | solution.py:113
  577.7 9.9 %convolution_convert_fusion.2 = bf16[512,2048]{1,0:T(8,128)(2,1)} fusion(bf16[512,2048]{1,0:T(8,128)(2,1)} %get-tuple-element.192.refs_2_, bf16[2048,2048]{1,0:T(8,128)(2,1)} %all-gather.11.cloned.1.call-done.down), kind=kOutput, calls=%fused_computation.5 | convolution fusion | flops 4296015872 | bytes 12582912 | tf_op jit(solution)/shard_map/dot_general | solution.py:26
  587.6 15.4 %all-to-all-done.10.refs_0_.refs_1_.refs_2_.refs_3_ = bf16[4,128,2048]{2,1,0:T(8,128)(2,1)S(1)} async-done(((bf16[4,128,2048]{2,1,0:T(8,128)(2,1)}), bf16[4,128,2048]{2,1,0:T(8,128)(2,1)S(1)}, u32[]{:S(2)}, u32[]{:S(2)}) %all-to-all-start.10) | async-done | bytes 2097184 | tf_op jit(solution)/shard_map/all_to_all | solution.py:50
  614.6 18.4 %all-to-all-done.9.refs_0_.refs_1_.refs_2_.refs_3_ = bf16[4,128,2048]{2,1,0:T(8,128)(2,1)S(1)} async-done(((bf16[4,128,2048]{2,1,0:T(8,128)(2,1)}), bf16[4,128,2048]{2,1,0:T(8,128)(2,1)S(1)}, u32[]{:S(2)}, u32[]{:S(2)}) %all-to-all-start.9) | async-done | bytes 2097184 | tf_op jit(solution)/shard_map/all_to_all | solution.py:50
  648.2 15.5 %all-to-all-done.12 = bf16[4,64,1024]{2,1,0:T(8,128)(2,1)} async-done(((bf16[4,64,1024]{2,1,0:T(8,128)(2,1)}), bf16[4,64,1024]{2,1,0:T(8,128)(2,1)}, u32[]{:S(2)}, u32[]{:S(2)}) %all-to-all-start.12) | async-done | bytes 524320 | tf_op jit(solution)/shard_map/all_to_all | solution.py:50
  683.4 10.2 %all-to-all-done.13 = bf16[8,64,1024]{2,1,0:T(8,128)(2,1)} async-done(((bf16[8,64,1024]{2,1,0:T(8,128)(2,1)}), bf16[8,64,1024]{2,1,0:T(8,128)(2,1)}, u32[]{:S(2)}, u32[]{:S(2)}) %all-to-all-start.13) | async-done | bytes 1048608 | tf_op jit(solution)/shard_map/all_to_all | solution.py:50
  (415 shorter events, 397.3 us)
Async XLA Ops:
  7.2 137.8 %all-gather.5.cloned.1.call-start = ((), (), s32[]{:S(2)}) async-start(), calls=%async_computation.20 | async-start | bytes 9437184 | tf_op jit(solution)/shard_map/all_gather | solution.py:85
  29.5 188.5 %all-gather.7.cloned.1.call-start = ((), (), s32[]{:S(2)}) async-start(), calls=%async_computation.21 | async-start | bytes 4718592 | tf_op jit(solution)/shard_map/all_gather | solution.py:85
  65.5 233.3 %all-gather.9.cloned.1.call-start = ((), (), s32[]{:S(2)}) async-start(), calls=%async_computation.22 | async-start | bytes 9437184 | tf_op jit(solution)/shard_map/all_gather | solution.py:85
  142.6 194.7 %all-gather.11.cloned.1.call-start = ((), (), s32[]{:S(2)}) async-start(), calls=%async_computation.23 | async-start | bytes 9437184 | tf_op jit(solution)/shard_map/all_gather | solution.py:85
  239.3 59.4 %all-to-all-start.3 = ((bf16[4,128,2048]{2,1,0:T(8,128)(2,1)}), bf16[4,128,2048]{2,1,0:T(8,128)(2,1)S(1)}, u32[]{:S(2)}, u32[]{:S(2)}) async-start(bf16[4,128,2048]{2,1,0:T(8,128)(2,1)} %broadcast_in_dim.17), calls=%async_computation.3 | async-start | bytes 4194304 | tf_op jit(solution)/shard_map/all_to_all | solution.py:50
  242.9 176.0 %reduce-scatter.4.cloned.1.call-start = ((), (), s32[]{:S(2)}) async-start(), calls=%async_computation.24 | async-start | bytes 5242880 | tf_op jit(solution)/shard_map/reduce_scatter | solution.py:89
  244.0 27.9 %collective-permute-start.16 = (bf16[64,2048]{1,0:T(8,128)(2,1)}, bf16[64,2048]{1,0:T(8,128)(2,1)S(1)}, u32[]{:S(2)}, u32[]{:S(2)}) collective-permute-start(bf16[64,2048]{1,0:T(8,128)(2,1)} %copy-done.55), channel_id=1, source_target_pairs={{0,1},{1,0},{2,3},{3,2},{4,5},{5,4},{6,7},{7,6},{8,9},{9,8},{10,11... | collective-permute-start | bytes 786440 | tf_op jit(solution)/shard_map/ppermute | solution.py:46
  248.3 32.5 %collective-permute-start.19 = (bf16[128,2048]{1,0:T(8,128)(2,1)S(1)}, bf16[128,2048]{1,0:T(8,128)(2,1)S(1)}, u32[]{:S(2)}, u32[]{:S(2)}) collective-permute-start(bf16[128,2048]{1,0:T(8,128)(2,1)S(1)} %pad_maximum_fusion.4), channel_id=1, source_target_pairs={{0,1},{1,0},{2,3},{3,2},{4,5},{5,4},{6,7},{7,6},{8,9},{9,8},{10,11... | collective-permute-start | bytes 1572872 | tf_op jit(solution)/shard_map/ppermute | solution.py:46
  298.7 21.7 %collective-permute-start.24 = (bf16[512,2048]{1,0:T(8,128)(2,1)S(1)}, bf16[512,2048]{1,0:T(8,128)(2,1)}, u32[]{:S(2)}, u32[]{:S(2)}) collective-permute-start(bf16[512,2048]{1,0:T(8,128)(2,1)S(1)} %bitcast.125), channel_id=1, source_target_pairs={{0,2},{2,0},{1,3},{3,1},{4,6},{6,4},{5,7},{7,5},{8,10},{10,8},{9,1... | collective-permute-start | bytes 6291464 | tf_op jit(solution)/shard_map/ppermute | solution.py:46
  336.7 199.9 %reduce-scatter.6.cloned.1.call-start = ((), (), s32[]{:S(2)}) async-start(), calls=%async_computation.25 | async-start | bytes 5242880 | tf_op jit(solution)/shard_map/reduce_scatter | solution.py:89
  356.8 52.1 %collective-permute-start.47 = (bf16[512,2048]{1,0:T(8,128)(2,1)S(1)}, bf16[512,2048]{1,0:T(8,128)(2,1)S(1)}, u32[]{:S(2)}, u32[]{:S(2)}) collective-permute-start(bf16[512,2048]{1,0:T(8,128)(2,1)S(1)} %feed_down.1.x.refs_2_), channel_id=1, source_target_pairs={{0,2},{2,0},{1,3},{3,1},{4,6},{6,4},{5,7},{7,5},{8,10},{10,8},{9,1... | collective-permute-start | bytes 6291464 | tf_op jit(solution)/shard_map/ppermute | solution.py:46
  433.1 37.8 %collective-permute-start.42 = (bf16[128,2048]{1,0:T(8,128)(2,1)}, bf16[128,2048]{1,0:T(8,128)(2,1)}, u32[]{:S(2)}, u32[]{:S(2)}) collective-permute-start(bf16[128,2048]{1,0:T(8,128)(2,1)} %pad_maximum_fusion.8), channel_id=1, source_target_pairs={{0,1},{1,0},{2,3},{3,2},{4,5},{5,4},{6,7},{7,6},{8,9},{9,8},{10,11... | collective-permute-start | bytes 1572872 | tf_op jit(solution)/shard_map/ppermute | solution.py:46
  434.7 31.8 %all-to-all-start.6 = ((bf16[4,64,1024]{2,1,0:T(8,128)(2,1)}), bf16[4,64,1024]{2,1,0:T(8,128)(2,1)S(1)}, u32[]{:S(2)}, u32[]{:S(2)}) async-start(bf16[4,64,1024]{2,1,0:T(8,128)(2,1)} %broadcast_in_dim.18), calls=%async_computation.7 | async-start | bytes 1048576 | tf_op jit(solution)/shard_map/all_to_all | solution.py:50
  441.2 29.7 %collective-permute-start.40 = (bf16[128,2048]{1,0:T(8,128)(2,1)}, bf16[128,2048]{1,0:T(8,128)(2,1)}, u32[]{:S(2)}, u32[]{:S(2)}) collective-permute-start(bf16[128,2048]{1,0:T(8,128)(2,1)} %pad_maximum_fusion.7), channel_id=1, source_target_pairs={{0,4},{4,0},{1,5},{5,1},{2,6},{6,2},{3,7},{7,3},{8,12},{12,8},{9,1... | collective-permute-start | bytes 1572872 | tf_op jit(solution)/shard_map/ppermute | solution.py:46
  486.1 33.0 %all-to-all-start.7 = ((bf16[8,64,1024]{2,1,0:T(8,128)(2,1)}), bf16[8,64,1024]{2,1,0:T(8,128)(2,1)}, u32[]{:S(2)}, u32[]{:S(2)}) async-start(bf16[8,64,1024]{2,1,0:T(8,128)(2,1)} %broadcast_in_dim.19), calls=%async_computation.8 | async-start | bytes 2097152 | tf_op jit(solution)/shard_map/all_to_all | solution.py:50
  490.4 207.8 %reduce-scatter.8.cloned.1.call-start = ((), (), s32[]{:S(2)}) async-start(), calls=%async_computation.26 | async-start | bytes 7864320 | tf_op jit(solution)/shard_map/reduce_scatter | solution.py:89
  494.6 28.9 %collective-permute-start.50 = (bf16[512,2048]{1,0:T(8,128)(2,1)}, bf16[512,2048]{1,0:T(8,128)(2,1)}, u32[]{:S(2)}, u32[]{:S(2)}) collective-permute-start(bf16[512,2048]{1,0:T(8,128)(2,1)} %copy-done.23), channel_id=1, source_target_pairs={{0,2},{2,0},{1,3},{3,1},{4,6},{6,4},{5,7},{7,5},{8,10},{10,8},{9,1... | collective-permute-start | bytes 6291464 | tf_op jit(solution)/shard_map/ppermute | solution.py:46
  573.9 29.1 %all-to-all-start.10 = ((bf16[4,128,2048]{2,1,0:T(8,128)(2,1)}), bf16[4,128,2048]{2,1,0:T(8,128)(2,1)S(1)}, u32[]{:S(2)}, u32[]{:S(2)}) async-start(bf16[4,128,2048]{2,1,0:T(8,128)(2,1)} %bitcast.150), calls=%async_computation.11 | async-start | bytes 4194304 | tf_op jit(solution)/shard_map/all_to_all | solution.py:50
  604.3 28.7 %all-to-all-start.9 = ((bf16[4,128,2048]{2,1,0:T(8,128)(2,1)}), bf16[4,128,2048]{2,1,0:T(8,128)(2,1)S(1)}, u32[]{:S(2)}, u32[]{:S(2)}) async-start(bf16[4,128,2048]{2,1,0:T(8,128)(2,1)} %bitcast.149), calls=%async_computation.10 | async-start | bytes 4194304 | tf_op jit(solution)/shard_map/all_to_all | solution.py:50
  643.9 19.7 %all-to-all-start.12 = ((bf16[4,64,1024]{2,1,0:T(8,128)(2,1)}), bf16[4,64,1024]{2,1,0:T(8,128)(2,1)}, u32[]{:S(2)}, u32[]{:S(2)}) async-start(bf16[4,64,1024]{2,1,0:T(8,128)(2,1)} %broadcast_in_dim.20), calls=%async_computation.13 | async-start | bytes 1048576 | tf_op jit(solution)/shard_map/all_to_all | solution.py:50
  693.7 21.5 %all-to-all-start.16 = ((bf16[4,64,2048]{2,1,0:T(8,128)(2,1)}), bf16[4,64,2048]{2,1,0:T(8,128)(2,1)}, u32[]{:S(2)}, u32[]{:S(2)}) async-start(bf16[4,64,2048]{2,1,0:T(8,128)(2,1)} %bitcast.156), calls=%async_computation.19 | async-start | bytes 2097152 | tf_op jit(solution)/shard_map/all_to_all | solution.py:50
  700.7 20.0 %collective-permute-start.53 = (bf16[64,3072]{1,0:T(8,128)(2,1)}, bf16[64,3072]{1,0:T(8,128)(2,1)}, u32[]{:S(2)}, u32[]{:S(2)}) collective-permute-start(bf16[64,3072]{1,0:T(8,128)(2,1)} %get-tuple-element.272), channel_id=1, source_target_pairs={{0,1},{1,0},{2,3},{3,2},{4,5},{5,4},{6,7},{7,6},{8,9},{9,8},{10,11... | collective-permute-start | bytes 1179656 | tf_op jit(solution)/shard_map/ppermute | solution.py:46
  702.7 19.0 %collective-permute-start.54 = (bf16[64,3072]{1,0:T(8,128)(2,1)}, bf16[64,3072]{1,0:T(8,128)(2,1)}, u32[]{:S(2)}, u32[]{:S(2)}) collective-permute-start(bf16[64,3072]{1,0:T(8,128)(2,1)} %get-tuple-element.271), channel_id=1, source_target_pairs={{0,4},{4,0},{1,5},{5,1},{2,6},{6,2},{3,7},{7,3},{8,12},{12,8},{9,1... | collective-permute-start | bytes 1179656 | tf_op jit(solution)/shard_map/ppermute | solution.py:46
  704.1 25.9 %collective-permute-start.55 = (bf16[64,3072]{1,0:T(8,128)(2,1)}, bf16[64,3072]{1,0:T(8,128)(2,1)}, u32[]{:S(2)}, u32[]{:S(2)}) collective-permute-start(bf16[64,3072]{1,0:T(8,128)(2,1)} %get-tuple-element.270), channel_id=1, source_target_pairs={{0,5},{1,4},{4,1},{5,0},{2,7},{3,6},{6,3},{7,2},{8,13},{9,12},{12,... | collective-permute-start | bytes 1179656 | tf_op jit(solution)/shard_map/ppermute | solution.py:80
  (123 other events, 1397.2 us)
Sparse Core Ops, SparseCore 0:
  29.6 94.5 all-gather.4
  125.8 45.5 all-gather.6
  173.0 80.7 all-gather.8
  255.3 80.5 all-gather.10
  338.1 75.2 reduce-scatter.3
  419.1 82.5 reduce-scatter.5
  536.7 109.9 reduce-scatter.7

commit v9 on v8

--- a/solution.py
+++ b/solution.py
@@ -600,20 +600,28 @@
     )
 
 
-def finish_wide(blocks):
-    count, rows, width = blocks.shape
-
-    def kernel(ref, out):
-        out[...] = ref[0].astype(F32)
-
-    return call(
-        kernel,
-        (count,),
-        [pl.BlockSpec((1, rows, width), lambda k: (k, 0, 0))],
-        pl.BlockSpec((rows, width), lambda k: (0, k)),
-        shape((rows, count * width), F32),
-        [blocks],
+def finish_wide(parts, rank):
+    rows, total = parts[0].shape
+    width = total // 2
+
+    def kernel(r, *refs):
+        for k in range(4):
+
+            @pl.when(pl.program_id(0) == k)
+            def _():
+                refs[4][...] = refs[k][:, :width].astype(F32)
+                refs[5][...] = refs[k][:, width:].astype(F32)
+
+    flat = pl.BlockSpec((rows, width), lambda k, r: (0, k ^ r[0]))
+    return call(
+        kernel,
+        (4,),
+        [whole(p) for p in parts],
+        [flat, flat],
+        [shape((rows, 4 * width), F32)] * 2,
+        parts,
         "finish_wide",
+        rank=rank,
     )
 
 
@@ -741,8 +749,9 @@
         )
         attn_in = gather_tokens(attn_in)
         mid = jnp.concatenate([column_blocks(w_cross[:, 0], 4), column_blocks(w_cross_out, 4)], axis=2)
-        attn_in, mid = lax.optimization_barrier((attn_in, mid))
-        mid = gather_rows(trade(mid))
+        up = column_blocks(w_up, 4)
+        attn_in, mid, up = lax.optimization_barrier((attn_in, mid, up))
+        mid, up = gather_rows(trade(mid)), gather_rows(trade(up))
 
         own_text = mm_t(caption, w_text).astype(BF)
         kv_rows = w_cross[:, 1:].reshape(shard_rows, 2 * width)
@@ -753,9 +762,7 @@
         text_kv = jnp.concatenate(
             [jnp.where(core == 0, text_kv, other), jnp.where(core == 0, other, text_kv)], axis=0
         )
-        up = column_blocks(w_up, 4)
-        attn_in, text_kv, up = lax.optimization_barrier((attn_in, text_kv, up))
-        up = gather_rows(trade(up))
+        attn_in, text_kv = lax.optimization_barrier((attn_in, text_kv))
 
         attn_in, projected = gather_mm(attn_in, rank, first, 0, 3 * group, "qkv_mm")
         down = column_blocks(w_down, 4)
@@ -814,18 +821,6 @@
             gather_tokens(attn_branch), rank, first, 3 * group, group, "out_back"
         )
         grad_projected = self_back(projected, grad_self_mixed, 2 * images)
-        kv_keep = lax.dynamic_index_in_dim(
-            kv_grad.reshape(2, -1, 2 * group), core, 0, keepdims=False
-        )
-        kv_send = lax.dynamic_index_in_dim(
-            kv_grad.reshape(2, -1, 2 * group), 1 - core, 0, keepdims=False
-        )
-        kv_sum = sum_z((kv_keep + swap(kv_send, "c")).astype(BF)).astype(BF)
-        kv_grads = spread(kv_sum, PLANE, 8)
-        down_rows = trade(down_rows)
-        grad_projected, kv_grads, down_rows = lax.optimization_barrier(
-            (grad_projected, kv_grads, down_rows)
-        )
         rest_part = grad_products(
             [
                 (early[0], both(grad_projected)),
@@ -836,15 +831,14 @@
             "attention_grads",
             *halves,
         )
-        grad_projected, activated, kv_grads, rest_part = lax.optimization_barrier(
-            (grad_projected, activated, kv_grads, rest_part)
+        grad_projected, activated, kv_grad, rest_part = lax.optimization_barrier(
+            (grad_projected, activated, kv_grad, rest_part)
         )
         rest_part, up_rows = lax.optimization_barrier((rest_part, up_rows))
         rest_rows = scatter_grad(rest_part, grad_axes)
-        grad_attn = mm_t(grad_projected, first[:, : 3 * group]).astype(BF)
-        grad_attn = trade(grad_attn.reshape(4, tokens, width))
+        parts = scatter_tokens(mm_scatter(grad_projected, rank, first, 0, "qkv_back"))
         grad_hidden, gain_grad_a, mask_grad = last_back(
-            [(grad_attn, k) for k in range(4)],
+            parts,
             grad_after_attn,
             start_x,
             gain_a,
@@ -855,10 +849,14 @@
         sums = jnp.concatenate([gain_grad_a, gain_grad_b, gain_grad_c, mask_grad], axis=0)
         sums = layer_order(sum_all(sums))
 
-        result = trade(mm_t(activated, down).astype(BF).reshape(4, tokens, width))
-        output = layer_output(after_cross, [(result, k) for k in range(4)], unit, order)
-
-        kv_grads = from_plane(kv_grads, 2)
+        parts = scatter_tokens(mm_scatter(activated, rank, down, 0, "down_mm"))
+        output = layer_output(after_cross, parts, unit, order)
+
+        kv_halves = kv_grad.reshape(2, -1, 2 * group)
+        kv_keep = lax.dynamic_index_in_dim(kv_halves, core, 0, keepdims=False)
+        kv_send = lax.dynamic_index_in_dim(kv_halves, 1 - core, 0, keepdims=False)
+        kv_sum = sum_z((kv_keep + swap(kv_send, "c")).astype(BF)).astype(BF)
+        kv_grads = from_plane(spread(kv_sum, PLANE, 8), 2)
         kv_weight_grad = t_mm(own_text, kv_grads)
         grad_text = mm_t(kv_grads, kv_rows).astype(BF)
         grad_text_w = t_mm(grad_text, caption)
@@ -867,8 +865,8 @@
         caption_own = sum_z(caption_own).astype(BF)
         grad_caption = from_plane(spread(caption_own, PLANE, 8), 1).astype(F32)
 
-        down_grad = finish_wide(down_rows)
-        up_grad = finish_wide(trade(up_rows))
+        wide_rows = jnp.concatenate([down_rows, up_rows], axis=2)
+        down_grad, up_grad = finish_wide(swap_blocks(wide_rows, rank), rank)
         qkv_grad, out_grad, grad_cross, cross_out_grad = finish_all(
             swap_blocks(rest_rows, rank), kv_weight_grad, rank
         )

time: 755 us -> 754 us (level)
  matrix products: 27.1 us -> 5.37 us
  Pallas kernels: 127 us -> 137 us
  local copies, waits for them, and re-layouts: 92.2 us -> 101 us
    all_to_all x12 -> x8, waiting for transfers between devices: 102 us -> 27.6 us  [trade(): return lax.all_to_all(blocks, axes, 0, 0, tiled=True)]
    ppermute x54 -> x64, waiting for transfers between devices: 163 us -> 227 us  [swap(): return lax.ppermute(values, axis, PAIR)]
    dot_general x8 -> x6, matrix products: 27.1 us -> 5.37 us  [dot(): return lax.dot_general(a, b, (dims, ((), ())), preferred_element_type=F32)]
    pallas_call x14 -> x17, Pallas kernels: 86.9 us -> 103 us  [call(): pl.pallas_call(kernel, grid_spec=spec, **options)]
    ppermute x54 -> x64, starting transfers between devices: 51.2 us -> 64.8 us  [swap(): return lax.ppermute(values, axis, PAIR)]
    all_to_all x12 -> x8, starting transfers between devices: 46.1 us -> 34.4 us  [trade(): return lax.all_to_all(blocks, axes, 0, 0, tiled=True)]
    pallas_call x14 -> x12, Pallas kernels: 40.3 us -> 33.7 us  [call(): pl.pallas_call(kernel, grid=grid, in_specs=in_specs, out_specs=out_specs,...]
    unnamed x147 -> x160, local copies, waits for them, and re-layouts: 37.9 us -> 38.1 us
  transfers between devices with their start and end apart: 75 -> 82, of which waited for: 44 -> 45; matrix products, arithmetic and copies ran while one was open for 12% -> 12% of each run, Pallas kernels for 16% -> 18%
where the time goes in v9:
time: 754 us; the launch traced here: 744 us
  waiting for transfers between devices  274 us (36%)
  Pallas kernels  137 us (18%)
  local copies, waits for them, and re-layouts  101 us (13%)
  starting transfers between devices  101 us (13%)
  blocking collectives  89.5 us (12%)
  other arithmetic  20.1 us (3%)
  between operations  16.3 us (2%)
    ppermute x64, waiting for transfers between devices, swap(): return lax.ppermute(values, axis, PAIR)  227 us
    pallas_call x17, Pallas kernels, call(): pl.pallas_call(kernel, grid_spec=spec, **options)  103 us
    all_to_all x5, blocking collectives, trade(): return lax.all_to_all(blocks, axes, 0, 0, tiled=True)  89.5 us
    ppermute x64, starting transfers between devices, swap(): return lax.ppermute(values, axis, PAIR)  64.8 us
    unnamed x160, local copies, waits for them, and re-layouts  38.1 us
    all_to_all x8, starting transfers between devices, trade(): return lax.all_to_all(blocks, axes, 0, 0, tiled=True)  34.4 us
    pallas_call x12, Pallas kernels, call(): pl.pallas_call(kernel, grid=grid, in_specs=in_specs, out_specs=out_specs,...  33.7 us
    all_to_all x8, waiting for transfers between devices, trade(): return lax.all_to_all(blocks, axes, 0, 0, tiled=True)  27.6 us
  transfers between devices with their start and end apart: 82, of which 45 were waited for; matrix products, arithmetic and copies ran while one was open for 12% of the time, Pallas kernels for 18%

profile of v9, /device:TPU:0, one launch (start us, length us, event | category | flops | bytes accessed | tf_op | source)
XLA Modules:
  0.0 744.3 jit_solution(12500333756272413931)
XLA Ops:
  36.1 9.6 %collective-permute-done.1.refs_2_ = bf16[128,2048]{1,0:T(8,128)(2,1)S(1)} collective-permute-done((bf16[128,2048]{1,0:T(8,128)(2,1)S(1)}, bf16[128,2048]{1,0:T(8,128)(2,1)S(1)}, u32[]{:S(2)}, u32[]{:S(2)}) %collective-permute-start.1) | collective-permute-done | bytes 524320 | tf_op jit(solution)/shard_map/ppermute | solution.py:46
  58.1 10.4 %all_to_all.65 = bf16[4,64,1024]{2,1,0:T(8,128)(2,1)} all-to-all(bf16[4,64,1024]{2,1,0:T(8,128)(2,1)S(1)} %pad_maximum_fusion), channel_id=1, replica_groups=mesh['z'=4,'x'=2,'c'=2,'y'=2] {'x','y'}, dimensions={0} | all-to-all | bytes 1048576 | tf_op jit(solution)/shard_map/all_to_all | solution.py:50
  68.5 14.1 %all_to_all.66 = bf16[4,64,2048]{2,1,0:T(8,128)(2,1)} all-to-all(bf16[4,64,2048]{2,1,0:T(8,128)(2,1)S(1)} %bitcast.148), channel_id=1, replica_groups=mesh['z'=4,'x'=2,'c'=2,'y'=2] {'x','y'}, dimensions={0} | all-to-all | bytes 2097152 | tf_op jit(solution)/shard_map/all_to_all | solution.py:50
  91.2 17.6 %all_to_all.67 = bf16[8,64,1024]{2,1,0:T(8,128)(2,1)} all-to-all(bf16[8,64,1024]{2,1,0:T(8,128)(2,1)S(1)} %reshape.268), channel_id=1, replica_groups=mesh['z'=4,'x'=2,'c'=2,'y'=2] {'x','c','y'}, dimensions={0} | all-to-all | bytes 2097152 | tf_op jit(solution)/shard_map/all_to_all | solution.py:50
  110.3 29.1 %all_to_all.68 = bf16[4,64,1024]{2,1,0:T(8,128)(2,1)S(1)} all-to-all(bf16[4,64,1024]{2,1,0:T(8,128)(2,1)S(1)} %broadcast_in_dim.16), channel_id=1, replica_groups=mesh['z'=4,'x'=2,'c'=2,'y'=2] {'z'}, dimensions={0} | all-to-all | bytes 1048576 | tf_op jit(solution)/shard_map/all_to_all | solution.py:50
  154.1 18.4 %all_to_all.69 = bf16[4,64,2048]{2,1,0:T(8,128)(2,1)} all-to-all(bf16[4,64,2048]{2,1,0:T(8,128)(2,1)S(1)} %bitcast.147), channel_id=1, replica_groups=mesh['z'=4,'x'=2,'c'=2,'y'=2] {'x','y'}, dimensions={0} | all-to-all | bytes 2097152 | tf_op jit(solution)/shard_map/all_to_all | solution.py:50
  189.6 10.3 %collective-permute-done.11.refs_3_ = bf16[128,2048]{1,0:T(8,128)(2,1)S(1)} collective-permute-done((bf16[128,2048]{1,0:T(8,128)(2,1)S(1)}, bf16[128,2048]{1,0:T(8,128)(2,1)S(1)}, u32[]{:S(2)}, u32[]{:S(2)}) %collective-permute-start.11) | collective-permute-done | bytes 524320 | tf_op jit(solution)/shard_map/ppermute | solution.py:46
  206.2 9.4 %collective-permute-done.13.refs_2_ = bf16[128,2048]{1,0:T(8,128)(2,1)S(1)} collective-permute-done((bf16[128,2048]{1,0:T(8,128)(2,1)S(1)}, bf16[128,2048]{1,0:T(8,128)(2,1)S(1)}, u32[]{:S(2)}, u32[]{:S(2)}) %collective-permute-start.13) | collective-permute-done | bytes 524320 | tf_op jit(solution)/shard_map/ppermute | solution.py:46
  252.8 23.1 %collective-permute-done.16 = bf16[64,2048]{1,0:T(8,128)(2,1)S(1)} collective-permute-done((bf16[64,2048]{1,0:T(8,128)(2,1)}, bf16[64,2048]{1,0:T(8,128)(2,1)S(1)}, u32[]{:S(2)}, u32[]{:S(2)}) %collective-permute-start.16) | collective-permute-done | bytes 262176 | tf_op jit(solution)/shard_map/ppermute | solution.py:46
  276.9 8.5 %collective-permute-done.19.refs_3_ = bf16[128,2048]{1,0:T(8,128)(2,1)S(1)} collective-permute-done((bf16[128,2048]{1,0:T(8,128)(2,1)S(1)}, bf16[128,2048]{1,0:T(8,128)(2,1)S(1)}, u32[]{:S(2)}, u32[]{:S(2)}) %collective-permute-start.19) | collective-permute-done | bytes 524320 | tf_op jit(solution)/shard_map/ppermute | solution.py:46
  290.8 8.6 %collective-permute-done.21.refs_2_ = bf16[128,2048]{1,0:T(8,128)(2,1)S(1)} collective-permute-done((bf16[128,2048]{1,0:T(8,128)(2,1)S(1)}, bf16[128,2048]{1,0:T(8,128)(2,1)S(1)}, u32[]{:S(2)}, u32[]{:S(2)}) %collective-permute-start.21) | collective-permute-done | bytes 524320 | tf_op jit(solution)/shard_map/ppermute | solution.py:46
  312.8 12.0 %feed_up.1 = (bf16[512,2048]{1,0:T(8,128)(2,1)}, bf16[512,2048]{1,0:T(8,128)(2,1)}, f32[512,2048]{1,0:T(8,128)}) custom-call(s32[1]{0:T(128)} %bitcast.r, bf16[128,2048]{1,0:T(8,128)(2,1)S(1)} %copy-done.53, bf16[128,2048]{1,0:T(8,128)(2,1)S(1)} %copy-done.48, bf16[128,2048]{1,0:T(8,128)(2,1)S(1)} %copy-done.46, ...), custom_call_target="tpu_custom_call" | custom-call | flops 4294967296 | bytes 12582912 | tf_op jit(solution)/shard_map/feed_up/pallas_call | solution.py:113
  333.4 8.7 %down_grads.1 = bf16[1024,2048]{1,0:T(8,128)(2,1)} custom-call(s32[1]{0:T(128)} %bitcast.28.r, bf16[512,2048]{1,0:T(8,128)(2,1)S(1)} %bitcast.129, bf16[512,2048]{1,0:T(8,128)(2,1)} %collective-permute-done.24.refs_1_, bf16[512,2048]{1,0:T(8,128)(2,1)} %get-tuple-element.198.refs_2_.x, bf16[512,2048]{1,0:T(8,128)(2,1)} %copy-done.77), custom_call_target="tpu_custom_call" | custom-call | flops 4294967296 | bytes 16777216 | tf_op jit(solution)/shard_map/down_grads/pallas_call | solution.py:113
  342.5 10.0 %feed_down.1.x.refs_2_ = bf16[512,2048]{1,0:T(8,128)(2,1)S(1)} custom-call(bf16[512,2048]{1,0:T(8,128)(2,1)S(1)} %bitcast.130, f32[512,2048]{1,0:T(8,128)} %get-tuple-element.158.slope_ref, bf16[2048,2048]{1,0:T(8,128)(2,1)} %all-gather.11.cloned.1.call-done.down.w), custom_call_target="tpu_custom_call" | custom-call | flops 4294967296 | bytes 25165824 | tf_op jit(solution)/shard_map/feed_down/pallas_call | solution.py:102
  372.8 10.0 %collective-permute-done.34.refs_2_ = bf16[128,2048]{1,0:T(8,128)(2,1)S(1)} collective-permute-done((bf16[128,2048]{1,0:T(8,128)(2,1)S(1)}, bf16[128,2048]{1,0:T(8,128)(2,1)S(1)}, u32[]{:S(2)}, u32[]{:S(2)}) %collective-permute-start.34) | collective-permute-done | bytes 524320 | tf_op jit(solution)/shard_map/ppermute | solution.py:46
  387.7 10.2 %collective-permute-done.36.refs_2_ = bf16[128,2048]{1,0:T(8,128)(2,1)S(1)} collective-permute-done((bf16[128,2048]{1,0:T(8,128)(2,1)S(1)}, bf16[128,2048]{1,0:T(8,128)(2,1)S(1)}, u32[]{:S(2)}, u32[]{:S(2)}) %collective-permute-start.36) | collective-permute-done | bytes 524320 | tf_op jit(solution)/shard_map/ppermute | solution.py:46
  415.3 8.7 %up_grads.1 = bf16[1024,2048]{1,0:T(8,128)(2,1)} custom-call(s32[1]{0:T(128)} %bitcast.28.r, bf16[512,2048]{1,0:T(8,128)(2,1)} %get-tuple-element.182.refs_0_, bf16[512,2048]{1,0:T(8,128)(2,1)} %collective-permute-done.30.refs_1_, bf16[512,2048]{1,0:T(8,128)(2,1)} %copy-done.18, bf16[512,2048]{1,0:T(8,128)(2,1)} %copy-done.76), custom_call_target="tpu_custom_call" | custom-call | flops 4294967296 | bytes 16777216 | tf_op jit(solution)/shard_map/up_grads/pallas_call | solution.py:113
  450.2 9.6 %collective-permute-done.44.refs_2_ = bf16[128,2048]{1,0:T(8,128)(2,1)S(1)} collective-permute-done((bf16[128,2048]{1,0:T(8,128)(2,1)S(1)}, bf16[128,2048]{1,0:T(8,128)(2,1)S(1)}, u32[]{:S(2)}, u32[]{:S(2)}) %collective-permute-start.44) | collective-permute-done | bytes 524320 | tf_op jit(solution)/shard_map/ppermute | solution.py:46
  483.4 12.0 %attention_grads.1 = bf16[1024,3072]{1,0:T(8,128)(2,1)} custom-call(s32[1]{0:T(128)} %bitcast.28.r, bf16[512,2048]{1,0:T(8,128)(2,1)} %get-tuple-element.188.refs_0_, bf16[512,2048]{1,0:T(8,128)(2,1)} %collective-permute-done.26.refs_1_, bf16[512,2048]{1,0:T(8,128)(2,1)} %copy-done.19, bf16[512,2048]{1,0:T(8,128)(2,1)} %collective-permute-done.48.refs_3_, ...), custom_call_target="tpu_custom_call" | custom-call | flops 6442450944 | bytes 25165824 | tf_op jit(solution)/shard_map/attention_grads/pallas_call | solution.py:113
  525.2 26.2 %all-to-all-done.6 = bf16[4,64,1024]{2,1,0:T(8,128)(2,1)S(1)} async-done(((bf16[4,64,1024]{2,1,0:T(8,128)(2,1)}), bf16[4,64,1024]{2,1,0:T(8,128)(2,1)S(1)}, u32[]{:S(2)}, u32[]{:S(2)}) %all-to-all-start.6) | async-done | bytes 524320 | tf_op jit(solution)/shard_map/all_to_all | solution.py:50
  561.5 22.7 %collective-permute-done.57.refs_1_ = bf16[128,2048]{1,0:T(8,128)(2,1)S(1)} collective-permute-done((bf16[128,2048]{1,0:T(8,128)(2,1)S(1)}, bf16[128,2048]{1,0:T(8,128)(2,1)S(1)}, u32[]{:S(2)}, u32[]{:S(2)}) %collective-permute-start.57) | collective-permute-done | bytes 524320 | tf_op jit(solution)/shard_map/ppermute | solution.py:46
  654.7 9.3 %collective-permute-done.53.refs_1_ = bf16[128,2048]{1,0:T(8,128)(2,1)S(1)} collective-permute-done((bf16[128,2048]{1,0:T(8,128)(2,1)S(1)}, bf16[128,2048]{1,0:T(8,128)(2,1)S(1)}, u32[]{:S(2)}, u32[]{:S(2)}) %collective-permute-start.53) | collective-permute-done | bytes 524320 | tf_op jit(solution)/shard_map/ppermute | solution.py:46
  688.1 12.5 %collective-permute-done.64.refs_1_ = bf16[64,4096]{1,0:T(8,128)(2,1)S(1)} collective-permute-done((bf16[64,4096]{1,0:T(8,128)(2,1)}, bf16[64,4096]{1,0:T(8,128)(2,1)S(1)}, u32[]{:S(2)}, u32[]{:S(2)}) %collective-permute-start.64) | collective-permute-done | bytes 524320 | tf_op jit(solution)/shard_map/ppermute | solution.py:46
  720.5 8.9 %collective-permute-done.63.refs_3_ = bf16[64,3072]{1,0:T(8,128)(2,1)} collective-permute-done((bf16[64,3072]{1,0:T(8,128)(2,1)}, bf16[64,3072]{1,0:T(8,128)(2,1)}, u32[]{:S(2)}, u32[]{:S(2)}) %collective-permute-start.63) | collective-permute-done | bytes 393248 | tf_op jit(solution)/shard_map/ppermute | solution.py:80
  (455 shorter events, 408.2 us)
Async XLA Ops:
  7.2 134.7 %all-gather.5.cloned.1.call-start = ((), (), s32[]{:S(2)}) async-start(), calls=%async_computation.16 | async-start | bytes 9437184 | tf_op jit(solution)/shard_map/all_gather | solution.py:85
  29.5 190.2 %all-gather.7.cloned.1.call-start = ((), (), s32[]{:S(2)}) async-start(), calls=%async_computation.17 | async-start | bytes 4718592 | tf_op jit(solution)/shard_map/all_gather | solution.py:85
  68.5 235.7 %all-gather.9.cloned.1.call-start = ((), (), s32[]{:S(2)}) async-start(), calls=%async_computation.18 | async-start | bytes 9437184 | tf_op jit(solution)/shard_map/all_gather | solution.py:85
  82.6 259.8 %all-gather.11.cloned.1.call-start = ((), (), s32[]{:S(2)}) async-start(), calls=%async_computation.19 | async-start | bytes 9437184 | tf_op jit(solution)/shard_map/all_gather | solution.py:85
  243.6 60.5 %all-to-all-start.3 = ((bf16[4,128,2048]{2,1,0:T(8,128)(2,1)}), bf16[4,128,2048]{2,1,0:T(8,128)(2,1)S(1)}, u32[]{:S(2)}, u32[]{:S(2)}) async-start(bf16[4,128,2048]{2,1,0:T(8,128)(2,1)} %broadcast_in_dim.17), calls=%async_computation.3 | async-start | bytes 4194304 | tf_op jit(solution)/shard_map/all_to_all | solution.py:50
  247.3 176.8 %reduce-scatter.4.cloned.1.call-start = ((), (), s32[]{:S(2)}) async-start(), calls=%async_computation.20 | async-start | bytes 5242880 | tf_op jit(solution)/shard_map/reduce_scatter | solution.py:89
  248.3 27.5 %collective-permute-start.16 = (bf16[64,2048]{1,0:T(8,128)(2,1)}, bf16[64,2048]{1,0:T(8,128)(2,1)S(1)}, u32[]{:S(2)}, u32[]{:S(2)}) collective-permute-start(bf16[64,2048]{1,0:T(8,128)(2,1)} %copy-done.56), channel_id=1, source_target_pairs={{0,1},{1,0},{2,3},{3,2},{4,5},{5,4},{6,7},{7,6},{8,9},{9,8},{10,11... | collective-permute-start | bytes 786440 | tf_op jit(solution)/shard_map/ppermute | solution.py:46
  252.6 32.8 %collective-permute-start.19 = (bf16[128,2048]{1,0:T(8,128)(2,1)S(1)}, bf16[128,2048]{1,0:T(8,128)(2,1)S(1)}, u32[]{:S(2)}, u32[]{:S(2)}) collective-permute-start(bf16[128,2048]{1,0:T(8,128)(2,1)S(1)} %pad_maximum_fusion.4), channel_id=1, source_target_pairs={{0,1},{1,0},{2,3},{3,2},{4,5},{5,4},{6,7},{7,6},{8,9},{9,8},{10,11... | collective-permute-start | bytes 1572872 | tf_op jit(solution)/shard_map/ppermute | solution.py:46
  342.2 158.4 %reduce-scatter.6.cloned.1.call-start = ((), (), s32[]{:S(2)}) async-start(), calls=%async_computation.21 | async-start | bytes 5242880 | tf_op jit(solution)/shard_map/reduce_scatter | solution.py:89
  364.1 49.8 %collective-permute-start.47 = (bf16[512,2048]{1,0:T(8,128)(2,1)S(1)}, bf16[512,2048]{1,0:T(8,128)(2,1)S(1)}, u32[]{:S(2)}, u32[]{:S(2)}) collective-permute-start(bf16[512,2048]{1,0:T(8,128)(2,1)S(1)} %feed_down.1.x.refs_2_), channel_id=1, source_target_pairs={{0,2},{2,0},{1,3},{3,1},{4,6},{6,4},{5,7},{7,5},{8,10},{10,8},{9,1... | collective-permute-start | bytes 6291464 | tf_op jit(solution)/shard_map/ppermute | solution.py:46
  424.1 258.2 %reduce-scatter.8.cloned.1.call-start = ((), (), s32[]{:S(2)}) async-start(), calls=%async_computation.22 | async-start | bytes 7864320 | tf_op jit(solution)/shard_map/reduce_scatter | solution.py:89
  517.5 33.8 %all-to-all-start.6 = ((bf16[4,64,1024]{2,1,0:T(8,128)(2,1)}), bf16[4,64,1024]{2,1,0:T(8,128)(2,1)S(1)}, u32[]{:S(2)}, u32[]{:S(2)}) async-start(bf16[4,64,1024]{2,1,0:T(8,128)(2,1)} %broadcast_in_dim.18), calls=%async_computation.7 | async-start | bytes 1048576 | tf_op jit(solution)/shard_map/all_to_all | solution.py:50
  523.6 37.9 %collective-permute-start.59 = (bf16[128,2048]{1,0:T(8,128)(2,1)}, bf16[128,2048]{1,0:T(8,128)(2,1)}, u32[]{:S(2)}, u32[]{:S(2)}) collective-permute-start(bf16[128,2048]{1,0:T(8,128)(2,1)} %pad_maximum_fusion.12), channel_id=1, source_target_pairs={{0,1},{1,0},{2,3},{3,2},{4,5},{5,4},{6,7},{7,6},{8,9},{9,8},{10,11... | collective-permute-start | bytes 1572872 | tf_op jit(solution)/shard_map/ppermute | solution.py:46
  554.3 35.2 %all-to-all-start.7 = ((bf16[8,64,1024]{2,1,0:T(8,128)(2,1)}), bf16[8,64,1024]{2,1,0:T(8,128)(2,1)}, u32[]{:S(2)}, u32[]{:S(2)}) async-start(bf16[8,64,1024]{2,1,0:T(8,128)(2,1)} %broadcast_in_dim.19), calls=%async_computation.8 | async-start | bytes 2097152 | tf_op jit(solution)/shard_map/all_to_all | solution.py:50
  559.5 24.7 %collective-permute-start.57 = (bf16[128,2048]{1,0:T(8,128)(2,1)S(1)}, bf16[128,2048]{1,0:T(8,128)(2,1)S(1)}, u32[]{:S(2)}, u32[]{:S(2)}) collective-permute-start(bf16[128,2048]{1,0:T(8,128)(2,1)S(1)} %pad_maximum_fusion.11), channel_id=1, source_target_pairs={{0,4},{4,0},{1,5},{5,1},{2,6},{6,2},{3,7},{7,3},{8,12},{12,8},{9,1... | collective-permute-start | bytes 1572872 | tf_op jit(solution)/shard_map/ppermute | solution.py:46
  605.9 26.1 %all-to-all-start.8 = ((bf16[8,64,1024]{2,1,0:T(8,128)(2,1)}), bf16[8,64,1024]{2,1,0:T(8,128)(2,1)}, u32[]{:S(2)}, u32[]{:S(2)}) async-start(bf16[8,64,1024]{2,1,0:T(8,128)(2,1)} %bitcast.38), calls=%async_computation.9 | async-start | bytes 2097152 | tf_op jit(solution)/shard_map/all_to_all | solution.py:50
  621.9 27.9 %collective-permute-start.52 = (bf16[64,2048]{1,0:T(8,128)(2,1)S(1)}, bf16[64,2048]{1,0:T(8,128)(2,1)}, u32[]{:S(2)}, u32[]{:S(2)}) collective-permute-start(bf16[64,2048]{1,0:T(8,128)(2,1)S(1)} %get-tuple-element.200), channel_id=1, source_target_pairs={{0,1},{1,0},{2,3},{3,2},{4,5},{5,4},{6,7},{7,6},{8,9},{9,8},{10,11... | collective-permute-start | bytes 786440 | tf_op jit(solution)/shard_map/ppermute | solution.py:46
  670.0 32.8 %all-to-all-start.10 = ((bf16[8,64,1024]{2,1,0:T(8,128)(2,1)}), bf16[8,64,1024]{2,1,0:T(8,128)(2,1)}, u32[]{:S(2)}, u32[]{:S(2)}) async-start(bf16[8,64,1024]{2,1,0:T(8,128)(2,1)} %broadcast_in_dim.21), calls=%async_computation.11 | async-start | bytes 2097152 | tf_op jit(solution)/shard_map/all_to_all | solution.py:50
  678.3 22.2 %collective-permute-start.64 = (bf16[64,4096]{1,0:T(8,128)(2,1)}, bf16[64,4096]{1,0:T(8,128)(2,1)S(1)}, u32[]{:S(2)}, u32[]{:S(2)}) collective-permute-start(bf16[64,4096]{1,0:T(8,128)(2,1)} %get-tuple-element.290), channel_id=1, source_target_pairs={{0,1},{1,0},{2,3},{3,2},{4,5},{5,4},{6,7},{7,6},{8,9},{9,8},{10,11... | collective-permute-start | bytes 1572872 | tf_op jit(solution)/shard_map/ppermute | solution.py:46
  680.6 30.7 %collective-permute-start.65 = (bf16[64,4096]{1,0:T(8,128)(2,1)}, bf16[64,4096]{1,0:T(8,128)(2,1)}, u32[]{:S(2)}, u32[]{:S(2)}) collective-permute-start(bf16[64,4096]{1,0:T(8,128)(2,1)} %get-tuple-element.289), channel_id=1, source_target_pairs={{0,4},{4,0},{1,5},{5,1},{2,6},{6,2},{3,7},{7,3},{8,12},{12,8},{9,1... | collective-permute-start | bytes 1572872 | tf_op jit(solution)/shard_map/ppermute | solution.py:46
  682.2 30.8 %collective-permute-start.66 = (bf16[64,4096]{1,0:T(8,128)(2,1)}, bf16[64,4096]{1,0:T(8,128)(2,1)}, u32[]{:S(2)}, u32[]{:S(2)}) collective-permute-start(bf16[64,4096]{1,0:T(8,128)(2,1)} %get-tuple-element.288), channel_id=1, source_target_pairs={{0,5},{1,4},{4,1},{5,0},{2,7},{3,6},{6,3},{7,2},{8,13},{9,12},{12,... | collective-permute-start | bytes 1572872 | tf_op jit(solution)/shard_map/ppermute | solution.py:80
  684.6 35.2 %collective-permute-start.61 = (bf16[64,3072]{1,0:T(8,128)(2,1)}, bf16[64,3072]{1,0:T(8,128)(2,1)}, u32[]{:S(2)}, u32[]{:S(2)}) collective-permute-start(bf16[64,3072]{1,0:T(8,128)(2,1)} %get-tuple-element.294), channel_id=1, source_target_pairs={{0,1},{1,0},{2,3},{3,2},{4,5},{5,4},{6,7},{7,6},{8,9},{9,8},{10,11... | collective-permute-start | bytes 1179656 | tf_op jit(solution)/shard_map/ppermute | solution.py:46
  686.6 33.9 %collective-permute-start.62 = (bf16[64,3072]{1,0:T(8,128)(2,1)}, bf16[64,3072]{1,0:T(8,128)(2,1)}, u32[]{:S(2)}, u32[]{:S(2)}) collective-permute-start(bf16[64,3072]{1,0:T(8,128)(2,1)} %get-tuple-element.293), channel_id=1, source_target_pairs={{0,4},{4,0},{1,5},{5,1},{2,6},{6,2},{3,7},{7,3},{8,12},{12,8},{9,1... | collective-permute-start | bytes 1179656 | tf_op jit(solution)/shard_map/ppermute | solution.py:46
  700.5 28.8 %collective-permute-start.63 = (bf16[64,3072]{1,0:T(8,128)(2,1)}, bf16[64,3072]{1,0:T(8,128)(2,1)}, u32[]{:S(2)}, u32[]{:S(2)}) collective-permute-start(bf16[64,3072]{1,0:T(8,128)(2,1)} %get-tuple-element.292), channel_id=1, source_target_pairs={{0,5},{1,4},{4,1},{5,0},{2,7},{3,6},{6,3},{7,2},{8,13},{9,12},{12,... | collective-permute-start | bytes 1179656 | tf_op jit(solution)/shard_map/ppermute | solution.py:80
  (136 other events, 1601.7 us)
Sparse Core Ops, SparseCore 0:
  29.6 83.4 all-gather.4
  114.7 50.7 all-gather.6
  167.1 79.9 all-gather.8
  248.5 83.7 all-gather.10
  342.3 78.5 reduce-scatter.3
  424.2 76.2 reduce-scatter.5
  502.8 119.6 reduce-scatter.7

commit v10 on v9

--- a/solution.py
+++ b/solution.py
@@ -123,82 +123,50 @@
     return jnp.concatenate([values[:, k * unit : (k + 1) * unit] for k in order], axis=1)
 
 
-def assemble(target, pieces, rank):
-    rows, half = pieces[0].shape[0], pieces[3].shape[0]
-    for k in range(3):
-        target[pl.ds(pl.multiple_of((rank ^ k) * rows, rows), rows), :] = pieces[k][...]
-    at = pl.multiple_of((rank ^ 3) * rows, rows)
-    target[pl.ds(at, half), :] = pieces[3][...]
-    target[pl.ds(pl.multiple_of(at + half, half), half), :] = pieces[4][...]
-
-
-def gather_mm(pieces, rank, weight, first, columns, name):
+def assemble(target, pieces):
+    at = 0
+    for piece in pieces:
+        rows = piece.shape[0]
+        target[at : at + rows, :] = piece[...]
+        at += rows
+
+
+def gather_mm(pieces, weight, first, columns, name):
     rows, width = pieces[0].shape
     step = 256
 
-    def kernel(r, *refs):
+    def kernel(*refs):
         tokens, out = refs[6], refs[7]
 
         @pl.when(pl.program_id(0) == 0)
         def _():
-            assemble(tokens, refs[:5], r[0])
+            assemble(tokens, refs[:5])
 
         out[...] = mm(tokens[...], refs[5][...]).astype(BF)
 
     return call(
         kernel,
         (columns // step,),
-        [whole(p) for p in pieces]
-        + [pl.BlockSpec((width, step), lambda j, r: (0, first // step + j))],
+        [whole(p) for p in pieces] + [pl.BlockSpec((width, step), lambda j: (0, first // step + j))],
         [
-            pl.BlockSpec((4 * rows, width), lambda j, r: (0, 0)),
-            pl.BlockSpec((4 * rows, step), lambda j, r: (0, j)),
+            pl.BlockSpec((4 * rows, width), lambda j: (0, 0)),
+            pl.BlockSpec((4 * rows, step), lambda j: (0, j)),
         ],
         [shape((4 * rows, width)), shape((4 * rows, columns))],
         [*pieces, weight],
         name,
         flops=8 * rows * width * columns,
         size=2 * width * (columns + 8 * rows),
-        rank=rank,
-    )
-
-
-def mm_scatter(values, rank, weight, first, name):
-    tokens, depth = values.shape
-    rows = tokens // 4
-    width = weight.shape[0]
-    step = 512
-
-    def kernel(r, x, w, own, for_y, for_x, low, high, total):
-        total[...] = mm_t(x[...], w[...])
-
-        def block(k):
-            return total[pl.ds(pl.multiple_of((r[0] ^ k) * rows, rows), rows), :]
-
-        own[...] = block(0)
-        for_y[...] = block(1).astype(BF)
-        for_x[...] = block(2).astype(BF)
-        diagonal = block(3).astype(BF)
-        low[...] = diagonal[: rows // 2]
-        high[...] = diagonal[rows // 2 :]
-
-    sizes = [rows, rows, rows, rows // 2, rows // 2]
-    return call(
-        kernel,
-        (width // step,),
-        [
-            pl.BlockSpec((tokens, depth), lambda j, r: (0, 0)),
-            pl.BlockSpec((step, depth), lambda j, r: (j, first // depth)),
-        ],
-        [pl.BlockSpec((n, step), lambda j, r: (0, j)) for n in sizes],
-        [shape((n, width), F32 if k == 0 else BF) for k, n in enumerate(sizes)],
-        [values, weight],
-        name,
-        flops=2 * tokens * depth * width,
-        size=2 * width * (depth + 6 * rows),
-        rank=rank,
-        scratch=[pltpu.VMEM((tokens, step), F32)],
-    )
+    )
+
+
+def mm_scatter(values, weight):
+    partial = mm_t(values, weight)
+    rows = partial.shape[0] // 4
+    low = partial[rows:].astype(BF)
+    half = rows // 2
+    cuts = [low[:rows], low[rows : 2 * rows], low[2 * rows : 2 * rows + half], low[2 * rows + half :]]
+    return scatter_tokens([partial[:rows], *cuts])
 
 
 def normalize(values):
@@ -363,17 +331,17 @@
     )
 
 
-def feed_up(pieces, rank, weight):
+def feed_up(pieces, weight):
     rows, width = pieces[0].shape
     hidden = weight.shape[1]
     step = 256
 
-    def kernel(r, *refs):
+    def kernel(*refs):
         up, tokens, act, slope = refs[5:]
 
         @pl.when(pl.program_id(0) == 0)
         def _():
-            assemble(tokens, refs[:5], r[0])
+            assemble(tokens, refs[:5])
 
         u = mm(tokens[...], up[...])
         square = u * u
@@ -382,18 +350,17 @@
         act[...] = (u * half).astype(BF)
         slope[...] = half + 0.5 * u * (1.0 - bend * bend) * SLOPE * (1.0 + 3.0 * CUBIC * square)
 
-    part = pl.BlockSpec((4 * rows, step), lambda j, r: (0, j))
+    part = pl.BlockSpec((4 * rows, step), lambda j: (0, j))
     return call(
         kernel,
         (hidden // step,),
-        [whole(p) for p in pieces] + [pl.BlockSpec((width, step), lambda j, r: (0, j))],
-        [pl.BlockSpec((4 * rows, width), lambda j, r: (0, 0)), part, part],
+        [whole(p) for p in pieces] + [pl.BlockSpec((width, step), lambda j: (0, j))],
+        [pl.BlockSpec((4 * rows, width), lambda j: (0, 0)), part, part],
         [shape((4 * rows, width)), shape((4 * rows, hidden)), shape((4 * rows, hidden), F32)],
         [*pieces, weight],
         "feed_up",
         flops=8 * rows * width * hidden,
         size=2 * width * (hidden + 8 * rows),
-        rank=rank,
     )
 
 
@@ -662,27 +629,116 @@
     )
 
 
+def plane_block(k):
+    return (k >> 1) & 1, (k >> 2) * 2 + (k & 1)
+
+
+def text_forward(caption, w_text, kv_rows):
+    context, rows = caption.shape[0], w_text.shape[0]
+    half, width = context // 2, kv_rows.shape[1] // 8
+
+    def kernel(cap, weight, kv, own, blocks):
+        own[...] = mm_t(cap[...], weight[...]).astype(BF)
+        part = mm(own[...], kv[...]).astype(BF)
+        for k in range(8):
+            core, group = plane_block(k)
+            for j in range(2):
+                at = (4 * j + group) * width
+                blocks[k, :, j * width : (j + 1) * width] = part[
+                    core * half : (core + 1) * half, at : at + width
+                ]
+
+    return call(
+        kernel,
+        (1,),
+        [whole(caption), whole(w_text), whole(kv_rows)],
+        [
+            pl.BlockSpec((context, rows), lambda i: (0, 0)),
+            pl.BlockSpec((8, half, 2 * width), lambda i: (0, 0, 0)),
+        ],
+        [shape((context, rows)), shape((8, half, 2 * width))],
+        [caption, w_text, kv_rows],
+        "text_forward",
+    )
+
+
+def text_back(blocks, own_text, kv_rows, caption, w_text, extra):
+    context, rows = own_text.shape
+    half, width = context // 2, kv_rows.shape[1] // 8
+    wide = caption.shape[1] // 4
+    tail = extra.shape[0]
+
+    def kernel(block, own, kv, cap, weight, more, kv_grad, text_grad, out, grads):
+        for k in range(8):
+            core, group = plane_block(k)
+            for j in range(2):
+                at = (4 * j + group) * width
+                grads[core * half : (core + 1) * half, at : at + width] = block[
+                    k, :, j * width : (j + 1) * width
+                ]
+        kv_grad[...] = t_mm(own[...], grads[...])
+        grad_text = mm_t(grads[...], kv[...]).astype(BF)
+        text_grad[...] = t_mm(grad_text, cap[...])
+        part = mm(grad_text, weight[...]).astype(BF)
+        for k in range(8):
+            core, group = plane_block(k)
+            out[k, :half, :] = part[core * half : (core + 1) * half, group * wide : (group + 1) * wide]
+            out[k, half:, :] = more[...]
+
+    operands = [blocks, own_text, kv_rows, caption, w_text, extra]
+    outs = [
+        shape((rows, 8 * width), F32),
+        shape((rows, 4 * wide), F32),
+        shape((8, half + tail, wide)),
+    ]
+    return call(
+        kernel,
+        (1,),
+        [whole(a) for a in operands],
+        [whole(a) for a in outs],
+        outs,
+        operands,
+        "text_back",
+        scratch=[pltpu.VMEM((context, 8 * width), BF)],
+    )
+
+
+def caption_output(blocks):
+    count, half, wide = blocks.shape
+
+    def kernel(block, out):
+        out[...] = block[0].astype(F32)
+
+    return call(
+        kernel,
+        (count,),
+        [pl.BlockSpec((1, half, wide), lambda k: (k, 0, 0))],
+        pl.BlockSpec((half, wide), lambda k: plane_block(k)),
+        shape((2 * half, 4 * wide), F32),
+        [blocks],
+        "caption_output",
+    )
+
+
 def column_blocks(weight, count):
     rows = weight.shape[0]
     return weight.reshape(rows, count, -1).transpose(1, 0, 2)
 
 
+def halves_of(values, width):
+    high = values.astype(BF)
+    low = (values - high.astype(F32)).astype(BF)
+    return jnp.concatenate([high.reshape(-1, width), low.reshape(-1, width)], axis=0)
+
+
+def whole_of(halves, width):
+    rows = halves.shape[0] // 2
+    return (halves[:rows] + halves[rows:]).reshape(-1, width)
+
+
 def make_local(z_size):
     def sum_z(values):
         return spread(values, "z", z_size).astype(F32).sum(axis=0)
-
-    def by_plane(values, parts):
-        rows = values.shape[0]
-        shaped = values.reshape(2, rows // 2, parts, 2, 2, -1)
-        return shaped.transpose(3, 0, 4, 1, 2, 5).reshape(8, rows // 2, -1)
-
-    def from_plane(blocks, parts):
-        rows = blocks.shape[1]
-        shaped = blocks.reshape(2, 2, 2, rows, parts, -1)
-        return shaped.transpose(1, 3, 4, 0, 2, 5).reshape(2 * rows, -1)
-
-    def sum_all(values):
-        return sum_z(spread(values, PLANE, 8).sum(axis=0))
 
     def layer_order(values):
         shaped = values.reshape(values.shape[:-1] + (z_size, 2, 2, -1))
@@ -753,9 +809,8 @@
         attn_in, mid, up = lax.optimization_barrier((attn_in, mid, up))
         mid, up = gather_rows(trade(mid)), gather_rows(trade(up))
 
-        own_text = mm_t(caption, w_text).astype(BF)
         kv_rows = w_cross[:, 1:].reshape(shard_rows, 2 * width)
-        kv_part = by_plane(mm(own_text, kv_rows).astype(BF), 2)
+        own_text, kv_part = text_forward(caption, w_text, kv_rows)
         text_kv = trade(kv_part, PLANE).astype(F32).sum(axis=0).astype(BF)
         text_kv = sum_z(text_kv).astype(BF)
         other = swap(text_kv, "c")
@@ -764,21 +819,23 @@
         )
         attn_in, text_kv = lax.optimization_barrier((attn_in, text_kv))
 
-        attn_in, projected = gather_mm(attn_in, rank, first, 0, 3 * group, "qkv_mm")
+        attn_in, projected = gather_mm(attn_in, first, 0, 3 * group, "qkv_mm")
+        self_mixed = self_forward(projected, 2 * images)
         down = column_blocks(w_down, 4)
-        projected, down, grad_top = lax.optimization_barrier((projected, down, grad_top))
+        self_mixed, down = lax.optimization_barrier((self_mixed, down))
         down = gather_rows(trade(down))
-        grad_y = spread(grad_top).reshape(4 * tokens, width)
-        self_mixed = self_forward(projected, 2 * images)
-        parts = scatter_tokens(mm_scatter(self_mixed, rank, first, 3 * group, "out_mm"))
+        parts = mm_scatter(self_mixed, first[:, 3 * group :])
         after_attn, cross_in = add_norm([start_x] + parts, gain_b)
 
-        cross_in, cross_queries = gather_mm(gather_tokens(cross_in), rank, mid, 0, group, "query_mm")
+        cross_in, cross_queries = gather_mm(gather_tokens(cross_in), mid, 0, group, "query_mm")
         cross_mixed = cross_forward(cross_queries, text_kv)
-        parts = scatter_tokens(mm_scatter(cross_mixed, rank, mid, group, "cross_out_mm"))
+        parts = mm_scatter(cross_mixed, mid[:, group:])
         after_cross, mlp_in = add_norm([after_attn] + parts, gain_c)
 
-        mlp_in, activated, slope = feed_up(gather_tokens(mlp_in), rank, up)
+        mlp_in = gather_tokens(mlp_in)
+        mlp_in, grad_top = lax.optimization_barrier((mlp_in, grad_top))
+        grad_y = jnp.concatenate(gather_tokens(grad_top), axis=0)
+        mlp_in, activated, slope = feed_up(mlp_in, up)
         early = [attn_in, self_mixed, cross_in, cross_mixed]
         if inside:
             grad_axes, halves = "z", (core, z_size)
@@ -798,27 +855,26 @@
         slope, down_part, early, mlp_in = lax.optimization_barrier((slope, down_part, early, mlp_in))
         down_rows = scatter_grad(down_part, grad_axes)
         grad_pre = feed_down(grad_y, slope, down)
-        parts = mm_scatter(grad_pre, rank, up, 0, "up_back")
-        parts, grad_pre = lax.optimization_barrier((parts, grad_pre))
+        parts = mm_scatter(grad_pre, up)
         up_part = grad_products([(mlp_in, both(grad_pre))], "up_grads", *halves)
         grad_after_cross, cross_branch, gain_grad_c = norm_back(
-            scatter_tokens(parts), grad_top, after_cross, gain_c
+            parts, grad_top, after_cross, gain_c
         )
 
         cross_branch, grad_cross_mixed = gather_mm(
-            gather_tokens(cross_branch), rank, mid, group, group, "cross_out_back"
+            gather_tokens(cross_branch), mid, group, group, "cross_out_back"
         )
         grad_cq, kv_grad = cross_back(cross_queries, text_kv, grad_cross_mixed)
         up_part, down_rows, kv_grad = lax.optimization_barrier((up_part, down_rows, kv_grad))
         up_rows = scatter_grad(up_part, grad_axes)
         cross_branch, grad_cq_both = both(cross_branch), both(grad_cq)
-        parts = scatter_tokens(mm_scatter(grad_cq, rank, mid, 0, "query_back"))
+        parts = mm_scatter(grad_cq, mid[:, :group])
         grad_after_attn, attn_branch, gain_grad_b = norm_back(
             parts, grad_after_cross, after_attn, gain_b
         )
 
         attn_branch, grad_self_mixed = gather_mm(
-            gather_tokens(attn_branch), rank, first, 3 * group, group, "out_back"
+            gather_tokens(attn_branch), first, 3 * group, group, "out_back"
         )
         grad_projected = self_back(projected, grad_self_mixed, 2 * images)
         rest_part = grad_products(
@@ -836,7 +892,7 @@
         )
         rest_part, up_rows = lax.optimization_barrier((rest_part, up_rows))
         rest_rows = scatter_grad(rest_part, grad_axes)
-        parts = scatter_tokens(mm_scatter(grad_projected, rank, first, 0, "qkv_back"))
+        parts = mm_scatter(grad_projected, first[:, : 3 * group])
         grad_hidden, gain_grad_a, mask_grad = last_back(
             parts,
             grad_after_attn,
@@ -847,23 +903,28 @@
             order,
         )
         sums = jnp.concatenate([gain_grad_a, gain_grad_b, gain_grad_c, mask_grad], axis=0)
-        sums = layer_order(sum_all(sums))
-
-        parts = scatter_tokens(mm_scatter(activated, rank, down, 0, "down_mm"))
+
+        parts = mm_scatter(activated, down)
         output = layer_output(after_cross, parts, unit, order)
 
         kv_halves = kv_grad.reshape(2, -1, 2 * group)
         kv_keep = lax.dynamic_index_in_dim(kv_halves, core, 0, keepdims=False)
         kv_send = lax.dynamic_index_in_dim(kv_halves, 1 - core, 0, keepdims=False)
         kv_sum = sum_z((kv_keep + swap(kv_send, "c")).astype(BF)).astype(BF)
-        kv_grads = from_plane(spread(kv_sum, PLANE, 8), 2)
-        kv_weight_grad = t_mm(own_text, kv_grads)
-        grad_text = mm_t(kv_grads, kv_rows).astype(BF)
-        grad_text_w = t_mm(grad_text, caption)
-        caption_part = by_plane(mm(grad_text, w_text).astype(BF), 1)
-        caption_own = trade(caption_part, PLANE).astype(F32).sum(axis=0).astype(BF)
-        caption_own = sum_z(caption_own).astype(BF)
-        grad_caption = from_plane(spread(caption_own, PLANE, 8), 1).astype(F32)
+        kv_grads = spread(kv_sum, PLANE, 8)
+        kv_weight_grad, grad_text_w, caption_part = text_back(
+            kv_grads, own_text, kv_rows, caption, w_text, halves_of(sums, text_width // 4)
+        )
+        half_context = caption.shape[0] // 2
+
+        def summed(total):
+            return total[:half_context].astype(BF), whole_of(total[half_context:], width)
+
+        caption_part, sums = summed(trade(caption_part, PLANE).astype(F32).sum(axis=0))
+        both_parts = jnp.concatenate([caption_part, halves_of(sums, text_width // 4)], axis=0)
+        caption_part, sums = summed(sum_z(both_parts))
+        grad_caption = caption_output(spread(caption_part, PLANE, 8))
+        sums = layer_order(sums)
 
         wide_rows = jnp.concatenate([down_rows, up_rows], axis=2)
         down_grad, up_grad = finish_wide(swap_blocks(wide_rows, rank), rank)

time: 754 us -> 706 us (0.936)
  Pallas kernels: 137 us -> 107 us
  matrix products: 5.37 us -> 33.5 us
  local copies, waits for them, and re-layouts: 101 us -> 77.4 us
  other arithmetic: 20.1 us -> 8.52 us
  starting transfers between devices: 101 us -> 90.8 us
  blocking collectives: 89.5 us -> 81.2 us
  waiting for transfers between devices: 274 us -> 282 us
    pallas_call x17 -> x6, Pallas kernels: 103 us -> 38.1 us  [call(): pl.pallas_call(kernel, grid_spec=spec, **options)]
    ppermute x64 -> x68, waiting for transfers between devices: 227 us -> 189 us  [swap(): return lax.ppermute(values, axis, PAIR)]
    pallas_call x12 -> x20, Pallas kernels: 33.7 us -> 68.8 us  [call(): pl.pallas_call(kernel, grid=grid, in_specs=in_specs, out_specs=out_specs,...]
    all_to_all x8 -> x5, waiting for transfers between devices: 27.6 us -> 56.8 us  [trade(): return lax.all_to_all(blocks, axes, 0, 0, tiled=True)]
    dot_general x6, matrix products: 5.37 us -> 33.5 us  [dot(): return lax.dot_general(a, b, (dims, ((), ())), preferred_element_type=F32)]
    all_gather x4, waiting for transfers between devices: 0.04 us -> 19.8 us  [gather_rows(): lax.all_gather(rows.reshape(-1, rows.shape[-1]), DATA, axis=0, tiled=True)]
    all_to_all x8 -> x5, starting transfers between devices: 34.4 us -> 19.8 us  [trade(): return lax.all_to_all(blocks, axes, 0, 0, tiled=True)]
    reshape x7 -> x0, local copies, waits for them, and re-layouts: 12.2 us -> none  [the longest x4 6.73 us: by_plane(): shaped = values.reshape(2, rows // 2, parts, 2, 2, -1)]
  transfers between devices with their start and end apart: 82 -> 83, of which waited for: 45 -> 51; matrix products, arithmetic and copies ran while one was open for 12% -> 10% of each run, Pallas kernels for 18% -> 15%
where the time goes in v10:
time: 706 us; the launch traced here: 697 us
  waiting for transfers between devices  282 us (40%)
  Pallas kernels  107 us (15%)
  starting transfers between devices  90.8 us (13%)
  blocking collectives  81.2 us (12%)
  local copies, waits for them, and re-layouts  77.4 us (11%)
  matrix products  33.5 us (5%)
  between operations  16.4 us (2%)
  other arithmetic  8.52 us (1%)
    ppermute x68, waiting for transfers between devices, swap(): return lax.ppermute(values, axis, PAIR)  189 us
    all_to_all x5, blocking collectives, trade(): return lax.all_to_all(blocks, axes, 0, 0, tiled=True)  81.2 us
    pallas_call x20, Pallas kernels, call(): pl.pallas_call(kernel, grid=grid, in_specs=in_specs, out_specs=out_specs,...  68.8 us
    ppermute x68, starting transfers between devices, swap(): return lax.ppermute(values, axis, PAIR)  68.6 us
    all_to_all x5, waiting for transfers between devices, trade(): return lax.all_to_all(blocks, axes, 0, 0, tiled=True)  56.8 us
    unnamed x180, local copies, waits for them, and re-layouts  49.2 us
    pallas_call x6, Pallas kernels, call(): pl.pallas_call(kernel, grid_spec=spec, **options)  38.1 us
    dot_general x6, matrix products, dot(): return lax.dot_general(a, b, (dims, ((), ())), preferred_element_type=F32)  33.5 us
  transfers between devices with their start and end apart: 83, of which 51 were waited for; matrix products, arithmetic and copies ran while one was open for 10% of the time, Pallas kernels for 15%

profile of v10, /device:TPU:0, one launch (start us, length us, event | category | flops | bytes accessed | tf_op | source)
XLA Modules:
  0.0 697.1 jit_solution(3785785840670501000)
XLA Ops:
  36.6 9.6 %collective-permute-done.1.refs_2_ = bf16[128,2048]{1,0:T(8,128)(2,1)S(1)} collective-permute-done((bf16[128,2048]{1,0:T(8,128)(2,1)S(1)}, bf16[128,2048]{1,0:T(8,128)(2,1)S(1)}, u32[]{:S(2)}, u32[]{:S(2)}) %collective-permute-start.1) | collective-permute-done | bytes 524320 | tf_op jit(solution)/shard_map/ppermute | solution.py:46
  56.5 10.2 %all_to_all.50 = bf16[4,64,1024]{2,1,0:T(8,128)(2,1)} all-to-all(bf16[4,64,1024]{2,1,0:T(8,128)(2,1)S(1)} %pad_maximum_fusion), channel_id=1, replica_groups=mesh['z'=4,'x'=2,'c'=2,'y'=2] {'x','y'}, dimensions={0} | all-to-all | bytes 1048576 | tf_op jit(solution)/shard_map/all_to_all | solution.py:50
  66.8 13.8 %all_to_all.51 = bf16[4,64,2048]{2,1,0:T(8,128)(2,1)} all-to-all(bf16[4,64,2048]{2,1,0:T(8,128)(2,1)S(1)} %bitcast.129), channel_id=1, replica_groups=mesh['z'=4,'x'=2,'c'=2,'y'=2] {'x','y'}, dimensions={0} | all-to-all | bytes 2097152 | tf_op jit(solution)/shard_map/all_to_all | solution.py:50
  83.3 16.9 %all_to_all.52 = bf16[8,64,1024]{2,1,0:T(8,128)(2,1)S(1)} all-to-all(bf16[8,64,1024]{2,1,0:T(8,128)(2,1)S(1)} %get-tuple-element.100), channel_id=1, replica_groups=mesh['z'=4,'x'=2,'c'=2,'y'=2] {'x','c','y'}, dimensions={0} | all-to-all | bytes 2097152 | tf_op jit(solution)/shard_map/all_to_all | solution.py:50
  100.4 22.2 %all_to_all.53 = bf16[4,64,1024]{2,1,0:T(8,128)(2,1)S(1)} all-to-all(bf16[4,64,1024]{2,1,0:T(8,128)(2,1)S(1)} %broadcast_in_dim.10), channel_id=1, replica_groups=mesh['z'=4,'x'=2,'c'=2,'y'=2] {'z'}, dimensions={0} | all-to-all | bytes 1048576 | tf_op jit(solution)/shard_map/all_to_all | solution.py:50
  137.3 18.1 %all_to_all.54 = bf16[4,64,2048]{2,1,0:T(8,128)(2,1)} all-to-all(bf16[4,64,2048]{2,1,0:T(8,128)(2,1)S(1)} %bitcast.128), channel_id=1, replica_groups=mesh['z'=4,'x'=2,'c'=2,'y'=2] {'x','y'}, dimensions={0} | all-to-all | bytes 2097152 | tf_op jit(solution)/shard_map/all_to_all | solution.py:50
  169.2 10.2 %collective-permute-done.11.refs_3_ = bf16[128,2048]{1,0:T(8,128)(2,1)S(1)} collective-permute-done((bf16[128,2048]{1,0:T(8,128)(2,1)S(1)}, bf16[128,2048]{1,0:T(8,128)(2,1)S(1)}, u32[]{:S(2)}, u32[]{:S(2)}) %collective-permute-start.11) | collective-permute-done | bytes 524320 | tf_op jit(solution)/shard_map/ppermute | solution.py:46
  184.0 8.8 %collective-permute-done.13.refs_2_ = bf16[128,2048]{1,0:T(8,128)(2,1)S(1)} collective-permute-done((bf16[128,2048]{1,0:T(8,128)(2,1)S(1)}, bf16[128,2048]{1,0:T(8,128)(2,1)S(1)}, u32[]{:S(2)}, u32[]{:S(2)}) %collective-permute-start.13) | collective-permute-done | bytes 524320 | tf_op jit(solution)/shard_map/ppermute | solution.py:46
  240.5 10.4 %collective-permute-done.21.refs_2_ = bf16[128,2048]{1,0:T(8,128)(2,1)S(1)} collective-permute-done((bf16[128,2048]{1,0:T(8,128)(2,1)S(1)}, bf16[128,2048]{1,0:T(8,128)(2,1)S(1)}, u32[]{:S(2)}, u32[]{:S(2)}) %collective-permute-start.21) | collective-permute-done | bytes 524320 | tf_op jit(solution)/shard_map/ppermute | solution.py:46
  269.7 11.9 %feed_up.1 = (bf16[512,2048]{1,0:T(8,128)(2,1)}, bf16[512,2048]{1,0:T(8,128)(2,1)}, f32[512,2048]{1,0:T(8,128)}) custom-call(bf16[128,2048]{1,0:T(8,128)(2,1)S(1)} %copy-done.57, bf16[128,2048]{1,0:T(8,128)(2,1)S(1)} %copy-done.53, bf16[128,2048]{1,0:T(8,128)(2,1)S(1)} %copy-done.51, bf16[64,2048]{1,0:T(8,128)(2,1)S(1)} %copy-done.63, ...), custom_call_target="tpu_custom_call" | custom-call | flops 4294967296 | bytes 12582912 | tf_op jit(solution)/shard_map/feed_up/pallas_call | solution.py:102
  301.2 8.7 %down_grads.1 = bf16[1024,2048]{1,0:T(8,128)(2,1)} custom-call(s32[1]{0:T(128)} %bitcast.26.r, bf16[512,2048]{1,0:T(8,128)(2,1)S(1)} %constant_dynamic-update-slice_fusion.refs_0_.dy, bf16[512,2048]{1,0:T(8,128)(2,1)S(1)} %collective-permute-done.28.refs_1_, bf16[512,2048]{1,0:T(8,128)(2,1)} %get-tuple-element.152.refs_2_, bf16[512,2048]{1,0:T(8,128)(2,1)} %copy-done.85), custom_call_target="tpu_custom_call" | custom-call | flops 4294967296 | bytes 16777216 | tf_op jit(solution)/shard_map/down_grads/pallas_call | solution.py:113
  311.9 19.8 %all-gather.11.cloned.1.call-done.down = bf16[2048,2048]{1,0:T(8,128)(2,1)} async-done(((bf16[256,2048]{1,0:T(8,128)(2,1)}), bf16[2048,2048]{1,0:T(8,128)(2,1)}) %all-gather.11.cloned.1.call-update) | async-done | bytes 8388624 | tf_op jit(solution)/shard_map/all_gather | solution.py:85
  333.3 9.9 %feed_down.1.refs_2_ = bf16[512,2048]{1,0:T(8,128)(2,1)S(1)} custom-call(bf16[512,2048]{1,0:T(8,128)(2,1)S(1)} %copy-done.18, f32[512,2048]{1,0:T(8,128)} %get-tuple-element.128.slope_ref, bf16[2048,2048]{1,0:T(8,128)(2,1)} %all-gather.11.cloned.1.call-done.down), custom_call_target="tpu_custom_call" | custom-call | flops 4294967296 | bytes 25165824 | tf_op jit(solution)/shard_map/feed_down/pallas_call | solution.py:102
  363.3 10.8 %collective-permute-done.38.refs_2_ = bf16[128,2048]{1,0:T(8,128)(2,1)S(1)} collective-permute-done((bf16[128,2048]{1,0:T(8,128)(2,1)S(1)}, bf16[128,2048]{1,0:T(8,128)(2,1)S(1)}, u32[]{:S(2)}, u32[]{:S(2)}) %collective-permute-start.38) | collective-permute-done | bytes 524320 | tf_op jit(solution)/shard_map/ppermute | solution.py:46
  380.5 9.2 %collective-permute-done.40.refs_2_ = bf16[128,2048]{1,0:T(8,128)(2,1)S(1)} collective-permute-done((bf16[128,2048]{1,0:T(8,128)(2,1)S(1)}, bf16[128,2048]{1,0:T(8,128)(2,1)S(1)}, u32[]{:S(2)}, u32[]{:S(2)}) %collective-permute-start.40) | collective-permute-done | bytes 524320 | tf_op jit(solution)/shard_map/ppermute | solution.py:46
  407.3 8.8 %up_grads.1 = bf16[1024,2048]{1,0:T(8,128)(2,1)} custom-call(s32[1]{0:T(128)} %bitcast.26.r, bf16[512,2048]{1,0:T(8,128)(2,1)} %get-tuple-element.137.refs_0_, bf16[512,2048]{1,0:T(8,128)(2,1)} %collective-permute-done.34.refs_1_, bf16[512,2048]{1,0:T(8,128)(2,1)} %copy-done.25, bf16[512,2048]{1,0:T(8,128)(2,1)} %copy-done.84), custom_call_target="tpu_custom_call" | custom-call | flops 4294967296 | bytes 16777216 | tf_op jit(solution)/shard_map/up_grads/pallas_call | solution.py:113
  431.0 9.6 %collective-permute-done.46.refs_2_ = bf16[128,2048]{1,0:T(8,128)(2,1)S(1)} collective-permute-done((bf16[128,2048]{1,0:T(8,128)(2,1)S(1)}, bf16[128,2048]{1,0:T(8,128)(2,1)S(1)}, u32[]{:S(2)}, u32[]{:S(2)}) %collective-permute-start.46) | collective-permute-done | bytes 524320 | tf_op jit(solution)/shard_map/ppermute | solution.py:46
  447.0 8.0 %collective-permute-done.48.refs_2_ = bf16[128,2048]{1,0:T(8,128)(2,1)S(1)} collective-permute-done((bf16[128,2048]{1,0:T(8,128)(2,1)S(1)}, bf16[128,2048]{1,0:T(8,128)(2,1)S(1)}, u32[]{:S(2)}, u32[]{:S(2)}) %collective-permute-start.48) | collective-permute-done | bytes 524320 | tf_op jit(solution)/shard_map/ppermute | solution.py:46
  480.7 11.6 %attention_grads.1 = bf16[1024,3072]{1,0:T(8,128)(2,1)} custom-call(s32[1]{0:T(128)} %bitcast.26.r, bf16[512,2048]{1,0:T(8,128)(2,1)} %get-tuple-element.142.refs_0_, bf16[512,2048]{1,0:T(8,128)(2,1)} %collective-permute-done.30.refs_1_, bf16[512,2048]{1,0:T(8,128)(2,1)} %copy-done.26, bf16[512,2048]{1,0:T(8,128)(2,1)} %copy-done.70, ...), custom_call_target="tpu_custom_call" | custom-call | flops 6442450944 | bytes 25165824 | tf_op jit(solution)/shard_map/attention_grads/pallas_call | solution.py:113
  517.8 19.6 %all-to-all-done.5 = bf16[4,64,1024]{2,1,0:T(8,128)(2,1)S(1)} async-done(((bf16[4,64,1024]{2,1,0:T(8,128)(2,1)}), bf16[4,64,1024]{2,1,0:T(8,128)(2,1)S(1)}, u32[]{:S(2)}, u32[]{:S(2)}) %all-to-all-start.5) | async-done | bytes 524320 | tf_op jit(solution)/shard_map/all_to_all | solution.py:50
  565.0 10.7 %fusion.30 = (bf16[512,2048]{1,0:T(8,128)(2,1)S(1)}, f32[512,2048]{1,0:T(8,128)}) fusion(bf16[512,2048]{1,0:T(8,128)(2,1)} %get-tuple-element.152.refs_2_, bf16[2048,2048]{1,0:T(8,128)(2,1)} %all-gather.11.cloned.1.call-done.down), kind=kOutput, calls=%fused_computation.106 | convolution fusion | flops 4296015872 | bytes 16777216 | tf_op jit(solution)/shard_map/dot_general | solution.py:26
  594.6 27.9 %all-to-all-done.8 = bf16[4,80,1024]{2,1,0:T(8,128)(2,1)S(1)} async-done(((bf16[4,80,1024]{2,1,0:T(8,128)(2,1)}), bf16[4,80,1024]{2,1,0:T(8,128)(2,1)S(1)}, u32[]{:S(2)}, u32[]{:S(2)}) %all-to-all-start.8) | async-done | bytes 655392 | tf_op jit(solution)/shard_map/all_to_all | solution.py:50
  641.8 11.6 %collective-permute-done.68.refs_1_ = bf16[64,4096]{1,0:T(8,128)(2,1)S(1)} collective-permute-done((bf16[64,4096]{1,0:T(8,128)(2,1)}, bf16[64,4096]{1,0:T(8,128)(2,1)S(1)}, u32[]{:S(2)}, u32[]{:S(2)}) %collective-permute-start.68) | collective-permute-done | bytes 524320 | tf_op jit(solution)/shard_map/ppermute | solution.py:46
  673.3 8.9 %collective-permute-done.67.refs_3_ = bf16[64,3072]{1,0:T(8,128)(2,1)} collective-permute-done((bf16[64,3072]{1,0:T(8,128)(2,1)}, bf16[64,3072]{1,0:T(8,128)(2,1)}, u32[]{:S(2)}, u32[]{:S(2)}) %collective-permute-start.67) | collective-permute-done | bytes 393248 | tf_op jit(solution)/shard_map/ppermute | solution.py:80
  (463 shorter events, 373.7 us)
Async XLA Ops:
  7.2 117.0 %all-gather.5.cloned.1.call-start = ((), (), s32[]{:S(2)}) async-start(), calls=%async_computation.13 | async-start | bytes 9437184 | tf_op jit(solution)/shard_map/all_gather | solution.py:85
  29.4 167.9 %all-gather.7.cloned.1.call-start = ((), (), s32[]{:S(2)}) async-start(), calls=%async_computation.14 | async-start | bytes 4718592 | tf_op jit(solution)/shard_map/all_gather | solution.py:85
  66.7 198.0 %all-gather.9.cloned.1.call-start = ((), (), s32[]{:S(2)}) async-start(), calls=%async_computation.15 | async-start | bytes 9437184 | tf_op jit(solution)/shard_map/all_gather | solution.py:85
  80.6 251.1 %all-gather.11.cloned.1.call-start = ((), (), s32[]{:S(2)}) async-start(), calls=%async_computation.16 | async-start | bytes 9437184 | tf_op jit(solution)/shard_map/all_gather | solution.py:85
  155.4 260.7 %reduce-scatter.4.cloned.1.call-start = ((), (), s32[]{:S(2)}) async-start(), calls=%async_computation.17 | async-start | bytes 5242880 | tf_op jit(solution)/shard_map/reduce_scatter | solution.py:89
  262.5 22.7 %collective-permute-start.24 = (bf16[128,2048]{1,0:T(8,128)(2,1)}, bf16[128,2048]{1,0:T(8,128)(2,1)}, u32[]{:S(2)}, u32[]{:S(2)}) collective-permute-start(bf16[128,2048]{1,0:T(8,128)(2,1)} %get-tuple-element.116.refs_3_), channel_id=1, source_target_pairs={{0,1},{1,0},{2,3},{3,2},{4,5},{5,4},{6,7},{7,6},{8,9},{9,8},{10,11... | collective-permute-start | bytes 1572872 | tf_op jit(solution)/shard_map/ppermute | solution.py:46
  263.9 18.7 %collective-permute-start.25 = (bf16[128,2048]{1,0:T(8,128)(2,1)}, bf16[128,2048]{1,0:T(8,128)(2,1)}, u32[]{:S(2)}, u32[]{:S(2)}) collective-permute-start(bf16[128,2048]{1,0:T(8,128)(2,1)} %get-tuple-element.116.refs_3_), channel_id=1, source_target_pairs={{0,4},{4,0},{1,5},{5,1},{2,6},{6,2},{3,7},{7,3},{8,12},{12,8},{9,1... | collective-permute-start | bytes 1572872 | tf_op jit(solution)/shard_map/ppermute | solution.py:46
  311.3 182.2 %reduce-scatter.6.cloned.1.call-start = ((), (), s32[]{:S(2)}) async-start(), calls=%async_computation.18 | async-start | bytes 5242880 | tf_op jit(solution)/shard_map/reduce_scatter | solution.py:89
  354.1 51.8 %collective-permute-start.51 = (bf16[512,2048]{1,0:T(8,128)(2,1)S(1)}, bf16[512,2048]{1,0:T(8,128)(2,1)S(1)}, u32[]{:S(2)}, u32[]{:S(2)}) collective-permute-start(bf16[512,2048]{1,0:T(8,128)(2,1)S(1)} %feed_down.1.refs_2_), channel_id=1, source_target_pairs={{0,2},{2,0},{1,3},{3,1},{4,6},{6,4},{5,7},{7,5},{8,10},{10,8},{9,1... | collective-permute-start | bytes 6291464 | tf_op jit(solution)/shard_map/ppermute | solution.py:46
  416.2 219.6 %reduce-scatter.8.cloned.1.call-start = ((), (), s32[]{:S(2)}) async-start(), calls=%async_computation.19 | async-start | bytes 7864320 | tf_op jit(solution)/shard_map/reduce_scatter | solution.py:89
  505.6 31.8 %all-to-all-start.5 = ((bf16[4,64,1024]{2,1,0:T(8,128)(2,1)}), bf16[4,64,1024]{2,1,0:T(8,128)(2,1)S(1)}, u32[]{:S(2)}, u32[]{:S(2)}) async-start(bf16[4,64,1024]{2,1,0:T(8,128)(2,1)} %broadcast_in_dim.11), calls=%async_computation.6 | async-start | bytes 1048576 | tf_op jit(solution)/shard_map/all_to_all | solution.py:50
  515.1 28.7 %collective-permute-start.63 = (bf16[128,2048]{1,0:T(8,128)(2,1)}, bf16[128,2048]{1,0:T(8,128)(2,1)S(1)}, u32[]{:S(2)}, u32[]{:S(2)}) collective-permute-start(bf16[128,2048]{1,0:T(8,128)(2,1)} %pad_maximum_fusion.12), channel_id=1, source_target_pairs={{0,1},{1,0},{2,3},{3,2},{4,5},{5,4},{6,7},{7,6},{8,9},{9,8},{10,11... | collective-permute-start | bytes 1572872 | tf_op jit(solution)/shard_map/ppermute | solution.py:46
  517.6 27.0 %collective-permute-start.61 = (bf16[128,2048]{1,0:T(8,128)(2,1)}, bf16[128,2048]{1,0:T(8,128)(2,1)S(1)}, u32[]{:S(2)}, u32[]{:S(2)}) collective-permute-start(bf16[128,2048]{1,0:T(8,128)(2,1)} %pad_maximum_fusion.11), channel_id=1, source_target_pairs={{0,4},{4,0},{1,5},{5,1},{2,6},{6,2},{3,7},{7,3},{8,12},{12,8},{9,1... | collective-permute-start | bytes 1572872 | tf_op jit(solution)/shard_map/ppermute | solution.py:46
  561.2 21.5 %all-to-all-start.7 = ((bf16[8,80,1024]{2,1,0:T(8,128)(2,1)}), bf16[8,80,1024]{2,1,0:T(8,128)(2,1)S(1)}, u32[]{:S(2)}, u32[]{:S(2)}) async-start(bf16[8,80,1024]{2,1,0:T(8,128)(2,1)} %copy-done.27), calls=%async_computation.8 | async-start | bytes 2621440 | tf_op jit(solution)/shard_map/all_to_all | solution.py:50
  583.9 38.6 %all-to-all-start.8 = ((bf16[4,80,1024]{2,1,0:T(8,128)(2,1)}), bf16[4,80,1024]{2,1,0:T(8,128)(2,1)S(1)}, u32[]{:S(2)}, u32[]{:S(2)}) async-start(bf16[4,80,1024]{2,1,0:T(8,128)(2,1)} %broadcast_in_dim.13), calls=%async_computation.9 | async-start | bytes 1310720 | tf_op jit(solution)/shard_map/all_to_all | solution.py:50
  591.8 46.6 %collective-permute-start.59 = (bf16[128,2048]{1,0:T(8,128)(2,1)}, bf16[128,2048]{1,0:T(8,128)(2,1)S(1)}, u32[]{:S(2)}, u32[]{:S(2)}) collective-permute-start(bf16[128,2048]{1,0:T(8,128)(2,1)} %pad_maximum_fusion.10), channel_id=1, source_target_pairs={{0,1},{1,0},{2,3},{3,2},{4,5},{5,4},{6,7},{7,6},{8,9},{9,8},{10,11... | collective-permute-start | bytes 1572872 | tf_op jit(solution)/shard_map/ppermute | solution.py:46
  594.1 46.2 %collective-permute-start.57 = (bf16[128,2048]{1,0:T(8,128)(2,1)}, bf16[128,2048]{1,0:T(8,128)(2,1)S(1)}, u32[]{:S(2)}, u32[]{:S(2)}) collective-permute-start(bf16[128,2048]{1,0:T(8,128)(2,1)} %pad_maximum_fusion.9), channel_id=1, source_target_pairs={{0,4},{4,0},{1,5},{5,1},{2,6},{6,2},{3,7},{7,3},{8,12},{12,8},{9,1... | collective-permute-start | bytes 1572872 | tf_op jit(solution)/shard_map/ppermute | solution.py:46
  623.7 35.6 %all-to-all-start.9 = ((bf16[8,64,1024]{2,1,0:T(8,128)(2,1)}), bf16[8,64,1024]{2,1,0:T(8,128)(2,1)S(1)}, u32[]{:S(2)}, u32[]{:S(2)}) async-start(bf16[8,64,1024]{2,1,0:T(8,128)(2,1)} %broadcast_in_dim.14), calls=%async_computation.10 | async-start | bytes 2097152 | tf_op jit(solution)/shard_map/all_to_all | solution.py:50
  632.3 21.1 %collective-permute-start.68 = (bf16[64,4096]{1,0:T(8,128)(2,1)}, bf16[64,4096]{1,0:T(8,128)(2,1)S(1)}, u32[]{:S(2)}, u32[]{:S(2)}) collective-permute-start(bf16[64,4096]{1,0:T(8,128)(2,1)} %get-tuple-element.242), channel_id=1, source_target_pairs={{0,1},{1,0},{2,3},{3,2},{4,5},{5,4},{6,7},{7,6},{8,9},{9,8},{10,11... | collective-permute-start | bytes 1572872 | tf_op jit(solution)/shard_map/ppermute | solution.py:46
  634.2 28.1 %collective-permute-start.69 = (bf16[64,4096]{1,0:T(8,128)(2,1)}, bf16[64,4096]{1,0:T(8,128)(2,1)}, u32[]{:S(2)}, u32[]{:S(2)}) collective-permute-start(bf16[64,4096]{1,0:T(8,128)(2,1)} %get-tuple-element.241), channel_id=1, source_target_pairs={{0,4},{4,0},{1,5},{5,1},{2,6},{6,2},{3,7},{7,3},{8,12},{12,8},{9,1... | collective-permute-start | bytes 1572872 | tf_op jit(solution)/shard_map/ppermute | solution.py:46
  635.7 30.1 %collective-permute-start.70 = (bf16[64,4096]{1,0:T(8,128)(2,1)}, bf16[64,4096]{1,0:T(8,128)(2,1)}, u32[]{:S(2)}, u32[]{:S(2)}) collective-permute-start(bf16[64,4096]{1,0:T(8,128)(2,1)} %get-tuple-element.240), channel_id=1, source_target_pairs={{0,5},{1,4},{4,1},{5,0},{2,7},{3,6},{6,3},{7,2},{8,13},{9,12},{12,... | collective-permute-start | bytes 1572872 | tf_op jit(solution)/shard_map/ppermute | solution.py:80
  638.4 34.3 %collective-permute-start.65 = (bf16[64,3072]{1,0:T(8,128)(2,1)}, bf16[64,3072]{1,0:T(8,128)(2,1)}, u32[]{:S(2)}, u32[]{:S(2)}) collective-permute-start(bf16[64,3072]{1,0:T(8,128)(2,1)} %get-tuple-element.282), channel_id=1, source_target_pairs={{0,1},{1,0},{2,3},{3,2},{4,5},{5,4},{6,7},{7,6},{8,9},{9,8},{10,11... | collective-permute-start | bytes 1179656 | tf_op jit(solution)/shard_map/ppermute | solution.py:46
  640.3 33.0 %collective-permute-start.66 = (bf16[64,3072]{1,0:T(8,128)(2,1)}, bf16[64,3072]{1,0:T(8,128)(2,1)}, u32[]{:S(2)}, u32[]{:S(2)}) collective-permute-start(bf16[64,3072]{1,0:T(8,128)(2,1)} %get-tuple-element.281), channel_id=1, source_target_pairs={{0,4},{4,0},{1,5},{5,1},{2,6},{6,2},{3,7},{7,3},{8,12},{12,8},{9,1... | collective-permute-start | bytes 1179656 | tf_op jit(solution)/shard_map/ppermute | solution.py:46
  653.4 28.8 %collective-permute-start.67 = (bf16[64,3072]{1,0:T(8,128)(2,1)}, bf16[64,3072]{1,0:T(8,128)(2,1)}, u32[]{:S(2)}, u32[]{:S(2)}) collective-permute-start(bf16[64,3072]{1,0:T(8,128)(2,1)} %get-tuple-element.280), channel_id=1, source_target_pairs={{0,5},{1,4},{4,1},{5,0},{2,7},{3,6},{6,3},{7,2},{8,13},{9,12},{12,... | collective-permute-start | bytes 1179656 | tf_op jit(solution)/shard_map/ppermute | solution.py:80
  (146 other events, 1169.0 us)
Sparse Core Ops, SparseCore 0:
  29.5 88.8 all-gather.4
  120.0 47.1 all-gather.6
  168.8 80.7 all-gather.8
  251.1 80.5 all-gather.10
  333.8 75.2 reduce-scatter.3
  416.3 74.4 reduce-scatter.5
  493.7 129.0 reduce-scatter.7

commit v11 on v10

--- a/solution.py
+++ b/solution.py
@@ -123,12 +123,19 @@
     return jnp.concatenate([values[:, k * unit : (k + 1) * unit] for k in order], axis=1)
 
 
-def assemble(target, pieces):
-    at = 0
-    for piece in pieces:
+def assemble(target, pieces, sems):
+    copies, at = [], 0
+    for k, piece in enumerate(pieces):
         rows = piece.shape[0]
-        target[at : at + rows, :] = piece[...]
+        copies.append(pltpu.make_async_copy(piece, target.at[at : at + rows], sems.at[k]))
         at += rows
+    for copy in copies:
+        copy.start()
+    for copy in copies:
+        copy.wait()
+
+
+ANY = pl.BlockSpec(memory_space=pltpu.MemorySpace.HBM)
 
 
 def gather_mm(pieces, weight, first, columns, name):
@@ -136,18 +143,18 @@
     step = 256
 
     def kernel(*refs):
-        tokens, out = refs[6], refs[7]
+        tokens, out, sems = refs[6:]
 
         @pl.when(pl.program_id(0) == 0)
         def _():
-            assemble(tokens, refs[:5])
+            assemble(tokens, refs[:5], sems)
 
         out[...] = mm(tokens[...], refs[5][...]).astype(BF)
 
     return call(
         kernel,
         (columns // step,),
-        [whole(p) for p in pieces] + [pl.BlockSpec((width, step), lambda j: (0, first // step + j))],
+        [ANY] * 5 + [pl.BlockSpec((width, step), lambda j: (0, first // step + j))],
         [
             pl.BlockSpec((4 * rows, width), lambda j: (0, 0)),
             pl.BlockSpec((4 * rows, step), lambda j: (0, j)),
@@ -157,6 +164,7 @@
         name,
         flops=8 * rows * width * columns,
         size=2 * width * (columns + 8 * rows),
+        scratch=[pltpu.SemaphoreType.DMA((5,))],
     )
 
 
@@ -337,11 +345,11 @@
     step = 256
 
     def kernel(*refs):
-        up, tokens, act, slope = refs[5:]
+        up, tokens, act, slope, sems = refs[5:]
 
         @pl.when(pl.program_id(0) == 0)
         def _():
-            assemble(tokens, refs[:5])
+            assemble(tokens, refs[:5], sems)
 
         u = mm(tokens[...], up[...])
         square = u * u
@@ -354,11 +362,12 @@
     return call(
         kernel,
         (hidden // step,),
-        [whole(p) for p in pieces] + [pl.BlockSpec((width, step), lambda j: (0, j))],
+        [ANY] * 5 + [pl.BlockSpec((width, step), lambda j: (0, j))],
         [pl.BlockSpec((4 * rows, width), lambda j: (0, 0)), part, part],
         [shape((4 * rows, width)), shape((4 * rows, hidden)), shape((4 * rows, hidden), F32)],
         [*pieces, weight],
         "feed_up",
+        scratch=[pltpu.SemaphoreType.DMA((5,))],
         flops=8 * rows * width * hidden,
         size=2 * width * (hidden + 8 * rows),
     )
@@ -738,7 +747,18 @@
 
 def make_local(z_size):
     def sum_z(values):
-        return spread(values, "z", z_size).astype(F32).sum(axis=0)
+        parts = values.reshape(z_size, -1, values.shape[-1])
+        mine = trade(parts, "z").astype(F32).sum(axis=0).astype(BF)
+        return spread(mine, "z", z_size).reshape(values.shape)
+
+    def add_z(values):
+        step = 1
+        while step < z_size:
+            values = values + lax.ppermute(
+                values, "z", tuple((k, k ^ step) for k in range(z_size))
+            )
+            step *= 2
+        return values
 
     def layer_order(values):
         shaped = values.reshape(values.shape[:-1] + (z_size, 2, 2, -1))
@@ -812,7 +832,7 @@
         kv_rows = w_cross[:, 1:].reshape(shard_rows, 2 * width)
         own_text, kv_part = text_forward(caption, w_text, kv_rows)
         text_kv = trade(kv_part, PLANE).astype(F32).sum(axis=0).astype(BF)
-        text_kv = sum_z(text_kv).astype(BF)
+        text_kv = sum_z(text_kv)
         other = swap(text_kv, "c")
         text_kv = jnp.concatenate(
             [jnp.where(core == 0, text_kv, other), jnp.where(core == 0, other, text_kv)], axis=0
@@ -861,8 +881,10 @@
             parts, grad_top, after_cross, gain_c
         )
 
+        cross_branch = gather_tokens(cross_branch)
+        cross_branch, up_part = lax.optimization_barrier((cross_branch, up_part))
         cross_branch, grad_cross_mixed = gather_mm(
-            gather_tokens(cross_branch), mid, group, group, "cross_out_back"
+            cross_branch, mid, group, group, "cross_out_back"
         )
         grad_cq, kv_grad = cross_back(cross_queries, text_kv, grad_cross_mixed)
         up_part, down_rows, kv_grad = lax.optimization_barrier((up_part, down_rows, kv_grad))
@@ -910,24 +932,21 @@
         kv_halves = kv_grad.reshape(2, -1, 2 * group)
         kv_keep = lax.dynamic_index_in_dim(kv_halves, core, 0, keepdims=False)
         kv_send = lax.dynamic_index_in_dim(kv_halves, 1 - core, 0, keepdims=False)
-        kv_sum = sum_z((kv_keep + swap(kv_send, "c")).astype(BF)).astype(BF)
+        kv_sum = sum_z((kv_keep + swap(kv_send, "c")).astype(BF))
+        wide_rows = jnp.concatenate([down_rows, up_rows], axis=2)
+        wide_rows = swap_blocks(wide_rows, rank)
+        kv_sum, wide_rows = lax.optimization_barrier((kv_sum, wide_rows))
         kv_grads = spread(kv_sum, PLANE, 8)
+        down_grad, up_grad = finish_wide(wide_rows, rank)
         kv_weight_grad, grad_text_w, caption_part = text_back(
             kv_grads, own_text, kv_rows, caption, w_text, halves_of(sums, text_width // 4)
         )
         half_context = caption.shape[0] // 2
-
-        def summed(total):
-            return total[:half_context].astype(BF), whole_of(total[half_context:], width)
-
-        caption_part, sums = summed(trade(caption_part, PLANE).astype(F32).sum(axis=0))
-        both_parts = jnp.concatenate([caption_part, halves_of(sums, text_width // 4)], axis=0)
-        caption_part, sums = summed(sum_z(both_parts))
+        caption_part = trade(caption_part, PLANE).astype(F32).sum(axis=0)
+        sums = layer_order(add_z(whole_of(caption_part[half_context:], width)))
+        caption_part = sum_z(caption_part[:half_context].astype(BF))
         grad_caption = caption_output(spread(caption_part, PLANE, 8))
-        sums = layer_order(sums)
-
-        wide_rows = jnp.concatenate([down_rows, up_rows], axis=2)
-        down_grad, up_grad = finish_wide(swap_blocks(wide_rows, rank), rank)
+
         qkv_grad, out_grad, grad_cross, cross_out_grad = finish_all(
             swap_blocks(rest_rows, rank), kv_weight_grad, rank
         )

time: 706 us -> 679 us (0.962)
  waiting for transfers between devices: 282 us -> 237 us
  starting transfers between devices: 90.8 us -> 103 us
    all_to_all x5 -> x7, waiting for transfers between devices: 56.8 us -> 20.9 us  [trade(): return lax.all_to_all(blocks, axes, 0, 0, tiled=True)]
    all_to_all x5 -> x7, starting transfers between devices: 19.8 us -> 28.8 us  [trade(): return lax.all_to_all(blocks, axes, 0, 0, tiled=True)]
    unnamed x180 -> x200, local copies, waits for them, and re-layouts: 49.2 us -> 52.6 us
    all_to_all x5 -> x6, blocking collectives: 81.2 us -> 80.9 us  [trade(): return lax.all_to_all(blocks, axes, 0, 0, tiled=True)]
  transfers between devices with their start and end apart: 83 -> 87, of which waited for: 51 -> 49; matrix products, arithmetic and copies ran while one was open for 10% -> 11% of each run, Pallas kernels for 15% -> 15%
where the time goes in v11:
time: 679 us; the launch traced here: 670 us
  waiting for transfers between devices  237 us (35%)
  Pallas kernels  108 us (16%)
  starting transfers between devices  103 us (15%)
  local copies, waits for them, and re-layouts  82.4 us (12%)
  blocking collectives  80.9 us (12%)
  matrix products  34.1 us (5%)
  between operations  16.5 us (2%)
  other arithmetic  9.09 us (1%)
    ppermute x68, waiting for transfers between devices, swap(): return lax.ppermute(values, axis, PAIR)  185 us
    all_to_all x6, blocking collectives, trade(): return lax.all_to_all(blocks, axes, 0, 0, tiled=True)  80.9 us
    pallas_call x20, Pallas kernels, call(): pl.pallas_call(kernel, grid=grid, in_specs=in_specs, out_specs=out_specs,...  71.3 us
    ppermute x68, starting transfers between devices, swap(): return lax.ppermute(values, axis, PAIR)  67.8 us
    unnamed x200, local copies, waits for them, and re-layouts  52.6 us
    pallas_call x6, Pallas kernels, call(): pl.pallas_call(kernel, grid_spec=spec, **options)  36.7 us
    dot_general x6, matrix products, dot(): return lax.dot_general(a, b, (dims, ((), ())), preferred_element_type=F32)  34.1 us
    all_to_all x7, starting transfers between devices, trade(): return lax.all_to_all(blocks, axes, 0, 0, tiled=True)  28.8 us
  transfers between devices with their start and end apart: 87, of which 49 were waited for; matrix products, arithmetic and copies ran while one was open for 11% of the time, Pallas kernels for 15%

profile of v11, /device:TPU:0, one launch (start us, length us, event | category | flops | bytes accessed | tf_op | source)
XLA Modules:
  0.0 670.1 jit_solution(7206909208433116535)
XLA Ops:
  36.6 9.6 %collective-permute-done.1.refs_2_ = bf16[128,2048]{1,0:T(8,128)(2,1)S(1)} collective-permute-done((bf16[128,2048]{1,0:T(8,128)(2,1)S(1)}, bf16[128,2048]{1,0:T(8,128)(2,1)S(1)}, u32[]{:S(2)}, u32[]{:S(2)}) %collective-permute-start.1) | collective-permute-done | bytes 524320 | tf_op jit(solution)/shard_map/ppermute | solution.py:46
  56.5 10.2 %all_to_all.65 = bf16[4,64,1024]{2,1,0:T(8,128)(2,1)} all-to-all(bf16[4,64,1024]{2,1,0:T(8,128)(2,1)S(1)} %pad_maximum_fusion), channel_id=1, replica_groups=mesh['z'=4,'x'=2,'c'=2,'y'=2] {'x','y'}, dimensions={0} | all-to-all | bytes 1048576 | tf_op jit(solution)/shard_map/all_to_all | solution.py:50
  66.8 13.8 %all_to_all.66 = bf16[4,64,2048]{2,1,0:T(8,128)(2,1)} all-to-all(bf16[4,64,2048]{2,1,0:T(8,128)(2,1)S(1)} %bitcast.135), channel_id=1, replica_groups=mesh['z'=4,'x'=2,'c'=2,'y'=2] {'x','y'}, dimensions={0} | all-to-all | bytes 2097152 | tf_op jit(solution)/shard_map/all_to_all | solution.py:50
  83.3 17.0 %all_to_all.67 = bf16[8,64,1024]{2,1,0:T(8,128)(2,1)S(1)} all-to-all(bf16[8,64,1024]{2,1,0:T(8,128)(2,1)S(1)} %get-tuple-element.111), channel_id=1, replica_groups=mesh['z'=4,'x'=2,'c'=2,'y'=2] {'x','c','y'}, dimensions={0} | all-to-all | bytes 2097152 | tf_op jit(solution)/shard_map/all_to_all | solution.py:50
  100.5 13.5 %all_to_all.68 = bf16[4,16,1024]{2,1,0:T(8,128)(2,1)S(1)} all-to-all(bf16[4,16,1024]{2,1,0:T(8,128)(2,1)S(1)} %bitcast.149), channel_id=1, replica_groups=mesh['z'=4,'x'=2,'c'=2,'y'=2] {'z'}, dimensions={0} | all-to-all | bytes 262144 | tf_op jit(solution)/shard_map/all_to_all | solution.py:50
  114.1 8.3 %all_to_all.69 = bf16[4,16,1024]{2,1,0:T(8,128)(2,1)S(1)} all-to-all(bf16[4,16,1024]{2,1,0:T(8,128)(2,1)S(1)} %broadcast_in_dim.12), channel_id=1, replica_groups=mesh['z'=4,'x'=2,'c'=2,'y'=2] {'z'}, dimensions={0} | all-to-all | bytes 262144 | tf_op jit(solution)/shard_map/all_to_all | solution.py:50
  126.8 7.9 %qkv_mm.1 = (bf16[512,2048]{1,0:T(8,128)(2,1)}, bf16[512,1536]{1,0:T(8,128)(2,1)S(1)}) custom-call(bf16[128,2048]{1,0:T(8,128)(2,1)S(1)} %copy-done.68, bf16[128,2048]{1,0:T(8,128)(2,1)S(1)} %copy-done.62, bf16[128,2048]{1,0:T(8,128)(2,1)S(1)} %copy-done.60, bf16[64,2048]{1,0:T(8,128)(2,1)S(1)} %copy-done.72, bf16[64,2048]{1,0:T(8,128)(2,1)S(1)} %copy-done.74, ...), custom_call_target="tpu_custom_call" | custom-call | flops 3221225472 | bytes 10485760 | tf_op jit(solution)/shard_map/qkv_mm/pallas_call | solution.py:102
  137.1 18.0 %all_to_all.70 = bf16[4,64,2048]{2,1,0:T(8,128)(2,1)} all-to-all(bf16[4,64,2048]{2,1,0:T(8,128)(2,1)S(1)} %bitcast.134), channel_id=1, replica_groups=mesh['z'=4,'x'=2,'c'=2,'y'=2] {'x','y'}, dimensions={0} | all-to-all | bytes 2097152 | tf_op jit(solution)/shard_map/all_to_all | solution.py:50
  169.2 10.0 %collective-permute-done.11.refs_3_ = bf16[128,2048]{1,0:T(8,128)(2,1)S(1)} collective-permute-done((bf16[128,2048]{1,0:T(8,128)(2,1)S(1)}, bf16[128,2048]{1,0:T(8,128)(2,1)S(1)}, u32[]{:S(2)}, u32[]{:S(2)}) %collective-permute-start.11) | collective-permute-done | bytes 524320 | tf_op jit(solution)/shard_map/ppermute | solution.py:46
  183.6 9.1 %collective-permute-done.13.refs_2_ = bf16[128,2048]{1,0:T(8,128)(2,1)S(1)} collective-permute-done((bf16[128,2048]{1,0:T(8,128)(2,1)S(1)}, bf16[128,2048]{1,0:T(8,128)(2,1)S(1)}, u32[]{:S(2)}, u32[]{:S(2)}) %collective-permute-start.13) | collective-permute-done | bytes 524320 | tf_op jit(solution)/shard_map/ppermute | solution.py:46
  243.0 8.4 %collective-permute-done.21.refs_2_ = bf16[128,2048]{1,0:T(8,128)(2,1)S(1)} collective-permute-done((bf16[128,2048]{1,0:T(8,128)(2,1)S(1)}, bf16[128,2048]{1,0:T(8,128)(2,1)S(1)}, u32[]{:S(2)}, u32[]{:S(2)}) %collective-permute-start.21) | collective-permute-done | bytes 524320 | tf_op jit(solution)/shard_map/ppermute | solution.py:46
  271.4 11.9 %feed_up.1 = (bf16[512,2048]{1,0:T(8,128)(2,1)}, bf16[512,2048]{1,0:T(8,128)(2,1)}, f32[512,2048]{1,0:T(8,128)}) custom-call(bf16[128,2048]{1,0:T(8,128)(2,1)S(1)} %copy-done.70, bf16[128,2048]{1,0:T(8,128)(2,1)S(1)} %copy-done.66, bf16[128,2048]{1,0:T(8,128)(2,1)S(1)} %copy-done.64, bf16[64,2048]{1,0:T(8,128)(2,1)S(1)} %copy-done.76, ...), custom_call_target="tpu_custom_call" | custom-call | flops 4294967296 | bytes 12582912 | tf_op jit(solution)/shard_map/feed_up/pallas_call | solution.py:102
  302.7 8.7 %down_grads.1 = bf16[1024,2048]{1,0:T(8,128)(2,1)} custom-call(s32[1]{0:T(128)} %bitcast.28.r, bf16[512,2048]{1,0:T(8,128)(2,1)S(1)} %constant_dynamic-update-slice_fusion.refs_0_.dy, bf16[512,2048]{1,0:T(8,128)(2,1)S(1)} %collective-permute-done.28.refs_1_, bf16[512,2048]{1,0:T(8,128)(2,1)} %get-tuple-element.169.refs_2_, bf16[512,2048]{1,0:T(8,128)(2,1)} %copy-done.95), custom_call_target="tpu_custom_call" | custom-call | flops 4294967296 | bytes 16777216 | tf_op jit(solution)/shard_map/down_grads/pallas_call | solution.py:113
  313.1 14.4 %all-gather.11.cloned.1.call-done.down = bf16[2048,2048]{1,0:T(8,128)(2,1)} async-done(((bf16[256,2048]{1,0:T(8,128)(2,1)}), bf16[2048,2048]{1,0:T(8,128)(2,1)}) %all-gather.11.cloned.1.call-update) | async-done | bytes 8388624 | tf_op jit(solution)/shard_map/all_gather | solution.py:85
  329.0 9.9 %feed_down.1.refs_2_ = bf16[512,2048]{1,0:T(8,128)(2,1)S(1)} custom-call(bf16[512,2048]{1,0:T(8,128)(2,1)S(1)} %copy-done.18, f32[512,2048]{1,0:T(8,128)} %get-tuple-element.139.slope_ref, bf16[2048,2048]{1,0:T(8,128)(2,1)} %all-gather.11.cloned.1.call-done.down), custom_call_target="tpu_custom_call" | custom-call | flops 4294967296 | bytes 25165824 | tf_op jit(solution)/shard_map/feed_down/pallas_call | solution.py:102
  359.1 10.8 %collective-permute-done.38.refs_2_ = bf16[128,2048]{1,0:T(8,128)(2,1)S(1)} collective-permute-done((bf16[128,2048]{1,0:T(8,128)(2,1)S(1)}, bf16[128,2048]{1,0:T(8,128)(2,1)S(1)}, u32[]{:S(2)}, u32[]{:S(2)}) %collective-permute-start.38) | collective-permute-done | bytes 524320 | tf_op jit(solution)/shard_map/ppermute | solution.py:46
  377.2 9.2 %collective-permute-done.40.refs_2_ = bf16[128,2048]{1,0:T(8,128)(2,1)S(1)} collective-permute-done((bf16[128,2048]{1,0:T(8,128)(2,1)S(1)}, bf16[128,2048]{1,0:T(8,128)(2,1)S(1)}, u32[]{:S(2)}, u32[]{:S(2)}) %collective-permute-start.40) | collective-permute-done | bytes 524320 | tf_op jit(solution)/shard_map/ppermute | solution.py:46
  392.2 8.8 %up_grads.1 = bf16[1024,2048]{1,0:T(8,128)(2,1)} custom-call(s32[1]{0:T(128)} %bitcast.28.r, bf16[512,2048]{1,0:T(8,128)(2,1)} %get-tuple-element.143.refs_0_, bf16[512,2048]{1,0:T(8,128)(2,1)} %collective-permute-done.34.refs_1_, bf16[512,2048]{1,0:T(8,128)(2,1)} %copy-done.26, bf16[512,2048]{1,0:T(8,128)(2,1)} %collective-permute-done.43.refs_3_), custom_call_target="tpu_custom_call" | custom-call | flops 4294967296 | bytes 16777216 | tf_op jit(solution)/shard_map/up_grads/pallas_call | solution.py:113
  439.5 11.6 %collective-permute-done.49.refs_2_ = bf16[128,2048]{1,0:T(8,128)(2,1)S(1)} collective-permute-done((bf16[128,2048]{1,0:T(8,128)(2,1)S(1)}, bf16[128,2048]{1,0:T(8,128)(2,1)S(1)}, u32[]{:S(2)}, u32[]{:S(2)}) %collective-permute-start.49) | collective-permute-done | bytes 524320 | tf_op jit(solution)/shard_map/ppermute | solution.py:46
  473.0 11.6 %attention_grads.1 = bf16[1024,3072]{1,0:T(8,128)(2,1)} custom-call(s32[1]{0:T(128)} %bitcast.28.r, bf16[512,2048]{1,0:T(8,128)(2,1)} %get-tuple-element.159.refs_0_, bf16[512,2048]{1,0:T(8,128)(2,1)} %collective-permute-done.30.refs_1_, bf16[512,2048]{1,0:T(8,128)(2,1)} %copy-done.27, bf16[512,2048]{1,0:T(8,128)(2,1)} %copy-done.83, ...), custom_call_target="tpu_custom_call" | custom-call | flops 6442450944 | bytes 25165824 | tf_op jit(solution)/shard_map/attention_grads/pallas_call | solution.py:113
  524.3 10.7 %all-to-all-done.7 = bf16[4,16,1024]{2,1,0:T(8,128)(2,1)S(1)} async-done(((bf16[4,16,1024]{2,1,0:T(8,128)(2,1)}), bf16[4,16,1024]{2,1,0:T(8,128)(2,1)S(1)}, u32[]{:S(2)}, u32[]{:S(2)}) %all-to-all-start.7) | async-done | bytes 131104 | tf_op jit(solution)/shard_map/all_to_all | solution.py:50
  542.8 11.3 %fusion.28 = (bf16[512,2048]{1,0:T(8,128)(2,1)}, f32[512,2048]{1,0:T(8,128)}) fusion(bf16[512,2048]{1,0:T(8,128)(2,1)} %get-tuple-element.169.refs_2_, bf16[2048,2048]{1,0:T(8,128)(2,1)} %all-gather.11.cloned.1.call-done.down), kind=kOutput, calls=%fused_computation.99 | convolution fusion | flops 4296015872 | bytes 16777216 | tf_op jit(solution)/shard_map/dot_general | solution.py:26
  575.3 18.1 %collective-permute-done.56 = bf16[64,2048]{1,0:T(8,128)(2,1)S(1)} collective-permute-done((bf16[64,2048]{1,0:T(8,128)(2,1)S(1)}, bf16[64,2048]{1,0:T(8,128)(2,1)S(1)}, u32[]{:S(2)}, u32[]{:S(2)}) %collective-permute-start.56) | collective-permute-done | bytes 262176 | tf_op jit(solution)/shard_map/ppermute | solution.py:46
  646.9 8.6 %collective-permute-done.72.refs_3_ = bf16[64,3072]{1,0:T(8,128)(2,1)} collective-permute-done((bf16[64,3072]{1,0:T(8,128)(2,1)}, bf16[64,3072]{1,0:T(8,128)(2,1)}, u32[]{:S(2)}, u32[]{:S(2)}) %collective-permute-start.72) | collective-permute-done | bytes 393248 | tf_op jit(solution)/shard_map/ppermute | solution.py:80
  (493 shorter events, 382.2 us)
Async XLA Ops:
  7.2 116.6 %all-gather.5.cloned.1.call-start = ((), (), s32[]{:S(2)}) async-start(), calls=%async_computation.16 | async-start | bytes 9437184 | tf_op jit(solution)/shard_map/all_gather | solution.py:85
  29.4 167.4 %all-gather.7.cloned.1.call-start = ((), (), s32[]{:S(2)}) async-start(), calls=%async_computation.17 | async-start | bytes 4718592 | tf_op jit(solution)/shard_map/all_gather | solution.py:85
  66.7 199.7 %all-gather.9.cloned.1.call-start = ((), (), s32[]{:S(2)}) async-start(), calls=%async_computation.18 | async-start | bytes 9437184 | tf_op jit(solution)/shard_map/all_gather | solution.py:85
  80.6 246.8 %all-gather.11.cloned.1.call-start = ((), (), s32[]{:S(2)}) async-start(), calls=%async_computation.19 | async-start | bytes 9437184 | tf_op jit(solution)/shard_map/all_gather | solution.py:85
  155.1 258.1 %reduce-scatter.4.cloned.1.call-start = ((), (), s32[]{:S(2)}) async-start(), calls=%async_computation.20 | async-start | bytes 5242880 | tf_op jit(solution)/shard_map/reduce_scatter | solution.py:89
  264.6 22.0 %collective-permute-start.24 = (bf16[128,2048]{1,0:T(8,128)(2,1)}, bf16[128,2048]{1,0:T(8,128)(2,1)}, u32[]{:S(2)}, u32[]{:S(2)}) collective-permute-start(bf16[128,2048]{1,0:T(8,128)(2,1)} %get-tuple-element.127.refs_3_), channel_id=1, source_target_pairs={{0,1},{1,0},{2,3},{3,2},{4,5},{5,4},{6,7},{7,6},{8,9},{9,8},{10,11... | collective-permute-start | bytes 1572872 | tf_op jit(solution)/shard_map/ppermute | solution.py:46
  265.1 19.4 %collective-permute-start.25 = (bf16[128,2048]{1,0:T(8,128)(2,1)}, bf16[128,2048]{1,0:T(8,128)(2,1)}, u32[]{:S(2)}, u32[]{:S(2)}) collective-permute-start(bf16[128,2048]{1,0:T(8,128)(2,1)} %get-tuple-element.127.refs_3_), channel_id=1, source_target_pairs={{0,4},{4,0},{1,5},{5,1},{2,6},{6,2},{3,7},{7,3},{8,12},{12,8},{9,1... | collective-permute-start | bytes 1572872 | tf_op jit(solution)/shard_map/ppermute | solution.py:46
  312.8 174.2 %reduce-scatter.6.cloned.1.call-start = ((), (), s32[]{:S(2)}) async-start(), calls=%async_computation.21 | async-start | bytes 5242880 | tf_op jit(solution)/shard_map/reduce_scatter | solution.py:89
  349.9 42.2 %collective-permute-start.43 = (bf16[512,2048]{1,0:T(8,128)(2,1)S(1)}, bf16[512,2048]{1,0:T(8,128)(2,1)}, u32[]{:S(2)}, u32[]{:S(2)}) collective-permute-start(bf16[512,2048]{1,0:T(8,128)(2,1)S(1)} %feed_down.1.refs_2_), channel_id=1, source_target_pairs={{0,2},{2,0},{1,3},{3,1},{4,6},{6,4},{5,7},{7,5},{8,10},{10,8},{9,1... | collective-permute-start | bytes 6291464 | tf_op jit(solution)/shard_map/ppermute | solution.py:46
  413.2 210.9 %reduce-scatter.8.cloned.1.call-start = ((), (), s32[]{:S(2)}) async-start(), calls=%async_computation.22 | async-start | bytes 7864320 | tf_op jit(solution)/shard_map/reduce_scatter | solution.py:89
  510.1 24.9 %collective-permute-start.65 = (bf16[64,4096]{1,0:T(8,128)(2,1)}, bf16[64,4096]{1,0:T(8,128)(2,1)S(1)}, u32[]{:S(2)}, u32[]{:S(2)}) collective-permute-start(bf16[64,4096]{1,0:T(8,128)(2,1)} %get-tuple-element.250), channel_id=1, source_target_pairs={{0,1},{1,0},{2,3},{3,2},{4,5},{5,4},{6,7},{7,6},{8,9},{9,8},{10,11... | collective-permute-start | bytes 1572872 | tf_op jit(solution)/shard_map/ppermute | solution.py:46
  510.6 24.4 %collective-permute-start.66 = (bf16[64,4096]{1,0:T(8,128)(2,1)}, bf16[64,4096]{1,0:T(8,128)(2,1)S(1)}, u32[]{:S(2)}, u32[]{:S(2)}) collective-permute-start(bf16[64,4096]{1,0:T(8,128)(2,1)} %get-tuple-element.249), channel_id=1, source_target_pairs={{0,4},{4,0},{1,5},{5,1},{2,6},{6,2},{3,7},{7,3},{8,12},{12,8},{9,1... | collective-permute-start | bytes 1572872 | tf_op jit(solution)/shard_map/ppermute | solution.py:46
  511.1 26.8 %collective-permute-start.67 = (bf16[64,4096]{1,0:T(8,128)(2,1)}, bf16[64,4096]{1,0:T(8,128)(2,1)S(1)}, u32[]{:S(2)}, u32[]{:S(2)}) collective-permute-start(bf16[64,4096]{1,0:T(8,128)(2,1)} %get-tuple-element.248), channel_id=1, source_target_pairs={{0,5},{1,4},{4,1},{5,0},{2,7},{3,6},{6,3},{7,2},{8,13},{9,12},{12,... | collective-permute-start | bytes 1572872 | tf_op jit(solution)/shard_map/ppermute | solution.py:80
  515.8 39.8 %collective-permute-start.63 = (bf16[128,2048]{1,0:T(8,128)(2,1)}, bf16[128,2048]{1,0:T(8,128)(2,1)S(1)}, u32[]{:S(2)}, u32[]{:S(2)}) collective-permute-start(bf16[128,2048]{1,0:T(8,128)(2,1)} %pad_maximum_fusion.12), channel_id=1, source_target_pairs={{0,1},{1,0},{2,3},{3,2},{4,5},{5,4},{6,7},{7,6},{8,9},{9,8},{10,11... | collective-permute-start | bytes 1572872 | tf_op jit(solution)/shard_map/ppermute | solution.py:46
  523.9 32.5 %collective-permute-start.61 = (bf16[128,2048]{1,0:T(8,128)(2,1)}, bf16[128,2048]{1,0:T(8,128)(2,1)S(1)}, u32[]{:S(2)}, u32[]{:S(2)}) collective-permute-start(bf16[128,2048]{1,0:T(8,128)(2,1)} %pad_maximum_fusion.11), channel_id=1, source_target_pairs={{0,4},{4,0},{1,5},{5,1},{2,6},{6,2},{3,7},{7,3},{8,12},{12,8},{9,1... | collective-permute-start | bytes 1572872 | tf_op jit(solution)/shard_map/ppermute | solution.py:46
  539.1 22.8 %all-to-all-start.8 = ((bf16[8,64,1024]{2,1,0:T(8,128)(2,1)}), bf16[8,64,1024]{2,1,0:T(8,128)(2,1)S(1)}, u32[]{:S(2)}, u32[]{:S(2)}) async-start(bf16[8,64,1024]{2,1,0:T(8,128)(2,1)} %broadcast_in_dim.14), calls=%async_computation.10 | async-start | bytes 2097152 | tf_op jit(solution)/shard_map/all_to_all | solution.py:50
  566.3 28.3 %all-to-all-start.9 = ((bf16[8,80,1024]{2,1,0:T(8,128)(2,1)}), bf16[8,80,1024]{2,1,0:T(8,128)(2,1)S(1)}, u32[]{:S(2)}, u32[]{:S(2)}) async-start(bf16[8,80,1024]{2,1,0:T(8,128)(2,1)} %copy-done.28), calls=%async_computation.11 | async-start | bytes 2621440 | tf_op jit(solution)/shard_map/all_to_all | solution.py:50
  571.7 21.6 %collective-permute-start.56 = (bf16[64,2048]{1,0:T(8,128)(2,1)S(1)}, bf16[64,2048]{1,0:T(8,128)(2,1)S(1)}, u32[]{:S(2)}, u32[]{:S(2)}) collective-permute-start(bf16[64,2048]{1,0:T(8,128)(2,1)S(1)} %get-tuple-element.261), channel_id=1, source_target_pairs={{0,1},{1,0},{2,3},{3,2},{4,5},{5,4},{6,7},{7,6},{8,9},{9,8},{10,11... | collective-permute-start | bytes 786440 | tf_op jit(solution)/shard_map/ppermute | solution.py:46
  573.8 19.6 %collective-permute-start.58 = (bf16[64,2048]{1,0:T(8,128)(2,1)S(1)}, bf16[64,2048]{1,0:T(8,128)(2,1)S(1)}, u32[]{:S(2)}, u32[]{:S(2)}) collective-permute-start(bf16[64,2048]{1,0:T(8,128)(2,1)S(1)} %get-tuple-element.259), channel_id=1, source_target_pairs={{0,4},{4,0},{1,5},{5,1},{2,6},{6,2},{3,7},{7,3},{8,12},{12,8},{9,1... | collective-permute-start | bytes 786440 | tf_op jit(solution)/shard_map/ppermute | solution.py:46
  601.3 28.9 %collective-permute-start.59 = (bf16[128,2048]{1,0:T(8,128)(2,1)}, bf16[128,2048]{1,0:T(8,128)(2,1)S(1)}, u32[]{:S(2)}, u32[]{:S(2)}) collective-permute-start(bf16[128,2048]{1,0:T(8,128)(2,1)} %pad_maximum_fusion.10), channel_id=1, source_target_pairs={{0,1},{1,0},{2,3},{3,2},{4,5},{5,4},{6,7},{7,6},{8,9},{9,8},{10,11... | collective-permute-start | bytes 1572872 | tf_op jit(solution)/shard_map/ppermute | solution.py:46
  613.1 19.2 %collective-permute-start.57 = (bf16[128,2048]{1,0:T(8,128)(2,1)}, bf16[128,2048]{1,0:T(8,128)(2,1)S(1)}, u32[]{:S(2)}, u32[]{:S(2)}) collective-permute-start(bf16[128,2048]{1,0:T(8,128)(2,1)} %pad_maximum_fusion.9), channel_id=1, source_target_pairs={{0,4},{4,0},{1,5},{5,1},{2,6},{6,2},{3,7},{7,3},{8,12},{12,8},{9,1... | collective-permute-start | bytes 1572872 | tf_op jit(solution)/shard_map/ppermute | solution.py:46
  619.2 19.2 %all-to-all-start.12 = ((bf16[8,64,1024]{2,1,0:T(8,128)(2,1)}), bf16[8,64,1024]{2,1,0:T(8,128)(2,1)S(1)}, u32[]{:S(2)}, u32[]{:S(2)}) async-start(bf16[8,64,1024]{2,1,0:T(8,128)(2,1)} %broadcast_in_dim.17), calls=%async_computation.14 | async-start | bytes 2097152 | tf_op jit(solution)/shard_map/all_to_all | solution.py:50
  626.7 19.1 %collective-permute-start.70 = (bf16[64,3072]{1,0:T(8,128)(2,1)}, bf16[64,3072]{1,0:T(8,128)(2,1)S(1)}, u32[]{:S(2)}, u32[]{:S(2)}) collective-permute-start(bf16[64,3072]{1,0:T(8,128)(2,1)} %get-tuple-element.290), channel_id=1, source_target_pairs={{0,1},{1,0},{2,3},{3,2},{4,5},{5,4},{6,7},{7,6},{8,9},{9,8},{10,11... | collective-permute-start | bytes 1179656 | tf_op jit(solution)/shard_map/ppermute | solution.py:46
  630.1 25.4 %collective-permute-start.72 = (bf16[64,3072]{1,0:T(8,128)(2,1)}, bf16[64,3072]{1,0:T(8,128)(2,1)}, u32[]{:S(2)}, u32[]{:S(2)}) collective-permute-start(bf16[64,3072]{1,0:T(8,128)(2,1)} %get-tuple-element.288), channel_id=1, source_target_pairs={{0,5},{1,4},{4,1},{5,0},{2,7},{3,6},{6,3},{7,2},{8,13},{9,12},{12,... | collective-permute-start | bytes 1179656 | tf_op jit(solution)/shard_map/ppermute | solution.py:80
  (160 other events, 1291.5 us)
Sparse Core Ops, SparseCore 0:
  29.5 86.2 all-gather.4
  117.4 45.5 all-gather.6
  164.6 80.7 all-gather.8
  246.8 80.5 all-gather.10
  329.6 75.2 reduce-scatter.3
  413.4 73.5 reduce-scatter.5
  489.2 115.6 reduce-scatter.7

commit v12 on v11

--- a/solution.py
+++ b/solution.py
@@ -71,8 +71,7 @@
     return [own, from_x, from_y]
 
 
-def swap_blocks(blocks, rank):
-    parts = [lax.dynamic_index_in_dim(blocks, rank ^ k, 0, keepdims=False) for k in range(4)]
+def swap_parts(parts):
     return [
         parts[0],
         swap(parts[1], "y"),
@@ -135,7 +134,7 @@
         copy.wait()
 
 
-ANY = pl.BlockSpec(memory_space=pltpu.MemorySpace.HBM)
+ANY = pl.BlockSpec(memory_space=pl.ANY)
 
 
 def gather_mm(pieces, weight, first, columns, name):
@@ -169,12 +168,10 @@
 
 
 def mm_scatter(values, weight):
-    partial = mm_t(values, weight)
+    partial = mm_t(values, weight).astype(BF)
     rows = partial.shape[0] // 4
-    low = partial[rows:].astype(BF)
-    half = rows // 2
-    cuts = [low[:rows], low[rows : 2 * rows], low[2 * rows : 2 * rows + half], low[2 * rows + half :]]
-    return scatter_tokens([partial[:rows], *cuts])
+    cuts = [0, rows, 2 * rows, 3 * rows, 3 * rows + rows // 2, 4 * rows]
+    return scatter_tokens([partial[a:b] for a, b in zip(cuts, cuts[1:])])
 
 
 def normalize(values):
@@ -555,6 +552,62 @@
     )
 
 
+def pick_weights(three, one, rank):
+    rows, width = one.shape[0], one.shape[1] // 4
+
+    def kernel(r, three_ref, one_ref, *outs):
+        for k in range(4):
+
+            @pl.when(pl.program_id(0) == k)
+            def _():
+                for j in range(3):
+                    outs[k][:, j * width : (j + 1) * width] = three_ref[j]
+                outs[k][:, 3 * width :] = one_ref[...]
+
+    outs = [shape((rows, 4 * width))] * 4
+    return call(
+        kernel,
+        (4,),
+        [
+            pl.BlockSpec((3, rows, width), lambda k, r: (0, 0, k ^ r[0])),
+            pl.BlockSpec((rows, width), lambda k, r: (0, k ^ r[0])),
+        ],
+        [whole(a) for a in outs],
+        outs,
+        [three, one],
+        "pick_weights",
+        rank=rank,
+    )
+
+
+def pick_rows(arrays, rank):
+    rows = arrays[0].shape[1]
+    widths = [a.shape[2] for a in arrays]
+    count = len(arrays)
+
+    def kernel(r, *refs):
+        for k in range(4):
+
+            @pl.when(pl.program_id(0) == k)
+            def _():
+                at = 0
+                for ref, width in zip(refs, widths):
+                    refs[count + k][:, at : at + width] = ref[0]
+                    at += width
+
+    outs = [shape((rows, sum(widths)))] * 4
+    return call(
+        kernel,
+        (4,),
+        [pl.BlockSpec((1, rows, w), lambda k, r: (k ^ r[0], 0, 0)) for w in widths],
+        [whole(a) for a in outs],
+        outs,
+        arrays,
+        "pick_rows",
+        rank=rank,
+    )
+
+
 def place(parts, rank):
     def kernel(r, *refs):
         for k in range(4):
@@ -615,15 +668,15 @@
                     return refs[k][:, j * width : (j + 1) * width].astype(F32)
 
                 for j in range(3):
-                    three[:, j, :] = part(j)
+                    three[j] = part(j)
                 out[...] = part(3)
-                cross[:, 0, :] = part(4)
+                cross[0] = part(4)
                 cross_out[...] = part(5)
 
-        cross[:, 1, :] = key[...]
-        cross[:, 2, :] = value[...]
-
-    wide = pl.BlockSpec((rows, 3, width), lambda k, r: (0, 0, k ^ r[0]))
+        cross[1] = key[...]
+        cross[2] = value[...]
+
+    wide = pl.BlockSpec((3, rows, width), lambda k, r: (0, 0, k ^ r[0]))
     flat = pl.BlockSpec((rows, width), lambda k, r: (0, k ^ r[0]))
     return call(
         kernel,
@@ -631,7 +684,7 @@
         [whole(p) for p in parts]
         + [flat, pl.BlockSpec((rows, width), lambda k, r: (0, 4 + (k ^ r[0])))],
         [wide, flat, wide, flat],
-        [shape((rows, 3, 4 * width), F32), shape((rows, 4 * width), F32)] * 2,
+        [shape((3, rows, 4 * width), F32), shape((rows, 4 * width), F32)] * 2,
         [*parts, text_grad, text_grad],
         "finish_all",
         rank=rank,
@@ -642,42 +695,41 @@
     return (k >> 1) & 1, (k >> 2) * 2 + (k & 1)
 
 
-def text_forward(caption, w_text, kv_rows):
+def text_forward(caption, w_text, w_cross):
     context, rows = caption.shape[0], w_text.shape[0]
-    half, width = context // 2, kv_rows.shape[1] // 8
-
-    def kernel(cap, weight, kv, own, blocks):
+    half, width = context // 2, w_cross.shape[2] // 4
+
+    def kernel(cap, weight, cross, own, blocks):
         own[...] = mm_t(cap[...], weight[...]).astype(BF)
-        part = mm(own[...], kv[...]).astype(BF)
-        for k in range(8):
-            core, group = plane_block(k)
-            for j in range(2):
-                at = (4 * j + group) * width
+        for j in range(2):
+            part = mm(own[...], cross[1 + j]).astype(BF)
+            for k in range(8):
+                core, group = plane_block(k)
                 blocks[k, :, j * width : (j + 1) * width] = part[
-                    core * half : (core + 1) * half, at : at + width
+                    core * half : (core + 1) * half, group * width : (group + 1) * width
                 ]
 
     return call(
         kernel,
         (1,),
-        [whole(caption), whole(w_text), whole(kv_rows)],
+        [whole(caption), whole(w_text), whole(w_cross)],
         [
             pl.BlockSpec((context, rows), lambda i: (0, 0)),
             pl.BlockSpec((8, half, 2 * width), lambda i: (0, 0, 0)),
         ],
         [shape((context, rows)), shape((8, half, 2 * width))],
-        [caption, w_text, kv_rows],
+        [caption, w_text, w_cross],
         "text_forward",
     )
 
 
-def text_back(blocks, own_text, kv_rows, caption, w_text, extra):
+def text_back(blocks, own_text, w_cross, caption, w_text, extra):
     context, rows = own_text.shape
-    half, width = context // 2, kv_rows.shape[1] // 8
+    half, width = context // 2, w_cross.shape[2] // 4
     wide = caption.shape[1] // 4
     tail = extra.shape[0]
 
-    def kernel(block, own, kv, cap, weight, more, kv_grad, text_grad, out, grads):
+    def kernel(block, own, cross, cap, weight, more, kv_grad, text_grad, out, grads):
         for k in range(8):
             core, group = plane_block(k)
             for j in range(2):
@@ -686,7 +738,9 @@
                     k, :, j * width : (j + 1) * width
                 ]
         kv_grad[...] = t_mm(own[...], grads[...])
-        grad_text = mm_t(grads[...], kv[...]).astype(BF)
+        grad_text = sum(
+            mm_t(grads[:, 4 * j * width : 4 * (j + 1) * width], cross[1 + j]) for j in range(2)
+        ).astype(BF)
         text_grad[...] = t_mm(grad_text, cap[...])
         part = mm(grad_text, weight[...]).astype(BF)
         for k in range(8):
@@ -694,7 +748,7 @@
             out[k, :half, :] = part[core * half : (core + 1) * half, group * wide : (group + 1) * wide]
             out[k, half:, :] = more[...]
 
-    operands = [blocks, own_text, kv_rows, caption, w_text, extra]
+    operands = [blocks, own_text, w_cross, caption, w_text, extra]
     outs = [
         shape((rows, 8 * width), F32),
         shape((rows, 4 * wide), F32),
@@ -782,7 +836,6 @@
     ):
         images, local_rows, width = hidden.shape
         full_length = mask_index.shape[1]
-        shard_rows = w_qkv.shape[0]
         rank = lax.axis_index("x") * 2 + lax.axis_index("y")
         core = lax.axis_index("c")
         tokens = images * local_rows
@@ -796,16 +849,10 @@
         def outer(values):
             return values if inside else layer_order(values)
 
-        first = jnp.concatenate(
-            [
-                w_qkv.reshape(shard_rows, 3, 4, group)
-                .transpose(2, 0, 1, 3)
-                .reshape(4, shard_rows, 3 * group),
-                column_blocks(w_out, 4),
-            ],
-            axis=2,
-        )
-        first = gather_rows(place(swap_blocks(first, rank), rank))
+        w_qkv, w_cross = w_qkv.transpose(1, 0, 2), w_cross.transpose(1, 0, 2)
+        first = swap_parts(pick_weights(w_qkv, w_out, rank))
+        first = gather_rows(place(first, rank))
+
         positions = lax.axis_index("y") * local_rows + jnp.arange(local_rows, dtype=jnp.int32)
         ranks = jnp.arange(full_length, dtype=jnp.int32)
         matches = (mask_index[:, :, None] == positions[None, None, :]) & (
@@ -824,13 +871,12 @@
             order,
         )
         attn_in = gather_tokens(attn_in)
-        mid = jnp.concatenate([column_blocks(w_cross[:, 0], 4), column_blocks(w_cross_out, 4)], axis=2)
+        mid = jnp.concatenate([column_blocks(w_cross[0], 4), column_blocks(w_cross_out, 4)], axis=2)
         up = column_blocks(w_up, 4)
         attn_in, mid, up = lax.optimization_barrier((attn_in, mid, up))
         mid, up = gather_rows(trade(mid)), gather_rows(trade(up))
 
-        kv_rows = w_cross[:, 1:].reshape(shard_rows, 2 * width)
-        own_text, kv_part = text_forward(caption, w_text, kv_rows)
+        own_text, kv_part = text_forward(caption, w_text, w_cross)
         text_kv = trade(kv_part, PLANE).astype(F32).sum(axis=0).astype(BF)
         text_kv = sum_z(text_kv)
         other = swap(text_kv, "c")
@@ -933,22 +979,22 @@
         kv_keep = lax.dynamic_index_in_dim(kv_halves, core, 0, keepdims=False)
         kv_send = lax.dynamic_index_in_dim(kv_halves, 1 - core, 0, keepdims=False)
         kv_sum = sum_z((kv_keep + swap(kv_send, "c")).astype(BF))
-        wide_rows = jnp.concatenate([down_rows, up_rows], axis=2)
-        wide_rows = swap_blocks(wide_rows, rank)
+        wide_rows = swap_parts(pick_rows([down_rows, up_rows], rank))
         kv_sum, wide_rows = lax.optimization_barrier((kv_sum, wide_rows))
         kv_grads = spread(kv_sum, PLANE, 8)
         down_grad, up_grad = finish_wide(wide_rows, rank)
         kv_weight_grad, grad_text_w, caption_part = text_back(
-            kv_grads, own_text, kv_rows, caption, w_text, halves_of(sums, text_width // 4)
+            kv_grads, own_text, w_cross, caption, w_text, halves_of(sums, text_width // 4)
         )
         half_context = caption.shape[0] // 2
         caption_part = trade(caption_part, PLANE).astype(F32).sum(axis=0)
         sums = layer_order(add_z(whole_of(caption_part[half_context:], width)))
         caption_part = sum_z(caption_part[:half_context].astype(BF))
+        caption_part, rest_rows = lax.optimization_barrier((caption_part, rest_rows))
         grad_caption = caption_output(spread(caption_part, PLANE, 8))
 
         qkv_grad, out_grad, grad_cross, cross_out_grad = finish_all(
-            swap_blocks(rest_rows, rank), kv_weight_grad, rank
+            swap_parts(pick_rows([rest_rows], rank)), kv_weight_grad, rank
         )
         return (
             outer(output).reshape(hidden.shape),
@@ -956,9 +1002,9 @@
             grad_caption,
             sums[:3],
             sums[3],
-            qkv_grad,
+            qkv_grad.transpose(1, 0, 2),
             out_grad,
-            grad_cross,
+            grad_cross.transpose(1, 0, 2),
             cross_out_grad,
             grad_text_w,
             up_grad,

time: 679 us -> 678 us (level)
  waiting for transfers between devices: 237 us -> 224 us
  blocking collectives: 80.9 us -> 93.3 us
  local copies, waits for them, and re-layouts: 82.4 us -> 72.1 us
  Pallas kernels: 108 us -> 115 us
    ppermute x68, waiting for transfers between devices: 185 us -> 169 us  [swap(): return lax.ppermute(values, axis, PAIR)]
    all_to_all x6 -> x7, blocking collectives: 80.9 us -> 93.3 us  [trade(): return lax.all_to_all(blocks, axes, 0, 0, tiled=True)]
    unnamed x200 -> x184, local copies, waits for them, and re-layouts: 52.6 us -> 46.6 us
    all_to_all x7 -> x6, waiting for transfers between devices: 20.9 us -> 26.5 us  [trade(): return lax.all_to_all(blocks, axes, 0, 0, tiled=True)]
    all_to_all x7 -> x6, starting transfers between devices: 28.8 us -> 24.5 us  [trade(): return lax.all_to_all(blocks, axes, 0, 0, tiled=True)]
    pallas_call x6 -> x9, Pallas kernels: 36.7 us -> 40.1 us  [call(): pl.pallas_call(kernel, grid_spec=spec, **options)]
  transfers between devices with their start and end apart: 87 -> 86, of which waited for: 49 -> 50; matrix products, arithmetic and copies ran while one was open for 11% -> 11% of each run, Pallas kernels for 15% -> 17%
where the time goes in v12:
time: 678 us; the launch traced here: 670 us
  waiting for transfers between devices  224 us (33%)
  Pallas kernels  115 us (17%)
  starting transfers between devices  104 us (15%)
  blocking collectives  93.3 us (14%)
  local copies, waits for them, and re-layouts  72.1 us (11%)
  matrix products  31.3 us (5%)
  between operations  16.4 us (2%)
  other arithmetic  13.5 us (2%)
    ppermute x68, waiting for transfers between devices, swap(): return lax.ppermute(values, axis, PAIR)  169 us
    all_to_all x7, blocking collectives, trade(): return lax.all_to_all(blocks, axes, 0, 0, tiled=True)  93.3 us
    pallas_call x20, Pallas kernels, call(): pl.pallas_call(kernel, grid=grid, in_specs=in_specs, out_specs=out_specs,...  75.3 us
    ppermute x68, starting transfers between devices, swap(): return lax.ppermute(values, axis, PAIR)  70.4 us
    unnamed x184, local copies, waits for them, and re-layouts  46.6 us
    pallas_call x9, Pallas kernels, call(): pl.pallas_call(kernel, grid_spec=spec, **options)  40.1 us
    dot_general x6, matrix products, dot(): return lax.dot_general(a, b, (dims, ((), ())), preferred_element_type=F32)  31.3 us
    all_to_all x6, waiting for transfers between devices, trade(): return lax.all_to_all(blocks, axes, 0, 0, tiled=True)  26.5 us
  transfers between devices with their start and end apart: 86, of which 50 were waited for; matrix products, arithmetic and copies ran while one was open for 11% of the time, Pallas kernels for 17%

profile of v12, /device:TPU:0, one launch (start us, length us, event | category | flops | bytes accessed | tf_op | source)
XLA Modules:
  0.0 669.8 jit_solution(163781377330917230)
XLA Ops:
  34.6 8.8 %collective-permute-done.1.refs_2_ = bf16[128,2048]{1,0:T(8,128)(2,1)S(1)} collective-permute-done((bf16[128,2048]{1,0:T(8,128)(2,1)S(1)}, bf16[128,2048]{1,0:T(8,128)(2,1)S(1)}, u32[]{:S(2)}, u32[]{:S(2)}) %collective-permute-start.1) | collective-permute-done | bytes 524320 | tf_op jit(solution)/shard_map/ppermute | solution.py:46
  55.0 10.2 %all_to_all.65 = bf16[4,64,1024]{2,1,0:T(8,128)(2,1)} all-to-all(bf16[4,64,1024]{2,1,0:T(8,128)(2,1)S(1)} %copy.71), channel_id=1, replica_groups=mesh['z'=4,'x'=2,'c'=2,'y'=2] {'x','y'}, dimensions={0} | all-to-all | bytes 1048576 | tf_op jit(solution)/shard_map/all_to_all | solution.py:50
  65.2 15.5 %all_to_all.66 = bf16[4,64,2048]{2,1,0:T(8,128)(2,1)} all-to-all(bf16[4,64,2048]{2,1,0:T(8,128)(2,1)} %bitcast.94), channel_id=1, replica_groups=mesh['z'=4,'x'=2,'c'=2,'y'=2] {'x','y'}, dimensions={0} | all-to-all | bytes 2097152 | tf_op jit(solution)/shard_map/all_to_all | solution.py:50
  83.4 16.9 %all_to_all.67 = bf16[8,64,1024]{2,1,0:T(8,128)(2,1)S(1)} all-to-all(bf16[8,64,1024]{2,1,0:T(8,128)(2,1)S(1)} %get-tuple-element.125), channel_id=1, replica_groups=mesh['z'=4,'x'=2,'c'=2,'y'=2] {'x','c','y'}, dimensions={0} | all-to-all | bytes 2097152 | tf_op jit(solution)/shard_map/all_to_all | solution.py:50
  100.4 11.5 %all_to_all.68 = bf16[4,16,1024]{2,1,0:T(8,128)(2,1)S(1)} all-to-all(bf16[4,16,1024]{2,1,0:T(8,128)(2,1)S(1)} %bitcast.103), channel_id=1, replica_groups=mesh['z'=4,'x'=2,'c'=2,'y'=2] {'z'}, dimensions={0} | all-to-all | bytes 262144 | tf_op jit(solution)/shard_map/all_to_all | solution.py:50
  112.0 8.8 %all_to_all.69 = bf16[4,16,1024]{2,1,0:T(8,128)(2,1)S(1)} all-to-all(bf16[4,16,1024]{2,1,0:T(8,128)(2,1)S(1)} %broadcast_in_dim.10), channel_id=1, replica_groups=mesh['z'=4,'x'=2,'c'=2,'y'=2] {'z'}, dimensions={0} | all-to-all | bytes 262144 | tf_op jit(solution)/shard_map/all_to_all | solution.py:50
  127.2 7.9 %qkv_mm.1 = (bf16[512,2048]{1,0:T(8,128)(2,1)}, bf16[512,1536]{1,0:T(8,128)(2,1)S(1)}) custom-call(bf16[128,2048]{1,0:T(8,128)(2,1)S(1)} %copy-done.62, bf16[128,2048]{1,0:T(8,128)(2,1)S(1)} %copy-done.56, bf16[128,2048]{1,0:T(8,128)(2,1)S(1)} %collective-permute-done.1.refs_2_, bf16[64,2048]{1,0:T(8,128)(2,1)S(1)} %copy-done.66, ...), custom_call_target="tpu_custom_call" | custom-call | flops 3221225472 | bytes 10485760 | tf_op jit(solution)/shard_map/qkv_mm/pallas_call | solution.py:101
  138.1 18.2 %all_to_all.70 = bf16[4,64,2048]{2,1,0:T(8,128)(2,1)} all-to-all(bf16[4,64,2048]{2,1,0:T(8,128)(2,1)S(1)} %bitcast.93), channel_id=1, replica_groups=mesh['z'=4,'x'=2,'c'=2,'y'=2] {'x','y'}, dimensions={0} | all-to-all | bytes 2097152 | tf_op jit(solution)/shard_map/all_to_all | solution.py:50
  170.8 10.0 %collective-permute-done.11.refs_3_ = bf16[128,2048]{1,0:T(8,128)(2,1)S(1)} collective-permute-done((bf16[128,2048]{1,0:T(8,128)(2,1)S(1)}, bf16[128,2048]{1,0:T(8,128)(2,1)S(1)}, u32[]{:S(2)}, u32[]{:S(2)}) %collective-permute-start.11) | collective-permute-done | bytes 524320 | tf_op jit(solution)/shard_map/ppermute | solution.py:46
  185.2 9.2 %collective-permute-done.13.refs_2_ = bf16[128,2048]{1,0:T(8,128)(2,1)S(1)} collective-permute-done((bf16[128,2048]{1,0:T(8,128)(2,1)S(1)}, bf16[128,2048]{1,0:T(8,128)(2,1)S(1)}, u32[]{:S(2)}, u32[]{:S(2)}) %collective-permute-start.13) | collective-permute-done | bytes 524320 | tf_op jit(solution)/shard_map/ppermute | solution.py:46
  268.8 11.9 %feed_up.1 = (bf16[512,2048]{1,0:T(8,128)(2,1)}, bf16[512,2048]{1,0:T(8,128)(2,1)}, f32[512,2048]{1,0:T(8,128)}) custom-call(bf16[128,2048]{1,0:T(8,128)(2,1)S(1)} %copy-done.64, bf16[128,2048]{1,0:T(8,128)(2,1)S(1)} %copy-done.60, bf16[128,2048]{1,0:T(8,128)(2,1)S(1)} %copy-done.58, bf16[64,2048]{1,0:T(8,128)(2,1)S(1)} %copy-done.70, ...), custom_call_target="tpu_custom_call" | custom-call | flops 4294967296 | bytes 12582912 | tf_op jit(solution)/shard_map/feed_up/pallas_call | solution.py:101
  300.1 8.7 %down_grads.1 = bf16[1024,2048]{1,0:T(8,128)(2,1)} custom-call(s32[1]{0:T(128)} %bitcast.24.r, bf16[512,2048]{1,0:T(8,128)(2,1)S(1)} %constant_dynamic-update-slice_fusion.refs_0_.dy, bf16[512,2048]{1,0:T(8,128)(2,1)S(1)} %collective-permute-done.28.refs_1_, bf16[512,2048]{1,0:T(8,128)(2,1)} %get-tuple-element.187.refs_2_, bf16[512,2048]{1,0:T(8,128)(2,1)} %copy-done.89), custom_call_target="tpu_custom_call" | custom-call | flops 4294967296 | bytes 16777216 | tf_op jit(solution)/shard_map/down_grads/pallas_call | solution.py:112
  310.4 15.0 %all-gather.11.cloned.1.call-done.down = bf16[2048,2048]{1,0:T(8,128)(2,1)} async-done(((bf16[256,2048]{1,0:T(8,128)(2,1)}), bf16[2048,2048]{1,0:T(8,128)(2,1)}) %all-gather.11.cloned.1.call-update) | async-done | bytes 8388624 | tf_op jit(solution)/shard_map/all_gather | solution.py:84
  326.9 9.9 %feed_down.1.refs_2_ = bf16[512,2048]{1,0:T(8,128)(2,1)S(1)} custom-call(bf16[512,2048]{1,0:T(8,128)(2,1)S(1)} %copy-done.14, f32[512,2048]{1,0:T(8,128)} %get-tuple-element.157.slope_ref, bf16[2048,2048]{1,0:T(8,128)(2,1)} %all-gather.11.cloned.1.call-done.down), custom_call_target="tpu_custom_call" | custom-call | flops 4294967296 | bytes 25165824 | tf_op jit(solution)/shard_map/feed_down/pallas_call | solution.py:101
  336.9 8.9 %convolution_convert_fusion.2 = bf16[512,2048]{1,0:T(8,128)(2,1)S(1)} fusion(bf16[512,2048]{1,0:T(8,128)(2,1)S(1)} %feed_down.1.refs_2_, bf16[2048,2048]{1,0:T(8,128)(2,1)} %all-gather.9.cloned.1.call-done.refs_5_), kind=kOutput, calls=%fused_computation.5 | convolution fusion | flops 4296015872 | bytes 12582912 | tf_op jit(solution)/shard_map/dot_general | solution.py:26
  358.2 10.9 %collective-permute-done.38.refs_2_ = bf16[128,2048]{1,0:T(8,128)(2,1)S(1)} collective-permute-done((bf16[128,2048]{1,0:T(8,128)(2,1)S(1)}, bf16[128,2048]{1,0:T(8,128)(2,1)S(1)}, u32[]{:S(2)}, u32[]{:S(2)}) %collective-permute-start.38) | collective-permute-done | bytes 524320 | tf_op jit(solution)/shard_map/ppermute | solution.py:46
  376.3 9.2 %collective-permute-done.40.refs_2_ = bf16[128,2048]{1,0:T(8,128)(2,1)S(1)} collective-permute-done((bf16[128,2048]{1,0:T(8,128)(2,1)S(1)}, bf16[128,2048]{1,0:T(8,128)(2,1)S(1)}, u32[]{:S(2)}, u32[]{:S(2)}) %collective-permute-start.40) | collective-permute-done | bytes 524320 | tf_op jit(solution)/shard_map/ppermute | solution.py:46
  391.1 8.8 %up_grads.1 = bf16[1024,2048]{1,0:T(8,128)(2,1)} custom-call(s32[1]{0:T(128)} %bitcast.24.r, bf16[512,2048]{1,0:T(8,128)(2,1)} %get-tuple-element.161.refs_0_, bf16[512,2048]{1,0:T(8,128)(2,1)} %collective-permute-done.34.refs_1_, bf16[512,2048]{1,0:T(8,128)(2,1)} %copy-done.23, bf16[512,2048]{1,0:T(8,128)(2,1)} %copy-done.88), custom_call_target="tpu_custom_call" | custom-call | flops 4294967296 | bytes 16777216 | tf_op jit(solution)/shard_map/up_grads/pallas_call | solution.py:112
  435.1 10.5 %collective-permute-done.49.refs_2_ = bf16[128,2048]{1,0:T(8,128)(2,1)S(1)} collective-permute-done((bf16[128,2048]{1,0:T(8,128)(2,1)S(1)}, bf16[128,2048]{1,0:T(8,128)(2,1)S(1)}, u32[]{:S(2)}, u32[]{:S(2)}) %collective-permute-start.49) | collective-permute-done | bytes 524320 | tf_op jit(solution)/shard_map/ppermute | solution.py:46
  468.9 11.9 %attention_grads.1 = bf16[1024,3072]{1,0:T(8,128)(2,1)} custom-call(s32[1]{0:T(128)} %bitcast.24.r, bf16[512,2048]{1,0:T(8,128)(2,1)} %get-tuple-element.177.refs_0_, bf16[512,2048]{1,0:T(8,128)(2,1)} %collective-permute-done.30.refs_1_, bf16[512,2048]{1,0:T(8,128)(2,1)} %copy-done.24, bf16[512,2048]{1,0:T(8,128)(2,1)} %copy-done.78, ...), custom_call_target="tpu_custom_call" | custom-call | flops 6442450944 | bytes 25165824 | tf_op jit(solution)/shard_map/attention_grads/pallas_call | solution.py:112
  520.1 9.6 %all-to-all-done.7 = bf16[4,16,1024]{2,1,0:T(8,128)(2,1)S(1)} async-done(((bf16[4,16,1024]{2,1,0:T(8,128)(2,1)}), bf16[4,16,1024]{2,1,0:T(8,128)(2,1)S(1)}, u32[]{:S(2)}, u32[]{:S(2)}) %all-to-all-start.7) | async-done | bytes 131104 | tf_op jit(solution)/shard_map/all_to_all | solution.py:50
  562.3 8.7 %convolution_convert_fusion = bf16[512,2048]{1,0:T(8,128)(2,1)S(1)} fusion(bf16[512,2048]{1,0:T(8,128)(2,1)} %get-tuple-element.187.refs_2_, bf16[2048,2048]{1,0:T(8,128)(2,1)} %all-gather.11.cloned.1.call-done.down), kind=kOutput, calls=%fused_computation.3 | convolution fusion | flops 4296015872 | bytes 12582912 | tf_op jit(solution)/shard_map/dot_general | solution.py:26
  581.1 12.3 %all_to_all.71 = bf16[4,16,1024]{2,1,0:T(8,128)(2,1)S(1)} all-to-all(bf16[4,16,1024]{2,1,0:T(8,128)(2,1)S(1)} %bitcast.104), channel_id=1, replica_groups=mesh['z'=4,'x'=2,'c'=2,'y'=2] {'z'}, dimensions={0} | all-to-all | bytes 262144 | tf_op jit(solution)/shard_map/all_to_all | solution.py:50
  626.8 10.6 %collective-permute-done.59.refs_2_ = bf16[128,2048]{1,0:T(8,128)(2,1)S(1)} collective-permute-done((bf16[128,2048]{1,0:T(8,128)(2,1)}, bf16[128,2048]{1,0:T(8,128)(2,1)S(1)}, u32[]{:S(2)}, u32[]{:S(2)}) %collective-permute-start.59) | collective-permute-done | bytes 524320 | tf_op jit(solution)/shard_map/ppermute | solution.py:46
  (469 shorter events, 389.5 us)
Async XLA Ops:
  7.2 116.0 %all-gather.5.cloned.1.call-start = ((), (), s32[]{:S(2)}) async-start(), calls=%async_computation.16 | async-start | bytes 9437184 | tf_op jit(solution)/shard_map/all_gather | solution.py:84
  27.5 170.5 %all-gather.7.cloned.1.call-start = ((), (), s32[]{:S(2)}) async-start(), calls=%async_computation.17 | async-start | bytes 4718592 | tf_op jit(solution)/shard_map/all_gather | solution.py:84
  65.2 198.6 %all-gather.9.cloned.1.call-start = ((), (), s32[]{:S(2)}) async-start(), calls=%async_computation.18 | async-start | bytes 9437184 | tf_op jit(solution)/shard_map/all_gather | solution.py:84
  80.8 244.6 %all-gather.11.cloned.1.call-start = ((), (), s32[]{:S(2)}) async-start(), calls=%async_computation.19 | async-start | bytes 9437184 | tf_op jit(solution)/shard_map/all_gather | solution.py:84
  156.3 251.8 %reduce-scatter.4.cloned.1.call-start = ((), (), s32[]{:S(2)}) async-start(), calls=%async_computation.20 | async-start | bytes 5242880 | tf_op jit(solution)/shard_map/reduce_scatter | solution.py:88
  261.5 22.5 %collective-permute-start.24 = (bf16[128,2048]{1,0:T(8,128)(2,1)}, bf16[128,2048]{1,0:T(8,128)(2,1)}, u32[]{:S(2)}, u32[]{:S(2)}) collective-permute-start(bf16[128,2048]{1,0:T(8,128)(2,1)} %get-tuple-element.145.refs_3_), channel_id=1, source_target_pairs={{0,1},{1,0},{2,3},{3,2},{4,5},{5,4},{6,7},{7,6},{8,9},{9,8},{10,11... | collective-permute-start | bytes 1572872 | tf_op jit(solution)/shard_map/ppermute | solution.py:46
  261.8 20.1 %collective-permute-start.25 = (bf16[128,2048]{1,0:T(8,128)(2,1)}, bf16[128,2048]{1,0:T(8,128)(2,1)}, u32[]{:S(2)}, u32[]{:S(2)}) collective-permute-start(bf16[128,2048]{1,0:T(8,128)(2,1)} %get-tuple-element.145.refs_3_), channel_id=1, source_target_pairs={{0,4},{4,0},{1,5},{5,1},{2,6},{6,2},{3,7},{7,3},{8,12},{12,8},{9,1... | collective-permute-start | bytes 1572872 | tf_op jit(solution)/shard_map/ppermute | solution.py:46
  310.2 172.2 %reduce-scatter.6.cloned.1.call-start = ((), (), s32[]{:S(2)}) async-start(), calls=%async_computation.21 | async-start | bytes 5242880 | tf_op jit(solution)/shard_map/reduce_scatter | solution.py:88
  349.0 40.8 %collective-permute-start.43 = (bf16[512,2048]{1,0:T(8,128)(2,1)S(1)}, bf16[512,2048]{1,0:T(8,128)(2,1)S(1)}, u32[]{:S(2)}, u32[]{:S(2)}) collective-permute-start(bf16[512,2048]{1,0:T(8,128)(2,1)S(1)} %feed_down.1.refs_2_), channel_id=1, source_target_pairs={{0,2},{2,0},{1,3},{3,1},{4,6},{6,4},{5,7},{7,5},{8,10},{10,8},{9,1... | collective-permute-start | bytes 6291464 | tf_op jit(solution)/shard_map/ppermute | solution.py:46
  408.2 198.3 %reduce-scatter.8.cloned.1.call-start = ((), (), s32[]{:S(2)}) async-start(), calls=%async_computation.22 | async-start | bytes 7864320 | tf_op jit(solution)/shard_map/reduce_scatter | solution.py:88
  505.2 24.8 %collective-permute-start.65 = (bf16[64,4096]{1,0:T(8,128)(2,1)}, bf16[64,4096]{1,0:T(8,128)(2,1)S(1)}, u32[]{:S(2)}, u32[]{:S(2)}) collective-permute-start(bf16[64,4096]{1,0:T(8,128)(2,1)} %get-tuple-element.197), channel_id=1, source_target_pairs={{0,1},{1,0},{2,3},{3,2},{4,5},{5,4},{6,7},{7,6},{8,9},{9,8},{10,11... | collective-permute-start | bytes 1572872 | tf_op jit(solution)/shard_map/ppermute | solution.py:46
  505.8 25.0 %collective-permute-start.66 = (bf16[64,4096]{1,0:T(8,128)(2,1)}, bf16[64,4096]{1,0:T(8,128)(2,1)S(1)}, u32[]{:S(2)}, u32[]{:S(2)}) collective-permute-start(bf16[64,4096]{1,0:T(8,128)(2,1)} %get-tuple-element.198), channel_id=1, source_target_pairs={{0,4},{4,0},{1,5},{5,1},{2,6},{6,2},{3,7},{7,3},{8,12},{12,8},{9,1... | collective-permute-start | bytes 1572872 | tf_op jit(solution)/shard_map/ppermute | solution.py:46
  507.2 25.8 %collective-permute-start.67 = (bf16[64,4096]{1,0:T(8,128)(2,1)}, bf16[64,4096]{1,0:T(8,128)(2,1)S(1)}, u32[]{:S(2)}, u32[]{:S(2)}) collective-permute-start(bf16[64,4096]{1,0:T(8,128)(2,1)} %get-tuple-element.199), channel_id=1, source_target_pairs={{0,5},{1,4},{4,1},{5,0},{2,7},{3,6},{6,3},{7,2},{8,13},{9,12},{12,... | collective-permute-start | bytes 1572872 | tf_op jit(solution)/shard_map/ppermute | solution.py:79
  510.5 30.7 %collective-permute-start.63 = (bf16[128,2048]{1,0:T(8,128)(2,1)}, bf16[128,2048]{1,0:T(8,128)(2,1)}, u32[]{:S(2)}, u32[]{:S(2)}) collective-permute-start(bf16[128,2048]{1,0:T(8,128)(2,1)} %pad_maximum_fusion.12), channel_id=1, source_target_pairs={{0,1},{1,0},{2,3},{3,2},{4,5},{5,4},{6,7},{7,6},{8,9},{9,8},{10,11... | collective-permute-start | bytes 1572872 | tf_op jit(solution)/shard_map/ppermute | solution.py:46
  518.8 22.8 %collective-permute-start.61 = (bf16[128,2048]{1,0:T(8,128)(2,1)}, bf16[128,2048]{1,0:T(8,128)(2,1)}, u32[]{:S(2)}, u32[]{:S(2)}) collective-permute-start(bf16[128,2048]{1,0:T(8,128)(2,1)} %pad_maximum_fusion.11), channel_id=1, source_target_pairs={{0,4},{4,0},{1,5},{5,1},{2,6},{6,2},{3,7},{7,3},{8,12},{12,8},{9,1... | collective-permute-start | bytes 1572872 | tf_op jit(solution)/shard_map/ppermute | solution.py:46
  558.5 21.6 %all-to-all-start.9 = ((bf16[8,80,1024]{2,1,0:T(8,128)(2,1)}), bf16[8,80,1024]{2,1,0:T(8,128)(2,1)S(1)}, u32[]{:S(2)}, u32[]{:S(2)}) async-start(bf16[8,80,1024]{2,1,0:T(8,128)(2,1)} %copy-done.26), calls=%async_computation.11 | async-start | bytes 2621440 | tf_op jit(solution)/shard_map/all_to_all | solution.py:50
  572.1 27.2 %collective-permute-start.56 = (bf16[64,2048]{1,0:T(8,128)(2,1)}, bf16[64,2048]{1,0:T(8,128)(2,1)}, u32[]{:S(2)}, u32[]{:S(2)}) collective-permute-start(bf16[64,2048]{1,0:T(8,128)(2,1)} %get-tuple-element.237), channel_id=1, source_target_pairs={{0,1},{1,0},{2,3},{3,2},{4,5},{5,4},{6,7},{7,6},{8,9},{9,8},{10,11... | collective-permute-start | bytes 786440 | tf_op jit(solution)/shard_map/ppermute | solution.py:46
  574.1 25.2 %collective-permute-start.58 = (bf16[64,2048]{1,0:T(8,128)(2,1)}, bf16[64,2048]{1,0:T(8,128)(2,1)}, u32[]{:S(2)}, u32[]{:S(2)}) collective-permute-start(bf16[64,2048]{1,0:T(8,128)(2,1)} %get-tuple-element.235), channel_id=1, source_target_pairs={{0,4},{4,0},{1,5},{5,1},{2,6},{6,2},{3,7},{7,3},{8,12},{12,8},{9,1... | collective-permute-start | bytes 786440 | tf_op jit(solution)/shard_map/ppermute | solution.py:46
  607.6 52.1 %all-to-all-start.12 = ((bf16[8,64,1024]{2,1,0:T(8,128)(2,1)}), bf16[8,64,1024]{2,1,0:T(8,128)(2,1)S(1)}, u32[]{:S(2)}, u32[]{:S(2)}) async-start(bf16[8,64,1024]{2,1,0:T(8,128)(2,1)} %broadcast_in_dim.14), calls=%async_computation.15 | async-start | bytes 2097152 | tf_op jit(solution)/shard_map/all_to_all | solution.py:50
  613.0 24.4 %collective-permute-start.59 = (bf16[128,2048]{1,0:T(8,128)(2,1)}, bf16[128,2048]{1,0:T(8,128)(2,1)S(1)}, u32[]{:S(2)}, u32[]{:S(2)}) collective-permute-start(bf16[128,2048]{1,0:T(8,128)(2,1)} %pad_maximum_fusion.10), channel_id=1, source_target_pairs={{0,1},{1,0},{2,3},{3,2},{4,5},{5,4},{6,7},{7,6},{8,9},{9,8},{10,11... | collective-permute-start | bytes 1572872 | tf_op jit(solution)/shard_map/ppermute | solution.py:46
  615.9 25.2 %collective-permute-start.57 = (bf16[128,2048]{1,0:T(8,128)(2,1)}, bf16[128,2048]{1,0:T(8,128)(2,1)}, u32[]{:S(2)}, u32[]{:S(2)}) collective-permute-start(bf16[128,2048]{1,0:T(8,128)(2,1)} %pad_maximum_fusion.9), channel_id=1, source_target_pairs={{0,4},{4,0},{1,5},{5,1},{2,6},{6,2},{3,7},{7,3},{8,12},{12,8},{9,1... | collective-permute-start | bytes 1572872 | tf_op jit(solution)/shard_map/ppermute | solution.py:46
  623.3 26.1 %collective-permute-start.70 = (bf16[64,3072]{1,0:T(8,128)(2,1)}, bf16[64,3072]{1,0:T(8,128)(2,1)}, u32[]{:S(2)}, u32[]{:S(2)}) collective-permute-start(bf16[64,3072]{1,0:T(8,128)(2,1)} %get-tuple-element.211), channel_id=1, source_target_pairs={{0,1},{1,0},{2,3},{3,2},{4,5},{5,4},{6,7},{7,6},{8,9},{9,8},{10,11... | collective-permute-start | bytes 1179656 | tf_op jit(solution)/shard_map/ppermute | solution.py:46
  623.9 25.5 %collective-permute-start.71 = (bf16[64,3072]{1,0:T(8,128)(2,1)}, bf16[64,3072]{1,0:T(8,128)(2,1)}, u32[]{:S(2)}, u32[]{:S(2)}) collective-permute-start(bf16[64,3072]{1,0:T(8,128)(2,1)} %get-tuple-element.212), channel_id=1, source_target_pairs={{0,4},{4,0},{1,5},{5,1},{2,6},{6,2},{3,7},{7,3},{8,12},{12,8},{9,1... | collective-permute-start | bytes 1179656 | tf_op jit(solution)/shard_map/ppermute | solution.py:46
  623.9 31.0 %collective-permute-start.72 = (bf16[64,3072]{1,0:T(8,128)(2,1)}, bf16[64,3072]{1,0:T(8,128)(2,1)}, u32[]{:S(2)}, u32[]{:S(2)}) collective-permute-start(bf16[64,3072]{1,0:T(8,128)(2,1)} %get-tuple-element.213), channel_id=1, source_target_pairs={{0,5},{1,4},{4,1},{5,0},{2,7},{3,6},{6,3},{7,2},{8,13},{9,12},{12,... | collective-permute-start | bytes 1179656 | tf_op jit(solution)/shard_map/ppermute | solution.py:79
  (152 other events, 1698.5 us)
Sparse Core Ops, SparseCore 0:
  27.6 83.6 all-gather.4
  112.9 47.9 all-gather.6
  162.5 80.7 all-gather.8
  244.7 80.5 all-gather.10
  327.5 75.2 reduce-scatter.3
  408.3 74.0 reduce-scatter.5
  484.7 117.5 reduce-scatter.7

commit v13 on v12

--- a/solution.py
+++ b/solution.py
@@ -90,8 +90,9 @@
 
 
 def call(kernel, grid, in_specs, out_specs, out_shape, operands, name, flops=0, size=1 << 22,
-         rank=None, scratch=()):
+         rank=None, scratch=(), aliases=None):
     options = dict(
+        input_output_aliases=aliases or {},
         out_shape=out_shape,
         compiler_params=pltpu.CompilerParams(vmem_limit_bytes=VMEM),
         cost_estimate=pl.CostEstimate(flops=flops, bytes_accessed=size, transcendentals=0),
@@ -168,7 +169,10 @@
 
 
 def mm_scatter(values, weight):
-    partial = mm_t(values, weight).astype(BF)
+    return scatter_partial(mm_t(values, weight).astype(BF))
+
+
+def scatter_partial(partial):
     rows = partial.shape[0] // 4
     cuts = [0, rows, 2 * rows, 3 * rows, 3 * rows + rows // 2, 4 * rows]
     return scatter_tokens([partial[a:b] for a, b in zip(cuts, cuts[1:])])
@@ -514,7 +518,7 @@
     )
 
 
-def grad_products(pairs, name, core=None, blocks=0):
+def grad_products(pairs, name, core=None, blocks=0, columns=0, first=0, into=None):
     count_in = len(pairs[0][0])
     tokens, width = pairs[0][0][0].shape
     widths = [y[0].shape[1] for _, y in pairs]
@@ -523,9 +527,11 @@
     steps = width // rows if core is None else blocks
     step = 512
     count = len(pairs) * count_in
+    columns = columns or total
+    extra = [] if into is None else [into]
 
     def kernel(r, *refs):
-        out = refs[2 * count]
+        out = refs[-1]
         offset = 0
         for k, wide in enumerate(widths):
             left = [refs[k * count_in + b][...].T for b in range(count_in)]
@@ -541,11 +547,13 @@
         kernel,
         (steps,),
         [pl.BlockSpec((tokens, rows), pick)] * count
-        + [pl.BlockSpec((tokens, w), lambda i, r: (0, 0)) for w in widths for _ in range(count_in)],
-        pl.BlockSpec((rows, total), lambda i, r: (i, 0)),
-        shape((steps * rows, total)),
-        [b for x, _ in pairs for b in x] + [b for _, y in pairs for b in y],
+        + [pl.BlockSpec((tokens, w), lambda i, r: (0, 0)) for w in widths for _ in range(count_in)]
+        + [ANY] * len(extra),
+        pl.BlockSpec((rows, total), lambda i, r: (i, first // total)),
+        shape((steps * rows, columns)),
+        [b for x, _ in pairs for b in x] + [b for _, y in pairs for b in y] + extra,
         name,
+        aliases={1 + 2 * count: 0} if extra else {},
         flops=2 * tokens * count_in * steps * rows * total,
         size=4 * width * total,
         rank=jnp.zeros((), jnp.int32) if core is None else core,
@@ -928,7 +936,12 @@
         )
 
         cross_branch = gather_tokens(cross_branch)
-        cross_branch, up_part = lax.optimization_barrier((cross_branch, up_part))
+        activated, cross_own = lax.optimization_barrier((activated, cross_branch[0]))
+        result = mm_t(activated, down).astype(BF)
+        cross_branch, up_part, result = lax.optimization_barrier(
+            ((cross_own,) + cross_branch[1:], up_part, result)
+        )
+        result = scatter_partial(result)
         cross_branch, grad_cross_mixed = gather_mm(
             cross_branch, mid, group, group, "cross_out_back"
         )
@@ -936,27 +949,33 @@
         up_part, down_rows, kv_grad = lax.optimization_barrier((up_part, down_rows, kv_grad))
         up_rows = scatter_grad(up_part, grad_axes)
         cross_branch, grad_cq_both = both(cross_branch), both(grad_cq)
+        grad_cq, result = lax.optimization_barrier((grad_cq, result))
         parts = mm_scatter(grad_cq, mid[:, :group])
         grad_after_attn, attn_branch, gain_grad_b = norm_back(
             parts, grad_after_cross, after_attn, gain_b
         )
 
-        attn_branch, grad_self_mixed = gather_mm(
-            gather_tokens(attn_branch), first, 3 * group, group, "out_back"
-        )
+        attn_branch = gather_tokens(attn_branch)
+        cross_part = grad_products(
+            [(early[2], grad_cq_both), (cross_branch, early[3])],
+            "cross_grads",
+            *(halves or (None, 0)),
+            6 * group,
+            4 * group,
+        )
+        attn_branch, cross_part = lax.optimization_barrier((attn_branch, cross_part))
+        attn_branch, grad_self_mixed = gather_mm(attn_branch, first, 3 * group, group, "out_back")
         grad_projected = self_back(projected, grad_self_mixed, 2 * images)
         rest_part = grad_products(
-            [
-                (early[0], both(grad_projected)),
-                (both(attn_branch), early[1]),
-                (early[2], grad_cq_both),
-                (cross_branch, early[3]),
-            ],
+            [(early[0], both(grad_projected)), (both(attn_branch), early[1])],
             "attention_grads",
-            *halves,
-        )
-        grad_projected, activated, kv_grad, rest_part = lax.optimization_barrier(
-            (grad_projected, activated, kv_grad, rest_part)
+            *(halves or (None, 0)),
+            6 * group,
+            0,
+            cross_part,
+        )
+        grad_projected, kv_grad, rest_part = lax.optimization_barrier(
+            (grad_projected, kv_grad, rest_part)
         )
         rest_part, up_rows = lax.optimization_barrier((rest_part, up_rows))
         rest_rows = scatter_grad(rest_part, grad_axes)
@@ -972,8 +991,7 @@
         )
         sums = jnp.concatenate([gain_grad_a, gain_grad_b, gain_grad_c, mask_grad], axis=0)
 
-        parts = mm_scatter(activated, down)
-        output = layer_output(after_cross, parts, unit, order)
+        output = layer_output(after_cross, result, unit, order)
 
         kv_halves = kv_grad.reshape(2, -1, 2 * group)
         kv_keep = lax.dynamic_index_in_dim(kv_halves, core, 0, keepdims=False)

time: 678 us -> 679 us (level)
  blocking collectives: 93.3 us -> 126 us
  starting transfers between devices: 104 us -> 83.8 us
  waiting for transfers between devices: 224 us -> 213 us
    all_to_all x7 -> x9, blocking collectives: 93.3 us -> 126 us  [trade(): return lax.all_to_all(blocks, axes, 0, 0, tiled=True)]
    all_to_all x6 -> x4, waiting for transfers between devices: 26.5 us -> 13.3 us  [trade(): return lax.all_to_all(blocks, axes, 0, 0, tiled=True)]
    all_to_all x6 -> x4, starting transfers between devices: 24.5 us -> 15.6 us  [trade(): return lax.all_to_all(blocks, axes, 0, 0, tiled=True)]
    ppermute x68, starting transfers between devices: 70.4 us -> 61.4 us  [swap(): return lax.ppermute(values, axis, PAIR)]
    unnamed x184 -> x182, local copies, waits for them, and re-layouts: 46.6 us -> 49 us
    pallas_call x9 -> x10, Pallas kernels: 40.1 us -> 42.3 us  [call(): pl.pallas_call(kernel, grid_spec=spec, **options)]
  transfers between devices with their start and end apart: 86 -> 84, of which waited for: 50 -> 44; matrix products, arithmetic and copies ran while one was open for 11% -> 10% of each run, Pallas kernels for 17% -> 17%
where the time goes in v13:
time: 679 us; the launch traced here: 671 us
  waiting for transfers between devices  213 us (31%)
  blocking collectives  126 us (19%)
  Pallas kernels  117 us (17%)
  starting transfers between devices  83.8 us (12%)
  local copies, waits for them, and re-layouts  74 us (11%)
  matrix products  30.8 us (5%)
  between operations  16.6 us (2%)
  other arithmetic  9.24 us (1%)
    ppermute x68, waiting for transfers between devices, swap(): return lax.ppermute(values, axis, PAIR)  168 us
    all_to_all x9, blocking collectives, trade(): return lax.all_to_all(blocks, axes, 0, 0, tiled=True)  126 us
    pallas_call x20, Pallas kernels, call(): pl.pallas_call(kernel, grid=grid, in_specs=in_specs, out_specs=out_specs,...  74.5 us
    ppermute x68, starting transfers between devices, swap(): return lax.ppermute(values, axis, PAIR)  61.4 us
    unnamed x182, local copies, waits for them, and re-layouts  49 us
    pallas_call x10, Pallas kernels, call(): pl.pallas_call(kernel, grid_spec=spec, **options)  42.3 us
    dot_general x6, matrix products, dot(): return lax.dot_general(a, b, (dims, ((), ())), preferred_element_type=F32)  30.8 us
    all_gather x4, waiting for transfers between devices, gather_rows(): lax.all_gather(rows.reshape(-1, rows.shape[-1]), DATA, axis=0, tiled=True)  16.4 us
  transfers between devices with their start and end apart: 84, of which 44 were waited for; matrix products, arithmetic and copies ran while one was open for 10% of the time, Pallas kernels for 17%

profile of v13, /device:TPU:0, one launch (start us, length us, event | category | flops | bytes accessed | tf_op | source)
XLA Modules:
  0.0 670.6 jit_solution(9019680549211581792)
XLA Ops:
  33.8 9.6 %collective-permute-done.1.refs_2_ = bf16[128,2048]{1,0:T(8,128)(2,1)S(1)} collective-permute-done((bf16[128,2048]{1,0:T(8,128)(2,1)S(1)}, bf16[128,2048]{1,0:T(8,128)(2,1)S(1)}, u32[]{:S(2)}, u32[]{:S(2)}) %collective-permute-start.1) | collective-permute-done | bytes 524320 | tf_op jit(solution)/shard_map/ppermute | solution.py:46
  55.0 10.2 %all_to_all.65 = bf16[4,64,1024]{2,1,0:T(8,128)(2,1)} all-to-all(bf16[4,64,1024]{2,1,0:T(8,128)(2,1)S(1)} %copy.72), channel_id=1, replica_groups=mesh['z'=4,'x'=2,'c'=2,'y'=2] {'x','y'}, dimensions={0} | all-to-all | bytes 1048576 | tf_op jit(solution)/shard_map/all_to_all | solution.py:50
  65.3 14.3 %all_to_all.66 = bf16[4,64,2048]{2,1,0:T(8,128)(2,1)} all-to-all(bf16[4,64,2048]{2,1,0:T(8,128)(2,1)S(1)} %bitcast.94), channel_id=1, replica_groups=mesh['z'=4,'x'=2,'c'=2,'y'=2] {'x','y'}, dimensions={0} | all-to-all | bytes 2097152 | tf_op jit(solution)/shard_map/all_to_all | solution.py:50
  82.3 16.9 %all_to_all.67 = bf16[8,64,1024]{2,1,0:T(8,128)(2,1)S(1)} all-to-all(bf16[8,64,1024]{2,1,0:T(8,128)(2,1)S(1)} %get-tuple-element.138), channel_id=1, replica_groups=mesh['z'=4,'x'=2,'c'=2,'y'=2] {'x','c','y'}, dimensions={0} | all-to-all | bytes 2097152 | tf_op jit(solution)/shard_map/all_to_all | solution.py:50
  99.3 12.9 %all_to_all.68 = bf16[4,16,1024]{2,1,0:T(8,128)(2,1)S(1)} all-to-all(bf16[4,16,1024]{2,1,0:T(8,128)(2,1)S(1)} %bitcast.103), channel_id=1, replica_groups=mesh['z'=4,'x'=2,'c'=2,'y'=2] {'z'}, dimensions={0} | all-to-all | bytes 262144 | tf_op jit(solution)/shard_map/all_to_all | solution.py:50
  112.3 8.8 %all_to_all.69 = bf16[4,16,1024]{2,1,0:T(8,128)(2,1)S(1)} all-to-all(bf16[4,16,1024]{2,1,0:T(8,128)(2,1)S(1)} %broadcast_in_dim.10), channel_id=1, replica_groups=mesh['z'=4,'x'=2,'c'=2,'y'=2] {'z'}, dimensions={0} | all-to-all | bytes 262144 | tf_op jit(solution)/shard_map/all_to_all | solution.py:50
  125.7 9.0 %qkv_mm.1 = (bf16[512,2048]{1,0:T(8,128)(2,1)}, bf16[512,1536]{1,0:T(8,128)(2,1)S(1)}) custom-call(bf16[128,2048]{1,0:T(8,128)(2,1)S(1)} %copy-done.66, bf16[128,2048]{1,0:T(8,128)(2,1)S(1)} %copy-done.60, bf16[128,2048]{1,0:T(8,128)(2,1)S(1)} %copy-done.58, bf16[64,2048]{1,0:T(8,128)(2,1)} %collective-permute-done.2.refs_3_, ...), custom_call_target="tpu_custom_call" | custom-call | flops 3221225472 | bytes 10485760 | tf_op jit(solution)/shard_map/qkv_mm/pallas_call | solution.py:102
  137.6 18.2 %all_to_all.70 = bf16[4,64,2048]{2,1,0:T(8,128)(2,1)} all-to-all(bf16[4,64,2048]{2,1,0:T(8,128)(2,1)S(1)} %bitcast.93), channel_id=1, replica_groups=mesh['z'=4,'x'=2,'c'=2,'y'=2] {'x','y'}, dimensions={0} | all-to-all | bytes 2097152 | tf_op jit(solution)/shard_map/all_to_all | solution.py:50
  170.2 10.7 %collective-permute-done.11.refs_3_ = bf16[128,2048]{1,0:T(8,128)(2,1)S(1)} collective-permute-done((bf16[128,2048]{1,0:T(8,128)(2,1)S(1)}, bf16[128,2048]{1,0:T(8,128)(2,1)S(1)}, u32[]{:S(2)}, u32[]{:S(2)}) %collective-permute-start.11) | collective-permute-done | bytes 524320 | tf_op jit(solution)/shard_map/ppermute | solution.py:46
  185.5 9.4 %collective-permute-done.13.refs_2_ = bf16[128,2048]{1,0:T(8,128)(2,1)S(1)} collective-permute-done((bf16[128,2048]{1,0:T(8,128)(2,1)S(1)}, bf16[128,2048]{1,0:T(8,128)(2,1)S(1)}, u32[]{:S(2)}, u32[]{:S(2)}) %collective-permute-start.13) | collective-permute-done | bytes 524320 | tf_op jit(solution)/shard_map/ppermute | solution.py:46
  237.8 10.6 %collective-permute-done.21.refs_2_ = bf16[128,2048]{1,0:T(8,128)(2,1)S(1)} collective-permute-done((bf16[128,2048]{1,0:T(8,128)(2,1)S(1)}, bf16[128,2048]{1,0:T(8,128)(2,1)S(1)}, u32[]{:S(2)}, u32[]{:S(2)}) %collective-permute-start.21) | collective-permute-done | bytes 524320 | tf_op jit(solution)/shard_map/ppermute | solution.py:46
  267.7 11.9 %feed_up.1 = (bf16[512,2048]{1,0:T(8,128)(2,1)}, bf16[512,2048]{1,0:T(8,128)(2,1)}, f32[512,2048]{1,0:T(8,128)}) custom-call(bf16[128,2048]{1,0:T(8,128)(2,1)S(1)} %copy-done.68, bf16[128,2048]{1,0:T(8,128)(2,1)S(1)} %copy-done.64, bf16[128,2048]{1,0:T(8,128)(2,1)S(1)} %copy-done.62, bf16[64,2048]{1,0:T(8,128)(2,1)S(1)} %copy-done.70, ...), custom_call_target="tpu_custom_call" | custom-call | flops 4294967296 | bytes 12582912 | tf_op jit(solution)/shard_map/feed_up/pallas_call | solution.py:102
  298.9 8.7 %down_grads.1 = bf16[1024,2048]{1,0:T(8,128)(2,1)} custom-call(s32[1]{0:T(128)} %bitcast.24.r, bf16[512,2048]{1,0:T(8,128)(2,1)S(1)} %constant_dynamic-update-slice_fusion.refs_0_.dy, bf16[512,2048]{1,0:T(8,128)(2,1)S(1)} %collective-permute-done.28.refs_1_, bf16[512,2048]{1,0:T(8,128)(2,1)} %get-tuple-element.176.refs_2_, bf16[512,2048]{1,0:T(8,128)(2,1)} %copy-done.88), custom_call_target="tpu_custom_call" | custom-call | flops 4294967296 | bytes 16777216 | tf_op jit(solution)/shard_map/down_grads/pallas_call | solution.py:113
  309.2 16.4 %all-gather.11.cloned.1.call-done.down = bf16[2048,2048]{1,0:T(8,128)(2,1)} async-done(((bf16[256,2048]{1,0:T(8,128)(2,1)}), bf16[2048,2048]{1,0:T(8,128)(2,1)}) %all-gather.11.cloned.1.call-update) | async-done | bytes 8388624 | tf_op jit(solution)/shard_map/all_gather | solution.py:84
  327.2 9.9 %feed_down.1.refs_2_ = bf16[512,2048]{1,0:T(8,128)(2,1)S(1)} custom-call(bf16[512,2048]{1,0:T(8,128)(2,1)S(1)} %copy-done.14, f32[512,2048]{1,0:T(8,128)} %get-tuple-element.169.slope_ref, bf16[2048,2048]{1,0:T(8,128)(2,1)} %all-gather.11.cloned.1.call-done.down), custom_call_target="tpu_custom_call" | custom-call | flops 4294967296 | bytes 25165824 | tf_op jit(solution)/shard_map/feed_down/pallas_call | solution.py:102
  337.1 8.9 %convolution_convert_fusion.2 = bf16[512,2048]{1,0:T(8,128)(2,1)S(1)} fusion(bf16[512,2048]{1,0:T(8,128)(2,1)S(1)} %feed_down.1.refs_2_, bf16[2048,2048]{1,0:T(8,128)(2,1)} %all-gather.9.cloned.1.call-done.refs_5_), kind=kOutput, calls=%fused_computation.5 | convolution fusion | flops 4296015872 | bytes 12582912 | tf_op jit(solution)/shard_map/dot_general | solution.py:26
  358.4 10.9 %collective-permute-done.38.refs_2_ = bf16[128,2048]{1,0:T(8,128)(2,1)S(1)} collective-permute-done((bf16[128,2048]{1,0:T(8,128)(2,1)S(1)}, bf16[128,2048]{1,0:T(8,128)(2,1)S(1)}, u32[]{:S(2)}, u32[]{:S(2)}) %collective-permute-start.38) | collective-permute-done | bytes 524320 | tf_op jit(solution)/shard_map/ppermute | solution.py:46
  375.7 9.2 %convolution_convert_fusion.1 = bf16[512,2048]{1,0:T(8,128)(2,1)} fusion(bf16[512,2048]{1,0:T(8,128)(2,1)S(1)} %copy-done.86, bf16[2048,2048]{1,0:T(8,128)(2,1)} %all-gather.11.cloned.1.call-done.down), kind=kOutput, calls=%fused_computation.4 | convolution fusion | flops 4296015872 | bytes 12582912 | tf_op jit(solution)/shard_map/dot_general | solution.py:26
  390.6 8.8 %up_grads.1 = bf16[1024,2048]{1,0:T(8,128)(2,1)} custom-call(s32[1]{0:T(128)} %bitcast.24.r, bf16[512,2048]{1,0:T(8,128)(2,1)} %get-tuple-element.174.refs_0_, bf16[512,2048]{1,0:T(8,128)(2,1)} %collective-permute-done.34.refs_1_, bf16[512,2048]{1,0:T(8,128)(2,1)} %copy-done.22, bf16[512,2048]{1,0:T(8,128)(2,1)} %copy-done.87), custom_call_target="tpu_custom_call" | custom-call | flops 4294967296 | bytes 16777216 | tf_op jit(solution)/shard_map/up_grads/pallas_call | solution.py:113
  456.9 12.0 %collective-permute-done.53.refs_2_ = bf16[128,2048]{1,0:T(8,128)(2,1)S(1)} collective-permute-done((bf16[128,2048]{1,0:T(8,128)(2,1)S(1)}, bf16[128,2048]{1,0:T(8,128)(2,1)S(1)}, u32[]{:S(2)}, u32[]{:S(2)}) %collective-permute-start.53) | collective-permute-done | bytes 524320 | tf_op jit(solution)/shard_map/ppermute | solution.py:46
  491.1 8.2 %attention_grads.1 = bf16[1024,3072]{1,0:T(8,128)(2,1)} custom-call(s32[1]{0:T(128)} %bitcast.24.r, bf16[512,2048]{1,0:T(8,128)(2,1)} %get-tuple-element.206.refs_0_, bf16[512,2048]{1,0:T(8,128)(2,1)} %collective-permute-done.30.refs_1_, bf16[512,2048]{1,0:T(8,128)(2,1)} %copy-done.23, bf16[512,2048]{1,0:T(8,128)(2,1)} %copy-done.80, ...), custom_call_target="tpu_custom_call", output_to_operand_aliasing={{}: (9, {})} | custom-call | flops 4294967296 | bytes 16777216 | tf_op jit(solution)/shard_map/attention_grads/pallas_call | solution.py:113
  573.3 19.8 %all_to_all.71 = bf16[8,80,1024]{2,1,0:T(8,128)(2,1)S(1)} all-to-all(bf16[8,80,1024]{2,1,0:T(8,128)(2,1)S(1)} %get-tuple-element.230), channel_id=1, replica_groups=mesh['z'=4,'x'=2,'c'=2,'y'=2] {'x','c','y'}, dimensions={0} | all-to-all | bytes 2621440 | tf_op jit(solution)/shard_map/all_to_all | solution.py:50
  593.4 11.7 %all_to_all.72 = bf16[4,16,1024]{2,1,0:T(8,128)(2,1)S(1)} all-to-all(bf16[4,16,1024]{2,1,0:T(8,128)(2,1)S(1)} %bitcast.104), channel_id=1, replica_groups=mesh['z'=4,'x'=2,'c'=2,'y'=2] {'z'}, dimensions={0} | all-to-all | bytes 262144 | tf_op jit(solution)/shard_map/all_to_all | solution.py:50
  605.2 13.0 %all_to_all.73 = bf16[4,16,1024]{2,1,0:T(8,128)(2,1)S(1)} all-to-all(bf16[4,16,1024]{2,1,0:T(8,128)(2,1)S(1)} %broadcast_in_dim.13), channel_id=1, replica_groups=mesh['z'=4,'x'=2,'c'=2,'y'=2] {'z'}, dimensions={0} | all-to-all | bytes 262144 | tf_op jit(solution)/shard_map/all_to_all | solution.py:50
  (466 shorter events, 373.9 us)
Async XLA Ops:
  7.2 116.4 %all-gather.5.cloned.1.call-start = ((), (), s32[]{:S(2)}) async-start(), calls=%async_computation.16 | async-start | bytes 9437184 | tf_op jit(solution)/shard_map/all_gather | solution.py:84
  27.5 171.1 %all-gather.7.cloned.1.call-start = ((), (), s32[]{:S(2)}) async-start(), calls=%async_computation.17 | async-start | bytes 4718592 | tf_op jit(solution)/shard_map/all_gather | solution.py:84
  65.3 197.3 %all-gather.9.cloned.1.call-start = ((), (), s32[]{:S(2)}) async-start(), calls=%async_computation.18 | async-start | bytes 9437184 | tf_op jit(solution)/shard_map/all_gather | solution.py:84
  79.7 245.9 %all-gather.11.cloned.1.call-start = ((), (), s32[]{:S(2)}) async-start(), calls=%async_computation.19 | async-start | bytes 9437184 | tf_op jit(solution)/shard_map/all_gather | solution.py:84
  155.8 253.9 %reduce-scatter.4.cloned.1.call-start = ((), (), s32[]{:S(2)}) async-start(), calls=%async_computation.20 | async-start | bytes 5242880 | tf_op jit(solution)/shard_map/reduce_scatter | solution.py:88
  260.0 22.4 %collective-permute-start.24 = (bf16[128,2048]{1,0:T(8,128)(2,1)}, bf16[128,2048]{1,0:T(8,128)(2,1)}, u32[]{:S(2)}, u32[]{:S(2)}) collective-permute-start(bf16[128,2048]{1,0:T(8,128)(2,1)} %get-tuple-element.164.refs_3_), channel_id=1, source_target_pairs={{0,1},{1,0},{2,3},{3,2},{4,5},{5,4},{6,7},{7,6},{8,9},{9,8},{10,11... | collective-permute-start | bytes 1572872 | tf_op jit(solution)/shard_map/ppermute | solution.py:46
  262.1 18.7 %collective-permute-start.25 = (bf16[128,2048]{1,0:T(8,128)(2,1)}, bf16[128,2048]{1,0:T(8,128)(2,1)}, u32[]{:S(2)}, u32[]{:S(2)}) collective-permute-start(bf16[128,2048]{1,0:T(8,128)(2,1)} %get-tuple-element.164.refs_3_), channel_id=1, source_target_pairs={{0,4},{4,0},{1,5},{5,1},{2,6},{6,2},{3,7},{7,3},{8,12},{12,8},{9,1... | collective-permute-start | bytes 1572872 | tf_op jit(solution)/shard_map/ppermute | solution.py:46
  292.0 16.9 %collective-permute-start.30 = (bf16[512,2048]{1,0:T(8,128)(2,1)}, bf16[512,2048]{1,0:T(8,128)(2,1)}, u32[]{:S(2)}, u32[]{:S(2)}) collective-permute-start(bf16[512,2048]{1,0:T(8,128)(2,1)} %get-tuple-element.206.refs_0_), channel_id=1, source_target_pairs={{0,2},{2,0},{1,3},{3,1},{4,6},{6,4},{5,7},{7,5},{8,10},{10,8},{9,1... | collective-permute-start | bytes 6291464 | tf_op jit(solution)/shard_map/ppermute | solution.py:46
  292.5 16.4 %collective-permute-start.32 = (bf16[512,2048]{1,0:T(8,128)(2,1)}, bf16[512,2048]{1,0:T(8,128)(2,1)}, u32[]{:S(2)}, u32[]{:S(2)}) collective-permute-start(bf16[512,2048]{1,0:T(8,128)(2,1)} %get-tuple-element.191.refs_0_), channel_id=1, source_target_pairs={{0,2},{2,0},{1,3},{3,1},{4,6},{6,4},{5,7},{7,5},{8,10},{10,8},{9,1... | collective-permute-start | bytes 6291464 | tf_op jit(solution)/shard_map/ppermute | solution.py:46
  292.6 16.3 %collective-permute-start.34 = (bf16[512,2048]{1,0:T(8,128)(2,1)}, bf16[512,2048]{1,0:T(8,128)(2,1)}, u32[]{:S(2)}, u32[]{:S(2)}) collective-permute-start(bf16[512,2048]{1,0:T(8,128)(2,1)} %get-tuple-element.174.refs_0_), channel_id=1, source_target_pairs={{0,2},{2,0},{1,3},{3,1},{4,6},{6,4},{5,7},{7,5},{8,10},{10,8},{9,1... | collective-permute-start | bytes 6291464 | tf_op jit(solution)/shard_map/ppermute | solution.py:46
  309.0 190.3 %reduce-scatter.6.cloned.1.call-start = ((), (), s32[]{:S(2)}) async-start(), calls=%async_computation.21 | async-start | bytes 5242880 | tf_op jit(solution)/shard_map/reduce_scatter | solution.py:88
  349.2 39.9 %collective-permute-start.43 = (bf16[512,2048]{1,0:T(8,128)(2,1)S(1)}, bf16[512,2048]{1,0:T(8,128)(2,1)S(1)}, u32[]{:S(2)}, u32[]{:S(2)}) collective-permute-start(bf16[512,2048]{1,0:T(8,128)(2,1)S(1)} %feed_down.1.refs_2_), channel_id=1, source_target_pairs={{0,2},{2,0},{1,3},{3,1},{4,6},{6,4},{5,7},{7,5},{8,10},{10,8},{9,1... | collective-permute-start | bytes 6291464 | tf_op jit(solution)/shard_map/ppermute | solution.py:46
  409.8 208.5 %reduce-scatter.8.cloned.1.call-start = ((), (), s32[]{:S(2)}) async-start(), calls=%async_computation.22 | async-start | bytes 7864320 | tf_op jit(solution)/shard_map/reduce_scatter | solution.py:88
  434.6 36.4 %collective-permute-start.56 = (bf16[512,2048]{1,0:T(8,128)(2,1)S(1)}, bf16[512,2048]{1,0:T(8,128)(2,1)S(1)}, u32[]{:S(2)}, u32[]{:S(2)}) collective-permute-start(bf16[512,2048]{1,0:T(8,128)(2,1)S(1)} %copy-done.16), channel_id=1, source_target_pairs={{0,2},{2,0},{1,3},{3,1},{4,6},{6,4},{5,7},{7,5},{8,10},{10,8},{9,1... | collective-permute-start | bytes 6291464 | tf_op jit(solution)/shard_map/ppermute | solution.py:46
  521.0 24.8 %collective-permute-start.65 = (bf16[64,4096]{1,0:T(8,128)(2,1)}, bf16[64,4096]{1,0:T(8,128)(2,1)S(1)}, u32[]{:S(2)}, u32[]{:S(2)}) collective-permute-start(bf16[64,4096]{1,0:T(8,128)(2,1)} %get-tuple-element.221), channel_id=1, source_target_pairs={{0,1},{1,0},{2,3},{3,2},{4,5},{5,4},{6,7},{7,6},{8,9},{9,8},{10,11... | collective-permute-start | bytes 1572872 | tf_op jit(solution)/shard_map/ppermute | solution.py:46
  522.7 23.1 %collective-permute-start.66 = (bf16[64,4096]{1,0:T(8,128)(2,1)}, bf16[64,4096]{1,0:T(8,128)(2,1)S(1)}, u32[]{:S(2)}, u32[]{:S(2)}) collective-permute-start(bf16[64,4096]{1,0:T(8,128)(2,1)} %get-tuple-element.222), channel_id=1, source_target_pairs={{0,4},{4,0},{1,5},{5,1},{2,6},{6,2},{3,7},{7,3},{8,12},{12,8},{9,1... | collective-permute-start | bytes 1572872 | tf_op jit(solution)/shard_map/ppermute | solution.py:46
  523.0 25.8 %collective-permute-start.67 = (bf16[64,4096]{1,0:T(8,128)(2,1)S(1)}, bf16[64,4096]{1,0:T(8,128)(2,1)S(1)}, u32[]{:S(2)}, u32[]{:S(2)}) collective-permute-start(bf16[64,4096]{1,0:T(8,128)(2,1)S(1)} %get-tuple-element.223), channel_id=1, source_target_pairs={{0,5},{1,4},{4,1},{5,0},{2,7},{3,6},{6,3},{7,2},{8,13},{9,12},{12,... | collective-permute-start | bytes 1572872 | tf_op jit(solution)/shard_map/ppermute | solution.py:79
  526.3 30.5 %collective-permute-start.63 = (bf16[128,2048]{1,0:T(8,128)(2,1)}, bf16[128,2048]{1,0:T(8,128)(2,1)}, u32[]{:S(2)}, u32[]{:S(2)}) collective-permute-start(bf16[128,2048]{1,0:T(8,128)(2,1)} %pad_maximum_fusion.12), channel_id=1, source_target_pairs={{0,1},{1,0},{2,3},{3,2},{4,5},{5,4},{6,7},{7,6},{8,9},{9,8},{10,11... | collective-permute-start | bytes 1572872 | tf_op jit(solution)/shard_map/ppermute | solution.py:46
  534.7 23.3 %collective-permute-start.61 = (bf16[128,2048]{1,0:T(8,128)(2,1)}, bf16[128,2048]{1,0:T(8,128)(2,1)}, u32[]{:S(2)}, u32[]{:S(2)}) collective-permute-start(bf16[128,2048]{1,0:T(8,128)(2,1)} %pad_maximum_fusion.11), channel_id=1, source_target_pairs={{0,4},{4,0},{1,5},{5,1},{2,6},{6,2},{3,7},{7,3},{8,12},{12,8},{9,1... | collective-permute-start | bytes 1572872 | tf_op jit(solution)/shard_map/ppermute | solution.py:46
  550.7 19.1 %all-to-all-start.8 = ((bf16[8,64,1024]{2,1,0:T(8,128)(2,1)}), bf16[8,64,1024]{2,1,0:T(8,128)(2,1)}, u32[]{:S(2)}, u32[]{:S(2)}) async-start(bf16[8,64,1024]{2,1,0:T(8,128)(2,1)} %broadcast_in_dim.12), calls=%async_computation.10 | async-start | bytes 2097152 | tf_op jit(solution)/shard_map/all_to_all | solution.py:50
  619.3 41.0 %all-to-all-start.12 = ((bf16[8,64,1024]{2,1,0:T(8,128)(2,1)}), bf16[8,64,1024]{2,1,0:T(8,128)(2,1)S(1)}, u32[]{:S(2)}, u32[]{:S(2)}) async-start(bf16[8,64,1024]{2,1,0:T(8,128)(2,1)} %broadcast_in_dim.14), calls=%async_computation.15 | async-start | bytes 2097152 | tf_op jit(solution)/shard_map/all_to_all | solution.py:50
  626.5 22.4 %collective-permute-start.70 = (bf16[64,3072]{1,0:T(8,128)(2,1)}, bf16[64,3072]{1,0:T(8,128)(2,1)}, u32[]{:S(2)}, u32[]{:S(2)}) collective-permute-start(bf16[64,3072]{1,0:T(8,128)(2,1)} %get-tuple-element.235), channel_id=1, source_target_pairs={{0,1},{1,0},{2,3},{3,2},{4,5},{5,4},{6,7},{7,6},{8,9},{9,8},{10,11... | collective-permute-start | bytes 1179656 | tf_op jit(solution)/shard_map/ppermute | solution.py:46
  628.5 20.3 %collective-permute-start.71 = (bf16[64,3072]{1,0:T(8,128)(2,1)}, bf16[64,3072]{1,0:T(8,128)(2,1)}, u32[]{:S(2)}, u32[]{:S(2)}) collective-permute-start(bf16[64,3072]{1,0:T(8,128)(2,1)} %get-tuple-element.236), channel_id=1, source_target_pairs={{0,4},{4,0},{1,5},{5,1},{2,6},{6,2},{3,7},{7,3},{8,12},{12,8},{9,1... | collective-permute-start | bytes 1179656 | tf_op jit(solution)/shard_map/ppermute | solution.py:46
  630.0 25.5 %collective-permute-start.72 = (bf16[64,3072]{1,0:T(8,128)(2,1)}, bf16[64,3072]{1,0:T(8,128)(2,1)}, u32[]{:S(2)}, u32[]{:S(2)}) collective-permute-start(bf16[64,3072]{1,0:T(8,128)(2,1)} %get-tuple-element.237), channel_id=1, source_target_pairs={{0,5},{1,4},{4,1},{5,0},{2,7},{3,6},{6,3},{7,2},{8,13},{9,12},{12,... | collective-permute-start | bytes 1179656 | tf_op jit(solution)/shard_map/ppermute | solution.py:79
  (149 other events, 1534.1 us)
Sparse Core Ops, SparseCore 0:
  27.6 86.0 all-gather.4
  115.3 45.7 all-gather.6
  162.7 80.7 all-gather.8
  245.0 80.5 all-gather.10
  327.7 75.2 reduce-scatter.3
  409.9 73.4 reduce-scatter.5
  499.4 114.5 reduce-scatter.7

commit v14 on v12

--- a/solution.py
+++ b/solution.py
@@ -972,8 +972,7 @@
         )
         sums = jnp.concatenate([gain_grad_a, gain_grad_b, gain_grad_c, mask_grad], axis=0)
 
-        parts = mm_scatter(activated, down)
-        output = layer_output(after_cross, parts, unit, order)
+        result = mm_scatter(activated, down)
 
         kv_halves = kv_grad.reshape(2, -1, 2 * group)
         kv_keep = lax.dynamic_index_in_dim(kv_halves, core, 0, keepdims=False)
@@ -982,7 +981,6 @@
         wide_rows = swap_parts(pick_rows([down_rows, up_rows], rank))
         kv_sum, wide_rows = lax.optimization_barrier((kv_sum, wide_rows))
         kv_grads = spread(kv_sum, PLANE, 8)
-        down_grad, up_grad = finish_wide(wide_rows, rank)
         kv_weight_grad, grad_text_w, caption_part = text_back(
             kv_grads, own_text, w_cross, caption, w_text, halves_of(sums, text_width // 4)
         )
@@ -990,7 +988,11 @@
         caption_part = trade(caption_part, PLANE).astype(F32).sum(axis=0)
         sums = layer_order(add_z(whole_of(caption_part[half_context:], width)))
         caption_part = sum_z(caption_part[:half_context].astype(BF))
-        caption_part, rest_rows = lax.optimization_barrier((caption_part, rest_rows))
+        output = layer_output(after_cross, result, unit, order)
+        down_grad, up_grad = finish_wide(wide_rows, rank)
+        caption_part, rest_rows, sums, output, down_grad, up_grad = lax.optimization_barrier(
+            (caption_part, rest_rows, sums, output, down_grad, up_grad)
+        )
         grad_caption = caption_output(spread(caption_part, PLANE, 8))
 
         qkv_grad, out_grad, grad_cross, cross_out_grad = finish_all(

time: 678 us -> 680 us (level)
  waiting for transfers between devices: 224 us -> 233 us
    ppermute x3, waiting for transfers between devices: 11.7 us -> 22.2 us  [swap_parts(): lax.ppermute(parts[3], GROUP, ((0, 3), (1, 2), (2, 1), (3, 0)))]
    unnamed x184 -> x186, local copies, waits for them, and re-layouts: 46.6 us -> 46.7 us
  transfers between devices with their start and end apart: 86 -> 86, of which waited for: 50 -> 49; matrix products, arithmetic and copies ran while one was open for 11% -> 10% of each run, Pallas kernels for 17% -> 16%
where the time goes in v14:
time: 680 us; the launch traced here: 672 us
  waiting for transfers between devices  233 us (34%)
  Pallas kernels  112 us (16%)
  starting transfers between devices  104 us (15%)
  blocking collectives  91.8 us (14%)
  local copies, waits for them, and re-layouts  72.6 us (11%)
  matrix products  31.8 us (5%)
  between operations  16.4 us (2%)
  other arithmetic  9.21 us (1%)
    ppermute x68, waiting for transfers between devices, swap(): return lax.ppermute(values, axis, PAIR)  174 us
    all_to_all x7, blocking collectives, trade(): return lax.all_to_all(blocks, axes, 0, 0, tiled=True)  91.8 us
    pallas_call x20, Pallas kernels, call(): pl.pallas_call(kernel, grid=grid, in_specs=in_specs, out_specs=out_specs,...  74.3 us
    ppermute x68, starting transfers between devices, swap(): return lax.ppermute(values, axis, PAIR)  73.6 us
    unnamed x186, local copies, waits for them, and re-layouts  46.7 us
    pallas_call x9, Pallas kernels, call(): pl.pallas_call(kernel, grid_spec=spec, **options)  38 us
    dot_general x6, matrix products, dot(): return lax.dot_general(a, b, (dims, ((), ())), preferred_element_type=F32)  31.8 us
    all_to_all x6, starting transfers between devices, trade(): return lax.all_to_all(blocks, axes, 0, 0, tiled=True)  22.9 us
  transfers between devices with their start and end apart: 86, of which 49 were waited for; matrix products, arithmetic and copies ran while one was open for 10% of the time, Pallas kernels for 16%

profile of v14, /device:TPU:0, one launch (start us, length us, event | category | flops | bytes accessed | tf_op | source)
XLA Modules:
  0.0 671.5 jit_solution(5867813593435316106)
XLA Ops:
  34.6 8.8 %collective-permute-done.1.refs_2_ = bf16[128,2048]{1,0:T(8,128)(2,1)S(1)} collective-permute-done((bf16[128,2048]{1,0:T(8,128)(2,1)S(1)}, bf16[128,2048]{1,0:T(8,128)(2,1)S(1)}, u32[]{:S(2)}, u32[]{:S(2)}) %collective-permute-start.1) | collective-permute-done | bytes 524320 | tf_op jit(solution)/shard_map/ppermute | solution.py:46
  54.9 10.2 %all_to_all.65 = bf16[4,64,1024]{2,1,0:T(8,128)(2,1)} all-to-all(bf16[4,64,1024]{2,1,0:T(8,128)(2,1)S(1)} %copy.68), channel_id=1, replica_groups=mesh['z'=4,'x'=2,'c'=2,'y'=2] {'x','y'}, dimensions={0} | all-to-all | bytes 1048576 | tf_op jit(solution)/shard_map/all_to_all | solution.py:50
  65.2 15.5 %all_to_all.66 = bf16[4,64,2048]{2,1,0:T(8,128)(2,1)} all-to-all(bf16[4,64,2048]{2,1,0:T(8,128)(2,1)} %bitcast.95), channel_id=1, replica_groups=mesh['z'=4,'x'=2,'c'=2,'y'=2] {'x','y'}, dimensions={0} | all-to-all | bytes 2097152 | tf_op jit(solution)/shard_map/all_to_all | solution.py:50
  83.4 16.9 %all_to_all.67 = bf16[8,64,1024]{2,1,0:T(8,128)(2,1)S(1)} all-to-all(bf16[8,64,1024]{2,1,0:T(8,128)(2,1)S(1)} %get-tuple-element.129), channel_id=1, replica_groups=mesh['z'=4,'x'=2,'c'=2,'y'=2] {'x','c','y'}, dimensions={0} | all-to-all | bytes 2097152 | tf_op jit(solution)/shard_map/all_to_all | solution.py:50
  100.4 11.5 %all_to_all.68 = bf16[4,16,1024]{2,1,0:T(8,128)(2,1)S(1)} all-to-all(bf16[4,16,1024]{2,1,0:T(8,128)(2,1)S(1)} %bitcast.104), channel_id=1, replica_groups=mesh['z'=4,'x'=2,'c'=2,'y'=2] {'z'}, dimensions={0} | all-to-all | bytes 262144 | tf_op jit(solution)/shard_map/all_to_all | solution.py:50
  138.1 18.2 %all_to_all.70 = bf16[4,64,2048]{2,1,0:T(8,128)(2,1)} all-to-all(bf16[4,64,2048]{2,1,0:T(8,128)(2,1)S(1)} %bitcast.94), channel_id=1, replica_groups=mesh['z'=4,'x'=2,'c'=2,'y'=2] {'x','y'}, dimensions={0} | all-to-all | bytes 2097152 | tf_op jit(solution)/shard_map/all_to_all | solution.py:50
  170.8 10.0 %collective-permute-done.11.refs_3_ = bf16[128,2048]{1,0:T(8,128)(2,1)S(1)} collective-permute-done((bf16[128,2048]{1,0:T(8,128)(2,1)S(1)}, bf16[128,2048]{1,0:T(8,128)(2,1)S(1)}, u32[]{:S(2)}, u32[]{:S(2)}) %collective-permute-start.11) | collective-permute-done | bytes 524320 | tf_op jit(solution)/shard_map/ppermute | solution.py:46
  185.2 9.2 %collective-permute-done.13.refs_2_ = bf16[128,2048]{1,0:T(8,128)(2,1)S(1)} collective-permute-done((bf16[128,2048]{1,0:T(8,128)(2,1)S(1)}, bf16[128,2048]{1,0:T(8,128)(2,1)S(1)}, u32[]{:S(2)}, u32[]{:S(2)}) %collective-permute-start.13) | collective-permute-done | bytes 524320 | tf_op jit(solution)/shard_map/ppermute | solution.py:46
  271.4 11.9 %feed_up.1 = (bf16[512,2048]{1,0:T(8,128)(2,1)}, bf16[512,2048]{1,0:T(8,128)(2,1)}, f32[512,2048]{1,0:T(8,128)}) custom-call(bf16[128,2048]{1,0:T(8,128)(2,1)S(1)} %copy-done.63, bf16[128,2048]{1,0:T(8,128)(2,1)S(1)} %copy-done.59, bf16[128,2048]{1,0:T(8,128)(2,1)S(1)} %copy-done.57, bf16[64,2048]{1,0:T(8,128)(2,1)S(1)} %copy-done.69, ...), custom_call_target="tpu_custom_call" | custom-call | flops 4294967296 | bytes 12582912 | tf_op jit(solution)/shard_map/feed_up/pallas_call | solution.py:101
  302.9 8.8 %down_grads.1 = bf16[1024,2048]{1,0:T(8,128)(2,1)} custom-call(s32[1]{0:T(128)} %bitcast.24.r, bf16[512,2048]{1,0:T(8,128)(2,1)S(1)} %constant_dynamic-update-slice_fusion.refs_0_.dy, bf16[512,2048]{1,0:T(8,128)(2,1)S(1)} %collective-permute-done.28.refs_1_, bf16[512,2048]{1,0:T(8,128)(2,1)} %get-tuple-element.210.refs_2_, bf16[512,2048]{1,0:T(8,128)(2,1)} %copy-done.90), custom_call_target="tpu_custom_call" | custom-call | flops 4294967296 | bytes 16777216 | tf_op jit(solution)/shard_map/down_grads/pallas_call | solution.py:112
  313.2 12.1 %all-gather.11.cloned.1.call-done.down = bf16[2048,2048]{1,0:T(8,128)(2,1)} async-done(((bf16[256,2048]{1,0:T(8,128)(2,1)}), bf16[2048,2048]{1,0:T(8,128)(2,1)}) %all-gather.11.cloned.1.call-update) | async-done | bytes 8388624 | tf_op jit(solution)/shard_map/all_gather | solution.py:84
  326.9 9.9 %feed_down.1.refs_2_ = bf16[512,2048]{1,0:T(8,128)(2,1)S(1)} custom-call(bf16[512,2048]{1,0:T(8,128)(2,1)S(1)} %copy-done.14, f32[512,2048]{1,0:T(8,128)} %get-tuple-element.161.slope_ref, bf16[2048,2048]{1,0:T(8,128)(2,1)} %all-gather.11.cloned.1.call-done.down), custom_call_target="tpu_custom_call" | custom-call | flops 4294967296 | bytes 25165824 | tf_op jit(solution)/shard_map/feed_down/pallas_call | solution.py:101
  336.9 8.9 %convolution_convert_fusion.2 = bf16[512,2048]{1,0:T(8,128)(2,1)S(1)} fusion(bf16[512,2048]{1,0:T(8,128)(2,1)S(1)} %feed_down.1.refs_2_, bf16[2048,2048]{1,0:T(8,128)(2,1)} %all-gather.9.cloned.1.call-done.refs_5_), kind=kOutput, calls=%fused_computation.5 | convolution fusion | flops 4296015872 | bytes 12582912 | tf_op jit(solution)/shard_map/dot_general | solution.py:26
  358.2 10.9 %collective-permute-done.38.refs_2_ = bf16[128,2048]{1,0:T(8,128)(2,1)S(1)} collective-permute-done((bf16[128,2048]{1,0:T(8,128)(2,1)S(1)}, bf16[128,2048]{1,0:T(8,128)(2,1)S(1)}, u32[]{:S(2)}, u32[]{:S(2)}) %collective-permute-start.38) | collective-permute-done | bytes 524320 | tf_op jit(solution)/shard_map/ppermute | solution.py:46
  376.3 9.2 %collective-permute-done.40.refs_2_ = bf16[128,2048]{1,0:T(8,128)(2,1)S(1)} collective-permute-done((bf16[128,2048]{1,0:T(8,128)(2,1)S(1)}, bf16[128,2048]{1,0:T(8,128)(2,1)S(1)}, u32[]{:S(2)}, u32[]{:S(2)}) %collective-permute-start.40) | collective-permute-done | bytes 524320 | tf_op jit(solution)/shard_map/ppermute | solution.py:46
  391.1 8.8 %up_grads.1 = bf16[1024,2048]{1,0:T(8,128)(2,1)} custom-call(s32[1]{0:T(128)} %bitcast.24.r, bf16[512,2048]{1,0:T(8,128)(2,1)} %get-tuple-element.165.refs_0_, bf16[512,2048]{1,0:T(8,128)(2,1)} %collective-permute-done.34.refs_1_, bf16[512,2048]{1,0:T(8,128)(2,1)} %copy-done.23, bf16[512,2048]{1,0:T(8,128)(2,1)} %copy-done.89), custom_call_target="tpu_custom_call" | custom-call | flops 4294967296 | bytes 16777216 | tf_op jit(solution)/shard_map/up_grads/pallas_call | solution.py:112
  434.5 11.8 %collective-permute-done.49.refs_2_ = bf16[128,2048]{1,0:T(8,128)(2,1)S(1)} collective-permute-done((bf16[128,2048]{1,0:T(8,128)(2,1)S(1)}, bf16[128,2048]{1,0:T(8,128)(2,1)S(1)}, u32[]{:S(2)}, u32[]{:S(2)}) %collective-permute-start.49) | collective-permute-done | bytes 524320 | tf_op jit(solution)/shard_map/ppermute | solution.py:46
  468.3 11.9 %attention_grads.1 = bf16[1024,3072]{1,0:T(8,128)(2,1)} custom-call(s32[1]{0:T(128)} %bitcast.24.r, bf16[512,2048]{1,0:T(8,128)(2,1)} %get-tuple-element.181.refs_0_, bf16[512,2048]{1,0:T(8,128)(2,1)} %collective-permute-done.30.refs_1_, bf16[512,2048]{1,0:T(8,128)(2,1)} %copy-done.24, bf16[512,2048]{1,0:T(8,128)(2,1)} %copy-done.76, ...), custom_call_target="tpu_custom_call" | custom-call | flops 6442450944 | bytes 25165824 | tf_op jit(solution)/shard_map/attention_grads/pallas_call | solution.py:112
  521.6 9.2 %convolution_convert_fusion = bf16[512,2048]{1,0:T(8,128)(2,1)} fusion(bf16[512,2048]{1,0:T(8,128)(2,1)S(1)} %copy-done.88, bf16[2048,2048]{1,0:T(8,128)(2,1)} %all-gather.11.cloned.1.call-done.down), kind=kOutput, calls=%fused_computation.3 | convolution fusion | flops 4296015872 | bytes 12582912 | tf_op jit(solution)/shard_map/dot_general | solution.py:26
  535.1 9.4 %collective-permute-done.59.refs_3_ = bf16[64,4096]{1,0:T(8,128)(2,1)S(1)} collective-permute-done((bf16[64,4096]{1,0:T(8,128)(2,1)}, bf16[64,4096]{1,0:T(8,128)(2,1)S(1)}, u32[]{:S(2)}, u32[]{:S(2)}) %collective-permute-start.59) | collective-permute-done | bytes 524320 | tf_op jit(solution)/shard_map/ppermute | solution.py:79
  581.7 11.3 %all-to-all-done.9 = bf16[8,80,1024]{2,1,0:T(8,128)(2,1)S(1)} async-done(((bf16[8,80,1024]{2,1,0:T(8,128)(2,1)}), bf16[8,80,1024]{2,1,0:T(8,128)(2,1)S(1)}, u32[]{:S(2)}, u32[]{:S(2)}) %all-to-all-start.9) | async-done | bytes 1310752 | tf_op jit(solution)/shard_map/all_to_all | solution.py:50
  594.0 10.7 %all_to_all.71 = bf16[4,16,1024]{2,1,0:T(8,128)(2,1)S(1)} all-to-all(bf16[4,16,1024]{2,1,0:T(8,128)(2,1)S(1)} %bitcast.105), channel_id=1, replica_groups=mesh['z'=4,'x'=2,'c'=2,'y'=2] {'z'}, dimensions={0} | all-to-all | bytes 262144 | tf_op jit(solution)/shard_map/all_to_all | solution.py:50
  632.4 17.0 %collective-permute-done.70.refs_1_ = bf16[64,3072]{1,0:T(8,128)(2,1)S(1)} collective-permute-done((bf16[64,3072]{1,0:T(8,128)(2,1)S(1)}, bf16[64,3072]{1,0:T(8,128)(2,1)S(1)}, u32[]{:S(2)}, u32[]{:S(2)}) %collective-permute-start.70) | collective-permute-done | bytes 393248 | tf_op jit(solution)/shard_map/ppermute | solution.py:46
  650.0 8.9 %collective-permute-done.72.refs_3_ = bf16[64,3072]{1,0:T(8,128)(2,1)S(1)} collective-permute-done((bf16[64,3072]{1,0:T(8,128)(2,1)S(1)}, bf16[64,3072]{1,0:T(8,128)(2,1)S(1)}, u32[]{:S(2)}, u32[]{:S(2)}) %collective-permute-start.72) | collective-permute-done | bytes 393248 | tf_op jit(solution)/shard_map/ppermute | solution.py:79
  (469 shorter events, 384.1 us)
Async XLA Ops:
  7.2 116.0 %all-gather.5.cloned.1.call-start = ((), (), s32[]{:S(2)}) async-start(), calls=%async_computation.16 | async-start | bytes 9437184 | tf_op jit(solution)/shard_map/all_gather | solution.py:84
  27.5 170.5 %all-gather.7.cloned.1.call-start = ((), (), s32[]{:S(2)}) async-start(), calls=%async_computation.17 | async-start | bytes 4718592 | tf_op jit(solution)/shard_map/all_gather | solution.py:84
  65.2 201.2 %all-gather.9.cloned.1.call-start = ((), (), s32[]{:S(2)}) async-start(), calls=%async_computation.18 | async-start | bytes 9437184 | tf_op jit(solution)/shard_map/all_gather | solution.py:84
  80.8 244.6 %all-gather.11.cloned.1.call-start = ((), (), s32[]{:S(2)}) async-start(), calls=%async_computation.19 | async-start | bytes 9437184 | tf_op jit(solution)/shard_map/all_gather | solution.py:84
  156.3 251.1 %reduce-scatter.4.cloned.1.call-start = ((), (), s32[]{:S(2)}) async-start(), calls=%async_computation.20 | async-start | bytes 5242880 | tf_op jit(solution)/shard_map/reduce_scatter | solution.py:88
  264.1 22.6 %collective-permute-start.24 = (bf16[128,2048]{1,0:T(8,128)(2,1)}, bf16[128,2048]{1,0:T(8,128)(2,1)}, u32[]{:S(2)}, u32[]{:S(2)}) collective-permute-start(bf16[128,2048]{1,0:T(8,128)(2,1)} %get-tuple-element.149.refs_3_), channel_id=1, source_target_pairs={{0,1},{1,0},{2,3},{3,2},{4,5},{5,4},{6,7},{7,6},{8,9},{9,8},{10,11... | collective-permute-start | bytes 1572872 | tf_op jit(solution)/shard_map/ppermute | solution.py:46
  264.4 20.1 %collective-permute-start.25 = (bf16[128,2048]{1,0:T(8,128)(2,1)}, bf16[128,2048]{1,0:T(8,128)(2,1)}, u32[]{:S(2)}, u32[]{:S(2)}) collective-permute-start(bf16[128,2048]{1,0:T(8,128)(2,1)} %get-tuple-element.149.refs_3_), channel_id=1, source_target_pairs={{0,4},{4,0},{1,5},{5,1},{2,6},{6,2},{3,7},{7,3},{8,12},{12,8},{9,1... | collective-permute-start | bytes 1572872 | tf_op jit(solution)/shard_map/ppermute | solution.py:46
  313.0 169.4 %reduce-scatter.6.cloned.1.call-start = ((), (), s32[]{:S(2)}) async-start(), calls=%async_computation.21 | async-start | bytes 5242880 | tf_op jit(solution)/shard_map/reduce_scatter | solution.py:88
  349.0 40.8 %collective-permute-start.43 = (bf16[512,2048]{1,0:T(8,128)(2,1)S(1)}, bf16[512,2048]{1,0:T(8,128)(2,1)S(1)}, u32[]{:S(2)}, u32[]{:S(2)}) collective-permute-start(bf16[512,2048]{1,0:T(8,128)(2,1)S(1)} %feed_down.1.refs_2_), channel_id=1, source_target_pairs={{0,2},{2,0},{1,3},{3,1},{4,6},{6,4},{5,7},{7,5},{8,10},{10,8},{9,1... | collective-permute-start | bytes 6291464 | tf_op jit(solution)/shard_map/ppermute | solution.py:46
  408.2 213.7 %reduce-scatter.8.cloned.1.call-start = ((), (), s32[]{:S(2)}) async-start(), calls=%async_computation.22 | async-start | bytes 7864320 | tf_op jit(solution)/shard_map/reduce_scatter | solution.py:88
  504.2 51.7 %collective-permute-start.63 = (bf16[128,2048]{1,0:T(8,128)(2,1)}, bf16[128,2048]{1,0:T(8,128)(2,1)}, u32[]{:S(2)}, u32[]{:S(2)}) collective-permute-start(bf16[128,2048]{1,0:T(8,128)(2,1)} %pad_maximum_fusion.10), channel_id=1, source_target_pairs={{0,1},{1,0},{2,3},{3,2},{4,5},{5,4},{6,7},{7,6},{8,9},{9,8},{10,11... | collective-permute-start | bytes 1572872 | tf_op jit(solution)/shard_map/ppermute | solution.py:46
  506.2 49.8 %collective-permute-start.61 = (bf16[128,2048]{1,0:T(8,128)(2,1)}, bf16[128,2048]{1,0:T(8,128)(2,1)}, u32[]{:S(2)}, u32[]{:S(2)}) collective-permute-start(bf16[128,2048]{1,0:T(8,128)(2,1)} %pad_maximum_fusion.9), channel_id=1, source_target_pairs={{0,4},{4,0},{1,5},{5,1},{2,6},{6,2},{3,7},{7,3},{8,12},{12,8},{9,1... | collective-permute-start | bytes 1572872 | tf_op jit(solution)/shard_map/ppermute | solution.py:46
  512.6 19.4 %all-to-all-start.7 = ((bf16[4,16,1024]{2,1,0:T(8,128)(2,1)}), bf16[4,16,1024]{2,1,0:T(8,128)(2,1)S(1)}, u32[]{:S(2)}, u32[]{:S(2)}) async-start(bf16[4,16,1024]{2,1,0:T(8,128)(2,1)} %broadcast_in_dim.11), calls=%async_computation.8 | async-start | bytes 262144 | tf_op jit(solution)/shard_map/all_to_all | solution.py:50
  519.9 24.6 %collective-permute-start.59 = (bf16[64,4096]{1,0:T(8,128)(2,1)}, bf16[64,4096]{1,0:T(8,128)(2,1)S(1)}, u32[]{:S(2)}, u32[]{:S(2)}) collective-permute-start(bf16[64,4096]{1,0:T(8,128)(2,1)} %get-tuple-element.199), channel_id=1, source_target_pairs={{0,5},{1,4},{4,1},{5,0},{2,7},{3,6},{6,3},{7,2},{8,13},{9,12},{12,... | collective-permute-start | bytes 1572872 | tf_op jit(solution)/shard_map/ppermute | solution.py:79
  545.6 19.6 %all-to-all-start.8 = ((bf16[8,64,1024]{2,1,0:T(8,128)(2,1)}), bf16[8,64,1024]{2,1,0:T(8,128)(2,1)}, u32[]{:S(2)}, u32[]{:S(2)}) async-start(bf16[8,64,1024]{2,1,0:T(8,128)(2,1)} %broadcast_in_dim.12), calls=%async_computation.10 | async-start | bytes 2097152 | tf_op jit(solution)/shard_map/all_to_all | solution.py:50
  552.5 22.7 %collective-permute-start.66 = (bf16[64,2048]{1,0:T(8,128)(2,1)}, bf16[64,2048]{1,0:T(8,128)(2,1)}, u32[]{:S(2)}, u32[]{:S(2)}) collective-permute-start(bf16[64,2048]{1,0:T(8,128)(2,1)} %get-tuple-element.239), channel_id=1, source_target_pairs={{0,1},{1,0},{2,3},{3,2},{4,5},{5,4},{6,7},{7,6},{8,9},{9,8},{10,11... | collective-permute-start | bytes 786440 | tf_op jit(solution)/shard_map/ppermute | solution.py:46
  554.5 20.8 %collective-permute-start.68 = (bf16[64,2048]{1,0:T(8,128)(2,1)}, bf16[64,2048]{1,0:T(8,128)(2,1)}, u32[]{:S(2)}, u32[]{:S(2)}) collective-permute-start(bf16[64,2048]{1,0:T(8,128)(2,1)} %get-tuple-element.237), channel_id=1, source_target_pairs={{0,4},{4,0},{1,5},{5,1},{2,6},{6,2},{3,7},{7,3},{8,12},{12,8},{9,1... | collective-permute-start | bytes 786440 | tf_op jit(solution)/shard_map/ppermute | solution.py:46
  571.5 21.5 %all-to-all-start.9 = ((bf16[8,80,1024]{2,1,0:T(8,128)(2,1)}), bf16[8,80,1024]{2,1,0:T(8,128)(2,1)S(1)}, u32[]{:S(2)}, u32[]{:S(2)}) async-start(bf16[8,80,1024]{2,1,0:T(8,128)(2,1)} %get-tuple-element.208), calls=%async_computation.11 | async-start | bytes 2621440 | tf_op jit(solution)/shard_map/all_to_all | solution.py:50
  577.4 40.2 %collective-permute-start.69 = (bf16[128,2048]{1,0:T(8,128)(2,1)}, bf16[128,2048]{1,0:T(8,128)(2,1)S(1)}, u32[]{:S(2)}, u32[]{:S(2)}) collective-permute-start(bf16[128,2048]{1,0:T(8,128)(2,1)} %pad_maximum_fusion.12), channel_id=1, source_target_pairs={{0,1},{1,0},{2,3},{3,2},{4,5},{5,4},{6,7},{7,6},{8,9},{9,8},{10,11... | collective-permute-start | bytes 1572872 | tf_op jit(solution)/shard_map/ppermute | solution.py:46
  580.2 37.5 %collective-permute-start.67 = (bf16[128,2048]{1,0:T(8,128)(2,1)}, bf16[128,2048]{1,0:T(8,128)(2,1)S(1)}, u32[]{:S(2)}, u32[]{:S(2)}) collective-permute-start(bf16[128,2048]{1,0:T(8,128)(2,1)} %pad_maximum_fusion.11), channel_id=1, source_target_pairs={{0,4},{4,0},{1,5},{5,1},{2,6},{6,2},{3,7},{7,3},{8,12},{12,8},{9,1... | collective-permute-start | bytes 1572872 | tf_op jit(solution)/shard_map/ppermute | solution.py:46
  623.0 38.5 %all-to-all-start.12 = ((bf16[8,64,1024]{2,1,0:T(8,128)(2,1)}), bf16[8,64,1024]{2,1,0:T(8,128)(2,1)S(1)}, u32[]{:S(2)}, u32[]{:S(2)}) async-start(bf16[8,64,1024]{2,1,0:T(8,128)(2,1)} %broadcast_in_dim.14), calls=%async_computation.15 | async-start | bytes 2097152 | tf_op jit(solution)/shard_map/all_to_all | solution.py:50
  628.3 21.2 %collective-permute-start.70 = (bf16[64,3072]{1,0:T(8,128)(2,1)S(1)}, bf16[64,3072]{1,0:T(8,128)(2,1)S(1)}, u32[]{:S(2)}, u32[]{:S(2)}) collective-permute-start(bf16[64,3072]{1,0:T(8,128)(2,1)S(1)} %get-tuple-element.223), channel_id=1, source_target_pairs={{0,1},{1,0},{2,3},{3,2},{4,5},{5,4},{6,7},{7,6},{8,9},{9,8},{10,11... | collective-permute-start | bytes 1179656 | tf_op jit(solution)/shard_map/ppermute | solution.py:46
  630.3 19.8 %collective-permute-start.71 = (bf16[64,3072]{1,0:T(8,128)(2,1)S(1)}, bf16[64,3072]{1,0:T(8,128)(2,1)S(1)}, u32[]{:S(2)}, u32[]{:S(2)}) collective-permute-start(bf16[64,3072]{1,0:T(8,128)(2,1)S(1)} %get-tuple-element.224), channel_id=1, source_target_pairs={{0,4},{4,0},{1,5},{5,1},{2,6},{6,2},{3,7},{7,3},{8,12},{12,8},{9,1... | collective-permute-start | bytes 1179656 | tf_op jit(solution)/shard_map/ppermute | solution.py:46
  631.8 27.1 %collective-permute-start.72 = (bf16[64,3072]{1,0:T(8,128)(2,1)S(1)}, bf16[64,3072]{1,0:T(8,128)(2,1)S(1)}, u32[]{:S(2)}, u32[]{:S(2)}) collective-permute-start(bf16[64,3072]{1,0:T(8,128)(2,1)S(1)} %get-tuple-element.225), channel_id=1, source_target_pairs={{0,5},{1,4},{4,1},{5,0},{2,7},{3,6},{6,3},{7,2},{8,13},{9,12},{12,... | collective-permute-start | bytes 1179656 | tf_op jit(solution)/shard_map/ppermute | solution.py:79
  (153 other events, 1622.4 us)
Sparse Core Ops, SparseCore 0:
  27.6 83.6 all-gather.4
  112.9 47.9 all-gather.6
  162.5 80.7 all-gather.8
  244.7 80.5 all-gather.10
  327.5 75.2 reduce-scatter.3
  407.6 74.7 reduce-scatter.5
  484.7 115.4 reduce-scatter.7

commit v15 on v14

--- a/solution.py
+++ b/solution.py
@@ -936,15 +936,22 @@
         up_part, down_rows, kv_grad = lax.optimization_barrier((up_part, down_rows, kv_grad))
         up_rows = scatter_grad(up_part, grad_axes)
         cross_branch, grad_cq_both = both(cross_branch), both(grad_cq)
+        kv_part = kv_grad.astype(BF).reshape(2, z_size, -1, 2 * group)
+        kv_part = kv_part.transpose(1, 0, 2, 3).reshape(2 * z_size, -1, 2 * group)
         parts = mm_scatter(grad_cq, mid[:, :group])
+        kv_part = trade(kv_part, DATA).astype(F32).sum(axis=0).astype(BF)
+        parts, kv_part = lax.optimization_barrier((parts, kv_part))
         grad_after_attn, attn_branch, gain_grad_b = norm_back(
             parts, grad_after_cross, after_attn, gain_b
         )
 
-        attn_branch, grad_self_mixed = gather_mm(
-            gather_tokens(attn_branch), first, 3 * group, group, "out_back"
-        )
+        attn_branch = gather_tokens(attn_branch)
+        kv_part = spread(kv_part, "z", z_size).reshape(-1, 2 * group)
+        attn_branch, kv_part = lax.optimization_barrier((attn_branch, kv_part))
+        attn_branch, grad_self_mixed = gather_mm(attn_branch, first, 3 * group, group, "out_back")
         grad_projected = self_back(projected, grad_self_mixed, 2 * images)
+        kv_grads = spread(kv_part, PLANE, 8)
+        grad_projected, kv_grads = lax.optimization_barrier((grad_projected, kv_grads))
         rest_part = grad_products(
             [
                 (early[0], both(grad_projected)),
@@ -955,8 +962,8 @@
             "attention_grads",
             *halves,
         )
-        grad_projected, activated, kv_grad, rest_part = lax.optimization_barrier(
-            (grad_projected, activated, kv_grad, rest_part)
+        grad_projected, activated, rest_part = lax.optimization_barrier(
+            (grad_projected, activated, rest_part)
         )
         rest_part, up_rows = lax.optimization_barrier((rest_part, up_rows))
         rest_rows = scatter_grad(rest_part, grad_axes)
@@ -974,13 +981,7 @@
 
         result = mm_scatter(activated, down)
 
-        kv_halves = kv_grad.reshape(2, -1, 2 * group)
-        kv_keep = lax.dynamic_index_in_dim(kv_halves, core, 0, keepdims=False)
-        kv_send = lax.dynamic_index_in_dim(kv_halves, 1 - core, 0, keepdims=False)
-        kv_sum = sum_z((kv_keep + swap(kv_send, "c")).astype(BF))
         wide_rows = swap_parts(pick_rows([down_rows, up_rows], rank))
-        kv_sum, wide_rows = lax.optimization_barrier((kv_sum, wide_rows))
-        kv_grads = spread(kv_sum, PLANE, 8)
         kv_weight_grad, grad_text_w, caption_part = text_back(
             kv_grads, own_text, w_cross, caption, w_text, halves_of(sums, text_width // 4)
         )

time: 680 us -> 693 us (1.019)
  blocking collectives: 91.8 us -> 110 us
  local copies, waits for them, and re-layouts: 72.6 us -> 65 us
    all_to_all x7 -> x8, blocking collectives: 91.8 us -> 110 us  [trade(): return lax.all_to_all(blocks, axes, 0, 0, tiled=True)]
    ppermute x68 -> x67, waiting for transfers between devices: 174 us -> 185 us  [swap(): return lax.ppermute(values, axis, PAIR)]
    ppermute x3, waiting for transfers between devices: 22.2 us -> 12.8 us  [swap_parts(): lax.ppermute(parts[3], GROUP, ((0, 3), (1, 2), (2, 1), (3, 0)))]
    unnamed x186 -> x154, local copies, waits for them, and re-layouts: 46.7 us -> 40.3 us
    all_to_all x6 -> x5, starting transfers between devices: 22.9 us -> 19.6 us  [trade(): return lax.all_to_all(blocks, axes, 0, 0, tiled=True)]
    all_to_all x6 -> x5, waiting for transfers between devices: 20.7 us -> 18.6 us  [trade(): return lax.all_to_all(blocks, axes, 0, 0, tiled=True)]
    ppermute x68 -> x67, starting transfers between devices: 73.6 us -> 72.4 us  [swap(): return lax.ppermute(values, axis, PAIR)]
  transfers between devices with their start and end apart: 86 -> 84, of which waited for: 49 -> 45; matrix products, arithmetic and copies ran while one was open for 10% -> 10% of each run, Pallas kernels for 16% -> 16%
where the time goes in v15:
time: 693 us; the launch traced here: 685 us
  waiting for transfers between devices  239 us (34%)
  Pallas kernels  116 us (17%)
  blocking collectives  110 us (16%)
  starting transfers between devices  98 us (14%)
  local copies, waits for them, and re-layouts  65 us (9%)
  matrix products  31.7 us (5%)
  between operations  16.5 us (2%)
  other arithmetic  8.38 us (1%)
    ppermute x67, waiting for transfers between devices, swap(): return lax.ppermute(values, axis, PAIR)  185 us
    all_to_all x8, blocking collectives, trade(): return lax.all_to_all(blocks, axes, 0, 0, tiled=True)  110 us
    pallas_call x20, Pallas kernels, call(): pl.pallas_call(kernel, grid=grid, in_specs=in_specs, out_specs=out_specs,...  77.4 us
    ppermute x67, starting transfers between devices, swap(): return lax.ppermute(values, axis, PAIR)  72.4 us
    unnamed x154, local copies, waits for them, and re-layouts  40.3 us
    pallas_call x9, Pallas kernels, call(): pl.pallas_call(kernel, grid_spec=spec, **options)  39 us
    dot_general x6, matrix products, dot(): return lax.dot_general(a, b, (dims, ((), ())), preferred_element_type=F32)  31.7 us
    all_to_all x5, starting transfers between devices, trade(): return lax.all_to_all(blocks, axes, 0, 0, tiled=True)  19.6 us
  transfers between devices with their start and end apart: 84, of which 45 were waited for; matrix products, arithmetic and copies ran while one was open for 10% of the time, Pallas kernels for 16%

profile of v15, /device:TPU:0, one launch (start us, length us, event | category | flops | bytes accessed | tf_op | source)
XLA Modules:
  0.0 685.5 jit_solution(17567408118338582873)
XLA Ops:
  34.6 8.8 %collective-permute-done.1.refs_2_ = bf16[128,2048]{1,0:T(8,128)(2,1)S(1)} collective-permute-done((bf16[128,2048]{1,0:T(8,128)(2,1)S(1)}, bf16[128,2048]{1,0:T(8,128)(2,1)S(1)}, u32[]{:S(2)}, u32[]{:S(2)}) %collective-permute-start.1) | collective-permute-done | bytes 524320 | tf_op jit(solution)/shard_map/ppermute | solution.py:46
  54.9 10.2 %all_to_all.65 = bf16[4,64,1024]{2,1,0:T(8,128)(2,1)} all-to-all(bf16[4,64,1024]{2,1,0:T(8,128)(2,1)S(1)} %copy.72), channel_id=1, replica_groups=mesh['z'=4,'x'=2,'c'=2,'y'=2] {'x','y'}, dimensions={0} | all-to-all | bytes 1048576 | tf_op jit(solution)/shard_map/all_to_all | solution.py:50
  65.2 15.5 %all_to_all.66 = bf16[4,64,2048]{2,1,0:T(8,128)(2,1)} all-to-all(bf16[4,64,2048]{2,1,0:T(8,128)(2,1)} %bitcast.89), channel_id=1, replica_groups=mesh['z'=4,'x'=2,'c'=2,'y'=2] {'x','y'}, dimensions={0} | all-to-all | bytes 2097152 | tf_op jit(solution)/shard_map/all_to_all | solution.py:50
  83.4 16.9 %all_to_all.67 = bf16[8,64,1024]{2,1,0:T(8,128)(2,1)S(1)} all-to-all(bf16[8,64,1024]{2,1,0:T(8,128)(2,1)S(1)} %get-tuple-element.135), channel_id=1, replica_groups=mesh['z'=4,'x'=2,'c'=2,'y'=2] {'x','c','y'}, dimensions={0} | all-to-all | bytes 2097152 | tf_op jit(solution)/shard_map/all_to_all | solution.py:50
  100.4 11.9 %all_to_all.68 = bf16[4,16,1024]{2,1,0:T(8,128)(2,1)S(1)} all-to-all(bf16[4,16,1024]{2,1,0:T(8,128)(2,1)S(1)} %bitcast.99), channel_id=1, replica_groups=mesh['z'=4,'x'=2,'c'=2,'y'=2] {'z'}, dimensions={0} | all-to-all | bytes 262144 | tf_op jit(solution)/shard_map/all_to_all | solution.py:50
  138.2 18.2 %all_to_all.70 = bf16[4,64,2048]{2,1,0:T(8,128)(2,1)} all-to-all(bf16[4,64,2048]{2,1,0:T(8,128)(2,1)S(1)} %bitcast.88), channel_id=1, replica_groups=mesh['z'=4,'x'=2,'c'=2,'y'=2] {'x','y'}, dimensions={0} | all-to-all | bytes 2097152 | tf_op jit(solution)/shard_map/all_to_all | solution.py:50
  170.5 10.0 %collective-permute-done.11.refs_3_ = bf16[128,2048]{1,0:T(8,128)(2,1)S(1)} collective-permute-done((bf16[128,2048]{1,0:T(8,128)(2,1)S(1)}, bf16[128,2048]{1,0:T(8,128)(2,1)S(1)}, u32[]{:S(2)}, u32[]{:S(2)}) %collective-permute-start.11) | collective-permute-done | bytes 524320 | tf_op jit(solution)/shard_map/ppermute | solution.py:46
  184.9 9.2 %collective-permute-done.13.refs_2_ = bf16[128,2048]{1,0:T(8,128)(2,1)S(1)} collective-permute-done((bf16[128,2048]{1,0:T(8,128)(2,1)S(1)}, bf16[128,2048]{1,0:T(8,128)(2,1)S(1)}, u32[]{:S(2)}, u32[]{:S(2)}) %collective-permute-start.13) | collective-permute-done | bytes 524320 | tf_op jit(solution)/shard_map/ppermute | solution.py:46
  268.4 11.9 %feed_up.1 = (bf16[512,2048]{1,0:T(8,128)(2,1)}, bf16[512,2048]{1,0:T(8,128)(2,1)}, f32[512,2048]{1,0:T(8,128)}) custom-call(bf16[128,2048]{1,0:T(8,128)(2,1)S(1)} %copy-done.50, bf16[128,2048]{1,0:T(8,128)(2,1)S(1)} %copy-done.46, bf16[128,2048]{1,0:T(8,128)(2,1)S(1)} %copy-done.44, bf16[64,2048]{1,0:T(8,128)(2,1)S(1)} %copy-done.56, ...), custom_call_target="tpu_custom_call" | custom-call | flops 4294967296 | bytes 12582912 | tf_op jit(solution)/shard_map/feed_up/pallas_call | solution.py:101
  310.1 15.3 %all-gather.11.cloned.1.call-done.down = bf16[2048,2048]{1,0:T(8,128)(2,1)} async-done(((bf16[256,2048]{1,0:T(8,128)(2,1)}), bf16[2048,2048]{1,0:T(8,128)(2,1)}) %all-gather.11.cloned.1.call-update) | async-done | bytes 8388624 | tf_op jit(solution)/shard_map/all_gather | solution.py:84
  326.9 9.9 %feed_down.1.refs_2_ = bf16[512,2048]{1,0:T(8,128)(2,1)S(1)} custom-call(bf16[512,2048]{1,0:T(8,128)(2,1)S(1)} %copy-done.12, f32[512,2048]{1,0:T(8,128)} %get-tuple-element.167.slope_ref, bf16[2048,2048]{1,0:T(8,128)(2,1)} %all-gather.11.cloned.1.call-done.down), custom_call_target="tpu_custom_call" | custom-call | flops 4294967296 | bytes 25165824 | tf_op jit(solution)/shard_map/feed_down/pallas_call | solution.py:101
  336.9 8.9 %convolution_convert_fusion.2 = bf16[512,2048]{1,0:T(8,128)(2,1)S(1)} fusion(bf16[512,2048]{1,0:T(8,128)(2,1)S(1)} %feed_down.1.refs_2_, bf16[2048,2048]{1,0:T(8,128)(2,1)} %all-gather.9.cloned.1.call-done.refs_5_), kind=kOutput, calls=%fused_computation.5 | convolution fusion | flops 4296015872 | bytes 12582912 | tf_op jit(solution)/shard_map/dot_general | solution.py:26
  358.2 10.9 %collective-permute-done.38.refs_2_ = bf16[128,2048]{1,0:T(8,128)(2,1)S(1)} collective-permute-done((bf16[128,2048]{1,0:T(8,128)(2,1)S(1)}, bf16[128,2048]{1,0:T(8,128)(2,1)S(1)}, u32[]{:S(2)}, u32[]{:S(2)}) %collective-permute-start.38) | collective-permute-done | bytes 524320 | tf_op jit(solution)/shard_map/ppermute | solution.py:46
  376.3 9.3 %collective-permute-done.40.refs_2_ = bf16[128,2048]{1,0:T(8,128)(2,1)S(1)} collective-permute-done((bf16[128,2048]{1,0:T(8,128)(2,1)S(1)}, bf16[128,2048]{1,0:T(8,128)(2,1)S(1)}, u32[]{:S(2)}, u32[]{:S(2)}) %collective-permute-start.40) | collective-permute-done | bytes 524320 | tf_op jit(solution)/shard_map/ppermute | solution.py:46
  391.1 8.8 %up_grads.1 = bf16[1024,2048]{1,0:T(8,128)(2,1)} custom-call(s32[1]{0:T(128)} %bitcast.24.r, bf16[512,2048]{1,0:T(8,128)(2,1)} %get-tuple-element.171.refs_0_, bf16[512,2048]{1,0:T(8,128)(2,1)} %collective-permute-done.34.refs_1_, bf16[512,2048]{1,0:T(8,128)(2,1)} %copy-done.20, bf16[512,2048]{1,0:T(8,128)(2,1)} %copy-done.73), custom_call_target="tpu_custom_call" | custom-call | flops 4294967296 | bytes 16777216 | tf_op jit(solution)/shard_map/up_grads/pallas_call | solution.py:112
  427.4 14.5 %all-to-all-done.6 = bf16[8,16,1024]{2,1,0:T(8,128)(2,1)S(1)} async-done(((bf16[8,16,1024]{2,1,0:T(8,128)(2,1)}), bf16[8,16,1024]{2,1,0:T(8,128)(2,1)S(1)}, u32[]{:S(2)}, u32[]{:S(2)}) %all-to-all-start.6) | async-done | bytes 262176 | tf_op jit(solution)/shard_map/all_to_all | solution.py:50
  450.0 11.2 %collective-permute-done.49.refs_2_ = bf16[128,2048]{1,0:T(8,128)(2,1)S(1)} collective-permute-done((bf16[128,2048]{1,0:T(8,128)(2,1)S(1)}, bf16[128,2048]{1,0:T(8,128)(2,1)S(1)}, u32[]{:S(2)}, u32[]{:S(2)}) %collective-permute-start.49) | collective-permute-done | bytes 524320 | tf_op jit(solution)/shard_map/ppermute | solution.py:46
  463.8 13.8 %all_to_all.71 = bf16[4,16,1024]{2,1,0:T(8,128)(2,1)S(1)} all-to-all(bf16[4,16,1024]{2,1,0:T(8,128)(2,1)S(1)} %broadcast_in_dim.11), channel_id=1, replica_groups=mesh['z'=4,'x'=2,'c'=2,'y'=2] {'z'}, dimensions={0} | all-to-all | bytes 262144 | tf_op jit(solution)/shard_map/all_to_all | solution.py:50
  505.7 11.7 %attention_grads.1 = bf16[1024,3072]{1,0:T(8,128)(2,1)} custom-call(s32[1]{0:T(128)} %bitcast.24.r, bf16[512,2048]{1,0:T(8,128)(2,1)} %get-tuple-element.200.refs_0_, bf16[512,2048]{1,0:T(8,128)(2,1)} %collective-permute-done.30.refs_1_, bf16[512,2048]{1,0:T(8,128)(2,1)} %get-tuple-element.202.refs_2_, bf16[512,2048]{1,0:T(8,128)(2,1)} %collective-permute-done.52.refs_3_, ...), custom_call_target="tpu_custom_call" | custom-call | flops 6442450944 | bytes 25165824 | tf_op jit(solution)/shard_map/attention_grads/pallas_call | solution.py:112
  536.2 9.1 %convolution_convert_fusion = bf16[512,2048]{1,0:T(8,128)(2,1)} fusion(bf16[512,2048]{1,0:T(8,128)(2,1)S(1)} %copy-done.72, bf16[2048,2048]{1,0:T(8,128)(2,1)} %all-gather.11.cloned.1.call-done.down), kind=kOutput, calls=%fused_computation.3 | convolution fusion | flops 4296015872 | bytes 12582912 | tf_op jit(solution)/shard_map/dot_general | solution.py:26
  563.4 18.6 %collective-permute-done.62 = bf16[64,2048]{1,0:T(8,128)(2,1)S(1)} collective-permute-done((bf16[64,2048]{1,0:T(8,128)(2,1)S(1)}, bf16[64,2048]{1,0:T(8,128)(2,1)S(1)}, u32[]{:S(2)}, u32[]{:S(2)}) %collective-permute-start.62) | collective-permute-done | bytes 262176 | tf_op jit(solution)/shard_map/ppermute | solution.py:46
  597.1 15.3 %all_to_all.72 = bf16[4,16,1024]{2,1,0:T(8,128)(2,1)S(1)} all-to-all(bf16[4,16,1024]{2,1,0:T(8,128)(2,1)S(1)} %bitcast.100), channel_id=1, replica_groups=mesh['z'=4,'x'=2,'c'=2,'y'=2] {'z'}, dimensions={0} | all-to-all | bytes 262144 | tf_op jit(solution)/shard_map/all_to_all | solution.py:50
  646.2 17.0 %collective-permute-done.69.refs_1_ = bf16[64,3072]{1,0:T(8,128)(2,1)S(1)} collective-permute-done((bf16[64,3072]{1,0:T(8,128)(2,1)S(1)}, bf16[64,3072]{1,0:T(8,128)(2,1)S(1)}, u32[]{:S(2)}, u32[]{:S(2)}) %collective-permute-start.69) | collective-permute-done | bytes 393248 | tf_op jit(solution)/shard_map/ppermute | solution.py:46
  663.8 8.9 %collective-permute-done.71.refs_3_ = bf16[64,3072]{1,0:T(8,128)(2,1)S(1)} collective-permute-done((bf16[64,3072]{1,0:T(8,128)(2,1)S(1)}, bf16[64,3072]{1,0:T(8,128)(2,1)S(1)}, u32[]{:S(2)}, u32[]{:S(2)}) %collective-permute-start.71) | collective-permute-done | bytes 393248 | tf_op jit(solution)/shard_map/ppermute | solution.py:79
  (434 shorter events, 373.2 us)
Async XLA Ops:
  7.2 116.0 %all-gather.5.cloned.1.call-start = ((), (), s32[]{:S(2)}) async-start(), calls=%async_computation.16 | async-start | bytes 9437184 | tf_op jit(solution)/shard_map/all_gather | solution.py:84
  27.5 169.9 %all-gather.7.cloned.1.call-start = ((), (), s32[]{:S(2)}) async-start(), calls=%async_computation.17 | async-start | bytes 4718592 | tf_op jit(solution)/shard_map/all_gather | solution.py:84
  65.2 198.2 %all-gather.9.cloned.1.call-start = ((), (), s32[]{:S(2)}) async-start(), calls=%async_computation.18 | async-start | bytes 9437184 | tf_op jit(solution)/shard_map/all_gather | solution.py:84
  80.7 244.6 %all-gather.11.cloned.1.call-start = ((), (), s32[]{:S(2)}) async-start(), calls=%async_computation.19 | async-start | bytes 9437184 | tf_op jit(solution)/shard_map/all_gather | solution.py:84
  156.3 251.1 %reduce-scatter.4.cloned.1.call-start = ((), (), s32[]{:S(2)}) async-start(), calls=%async_computation.20 | async-start | bytes 5242880 | tf_op jit(solution)/shard_map/reduce_scatter | solution.py:88
  261.2 22.4 %collective-permute-start.24 = (bf16[128,2048]{1,0:T(8,128)(2,1)}, bf16[128,2048]{1,0:T(8,128)(2,1)}, u32[]{:S(2)}, u32[]{:S(2)}) collective-permute-start(bf16[128,2048]{1,0:T(8,128)(2,1)} %get-tuple-element.155.refs_3_), channel_id=1, source_target_pairs={{0,1},{1,0},{2,3},{3,2},{4,5},{5,4},{6,7},{7,6},{8,9},{9,8},{10,11... | collective-permute-start | bytes 1572872 | tf_op jit(solution)/shard_map/ppermute | solution.py:46
  261.5 20.0 %collective-permute-start.25 = (bf16[128,2048]{1,0:T(8,128)(2,1)}, bf16[128,2048]{1,0:T(8,128)(2,1)}, u32[]{:S(2)}, u32[]{:S(2)}) collective-permute-start(bf16[128,2048]{1,0:T(8,128)(2,1)} %get-tuple-element.155.refs_3_), channel_id=1, source_target_pairs={{0,4},{4,0},{1,5},{5,1},{2,6},{6,2},{3,7},{7,3},{8,12},{12,8},{9,1... | collective-permute-start | bytes 1572872 | tf_op jit(solution)/shard_map/ppermute | solution.py:46
  309.8 207.6 %reduce-scatter.6.cloned.1.call-start = ((), (), s32[]{:S(2)}) async-start(), calls=%async_computation.21 | async-start | bytes 5242880 | tf_op jit(solution)/shard_map/reduce_scatter | solution.py:88
  349.0 40.8 %collective-permute-start.43 = (bf16[512,2048]{1,0:T(8,128)(2,1)S(1)}, bf16[512,2048]{1,0:T(8,128)(2,1)S(1)}, u32[]{:S(2)}, u32[]{:S(2)}) collective-permute-start(bf16[512,2048]{1,0:T(8,128)(2,1)S(1)} %feed_down.1.refs_2_), channel_id=1, source_target_pairs={{0,2},{2,0},{1,3},{3,1},{4,6},{6,4},{5,7},{7,5},{8,10},{10,8},{9,1... | collective-permute-start | bytes 6291464 | tf_op jit(solution)/shard_map/ppermute | solution.py:46
  419.3 23.3 %collective-permute-start.47 = (bf16[128,2048]{1,0:T(8,128)(2,1)}, bf16[128,2048]{1,0:T(8,128)(2,1)}, u32[]{:S(2)}, u32[]{:S(2)}) collective-permute-start(bf16[128,2048]{1,0:T(8,128)(2,1)} %pad_maximum_fusion.8), channel_id=1, source_target_pairs={{0,1},{1,0},{2,3},{3,2},{4,5},{5,4},{6,7},{7,6},{8,9},{9,8},{10,11... | collective-permute-start | bytes 1572872 | tf_op jit(solution)/shard_map/ppermute | solution.py:46
  421.5 21.1 %collective-permute-start.45 = (bf16[128,2048]{1,0:T(8,128)(2,1)}, bf16[128,2048]{1,0:T(8,128)(2,1)}, u32[]{:S(2)}, u32[]{:S(2)}) collective-permute-start(bf16[128,2048]{1,0:T(8,128)(2,1)} %pad_maximum_fusion.7), channel_id=1, source_target_pairs={{0,4},{4,0},{1,5},{5,1},{2,6},{6,2},{3,7},{7,3},{8,12},{12,8},{9,1... | collective-permute-start | bytes 1572872 | tf_op jit(solution)/shard_map/ppermute | solution.py:46
  483.7 152.0 %reduce-scatter.8.cloned.1.call-start = ((), (), s32[]{:S(2)}) async-start(), calls=%async_computation.22 | async-start | bytes 7864320 | tf_op jit(solution)/shard_map/reduce_scatter | solution.py:88
  554.8 29.7 %all-to-all-start.9 = ((bf16[8,80,1024]{2,1,0:T(8,128)(2,1)}), bf16[8,80,1024]{2,1,0:T(8,128)(2,1)}, u32[]{:S(2)}, u32[]{:S(2)}) async-start(bf16[8,80,1024]{2,1,0:T(8,128)(2,1)} %copy-done.22), calls=%async_computation.10 | async-start | bytes 2621440 | tf_op jit(solution)/shard_map/all_to_all | solution.py:50
  560.0 22.0 %collective-permute-start.62 = (bf16[64,2048]{1,0:T(8,128)(2,1)S(1)}, bf16[64,2048]{1,0:T(8,128)(2,1)S(1)}, u32[]{:S(2)}, u32[]{:S(2)}) collective-permute-start(bf16[64,2048]{1,0:T(8,128)(2,1)S(1)} %get-tuple-element.251), channel_id=1, source_target_pairs={{0,1},{1,0},{2,3},{3,2},{4,5},{5,4},{6,7},{7,6},{8,9},{9,8},{10,11... | collective-permute-start | bytes 786440 | tf_op jit(solution)/shard_map/ppermute | solution.py:46
  561.9 20.2 %collective-permute-start.64 = (bf16[64,2048]{1,0:T(8,128)(2,1)S(1)}, bf16[64,2048]{1,0:T(8,128)(2,1)S(1)}, u32[]{:S(2)}, u32[]{:S(2)}) collective-permute-start(bf16[64,2048]{1,0:T(8,128)(2,1)S(1)} %get-tuple-element.249), channel_id=1, source_target_pairs={{0,4},{4,0},{1,5},{5,1},{2,6},{6,2},{3,7},{7,3},{8,12},{12,8},{9,1... | collective-permute-start | bytes 786440 | tf_op jit(solution)/shard_map/ppermute | solution.py:46
  583.1 34.1 %collective-permute-start.65 = (bf16[128,2048]{1,0:T(8,128)(2,1)}, bf16[128,2048]{1,0:T(8,128)(2,1)}, u32[]{:S(2)}, u32[]{:S(2)}) collective-permute-start(bf16[128,2048]{1,0:T(8,128)(2,1)} %pad_maximum_fusion.12), channel_id=1, source_target_pairs={{0,1},{1,0},{2,3},{3,2},{4,5},{5,4},{6,7},{7,6},{8,9},{9,8},{10,11... | collective-permute-start | bytes 1572872 | tf_op jit(solution)/shard_map/ppermute | solution.py:46
  588.7 32.6 %collective-permute-start.63 = (bf16[128,2048]{1,0:T(8,128)(2,1)}, bf16[128,2048]{1,0:T(8,128)(2,1)}, u32[]{:S(2)}, u32[]{:S(2)}) collective-permute-start(bf16[128,2048]{1,0:T(8,128)(2,1)} %pad_maximum_fusion.11), channel_id=1, source_target_pairs={{0,4},{4,0},{1,5},{5,1},{2,6},{6,2},{3,7},{7,3},{8,12},{12,8},{9,1... | collective-permute-start | bytes 1572872 | tf_op jit(solution)/shard_map/ppermute | solution.py:46
  592.6 39.4 %collective-permute-start.66 = (bf16[64,4096]{1,0:T(8,128)(2,1)}, bf16[64,4096]{1,0:T(8,128)(2,1)S(1)}, u32[]{:S(2)}, u32[]{:S(2)}) collective-permute-start(bf16[64,4096]{1,0:T(8,128)(2,1)} %get-tuple-element.224), channel_id=1, source_target_pairs={{0,1},{1,0},{2,3},{3,2},{4,5},{5,4},{6,7},{7,6},{8,9},{9,8},{10,11... | collective-permute-start | bytes 1572872 | tf_op jit(solution)/shard_map/ppermute | solution.py:46
  594.0 38.0 %collective-permute-start.67 = (bf16[64,4096]{1,0:T(8,128)(2,1)}, bf16[64,4096]{1,0:T(8,128)(2,1)}, u32[]{:S(2)}, u32[]{:S(2)}) collective-permute-start(bf16[64,4096]{1,0:T(8,128)(2,1)} %get-tuple-element.225), channel_id=1, source_target_pairs={{0,4},{4,0},{1,5},{5,1},{2,6},{6,2},{3,7},{7,3},{8,12},{12,8},{9,1... | collective-permute-start | bytes 1572872 | tf_op jit(solution)/shard_map/ppermute | solution.py:46
  594.7 37.4 %collective-permute-start.68 = (bf16[64,4096]{1,0:T(8,128)(2,1)}, bf16[64,4096]{1,0:T(8,128)(2,1)}, u32[]{:S(2)}, u32[]{:S(2)}) collective-permute-start(bf16[64,4096]{1,0:T(8,128)(2,1)} %get-tuple-element.226), channel_id=1, source_target_pairs={{0,5},{1,4},{4,1},{5,0},{2,7},{3,6},{6,3},{7,2},{8,13},{9,12},{12,... | collective-permute-start | bytes 1572872 | tf_op jit(solution)/shard_map/ppermute | solution.py:79
  613.1 22.6 %all-to-all-start.11 = ((bf16[4,16,1024]{2,1,0:T(8,128)(2,1)}), bf16[4,16,1024]{2,1,0:T(8,128)(2,1)S(1)}, u32[]{:S(2)}, u32[]{:S(2)}) async-start(bf16[4,16,1024]{2,1,0:T(8,128)(2,1)} %broadcast_in_dim.13), calls=%async_computation.12 | async-start | bytes 262144 | tf_op jit(solution)/shard_map/all_to_all | solution.py:50
  636.9 38.4 %all-to-all-start.12 = ((bf16[8,64,1024]{2,1,0:T(8,128)(2,1)}), bf16[8,64,1024]{2,1,0:T(8,128)(2,1)S(1)}, u32[]{:S(2)}, u32[]{:S(2)}) async-start(bf16[8,64,1024]{2,1,0:T(8,128)(2,1)} %broadcast_in_dim.14), calls=%async_computation.15 | async-start | bytes 2097152 | tf_op jit(solution)/shard_map/all_to_all | solution.py:50
  642.0 21.2 %collective-permute-start.69 = (bf16[64,3072]{1,0:T(8,128)(2,1)S(1)}, bf16[64,3072]{1,0:T(8,128)(2,1)S(1)}, u32[]{:S(2)}, u32[]{:S(2)}) collective-permute-start(bf16[64,3072]{1,0:T(8,128)(2,1)S(1)} %get-tuple-element.235), channel_id=1, source_target_pairs={{0,1},{1,0},{2,3},{3,2},{4,5},{5,4},{6,7},{7,6},{8,9},{9,8},{10,11... | collective-permute-start | bytes 1179656 | tf_op jit(solution)/shard_map/ppermute | solution.py:46
  645.5 27.1 %collective-permute-start.71 = (bf16[64,3072]{1,0:T(8,128)(2,1)S(1)}, bf16[64,3072]{1,0:T(8,128)(2,1)S(1)}, u32[]{:S(2)}, u32[]{:S(2)}) collective-permute-start(bf16[64,3072]{1,0:T(8,128)(2,1)S(1)} %get-tuple-element.237), channel_id=1, source_target_pairs={{0,5},{1,4},{4,1},{5,0},{2,7},{3,6},{6,3},{7,2},{8,13},{9,12},{12,... | collective-permute-start | bytes 1179656 | tf_op jit(solution)/shard_map/ppermute | solution.py:79
  (135 other events, 1561.0 us)
Sparse Core Ops, SparseCore 0:
  27.6 83.6 all-gather.4
  112.9 47.9 all-gather.6
  162.5 80.7 all-gather.8
  244.7 80.5 all-gather.10
  327.5 75.2 reduce-scatter.3
  407.6 81.0 reduce-scatter.5
  517.6 115.8 reduce-scatter.7

commit v16 on v12

--- a/solution.py
+++ b/solution.py
@@ -61,14 +61,25 @@
     return own, from_y, from_x, swap(from_x[:half], "y"), swap(from_y[half:], "x")
 
 
-def scatter_tokens(parts):
+def scatter_first(parts):
     own, for_y, for_x, for_low, for_high = parts
     half = for_low.shape[0]
     low = swap(for_low, "y").astype(F32) + for_x[:half].astype(F32)
     high = swap(for_high, "x").astype(F32) + for_y[half:].astype(F32)
-    from_x = swap(jnp.concatenate([low.astype(BF), for_x[half:]], axis=0), "x")
-    from_y = swap(jnp.concatenate([for_y[:half], high.astype(BF)], axis=0), "y")
-    return [own, from_x, from_y]
+    return (
+        own,
+        jnp.concatenate([low.astype(BF), for_x[half:]], axis=0),
+        jnp.concatenate([for_y[:half], high.astype(BF)], axis=0),
+    )
+
+
+def scatter_second(parts):
+    own, for_x, for_y = parts
+    return [own, swap(for_x, "x"), swap(for_y, "y")]
+
+
+def scatter_tokens(parts):
+    return scatter_second(scatter_first(parts))
 
 
 def swap_parts(parts):
@@ -168,10 +179,13 @@
 
 
 def mm_scatter(values, weight):
-    partial = mm_t(values, weight).astype(BF)
+    return scatter_tokens(token_blocks(mm_t(values, weight).astype(BF)))
+
+
+def token_blocks(partial):
     rows = partial.shape[0] // 4
     cuts = [0, rows, 2 * rows, 3 * rows, 3 * rows + rows // 2, 4 * rows]
-    return scatter_tokens([partial[a:b] for a, b in zip(cuts, cuts[1:])])
+    return [partial[a:b] for a, b in zip(cuts, cuts[1:])]
 
 
 def normalize(values):
@@ -630,24 +644,21 @@
 
 
 def finish_wide(parts, rank):
-    rows, total = parts[0].shape
-    width = total // 2
+    rows, width = parts[0].shape
 
     def kernel(r, *refs):
         for k in range(4):
 
             @pl.when(pl.program_id(0) == k)
             def _():
-                refs[4][...] = refs[k][:, :width].astype(F32)
-                refs[5][...] = refs[k][:, width:].astype(F32)
-
-    flat = pl.BlockSpec((rows, width), lambda k, r: (0, k ^ r[0]))
+                refs[4][...] = refs[k][...].astype(F32)
+
     return call(
         kernel,
         (4,),
         [whole(p) for p in parts],
-        [flat, flat],
-        [shape((rows, 4 * width), F32)] * 2,
+        pl.BlockSpec((rows, width), lambda k, r: (0, k ^ r[0])),
+        shape((rows, 4 * width), F32),
         parts,
         "finish_wide",
         rank=rank,
@@ -723,13 +734,12 @@
     )
 
 
-def text_back(blocks, own_text, w_cross, caption, w_text, extra):
+def text_back(blocks, own_text, w_cross, caption, w_text):
     context, rows = own_text.shape
     half, width = context // 2, w_cross.shape[2] // 4
     wide = caption.shape[1] // 4
-    tail = extra.shape[0]
-
-    def kernel(block, own, cross, cap, weight, more, kv_grad, text_grad, out, grads):
+
+    def kernel(block, own, cross, cap, weight, kv_grad, text_grad, out, grads):
         for k in range(8):
             core, group = plane_block(k)
             for j in range(2):
@@ -745,14 +755,13 @@
         part = mm(grad_text, weight[...]).astype(BF)
         for k in range(8):
             core, group = plane_block(k)
-            out[k, :half, :] = part[core * half : (core + 1) * half, group * wide : (group + 1) * wide]
-            out[k, half:, :] = more[...]
-
-    operands = [blocks, own_text, w_cross, caption, w_text, extra]
+            out[k] = part[core * half : (core + 1) * half, group * wide : (group + 1) * wide]
+
+    operands = [blocks, own_text, w_cross, caption, w_text]
     outs = [
         shape((rows, 8 * width), F32),
         shape((rows, 4 * wide), F32),
-        shape((8, half + tail, wide)),
+        shape((8, half, wide)),
     ]
     return call(
         kernel,
@@ -766,8 +775,8 @@
     )
 
 
-def caption_output(blocks):
-    count, half, wide = blocks.shape
+def caption_output(blocks, half):
+    count, _, wide = blocks.shape
 
     def kernel(block, out):
         out[...] = block[0].astype(F32)
@@ -955,47 +964,67 @@
             "attention_grads",
             *halves,
         )
-        grad_projected, activated, kv_grad, rest_part = lax.optimization_barrier(
-            (grad_projected, activated, kv_grad, rest_part)
+        kv_part = kv_grad.astype(BF).reshape(2, z_size, -1, 2 * group)
+        kv_part = kv_part.transpose(1, 0, 2, 3).reshape(2 * z_size, -1, 2 * group)
+        grad_projected, activated, kv_part, rest_part = lax.optimization_barrier(
+            (grad_projected, activated, kv_part, rest_part)
         )
         rest_part, up_rows = lax.optimization_barrier((rest_part, up_rows))
         rest_rows = scatter_grad(rest_part, grad_axes)
-        parts = mm_scatter(grad_projected, first[:, : 3 * group])
+
+        kv_part = trade(kv_part, DATA).astype(F32).sum(axis=0).astype(BF)
+        grad_attn = mm_t(grad_projected, first[:, : 3 * group]).astype(BF)
+        down_parts = swap_parts(pick_rows([down_rows], rank))
+        kv_part, grad_attn, down_parts, activated = lax.optimization_barrier(
+            (kv_part, grad_attn, down_parts, activated)
+        )
+
+        kv_part = spread(kv_part, "z", z_size).reshape(-1, 2 * group)
+        grad_attn = scatter_first(token_blocks(grad_attn))
+        result = mm_t(activated, down).astype(BF)
+        kv_part, grad_attn, result = lax.optimization_barrier((kv_part, grad_attn, result))
+
+        kv_grads = spread(kv_part, PLANE, 8)
+        grad_attn = scatter_second(grad_attn)
+        result = scatter_first(token_blocks(result))
+        kv_grads, grad_attn, result = lax.optimization_barrier((kv_grads, grad_attn, result))
+
+        kv_weight_grad, grad_text_w, caption_part = text_back(
+            kv_grads, own_text, w_cross, caption, w_text
+        )
+        caption_part = trade(caption_part, PLANE).astype(F32).sum(axis=0).astype(BF)
         grad_hidden, gain_grad_a, mask_grad = last_back(
-            parts,
-            grad_after_attn,
-            start_x,
-            gain_a,
-            masked,
-            unit,
-            order,
+            grad_attn, grad_after_attn, start_x, gain_a, masked, unit, order
         )
         sums = jnp.concatenate([gain_grad_a, gain_grad_b, gain_grad_c, mask_grad], axis=0)
-
-        parts = mm_scatter(activated, down)
-        output = layer_output(after_cross, parts, unit, order)
-
-        kv_halves = kv_grad.reshape(2, -1, 2 * group)
-        kv_keep = lax.dynamic_index_in_dim(kv_halves, core, 0, keepdims=False)
-        kv_send = lax.dynamic_index_in_dim(kv_halves, 1 - core, 0, keepdims=False)
-        kv_sum = sum_z((kv_keep + swap(kv_send, "c")).astype(BF))
-        wide_rows = swap_parts(pick_rows([down_rows, up_rows], rank))
-        kv_sum, wide_rows = lax.optimization_barrier((kv_sum, wide_rows))
-        kv_grads = spread(kv_sum, PLANE, 8)
-        down_grad, up_grad = finish_wide(wide_rows, rank)
-        kv_weight_grad, grad_text_w, caption_part = text_back(
-            kv_grads, own_text, w_cross, caption, w_text, halves_of(sums, text_width // 4)
-        )
+        result = scatter_second(result)
+        caption_part, sums, result, up_rows = lax.optimization_barrier(
+            (caption_part, sums, result, up_rows)
+        )
+
+        caption_part = caption_part.reshape(z_size, -1, text_width // 4)
+        caption_part = trade(caption_part, "z").astype(F32).sum(axis=0).astype(BF)
+        output = layer_output(after_cross, result, unit, order)
+        up_parts = swap_parts(pick_rows([up_rows], rank))
+        caption_part, output, up_parts = lax.optimization_barrier((caption_part, output, up_parts))
+
         half_context = caption.shape[0] // 2
-        caption_part = trade(caption_part, PLANE).astype(F32).sum(axis=0)
-        sums = layer_order(add_z(whole_of(caption_part[half_context:], width)))
-        caption_part = sum_z(caption_part[:half_context].astype(BF))
+        caption_part = spread(caption_part, "z", z_size).reshape(half_context, -1)
+        down_grad, up_grad = finish_wide(down_parts, rank), finish_wide(up_parts, rank)
+        caption_part, down_grad, up_grad = lax.optimization_barrier(
+            (caption_part, down_grad, up_grad)
+        )
+
+        caption_part = jnp.concatenate([caption_part, halves_of(sums, text_width // 4)], axis=0)
+        caption_part = spread(caption_part, PLANE, 8)
         caption_part, rest_rows = lax.optimization_barrier((caption_part, rest_rows))
-        grad_caption = caption_output(spread(caption_part, PLANE, 8))
 
         qkv_grad, out_grad, grad_cross, cross_out_grad = finish_all(
             swap_parts(pick_rows([rest_rows], rank)), kv_weight_grad, rank
         )
+        sums = whole_of(caption_part[:, half_context:].astype(F32).sum(axis=0), width)
+        sums = layer_order(add_z(sums))
+        grad_caption = caption_output(caption_part, half_context)
         return (
             outer(output).reshape(hidden.shape),
             outer(grad_hidden).reshape(hidden.shape),

time: 678 us -> 705 us (1.040)
  waiting for transfers between devices: 224 us -> 239 us
  blocking collectives: 93.3 us -> 101 us
    ppermute x68 -> x69, waiting for transfers between devices: 169 us -> 181 us  [swap(): return lax.ppermute(values, axis, PAIR)]
    all_to_all x7, blocking collectives: 93.3 us -> 101 us  [trade(): return lax.all_to_all(blocks, axes, 0, 0, tiled=True)]
    ppermute x68 -> x69, starting transfers between devices: 70.4 us -> 73.2 us  [swap(): return lax.ppermute(values, axis, PAIR)]
    pallas_call x9 -> x11, Pallas kernels: 40.1 us -> 42.7 us  [call(): pl.pallas_call(kernel, grid_spec=spec, **options)]
    unnamed x184 -> x186, local copies, waits for them, and re-layouts: 46.6 us -> 45.2 us
  transfers between devices with their start and end apart: 86 -> 88, of which waited for: 50 -> 48; matrix products, arithmetic and copies ran while one was open for 11% -> 11% of each run, Pallas kernels for 17% -> 16%
where the time goes in v16:
time: 705 us; the launch traced here: 697 us
  waiting for transfers between devices  239 us (34%)
  Pallas kernels  116 us (16%)
  starting transfers between devices  104 us (15%)
  blocking collectives  101 us (14%)
  local copies, waits for them, and re-layouts  72.9 us (10%)
  matrix products  33.6 us (5%)
  between operations  16.3 us (2%)
  other arithmetic  13.7 us (2%)
    ppermute x69, waiting for transfers between devices, swap(): return lax.ppermute(values, axis, PAIR)  181 us
    all_to_all x7, blocking collectives, trade(): return lax.all_to_all(blocks, axes, 0, 0, tiled=True)  101 us
    pallas_call x20, Pallas kernels, call(): pl.pallas_call(kernel, grid=grid, in_specs=in_specs, out_specs=out_specs,...  73.6 us
    ppermute x69, starting transfers between devices, swap(): return lax.ppermute(values, axis, PAIR)  73.2 us
    unnamed x186, local copies, waits for them, and re-layouts  45.2 us
    pallas_call x11, Pallas kernels, call(): pl.pallas_call(kernel, grid_spec=spec, **options)  42.7 us
    dot_general x6, matrix products, dot(): return lax.dot_general(a, b, (dims, ((), ())), preferred_element_type=F32)  33.6 us
    all_to_all x6, waiting for transfers between devices, trade(): return lax.all_to_all(blocks, axes, 0, 0, tiled=True)  26.1 us
  transfers between devices with their start and end apart: 88, of which 48 were waited for; matrix products, arithmetic and copies ran while one was open for 11% of the time, Pallas kernels for 16%

profile of v16, /device:TPU:0, one launch (start us, length us, event | category | flops | bytes accessed | tf_op | source)
XLA Modules:
  0.0 696.6 jit_solution(6538180482562530546)
XLA Ops:
  34.6 8.8 %collective-permute-done.1.refs_2_ = bf16[128,2048]{1,0:T(8,128)(2,1)S(1)} collective-permute-done((bf16[128,2048]{1,0:T(8,128)(2,1)S(1)}, bf16[128,2048]{1,0:T(8,128)(2,1)S(1)}, u32[]{:S(2)}, u32[]{:S(2)}) %collective-permute-start.1) | collective-permute-done | bytes 524320 | tf_op jit(solution)/shard_map/ppermute | solution.py:46
  55.0 10.2 %all_to_all.65 = bf16[4,64,1024]{2,1,0:T(8,128)(2,1)} all-to-all(bf16[4,64,1024]{2,1,0:T(8,128)(2,1)S(1)} %copy.75), channel_id=1, replica_groups=mesh['z'=4,'x'=2,'c'=2,'y'=2] {'x','y'}, dimensions={0} | all-to-all | bytes 1048576 | tf_op jit(solution)/shard_map/all_to_all | solution.py:50
  65.3 15.5 %all_to_all.66 = bf16[4,64,2048]{2,1,0:T(8,128)(2,1)} all-to-all(bf16[4,64,2048]{2,1,0:T(8,128)(2,1)} %bitcast.88), channel_id=1, replica_groups=mesh['z'=4,'x'=2,'c'=2,'y'=2] {'x','y'}, dimensions={0} | all-to-all | bytes 2097152 | tf_op jit(solution)/shard_map/all_to_all | solution.py:50
  83.4 16.9 %all_to_all.67 = bf16[8,64,1024]{2,1,0:T(8,128)(2,1)S(1)} all-to-all(bf16[8,64,1024]{2,1,0:T(8,128)(2,1)S(1)} %get-tuple-element.156), channel_id=1, replica_groups=mesh['z'=4,'x'=2,'c'=2,'y'=2] {'x','c','y'}, dimensions={0} | all-to-all | bytes 2097152 | tf_op jit(solution)/shard_map/all_to_all | solution.py:50
  100.4 11.5 %all_to_all.68 = bf16[4,16,1024]{2,1,0:T(8,128)(2,1)S(1)} all-to-all(bf16[4,16,1024]{2,1,0:T(8,128)(2,1)S(1)} %bitcast.98), channel_id=1, replica_groups=mesh['z'=4,'x'=2,'c'=2,'y'=2] {'z'}, dimensions={0} | all-to-all | bytes 262144 | tf_op jit(solution)/shard_map/all_to_all | solution.py:50
  112.0 8.8 %all_to_all.69 = bf16[4,16,1024]{2,1,0:T(8,128)(2,1)S(1)} all-to-all(bf16[4,16,1024]{2,1,0:T(8,128)(2,1)S(1)} %broadcast_in_dim.10), channel_id=1, replica_groups=mesh['z'=4,'x'=2,'c'=2,'y'=2] {'z'}, dimensions={0} | all-to-all | bytes 262144 | tf_op jit(solution)/shard_map/all_to_all | solution.py:50
  127.2 7.9 %qkv_mm.1 = (bf16[512,2048]{1,0:T(8,128)(2,1)}, bf16[512,1536]{1,0:T(8,128)(2,1)S(1)}) custom-call(bf16[128,2048]{1,0:T(8,128)(2,1)S(1)} %copy-done.63, bf16[128,2048]{1,0:T(8,128)(2,1)S(1)} %copy-done.57, bf16[128,2048]{1,0:T(8,128)(2,1)S(1)} %collective-permute-done.1.refs_2_, bf16[64,2048]{1,0:T(8,128)(2,1)S(1)} %copy-done.67, ...), custom_call_target="tpu_custom_call" | custom-call | flops 3221225472 | bytes 10485760 | tf_op jit(solution)/shard_map/qkv_mm/pallas_call | solution.py:112
  138.1 18.2 %all_to_all.70 = bf16[4,64,2048]{2,1,0:T(8,128)(2,1)} all-to-all(bf16[4,64,2048]{2,1,0:T(8,128)(2,1)S(1)} %bitcast.87), channel_id=1, replica_groups=mesh['z'=4,'x'=2,'c'=2,'y'=2] {'x','y'}, dimensions={0} | all-to-all | bytes 2097152 | tf_op jit(solution)/shard_map/all_to_all | solution.py:50
  170.8 10.0 %collective-permute-done.11.refs_3_ = bf16[128,2048]{1,0:T(8,128)(2,1)S(1)} collective-permute-done((bf16[128,2048]{1,0:T(8,128)(2,1)S(1)}, bf16[128,2048]{1,0:T(8,128)(2,1)S(1)}, u32[]{:S(2)}, u32[]{:S(2)}) %collective-permute-start.11) | collective-permute-done | bytes 524320 | tf_op jit(solution)/shard_map/ppermute | solution.py:46
  185.2 9.3 %collective-permute-done.13.refs_2_ = bf16[128,2048]{1,0:T(8,128)(2,1)S(1)} collective-permute-done((bf16[128,2048]{1,0:T(8,128)(2,1)S(1)}, bf16[128,2048]{1,0:T(8,128)(2,1)S(1)}, u32[]{:S(2)}, u32[]{:S(2)}) %collective-permute-start.13) | collective-permute-done | bytes 524320 | tf_op jit(solution)/shard_map/ppermute | solution.py:46
  268.9 11.9 %feed_up.1 = (bf16[512,2048]{1,0:T(8,128)(2,1)}, bf16[512,2048]{1,0:T(8,128)(2,1)}, f32[512,2048]{1,0:T(8,128)}) custom-call(bf16[128,2048]{1,0:T(8,128)(2,1)S(1)} %copy-done.65, bf16[128,2048]{1,0:T(8,128)(2,1)S(1)} %copy-done.61, bf16[128,2048]{1,0:T(8,128)(2,1)S(1)} %copy-done.59, bf16[64,2048]{1,0:T(8,128)(2,1)S(1)} %copy-done.71, ...), custom_call_target="tpu_custom_call" | custom-call | flops 4294967296 | bytes 12582912 | tf_op jit(solution)/shard_map/feed_up/pallas_call | solution.py:112
  300.1 8.7 %down_grads.1 = bf16[1024,2048]{1,0:T(8,128)(2,1)} custom-call(s32[1]{0:T(128)} %bitcast.24.r, bf16[512,2048]{1,0:T(8,128)(2,1)S(1)} %constant_dynamic-update-slice_fusion.refs_0_.dy, bf16[512,2048]{1,0:T(8,128)(2,1)S(1)} %collective-permute-done.28.refs_1_, bf16[512,2048]{1,0:T(8,128)(2,1)} %get-tuple-element.228.refs_2_, bf16[512,2048]{1,0:T(8,128)(2,1)} %copy-done.90), custom_call_target="tpu_custom_call" | custom-call | flops 4294967296 | bytes 16777216 | tf_op jit(solution)/shard_map/down_grads/pallas_call | solution.py:123
  310.4 15.0 %all-gather.11.cloned.1.call-done.down = bf16[2048,2048]{1,0:T(8,128)(2,1)} async-done(((bf16[256,2048]{1,0:T(8,128)(2,1)}), bf16[2048,2048]{1,0:T(8,128)(2,1)}) %all-gather.11.cloned.1.call-update) | async-done | bytes 8388624 | tf_op jit(solution)/shard_map/all_gather | solution.py:95
  326.9 9.9 %feed_down.1.refs_2_ = bf16[512,2048]{1,0:T(8,128)(2,1)S(1)} custom-call(bf16[512,2048]{1,0:T(8,128)(2,1)S(1)} %copy-done.16, f32[512,2048]{1,0:T(8,128)} %get-tuple-element.188.slope_ref, bf16[2048,2048]{1,0:T(8,128)(2,1)} %all-gather.11.cloned.1.call-done.down), custom_call_target="tpu_custom_call" | custom-call | flops 4294967296 | bytes 25165824 | tf_op jit(solution)/shard_map/feed_down/pallas_call | solution.py:112
  336.9 8.9 %convolution_convert_fusion.2 = bf16[512,2048]{1,0:T(8,128)(2,1)S(1)} fusion(bf16[512,2048]{1,0:T(8,128)(2,1)S(1)} %feed_down.1.refs_2_, bf16[2048,2048]{1,0:T(8,128)(2,1)} %all-gather.9.cloned.1.call-done.refs_5_), kind=kOutput, calls=%fused_computation.5 | convolution fusion | flops 4296015872 | bytes 12582912 | tf_op jit(solution)/shard_map/dot_general | solution.py:26
  358.2 10.9 %collective-permute-done.38.refs_2_ = bf16[128,2048]{1,0:T(8,128)(2,1)S(1)} collective-permute-done((bf16[128,2048]{1,0:T(8,128)(2,1)S(1)}, bf16[128,2048]{1,0:T(8,128)(2,1)S(1)}, u32[]{:S(2)}, u32[]{:S(2)}) %collective-permute-start.38) | collective-permute-done | bytes 524320 | tf_op jit(solution)/shard_map/ppermute | solution.py:46
  376.3 9.2 %collective-permute-done.40.refs_2_ = bf16[128,2048]{1,0:T(8,128)(2,1)S(1)} collective-permute-done((bf16[128,2048]{1,0:T(8,128)(2,1)S(1)}, bf16[128,2048]{1,0:T(8,128)(2,1)S(1)}, u32[]{:S(2)}, u32[]{:S(2)}) %collective-permute-start.40) | collective-permute-done | bytes 524320 | tf_op jit(solution)/shard_map/ppermute | solution.py:46
  391.1 8.8 %up_grads.1 = bf16[1024,2048]{1,0:T(8,128)(2,1)} custom-call(s32[1]{0:T(128)} %bitcast.24.r, bf16[512,2048]{1,0:T(8,128)(2,1)} %get-tuple-element.192.refs_0_, bf16[512,2048]{1,0:T(8,128)(2,1)} %collective-permute-done.34.refs_1_, bf16[512,2048]{1,0:T(8,128)(2,1)} %copy-done.26, bf16[512,2048]{1,0:T(8,128)(2,1)} %copy-done.89), custom_call_target="tpu_custom_call" | custom-call | flops 4294967296 | bytes 16777216 | tf_op jit(solution)/shard_map/up_grads/pallas_call | solution.py:123
  434.5 11.7 %collective-permute-done.49.refs_2_ = bf16[128,2048]{1,0:T(8,128)(2,1)S(1)} collective-permute-done((bf16[128,2048]{1,0:T(8,128)(2,1)S(1)}, bf16[128,2048]{1,0:T(8,128)(2,1)S(1)}, u32[]{:S(2)}, u32[]{:S(2)}) %collective-permute-start.49) | collective-permute-done | bytes 524320 | tf_op jit(solution)/shard_map/ppermute | solution.py:46
  468.3 11.8 %attention_grads.1 = bf16[1024,3072]{1,0:T(8,128)(2,1)} custom-call(s32[1]{0:T(128)} %bitcast.24.r, bf16[512,2048]{1,0:T(8,128)(2,1)} %get-tuple-element.208.refs_0_, bf16[512,2048]{1,0:T(8,128)(2,1)} %collective-permute-done.30.refs_1_, bf16[512,2048]{1,0:T(8,128)(2,1)} %copy-done.27, bf16[512,2048]{1,0:T(8,128)(2,1)} %copy-done.78, ...), custom_call_target="tpu_custom_call" | custom-call | flops 6442450944 | bytes 25165824 | tf_op jit(solution)/shard_map/attention_grads/pallas_call | solution.py:123
  513.9 10.0 %convolution_convert_fusion = bf16[512,2048]{1,0:T(8,128)(2,1)} fusion(bf16[512,2048]{1,0:T(8,128)(2,1)} %get-tuple-element.228.refs_2_, bf16[2048,2048]{1,0:T(8,128)(2,1)} %all-gather.11.cloned.1.call-done.down), kind=kOutput, calls=%fused_computation.3 | convolution fusion | flops 4296015872 | bytes 12582912 | tf_op jit(solution)/shard_map/dot_general | solution.py:26
  557.1 18.3 %collective-permute-done.61.refs_1_ = bf16[128,2048]{1,0:T(8,128)(2,1)S(1)} collective-permute-done((bf16[128,2048]{1,0:T(8,128)(2,1)}, bf16[128,2048]{1,0:T(8,128)(2,1)S(1)}, u32[]{:S(2)}, u32[]{:S(2)}) %collective-permute-start.61) | collective-permute-done | bytes 524320 | tf_op jit(solution)/shard_map/ppermute | solution.py:46
  606.0 8.7 %collective-permute-done.65.refs_1_ = bf16[128,2048]{1,0:T(8,128)(2,1)} collective-permute-done((bf16[128,2048]{1,0:T(8,128)(2,1)}, bf16[128,2048]{1,0:T(8,128)(2,1)}, u32[]{:S(2)}, u32[]{:S(2)}) %collective-permute-start.65) | collective-permute-done | bytes 524320 | tf_op jit(solution)/shard_map/ppermute | solution.py:46
  642.0 20.1 %all_to_all.71.block = bf16[8,80,1024]{2,1,0:T(8,128)(2,1)S(1)} all-to-all(bf16[8,80,1024]{2,1,0:T(8,128)(2,1)S(1)} %broadcast_in_dim.14), channel_id=1, replica_groups=mesh['z'=4,'x'=2,'c'=2,'y'=2] {'x','c','y'}, dimensions={0} | all-to-all | bytes 2621440 | tf_op jit(solution)/shard_map/all_to_all | solution.py:50
  (477 shorter events, 399.5 us)
Async XLA Ops:
  7.2 116.0 %all-gather.5.cloned.1.call-start = ((), (), s32[]{:S(2)}) async-start(), calls=%async_computation.16 | async-start | bytes 9437184 | tf_op jit(solution)/shard_map/all_gather | solution.py:95
  27.5 170.5 %all-gather.7.cloned.1.call-start = ((), (), s32[]{:S(2)}) async-start(), calls=%async_computation.17 | async-start | bytes 4718592 | tf_op jit(solution)/shard_map/all_gather | solution.py:95
  65.2 198.6 %all-gather.9.cloned.1.call-start = ((), (), s32[]{:S(2)}) async-start(), calls=%async_computation.18 | async-start | bytes 9437184 | tf_op jit(solution)/shard_map/all_gather | solution.py:95
  80.8 244.6 %all-gather.11.cloned.1.call-start = ((), (), s32[]{:S(2)}) async-start(), calls=%async_computation.19 | async-start | bytes 9437184 | tf_op jit(solution)/shard_map/all_gather | solution.py:95
  156.3 251.1 %reduce-scatter.4.cloned.1.call-start = ((), (), s32[]{:S(2)}) async-start(), calls=%async_computation.20 | async-start | bytes 5242880 | tf_op jit(solution)/shard_map/reduce_scatter | solution.py:99
  261.6 22.4 %collective-permute-start.24 = (bf16[128,2048]{1,0:T(8,128)(2,1)}, bf16[128,2048]{1,0:T(8,128)(2,1)}, u32[]{:S(2)}, u32[]{:S(2)}) collective-permute-start(bf16[128,2048]{1,0:T(8,128)(2,1)} %get-tuple-element.176.refs_3_), channel_id=1, source_target_pairs={{0,1},{1,0},{2,3},{3,2},{4,5},{5,4},{6,7},{7,6},{8,9},{9,8},{10,11... | collective-permute-start | bytes 1572872 | tf_op jit(solution)/shard_map/ppermute | solution.py:46
  261.9 20.1 %collective-permute-start.25 = (bf16[128,2048]{1,0:T(8,128)(2,1)}, bf16[128,2048]{1,0:T(8,128)(2,1)}, u32[]{:S(2)}, u32[]{:S(2)}) collective-permute-start(bf16[128,2048]{1,0:T(8,128)(2,1)} %get-tuple-element.176.refs_3_), channel_id=1, source_target_pairs={{0,4},{4,0},{1,5},{5,1},{2,6},{6,2},{3,7},{7,3},{8,12},{12,8},{9,1... | collective-permute-start | bytes 1572872 | tf_op jit(solution)/shard_map/ppermute | solution.py:46
  310.2 172.2 %reduce-scatter.6.cloned.1.call-start = ((), (), s32[]{:S(2)}) async-start(), calls=%async_computation.21 | async-start | bytes 5242880 | tf_op jit(solution)/shard_map/reduce_scatter | solution.py:99
  349.0 40.8 %collective-permute-start.43 = (bf16[512,2048]{1,0:T(8,128)(2,1)S(1)}, bf16[512,2048]{1,0:T(8,128)(2,1)S(1)}, u32[]{:S(2)}, u32[]{:S(2)}) collective-permute-start(bf16[512,2048]{1,0:T(8,128)(2,1)S(1)} %feed_down.1.refs_2_), channel_id=1, source_target_pairs={{0,2},{2,0},{1,3},{3,1},{4,6},{6,4},{5,7},{7,5},{8,10},{10,8},{9,1... | collective-permute-start | bytes 6291464 | tf_op jit(solution)/shard_map/ppermute | solution.py:46
  408.2 253.9 %reduce-scatter.8.cloned.1.call-start = ((), (), s32[]{:S(2)}) async-start(), calls=%async_computation.22 | async-start | bytes 7864320 | tf_op jit(solution)/shard_map/reduce_scatter | solution.py:99
  448.1 17.0 %collective-permute-start.53 = (bf16[512,2048]{1,0:T(8,128)(2,1)S(1)}, bf16[512,2048]{1,0:T(8,128)(2,1)S(1)}, u32[]{:S(2)}, u32[]{:S(2)}) collective-permute-start(bf16[512,2048]{1,0:T(8,128)(2,1)S(1)} %copy-done.25), channel_id=1, source_target_pairs={{0,2},{2,0},{1,3},{3,1},{4,6},{6,4},{5,7},{7,5},{8,10},{10,8},{9,1... | collective-permute-start | bytes 6291464 | tf_op jit(solution)/shard_map/ppermute | solution.py:46
  484.7 24.0 %collective-permute-start.56 = (bf16[64,2048]{1,0:T(8,128)(2,1)}, bf16[64,2048]{1,0:T(8,128)(2,1)S(1)}, u32[]{:S(2)}, u32[]{:S(2)}) collective-permute-start(bf16[64,2048]{1,0:T(8,128)(2,1)} %get-tuple-element.222), channel_id=1, source_target_pairs={{0,1},{1,0},{2,3},{3,2},{4,5},{5,4},{6,7},{7,6},{8,9},{9,8},{10,11... | collective-permute-start | bytes 786440 | tf_op jit(solution)/shard_map/ppermute | solution.py:46
  486.1 22.5 %collective-permute-start.57 = (bf16[64,2048]{1,0:T(8,128)(2,1)}, bf16[64,2048]{1,0:T(8,128)(2,1)S(1)}, u32[]{:S(2)}, u32[]{:S(2)}) collective-permute-start(bf16[64,2048]{1,0:T(8,128)(2,1)} %get-tuple-element.223), channel_id=1, source_target_pairs={{0,4},{4,0},{1,5},{5,1},{2,6},{6,2},{3,7},{7,3},{8,12},{12,8},{9,1... | collective-permute-start | bytes 786440 | tf_op jit(solution)/shard_map/ppermute | solution.py:46
  487.6 21.0 %collective-permute-start.58 = (bf16[64,2048]{1,0:T(8,128)(2,1)}, bf16[64,2048]{1,0:T(8,128)(2,1)S(1)}, u32[]{:S(2)}, u32[]{:S(2)}) collective-permute-start(bf16[64,2048]{1,0:T(8,128)(2,1)} %get-tuple-element.224), channel_id=1, source_target_pairs={{0,5},{1,4},{4,1},{5,0},{2,7},{3,6},{6,3},{7,2},{8,13},{9,12},{12,... | collective-permute-start | bytes 786440 | tf_op jit(solution)/shard_map/ppermute | solution.py:90
  488.2 19.8 %all-to-all-start.6 = ((bf16[8,16,1024]{2,1,0:T(8,128)(2,1)}), bf16[8,16,1024]{2,1,0:T(8,128)(2,1)S(1)}, u32[]{:S(2)}, u32[]{:S(2)}) async-start(bf16[8,16,1024]{2,1,0:T(8,128)(2,1)} %bitcast.93), calls=%async_computation.7 | async-start | bytes 524288 | tf_op jit(solution)/shard_map/all_to_all | solution.py:50
  511.0 19.0 %collective-permute-start.59 = (bf16[64,2048]{1,0:T(8,128)(2,1)}, bf16[64,2048]{1,0:T(8,128)(2,1)S(1)}, u32[]{:S(2)}, u32[]{:S(2)}) collective-permute-start(bf16[64,2048]{1,0:T(8,128)(2,1)} %get-tuple-element.299), channel_id=1, source_target_pairs={{0,1},{1,0},{2,3},{3,2},{4,5},{5,4},{6,7},{7,6},{8,9},{9,8},{10,11... | collective-permute-start | bytes 786440 | tf_op jit(solution)/shard_map/ppermute | solution.py:46
  512.5 18.3 %collective-permute-start.60 = (bf16[64,2048]{1,0:T(8,128)(2,1)S(1)}, bf16[64,2048]{1,0:T(8,128)(2,1)}, u32[]{:S(2)}, u32[]{:S(2)}) collective-permute-start(bf16[64,2048]{1,0:T(8,128)(2,1)S(1)} %get-tuple-element.297), channel_id=1, source_target_pairs={{0,4},{4,0},{1,5},{5,1},{2,6},{6,2},{3,7},{7,3},{8,12},{12,8},{9,1... | collective-permute-start | bytes 786440 | tf_op jit(solution)/shard_map/ppermute | solution.py:46
  546.1 30.9 %all-to-all-start.8 = ((bf16[8,64,1024]{2,1,0:T(8,128)(2,1)}), bf16[8,64,1024]{2,1,0:T(8,128)(2,1)S(1)}, u32[]{:S(2)}, u32[]{:S(2)}) async-start(bf16[8,64,1024]{2,1,0:T(8,128)(2,1)} %broadcast_in_dim.12), calls=%async_computation.9 | async-start | bytes 2097152 | tf_op jit(solution)/shard_map/all_to_all | solution.py:50
  549.7 25.7 %collective-permute-start.61 = (bf16[128,2048]{1,0:T(8,128)(2,1)}, bf16[128,2048]{1,0:T(8,128)(2,1)S(1)}, u32[]{:S(2)}, u32[]{:S(2)}) collective-permute-start(bf16[128,2048]{1,0:T(8,128)(2,1)} %get-tuple-element.231), channel_id=1, source_target_pairs={{0,4},{4,0},{1,5},{5,1},{2,6},{6,2},{3,7},{7,3},{8,12},{12,8},{9,1... | collective-permute-start | bytes 1572872 | tf_op jit(solution)/shard_map/ppermute | solution.py:46
  551.7 24.5 %collective-permute-start.62 = (bf16[128,2048]{1,0:T(8,128)(2,1)}, bf16[128,2048]{1,0:T(8,128)(2,1)S(1)}, u32[]{:S(2)}, u32[]{:S(2)}) collective-permute-start(bf16[128,2048]{1,0:T(8,128)(2,1)} %get-tuple-element.232), channel_id=1, source_target_pairs={{0,1},{1,0},{2,3},{3,2},{4,5},{5,4},{6,7},{7,6},{8,9},{9,8},{10,11... | collective-permute-start | bytes 1572872 | tf_op jit(solution)/shard_map/ppermute | solution.py:46
  584.5 19.4 %all-to-all-start.9 = ((bf16[8,64,1024]{2,1,0:T(8,128)(2,1)}), bf16[8,64,1024]{2,1,0:T(8,128)(2,1)}, u32[]{:S(2)}, u32[]{:S(2)}) async-start(bf16[8,64,1024]{2,1,0:T(8,128)(2,1)} %copy-done.35), calls=%async_computation.10 | async-start | bytes 2097152 | tf_op jit(solution)/shard_map/all_to_all | solution.py:50
  588.8 25.8 %collective-permute-start.65 = (bf16[128,2048]{1,0:T(8,128)(2,1)}, bf16[128,2048]{1,0:T(8,128)(2,1)}, u32[]{:S(2)}, u32[]{:S(2)}) collective-permute-start(bf16[128,2048]{1,0:T(8,128)(2,1)} %pad_maximum_fusion.11), channel_id=1, source_target_pairs={{0,4},{4,0},{1,5},{5,1},{2,6},{6,2},{3,7},{7,3},{8,12},{12,8},{9,1... | collective-permute-start | bytes 1572872 | tf_op jit(solution)/shard_map/ppermute | solution.py:46
  590.8 23.9 %collective-permute-start.66 = (bf16[128,2048]{1,0:T(8,128)(2,1)}, bf16[128,2048]{1,0:T(8,128)(2,1)}, u32[]{:S(2)}, u32[]{:S(2)}) collective-permute-start(bf16[128,2048]{1,0:T(8,128)(2,1)} %pad_maximum_fusion.12), channel_id=1, source_target_pairs={{0,1},{1,0},{2,3},{3,2},{4,5},{5,4},{6,7},{7,6},{8,9},{9,8},{10,11... | collective-permute-start | bytes 1572872 | tf_op jit(solution)/shard_map/ppermute | solution.py:46
  666.7 19.3 %collective-permute-start.74 = (bf16[64,3072]{1,0:T(8,128)(2,1)}, bf16[64,3072]{1,0:T(8,128)(2,1)}, u32[]{:S(2)}, u32[]{:S(2)}) collective-permute-start(bf16[64,3072]{1,0:T(8,128)(2,1)} %get-tuple-element.279), channel_id=1, source_target_pairs={{0,5},{1,4},{4,1},{5,0},{2,7},{3,6},{6,3},{7,2},{8,13},{9,12},{12,... | collective-permute-start | bytes 1179656 | tf_op jit(solution)/shard_map/ppermute | solution.py:90
  (155 other events, 1778.4 us)
Sparse Core Ops, SparseCore 0:
  27.6 83.6 all-gather.4
  112.9 47.9 all-gather.6
  162.5 80.7 all-gather.8
  244.7 80.5 all-gather.10
  327.5 75.2 reduce-scatter.3
  407.6 74.7 reduce-scatter.5
  484.7 117.5 reduce-scatter.7

commit v17 on v14

--- a/solution.py
+++ b/solution.py
@@ -987,16 +987,19 @@
         half_context = caption.shape[0] // 2
         caption_part = trade(caption_part, PLANE).astype(F32).sum(axis=0)
         sums = layer_order(add_z(whole_of(caption_part[half_context:], width)))
-        caption_part = sum_z(caption_part[:half_context].astype(BF))
+        caption_part = caption_part[:half_context].astype(BF).reshape(z_size, -1, text_width // 4)
+        caption_part = trade(caption_part, "z").astype(F32).sum(axis=0).astype(BF)
         output = layer_output(after_cross, result, unit, order)
         down_grad, up_grad = finish_wide(wide_rows, rank)
+        rest_rows = pick_rows([rest_rows], rank)
         caption_part, rest_rows, sums, output, down_grad, up_grad = lax.optimization_barrier(
             (caption_part, rest_rows, sums, output, down_grad, up_grad)
         )
+        caption_part = spread(caption_part, "z", z_size).reshape(half_context, -1)
         grad_caption = caption_output(spread(caption_part, PLANE, 8))
 
         qkv_grad, out_grad, grad_cross, cross_out_grad = finish_all(
-            swap_parts(pick_rows([rest_rows], rank)), kv_weight_grad, rank
+            swap_parts(rest_rows), kv_weight_grad, rank
         )
         return (
             outer(output).reshape(hidden.shape),

time: 680 us -> 681 us (level)
    unnamed x186 -> x188, local copies, waits for them, and re-layouts: 46.7 us -> 47.4 us
where the time goes in v17:
time: 681 us; the launch traced here: 673 us
  waiting for transfers between devices  235 us (35%)
  Pallas kernels  112 us (16%)
  starting transfers between devices  106 us (16%)
  blocking collectives  89.5 us (13%)
  local copies, waits for them, and re-layouts  73.3 us (11%)
  matrix products  31.8 us (5%)
  between operations  16.4 us (2%)
  other arithmetic  9.26 us (1%)
    ppermute x68, waiting for transfers between devices, swap(): return lax.ppermute(values, axis, PAIR)  175 us
    all_to_all x7, blocking collectives, trade(): return lax.all_to_all(blocks, axes, 0, 0, tiled=True)  89.5 us
    pallas_call x20, Pallas kernels, call(): pl.pallas_call(kernel, grid=grid, in_specs=in_specs, out_specs=out_specs,...  74.4 us
    ppermute x68, starting transfers between devices, swap(): return lax.ppermute(values, axis, PAIR)  73.5 us
    unnamed x188, local copies, waits for them, and re-layouts  47.4 us
    pallas_call x9, Pallas kernels, call(): pl.pallas_call(kernel, grid_spec=spec, **options)  37.9 us
    dot_general x6, matrix products, dot(): return lax.dot_general(a, b, (dims, ((), ())), preferred_element_type=F32)  31.8 us
    all_to_all x6, starting transfers between devices, trade(): return lax.all_to_all(blocks, axes, 0, 0, tiled=True)  24.2 us
  transfers between devices with their start and end apart: 86, of which 49 were waited for; matrix products, arithmetic and copies ran while one was open for 10% of the time, Pallas kernels for 16%

profile of v17, /device:TPU:0, one launch (start us, length us, event | category | flops | bytes accessed | tf_op | source)
XLA Modules:
  0.0 673.1 jit_solution(4383928340020520011)
XLA Ops:
  34.6 8.8 %collective-permute-done.1.refs_2_ = bf16[128,2048]{1,0:T(8,128)(2,1)S(1)} collective-permute-done((bf16[128,2048]{1,0:T(8,128)(2,1)S(1)}, bf16[128,2048]{1,0:T(8,128)(2,1)S(1)}, u32[]{:S(2)}, u32[]{:S(2)}) %collective-permute-start.1) | collective-permute-done | bytes 524320 | tf_op jit(solution)/shard_map/ppermute | solution.py:46
  54.9 10.2 %all_to_all.65 = bf16[4,64,1024]{2,1,0:T(8,128)(2,1)} all-to-all(bf16[4,64,1024]{2,1,0:T(8,128)(2,1)S(1)} %copy.68), channel_id=1, replica_groups=mesh['z'=4,'x'=2,'c'=2,'y'=2] {'x','y'}, dimensions={0} | all-to-all | bytes 1048576 | tf_op jit(solution)/shard_map/all_to_all | solution.py:50
  65.2 15.5 %all_to_all.66 = bf16[4,64,2048]{2,1,0:T(8,128)(2,1)} all-to-all(bf16[4,64,2048]{2,1,0:T(8,128)(2,1)} %bitcast.95), channel_id=1, replica_groups=mesh['z'=4,'x'=2,'c'=2,'y'=2] {'x','y'}, dimensions={0} | all-to-all | bytes 2097152 | tf_op jit(solution)/shard_map/all_to_all | solution.py:50
  83.4 16.9 %all_to_all.67 = bf16[8,64,1024]{2,1,0:T(8,128)(2,1)S(1)} all-to-all(bf16[8,64,1024]{2,1,0:T(8,128)(2,1)S(1)} %get-tuple-element.132), channel_id=1, replica_groups=mesh['z'=4,'x'=2,'c'=2,'y'=2] {'x','c','y'}, dimensions={0} | all-to-all | bytes 2097152 | tf_op jit(solution)/shard_map/all_to_all | solution.py:50
  100.4 11.5 %all_to_all.68 = bf16[4,16,1024]{2,1,0:T(8,128)(2,1)S(1)} all-to-all(bf16[4,16,1024]{2,1,0:T(8,128)(2,1)S(1)} %bitcast.103), channel_id=1, replica_groups=mesh['z'=4,'x'=2,'c'=2,'y'=2] {'z'}, dimensions={0} | all-to-all | bytes 262144 | tf_op jit(solution)/shard_map/all_to_all | solution.py:50
  112.0 8.8 %all_to_all.69 = bf16[4,16,1024]{2,1,0:T(8,128)(2,1)S(1)} all-to-all(bf16[4,16,1024]{2,1,0:T(8,128)(2,1)S(1)} %broadcast_in_dim.12), channel_id=1, replica_groups=mesh['z'=4,'x'=2,'c'=2,'y'=2] {'z'}, dimensions={0} | all-to-all | bytes 262144 | tf_op jit(solution)/shard_map/all_to_all | solution.py:50
  138.1 18.2 %all_to_all.70 = bf16[4,64,2048]{2,1,0:T(8,128)(2,1)} all-to-all(bf16[4,64,2048]{2,1,0:T(8,128)(2,1)S(1)} %bitcast.94), channel_id=1, replica_groups=mesh['z'=4,'x'=2,'c'=2,'y'=2] {'x','y'}, dimensions={0} | all-to-all | bytes 2097152 | tf_op jit(solution)/shard_map/all_to_all | solution.py:50
  170.8 10.0 %collective-permute-done.11.refs_3_ = bf16[128,2048]{1,0:T(8,128)(2,1)S(1)} collective-permute-done((bf16[128,2048]{1,0:T(8,128)(2,1)S(1)}, bf16[128,2048]{1,0:T(8,128)(2,1)S(1)}, u32[]{:S(2)}, u32[]{:S(2)}) %collective-permute-start.11) | collective-permute-done | bytes 524320 | tf_op jit(solution)/shard_map/ppermute | solution.py:46
  185.2 9.2 %collective-permute-done.13.refs_2_ = bf16[128,2048]{1,0:T(8,128)(2,1)S(1)} collective-permute-done((bf16[128,2048]{1,0:T(8,128)(2,1)S(1)}, bf16[128,2048]{1,0:T(8,128)(2,1)S(1)}, u32[]{:S(2)}, u32[]{:S(2)}) %collective-permute-start.13) | collective-permute-done | bytes 524320 | tf_op jit(solution)/shard_map/ppermute | solution.py:46
  271.5 12.0 %feed_up.1 = (bf16[512,2048]{1,0:T(8,128)(2,1)}, bf16[512,2048]{1,0:T(8,128)(2,1)}, f32[512,2048]{1,0:T(8,128)}) custom-call(bf16[128,2048]{1,0:T(8,128)(2,1)S(1)} %copy-done.63, bf16[128,2048]{1,0:T(8,128)(2,1)S(1)} %copy-done.59, bf16[128,2048]{1,0:T(8,128)(2,1)S(1)} %copy-done.57, bf16[64,2048]{1,0:T(8,128)(2,1)S(1)} %copy-done.70, ...), custom_call_target="tpu_custom_call" | custom-call | flops 4294967296 | bytes 12582912 | tf_op jit(solution)/shard_map/feed_up/pallas_call | solution.py:101
  302.9 8.7 %down_grads.1 = bf16[1024,2048]{1,0:T(8,128)(2,1)} custom-call(s32[1]{0:T(128)} %bitcast.24.r, bf16[512,2048]{1,0:T(8,128)(2,1)S(1)} %constant_dynamic-update-slice_fusion.refs_0_.dy, bf16[512,2048]{1,0:T(8,128)(2,1)S(1)} %collective-permute-done.28.refs_1_, bf16[512,2048]{1,0:T(8,128)(2,1)} %get-tuple-element.217.refs_2_, bf16[512,2048]{1,0:T(8,128)(2,1)} %copy-done.91), custom_call_target="tpu_custom_call" | custom-call | flops 4294967296 | bytes 16777216 | tf_op jit(solution)/shard_map/down_grads/pallas_call | solution.py:112
  313.2 12.2 %all-gather.11.cloned.1.call-done.down = bf16[2048,2048]{1,0:T(8,128)(2,1)} async-done(((bf16[256,2048]{1,0:T(8,128)(2,1)}), bf16[2048,2048]{1,0:T(8,128)(2,1)}) %all-gather.11.cloned.1.call-update) | async-done | bytes 8388624 | tf_op jit(solution)/shard_map/all_gather | solution.py:84
  326.9 9.9 %feed_down.1.refs_2_ = bf16[512,2048]{1,0:T(8,128)(2,1)S(1)} custom-call(bf16[512,2048]{1,0:T(8,128)(2,1)S(1)} %copy-done.14, f32[512,2048]{1,0:T(8,128)} %get-tuple-element.164.slope_ref, bf16[2048,2048]{1,0:T(8,128)(2,1)} %all-gather.11.cloned.1.call-done.down), custom_call_target="tpu_custom_call" | custom-call | flops 4294967296 | bytes 25165824 | tf_op jit(solution)/shard_map/feed_down/pallas_call | solution.py:101
  336.9 8.9 %convolution_convert_fusion.2 = bf16[512,2048]{1,0:T(8,128)(2,1)S(1)} fusion(bf16[512,2048]{1,0:T(8,128)(2,1)S(1)} %feed_down.1.refs_2_, bf16[2048,2048]{1,0:T(8,128)(2,1)} %all-gather.9.cloned.1.call-done.refs_5_), kind=kOutput, calls=%fused_computation.5 | convolution fusion | flops 4296015872 | bytes 12582912 | tf_op jit(solution)/shard_map/dot_general | solution.py:26
  358.2 10.9 %collective-permute-done.38.refs_2_ = bf16[128,2048]{1,0:T(8,128)(2,1)S(1)} collective-permute-done((bf16[128,2048]{1,0:T(8,128)(2,1)S(1)}, bf16[128,2048]{1,0:T(8,128)(2,1)S(1)}, u32[]{:S(2)}, u32[]{:S(2)}) %collective-permute-start.38) | collective-permute-done | bytes 524320 | tf_op jit(solution)/shard_map/ppermute | solution.py:46
  376.3 9.2 %collective-permute-done.40.refs_2_ = bf16[128,2048]{1,0:T(8,128)(2,1)S(1)} collective-permute-done((bf16[128,2048]{1,0:T(8,128)(2,1)S(1)}, bf16[128,2048]{1,0:T(8,128)(2,1)S(1)}, u32[]{:S(2)}, u32[]{:S(2)}) %collective-permute-start.40) | collective-permute-done | bytes 524320 | tf_op jit(solution)/shard_map/ppermute | solution.py:46
  391.1 8.8 %up_grads.1 = bf16[1024,2048]{1,0:T(8,128)(2,1)} custom-call(s32[1]{0:T(128)} %bitcast.24.r, bf16[512,2048]{1,0:T(8,128)(2,1)} %get-tuple-element.168.refs_0_, bf16[512,2048]{1,0:T(8,128)(2,1)} %collective-permute-done.34.refs_1_, bf16[512,2048]{1,0:T(8,128)(2,1)} %copy-done.23, bf16[512,2048]{1,0:T(8,128)(2,1)} %copy-done.90), custom_call_target="tpu_custom_call" | custom-call | flops 4294967296 | bytes 16777216 | tf_op jit(solution)/shard_map/up_grads/pallas_call | solution.py:112
  434.5 11.7 %collective-permute-done.49.refs_2_ = bf16[128,2048]{1,0:T(8,128)(2,1)S(1)} collective-permute-done((bf16[128,2048]{1,0:T(8,128)(2,1)S(1)}, bf16[128,2048]{1,0:T(8,128)(2,1)S(1)}, u32[]{:S(2)}, u32[]{:S(2)}) %collective-permute-start.49) | collective-permute-done | bytes 524320 | tf_op jit(solution)/shard_map/ppermute | solution.py:46
  468.3 11.8 %attention_grads.1 = bf16[1024,3072]{1,0:T(8,128)(2,1)} custom-call(s32[1]{0:T(128)} %bitcast.24.r, bf16[512,2048]{1,0:T(8,128)(2,1)} %get-tuple-element.184.refs_0_, bf16[512,2048]{1,0:T(8,128)(2,1)} %collective-permute-done.30.refs_1_, bf16[512,2048]{1,0:T(8,128)(2,1)} %copy-done.24, bf16[512,2048]{1,0:T(8,128)(2,1)} %copy-done.77, ...), custom_call_target="tpu_custom_call" | custom-call | flops 6442450944 | bytes 25165824 | tf_op jit(solution)/shard_map/attention_grads/pallas_call | solution.py:112
  521.6 9.2 %convolution_convert_fusion = bf16[512,2048]{1,0:T(8,128)(2,1)} fusion(bf16[512,2048]{1,0:T(8,128)(2,1)S(1)} %copy-done.89, bf16[2048,2048]{1,0:T(8,128)(2,1)} %all-gather.11.cloned.1.call-done.down), kind=kOutput, calls=%fused_computation.3 | convolution fusion | flops 4296015872 | bytes 12582912 | tf_op jit(solution)/shard_map/dot_general | solution.py:26
  535.1 9.4 %collective-permute-done.59.refs_3_ = bf16[64,4096]{1,0:T(8,128)(2,1)S(1)} collective-permute-done((bf16[64,4096]{1,0:T(8,128)(2,1)}, bf16[64,4096]{1,0:T(8,128)(2,1)S(1)}, u32[]{:S(2)}, u32[]{:S(2)}) %collective-permute-start.59) | collective-permute-done | bytes 524320 | tf_op jit(solution)/shard_map/ppermute | solution.py:79
  581.7 11.3 %all-to-all-done.9 = bf16[8,80,1024]{2,1,0:T(8,128)(2,1)S(1)} async-done(((bf16[8,80,1024]{2,1,0:T(8,128)(2,1)}), bf16[8,80,1024]{2,1,0:T(8,128)(2,1)S(1)}, u32[]{:S(2)}, u32[]{:S(2)}) %all-to-all-start.9) | async-done | bytes 1310752 | tf_op jit(solution)/shard_map/all_to_all | solution.py:50
  632.4 18.6 %collective-permute-done.70.refs_1_ = bf16[64,3072]{1,0:T(8,128)(2,1)S(1)} collective-permute-done((bf16[64,3072]{1,0:T(8,128)(2,1)}, bf16[64,3072]{1,0:T(8,128)(2,1)S(1)}, u32[]{:S(2)}, u32[]{:S(2)}) %collective-permute-start.70) | collective-permute-done | bytes 393248 | tf_op jit(solution)/shard_map/ppermute | solution.py:46
  651.6 8.9 %collective-permute-done.72.refs_3_ = bf16[64,3072]{1,0:T(8,128)(2,1)S(1)} collective-permute-done((bf16[64,3072]{1,0:T(8,128)(2,1)S(1)}, bf16[64,3072]{1,0:T(8,128)(2,1)S(1)}, u32[]{:S(2)}, u32[]{:S(2)}) %collective-permute-start.72) | collective-permute-done | bytes 393248 | tf_op jit(solution)/shard_map/ppermute | solution.py:79
  (471 shorter events, 386.2 us)
Async XLA Ops:
  7.2 116.0 %all-gather.5.cloned.1.call-start = ((), (), s32[]{:S(2)}) async-start(), calls=%async_computation.16 | async-start | bytes 9437184 | tf_op jit(solution)/shard_map/all_gather | solution.py:84
  27.5 170.5 %all-gather.7.cloned.1.call-start = ((), (), s32[]{:S(2)}) async-start(), calls=%async_computation.17 | async-start | bytes 4718592 | tf_op jit(solution)/shard_map/all_gather | solution.py:84
  65.2 201.2 %all-gather.9.cloned.1.call-start = ((), (), s32[]{:S(2)}) async-start(), calls=%async_computation.18 | async-start | bytes 9437184 | tf_op jit(solution)/shard_map/all_gather | solution.py:84
  80.8 244.6 %all-gather.11.cloned.1.call-start = ((), (), s32[]{:S(2)}) async-start(), calls=%async_computation.19 | async-start | bytes 9437184 | tf_op jit(solution)/shard_map/all_gather | solution.py:84
  156.3 251.1 %reduce-scatter.4.cloned.1.call-start = ((), (), s32[]{:S(2)}) async-start(), calls=%async_computation.20 | async-start | bytes 5242880 | tf_op jit(solution)/shard_map/reduce_scatter | solution.py:88
  264.1 22.6 %collective-permute-start.24 = (bf16[128,2048]{1,0:T(8,128)(2,1)}, bf16[128,2048]{1,0:T(8,128)(2,1)}, u32[]{:S(2)}, u32[]{:S(2)}) collective-permute-start(bf16[128,2048]{1,0:T(8,128)(2,1)} %get-tuple-element.152.refs_3_), channel_id=1, source_target_pairs={{0,1},{1,0},{2,3},{3,2},{4,5},{5,4},{6,7},{7,6},{8,9},{9,8},{10,11... | collective-permute-start | bytes 1572872 | tf_op jit(solution)/shard_map/ppermute | solution.py:46
  264.5 20.1 %collective-permute-start.25 = (bf16[128,2048]{1,0:T(8,128)(2,1)}, bf16[128,2048]{1,0:T(8,128)(2,1)}, u32[]{:S(2)}, u32[]{:S(2)}) collective-permute-start(bf16[128,2048]{1,0:T(8,128)(2,1)} %get-tuple-element.152.refs_3_), channel_id=1, source_target_pairs={{0,4},{4,0},{1,5},{5,1},{2,6},{6,2},{3,7},{7,3},{8,12},{12,8},{9,1... | collective-permute-start | bytes 1572872 | tf_op jit(solution)/shard_map/ppermute | solution.py:46
  313.0 169.4 %reduce-scatter.6.cloned.1.call-start = ((), (), s32[]{:S(2)}) async-start(), calls=%async_computation.21 | async-start | bytes 5242880 | tf_op jit(solution)/shard_map/reduce_scatter | solution.py:88
  349.0 40.8 %collective-permute-start.43 = (bf16[512,2048]{1,0:T(8,128)(2,1)S(1)}, bf16[512,2048]{1,0:T(8,128)(2,1)S(1)}, u32[]{:S(2)}, u32[]{:S(2)}) collective-permute-start(bf16[512,2048]{1,0:T(8,128)(2,1)S(1)} %feed_down.1.refs_2_), channel_id=1, source_target_pairs={{0,2},{2,0},{1,3},{3,1},{4,6},{6,4},{5,7},{7,5},{8,10},{10,8},{9,1... | collective-permute-start | bytes 6291464 | tf_op jit(solution)/shard_map/ppermute | solution.py:46
  408.2 204.5 %reduce-scatter.8.cloned.1.call-start = ((), (), s32[]{:S(2)}) async-start(), calls=%async_computation.22 | async-start | bytes 7864320 | tf_op jit(solution)/shard_map/reduce_scatter | solution.py:88
  504.2 51.7 %collective-permute-start.63 = (bf16[128,2048]{1,0:T(8,128)(2,1)}, bf16[128,2048]{1,0:T(8,128)(2,1)}, u32[]{:S(2)}, u32[]{:S(2)}) collective-permute-start(bf16[128,2048]{1,0:T(8,128)(2,1)} %pad_maximum_fusion.10), channel_id=1, source_target_pairs={{0,1},{1,0},{2,3},{3,2},{4,5},{5,4},{6,7},{7,6},{8,9},{9,8},{10,11... | collective-permute-start | bytes 1572872 | tf_op jit(solution)/shard_map/ppermute | solution.py:46
  506.2 49.8 %collective-permute-start.61 = (bf16[128,2048]{1,0:T(8,128)(2,1)}, bf16[128,2048]{1,0:T(8,128)(2,1)}, u32[]{:S(2)}, u32[]{:S(2)}) collective-permute-start(bf16[128,2048]{1,0:T(8,128)(2,1)} %pad_maximum_fusion.9), channel_id=1, source_target_pairs={{0,4},{4,0},{1,5},{5,1},{2,6},{6,2},{3,7},{7,3},{8,12},{12,8},{9,1... | collective-permute-start | bytes 1572872 | tf_op jit(solution)/shard_map/ppermute | solution.py:46
  512.6 19.4 %all-to-all-start.7 = ((bf16[4,16,1024]{2,1,0:T(8,128)(2,1)}), bf16[4,16,1024]{2,1,0:T(8,128)(2,1)S(1)}, u32[]{:S(2)}, u32[]{:S(2)}) async-start(bf16[4,16,1024]{2,1,0:T(8,128)(2,1)} %broadcast_in_dim.13), calls=%async_computation.8 | async-start | bytes 262144 | tf_op jit(solution)/shard_map/all_to_all | solution.py:50
  519.9 24.6 %collective-permute-start.59 = (bf16[64,4096]{1,0:T(8,128)(2,1)}, bf16[64,4096]{1,0:T(8,128)(2,1)S(1)}, u32[]{:S(2)}, u32[]{:S(2)}) collective-permute-start(bf16[64,4096]{1,0:T(8,128)(2,1)} %get-tuple-element.202), channel_id=1, source_target_pairs={{0,5},{1,4},{4,1},{5,0},{2,7},{3,6},{6,3},{7,2},{8,13},{9,12},{12,... | collective-permute-start | bytes 1572872 | tf_op jit(solution)/shard_map/ppermute | solution.py:79
  545.6 19.6 %all-to-all-start.8 = ((bf16[8,64,1024]{2,1,0:T(8,128)(2,1)}), bf16[8,64,1024]{2,1,0:T(8,128)(2,1)}, u32[]{:S(2)}, u32[]{:S(2)}) async-start(bf16[8,64,1024]{2,1,0:T(8,128)(2,1)} %broadcast_in_dim.14), calls=%async_computation.10 | async-start | bytes 2097152 | tf_op jit(solution)/shard_map/all_to_all | solution.py:50
  552.5 22.8 %collective-permute-start.66 = (bf16[64,2048]{1,0:T(8,128)(2,1)}, bf16[64,2048]{1,0:T(8,128)(2,1)}, u32[]{:S(2)}, u32[]{:S(2)}) collective-permute-start(bf16[64,2048]{1,0:T(8,128)(2,1)} %get-tuple-element.245), channel_id=1, source_target_pairs={{0,1},{1,0},{2,3},{3,2},{4,5},{5,4},{6,7},{7,6},{8,9},{9,8},{10,11... | collective-permute-start | bytes 786440 | tf_op jit(solution)/shard_map/ppermute | solution.py:46
  554.5 20.8 %collective-permute-start.68 = (bf16[64,2048]{1,0:T(8,128)(2,1)}, bf16[64,2048]{1,0:T(8,128)(2,1)}, u32[]{:S(2)}, u32[]{:S(2)}) collective-permute-start(bf16[64,2048]{1,0:T(8,128)(2,1)} %get-tuple-element.243), channel_id=1, source_target_pairs={{0,4},{4,0},{1,5},{5,1},{2,6},{6,2},{3,7},{7,3},{8,12},{12,8},{9,1... | collective-permute-start | bytes 786440 | tf_op jit(solution)/shard_map/ppermute | solution.py:46
  571.5 21.5 %all-to-all-start.9 = ((bf16[8,80,1024]{2,1,0:T(8,128)(2,1)}), bf16[8,80,1024]{2,1,0:T(8,128)(2,1)S(1)}, u32[]{:S(2)}, u32[]{:S(2)}) async-start(bf16[8,80,1024]{2,1,0:T(8,128)(2,1)} %get-tuple-element.211), calls=%async_computation.11 | async-start | bytes 2621440 | tf_op jit(solution)/shard_map/all_to_all | solution.py:50
  577.4 30.9 %collective-permute-start.69 = (bf16[128,2048]{1,0:T(8,128)(2,1)}, bf16[128,2048]{1,0:T(8,128)(2,1)S(1)}, u32[]{:S(2)}, u32[]{:S(2)}) collective-permute-start(bf16[128,2048]{1,0:T(8,128)(2,1)} %pad_maximum_fusion.12), channel_id=1, source_target_pairs={{0,1},{1,0},{2,3},{3,2},{4,5},{5,4},{6,7},{7,6},{8,9},{9,8},{10,11... | collective-permute-start | bytes 1572872 | tf_op jit(solution)/shard_map/ppermute | solution.py:46
  580.2 28.2 %collective-permute-start.67 = (bf16[128,2048]{1,0:T(8,128)(2,1)}, bf16[128,2048]{1,0:T(8,128)(2,1)S(1)}, u32[]{:S(2)}, u32[]{:S(2)}) collective-permute-start(bf16[128,2048]{1,0:T(8,128)(2,1)} %pad_maximum_fusion.11), channel_id=1, source_target_pairs={{0,4},{4,0},{1,5},{5,1},{2,6},{6,2},{3,7},{7,3},{8,12},{12,8},{9,1... | collective-permute-start | bytes 1572872 | tf_op jit(solution)/shard_map/ppermute | solution.py:46
  624.6 38.4 %all-to-all-start.12 = ((bf16[8,64,1024]{2,1,0:T(8,128)(2,1)}), bf16[8,64,1024]{2,1,0:T(8,128)(2,1)S(1)}, u32[]{:S(2)}, u32[]{:S(2)}) async-start(bf16[8,64,1024]{2,1,0:T(8,128)(2,1)} %broadcast_in_dim.17), calls=%async_computation.15 | async-start | bytes 2097152 | tf_op jit(solution)/shard_map/all_to_all | solution.py:50
  628.2 22.8 %collective-permute-start.70 = (bf16[64,3072]{1,0:T(8,128)(2,1)}, bf16[64,3072]{1,0:T(8,128)(2,1)S(1)}, u32[]{:S(2)}, u32[]{:S(2)}) collective-permute-start(bf16[64,3072]{1,0:T(8,128)(2,1)} %copy-done.64), channel_id=1, source_target_pairs={{0,1},{1,0},{2,3},{3,2},{4,5},{5,4},{6,7},{7,6},{8,9},{9,8},{10,11... | collective-permute-start | bytes 1179656 | tf_op jit(solution)/shard_map/ppermute | solution.py:46
  630.1 21.4 %collective-permute-start.71 = (bf16[64,3072]{1,0:T(8,128)(2,1)S(1)}, bf16[64,3072]{1,0:T(8,128)(2,1)S(1)}, u32[]{:S(2)}, u32[]{:S(2)}) collective-permute-start(bf16[64,3072]{1,0:T(8,128)(2,1)S(1)} %get-tuple-element.230), channel_id=1, source_target_pairs={{0,4},{4,0},{1,5},{5,1},{2,6},{6,2},{3,7},{7,3},{8,12},{12,8},{9,1... | collective-permute-start | bytes 1179656 | tf_op jit(solution)/shard_map/ppermute | solution.py:46
  631.6 28.8 %collective-permute-start.72 = (bf16[64,3072]{1,0:T(8,128)(2,1)S(1)}, bf16[64,3072]{1,0:T(8,128)(2,1)S(1)}, u32[]{:S(2)}, u32[]{:S(2)}) collective-permute-start(bf16[64,3072]{1,0:T(8,128)(2,1)S(1)} %get-tuple-element.231), channel_id=1, source_target_pairs={{0,5},{1,4},{4,1},{5,0},{2,7},{3,6},{6,3},{7,2},{8,13},{9,12},{12,... | collective-permute-start | bytes 1179656 | tf_op jit(solution)/shard_map/ppermute | solution.py:79
  (154 other events, 1630.0 us)
Sparse Core Ops, SparseCore 0:
  27.6 83.6 all-gather.4
  112.9 47.9 all-gather.6
  162.5 80.7 all-gather.8
  244.7 80.5 all-gather.10
  327.5 75.2 reduce-scatter.3
  407.6 74.7 reduce-scatter.5
  484.7 115.4 reduce-scatter.7

commit v18 on v17

--- a/solution.py
+++ b/solution.py
@@ -61,14 +61,25 @@
     return own, from_y, from_x, swap(from_x[:half], "y"), swap(from_y[half:], "x")
 
 
-def scatter_tokens(parts):
+def scatter_first(parts):
     own, for_y, for_x, for_low, for_high = parts
     half = for_low.shape[0]
     low = swap(for_low, "y").astype(F32) + for_x[:half].astype(F32)
     high = swap(for_high, "x").astype(F32) + for_y[half:].astype(F32)
-    from_x = swap(jnp.concatenate([low.astype(BF), for_x[half:]], axis=0), "x")
-    from_y = swap(jnp.concatenate([for_y[:half], high.astype(BF)], axis=0), "y")
-    return [own, from_x, from_y]
+    return (
+        own,
+        jnp.concatenate([low.astype(BF), for_x[half:]], axis=0),
+        jnp.concatenate([for_y[:half], high.astype(BF)], axis=0),
+    )
+
+
+def scatter_second(parts):
+    own, for_x, for_y = parts
+    return [own, swap(for_x, "x"), swap(for_y, "y")]
+
+
+def scatter_tokens(parts):
+    return scatter_second(scatter_first(parts))
 
 
 def swap_parts(parts):
@@ -168,10 +179,13 @@
 
 
 def mm_scatter(values, weight):
-    partial = mm_t(values, weight).astype(BF)
+    return scatter_tokens(token_blocks(mm_t(values, weight).astype(BF)))
+
+
+def token_blocks(partial):
     rows = partial.shape[0] // 4
     cuts = [0, rows, 2 * rows, 3 * rows, 3 * rows + rows // 2, 4 * rows]
-    return scatter_tokens([partial[a:b] for a, b in zip(cuts, cuts[1:])])
+    return [partial[a:b] for a, b in zip(cuts, cuts[1:])]
 
 
 def normalize(values):
@@ -928,7 +942,11 @@
         )
 
         cross_branch = gather_tokens(cross_branch)
-        cross_branch, up_part = lax.optimization_barrier((cross_branch, up_part))
+        activated, cross_own = lax.optimization_barrier((activated, cross_branch[0]))
+        result = mm_t(activated, down).astype(BF)
+        cross_branch, up_part, result = lax.optimization_barrier(
+            ((cross_own,) + cross_branch[1:], up_part, result)
+        )
         cross_branch, grad_cross_mixed = gather_mm(
             cross_branch, mid, group, group, "cross_out_back"
         )
@@ -941,10 +959,12 @@
             parts, grad_after_cross, after_attn, gain_b
         )
 
-        attn_branch, grad_self_mixed = gather_mm(
-            gather_tokens(attn_branch), first, 3 * group, group, "out_back"
-        )
+        attn_branch, result = lax.optimization_barrier((gather_tokens(attn_branch), result))
+        result = scatter_first(token_blocks(result))
+        attn_branch, grad_self_mixed = gather_mm(attn_branch, first, 3 * group, group, "out_back")
         grad_projected = self_back(projected, grad_self_mixed, 2 * images)
+        grad_projected, result = lax.optimization_barrier((grad_projected, result))
+        result = scatter_second(result)
         rest_part = grad_products(
             [
                 (early[0], both(grad_projected)),
@@ -955,8 +975,8 @@
             "attention_grads",
             *halves,
         )
-        grad_projected, activated, kv_grad, rest_part = lax.optimization_barrier(
-            (grad_projected, activated, kv_grad, rest_part)
+        grad_projected, result, kv_grad, rest_part = lax.optimization_barrier(
+            (grad_projected, result, kv_grad, rest_part)
         )
         rest_part, up_rows = lax.optimization_barrier((rest_part, up_rows))
         rest_rows = scatter_grad(rest_part, grad_axes)
@@ -972,7 +992,6 @@
         )
         sums = jnp.concatenate([gain_grad_a, gain_grad_b, gain_grad_c, mask_grad], axis=0)
 
-        result = mm_scatter(activated, down)
 
         kv_halves = kv_grad.reshape(2, -1, 2 * group)
         kv_keep = lax.dynamic_index_in_dim(kv_halves, core, 0, keepdims=False)

time: 681 us -> 675 us (level)
  blocking collectives: 89.5 us -> 112 us
  waiting for transfers between devices: 235 us -> 218 us
  local copies, waits for them, and re-layouts: 73.3 us -> 66.4 us
    all_to_all x7 -> x8, blocking collectives: 89.5 us -> 112 us  [trade(): return lax.all_to_all(blocks, axes, 0, 0, tiled=True)]
    ppermute x68, waiting for transfers between devices: 175 us -> 166 us  [swap(): return lax.ppermute(values, axis, PAIR)]
    all_to_all x6 -> x5, waiting for transfers between devices: 20.6 us -> 15.1 us  [trade(): return lax.all_to_all(blocks, axes, 0, 0, tiled=True)]
    unnamed x188 -> x186, local copies, waits for them, and re-layouts: 47.4 us -> 42.7 us
    all_to_all x6 -> x5, starting transfers between devices: 24.2 us -> 21.1 us  [trade(): return lax.all_to_all(blocks, axes, 0, 0, tiled=True)]
  transfers between devices with their start and end apart: 86 -> 85, of which waited for: 49 -> 47; matrix products, arithmetic and copies ran while one was open for 10% -> 10% of each run, Pallas kernels for 16% -> 16%
where the time goes in v18:
time: 675 us; the launch traced here: 667 us
  waiting for transfers between devices  218 us (32%)
  blocking collectives  112 us (17%)
  Pallas kernels  110 us (16%)
  starting transfers between devices  101 us (15%)
  local copies, waits for them, and re-layouts  66.4 us (10%)
  matrix products  31.8 us (5%)
  between operations  16.4 us (2%)
  other arithmetic  11 us (2%)
    ppermute x68, waiting for transfers between devices, swap(): return lax.ppermute(values, axis, PAIR)  166 us
    all_to_all x8, blocking collectives, trade(): return lax.all_to_all(blocks, axes, 0, 0, tiled=True)  112 us
    pallas_call x20, Pallas kernels, call(): pl.pallas_call(kernel, grid=grid, in_specs=in_specs, out_specs=out_specs,...  72.4 us
    ppermute x68, starting transfers between devices, swap(): return lax.ppermute(values, axis, PAIR)  71.4 us
    unnamed x186, local copies, waits for them, and re-layouts  42.7 us
    pallas_call x9, Pallas kernels, call(): pl.pallas_call(kernel, grid_spec=spec, **options)  37.5 us
    dot_general x6, matrix products, dot(): return lax.dot_general(a, b, (dims, ((), ())), preferred_element_type=F32)  31.8 us
    all_to_all x5, starting transfers between devices, trade(): return lax.all_to_all(blocks, axes, 0, 0, tiled=True)  21.1 us
  transfers between devices with their start and end apart: 85, of which 47 were waited for; matrix products, arithmetic and copies ran while one was open for 10% of the time, Pallas kernels for 16%

profile of v18, /device:TPU:0, one launch (start us, length us, event | category | flops | bytes accessed | tf_op | source)
XLA Modules:
  0.0 667.1 jit_solution(15944668761836782678)
XLA Ops:
  34.6 8.8 %collective-permute-done.1.refs_2_ = bf16[128,2048]{1,0:T(8,128)(2,1)S(1)} collective-permute-done((bf16[128,2048]{1,0:T(8,128)(2,1)S(1)}, bf16[128,2048]{1,0:T(8,128)(2,1)S(1)}, u32[]{:S(2)}, u32[]{:S(2)}) %collective-permute-start.1) | collective-permute-done | bytes 524320 | tf_op jit(solution)/shard_map/ppermute | solution.py:46
  54.9 10.2 %all_to_all.65 = bf16[4,64,1024]{2,1,0:T(8,128)(2,1)} all-to-all(bf16[4,64,1024]{2,1,0:T(8,128)(2,1)S(1)} %copy.68), channel_id=1, replica_groups=mesh['z'=4,'x'=2,'c'=2,'y'=2] {'x','y'}, dimensions={0} | all-to-all | bytes 1048576 | tf_op jit(solution)/shard_map/all_to_all | solution.py:50
  65.2 15.5 %all_to_all.66 = bf16[4,64,2048]{2,1,0:T(8,128)(2,1)} all-to-all(bf16[4,64,2048]{2,1,0:T(8,128)(2,1)} %bitcast.95), channel_id=1, replica_groups=mesh['z'=4,'x'=2,'c'=2,'y'=2] {'x','y'}, dimensions={0} | all-to-all | bytes 2097152 | tf_op jit(solution)/shard_map/all_to_all | solution.py:50
  83.3 16.9 %all_to_all.67 = bf16[8,64,1024]{2,1,0:T(8,128)(2,1)S(1)} all-to-all(bf16[8,64,1024]{2,1,0:T(8,128)(2,1)S(1)} %get-tuple-element.147), channel_id=1, replica_groups=mesh['z'=4,'x'=2,'c'=2,'y'=2] {'x','c','y'}, dimensions={0} | all-to-all | bytes 2097152 | tf_op jit(solution)/shard_map/all_to_all | solution.py:50
  100.4 11.9 %all_to_all.68 = bf16[4,16,1024]{2,1,0:T(8,128)(2,1)S(1)} all-to-all(bf16[4,16,1024]{2,1,0:T(8,128)(2,1)S(1)} %bitcast.103), channel_id=1, replica_groups=mesh['z'=4,'x'=2,'c'=2,'y'=2] {'z'}, dimensions={0} | all-to-all | bytes 262144 | tf_op jit(solution)/shard_map/all_to_all | solution.py:50
  112.3 8.5 %all_to_all.69 = bf16[4,16,1024]{2,1,0:T(8,128)(2,1)S(1)} all-to-all(bf16[4,16,1024]{2,1,0:T(8,128)(2,1)S(1)} %broadcast_in_dim.12), channel_id=1, replica_groups=mesh['z'=4,'x'=2,'c'=2,'y'=2] {'z'}, dimensions={0} | all-to-all | bytes 262144 | tf_op jit(solution)/shard_map/all_to_all | solution.py:50
  138.2 18.2 %all_to_all.70 = bf16[4,64,2048]{2,1,0:T(8,128)(2,1)} all-to-all(bf16[4,64,2048]{2,1,0:T(8,128)(2,1)S(1)} %bitcast.94), channel_id=1, replica_groups=mesh['z'=4,'x'=2,'c'=2,'y'=2] {'x','y'}, dimensions={0} | all-to-all | bytes 2097152 | tf_op jit(solution)/shard_map/all_to_all | solution.py:50
  170.9 9.9 %collective-permute-done.11.refs_3_ = bf16[128,2048]{1,0:T(8,128)(2,1)S(1)} collective-permute-done((bf16[128,2048]{1,0:T(8,128)(2,1)S(1)}, bf16[128,2048]{1,0:T(8,128)(2,1)S(1)}, u32[]{:S(2)}, u32[]{:S(2)}) %collective-permute-start.11) | collective-permute-done | bytes 524320 | tf_op jit(solution)/shard_map/ppermute | solution.py:46
  185.3 9.3 %collective-permute-done.13.refs_2_ = bf16[128,2048]{1,0:T(8,128)(2,1)S(1)} collective-permute-done((bf16[128,2048]{1,0:T(8,128)(2,1)S(1)}, bf16[128,2048]{1,0:T(8,128)(2,1)S(1)}, u32[]{:S(2)}, u32[]{:S(2)}) %collective-permute-start.13) | collective-permute-done | bytes 524320 | tf_op jit(solution)/shard_map/ppermute | solution.py:46
  269.0 11.9 %feed_up.1 = (bf16[512,2048]{1,0:T(8,128)(2,1)}, bf16[512,2048]{1,0:T(8,128)(2,1)}, f32[512,2048]{1,0:T(8,128)}) custom-call(bf16[128,2048]{1,0:T(8,128)(2,1)S(1)} %copy-done.66, bf16[128,2048]{1,0:T(8,128)(2,1)S(1)} %copy-done.62, bf16[128,2048]{1,0:T(8,128)(2,1)S(1)} %copy-done.60, bf16[64,2048]{1,0:T(8,128)(2,1)S(1)} %copy-done.73, ...), custom_call_target="tpu_custom_call" | custom-call | flops 4294967296 | bytes 12582912 | tf_op jit(solution)/shard_map/feed_up/pallas_call | solution.py:112
  300.2 8.7 %down_grads.1 = bf16[1024,2048]{1,0:T(8,128)(2,1)} custom-call(s32[1]{0:T(128)} %bitcast.24.r, bf16[512,2048]{1,0:T(8,128)(2,1)S(1)} %constant_dynamic-update-slice_fusion.refs_0_.dy, bf16[512,2048]{1,0:T(8,128)(2,1)S(1)} %collective-permute-done.28.refs_1_, bf16[512,2048]{1,0:T(8,128)(2,1)} %get-tuple-element.186.refs_2_, bf16[512,2048]{1,0:T(8,128)(2,1)} %copy-done.90), custom_call_target="tpu_custom_call" | custom-call | flops 4294967296 | bytes 16777216 | tf_op jit(solution)/shard_map/down_grads/pallas_call | solution.py:123
  310.4 15.0 %all-gather.11.cloned.1.call-done.down = bf16[2048,2048]{1,0:T(8,128)(2,1)} async-done(((bf16[256,2048]{1,0:T(8,128)(2,1)}), bf16[2048,2048]{1,0:T(8,128)(2,1)}) %all-gather.11.cloned.1.call-update) | async-done | bytes 8388624 | tf_op jit(solution)/shard_map/all_gather | solution.py:95
  326.9 9.9 %feed_down.1.refs_2_ = bf16[512,2048]{1,0:T(8,128)(2,1)S(1)} custom-call(bf16[512,2048]{1,0:T(8,128)(2,1)S(1)} %copy-done.14, f32[512,2048]{1,0:T(8,128)} %get-tuple-element.179.slope_ref, bf16[2048,2048]{1,0:T(8,128)(2,1)} %all-gather.11.cloned.1.call-done.down), custom_call_target="tpu_custom_call" | custom-call | flops 4294967296 | bytes 25165824 | tf_op jit(solution)/shard_map/feed_down/pallas_call | solution.py:112
  336.9 8.9 %convolution_convert_fusion.2 = bf16[512,2048]{1,0:T(8,128)(2,1)S(1)} fusion(bf16[512,2048]{1,0:T(8,128)(2,1)S(1)} %feed_down.1.refs_2_, bf16[2048,2048]{1,0:T(8,128)(2,1)} %all-gather.9.cloned.1.call-done.refs_5_), kind=kOutput, calls=%fused_computation.5 | convolution fusion | flops 4296015872 | bytes 12582912 | tf_op jit(solution)/shard_map/dot_general | solution.py:26
  358.2 10.9 %collective-permute-done.38.refs_2_ = bf16[128,2048]{1,0:T(8,128)(2,1)S(1)} collective-permute-done((bf16[128,2048]{1,0:T(8,128)(2,1)S(1)}, bf16[128,2048]{1,0:T(8,128)(2,1)S(1)}, u32[]{:S(2)}, u32[]{:S(2)}) %collective-permute-start.38) | collective-permute-done | bytes 524320 | tf_op jit(solution)/shard_map/ppermute | solution.py:46
  375.5 9.2 %convolution_convert_fusion.1 = bf16[512,2048]{1,0:T(8,128)(2,1)} fusion(bf16[512,2048]{1,0:T(8,128)(2,1)S(1)} %copy-done.88, bf16[2048,2048]{1,0:T(8,128)(2,1)} %all-gather.11.cloned.1.call-done.down), kind=kOutput, calls=%fused_computation.4 | convolution fusion | flops 4296015872 | bytes 12582912 | tf_op jit(solution)/shard_map/dot_general | solution.py:26
  390.3 8.8 %up_grads.1 = bf16[1024,2048]{1,0:T(8,128)(2,1)} custom-call(s32[1]{0:T(128)} %bitcast.24.r, bf16[512,2048]{1,0:T(8,128)(2,1)} %get-tuple-element.184.refs_0_, bf16[512,2048]{1,0:T(8,128)(2,1)} %collective-permute-done.34.refs_1_, bf16[512,2048]{1,0:T(8,128)(2,1)} %copy-done.24, bf16[512,2048]{1,0:T(8,128)(2,1)} %copy-done.89), custom_call_target="tpu_custom_call" | custom-call | flops 4294967296 | bytes 16777216 | tf_op jit(solution)/shard_map/up_grads/pallas_call | solution.py:123
  434.1 12.0 %collective-permute-done.49.refs_2_ = bf16[128,2048]{1,0:T(8,128)(2,1)S(1)} collective-permute-done((bf16[128,2048]{1,0:T(8,128)(2,1)S(1)}, bf16[128,2048]{1,0:T(8,128)(2,1)S(1)}, u32[]{:S(2)}, u32[]{:S(2)}) %collective-permute-start.49) | collective-permute-done | bytes 524320 | tf_op jit(solution)/shard_map/ppermute | solution.py:46
  472.5 11.7 %attention_grads.1 = bf16[1024,3072]{1,0:T(8,128)(2,1)} custom-call(s32[1]{0:T(128)} %bitcast.24.r, bf16[512,2048]{1,0:T(8,128)(2,1)} %get-tuple-element.212.refs_0_, bf16[512,2048]{1,0:T(8,128)(2,1)} %collective-permute-done.30.refs_1_, bf16[512,2048]{1,0:T(8,128)(2,1)} %copy-done.25, bf16[512,2048]{1,0:T(8,128)(2,1)} %collective-permute-done.56.refs_3_, ...), custom_call_target="tpu_custom_call" | custom-call | flops 6442450944 | bytes 25165824 | tf_op jit(solution)/shard_map/attention_grads/pallas_call | solution.py:123
  523.1 8.2 %all-to-all-done.7 = bf16[4,16,1024]{2,1,0:T(8,128)(2,1)S(1)} async-done(((bf16[4,16,1024]{2,1,0:T(8,128)(2,1)}), bf16[4,16,1024]{2,1,0:T(8,128)(2,1)S(1)}, u32[]{:S(2)}, u32[]{:S(2)}) %all-to-all-start.7) | async-done | bytes 131104 | tf_op jit(solution)/shard_map/all_to_all | solution.py:50
  560.0 20.1 %all_to_all.71 = bf16[8,80,1024]{2,1,0:T(8,128)(2,1)S(1)} all-to-all(bf16[8,80,1024]{2,1,0:T(8,128)(2,1)S(1)} %get-tuple-element.239), channel_id=1, replica_groups=mesh['z'=4,'x'=2,'c'=2,'y'=2] {'x','c','y'}, dimensions={0} | all-to-all | bytes 2621440 | tf_op jit(solution)/shard_map/all_to_all | solution.py:50
  606.3 11.0 %all_to_all.72 = bf16[4,16,1024]{2,1,0:T(8,128)(2,1)S(1)} all-to-all(bf16[4,16,1024]{2,1,0:T(8,128)(2,1)S(1)} %broadcast_in_dim.15), channel_id=1, replica_groups=mesh['z'=4,'x'=2,'c'=2,'y'=2] {'z'}, dimensions={0} | all-to-all | bytes 262144 | tf_op jit(solution)/shard_map/all_to_all | solution.py:50
  626.3 18.7 %collective-permute-done.70.refs_1_ = bf16[64,3072]{1,0:T(8,128)(2,1)S(1)} collective-permute-done((bf16[64,3072]{1,0:T(8,128)(2,1)}, bf16[64,3072]{1,0:T(8,128)(2,1)S(1)}, u32[]{:S(2)}, u32[]{:S(2)}) %collective-permute-start.70) | collective-permute-done | bytes 393248 | tf_op jit(solution)/shard_map/ppermute | solution.py:46
  645.6 8.9 %collective-permute-done.72.refs_3_ = bf16[64,3072]{1,0:T(8,128)(2,1)S(1)} collective-permute-done((bf16[64,3072]{1,0:T(8,128)(2,1)S(1)}, bf16[64,3072]{1,0:T(8,128)(2,1)S(1)}, u32[]{:S(2)}, u32[]{:S(2)}) %collective-permute-start.72) | collective-permute-done | bytes 393248 | tf_op jit(solution)/shard_map/ppermute | solution.py:90
  (467 shorter events, 367.8 us)
Async XLA Ops:
  7.2 116.0 %all-gather.5.cloned.1.call-start = ((), (), s32[]{:S(2)}) async-start(), calls=%async_computation.16 | async-start | bytes 9437184 | tf_op jit(solution)/shard_map/all_gather | solution.py:95
  27.5 170.5 %all-gather.7.cloned.1.call-start = ((), (), s32[]{:S(2)}) async-start(), calls=%async_computation.17 | async-start | bytes 4718592 | tf_op jit(solution)/shard_map/all_gather | solution.py:95
  65.2 198.7 %all-gather.9.cloned.1.call-start = ((), (), s32[]{:S(2)}) async-start(), calls=%async_computation.18 | async-start | bytes 9437184 | tf_op jit(solution)/shard_map/all_gather | solution.py:95
  80.7 244.6 %all-gather.11.cloned.1.call-start = ((), (), s32[]{:S(2)}) async-start(), calls=%async_computation.19 | async-start | bytes 9437184 | tf_op jit(solution)/shard_map/all_gather | solution.py:95
  156.4 251.0 %reduce-scatter.4.cloned.1.call-start = ((), (), s32[]{:S(2)}) async-start(), calls=%async_computation.20 | async-start | bytes 5242880 | tf_op jit(solution)/shard_map/reduce_scatter | solution.py:99
  261.3 22.8 %collective-permute-start.24 = (bf16[128,2048]{1,0:T(8,128)(2,1)}, bf16[128,2048]{1,0:T(8,128)(2,1)}, u32[]{:S(2)}, u32[]{:S(2)}) collective-permute-start(bf16[128,2048]{1,0:T(8,128)(2,1)} %get-tuple-element.174.refs_3_), channel_id=1, source_target_pairs={{0,1},{1,0},{2,3},{3,2},{4,5},{5,4},{6,7},{7,6},{8,9},{9,8},{10,11... | collective-permute-start | bytes 1572872 | tf_op jit(solution)/shard_map/ppermute | solution.py:46
  262.0 20.1 %collective-permute-start.25 = (bf16[128,2048]{1,0:T(8,128)(2,1)}, bf16[128,2048]{1,0:T(8,128)(2,1)}, u32[]{:S(2)}, u32[]{:S(2)}) collective-permute-start(bf16[128,2048]{1,0:T(8,128)(2,1)} %get-tuple-element.174.refs_3_), channel_id=1, source_target_pairs={{0,4},{4,0},{1,5},{5,1},{2,6},{6,2},{3,7},{7,3},{8,12},{12,8},{9,1... | collective-permute-start | bytes 1572872 | tf_op jit(solution)/shard_map/ppermute | solution.py:46
  293.7 16.5 %collective-permute-start.30 = (bf16[512,2048]{1,0:T(8,128)(2,1)}, bf16[512,2048]{1,0:T(8,128)(2,1)}, u32[]{:S(2)}, u32[]{:S(2)}) collective-permute-start(bf16[512,2048]{1,0:T(8,128)(2,1)} %get-tuple-element.212.refs_0_), channel_id=1, source_target_pairs={{0,2},{2,0},{1,3},{3,1},{4,6},{6,4},{5,7},{7,5},{8,10},{10,8},{9,1... | collective-permute-start | bytes 6291464 | tf_op jit(solution)/shard_map/ppermute | solution.py:46
  310.2 174.8 %reduce-scatter.6.cloned.1.call-start = ((), (), s32[]{:S(2)}) async-start(), calls=%async_computation.21 | async-start | bytes 5242880 | tf_op jit(solution)/shard_map/reduce_scatter | solution.py:99
  349.0 39.9 %collective-permute-start.43 = (bf16[512,2048]{1,0:T(8,128)(2,1)S(1)}, bf16[512,2048]{1,0:T(8,128)(2,1)S(1)}, u32[]{:S(2)}, u32[]{:S(2)}) collective-permute-start(bf16[512,2048]{1,0:T(8,128)(2,1)S(1)} %feed_down.1.refs_2_), channel_id=1, source_target_pairs={{0,2},{2,0},{1,3},{3,1},{4,6},{6,4},{5,7},{7,5},{8,10},{10,8},{9,1... | collective-permute-start | bytes 6291464 | tf_op jit(solution)/shard_map/ppermute | solution.py:46
  407.4 196.5 %reduce-scatter.8.cloned.1.call-start = ((), (), s32[]{:S(2)}) async-start(), calls=%async_computation.22 | async-start | bytes 7864320 | tf_op jit(solution)/shard_map/reduce_scatter | solution.py:99
  466.6 17.6 %collective-permute-start.54 = (bf16[128,2048]{1,0:T(8,128)(2,1)}, bf16[128,2048]{1,0:T(8,128)(2,1)S(1)}, u32[]{:S(2)}, u32[]{:S(2)}) collective-permute-start(bf16[128,2048]{1,0:T(8,128)(2,1)} %get-tuple-element.206), channel_id=1, source_target_pairs={{0,4},{4,0},{1,5},{5,1},{2,6},{6,2},{3,7},{7,3},{8,12},{12,8},{9,1... | collective-permute-start | bytes 1572872 | tf_op jit(solution)/shard_map/ppermute | solution.py:46
  507.7 24.8 %collective-permute-start.61 = (bf16[64,4096]{1,0:T(8,128)(2,1)}, bf16[64,4096]{1,0:T(8,128)(2,1)S(1)}, u32[]{:S(2)}, u32[]{:S(2)}) collective-permute-start(bf16[64,4096]{1,0:T(8,128)(2,1)} %get-tuple-element.228), channel_id=1, source_target_pairs={{0,1},{1,0},{2,3},{3,2},{4,5},{5,4},{6,7},{7,6},{8,9},{9,8},{10,11... | collective-permute-start | bytes 1572872 | tf_op jit(solution)/shard_map/ppermute | solution.py:46
  508.1 24.4 %collective-permute-start.62 = (bf16[64,4096]{1,0:T(8,128)(2,1)}, bf16[64,4096]{1,0:T(8,128)(2,1)S(1)}, u32[]{:S(2)}, u32[]{:S(2)}) collective-permute-start(bf16[64,4096]{1,0:T(8,128)(2,1)} %get-tuple-element.229), channel_id=1, source_target_pairs={{0,4},{4,0},{1,5},{5,1},{2,6},{6,2},{3,7},{7,3},{8,12},{12,8},{9,1... | collective-permute-start | bytes 1572872 | tf_op jit(solution)/shard_map/ppermute | solution.py:46
  509.7 25.9 %collective-permute-start.63 = (bf16[64,4096]{1,0:T(8,128)(2,1)S(1)}, bf16[64,4096]{1,0:T(8,128)(2,1)S(1)}, u32[]{:S(2)}, u32[]{:S(2)}) collective-permute-start(bf16[64,4096]{1,0:T(8,128)(2,1)S(1)} %get-tuple-element.230), channel_id=1, source_target_pairs={{0,5},{1,4},{4,1},{5,0},{2,7},{3,6},{6,3},{7,2},{8,13},{9,12},{12,... | collective-permute-start | bytes 1572872 | tf_op jit(solution)/shard_map/ppermute | solution.py:90
  513.0 30.8 %collective-permute-start.67 = (bf16[128,2048]{1,0:T(8,128)(2,1)}, bf16[128,2048]{1,0:T(8,128)(2,1)}, u32[]{:S(2)}, u32[]{:S(2)}) collective-permute-start(bf16[128,2048]{1,0:T(8,128)(2,1)} %pad_maximum_fusion.12), channel_id=1, source_target_pairs={{0,1},{1,0},{2,3},{3,2},{4,5},{5,4},{6,7},{7,6},{8,9},{9,8},{10,11... | collective-permute-start | bytes 1572872 | tf_op jit(solution)/shard_map/ppermute | solution.py:46
  515.0 16.2 %all-to-all-start.7 = ((bf16[4,16,1024]{2,1,0:T(8,128)(2,1)}), bf16[4,16,1024]{2,1,0:T(8,128)(2,1)S(1)}, u32[]{:S(2)}, u32[]{:S(2)}) async-start(bf16[4,16,1024]{2,1,0:T(8,128)(2,1)} %broadcast_in_dim.13), calls=%async_computation.8 | async-start | bytes 262144 | tf_op jit(solution)/shard_map/all_to_all | solution.py:50
  521.7 22.5 %collective-permute-start.65 = (bf16[128,2048]{1,0:T(8,128)(2,1)}, bf16[128,2048]{1,0:T(8,128)(2,1)}, u32[]{:S(2)}, u32[]{:S(2)}) collective-permute-start(bf16[128,2048]{1,0:T(8,128)(2,1)} %pad_maximum_fusion.11), channel_id=1, source_target_pairs={{0,4},{4,0},{1,5},{5,1},{2,6},{6,2},{3,7},{7,3},{8,12},{12,8},{9,1... | collective-permute-start | bytes 1572872 | tf_op jit(solution)/shard_map/ppermute | solution.py:46
  537.4 19.0 %all-to-all-start.8 = ((bf16[8,64,1024]{2,1,0:T(8,128)(2,1)}), bf16[8,64,1024]{2,1,0:T(8,128)(2,1)}, u32[]{:S(2)}, u32[]{:S(2)}) async-start(bf16[8,64,1024]{2,1,0:T(8,128)(2,1)} %broadcast_in_dim.14), calls=%async_computation.10 | async-start | bytes 2097152 | tf_op jit(solution)/shard_map/all_to_all | solution.py:50
  581.0 21.8 %all-to-all-start.10 = ((bf16[4,16,1024]{2,1,0:T(8,128)(2,1)}), bf16[4,16,1024]{2,1,0:T(8,128)(2,1)}, u32[]{:S(2)}, u32[]{:S(2)}) async-start(bf16[4,16,1024]{2,1,0:T(8,128)(2,1)} %bitcast.105), calls=%async_computation.12 | async-start | bytes 262144 | tf_op jit(solution)/shard_map/all_to_all | solution.py:50
  618.4 38.7 %all-to-all-start.12 = ((bf16[8,64,1024]{2,1,0:T(8,128)(2,1)}), bf16[8,64,1024]{2,1,0:T(8,128)(2,1)S(1)}, u32[]{:S(2)}, u32[]{:S(2)}) async-start(bf16[8,64,1024]{2,1,0:T(8,128)(2,1)} %broadcast_in_dim.17), calls=%async_computation.15 | async-start | bytes 2097152 | tf_op jit(solution)/shard_map/all_to_all | solution.py:50
  622.2 22.9 %collective-permute-start.70 = (bf16[64,3072]{1,0:T(8,128)(2,1)}, bf16[64,3072]{1,0:T(8,128)(2,1)S(1)}, u32[]{:S(2)}, u32[]{:S(2)}) collective-permute-start(bf16[64,3072]{1,0:T(8,128)(2,1)} %copy-done.67), channel_id=1, source_target_pairs={{0,1},{1,0},{2,3},{3,2},{4,5},{5,4},{6,7},{7,6},{8,9},{9,8},{10,11... | collective-permute-start | bytes 1179656 | tf_op jit(solution)/shard_map/ppermute | solution.py:46
  624.2 21.4 %collective-permute-start.71 = (bf16[64,3072]{1,0:T(8,128)(2,1)S(1)}, bf16[64,3072]{1,0:T(8,128)(2,1)S(1)}, u32[]{:S(2)}, u32[]{:S(2)}) collective-permute-start(bf16[64,3072]{1,0:T(8,128)(2,1)S(1)} %get-tuple-element.260), channel_id=1, source_target_pairs={{0,4},{4,0},{1,5},{5,1},{2,6},{6,2},{3,7},{7,3},{8,12},{12,8},{9,1... | collective-permute-start | bytes 1179656 | tf_op jit(solution)/shard_map/ppermute | solution.py:46
  625.7 28.8 %collective-permute-start.72 = (bf16[64,3072]{1,0:T(8,128)(2,1)S(1)}, bf16[64,3072]{1,0:T(8,128)(2,1)S(1)}, u32[]{:S(2)}, u32[]{:S(2)}) collective-permute-start(bf16[64,3072]{1,0:T(8,128)(2,1)S(1)} %get-tuple-element.261), channel_id=1, source_target_pairs={{0,5},{1,4},{4,1},{5,0},{2,7},{3,6},{6,3},{7,2},{8,13},{9,12},{12,... | collective-permute-start | bytes 1179656 | tf_op jit(solution)/shard_map/ppermute | solution.py:90
  (152 other events, 1813.9 us)
Sparse Core Ops, SparseCore 0:
  27.6 83.6 all-gather.4
  112.9 47.8 all-gather.6
  162.5 80.7 all-gather.8
  244.7 80.5 all-gather.10
  327.5 75.2 reduce-scatter.3
  407.5 74.7 reduce-scatter.5
  485.1 118.7 reduce-scatter.7

commit v19 on v18

--- a/solution.py
+++ b/solution.py
@@ -993,10 +993,10 @@
         sums = jnp.concatenate([gain_grad_a, gain_grad_b, gain_grad_c, mask_grad], axis=0)
 
 
-        kv_halves = kv_grad.reshape(2, -1, 2 * group)
-        kv_keep = lax.dynamic_index_in_dim(kv_halves, core, 0, keepdims=False)
-        kv_send = lax.dynamic_index_in_dim(kv_halves, 1 - core, 0, keepdims=False)
-        kv_sum = sum_z((kv_keep + swap(kv_send, "c")).astype(BF))
+        kv_part = kv_grad.astype(BF).reshape(2, z_size, -1, 2 * group)
+        kv_part = kv_part.transpose(1, 0, 2, 3).reshape(2 * z_size, -1, 2 * group)
+        kv_part = trade(kv_part, DATA).astype(F32).sum(axis=0).astype(BF)
+        kv_sum = spread(kv_part, "z", z_size).reshape(-1, 2 * group)
         wide_rows = swap_parts(pick_rows([down_rows, up_rows], rank))
         kv_sum, wide_rows = lax.optimization_barrier((kv_sum, wide_rows))
         kv_grads = spread(kv_sum, PLANE, 8)
@@ -1004,21 +1004,24 @@
             kv_grads, own_text, w_cross, caption, w_text, halves_of(sums, text_width // 4)
         )
         half_context = caption.shape[0] // 2
-        caption_part = trade(caption_part, PLANE).astype(F32).sum(axis=0)
+        caption_part = trade(caption_part, PLANE)
+        output = layer_output(after_cross, result, unit, order)
+        down_grad, up_grad = finish_wide(wide_rows, rank)
+        caption_part, output, down_grad, up_grad = lax.optimization_barrier(
+            (caption_part, output, down_grad, up_grad)
+        )
+        caption_part = caption_part.astype(F32).sum(axis=0)
         sums = layer_order(add_z(whole_of(caption_part[half_context:], width)))
         caption_part = caption_part[:half_context].astype(BF).reshape(z_size, -1, text_width // 4)
         caption_part = trade(caption_part, "z").astype(F32).sum(axis=0).astype(BF)
-        output = layer_output(after_cross, result, unit, order)
-        down_grad, up_grad = finish_wide(wide_rows, rank)
         rest_rows = pick_rows([rest_rows], rank)
-        caption_part, rest_rows, sums, output, down_grad, up_grad = lax.optimization_barrier(
-            (caption_part, rest_rows, sums, output, down_grad, up_grad)
-        )
+        caption_part, rest_rows = lax.optimization_barrier((caption_part, rest_rows))
         caption_part = spread(caption_part, "z", z_size).reshape(half_context, -1)
+        rest_rows = swap_parts(rest_rows)
+        caption_part, rest_rows = lax.optimization_barrier((caption_part, rest_rows))
         grad_caption = caption_output(spread(caption_part, PLANE, 8))
-
         qkv_grad, out_grad, grad_cross, cross_out_grad = finish_all(
-            swap_parts(rest_rows), kv_weight_grad, rank
+            rest_rows, kv_weight_grad, rank
         )
         return (
             outer(output).reshape(hidden.shape),

time: 675 us -> 667 us (0.988)
  blocking collectives: 112 us -> 104 us
    all_to_all x5, waiting for transfers between devices: 15.1 us -> 37.4 us  [trade(): return lax.all_to_all(blocks, axes, 0, 0, tiled=True)]
    ppermute x68 -> x67, waiting for transfers between devices: 166 us -> 146 us  [swap(): return lax.ppermute(values, axis, PAIR)]
    reduce_scatter x3, waiting for transfers between devices: 0.08 us -> 9.63 us  [scatter_grad(): summed = lax.psum_scatter(partial, axes, scatter_dimension=0, tiled=True)]
    all_to_all x8, blocking collectives: 112 us -> 104 us  [trade(): return lax.all_to_all(blocks, axes, 0, 0, tiled=True)]
    ppermute x68 -> x67, starting transfers between devices: 71.4 us -> 70 us  [swap(): return lax.ppermute(values, axis, PAIR)]
    unnamed x186 -> x196, local copies, waits for them, and re-layouts: 42.7 us -> 42.2 us
  transfers between devices with their start and end apart: 85 -> 84, of which waited for: 47 -> 46; matrix products, arithmetic and copies ran while one was open for 10% -> 10% of each run, Pallas kernels for 16% -> 16%
where the time goes in v19:
time: 667 us; the launch traced here: 659 us
  waiting for transfers between devices  220 us (33%)
  Pallas kernels  111 us (17%)
  blocking collectives  104 us (16%)
  starting transfers between devices  99.6 us (15%)
  local copies, waits for them, and re-layouts  66.5 us (10%)
  matrix products  31.8 us (5%)
  between operations  16.5 us (2%)
  other arithmetic  9.63 us (1%)
    ppermute x67, waiting for transfers between devices, swap(): return lax.ppermute(values, axis, PAIR)  146 us
    all_to_all x8, blocking collectives, trade(): return lax.all_to_all(blocks, axes, 0, 0, tiled=True)  104 us
    pallas_call x20, Pallas kernels, call(): pl.pallas_call(kernel, grid=grid, in_specs=in_specs, out_specs=out_specs,...  73.5 us
    ppermute x67, starting transfers between devices, swap(): return lax.ppermute(values, axis, PAIR)  70 us
    unnamed x196, local copies, waits for them, and re-layouts  42.2 us
    pallas_call x9, Pallas kernels, call(): pl.pallas_call(kernel, grid_spec=spec, **options)  37.7 us
    all_to_all x5, waiting for transfers between devices, trade(): return lax.all_to_all(blocks, axes, 0, 0, tiled=True)  37.4 us
    dot_general x6, matrix products, dot(): return lax.dot_general(a, b, (dims, ((), ())), preferred_element_type=F32)  31.8 us
  transfers between devices with their start and end apart: 84, of which 46 were waited for; matrix products, arithmetic and copies ran while one was open for 10% of the time, Pallas kernels for 16%

profile of v19, /device:TPU:0, one launch (start us, length us, event | category | flops | bytes accessed | tf_op | source)
XLA Modules:
  0.0 658.9 jit_solution(13975204115817504687)
XLA Ops:
  34.6 8.8 %collective-permute-done.1.refs_2_ = bf16[128,2048]{1,0:T(8,128)(2,1)S(1)} collective-permute-done((bf16[128,2048]{1,0:T(8,128)(2,1)S(1)}, bf16[128,2048]{1,0:T(8,128)(2,1)S(1)}, u32[]{:S(2)}, u32[]{:S(2)}) %collective-permute-start.1) | collective-permute-done | bytes 524320 | tf_op jit(solution)/shard_map/ppermute | solution.py:46
  54.9 10.2 %all_to_all.65 = bf16[4,64,1024]{2,1,0:T(8,128)(2,1)} all-to-all(bf16[4,64,1024]{2,1,0:T(8,128)(2,1)S(1)} %copy.75), channel_id=1, replica_groups=mesh['z'=4,'x'=2,'c'=2,'y'=2] {'x','y'}, dimensions={0} | all-to-all | bytes 1048576 | tf_op jit(solution)/shard_map/all_to_all | solution.py:50
  65.2 15.5 %all_to_all.66 = bf16[4,64,2048]{2,1,0:T(8,128)(2,1)} all-to-all(bf16[4,64,2048]{2,1,0:T(8,128)(2,1)} %bitcast.88), channel_id=1, replica_groups=mesh['z'=4,'x'=2,'c'=2,'y'=2] {'x','y'}, dimensions={0} | all-to-all | bytes 2097152 | tf_op jit(solution)/shard_map/all_to_all | solution.py:50
  83.4 16.9 %all_to_all.67 = bf16[8,64,1024]{2,1,0:T(8,128)(2,1)S(1)} all-to-all(bf16[8,64,1024]{2,1,0:T(8,128)(2,1)S(1)} %get-tuple-element.152), channel_id=1, replica_groups=mesh['z'=4,'x'=2,'c'=2,'y'=2] {'x','c','y'}, dimensions={0} | all-to-all | bytes 2097152 | tf_op jit(solution)/shard_map/all_to_all | solution.py:50
  100.4 11.5 %all_to_all.68 = bf16[4,16,1024]{2,1,0:T(8,128)(2,1)S(1)} all-to-all(bf16[4,16,1024]{2,1,0:T(8,128)(2,1)S(1)} %bitcast.98), channel_id=1, replica_groups=mesh['z'=4,'x'=2,'c'=2,'y'=2] {'z'}, dimensions={0} | all-to-all | bytes 262144 | tf_op jit(solution)/shard_map/all_to_all | solution.py:50
  112.0 8.8 %all_to_all.69 = bf16[4,16,1024]{2,1,0:T(8,128)(2,1)S(1)} all-to-all(bf16[4,16,1024]{2,1,0:T(8,128)(2,1)S(1)} %broadcast_in_dim.10), channel_id=1, replica_groups=mesh['z'=4,'x'=2,'c'=2,'y'=2] {'z'}, dimensions={0} | all-to-all | bytes 262144 | tf_op jit(solution)/shard_map/all_to_all | solution.py:50
  138.1 18.2 %all_to_all.70 = bf16[4,64,2048]{2,1,0:T(8,128)(2,1)} all-to-all(bf16[4,64,2048]{2,1,0:T(8,128)(2,1)S(1)} %bitcast.87), channel_id=1, replica_groups=mesh['z'=4,'x'=2,'c'=2,'y'=2] {'x','y'}, dimensions={0} | all-to-all | bytes 2097152 | tf_op jit(solution)/shard_map/all_to_all | solution.py:50
  170.8 10.0 %collective-permute-done.11.refs_3_ = bf16[128,2048]{1,0:T(8,128)(2,1)S(1)} collective-permute-done((bf16[128,2048]{1,0:T(8,128)(2,1)S(1)}, bf16[128,2048]{1,0:T(8,128)(2,1)S(1)}, u32[]{:S(2)}, u32[]{:S(2)}) %collective-permute-start.11) | collective-permute-done | bytes 524320 | tf_op jit(solution)/shard_map/ppermute | solution.py:46
  185.2 9.2 %collective-permute-done.13.refs_2_ = bf16[128,2048]{1,0:T(8,128)(2,1)S(1)} collective-permute-done((bf16[128,2048]{1,0:T(8,128)(2,1)S(1)}, bf16[128,2048]{1,0:T(8,128)(2,1)S(1)}, u32[]{:S(2)}, u32[]{:S(2)}) %collective-permute-start.13) | collective-permute-done | bytes 524320 | tf_op jit(solution)/shard_map/ppermute | solution.py:46
  271.5 11.9 %feed_up.1 = (bf16[512,2048]{1,0:T(8,128)(2,1)}, bf16[512,2048]{1,0:T(8,128)(2,1)}, f32[512,2048]{1,0:T(8,128)}) custom-call(bf16[128,2048]{1,0:T(8,128)(2,1)S(1)} %copy-done.71, bf16[128,2048]{1,0:T(8,128)(2,1)S(1)} %copy-done.67, bf16[128,2048]{1,0:T(8,128)(2,1)S(1)} %copy-done.65, bf16[64,2048]{1,0:T(8,128)(2,1)S(1)} %copy-done.77, ...), custom_call_target="tpu_custom_call" | custom-call | flops 4294967296 | bytes 12582912 | tf_op jit(solution)/shard_map/feed_up/pallas_call | solution.py:112
  303.2 8.7 %down_grads.1 = bf16[1024,2048]{1,0:T(8,128)(2,1)} custom-call(s32[1]{0:T(128)} %bitcast.24.r, bf16[512,2048]{1,0:T(8,128)(2,1)S(1)} %constant_dynamic-update-slice_fusion.refs_0_.dy, bf16[512,2048]{1,0:T(8,128)(2,1)S(1)} %collective-permute-done.28.refs_1_, bf16[512,2048]{1,0:T(8,128)(2,1)} %get-tuple-element.191.refs_2_, bf16[512,2048]{1,0:T(8,128)(2,1)} %copy-done.95), custom_call_target="tpu_custom_call" | custom-call | flops 4294967296 | bytes 16777216 | tf_op jit(solution)/shard_map/down_grads/pallas_call | solution.py:123
  313.4 12.0 %all-gather.11.cloned.1.call-done.down = bf16[2048,2048]{1,0:T(8,128)(2,1)} async-done(((bf16[256,2048]{1,0:T(8,128)(2,1)}), bf16[2048,2048]{1,0:T(8,128)(2,1)}) %all-gather.11.cloned.1.call-update) | async-done | bytes 8388624 | tf_op jit(solution)/shard_map/all_gather | solution.py:95
  326.9 9.9 %feed_down.1.refs_2_ = bf16[512,2048]{1,0:T(8,128)(2,1)S(1)} custom-call(bf16[512,2048]{1,0:T(8,128)(2,1)S(1)} %copy-done.14, f32[512,2048]{1,0:T(8,128)} %get-tuple-element.184.slope_ref, bf16[2048,2048]{1,0:T(8,128)(2,1)} %all-gather.11.cloned.1.call-done.down), custom_call_target="tpu_custom_call" | custom-call | flops 4294967296 | bytes 25165824 | tf_op jit(solution)/shard_map/feed_down/pallas_call | solution.py:112
  336.9 8.9 %convolution_convert_fusion.2 = bf16[512,2048]{1,0:T(8,128)(2,1)S(1)} fusion(bf16[512,2048]{1,0:T(8,128)(2,1)S(1)} %feed_down.1.refs_2_, bf16[2048,2048]{1,0:T(8,128)(2,1)} %all-gather.9.cloned.1.call-done.refs_5_), kind=kOutput, calls=%fused_computation.5 | convolution fusion | flops 4296015872 | bytes 12582912 | tf_op jit(solution)/shard_map/dot_general | solution.py:26
  358.2 10.9 %collective-permute-done.38.refs_2_ = bf16[128,2048]{1,0:T(8,128)(2,1)S(1)} collective-permute-done((bf16[128,2048]{1,0:T(8,128)(2,1)S(1)}, bf16[128,2048]{1,0:T(8,128)(2,1)S(1)}, u32[]{:S(2)}, u32[]{:S(2)}) %collective-permute-start.38) | collective-permute-done | bytes 524320 | tf_op jit(solution)/shard_map/ppermute | solution.py:46
  375.5 9.2 %convolution_convert_fusion.1 = bf16[512,2048]{1,0:T(8,128)(2,1)} fusion(bf16[512,2048]{1,0:T(8,128)(2,1)S(1)} %copy-done.93, bf16[2048,2048]{1,0:T(8,128)(2,1)} %all-gather.11.cloned.1.call-done.down), kind=kOutput, calls=%fused_computation.4 | convolution fusion | flops 4296015872 | bytes 12582912 | tf_op jit(solution)/shard_map/dot_general | solution.py:26
  390.3 8.8 %up_grads.1 = bf16[1024,2048]{1,0:T(8,128)(2,1)} custom-call(s32[1]{0:T(128)} %bitcast.24.r, bf16[512,2048]{1,0:T(8,128)(2,1)} %get-tuple-element.189.refs_0_, bf16[512,2048]{1,0:T(8,128)(2,1)} %collective-permute-done.34.refs_1_, bf16[512,2048]{1,0:T(8,128)(2,1)} %copy-done.24, bf16[512,2048]{1,0:T(8,128)(2,1)} %copy-done.94), custom_call_target="tpu_custom_call" | custom-call | flops 4294967296 | bytes 16777216 | tf_op jit(solution)/shard_map/up_grads/pallas_call | solution.py:123
  433.7 11.9 %collective-permute-done.49.refs_2_ = bf16[128,2048]{1,0:T(8,128)(2,1)S(1)} collective-permute-done((bf16[128,2048]{1,0:T(8,128)(2,1)S(1)}, bf16[128,2048]{1,0:T(8,128)(2,1)S(1)}, u32[]{:S(2)}, u32[]{:S(2)}) %collective-permute-start.49) | collective-permute-done | bytes 524320 | tf_op jit(solution)/shard_map/ppermute | solution.py:46
  472.0 11.7 %attention_grads.1 = bf16[1024,3072]{1,0:T(8,128)(2,1)} custom-call(s32[1]{0:T(128)} %bitcast.24.r, bf16[512,2048]{1,0:T(8,128)(2,1)} %get-tuple-element.217.refs_0_, bf16[512,2048]{1,0:T(8,128)(2,1)} %collective-permute-done.30.refs_1_, bf16[512,2048]{1,0:T(8,128)(2,1)} %copy-done.25, bf16[512,2048]{1,0:T(8,128)(2,1)} %collective-permute-done.56.refs_3_, ...), custom_call_target="tpu_custom_call" | custom-call | flops 6442450944 | bytes 25165824 | tf_op jit(solution)/shard_map/attention_grads/pallas_call | solution.py:123
  523.0 9.9 %all-to-all-done.7 = bf16[4,16,1024]{2,1,0:T(8,128)(2,1)S(1)} async-done(((bf16[4,16,1024]{2,1,0:T(8,128)(2,1)}), bf16[4,16,1024]{2,1,0:T(8,128)(2,1)S(1)}, u32[]{:S(2)}, u32[]{:S(2)}) %all-to-all-start.7) | async-done | bytes 131104 | tf_op jit(solution)/shard_map/all_to_all | solution.py:50
  568.1 13.2 %all-to-all-done.9 = bf16[8,80,1024]{2,1,0:T(8,128)(2,1)} async-done(((bf16[8,80,1024]{2,1,0:T(8,128)(2,1)}), bf16[8,80,1024]{2,1,0:T(8,128)(2,1)}, u32[]{:S(2)}, u32[]{:S(2)}) %all-to-all-start.9) | async-done | bytes 1310752 | tf_op jit(solution)/shard_map/all_to_all | solution.py:50
  583.7 11.1 %all_to_all.71 = bf16[4,16,1024]{2,1,0:T(8,128)(2,1)S(1)} all-to-all(bf16[4,16,1024]{2,1,0:T(8,128)(2,1)S(1)} %bitcast.99), channel_id=1, replica_groups=mesh['z'=4,'x'=2,'c'=2,'y'=2] {'z'}, dimensions={0} | all-to-all | bytes 262144 | tf_op jit(solution)/shard_map/all_to_all | solution.py:50
  594.8 9.6 %reduce-scatter.8.cloned.1.call-done = bf16[256,3072]{1,0:T(8,128)(2,1)} async-done(((bf16[1024,3072]{1,0:T(8,128)(2,1)}), bf16[256,3072]{1,0:T(8,128)(2,1)}) %reduce-scatter.8.cloned.1.call-update) | async-done | bytes 1572880 | tf_op jit(solution)/shard_map/reduce_scatter | solution.py:99
  609.6 11.4 %all_to_all.72 = bf16[4,16,1024]{2,1,0:T(8,128)(2,1)S(1)} all-to-all(bf16[4,16,1024]{2,1,0:T(8,128)(2,1)S(1)} %broadcast_in_dim.13), channel_id=1, replica_groups=mesh['z'=4,'x'=2,'c'=2,'y'=2] {'z'}, dimensions={0} | all-to-all | bytes 262144 | tf_op jit(solution)/shard_map/all_to_all | solution.py:50
  (477 shorter events, 374.2 us)
Async XLA Ops:
  7.2 116.0 %all-gather.5.cloned.1.call-start = ((), (), s32[]{:S(2)}) async-start(), calls=%async_computation.16 | async-start | bytes 9437184 | tf_op jit(solution)/shard_map/all_gather | solution.py:95
  27.5 170.5 %all-gather.7.cloned.1.call-start = ((), (), s32[]{:S(2)}) async-start(), calls=%async_computation.17 | async-start | bytes 4718592 | tf_op jit(solution)/shard_map/all_gather | solution.py:95
  65.2 201.3 %all-gather.9.cloned.1.call-start = ((), (), s32[]{:S(2)}) async-start(), calls=%async_computation.18 | async-start | bytes 9437184 | tf_op jit(solution)/shard_map/all_gather | solution.py:95
  80.8 244.6 %all-gather.11.cloned.1.call-start = ((), (), s32[]{:S(2)}) async-start(), calls=%async_computation.19 | async-start | bytes 9437184 | tf_op jit(solution)/shard_map/all_gather | solution.py:95
  156.3 250.3 %reduce-scatter.4.cloned.1.call-start = ((), (), s32[]{:S(2)}) async-start(), calls=%async_computation.20 | async-start | bytes 5242880 | tf_op jit(solution)/shard_map/reduce_scatter | solution.py:99
  264.0 22.7 %collective-permute-start.24 = (bf16[128,2048]{1,0:T(8,128)(2,1)}, bf16[128,2048]{1,0:T(8,128)(2,1)}, u32[]{:S(2)}, u32[]{:S(2)}) collective-permute-start(bf16[128,2048]{1,0:T(8,128)(2,1)} %get-tuple-element.179.refs_3_), channel_id=1, source_target_pairs={{0,1},{1,0},{2,3},{3,2},{4,5},{5,4},{6,7},{7,6},{8,9},{9,8},{10,11... | collective-permute-start | bytes 1572872 | tf_op jit(solution)/shard_map/ppermute | solution.py:46
  264.7 19.9 %collective-permute-start.25 = (bf16[128,2048]{1,0:T(8,128)(2,1)}, bf16[128,2048]{1,0:T(8,128)(2,1)}, u32[]{:S(2)}, u32[]{:S(2)}) collective-permute-start(bf16[128,2048]{1,0:T(8,128)(2,1)} %get-tuple-element.179.refs_3_), channel_id=1, source_target_pairs={{0,4},{4,0},{1,5},{5,1},{2,6},{6,2},{3,7},{7,3},{8,12},{12,8},{9,1... | collective-permute-start | bytes 1572872 | tf_op jit(solution)/shard_map/ppermute | solution.py:46
  296.3 16.8 %collective-permute-start.30 = (bf16[512,2048]{1,0:T(8,128)(2,1)}, bf16[512,2048]{1,0:T(8,128)(2,1)}, u32[]{:S(2)}, u32[]{:S(2)}) collective-permute-start(bf16[512,2048]{1,0:T(8,128)(2,1)} %get-tuple-element.217.refs_0_), channel_id=1, source_target_pairs={{0,2},{2,0},{1,3},{3,1},{4,6},{6,4},{5,7},{7,5},{8,10},{10,8},{9,1... | collective-permute-start | bytes 6291464 | tf_op jit(solution)/shard_map/ppermute | solution.py:46
  296.8 16.4 %collective-permute-start.32 = (bf16[512,2048]{1,0:T(8,128)(2,1)}, bf16[512,2048]{1,0:T(8,128)(2,1)}, u32[]{:S(2)}, u32[]{:S(2)}) collective-permute-start(bf16[512,2048]{1,0:T(8,128)(2,1)} %get-tuple-element.220.refs_4_), channel_id=1, source_target_pairs={{0,2},{2,0},{1,3},{3,1},{4,6},{6,4},{5,7},{7,5},{8,10},{10,8},{9,1... | collective-permute-start | bytes 6291464 | tf_op jit(solution)/shard_map/ppermute | solution.py:46
  296.9 16.3 %collective-permute-start.34 = (bf16[512,2048]{1,0:T(8,128)(2,1)}, bf16[512,2048]{1,0:T(8,128)(2,1)}, u32[]{:S(2)}, u32[]{:S(2)}) collective-permute-start(bf16[512,2048]{1,0:T(8,128)(2,1)} %get-tuple-element.189.refs_0_), channel_id=1, source_target_pairs={{0,2},{2,0},{1,3},{3,1},{4,6},{6,4},{5,7},{7,5},{8,10},{10,8},{9,1... | collective-permute-start | bytes 6291464 | tf_op jit(solution)/shard_map/ppermute | solution.py:46
  313.2 170.5 %reduce-scatter.6.cloned.1.call-start = ((), (), s32[]{:S(2)}) async-start(), calls=%async_computation.21 | async-start | bytes 5242880 | tf_op jit(solution)/shard_map/reduce_scatter | solution.py:99
  349.0 39.9 %collective-permute-start.43 = (bf16[512,2048]{1,0:T(8,128)(2,1)S(1)}, bf16[512,2048]{1,0:T(8,128)(2,1)S(1)}, u32[]{:S(2)}, u32[]{:S(2)}) collective-permute-start(bf16[512,2048]{1,0:T(8,128)(2,1)S(1)} %feed_down.1.refs_2_), channel_id=1, source_target_pairs={{0,2},{2,0},{1,3},{3,1},{4,6},{6,4},{5,7},{7,5},{8,10},{10,8},{9,1... | collective-permute-start | bytes 6291464 | tf_op jit(solution)/shard_map/ppermute | solution.py:46
  407.4 197.0 %reduce-scatter.8.cloned.1.call-start = ((), (), s32[]{:S(2)}) async-start(), calls=%async_computation.22 | async-start | bytes 7864320 | tf_op jit(solution)/shard_map/reduce_scatter | solution.py:99
  466.0 17.6 %collective-permute-start.54 = (bf16[128,2048]{1,0:T(8,128)(2,1)}, bf16[128,2048]{1,0:T(8,128)(2,1)S(1)}, u32[]{:S(2)}, u32[]{:S(2)}) collective-permute-start(bf16[128,2048]{1,0:T(8,128)(2,1)} %get-tuple-element.211), channel_id=1, source_target_pairs={{0,4},{4,0},{1,5},{5,1},{2,6},{6,2},{3,7},{7,3},{8,12},{12,8},{9,1... | collective-permute-start | bytes 1572872 | tf_op jit(solution)/shard_map/ppermute | solution.py:46
  496.0 20.5 %all-to-all-start.6 = ((bf16[8,16,1024]{2,1,0:T(8,128)(2,1)}), bf16[8,16,1024]{2,1,0:T(8,128)(2,1)S(1)}, u32[]{:S(2)}, u32[]{:S(2)}) async-start(bf16[8,16,1024]{2,1,0:T(8,128)(2,1)} %bitcast.29), calls=%async_computation.7 | async-start | bytes 524288 | tf_op jit(solution)/shard_map/all_to_all | solution.py:50
  505.1 27.9 %collective-permute-start.60 = (bf16[64,4096]{1,0:T(8,128)(2,1)}, bf16[64,4096]{1,0:T(8,128)(2,1)S(1)}, u32[]{:S(2)}, u32[]{:S(2)}) collective-permute-start(bf16[64,4096]{1,0:T(8,128)(2,1)} %get-tuple-element.233), channel_id=1, source_target_pairs={{0,1},{1,0},{2,3},{3,2},{4,5},{5,4},{6,7},{7,6},{8,9},{9,8},{10,11... | collective-permute-start | bytes 1572872 | tf_op jit(solution)/shard_map/ppermute | solution.py:46
  505.5 28.2 %collective-permute-start.61 = (bf16[64,4096]{1,0:T(8,128)(2,1)}, bf16[64,4096]{1,0:T(8,128)(2,1)S(1)}, u32[]{:S(2)}, u32[]{:S(2)}) collective-permute-start(bf16[64,4096]{1,0:T(8,128)(2,1)} %get-tuple-element.234), channel_id=1, source_target_pairs={{0,4},{4,0},{1,5},{5,1},{2,6},{6,2},{3,7},{7,3},{8,12},{12,8},{9,1... | collective-permute-start | bytes 1572872 | tf_op jit(solution)/shard_map/ppermute | solution.py:46
  507.0 26.8 %collective-permute-start.62 = (bf16[64,4096]{1,0:T(8,128)(2,1)}, bf16[64,4096]{1,0:T(8,128)(2,1)S(1)}, u32[]{:S(2)}, u32[]{:S(2)}) collective-permute-start(bf16[64,4096]{1,0:T(8,128)(2,1)} %get-tuple-element.235), channel_id=1, source_target_pairs={{0,5},{1,4},{4,1},{5,0},{2,7},{3,6},{6,3},{7,2},{8,13},{9,12},{12,... | collective-permute-start | bytes 1572872 | tf_op jit(solution)/shard_map/ppermute | solution.py:90
  509.4 31.1 %collective-permute-start.66 = (bf16[128,2048]{1,0:T(8,128)(2,1)}, bf16[128,2048]{1,0:T(8,128)(2,1)}, u32[]{:S(2)}, u32[]{:S(2)}) collective-permute-start(bf16[128,2048]{1,0:T(8,128)(2,1)} %pad_maximum_fusion.12), channel_id=1, source_target_pairs={{0,1},{1,0},{2,3},{3,2},{4,5},{5,4},{6,7},{7,6},{8,9},{9,8},{10,11... | collective-permute-start | bytes 1572872 | tf_op jit(solution)/shard_map/ppermute | solution.py:46
  522.3 18.4 %collective-permute-start.64 = (bf16[128,2048]{1,0:T(8,128)(2,1)}, bf16[128,2048]{1,0:T(8,128)(2,1)}, u32[]{:S(2)}, u32[]{:S(2)}) collective-permute-start(bf16[128,2048]{1,0:T(8,128)(2,1)} %pad_maximum_fusion.11), channel_id=1, source_target_pairs={{0,4},{4,0},{1,5},{5,1},{2,6},{6,2},{3,7},{7,3},{8,12},{12,8},{9,1... | collective-permute-start | bytes 1572872 | tf_op jit(solution)/shard_map/ppermute | solution.py:46
  534.9 19.1 %all-to-all-start.8 = ((bf16[8,64,1024]{2,1,0:T(8,128)(2,1)}), bf16[8,64,1024]{2,1,0:T(8,128)(2,1)}, u32[]{:S(2)}, u32[]{:S(2)}) async-start(bf16[8,64,1024]{2,1,0:T(8,128)(2,1)} %broadcast_in_dim.12), calls=%async_computation.10 | async-start | bytes 2097152 | tf_op jit(solution)/shard_map/all_to_all | solution.py:50
  559.6 21.8 %all-to-all-start.9 = ((bf16[8,80,1024]{2,1,0:T(8,128)(2,1)}), bf16[8,80,1024]{2,1,0:T(8,128)(2,1)}, u32[]{:S(2)}, u32[]{:S(2)}) async-start(bf16[8,80,1024]{2,1,0:T(8,128)(2,1)} %copy-done.27), calls=%async_computation.11 | async-start | bytes 2621440 | tf_op jit(solution)/shard_map/all_to_all | solution.py:50
  609.0 17.6 %collective-permute-start.69 = (bf16[64,3072]{1,0:T(8,128)(2,1)S(1)}, bf16[64,3072]{1,0:T(8,128)(2,1)S(1)}, u32[]{:S(2)}, u32[]{:S(2)}) collective-permute-start(bf16[64,3072]{1,0:T(8,128)(2,1)S(1)} %get-tuple-element.266), channel_id=1, source_target_pairs={{0,5},{1,4},{4,1},{5,0},{2,7},{3,6},{6,3},{7,2},{8,13},{9,12},{12,... | collective-permute-start | bytes 1179656 | tf_op jit(solution)/shard_map/ppermute | solution.py:90
  627.7 21.0 %all-to-all-start.12 = ((bf16[8,64,1024]{2,1,0:T(8,128)(2,1)}), bf16[8,64,1024]{2,1,0:T(8,128)(2,1)S(1)}, u32[]{:S(2)}, u32[]{:S(2)}) async-start(bf16[8,64,1024]{2,1,0:T(8,128)(2,1)} %broadcast_in_dim.14), calls=%async_computation.15 | async-start | bytes 2097152 | tf_op jit(solution)/shard_map/all_to_all | solution.py:50
  (156 other events, 1631.5 us)
Sparse Core Ops, SparseCore 0:
  27.6 83.6 all-gather.4
  112.9 47.9 all-gather.6
  162.5 80.7 all-gather.8
  244.7 80.5 all-gather.10
  327.5 75.2 reduce-scatter.3
  406.8 75.5 reduce-scatter.5
  484.7 119.6 reduce-scatter.7

commit v20 on v19

--- a/solution.py
+++ b/solution.py
@@ -963,7 +963,12 @@
         result = scatter_first(token_blocks(result))
         attn_branch, grad_self_mixed = gather_mm(attn_branch, first, 3 * group, group, "out_back")
         grad_projected = self_back(projected, grad_self_mixed, 2 * images)
-        grad_projected, result = lax.optimization_barrier((grad_projected, result))
+        kv_part = kv_grad.astype(BF).reshape(2, z_size, -1, 2 * group)
+        kv_part = kv_part.transpose(1, 0, 2, 3).reshape(2 * z_size, -1, 2 * group)
+        grad_projected, result, kv_part = lax.optimization_barrier(
+            (grad_projected, result, kv_part)
+        )
+        kv_part = trade(kv_part, DATA)
         result = scatter_second(result)
         rest_part = grad_products(
             [
@@ -975,8 +980,8 @@
             "attention_grads",
             *halves,
         )
-        grad_projected, result, kv_grad, rest_part = lax.optimization_barrier(
-            (grad_projected, result, kv_grad, rest_part)
+        grad_projected, result, kv_part, rest_part = lax.optimization_barrier(
+            (grad_projected, result, kv_part, rest_part)
         )
         rest_part, up_rows = lax.optimization_barrier((rest_part, up_rows))
         rest_rows = scatter_grad(rest_part, grad_axes)
@@ -993,9 +998,7 @@
         sums = jnp.concatenate([gain_grad_a, gain_grad_b, gain_grad_c, mask_grad], axis=0)
 
 
-        kv_part = kv_grad.astype(BF).reshape(2, z_size, -1, 2 * group)
-        kv_part = kv_part.transpose(1, 0, 2, 3).reshape(2 * z_size, -1, 2 * group)
-        kv_part = trade(kv_part, DATA).astype(F32).sum(axis=0).astype(BF)
+        kv_part = kv_part.astype(F32).sum(axis=0).astype(BF)
         kv_sum = spread(kv_part, "z", z_size).reshape(-1, 2 * group)
         wide_rows = swap_parts(pick_rows([down_rows, up_rows], rank))
         kv_sum, wide_rows = lax.optimization_barrier((kv_sum, wide_rows))
@@ -1014,12 +1017,11 @@
         sums = layer_order(add_z(whole_of(caption_part[half_context:], width)))
         caption_part = caption_part[:half_context].astype(BF).reshape(z_size, -1, text_width // 4)
         caption_part = trade(caption_part, "z").astype(F32).sum(axis=0).astype(BF)
-        rest_rows = pick_rows([rest_rows], rank)
+        caption_part = spread(caption_part, "z", z_size).reshape(half_context, -1)
+        caption_part = spread(caption_part, PLANE, 8)
         caption_part, rest_rows = lax.optimization_barrier((caption_part, rest_rows))
-        caption_part = spread(caption_part, "z", z_size).reshape(half_context, -1)
-        rest_rows = swap_parts(rest_rows)
-        caption_part, rest_rows = lax.optimization_barrier((caption_part, rest_rows))
-        grad_caption = caption_output(spread(caption_part, PLANE, 8))
+        grad_caption = caption_output(caption_part)
+        rest_rows = swap_parts(pick_rows([rest_rows], rank))
         qkv_grad, out_grad, grad_cross, cross_out_grad = finish_all(
             rest_rows, kv_weight_grad, rank
         )

time: 667 us -> 671 us (level)
  blocking collectives: 104 us -> 124 us
  starting transfers between devices: 99.6 us -> 88.3 us
  waiting for transfers between devices: 220 us -> 211 us
  Pallas kernels: 111 us -> 118 us
    all_to_all x8 -> x9, blocking collectives: 104 us -> 124 us  [trade(): return lax.all_to_all(blocks, axes, 0, 0, tiled=True)]
    all_to_all x5 -> x4, waiting for transfers between devices: 37.4 us -> 18.5 us  [trade(): return lax.all_to_all(blocks, axes, 0, 0, tiled=True)]
    ppermute x67, waiting for transfers between devices: 146 us -> 163 us  [swap(): return lax.ppermute(values, axis, PAIR)]
    reduce_scatter x3, waiting for transfers between devices: 9.63 us -> 0.02 us  [scatter_grad(): summed = lax.psum_scatter(partial, axes, scatter_dimension=0, tiled=True)]
    all_to_all x5 -> x4, starting transfers between devices: 20 us -> 18.2 us  [trade(): return lax.all_to_all(blocks, axes, 0, 0, tiled=True)]
    unnamed x196 -> x174, local copies, waits for them, and re-layouts: 42.2 us -> 41.2 us
  transfers between devices with their start and end apart: 84 -> 83, of which waited for: 46 -> 45; matrix products, arithmetic and copies ran while one was open for 10% -> 10% of each run, Pallas kernels for 16% -> 17%
where the time goes in v20:
time: 671 us; the launch traced here: 663 us
  waiting for transfers between devices  211 us (31%)
  blocking collectives  124 us (18%)
  Pallas kernels  118 us (18%)
  starting transfers between devices  88.3 us (13%)
  local copies, waits for them, and re-layouts  66.2 us (10%)
  matrix products  31.8 us (5%)
  between operations  16.6 us (2%)
  other arithmetic  8.22 us (1%)
    ppermute x67, waiting for transfers between devices, swap(): return lax.ppermute(values, axis, PAIR)  163 us
    all_to_all x9, blocking collectives, trade(): return lax.all_to_all(blocks, axes, 0, 0, tiled=True)  124 us
    pallas_call x20, Pallas kernels, call(): pl.pallas_call(kernel, grid=grid, in_specs=in_specs, out_specs=out_specs,...  77.7 us
    ppermute x67, starting transfers between devices, swap(): return lax.ppermute(values, axis, PAIR)  64.6 us
    unnamed x174, local copies, waits for them, and re-layouts  41.2 us
    pallas_call x9, Pallas kernels, call(): pl.pallas_call(kernel, grid_spec=spec, **options)  39.9 us
    dot_general x6, matrix products, dot(): return lax.dot_general(a, b, (dims, ((), ())), preferred_element_type=F32)  31.8 us
    all_to_all x4, waiting for transfers between devices, trade(): return lax.all_to_all(blocks, axes, 0, 0, tiled=True)  18.5 us
  transfers between devices with their start and end apart: 83, of which 45 were waited for; matrix products, arithmetic and copies ran while one was open for 10% of the time, Pallas kernels for 17%

profile of v20, /device:TPU:0, one launch (start us, length us, event | category | flops | bytes accessed | tf_op | source)
XLA Modules:
  0.0 663.3 jit_solution(296204363060809982)
XLA Ops:
  34.6 8.8 %collective-permute-done.1.refs_2_ = bf16[128,2048]{1,0:T(8,128)(2,1)S(1)} collective-permute-done((bf16[128,2048]{1,0:T(8,128)(2,1)S(1)}, bf16[128,2048]{1,0:T(8,128)(2,1)S(1)}, u32[]{:S(2)}, u32[]{:S(2)}) %collective-permute-start.1) | collective-permute-done | bytes 524320 | tf_op jit(solution)/shard_map/ppermute | solution.py:46
  54.9 10.2 %all_to_all.65 = bf16[4,64,1024]{2,1,0:T(8,128)(2,1)} all-to-all(bf16[4,64,1024]{2,1,0:T(8,128)(2,1)S(1)} %copy.75), channel_id=1, replica_groups=mesh['z'=4,'x'=2,'c'=2,'y'=2] {'x','y'}, dimensions={0} | all-to-all | bytes 1048576 | tf_op jit(solution)/shard_map/all_to_all | solution.py:50
  65.2 15.5 %all_to_all.66 = bf16[4,64,2048]{2,1,0:T(8,128)(2,1)} all-to-all(bf16[4,64,2048]{2,1,0:T(8,128)(2,1)} %bitcast.88), channel_id=1, replica_groups=mesh['z'=4,'x'=2,'c'=2,'y'=2] {'x','y'}, dimensions={0} | all-to-all | bytes 2097152 | tf_op jit(solution)/shard_map/all_to_all | solution.py:50
  83.4 16.9 %all_to_all.67 = bf16[8,64,1024]{2,1,0:T(8,128)(2,1)S(1)} all-to-all(bf16[8,64,1024]{2,1,0:T(8,128)(2,1)S(1)} %get-tuple-element.145), channel_id=1, replica_groups=mesh['z'=4,'x'=2,'c'=2,'y'=2] {'x','c','y'}, dimensions={0} | all-to-all | bytes 2097152 | tf_op jit(solution)/shard_map/all_to_all | solution.py:50
  100.4 11.9 %all_to_all.68 = bf16[4,16,1024]{2,1,0:T(8,128)(2,1)S(1)} all-to-all(bf16[4,16,1024]{2,1,0:T(8,128)(2,1)S(1)} %bitcast.96), channel_id=1, replica_groups=mesh['z'=4,'x'=2,'c'=2,'y'=2] {'z'}, dimensions={0} | all-to-all | bytes 262144 | tf_op jit(solution)/shard_map/all_to_all | solution.py:50
  112.3 8.5 %all_to_all.69 = bf16[4,16,1024]{2,1,0:T(8,128)(2,1)S(1)} all-to-all(bf16[4,16,1024]{2,1,0:T(8,128)(2,1)S(1)} %broadcast_in_dim.12), channel_id=1, replica_groups=mesh['z'=4,'x'=2,'c'=2,'y'=2] {'z'}, dimensions={0} | all-to-all | bytes 262144 | tf_op jit(solution)/shard_map/all_to_all | solution.py:50
  138.2 18.2 %all_to_all.70 = bf16[4,64,2048]{2,1,0:T(8,128)(2,1)} all-to-all(bf16[4,64,2048]{2,1,0:T(8,128)(2,1)S(1)} %bitcast.87), channel_id=1, replica_groups=mesh['z'=4,'x'=2,'c'=2,'y'=2] {'x','y'}, dimensions={0} | all-to-all | bytes 2097152 | tf_op jit(solution)/shard_map/all_to_all | solution.py:50
  170.5 10.0 %collective-permute-done.11.refs_3_ = bf16[128,2048]{1,0:T(8,128)(2,1)S(1)} collective-permute-done((bf16[128,2048]{1,0:T(8,128)(2,1)S(1)}, bf16[128,2048]{1,0:T(8,128)(2,1)S(1)}, u32[]{:S(2)}, u32[]{:S(2)}) %collective-permute-start.11) | collective-permute-done | bytes 524320 | tf_op jit(solution)/shard_map/ppermute | solution.py:46
  184.9 9.2 %collective-permute-done.13.refs_2_ = bf16[128,2048]{1,0:T(8,128)(2,1)S(1)} collective-permute-done((bf16[128,2048]{1,0:T(8,128)(2,1)S(1)}, bf16[128,2048]{1,0:T(8,128)(2,1)S(1)}, u32[]{:S(2)}, u32[]{:S(2)}) %collective-permute-start.13) | collective-permute-done | bytes 524320 | tf_op jit(solution)/shard_map/ppermute | solution.py:46
  270.9 11.9 %feed_up.1 = (bf16[512,2048]{1,0:T(8,128)(2,1)}, bf16[512,2048]{1,0:T(8,128)(2,1)}, f32[512,2048]{1,0:T(8,128)}) custom-call(bf16[128,2048]{1,0:T(8,128)(2,1)S(1)} %copy-done.62, bf16[128,2048]{1,0:T(8,128)(2,1)S(1)} %copy-done.58, bf16[128,2048]{1,0:T(8,128)(2,1)S(1)} %copy-done.56, bf16[64,2048]{1,0:T(8,128)(2,1)S(1)} %copy-done.68, ...), custom_call_target="tpu_custom_call" | custom-call | flops 4294967296 | bytes 12582912 | tf_op jit(solution)/shard_map/feed_up/pallas_call | solution.py:112
  302.2 8.8 %down_grads.1 = bf16[1024,2048]{1,0:T(8,128)(2,1)} custom-call(s32[1]{0:T(128)} %bitcast.24.r, bf16[512,2048]{1,0:T(8,128)(2,1)S(1)} %constant_dynamic-update-slice_fusion.refs_0_.dy, bf16[512,2048]{1,0:T(8,128)(2,1)S(1)} %collective-permute-done.28.refs_1_, bf16[512,2048]{1,0:T(8,128)(2,1)} %get-tuple-element.184.refs_2_, bf16[512,2048]{1,0:T(8,128)(2,1)} %copy-done.84), custom_call_target="tpu_custom_call" | custom-call | flops 4294967296 | bytes 16777216 | tf_op jit(solution)/shard_map/down_grads/pallas_call | solution.py:123
  312.6 12.7 %all-gather.11.cloned.1.call-done.down = bf16[2048,2048]{1,0:T(8,128)(2,1)} async-done(((bf16[256,2048]{1,0:T(8,128)(2,1)}), bf16[2048,2048]{1,0:T(8,128)(2,1)}) %all-gather.11.cloned.1.call-update) | async-done | bytes 8388624 | tf_op jit(solution)/shard_map/all_gather | solution.py:95
  326.9 9.9 %feed_down.1.refs_2_ = bf16[512,2048]{1,0:T(8,128)(2,1)S(1)} custom-call(bf16[512,2048]{1,0:T(8,128)(2,1)S(1)} %copy-done.14, f32[512,2048]{1,0:T(8,128)} %get-tuple-element.177.slope_ref, bf16[2048,2048]{1,0:T(8,128)(2,1)} %all-gather.11.cloned.1.call-done.down), custom_call_target="tpu_custom_call" | custom-call | flops 4294967296 | bytes 25165824 | tf_op jit(solution)/shard_map/feed_down/pallas_call | solution.py:112
  336.9 8.9 %convolution_convert_fusion.2 = bf16[512,2048]{1,0:T(8,128)(2,1)S(1)} fusion(bf16[512,2048]{1,0:T(8,128)(2,1)S(1)} %feed_down.1.refs_2_, bf16[2048,2048]{1,0:T(8,128)(2,1)} %all-gather.9.cloned.1.call-done.refs_5_), kind=kOutput, calls=%fused_computation.5 | convolution fusion | flops 4296015872 | bytes 12582912 | tf_op jit(solution)/shard_map/dot_general | solution.py:26
  358.2 10.9 %collective-permute-done.38.refs_2_ = bf16[128,2048]{1,0:T(8,128)(2,1)S(1)} collective-permute-done((bf16[128,2048]{1,0:T(8,128)(2,1)S(1)}, bf16[128,2048]{1,0:T(8,128)(2,1)S(1)}, u32[]{:S(2)}, u32[]{:S(2)}) %collective-permute-start.38) | collective-permute-done | bytes 524320 | tf_op jit(solution)/shard_map/ppermute | solution.py:46
  375.5 9.2 %convolution_convert_fusion.1 = bf16[512,2048]{1,0:T(8,128)(2,1)} fusion(bf16[512,2048]{1,0:T(8,128)(2,1)S(1)} %copy-done.82, bf16[2048,2048]{1,0:T(8,128)(2,1)} %all-gather.11.cloned.1.call-done.down), kind=kOutput, calls=%fused_computation.4 | convolution fusion | flops 4296015872 | bytes 12582912 | tf_op jit(solution)/shard_map/dot_general | solution.py:26
  390.3 8.8 %up_grads.1 = bf16[1024,2048]{1,0:T(8,128)(2,1)} custom-call(s32[1]{0:T(128)} %bitcast.24.r, bf16[512,2048]{1,0:T(8,128)(2,1)} %get-tuple-element.182.refs_0_, bf16[512,2048]{1,0:T(8,128)(2,1)} %collective-permute-done.34.refs_1_, bf16[512,2048]{1,0:T(8,128)(2,1)} %copy-done.22, bf16[512,2048]{1,0:T(8,128)(2,1)} %copy-done.83), custom_call_target="tpu_custom_call" | custom-call | flops 4294967296 | bytes 16777216 | tf_op jit(solution)/shard_map/up_grads/pallas_call | solution.py:123
  433.2 12.0 %collective-permute-done.49.refs_2_ = bf16[128,2048]{1,0:T(8,128)(2,1)S(1)} collective-permute-done((bf16[128,2048]{1,0:T(8,128)(2,1)S(1)}, bf16[128,2048]{1,0:T(8,128)(2,1)S(1)}, u32[]{:S(2)}, u32[]{:S(2)}) %collective-permute-start.49) | collective-permute-done | bytes 524320 | tf_op jit(solution)/shard_map/ppermute | solution.py:46
  476.3 11.8 %attention_grads.1 = bf16[1024,3072]{1,0:T(8,128)(2,1)} custom-call(s32[1]{0:T(128)} %bitcast.24.r, bf16[512,2048]{1,0:T(8,128)(2,1)} %get-tuple-element.211.refs_0_, bf16[512,2048]{1,0:T(8,128)(2,1)} %collective-permute-done.30.refs_1_, bf16[512,2048]{1,0:T(8,128)(2,1)} %get-tuple-element.213.refs_2_, bf16[512,2048]{1,0:T(8,128)(2,1)} %collective-permute-done.56.refs_3_, ...), custom_call_target="tpu_custom_call" | custom-call | flops 6442450944 | bytes 25165824 | tf_op jit(solution)/shard_map/attention_grads/pallas_call | solution.py:123
  518.1 16.2 %collective-permute-done.60.refs_1_ = bf16[64,4096]{1,0:T(8,128)(2,1)S(1)} collective-permute-done((bf16[64,4096]{1,0:T(8,128)(2,1)}, bf16[64,4096]{1,0:T(8,128)(2,1)S(1)}, u32[]{:S(2)}, u32[]{:S(2)}) %collective-permute-start.60) | collective-permute-done | bytes 524320 | tf_op jit(solution)/shard_map/ppermute | solution.py:46
  573.8 11.2 %all-to-all-done.9 = bf16[8,80,1024]{2,1,0:T(8,128)(2,1)S(1)} async-done(((bf16[8,80,1024]{2,1,0:T(8,128)(2,1)}), bf16[8,80,1024]{2,1,0:T(8,128)(2,1)S(1)}, u32[]{:S(2)}, u32[]{:S(2)}) %all-to-all-start.9) | async-done | bytes 1310752 | tf_op jit(solution)/shard_map/all_to_all | solution.py:50
  585.9 16.9 %all_to_all.71 = bf16[4,16,1024]{2,1,0:T(8,128)(2,1)S(1)} all-to-all(bf16[4,16,1024]{2,1,0:T(8,128)(2,1)S(1)} %bitcast.98), channel_id=1, replica_groups=mesh['z'=4,'x'=2,'c'=2,'y'=2] {'z'}, dimensions={0} | all-to-all | bytes 262144 | tf_op jit(solution)/shard_map/all_to_all | solution.py:50
  602.9 8.5 %all_to_all.72 = bf16[4,16,1024]{2,1,0:T(8,128)(2,1)S(1)} all-to-all(bf16[4,16,1024]{2,1,0:T(8,128)(2,1)S(1)} %broadcast_in_dim.15), channel_id=1, replica_groups=mesh['z'=4,'x'=2,'c'=2,'y'=2] {'z'}, dimensions={0} | all-to-all | bytes 262144 | tf_op jit(solution)/shard_map/all_to_all | solution.py:50
  611.5 17.1 %all_to_all.73.block = bf16[8,64,1024]{2,1,0:T(8,128)(2,1)S(1)} all-to-all(bf16[8,64,1024]{2,1,0:T(8,128)(2,1)S(1)} %broadcast_in_dim.17), channel_id=1, replica_groups=mesh['z'=4,'x'=2,'c'=2,'y'=2] {'x','c','y'}, dimensions={0} | all-to-all | bytes 2097152 | tf_op jit(solution)/shard_map/all_to_all | solution.py:50
  (454 shorter events, 363.0 us)
Async XLA Ops:
  7.2 116.0 %all-gather.5.cloned.1.call-start = ((), (), s32[]{:S(2)}) async-start(), calls=%async_computation.16 | async-start | bytes 9437184 | tf_op jit(solution)/shard_map/all_gather | solution.py:95
  27.5 170.0 %all-gather.7.cloned.1.call-start = ((), (), s32[]{:S(2)}) async-start(), calls=%async_computation.17 | async-start | bytes 4718592 | tf_op jit(solution)/shard_map/all_gather | solution.py:95
  65.2 200.7 %all-gather.9.cloned.1.call-start = ((), (), s32[]{:S(2)}) async-start(), calls=%async_computation.18 | async-start | bytes 9437184 | tf_op jit(solution)/shard_map/all_gather | solution.py:95
  80.7 244.6 %all-gather.11.cloned.1.call-start = ((), (), s32[]{:S(2)}) async-start(), calls=%async_computation.19 | async-start | bytes 9437184 | tf_op jit(solution)/shard_map/all_gather | solution.py:95
  156.4 249.9 %reduce-scatter.4.cloned.1.call-start = ((), (), s32[]{:S(2)}) async-start(), calls=%async_computation.20 | async-start | bytes 5242880 | tf_op jit(solution)/shard_map/reduce_scatter | solution.py:99
  263.9 22.3 %collective-permute-start.24 = (bf16[128,2048]{1,0:T(8,128)(2,1)}, bf16[128,2048]{1,0:T(8,128)(2,1)}, u32[]{:S(2)}, u32[]{:S(2)}) collective-permute-start(bf16[128,2048]{1,0:T(8,128)(2,1)} %get-tuple-element.172.refs_3_), channel_id=1, source_target_pairs={{0,1},{1,0},{2,3},{3,2},{4,5},{5,4},{6,7},{7,6},{8,9},{9,8},{10,11... | collective-permute-start | bytes 1572872 | tf_op jit(solution)/shard_map/ppermute | solution.py:46
  263.9 20.1 %collective-permute-start.25 = (bf16[128,2048]{1,0:T(8,128)(2,1)}, bf16[128,2048]{1,0:T(8,128)(2,1)}, u32[]{:S(2)}, u32[]{:S(2)}) collective-permute-start(bf16[128,2048]{1,0:T(8,128)(2,1)} %get-tuple-element.172.refs_3_), channel_id=1, source_target_pairs={{0,4},{4,0},{1,5},{5,1},{2,6},{6,2},{3,7},{7,3},{8,12},{12,8},{9,1... | collective-permute-start | bytes 1572872 | tf_op jit(solution)/shard_map/ppermute | solution.py:46
  295.7 16.6 %collective-permute-start.30 = (bf16[512,2048]{1,0:T(8,128)(2,1)}, bf16[512,2048]{1,0:T(8,128)(2,1)}, u32[]{:S(2)}, u32[]{:S(2)}) collective-permute-start(bf16[512,2048]{1,0:T(8,128)(2,1)} %get-tuple-element.211.refs_0_), channel_id=1, source_target_pairs={{0,2},{2,0},{1,3},{3,1},{4,6},{6,4},{5,7},{7,5},{8,10},{10,8},{9,1... | collective-permute-start | bytes 6291464 | tf_op jit(solution)/shard_map/ppermute | solution.py:46
  312.4 177.4 %reduce-scatter.6.cloned.1.call-start = ((), (), s32[]{:S(2)}) async-start(), calls=%async_computation.21 | async-start | bytes 5242880 | tf_op jit(solution)/shard_map/reduce_scatter | solution.py:99
  349.0 39.9 %collective-permute-start.43 = (bf16[512,2048]{1,0:T(8,128)(2,1)S(1)}, bf16[512,2048]{1,0:T(8,128)(2,1)S(1)}, u32[]{:S(2)}, u32[]{:S(2)}) collective-permute-start(bf16[512,2048]{1,0:T(8,128)(2,1)S(1)} %feed_down.1.refs_2_), channel_id=1, source_target_pairs={{0,2},{2,0},{1,3},{3,1},{4,6},{6,4},{5,7},{7,5},{8,10},{10,8},{9,1... | collective-permute-start | bytes 6291464 | tf_op jit(solution)/shard_map/ppermute | solution.py:46
  455.7 19.6 %collective-permute-start.57 = (bf16[512,2048]{1,0:T(8,128)(2,1)}, bf16[512,2048]{1,0:T(8,128)(2,1)}, u32[]{:S(2)}, u32[]{:S(2)}) collective-permute-start(bf16[512,2048]{1,0:T(8,128)(2,1)} %get-tuple-element.216.refs_6_), channel_id=1, source_target_pairs={{0,2},{2,0},{1,3},{3,1},{4,6},{6,4},{5,7},{7,5},{8,10},{10,8},{9,1... | collective-permute-start | bytes 6291464 | tf_op jit(solution)/shard_map/ppermute | solution.py:46
  467.5 20.6 %collective-permute-start.54 = (bf16[128,2048]{1,0:T(8,128)(2,1)}, bf16[128,2048]{1,0:T(8,128)(2,1)}, u32[]{:S(2)}, u32[]{:S(2)}) collective-permute-start(bf16[128,2048]{1,0:T(8,128)(2,1)} %get-tuple-element.208), channel_id=1, source_target_pairs={{0,4},{4,0},{1,5},{5,1},{2,6},{6,2},{3,7},{7,3},{8,12},{12,8},{9,1... | collective-permute-start | bytes 1572872 | tf_op jit(solution)/shard_map/ppermute | solution.py:46
  469.1 19.0 %all-to-all-start.6 = ((bf16[8,16,1024]{2,1,0:T(8,128)(2,1)}), bf16[8,16,1024]{2,1,0:T(8,128)(2,1)S(1)}, u32[]{:S(2)}, u32[]{:S(2)}) async-start(bf16[8,16,1024]{2,1,0:T(8,128)(2,1)} %bitcast.29), calls=%async_computation.7 | async-start | bytes 524288 | tf_op jit(solution)/shard_map/all_to_all | solution.py:50
  474.3 154.2 %reduce-scatter.8.cloned.1.call-start = ((), (), s32[]{:S(2)}) async-start(), calls=%async_computation.22 | async-start | bytes 7864320 | tf_op jit(solution)/shard_map/reduce_scatter | solution.py:99
  501.0 17.1 %all-to-all-start.7 = ((bf16[4,16,1024]{2,1,0:T(8,128)(2,1)}), bf16[4,16,1024]{2,1,0:T(8,128)(2,1)}, u32[]{:S(2)}, u32[]{:S(2)}) async-start(bf16[4,16,1024]{2,1,0:T(8,128)(2,1)} %broadcast_in_dim.13), calls=%async_computation.8 | async-start | bytes 262144 | tf_op jit(solution)/shard_map/all_to_all | solution.py:50
  509.6 24.8 %collective-permute-start.60 = (bf16[64,4096]{1,0:T(8,128)(2,1)}, bf16[64,4096]{1,0:T(8,128)(2,1)S(1)}, u32[]{:S(2)}, u32[]{:S(2)}) collective-permute-start(bf16[64,4096]{1,0:T(8,128)(2,1)} %get-tuple-element.227), channel_id=1, source_target_pairs={{0,1},{1,0},{2,3},{3,2},{4,5},{5,4},{6,7},{7,6},{8,9},{9,8},{10,11... | collective-permute-start | bytes 1572872 | tf_op jit(solution)/shard_map/ppermute | solution.py:46
  510.7 24.4 %collective-permute-start.61 = (bf16[64,4096]{1,0:T(8,128)(2,1)}, bf16[64,4096]{1,0:T(8,128)(2,1)S(1)}, u32[]{:S(2)}, u32[]{:S(2)}) collective-permute-start(bf16[64,4096]{1,0:T(8,128)(2,1)} %get-tuple-element.228), channel_id=1, source_target_pairs={{0,4},{4,0},{1,5},{5,1},{2,6},{6,2},{3,7},{7,3},{8,12},{12,8},{9,1... | collective-permute-start | bytes 1572872 | tf_op jit(solution)/shard_map/ppermute | solution.py:46
  512.0 25.4 %collective-permute-start.62 = (bf16[64,4096]{1,0:T(8,128)(2,1)}, bf16[64,4096]{1,0:T(8,128)(2,1)S(1)}, u32[]{:S(2)}, u32[]{:S(2)}) collective-permute-start(bf16[64,4096]{1,0:T(8,128)(2,1)} %get-tuple-element.229), channel_id=1, source_target_pairs={{0,5},{1,4},{4,1},{5,0},{2,7},{3,6},{6,3},{7,2},{8,13},{9,12},{12,... | collective-permute-start | bytes 1572872 | tf_op jit(solution)/shard_map/ppermute | solution.py:90
  514.9 30.4 %collective-permute-start.66 = (bf16[128,2048]{1,0:T(8,128)(2,1)}, bf16[128,2048]{1,0:T(8,128)(2,1)}, u32[]{:S(2)}, u32[]{:S(2)}) collective-permute-start(bf16[128,2048]{1,0:T(8,128)(2,1)} %pad_maximum_fusion.12), channel_id=1, source_target_pairs={{0,1},{1,0},{2,3},{3,2},{4,5},{5,4},{6,7},{7,6},{8,9},{9,8},{10,11... | collective-permute-start | bytes 1572872 | tf_op jit(solution)/shard_map/ppermute | solution.py:46
  516.9 28.8 %collective-permute-start.64 = (bf16[128,2048]{1,0:T(8,128)(2,1)}, bf16[128,2048]{1,0:T(8,128)(2,1)}, u32[]{:S(2)}, u32[]{:S(2)}) collective-permute-start(bf16[128,2048]{1,0:T(8,128)(2,1)} %pad_maximum_fusion.11), channel_id=1, source_target_pairs={{0,4},{4,0},{1,5},{5,1},{2,6},{6,2},{3,7},{7,3},{8,12},{12,8},{9,1... | collective-permute-start | bytes 1572872 | tf_op jit(solution)/shard_map/ppermute | solution.py:46
  539.6 18.8 %all-to-all-start.8 = ((bf16[8,64,1024]{2,1,0:T(8,128)(2,1)}), bf16[8,64,1024]{2,1,0:T(8,128)(2,1)}, u32[]{:S(2)}, u32[]{:S(2)}) async-start(bf16[8,64,1024]{2,1,0:T(8,128)(2,1)} %broadcast_in_dim.14), calls=%async_computation.10 | async-start | bytes 2097152 | tf_op jit(solution)/shard_map/all_to_all | solution.py:50
  564.0 21.0 %all-to-all-start.9 = ((bf16[8,80,1024]{2,1,0:T(8,128)(2,1)}), bf16[8,80,1024]{2,1,0:T(8,128)(2,1)S(1)}, u32[]{:S(2)}, u32[]{:S(2)}) async-start(bf16[8,80,1024]{2,1,0:T(8,128)(2,1)} %copy-done.24), calls=%async_computation.11 | async-start | bytes 2621440 | tf_op jit(solution)/shard_map/all_to_all | solution.py:50
  631.2 17.5 %collective-permute-start.69 = (bf16[64,3072]{1,0:T(8,128)(2,1)}, bf16[64,3072]{1,0:T(8,128)(2,1)S(1)}, u32[]{:S(2)}, u32[]{:S(2)}) collective-permute-start(bf16[64,3072]{1,0:T(8,128)(2,1)} %get-tuple-element.255), channel_id=1, source_target_pairs={{0,1},{1,0},{2,3},{3,2},{4,5},{5,4},{6,7},{7,6},{8,9},{9,8},{10,11... | collective-permute-start | bytes 1179656 | tf_op jit(solution)/shard_map/ppermute | solution.py:46
  633.2 19.3 %collective-permute-start.71 = (bf16[64,3072]{1,0:T(8,128)(2,1)}, bf16[64,3072]{1,0:T(8,128)(2,1)}, u32[]{:S(2)}, u32[]{:S(2)}) collective-permute-start(bf16[64,3072]{1,0:T(8,128)(2,1)} %get-tuple-element.257), channel_id=1, source_target_pairs={{0,5},{1,4},{4,1},{5,0},{2,7},{3,6},{6,3},{7,2},{8,13},{9,12},{12,... | collective-permute-start | bytes 1179656 | tf_op jit(solution)/shard_map/ppermute | solution.py:90
  (144 other events, 1555.1 us)
Sparse Core Ops, SparseCore 0:
  27.6 83.6 all-gather.4
  112.9 47.9 all-gather.6
  162.5 80.7 all-gather.8
  244.7 80.5 all-gather.10
  327.5 75.2 reduce-scatter.3
  406.4 78.0 reduce-scatter.5
  489.9 114.2 reduce-scatter.7

commit v21 on v19

--- a/solution.py
+++ b/solution.py
@@ -780,20 +780,23 @@
     )
 
 
-def caption_output(blocks):
-    count, half, wide = blocks.shape
-
-    def kernel(block, out):
-        out[...] = block[0].astype(F32)
-
-    return call(
-        kernel,
-        (count,),
-        [pl.BlockSpec((1, half, wide), lambda k: (k, 0, 0))],
-        pl.BlockSpec((half, wide), lambda k: plane_block(k)),
+def caption_output(own, other, core):
+    count, half, wide = own.shape
+
+    def kernel(r, own_ref, other_ref, out):
+        block = jnp.where(pl.program_id(0) == r[0], own_ref[0], other_ref[0])
+        out[...] = block.astype(F32)
+
+    block = pl.BlockSpec((1, half, wide), lambda i, k, r: (k, 0, 0))
+    return call(
+        kernel,
+        (2, count),
+        [block, block],
+        pl.BlockSpec((half, wide), lambda i, k, r: (i, k)),
         shape((2 * half, 4 * wide), F32),
-        [blocks],
+        [own, other],
         "caption_output",
+        rank=core,
     )
 
 
@@ -1015,11 +1018,11 @@
         caption_part = caption_part[:half_context].astype(BF).reshape(z_size, -1, text_width // 4)
         caption_part = trade(caption_part, "z").astype(F32).sum(axis=0).astype(BF)
         rest_rows = pick_rows([rest_rows], rank)
+        caption_part = spread(caption_part, "z", z_size).reshape(half_context, -1)
         caption_part, rest_rows = lax.optimization_barrier((caption_part, rest_rows))
-        caption_part = spread(caption_part, "z", z_size).reshape(half_context, -1)
         rest_rows = swap_parts(rest_rows)
-        caption_part, rest_rows = lax.optimization_barrier((caption_part, rest_rows))
-        grad_caption = caption_output(spread(caption_part, PLANE, 8))
+        caption_part = spread(caption_part)
+        grad_caption = caption_output(caption_part, swap(caption_part, "c"), core)
         qkv_grad, out_grad, grad_cross, cross_out_grad = finish_all(
             rest_rows, kv_weight_grad, rank
         )

time: 667 us -> 667 us (level)
  waiting for transfers between devices: 220 us -> 210 us
    pallas_call x9 -> x10, Pallas kernels: 37.7 us -> 42.4 us  [call(): pl.pallas_call(kernel, grid_spec=spec, **options)]
    pallas_call x20 -> x19, Pallas kernels: 73.5 us -> 70.6 us  [call(): pl.pallas_call(kernel, grid=grid, in_specs=in_specs, out_specs=out_specs,...]
    ppermute x67 -> x68, starting transfers between devices: 70 us -> 68.4 us  [swap(): return lax.ppermute(values, axis, PAIR)]
    ppermute x67 -> x68, waiting for transfers between devices: 146 us -> 146 us  [swap(): return lax.ppermute(values, axis, PAIR)]
  transfers between devices with their start and end apart: 84 -> 85, of which waited for: 46 -> 46; matrix products, arithmetic and copies ran while one was open for 10% -> 10% of each run, Pallas kernels for 16% -> 16%
where the time goes in v21:
time: 667 us; the launch traced here: 655 us
  waiting for transfers between devices  210 us (31%)
  Pallas kernels  113 us (17%)
  starting transfers between devices  105 us (16%)
  blocking collectives  103 us (15%)
  local copies, waits for them, and re-layouts  66.6 us (10%)
  matrix products  31.8 us (5%)
  between operations  16.5 us (2%)
  other arithmetic  9.61 us (1%)
    ppermute x68, waiting for transfers between devices, swap(): return lax.ppermute(values, axis, PAIR)  146 us
    all_to_all x8, blocking collectives, trade(): return lax.all_to_all(blocks, axes, 0, 0, tiled=True)  103 us
    pallas_call x19, Pallas kernels, call(): pl.pallas_call(kernel, grid=grid, in_specs=in_specs, out_specs=out_specs,...  70.6 us
    ppermute x68, starting transfers between devices, swap(): return lax.ppermute(values, axis, PAIR)  68.4 us
    unnamed x196, local copies, waits for them, and re-layouts  42.7 us
    pallas_call x10, Pallas kernels, call(): pl.pallas_call(kernel, grid_spec=spec, **options)  42.4 us
    all_to_all x5, waiting for transfers between devices, trade(): return lax.all_to_all(blocks, axes, 0, 0, tiled=True)  38.5 us
    dot_general x6, matrix products, dot(): return lax.dot_general(a, b, (dims, ((), ())), preferred_element_type=F32)  31.8 us
  transfers between devices with their start and end apart: 85, of which 46 were waited for; matrix products, arithmetic and copies ran while one was open for 10% of the time, Pallas kernels for 16%

profile of v21, /device:TPU:0, one launch (start us, length us, event | category | flops | bytes accessed | tf_op | source)
XLA Modules:
  0.0 655.4 jit_solution(16261895950661255112)
XLA Ops:
  34.6 8.8 %collective-permute-done.1.refs_2_ = bf16[128,2048]{1,0:T(8,128)(2,1)S(1)} collective-permute-done((bf16[128,2048]{1,0:T(8,128)(2,1)S(1)}, bf16[128,2048]{1,0:T(8,128)(2,1)S(1)}, u32[]{:S(2)}, u32[]{:S(2)}) %collective-permute-start.1) | collective-permute-done | bytes 524320 | tf_op jit(solution)/shard_map/ppermute | solution.py:46
  55.0 10.2 %all_to_all.65 = bf16[4,64,1024]{2,1,0:T(8,128)(2,1)} all-to-all(bf16[4,64,1024]{2,1,0:T(8,128)(2,1)S(1)} %copy.75), channel_id=1, replica_groups=mesh['z'=4,'x'=2,'c'=2,'y'=2] {'x','y'}, dimensions={0} | all-to-all | bytes 1048576 | tf_op jit(solution)/shard_map/all_to_all | solution.py:50
  65.3 15.5 %all_to_all.66 = bf16[4,64,2048]{2,1,0:T(8,128)(2,1)} all-to-all(bf16[4,64,2048]{2,1,0:T(8,128)(2,1)} %bitcast.88), channel_id=1, replica_groups=mesh['z'=4,'x'=2,'c'=2,'y'=2] {'x','y'}, dimensions={0} | all-to-all | bytes 2097152 | tf_op jit(solution)/shard_map/all_to_all | solution.py:50
  83.4 16.9 %all_to_all.67 = bf16[8,64,1024]{2,1,0:T(8,128)(2,1)S(1)} all-to-all(bf16[8,64,1024]{2,1,0:T(8,128)(2,1)S(1)} %get-tuple-element.147), channel_id=1, replica_groups=mesh['z'=4,'x'=2,'c'=2,'y'=2] {'x','c','y'}, dimensions={0} | all-to-all | bytes 2097152 | tf_op jit(solution)/shard_map/all_to_all | solution.py:50
  100.5 11.5 %all_to_all.68 = bf16[4,16,1024]{2,1,0:T(8,128)(2,1)S(1)} all-to-all(bf16[4,16,1024]{2,1,0:T(8,128)(2,1)S(1)} %bitcast.98), channel_id=1, replica_groups=mesh['z'=4,'x'=2,'c'=2,'y'=2] {'z'}, dimensions={0} | all-to-all | bytes 262144 | tf_op jit(solution)/shard_map/all_to_all | solution.py:50
  112.0 8.8 %all_to_all.69 = bf16[4,16,1024]{2,1,0:T(8,128)(2,1)S(1)} all-to-all(bf16[4,16,1024]{2,1,0:T(8,128)(2,1)S(1)} %broadcast_in_dim.10), channel_id=1, replica_groups=mesh['z'=4,'x'=2,'c'=2,'y'=2] {'z'}, dimensions={0} | all-to-all | bytes 262144 | tf_op jit(solution)/shard_map/all_to_all | solution.py:50
  127.2 7.9 %qkv_mm.1 = (bf16[512,2048]{1,0:T(8,128)(2,1)}, bf16[512,1536]{1,0:T(8,128)(2,1)S(1)}) custom-call(bf16[128,2048]{1,0:T(8,128)(2,1)S(1)} %copy-done.67, bf16[128,2048]{1,0:T(8,128)(2,1)S(1)} %copy-done.61, bf16[128,2048]{1,0:T(8,128)(2,1)S(1)} %collective-permute-done.1.refs_2_, bf16[64,2048]{1,0:T(8,128)(2,1)S(1)} %copy-done.73, ...), custom_call_target="tpu_custom_call" | custom-call | flops 3221225472 | bytes 10485760 | tf_op jit(solution)/shard_map/qkv_mm/pallas_call | solution.py:112
  138.1 18.2 %all_to_all.70 = bf16[4,64,2048]{2,1,0:T(8,128)(2,1)} all-to-all(bf16[4,64,2048]{2,1,0:T(8,128)(2,1)S(1)} %bitcast.87), channel_id=1, replica_groups=mesh['z'=4,'x'=2,'c'=2,'y'=2] {'x','y'}, dimensions={0} | all-to-all | bytes 2097152 | tf_op jit(solution)/shard_map/all_to_all | solution.py:50
  170.8 10.0 %collective-permute-done.11.refs_3_ = bf16[128,2048]{1,0:T(8,128)(2,1)S(1)} collective-permute-done((bf16[128,2048]{1,0:T(8,128)(2,1)S(1)}, bf16[128,2048]{1,0:T(8,128)(2,1)S(1)}, u32[]{:S(2)}, u32[]{:S(2)}) %collective-permute-start.11) | collective-permute-done | bytes 524320 | tf_op jit(solution)/shard_map/ppermute | solution.py:46
  185.2 9.3 %collective-permute-done.13.refs_2_ = bf16[128,2048]{1,0:T(8,128)(2,1)S(1)} collective-permute-done((bf16[128,2048]{1,0:T(8,128)(2,1)S(1)}, bf16[128,2048]{1,0:T(8,128)(2,1)S(1)}, u32[]{:S(2)}, u32[]{:S(2)}) %collective-permute-start.13) | collective-permute-done | bytes 524320 | tf_op jit(solution)/shard_map/ppermute | solution.py:46
  271.4 12.0 %feed_up.1 = (bf16[512,2048]{1,0:T(8,128)(2,1)}, bf16[512,2048]{1,0:T(8,128)(2,1)}, f32[512,2048]{1,0:T(8,128)}) custom-call(bf16[128,2048]{1,0:T(8,128)(2,1)S(1)} %copy-done.69, bf16[128,2048]{1,0:T(8,128)(2,1)S(1)} %copy-done.65, bf16[128,2048]{1,0:T(8,128)(2,1)S(1)} %copy-done.63, bf16[64,2048]{1,0:T(8,128)(2,1)S(1)} %copy-done.77, ...), custom_call_target="tpu_custom_call" | custom-call | flops 4294967296 | bytes 12582912 | tf_op jit(solution)/shard_map/feed_up/pallas_call | solution.py:112
  303.0 8.7 %down_grads.1 = bf16[1024,2048]{1,0:T(8,128)(2,1)} custom-call(s32[1]{0:T(128)} %bitcast.24.r, bf16[512,2048]{1,0:T(8,128)(2,1)S(1)} %constant_dynamic-update-slice_fusion.refs_0_.dy, bf16[512,2048]{1,0:T(8,128)(2,1)S(1)} %collective-permute-done.28.refs_1_, bf16[512,2048]{1,0:T(8,128)(2,1)} %get-tuple-element.186.refs_2_, bf16[512,2048]{1,0:T(8,128)(2,1)} %copy-done.95), custom_call_target="tpu_custom_call" | custom-call | flops 4294967296 | bytes 16777216 | tf_op jit(solution)/shard_map/down_grads/pallas_call | solution.py:123
  313.3 12.1 %all-gather.11.cloned.1.call-done.down = bf16[2048,2048]{1,0:T(8,128)(2,1)} async-done(((bf16[256,2048]{1,0:T(8,128)(2,1)}), bf16[2048,2048]{1,0:T(8,128)(2,1)}) %all-gather.11.cloned.1.call-update) | async-done | bytes 8388624 | tf_op jit(solution)/shard_map/all_gather | solution.py:95
  326.9 9.9 %feed_down.1.refs_2_ = bf16[512,2048]{1,0:T(8,128)(2,1)S(1)} custom-call(bf16[512,2048]{1,0:T(8,128)(2,1)S(1)} %copy-done.14, f32[512,2048]{1,0:T(8,128)} %get-tuple-element.179.slope_ref, bf16[2048,2048]{1,0:T(8,128)(2,1)} %all-gather.11.cloned.1.call-done.down), custom_call_target="tpu_custom_call" | custom-call | flops 4294967296 | bytes 25165824 | tf_op jit(solution)/shard_map/feed_down/pallas_call | solution.py:112
  336.9 8.9 %convolution_convert_fusion.2 = bf16[512,2048]{1,0:T(8,128)(2,1)S(1)} fusion(bf16[512,2048]{1,0:T(8,128)(2,1)S(1)} %feed_down.1.refs_2_, bf16[2048,2048]{1,0:T(8,128)(2,1)} %all-gather.9.cloned.1.call-done.refs_5_), kind=kOutput, calls=%fused_computation.5 | convolution fusion | flops 4296015872 | bytes 12582912 | tf_op jit(solution)/shard_map/dot_general | solution.py:26
  358.2 10.9 %collective-permute-done.38.refs_2_ = bf16[128,2048]{1,0:T(8,128)(2,1)S(1)} collective-permute-done((bf16[128,2048]{1,0:T(8,128)(2,1)S(1)}, bf16[128,2048]{1,0:T(8,128)(2,1)S(1)}, u32[]{:S(2)}, u32[]{:S(2)}) %collective-permute-start.38) | collective-permute-done | bytes 524320 | tf_op jit(solution)/shard_map/ppermute | solution.py:46
  375.5 9.2 %convolution_convert_fusion.1 = bf16[512,2048]{1,0:T(8,128)(2,1)} fusion(bf16[512,2048]{1,0:T(8,128)(2,1)S(1)} %copy-done.93, bf16[2048,2048]{1,0:T(8,128)(2,1)} %all-gather.11.cloned.1.call-done.down), kind=kOutput, calls=%fused_computation.4 | convolution fusion | flops 4296015872 | bytes 12582912 | tf_op jit(solution)/shard_map/dot_general | solution.py:26
  390.3 8.8 %up_grads.1 = bf16[1024,2048]{1,0:T(8,128)(2,1)} custom-call(s32[1]{0:T(128)} %bitcast.24.r, bf16[512,2048]{1,0:T(8,128)(2,1)} %get-tuple-element.184.refs_0_, bf16[512,2048]{1,0:T(8,128)(2,1)} %collective-permute-done.34.refs_1_, bf16[512,2048]{1,0:T(8,128)(2,1)} %copy-done.24, bf16[512,2048]{1,0:T(8,128)(2,1)} %copy-done.94), custom_call_target="tpu_custom_call" | custom-call | flops 4294967296 | bytes 16777216 | tf_op jit(solution)/shard_map/up_grads/pallas_call | solution.py:123
  433.8 11.9 %collective-permute-done.49.refs_2_ = bf16[128,2048]{1,0:T(8,128)(2,1)S(1)} collective-permute-done((bf16[128,2048]{1,0:T(8,128)(2,1)S(1)}, bf16[128,2048]{1,0:T(8,128)(2,1)S(1)}, u32[]{:S(2)}, u32[]{:S(2)}) %collective-permute-start.49) | collective-permute-done | bytes 524320 | tf_op jit(solution)/shard_map/ppermute | solution.py:46
  472.0 11.7 %attention_grads.1 = bf16[1024,3072]{1,0:T(8,128)(2,1)} custom-call(s32[1]{0:T(128)} %bitcast.24.r, bf16[512,2048]{1,0:T(8,128)(2,1)} %get-tuple-element.212.refs_0_, bf16[512,2048]{1,0:T(8,128)(2,1)} %collective-permute-done.30.refs_1_, bf16[512,2048]{1,0:T(8,128)(2,1)} %copy-done.25, bf16[512,2048]{1,0:T(8,128)(2,1)} %collective-permute-done.56.refs_3_, ...), custom_call_target="tpu_custom_call" | custom-call | flops 6442450944 | bytes 25165824 | tf_op jit(solution)/shard_map/attention_grads/pallas_call | solution.py:123
  523.1 9.9 %all-to-all-done.7 = bf16[4,16,1024]{2,1,0:T(8,128)(2,1)S(1)} async-done(((bf16[4,16,1024]{2,1,0:T(8,128)(2,1)}), bf16[4,16,1024]{2,1,0:T(8,128)(2,1)S(1)}, u32[]{:S(2)}, u32[]{:S(2)}) %all-to-all-start.7) | async-done | bytes 131104 | tf_op jit(solution)/shard_map/all_to_all | solution.py:50
  568.1 13.2 %all-to-all-done.9 = bf16[8,80,1024]{2,1,0:T(8,128)(2,1)} async-done(((bf16[8,80,1024]{2,1,0:T(8,128)(2,1)}), bf16[8,80,1024]{2,1,0:T(8,128)(2,1)}, u32[]{:S(2)}, u32[]{:S(2)}) %all-to-all-start.9) | async-done | bytes 1310752 | tf_op jit(solution)/shard_map/all_to_all | solution.py:50
  583.7 11.1 %all_to_all.71 = bf16[4,16,1024]{2,1,0:T(8,128)(2,1)S(1)} all-to-all(bf16[4,16,1024]{2,1,0:T(8,128)(2,1)S(1)} %bitcast.99), channel_id=1, replica_groups=mesh['z'=4,'x'=2,'c'=2,'y'=2] {'z'}, dimensions={0} | all-to-all | bytes 262144 | tf_op jit(solution)/shard_map/all_to_all | solution.py:50
  609.3 11.0 %all_to_all.72.own_ref = bf16[4,64,1024]{2,1,0:T(8,128)(2,1)S(1)} all-to-all(bf16[4,64,1024]{2,1,0:T(8,128)(2,1)S(1)} %broadcast_in_dim.14), channel_id=1, replica_groups=mesh['z'=4,'x'=2,'c'=2,'y'=2] {'x','y'}, dimensions={0} | all-to-all | bytes 1048576 | tf_op jit(solution)/shard_map/all_to_all | solution.py:50
  (479 shorter events, 372.7 us)
Async XLA Ops:
  7.2 116.0 %all-gather.5.cloned.1.call-start = ((), (), s32[]{:S(2)}) async-start(), calls=%async_computation.16 | async-start | bytes 9437184 | tf_op jit(solution)/shard_map/all_gather | solution.py:95
  27.5 170.6 %all-gather.7.cloned.1.call-start = ((), (), s32[]{:S(2)}) async-start(), calls=%async_computation.17 | async-start | bytes 4718592 | tf_op jit(solution)/shard_map/all_gather | solution.py:95
  65.2 201.2 %all-gather.9.cloned.1.call-start = ((), (), s32[]{:S(2)}) async-start(), calls=%async_computation.18 | async-start | bytes 9437184 | tf_op jit(solution)/shard_map/all_gather | solution.py:95
  80.8 244.6 %all-gather.11.cloned.1.call-start = ((), (), s32[]{:S(2)}) async-start(), calls=%async_computation.19 | async-start | bytes 9437184 | tf_op jit(solution)/shard_map/all_gather | solution.py:95
  156.4 250.3 %reduce-scatter.4.cloned.1.call-start = ((), (), s32[]{:S(2)}) async-start(), calls=%async_computation.20 | async-start | bytes 5242880 | tf_op jit(solution)/shard_map/reduce_scatter | solution.py:99
  264.0 22.7 %collective-permute-start.24 = (bf16[128,2048]{1,0:T(8,128)(2,1)}, bf16[128,2048]{1,0:T(8,128)(2,1)}, u32[]{:S(2)}, u32[]{:S(2)}) collective-permute-start(bf16[128,2048]{1,0:T(8,128)(2,1)} %get-tuple-element.174.refs_3_), channel_id=1, source_target_pairs={{0,1},{1,0},{2,3},{3,2},{4,5},{5,4},{6,7},{7,6},{8,9},{9,8},{10,11... | collective-permute-start | bytes 1572872 | tf_op jit(solution)/shard_map/ppermute | solution.py:46
  264.5 20.1 %collective-permute-start.25 = (bf16[128,2048]{1,0:T(8,128)(2,1)}, bf16[128,2048]{1,0:T(8,128)(2,1)}, u32[]{:S(2)}, u32[]{:S(2)}) collective-permute-start(bf16[128,2048]{1,0:T(8,128)(2,1)} %get-tuple-element.174.refs_3_), channel_id=1, source_target_pairs={{0,4},{4,0},{1,5},{5,1},{2,6},{6,2},{3,7},{7,3},{8,12},{12,8},{9,1... | collective-permute-start | bytes 1572872 | tf_op jit(solution)/shard_map/ppermute | solution.py:46
  296.3 16.7 %collective-permute-start.30 = (bf16[512,2048]{1,0:T(8,128)(2,1)}, bf16[512,2048]{1,0:T(8,128)(2,1)}, u32[]{:S(2)}, u32[]{:S(2)}) collective-permute-start(bf16[512,2048]{1,0:T(8,128)(2,1)} %get-tuple-element.212.refs_0_), channel_id=1, source_target_pairs={{0,2},{2,0},{1,3},{3,1},{4,6},{6,4},{5,7},{7,5},{8,10},{10,8},{9,1... | collective-permute-start | bytes 6291464 | tf_op jit(solution)/shard_map/ppermute | solution.py:46
  313.1 170.7 %reduce-scatter.6.cloned.1.call-start = ((), (), s32[]{:S(2)}) async-start(), calls=%async_computation.21 | async-start | bytes 5242880 | tf_op jit(solution)/shard_map/reduce_scatter | solution.py:99
  349.0 39.9 %collective-permute-start.43 = (bf16[512,2048]{1,0:T(8,128)(2,1)S(1)}, bf16[512,2048]{1,0:T(8,128)(2,1)S(1)}, u32[]{:S(2)}, u32[]{:S(2)}) collective-permute-start(bf16[512,2048]{1,0:T(8,128)(2,1)S(1)} %feed_down.1.refs_2_), channel_id=1, source_target_pairs={{0,2},{2,0},{1,3},{3,1},{4,6},{6,4},{5,7},{7,5},{8,10},{10,8},{9,1... | collective-permute-start | bytes 6291464 | tf_op jit(solution)/shard_map/ppermute | solution.py:46
  407.5 196.9 %reduce-scatter.8.cloned.1.call-start = ((), (), s32[]{:S(2)}) async-start(), calls=%async_computation.22 | async-start | bytes 7864320 | tf_op jit(solution)/shard_map/reduce_scatter | solution.py:99
  466.0 17.6 %collective-permute-start.54 = (bf16[128,2048]{1,0:T(8,128)(2,1)}, bf16[128,2048]{1,0:T(8,128)(2,1)S(1)}, u32[]{:S(2)}, u32[]{:S(2)}) collective-permute-start(bf16[128,2048]{1,0:T(8,128)(2,1)} %get-tuple-element.206), channel_id=1, source_target_pairs={{0,4},{4,0},{1,5},{5,1},{2,6},{6,2},{3,7},{7,3},{8,12},{12,8},{9,1... | collective-permute-start | bytes 1572872 | tf_op jit(solution)/shard_map/ppermute | solution.py:46
  496.0 20.4 %all-to-all-start.6 = ((bf16[8,16,1024]{2,1,0:T(8,128)(2,1)}), bf16[8,16,1024]{2,1,0:T(8,128)(2,1)S(1)}, u32[]{:S(2)}, u32[]{:S(2)}) async-start(bf16[8,16,1024]{2,1,0:T(8,128)(2,1)} %bitcast.29), calls=%async_computation.7 | async-start | bytes 524288 | tf_op jit(solution)/shard_map/all_to_all | solution.py:50
  505.1 27.9 %collective-permute-start.60 = (bf16[64,4096]{1,0:T(8,128)(2,1)}, bf16[64,4096]{1,0:T(8,128)(2,1)S(1)}, u32[]{:S(2)}, u32[]{:S(2)}) collective-permute-start(bf16[64,4096]{1,0:T(8,128)(2,1)} %get-tuple-element.228), channel_id=1, source_target_pairs={{0,1},{1,0},{2,3},{3,2},{4,5},{5,4},{6,7},{7,6},{8,9},{9,8},{10,11... | collective-permute-start | bytes 1572872 | tf_op jit(solution)/shard_map/ppermute | solution.py:46
  505.5 28.2 %collective-permute-start.61 = (bf16[64,4096]{1,0:T(8,128)(2,1)}, bf16[64,4096]{1,0:T(8,128)(2,1)S(1)}, u32[]{:S(2)}, u32[]{:S(2)}) collective-permute-start(bf16[64,4096]{1,0:T(8,128)(2,1)} %get-tuple-element.229), channel_id=1, source_target_pairs={{0,4},{4,0},{1,5},{5,1},{2,6},{6,2},{3,7},{7,3},{8,12},{12,8},{9,1... | collective-permute-start | bytes 1572872 | tf_op jit(solution)/shard_map/ppermute | solution.py:46
  507.0 26.8 %collective-permute-start.62 = (bf16[64,4096]{1,0:T(8,128)(2,1)}, bf16[64,4096]{1,0:T(8,128)(2,1)S(1)}, u32[]{:S(2)}, u32[]{:S(2)}) collective-permute-start(bf16[64,4096]{1,0:T(8,128)(2,1)} %get-tuple-element.230), channel_id=1, source_target_pairs={{0,5},{1,4},{4,1},{5,0},{2,7},{3,6},{6,3},{7,2},{8,13},{9,12},{12,... | collective-permute-start | bytes 1572872 | tf_op jit(solution)/shard_map/ppermute | solution.py:90
  509.4 31.2 %collective-permute-start.66 = (bf16[128,2048]{1,0:T(8,128)(2,1)}, bf16[128,2048]{1,0:T(8,128)(2,1)}, u32[]{:S(2)}, u32[]{:S(2)}) collective-permute-start(bf16[128,2048]{1,0:T(8,128)(2,1)} %pad_maximum_fusion.12), channel_id=1, source_target_pairs={{0,1},{1,0},{2,3},{3,2},{4,5},{5,4},{6,7},{7,6},{8,9},{9,8},{10,11... | collective-permute-start | bytes 1572872 | tf_op jit(solution)/shard_map/ppermute | solution.py:46
  522.3 18.4 %collective-permute-start.64 = (bf16[128,2048]{1,0:T(8,128)(2,1)}, bf16[128,2048]{1,0:T(8,128)(2,1)}, u32[]{:S(2)}, u32[]{:S(2)}) collective-permute-start(bf16[128,2048]{1,0:T(8,128)(2,1)} %pad_maximum_fusion.11), channel_id=1, source_target_pairs={{0,4},{4,0},{1,5},{5,1},{2,6},{6,2},{3,7},{7,3},{8,12},{12,8},{9,1... | collective-permute-start | bytes 1572872 | tf_op jit(solution)/shard_map/ppermute | solution.py:46
  534.9 19.1 %all-to-all-start.8 = ((bf16[8,64,1024]{2,1,0:T(8,128)(2,1)}), bf16[8,64,1024]{2,1,0:T(8,128)(2,1)}, u32[]{:S(2)}, u32[]{:S(2)}) async-start(bf16[8,64,1024]{2,1,0:T(8,128)(2,1)} %broadcast_in_dim.12), calls=%async_computation.10 | async-start | bytes 2097152 | tf_op jit(solution)/shard_map/all_to_all | solution.py:50
  559.5 21.8 %all-to-all-start.9 = ((bf16[8,80,1024]{2,1,0:T(8,128)(2,1)}), bf16[8,80,1024]{2,1,0:T(8,128)(2,1)}, u32[]{:S(2)}, u32[]{:S(2)}) async-start(bf16[8,80,1024]{2,1,0:T(8,128)(2,1)} %copy-done.27), calls=%async_computation.11 | async-start | bytes 2621440 | tf_op jit(solution)/shard_map/all_to_all | solution.py:50
  620.3 25.0 %collective-permute-start.67 = (bf16[4,64,1024]{2,1,0:T(8,128)(2,1)S(1)}, bf16[4,64,1024]{2,1,0:T(8,128)(2,1)S(1)}, u32[]{:S(2)}, u32[]{:S(2)}) collective-permute-start(bf16[4,64,1024]{2,1,0:T(8,128)(2,1)S(1)} %all_to_all.72.own_ref), channel_id=1, source_target_pairs={{0,2},{2,0},{1,3},{3,1},{4,6},{6,4},{5,7},{7,5},{8,10},{10,8},{9,1... | collective-permute-start | bytes 1572872 | tf_op jit(solution)/shard_map/ppermute | solution.py:46
  620.3 19.4 %collective-permute-start.70 = (bf16[64,3072]{1,0:T(8,128)(2,1)}, bf16[64,3072]{1,0:T(8,128)(2,1)S(1)}, u32[]{:S(2)}, u32[]{:S(2)}) collective-permute-start(bf16[64,3072]{1,0:T(8,128)(2,1)} %get-tuple-element.259), channel_id=1, source_target_pairs={{0,1},{1,0},{2,3},{3,2},{4,5},{5,4},{6,7},{7,6},{8,9},{9,8},{10,11... | collective-permute-start | bytes 1179656 | tf_op jit(solution)/shard_map/ppermute | solution.py:46
  621.3 18.5 %collective-permute-start.71 = (bf16[64,3072]{1,0:T(8,128)(2,1)}, bf16[64,3072]{1,0:T(8,128)(2,1)S(1)}, u32[]{:S(2)}, u32[]{:S(2)}) collective-permute-start(bf16[64,3072]{1,0:T(8,128)(2,1)} %copy-done.71), channel_id=1, source_target_pairs={{0,4},{4,0},{1,5},{5,1},{2,6},{6,2},{3,7},{7,3},{8,12},{12,8},{9,1... | collective-permute-start | bytes 1179656 | tf_op jit(solution)/shard_map/ppermute | solution.py:46
  621.8 20.0 %collective-permute-start.72 = (bf16[64,3072]{1,0:T(8,128)(2,1)}, bf16[64,3072]{1,0:T(8,128)(2,1)}, u32[]{:S(2)}, u32[]{:S(2)}) collective-permute-start(bf16[64,3072]{1,0:T(8,128)(2,1)} %copy-done.70), channel_id=1, source_target_pairs={{0,5},{1,4},{4,1},{5,0},{2,7},{3,6},{6,3},{7,2},{8,13},{9,12},{12,... | collective-permute-start | bytes 1179656 | tf_op jit(solution)/shard_map/ppermute | solution.py:90
  (157 other events, 1660.6 us)
Sparse Core Ops, SparseCore 0:
  27.6 83.6 all-gather.4
  112.9 47.9 all-gather.6
  162.5 80.7 all-gather.8
  244.7 80.5 all-gather.10
  327.5 75.2 reduce-scatter.3
  406.8 75.5 reduce-scatter.5
  484.7 119.6 reduce-scatter.7

commit v22 on v21

--- a/solution.py
+++ b/solution.py
@@ -737,36 +737,34 @@
     )
 
 
-def text_back(blocks, own_text, w_cross, caption, w_text, extra):
+def text_back(own_blocks, other_blocks, own_text, w_cross, caption, w_text, core):
     context, rows = own_text.shape
     half, width = context // 2, w_cross.shape[2] // 4
     wide = caption.shape[1] // 4
-    tail = extra.shape[0]
-
-    def kernel(block, own, cross, cap, weight, more, kv_grad, text_grad, out, grads):
-        for k in range(8):
-            core, group = plane_block(k)
+
+    def kernel(r, mine, other, own, cross, cap, weight, kv_grad, text_grad, near, far, grads, part):
+        spans = [pl.ds(pl.multiple_of((r[0] ^ c) * half, half), half) for c in range(2)]
+        for k in range(4):
             for j in range(2):
-                at = (4 * j + group) * width
-                grads[core * half : (core + 1) * half, at : at + width] = block[
-                    k, :, j * width : (j + 1) * width
-                ]
+                at = (4 * j + k) * width
+                for c, ref in enumerate((mine, other)):
+                    grads[spans[c], at : at + width] = ref[k, :, j * width : (j + 1) * width]
         kv_grad[...] = t_mm(own[...], grads[...])
         grad_text = sum(
             mm_t(grads[:, 4 * j * width : 4 * (j + 1) * width], cross[1 + j]) for j in range(2)
         ).astype(BF)
         text_grad[...] = t_mm(grad_text, cap[...])
-        part = mm(grad_text, weight[...]).astype(BF)
-        for k in range(8):
-            core, group = plane_block(k)
-            out[k, :half, :] = part[core * half : (core + 1) * half, group * wide : (group + 1) * wide]
-            out[k, half:, :] = more[...]
-
-    operands = [blocks, own_text, w_cross, caption, w_text, extra]
+        part[...] = mm(grad_text, weight[...]).astype(BF)
+        for k in range(4):
+            for c, ref in enumerate((near, far)):
+                ref[k] = part[spans[c], k * wide : (k + 1) * wide]
+
+    operands = [own_blocks, other_blocks, own_text, w_cross, caption, w_text]
     outs = [
         shape((rows, 8 * width), F32),
         shape((rows, 4 * wide), F32),
-        shape((8, half + tail, wide)),
+        shape((4, half, wide)),
+        shape((4, half, wide)),
     ]
     return call(
         kernel,
@@ -776,7 +774,8 @@
         outs,
         operands,
         "text_back",
-        scratch=[pltpu.VMEM((context, 8 * width), BF)],
+        rank=core,
+        scratch=[pltpu.VMEM((context, 8 * width), BF), pltpu.VMEM((context, 4 * wide), BF)],
     )
 
 
@@ -805,24 +804,15 @@
     return weight.reshape(rows, count, -1).transpose(1, 0, 2)
 
 
-def halves_of(values, width):
-    high = values.astype(BF)
-    low = (values - high.astype(F32)).astype(BF)
-    return jnp.concatenate([high.reshape(-1, width), low.reshape(-1, width)], axis=0)
-
-
-def whole_of(halves, width):
-    rows = halves.shape[0] // 2
-    return (halves[:rows] + halves[rows:]).reshape(-1, width)
-
-
 def make_local(z_size):
     def sum_z(values):
         parts = values.reshape(z_size, -1, values.shape[-1])
         mine = trade(parts, "z").astype(F32).sum(axis=0).astype(BF)
         return spread(mine, "z", z_size).reshape(values.shape)
 
-    def add_z(values):
+    def sum_all(values):
+        for axis in ("c", "x", "y"):
+            values = values + swap(values, axis)
         step = 1
         while step < z_size:
             values = values + lax.ppermute(
@@ -983,46 +973,37 @@
         )
         rest_part, up_rows = lax.optimization_barrier((rest_part, up_rows))
         rest_rows = scatter_grad(rest_part, grad_axes)
-        parts = mm_scatter(grad_projected, first[:, : 3 * group])
-        grad_hidden, gain_grad_a, mask_grad = last_back(
-            parts,
-            grad_after_attn,
-            start_x,
-            gain_a,
-            masked,
-            unit,
-            order,
-        )
-        sums = jnp.concatenate([gain_grad_a, gain_grad_b, gain_grad_c, mask_grad], axis=0)
-
-
         kv_part = kv_grad.astype(BF).reshape(2, z_size, -1, 2 * group)
         kv_part = kv_part.transpose(1, 0, 2, 3).reshape(2 * z_size, -1, 2 * group)
         kv_part = trade(kv_part, DATA).astype(F32).sum(axis=0).astype(BF)
-        kv_sum = spread(kv_part, "z", z_size).reshape(-1, 2 * group)
+        kv_part, grad_projected = lax.optimization_barrier((kv_part, grad_projected))
+        kv_part = spread(spread(kv_part, "z", z_size).reshape(-1, 2 * group))
         wide_rows = swap_parts(pick_rows([down_rows, up_rows], rank))
-        kv_sum, wide_rows = lax.optimization_barrier((kv_sum, wide_rows))
-        kv_grads = spread(kv_sum, PLANE, 8)
-        kv_weight_grad, grad_text_w, caption_part = text_back(
-            kv_grads, own_text, w_cross, caption, w_text, halves_of(sums, text_width // 4)
-        )
-        half_context = caption.shape[0] // 2
-        caption_part = trade(caption_part, PLANE)
+        kv_part, wide_rows = lax.optimization_barrier((kv_part, wide_rows))
+        kv_weight_grad, grad_text_w, caption_part, caption_far = text_back(
+            kv_part, swap(kv_part, "c"), own_text, w_cross, caption, w_text, core
+        )
+        caption_part = caption_part.astype(F32) + swap(caption_far, "c").astype(F32)
+        caption_part = trade(caption_part.astype(BF))
+        parts = mm_scatter(grad_projected, first[:, : 3 * group])
+        grad_hidden, gain_grad_a, mask_grad = last_back(
+            parts, grad_after_attn, start_x, gain_a, masked, unit, order
+        )
+        sums = jnp.concatenate([gain_grad_a, gain_grad_b, gain_grad_c, mask_grad], axis=0)
         output = layer_output(after_cross, result, unit, order)
         down_grad, up_grad = finish_wide(wide_rows, rank)
-        caption_part, output, down_grad, up_grad = lax.optimization_barrier(
-            (caption_part, output, down_grad, up_grad)
-        )
-        caption_part = caption_part.astype(F32).sum(axis=0)
-        sums = layer_order(add_z(whole_of(caption_part[half_context:], width)))
-        caption_part = caption_part[:half_context].astype(BF).reshape(z_size, -1, text_width // 4)
-        caption_part = trade(caption_part, "z").astype(F32).sum(axis=0).astype(BF)
-        rest_rows = pick_rows([rest_rows], rank)
-        caption_part = spread(caption_part, "z", z_size).reshape(half_context, -1)
+        caption_part, sums, output, down_grad, up_grad = lax.optimization_barrier(
+            (caption_part, sums, output, down_grad, up_grad)
+        )
+        caption_part = caption_part.astype(F32).sum(axis=0).astype(BF)
+        caption_part = trade(caption_part.reshape(z_size, -1, text_width // 4), "z")
+        caption_part = caption_part.astype(F32).sum(axis=0).astype(BF)
+        half_context = caption.shape[0] // 2
+        caption_part = spread(spread(caption_part, "z", z_size).reshape(half_context, -1))
         caption_part, rest_rows = lax.optimization_barrier((caption_part, rest_rows))
-        rest_rows = swap_parts(rest_rows)
-        caption_part = spread(caption_part)
+        rest_rows = swap_parts(pick_rows([rest_rows], rank))
         grad_caption = caption_output(caption_part, swap(caption_part, "c"), core)
+        sums = layer_order(sum_all(sums))
         qkv_grad, out_grad, grad_cross, cross_out_grad = finish_all(
             rest_rows, kv_weight_grad, rank
         )

time: 667 us -> 685 us (1.027)
  blocking collectives: 103 us -> 133 us
  starting transfers between devices: 105 us -> 91.6 us
  waiting for transfers between devices: 210 us -> 217 us
    ppermute x68 -> x73, waiting for transfers between devices: 146 us -> 185 us  [swap(): return lax.ppermute(values, axis, PAIR)]
    all_to_all x5 -> x3, waiting for transfers between devices: 38.5 us -> 5.21 us  [trade(): return lax.all_to_all(blocks, axes, 0, 0, tiled=True)]
    all_to_all x8 -> x10, blocking collectives: 103 us -> 133 us  [trade(): return lax.all_to_all(blocks, axes, 0, 0, tiled=True)]
    all_to_all x5 -> x3, starting transfers between devices: 22.3 us -> 11.2 us  [trade(): return lax.all_to_all(blocks, axes, 0, 0, tiled=True)]
    ppermute x68 -> x73, starting transfers between devices: 68.4 us -> 74.6 us  [swap(): return lax.ppermute(values, axis, PAIR)]
    pallas_call x10 -> x11, Pallas kernels: 42.4 us -> 46.6 us  [call(): pl.pallas_call(kernel, grid_spec=spec, **options)]
    pallas_call x19 -> x18, Pallas kernels: 70.6 us -> 67.1 us  [call(): pl.pallas_call(kernel, grid=grid, in_specs=in_specs, out_specs=out_specs,...]
    unnamed x196 -> x178, local copies, waits for them, and re-layouts: 42.7 us -> 42.5 us
  transfers between devices with their start and end apart: 85 -> 88, of which waited for: 46 -> 48; matrix products, arithmetic and copies ran while one was open for 10% -> 10% of each run, Pallas kernels for 16% -> 16%
where the time goes in v22:
time: 685 us; the launch traced here: 677 us
  waiting for transfers between devices  217 us (32%)
  blocking collectives  133 us (19%)
  Pallas kernels  114 us (17%)
  starting transfers between devices  91.6 us (13%)
  local copies, waits for them, and re-layouts  64.7 us (9%)
  matrix products  32.7 us (5%)
  between operations  16.4 us (2%)
  other arithmetic  7.62 us (1%)
    ppermute x73, waiting for transfers between devices, swap(): return lax.ppermute(values, axis, PAIR)  185 us
    all_to_all x10, blocking collectives, trade(): return lax.all_to_all(blocks, axes, 0, 0, tiled=True)  133 us
    ppermute x73, starting transfers between devices, swap(): return lax.ppermute(values, axis, PAIR)  74.6 us
    pallas_call x18, Pallas kernels, call(): pl.pallas_call(kernel, grid=grid, in_specs=in_specs, out_specs=out_specs,...  67.1 us
    pallas_call x11, Pallas kernels, call(): pl.pallas_call(kernel, grid_spec=spec, **options)  46.6 us
    unnamed x178, local copies, waits for them, and re-layouts  42.5 us
    dot_general x6, matrix products, dot(): return lax.dot_general(a, b, (dims, ((), ())), preferred_element_type=F32)  32.7 us
  transfers between devices with their start and end apart: 88, of which 48 were waited for; matrix products, arithmetic and copies ran while one was open for 10% of the time, Pallas kernels for 16%

profile of v22, /device:TPU:0, one launch (start us, length us, event | category | flops | bytes accessed | tf_op | source)
XLA Modules:
  0.0 677.1 jit_solution(14894352643257135267)
XLA Ops:
  34.6 8.8 %collective-permute-done.1.refs_2_ = bf16[128,2048]{1,0:T(8,128)(2,1)S(1)} collective-permute-done((bf16[128,2048]{1,0:T(8,128)(2,1)S(1)}, bf16[128,2048]{1,0:T(8,128)(2,1)S(1)}, u32[]{:S(2)}, u32[]{:S(2)}) %collective-permute-start.1) | collective-permute-done | bytes 524320 | tf_op jit(solution)/shard_map/ppermute | solution.py:46
  54.9 10.2 %all_to_all.65 = bf16[4,64,1024]{2,1,0:T(8,128)(2,1)} all-to-all(bf16[4,64,1024]{2,1,0:T(8,128)(2,1)S(1)} %copy.65), channel_id=1, replica_groups=mesh['z'=4,'x'=2,'c'=2,'y'=2] {'x','y'}, dimensions={0} | all-to-all | bytes 1048576 | tf_op jit(solution)/shard_map/all_to_all | solution.py:50
  65.2 15.5 %all_to_all.66 = bf16[4,64,2048]{2,1,0:T(8,128)(2,1)} all-to-all(bf16[4,64,2048]{2,1,0:T(8,128)(2,1)} %bitcast.90), channel_id=1, replica_groups=mesh['z'=4,'x'=2,'c'=2,'y'=2] {'x','y'}, dimensions={0} | all-to-all | bytes 2097152 | tf_op jit(solution)/shard_map/all_to_all | solution.py:50
  83.4 16.9 %all_to_all.67 = bf16[8,64,1024]{2,1,0:T(8,128)(2,1)S(1)} all-to-all(bf16[8,64,1024]{2,1,0:T(8,128)(2,1)S(1)} %get-tuple-element.148), channel_id=1, replica_groups=mesh['z'=4,'x'=2,'c'=2,'y'=2] {'x','c','y'}, dimensions={0} | all-to-all | bytes 2097152 | tf_op jit(solution)/shard_map/all_to_all | solution.py:50
  100.4 11.8 %all_to_all.68 = bf16[4,16,1024]{2,1,0:T(8,128)(2,1)S(1)} all-to-all(bf16[4,16,1024]{2,1,0:T(8,128)(2,1)S(1)} %bitcast.100), channel_id=1, replica_groups=mesh['z'=4,'x'=2,'c'=2,'y'=2] {'z'}, dimensions={0} | all-to-all | bytes 262144 | tf_op jit(solution)/shard_map/all_to_all | solution.py:50
  138.2 18.2 %all_to_all.70 = bf16[4,64,2048]{2,1,0:T(8,128)(2,1)} all-to-all(bf16[4,64,2048]{2,1,0:T(8,128)(2,1)S(1)} %bitcast.89), channel_id=1, replica_groups=mesh['z'=4,'x'=2,'c'=2,'y'=2] {'x','y'}, dimensions={0} | all-to-all | bytes 2097152 | tf_op jit(solution)/shard_map/all_to_all | solution.py:50
  170.9 9.9 %collective-permute-done.11.refs_3_ = bf16[128,2048]{1,0:T(8,128)(2,1)S(1)} collective-permute-done((bf16[128,2048]{1,0:T(8,128)(2,1)S(1)}, bf16[128,2048]{1,0:T(8,128)(2,1)S(1)}, u32[]{:S(2)}, u32[]{:S(2)}) %collective-permute-start.11) | collective-permute-done | bytes 524320 | tf_op jit(solution)/shard_map/ppermute | solution.py:46
  185.3 9.3 %collective-permute-done.13.refs_2_ = bf16[128,2048]{1,0:T(8,128)(2,1)S(1)} collective-permute-done((bf16[128,2048]{1,0:T(8,128)(2,1)S(1)}, bf16[128,2048]{1,0:T(8,128)(2,1)S(1)}, u32[]{:S(2)}, u32[]{:S(2)}) %collective-permute-start.13) | collective-permute-done | bytes 524320 | tf_op jit(solution)/shard_map/ppermute | solution.py:46
  271.5 11.9 %feed_up.1 = (bf16[512,2048]{1,0:T(8,128)(2,1)}, bf16[512,2048]{1,0:T(8,128)(2,1)}, f32[512,2048]{1,0:T(8,128)}) custom-call(bf16[128,2048]{1,0:T(8,128)(2,1)S(1)} %copy-done.62, bf16[128,2048]{1,0:T(8,128)(2,1)S(1)} %copy-done.58, bf16[128,2048]{1,0:T(8,128)(2,1)S(1)} %copy-done.56, bf16[64,2048]{1,0:T(8,128)(2,1)S(1)} %copy-done.68, ...), custom_call_target="tpu_custom_call" | custom-call | flops 4294967296 | bytes 12582912 | tf_op jit(solution)/shard_map/feed_up/pallas_call | solution.py:112
  303.0 8.7 %down_grads.1 = bf16[1024,2048]{1,0:T(8,128)(2,1)} custom-call(s32[1]{0:T(128)} %bitcast.r, bf16[512,2048]{1,0:T(8,128)(2,1)S(1)} %constant_dynamic-update-slice_fusion.refs_0_.dy, bf16[512,2048]{1,0:T(8,128)(2,1)S(1)} %collective-permute-done.28.refs_1_, bf16[512,2048]{1,0:T(8,128)(2,1)} %get-tuple-element.187.refs_2_, bf16[512,2048]{1,0:T(8,128)(2,1)} %copy-done.86), custom_call_target="tpu_custom_call" | custom-call | flops 4294967296 | bytes 16777216 | tf_op jit(solution)/shard_map/down_grads/pallas_call | solution.py:123
  313.3 12.1 %all-gather.11.cloned.1.call-done.down = bf16[2048,2048]{1,0:T(8,128)(2,1)} async-done(((bf16[256,2048]{1,0:T(8,128)(2,1)}), bf16[2048,2048]{1,0:T(8,128)(2,1)}) %all-gather.11.cloned.1.call-update) | async-done | bytes 8388624 | tf_op jit(solution)/shard_map/all_gather | solution.py:95
  326.9 9.9 %feed_down.1.refs_2_ = bf16[512,2048]{1,0:T(8,128)(2,1)S(1)} custom-call(bf16[512,2048]{1,0:T(8,128)(2,1)S(1)} %copy-done.12, f32[512,2048]{1,0:T(8,128)} %get-tuple-element.180.slope_ref, bf16[2048,2048]{1,0:T(8,128)(2,1)} %all-gather.11.cloned.1.call-done.down), custom_call_target="tpu_custom_call" | custom-call | flops 4294967296 | bytes 25165824 | tf_op jit(solution)/shard_map/feed_down/pallas_call | solution.py:112
  336.9 8.9 %convolution_convert_fusion.2 = bf16[512,2048]{1,0:T(8,128)(2,1)S(1)} fusion(bf16[512,2048]{1,0:T(8,128)(2,1)S(1)} %feed_down.1.refs_2_, bf16[2048,2048]{1,0:T(8,128)(2,1)} %all-gather.9.cloned.1.call-done.refs_5_), kind=kOutput, calls=%fused_computation.5 | convolution fusion | flops 4296015872 | bytes 12582912 | tf_op jit(solution)/shard_map/dot_general | solution.py:26
  358.2 10.9 %collective-permute-done.38.refs_2_ = bf16[128,2048]{1,0:T(8,128)(2,1)S(1)} collective-permute-done((bf16[128,2048]{1,0:T(8,128)(2,1)S(1)}, bf16[128,2048]{1,0:T(8,128)(2,1)S(1)}, u32[]{:S(2)}, u32[]{:S(2)}) %collective-permute-start.38) | collective-permute-done | bytes 524320 | tf_op jit(solution)/shard_map/ppermute | solution.py:46
  375.5 9.2 %convolution_convert_fusion.1 = bf16[512,2048]{1,0:T(8,128)(2,1)} fusion(bf16[512,2048]{1,0:T(8,128)(2,1)S(1)} %copy-done.84, bf16[2048,2048]{1,0:T(8,128)(2,1)} %all-gather.11.cloned.1.call-done.down), kind=kOutput, calls=%fused_computation.4 | convolution fusion | flops 4296015872 | bytes 12582912 | tf_op jit(solution)/shard_map/dot_general | solution.py:26
  390.3 8.8 %up_grads.1 = bf16[1024,2048]{1,0:T(8,128)(2,1)} custom-call(s32[1]{0:T(128)} %bitcast.r, bf16[512,2048]{1,0:T(8,128)(2,1)} %get-tuple-element.185.refs_0_, bf16[512,2048]{1,0:T(8,128)(2,1)} %collective-permute-done.34.refs_1_, bf16[512,2048]{1,0:T(8,128)(2,1)} %copy-done.22, bf16[512,2048]{1,0:T(8,128)(2,1)} %copy-done.85), custom_call_target="tpu_custom_call" | custom-call | flops 4294967296 | bytes 16777216 | tf_op jit(solution)/shard_map/up_grads/pallas_call | solution.py:123
  434.4 11.4 %collective-permute-done.49.refs_2_ = bf16[128,2048]{1,0:T(8,128)(2,1)S(1)} collective-permute-done((bf16[128,2048]{1,0:T(8,128)(2,1)S(1)}, bf16[128,2048]{1,0:T(8,128)(2,1)S(1)}, u32[]{:S(2)}, u32[]{:S(2)}) %collective-permute-start.49) | collective-permute-done | bytes 524320 | tf_op jit(solution)/shard_map/ppermute | solution.py:46
  472.9 11.7 %attention_grads.1 = bf16[1024,3072]{1,0:T(8,128)(2,1)} custom-call(s32[1]{0:T(128)} %bitcast.r, bf16[512,2048]{1,0:T(8,128)(2,1)} %get-tuple-element.213.refs_0_, bf16[512,2048]{1,0:T(8,128)(2,1)} %collective-permute-done.30.refs_1_, bf16[512,2048]{1,0:T(8,128)(2,1)} %copy-done.23, bf16[512,2048]{1,0:T(8,128)(2,1)} %collective-permute-done.56.refs_3_, ...), custom_call_target="tpu_custom_call" | custom-call | flops 6442450944 | bytes 25165824 | tf_op jit(solution)/shard_map/attention_grads/pallas_call | solution.py:123
  486.7 20.1 %all_to_all.71 = bf16[8,16,1024]{2,1,0:T(8,128)(2,1)S(1)} all-to-all(bf16[8,16,1024]{2,1,0:T(8,128)(2,1)S(1)} %bitcast.95), channel_id=1, replica_groups=mesh['z'=4,'x'=2,'c'=2,'y'=2] {'z','c'}, dimensions={0} | all-to-all | bytes 524288 | tf_op jit(solution)/shard_map/all_to_all | solution.py:50
  538.5 15.7 %collective-permute-done.60.refs_1_ = bf16[64,4096]{1,0:T(8,128)(2,1)} collective-permute-done((bf16[64,4096]{1,0:T(8,128)(2,1)}, bf16[64,4096]{1,0:T(8,128)(2,1)}, u32[]{:S(2)}, u32[]{:S(2)}) %collective-permute-start.60) | collective-permute-done | bytes 524320 | tf_op jit(solution)/shard_map/ppermute | solution.py:46
  592.7 11.1 %all_to_all.72 = bf16[4,16,1024]{2,1,0:T(8,128)(2,1)S(1)} all-to-all(bf16[4,16,1024]{2,1,0:T(8,128)(2,1)S(1)} %bitcast.102), channel_id=1, replica_groups=mesh['z'=4,'x'=2,'c'=2,'y'=2] {'z'}, dimensions={0} | all-to-all | bytes 262144 | tf_op jit(solution)/shard_map/all_to_all | solution.py:50
  603.8 11.1 %all_to_all.73 = bf16[4,16,1024]{2,1,0:T(8,128)(2,1)S(1)} all-to-all(bf16[4,16,1024]{2,1,0:T(8,128)(2,1)S(1)} %broadcast_in_dim.18), channel_id=1, replica_groups=mesh['z'=4,'x'=2,'c'=2,'y'=2] {'z'}, dimensions={0} | all-to-all | bytes 262144 | tf_op jit(solution)/shard_map/all_to_all | solution.py:50
  615.0 10.0 %all_to_all.74.own_ref = bf16[4,64,1024]{2,1,0:T(8,128)(2,1)S(1)} all-to-all(bf16[4,64,1024]{2,1,0:T(8,128)(2,1)S(1)} %broadcast_in_dim.20), channel_id=1, replica_groups=mesh['z'=4,'x'=2,'c'=2,'y'=2] {'x','y'}, dimensions={0} | all-to-all | bytes 1048576 | tf_op jit(solution)/shard_map/all_to_all | solution.py:50
  633.4 15.8 %collective-permute-done.71 = f32[4,2048]{1,0:T(4,128)S(1)} collective-permute-done((f32[4,2048]{1,0:T(4,128)S(1)}, f32[4,2048]{1,0:T(4,128)S(1)}, u32[]{:S(2)}, u32[]{:S(2)}) %collective-permute-start.71) | collective-permute-done | bytes 32800 | tf_op jit(solution)/shard_map/ppermute | solution.py:46
  (466 shorter events, 372.8 us)
Async XLA Ops:
  7.2 116.0 %all-gather.5.cloned.1.call-start = ((), (), s32[]{:S(2)}) async-start(), calls=%async_computation.16 | async-start | bytes 9437184 | tf_op jit(solution)/shard_map/all_gather | solution.py:95
  27.5 170.5 %all-gather.7.cloned.1.call-start = ((), (), s32[]{:S(2)}) async-start(), calls=%async_computation.17 | async-start | bytes 4718592 | tf_op jit(solution)/shard_map/all_gather | solution.py:95
  65.2 201.2 %all-gather.9.cloned.1.call-start = ((), (), s32[]{:S(2)}) async-start(), calls=%async_computation.18 | async-start | bytes 9437184 | tf_op jit(solution)/shard_map/all_gather | solution.py:95
  80.8 244.6 %all-gather.11.cloned.1.call-start = ((), (), s32[]{:S(2)}) async-start(), calls=%async_computation.19 | async-start | bytes 9437184 | tf_op jit(solution)/shard_map/all_gather | solution.py:95
  156.4 251.3 %reduce-scatter.4.cloned.1.call-start = ((), (), s32[]{:S(2)}) async-start(), calls=%async_computation.20 | async-start | bytes 5242880 | tf_op jit(solution)/shard_map/reduce_scatter | solution.py:99
  263.9 22.8 %collective-permute-start.24 = (bf16[128,2048]{1,0:T(8,128)(2,1)}, bf16[128,2048]{1,0:T(8,128)(2,1)}, u32[]{:S(2)}, u32[]{:S(2)}) collective-permute-start(bf16[128,2048]{1,0:T(8,128)(2,1)} %get-tuple-element.175.refs_3_), channel_id=1, source_target_pairs={{0,1},{1,0},{2,3},{3,2},{4,5},{5,4},{6,7},{7,6},{8,9},{9,8},{10,11... | collective-permute-start | bytes 1572872 | tf_op jit(solution)/shard_map/ppermute | solution.py:46
  264.5 20.1 %collective-permute-start.25 = (bf16[128,2048]{1,0:T(8,128)(2,1)}, bf16[128,2048]{1,0:T(8,128)(2,1)}, u32[]{:S(2)}, u32[]{:S(2)}) collective-permute-start(bf16[128,2048]{1,0:T(8,128)(2,1)} %get-tuple-element.175.refs_3_), channel_id=1, source_target_pairs={{0,4},{4,0},{1,5},{5,1},{2,6},{6,2},{3,7},{7,3},{8,12},{12,8},{9,1... | collective-permute-start | bytes 1572872 | tf_op jit(solution)/shard_map/ppermute | solution.py:46
  296.3 16.8 %collective-permute-start.30 = (bf16[512,2048]{1,0:T(8,128)(2,1)}, bf16[512,2048]{1,0:T(8,128)(2,1)}, u32[]{:S(2)}, u32[]{:S(2)}) collective-permute-start(bf16[512,2048]{1,0:T(8,128)(2,1)} %get-tuple-element.213.refs_0_), channel_id=1, source_target_pairs={{0,2},{2,0},{1,3},{3,1},{4,6},{6,4},{5,7},{7,5},{8,10},{10,8},{9,1... | collective-permute-start | bytes 6291464 | tf_op jit(solution)/shard_map/ppermute | solution.py:46
  296.8 16.3 %collective-permute-start.32 = (bf16[512,2048]{1,0:T(8,128)(2,1)}, bf16[512,2048]{1,0:T(8,128)(2,1)}, u32[]{:S(2)}, u32[]{:S(2)}) collective-permute-start(bf16[512,2048]{1,0:T(8,128)(2,1)} %get-tuple-element.216.refs_4_), channel_id=1, source_target_pairs={{0,2},{2,0},{1,3},{3,1},{4,6},{6,4},{5,7},{7,5},{8,10},{10,8},{9,1... | collective-permute-start | bytes 6291464 | tf_op jit(solution)/shard_map/ppermute | solution.py:46
  313.1 172.3 %reduce-scatter.6.cloned.1.call-start = ((), (), s32[]{:S(2)}) async-start(), calls=%async_computation.21 | async-start | bytes 5242880 | tf_op jit(solution)/shard_map/reduce_scatter | solution.py:99
  349.0 39.9 %collective-permute-start.43 = (bf16[512,2048]{1,0:T(8,128)(2,1)S(1)}, bf16[512,2048]{1,0:T(8,128)(2,1)S(1)}, u32[]{:S(2)}, u32[]{:S(2)}) collective-permute-start(bf16[512,2048]{1,0:T(8,128)(2,1)S(1)} %feed_down.1.refs_2_), channel_id=1, source_target_pairs={{0,2},{2,0},{1,3},{3,1},{4,6},{6,4},{5,7},{7,5},{8,10},{10,8},{9,1... | collective-permute-start | bytes 6291464 | tf_op jit(solution)/shard_map/ppermute | solution.py:46
  408.4 216.7 %reduce-scatter.8.cloned.1.call-start = ((), (), s32[]{:S(2)}) async-start(), calls=%async_computation.22 | async-start | bytes 7864320 | tf_op jit(solution)/shard_map/reduce_scatter | solution.py:99
  467.0 17.6 %collective-permute-start.54 = (bf16[128,2048]{1,0:T(8,128)(2,1)}, bf16[128,2048]{1,0:T(8,128)(2,1)S(1)}, u32[]{:S(2)}, u32[]{:S(2)}) collective-permute-start(bf16[128,2048]{1,0:T(8,128)(2,1)} %get-tuple-element.207), channel_id=1, source_target_pairs={{0,4},{4,0},{1,5},{5,1},{2,6},{6,2},{3,7},{7,3},{8,12},{12,8},{9,1... | collective-permute-start | bytes 1572872 | tf_op jit(solution)/shard_map/ppermute | solution.py:46
  530.6 23.7 %collective-permute-start.60 = (bf16[64,4096]{1,0:T(8,128)(2,1)}, bf16[64,4096]{1,0:T(8,128)(2,1)}, u32[]{:S(2)}, u32[]{:S(2)}) collective-permute-start(bf16[64,4096]{1,0:T(8,128)(2,1)} %get-tuple-element.231), channel_id=1, source_target_pairs={{0,1},{1,0},{2,3},{3,2},{4,5},{5,4},{6,7},{7,6},{8,9},{9,8},{10,11... | collective-permute-start | bytes 1572872 | tf_op jit(solution)/shard_map/ppermute | solution.py:46
  532.6 21.7 %collective-permute-start.61 = (bf16[64,4096]{1,0:T(8,128)(2,1)}, bf16[64,4096]{1,0:T(8,128)(2,1)}, u32[]{:S(2)}, u32[]{:S(2)}) collective-permute-start(bf16[64,4096]{1,0:T(8,128)(2,1)} %get-tuple-element.232), channel_id=1, source_target_pairs={{0,4},{4,0},{1,5},{5,1},{2,6},{6,2},{3,7},{7,3},{8,12},{12,8},{9,1... | collective-permute-start | bytes 1572872 | tf_op jit(solution)/shard_map/ppermute | solution.py:46
  534.1 24.7 %collective-permute-start.62 = (bf16[64,4096]{1,0:T(8,128)(2,1)}, bf16[64,4096]{1,0:T(8,128)(2,1)}, u32[]{:S(2)}, u32[]{:S(2)}) collective-permute-start(bf16[64,4096]{1,0:T(8,128)(2,1)} %get-tuple-element.233), channel_id=1, source_target_pairs={{0,5},{1,4},{4,1},{5,0},{2,7},{3,6},{6,3},{7,2},{8,13},{9,12},{12,... | collective-permute-start | bytes 1572872 | tf_op jit(solution)/shard_map/ppermute | solution.py:90
  535.1 25.2 %collective-permute-start.65 = (bf16[64,2048]{1,0:T(8,128)(2,1)}, bf16[64,2048]{1,0:T(8,128)(2,1)S(1)}, u32[]{:S(2)}, u32[]{:S(2)}) collective-permute-start(bf16[64,2048]{1,0:T(8,128)(2,1)} %get-tuple-element.275), channel_id=1, source_target_pairs={{0,1},{1,0},{2,3},{3,2},{4,5},{5,4},{6,7},{7,6},{8,9},{9,8},{10,11... | collective-permute-start | bytes 786440 | tf_op jit(solution)/shard_map/ppermute | solution.py:46
  537.1 24.6 %collective-permute-start.67 = (bf16[64,2048]{1,0:T(8,128)(2,1)}, bf16[64,2048]{1,0:T(8,128)(2,1)S(1)}, u32[]{:S(2)}, u32[]{:S(2)}) collective-permute-start(bf16[64,2048]{1,0:T(8,128)(2,1)} %get-tuple-element.273), channel_id=1, source_target_pairs={{0,4},{4,0},{1,5},{5,1},{2,6},{6,2},{3,7},{7,3},{8,12},{12,8},{9,1... | collective-permute-start | bytes 786440 | tf_op jit(solution)/shard_map/ppermute | solution.py:46
  571.2 20.4 %all-to-all-start.9 = ((bf16[4,64,1024]{2,1,0:T(8,128)(2,1)}), bf16[4,64,1024]{2,1,0:T(8,128)(2,1)}, u32[]{:S(2)}, u32[]{:S(2)}) async-start(bf16[4,64,1024]{2,1,0:T(8,128)(2,1)} %add_convert_fusion), calls=%async_computation.11 | async-start | bytes 1048576 | tf_op jit(solution)/shard_map/all_to_all | solution.py:50
  625.0 41.9 %collective-permute-start.69 = (bf16[4,64,1024]{2,1,0:T(8,128)(2,1)S(1)}, bf16[4,64,1024]{2,1,0:T(8,128)(2,1)S(1)}, u32[]{:S(2)}, u32[]{:S(2)}) collective-permute-start(bf16[4,64,1024]{2,1,0:T(8,128)(2,1)S(1)} %all_to_all.74.own_ref), channel_id=1, source_target_pairs={{0,2},{2,0},{1,3},{3,1},{4,6},{6,4},{5,7},{7,5},{8,10},{10,8},{9,1... | collective-permute-start | bytes 1572872 | tf_op jit(solution)/shard_map/ppermute | solution.py:46
  627.7 35.7 %collective-permute-start.75 = (bf16[64,3072]{1,0:T(8,128)(2,1)}, bf16[64,3072]{1,0:T(8,128)(2,1)S(1)}, u32[]{:S(2)}, u32[]{:S(2)}) collective-permute-start(bf16[64,3072]{1,0:T(8,128)(2,1)} %get-tuple-element.261), channel_id=1, source_target_pairs={{0,1},{1,0},{2,3},{3,2},{4,5},{5,4},{6,7},{7,6},{8,9},{9,8},{10,11... | collective-permute-start | bytes 1179656 | tf_op jit(solution)/shard_map/ppermute | solution.py:46
  628.6 34.8 %collective-permute-start.76 = (bf16[64,3072]{1,0:T(8,128)(2,1)}, bf16[64,3072]{1,0:T(8,128)(2,1)S(1)}, u32[]{:S(2)}, u32[]{:S(2)}) collective-permute-start(bf16[64,3072]{1,0:T(8,128)(2,1)} %get-tuple-element.262), channel_id=1, source_target_pairs={{0,4},{4,0},{1,5},{5,1},{2,6},{6,2},{3,7},{7,3},{8,12},{12,8},{9,1... | collective-permute-start | bytes 1179656 | tf_op jit(solution)/shard_map/ppermute | solution.py:46
  629.2 34.3 %collective-permute-start.77 = (bf16[64,3072]{1,0:T(8,128)(2,1)}, bf16[64,3072]{1,0:T(8,128)(2,1)}, u32[]{:S(2)}, u32[]{:S(2)}) collective-permute-start(bf16[64,3072]{1,0:T(8,128)(2,1)} %get-tuple-element.263), channel_id=1, source_target_pairs={{0,5},{1,4},{4,1},{5,0},{2,7},{3,6},{6,3},{7,2},{8,13},{9,12},{12,... | collective-permute-start | bytes 1179656 | tf_op jit(solution)/shard_map/ppermute | solution.py:90
  632.4 16.8 %collective-permute-start.71 = (f32[4,2048]{1,0:T(4,128)S(1)}, f32[4,2048]{1,0:T(4,128)S(1)}, u32[]{:S(2)}, u32[]{:S(2)}) collective-permute-start(f32[4,2048]{1,0:T(4,128)S(1)} %add.89), channel_id=1, source_target_pairs={{0,4},{4,0},{1,5},{5,1},{2,6},{6,2},{3,7},{7,3},{8,12},{12,8},{9,1... | collective-permute-start | bytes 98312 | tf_op jit(solution)/shard_map/ppermute | solution.py:46
  (151 other events, 1626.5 us)
Sparse Core Ops, SparseCore 0:
  27.6 83.6 all-gather.4
  112.9 47.9 all-gather.6
  162.5 80.7 all-gather.8
  244.7 80.5 all-gather.10
  327.5 75.2 reduce-scatter.3
  407.8 74.5 reduce-scatter.5
  485.5 118.1 reduce-scatter.7

commit v23 on v21

--- a/solution.py
+++ b/solution.py
@@ -966,7 +966,12 @@
         result = scatter_first(token_blocks(result))
         attn_branch, grad_self_mixed = gather_mm(attn_branch, first, 3 * group, group, "out_back")
         grad_projected = self_back(projected, grad_self_mixed, 2 * images)
-        grad_projected, result = lax.optimization_barrier((grad_projected, result))
+        kv_part = kv_grad.astype(BF).reshape(2, z_size, -1, 2 * group)
+        kv_part = kv_part.transpose(1, 0, 2, 3).reshape(2 * z_size, -1, 2 * group)
+        grad_projected, result, kv_part = lax.optimization_barrier(
+            (grad_projected, result, kv_part)
+        )
+        kv_part = trade(kv_part, DATA)
         result = scatter_second(result)
         rest_part = grad_products(
             [
@@ -978,8 +983,8 @@
             "attention_grads",
             *halves,
         )
-        grad_projected, result, kv_grad, rest_part = lax.optimization_barrier(
-            (grad_projected, result, kv_grad, rest_part)
+        grad_projected, result, kv_part, rest_part = lax.optimization_barrier(
+            (grad_projected, result, kv_part, rest_part)
         )
         rest_part, up_rows = lax.optimization_barrier((rest_part, up_rows))
         rest_rows = scatter_grad(rest_part, grad_axes)
@@ -996,13 +1001,11 @@
         sums = jnp.concatenate([gain_grad_a, gain_grad_b, gain_grad_c, mask_grad], axis=0)
 
 
-        kv_part = kv_grad.astype(BF).reshape(2, z_size, -1, 2 * group)
-        kv_part = kv_part.transpose(1, 0, 2, 3).reshape(2 * z_size, -1, 2 * group)
-        kv_part = trade(kv_part, DATA).astype(F32).sum(axis=0).astype(BF)
+        kv_part = kv_part.astype(F32).sum(axis=0).astype(BF)
         kv_sum = spread(kv_part, "z", z_size).reshape(-1, 2 * group)
         wide_rows = swap_parts(pick_rows([down_rows, up_rows], rank))
-        kv_sum, wide_rows = lax.optimization_barrier((kv_sum, wide_rows))
         kv_grads = spread(kv_sum, PLANE, 8)
+        kv_grads, wide_rows = lax.optimization_barrier((kv_grads, wide_rows))
         kv_weight_grad, grad_text_w, caption_part = text_back(
             kv_grads, own_text, w_cross, caption, w_text, halves_of(sums, text_width // 4)
         )
@@ -1017,12 +1020,11 @@
         sums = layer_order(add_z(whole_of(caption_part[half_context:], width)))
         caption_part = caption_part[:half_context].astype(BF).reshape(z_size, -1, text_width // 4)
         caption_part = trade(caption_part, "z").astype(F32).sum(axis=0).astype(BF)
-        rest_rows = pick_rows([rest_rows], rank)
         caption_part = spread(caption_part, "z", z_size).reshape(half_context, -1)
+        caption_part = spread(caption_part)
         caption_part, rest_rows = lax.optimization_barrier((caption_part, rest_rows))
-        rest_rows = swap_parts(rest_rows)
-        caption_part = spread(caption_part)
         grad_caption = caption_output(caption_part, swap(caption_part, "c"), core)
+        rest_rows = swap_parts(pick_rows([rest_rows], rank))
         qkv_grad, out_grad, grad_cross, cross_out_grad = finish_all(
             rest_rows, kv_weight_grad, rank
         )

time: 667 us -> 666 us (level)
  starting transfers between devices: 105 us -> 84.9 us
  blocking collectives: 103 us -> 116 us
  waiting for transfers between devices: 210 us -> 222 us
    all_to_all x5 -> x4, waiting for transfers between devices: 38.5 us -> 18.2 us  [trade(): return lax.all_to_all(blocks, axes, 0, 0, tiled=True)]
    ppermute x3, waiting for transfers between devices: 5.98 us -> 22.5 us  [swap_parts(): lax.ppermute(parts[3], GROUP, ((0, 3), (1, 2), (2, 1), (3, 0)))]
    ppermute x68, waiting for transfers between devices: 146 us -> 160 us  [swap(): return lax.ppermute(values, axis, PAIR)]
    all_to_all x8 -> x9, blocking collectives: 103 us -> 116 us  [trade(): return lax.all_to_all(blocks, axes, 0, 0, tiled=True)]
    ppermute x2, starting transfers between devices: 9.14 us -> 0.27 us  [add_z(): lax.ppermute(values, 'z', tuple(((k, k ^ step) for k in range(z_size))))]
    all_to_all x5 -> x4, starting transfers between devices: 22.3 us -> 17.5 us  [trade(): return lax.all_to_all(blocks, axes, 0, 0, tiled=True)]
    unnamed x196 -> x160, local copies, waits for them, and re-layouts: 42.7 us -> 39.9 us
  transfers between devices with their start and end apart: 85 -> 84, of which waited for: 46 -> 46; matrix products, arithmetic and copies ran while one was open for 10% -> 10% of each run, Pallas kernels for 16% -> 17%
where the time goes in v23:
time: 666 us; the launch traced here: 658 us
  waiting for transfers between devices  222 us (33%)
  Pallas kernels  118 us (18%)
  blocking collectives  116 us (17%)
  starting transfers between devices  84.9 us (13%)
  local copies, waits for them, and re-layouts  62.2 us (9%)
  matrix products  31.8 us (5%)
  between operations  16.5 us (2%)
    ppermute x68, waiting for transfers between devices, swap(): return lax.ppermute(values, axis, PAIR)  160 us
    all_to_all x9, blocking collectives, trade(): return lax.all_to_all(blocks, axes, 0, 0, tiled=True)  116 us
    pallas_call x19, Pallas kernels, call(): pl.pallas_call(kernel, grid=grid, in_specs=in_specs, out_specs=out_specs,...  73.5 us
    ppermute x68, starting transfers between devices, swap(): return lax.ppermute(values, axis, PAIR)  63.5 us
    pallas_call x10, Pallas kernels, call(): pl.pallas_call(kernel, grid_spec=spec, **options)  44.1 us
    unnamed x160, local copies, waits for them, and re-layouts  39.9 us
    dot_general x6, matrix products, dot(): return lax.dot_general(a, b, (dims, ((), ())), preferred_element_type=F32)  31.8 us
    ppermute x3, waiting for transfers between devices, swap_parts(): lax.ppermute(parts[3], GROUP, ((0, 3), (1, 2), (2, 1), (3, 0)))  22.5 us
  transfers between devices with their start and end apart: 84, of which 46 were waited for; matrix products, arithmetic and copies ran while one was open for 10% of the time, Pallas kernels for 17%

profile of v23, /device:TPU:0, one launch (start us, length us, event | category | flops | bytes accessed | tf_op | source)
XLA Modules:
  0.0 657.7 jit_solution(17317109655722039897)
XLA Ops:
  34.6 8.8 %collective-permute-done.1.refs_2_ = bf16[128,2048]{1,0:T(8,128)(2,1)S(1)} collective-permute-done((bf16[128,2048]{1,0:T(8,128)(2,1)S(1)}, bf16[128,2048]{1,0:T(8,128)(2,1)S(1)}, u32[]{:S(2)}, u32[]{:S(2)}) %collective-permute-start.1) | collective-permute-done | bytes 524320 | tf_op jit(solution)/shard_map/ppermute | solution.py:46
  54.9 10.2 %all_to_all.65 = bf16[4,64,1024]{2,1,0:T(8,128)(2,1)} all-to-all(bf16[4,64,1024]{2,1,0:T(8,128)(2,1)S(1)} %copy.75), channel_id=1, replica_groups=mesh['z'=4,'x'=2,'c'=2,'y'=2] {'x','y'}, dimensions={0} | all-to-all | bytes 1048576 | tf_op jit(solution)/shard_map/all_to_all | solution.py:50
  65.2 15.5 %all_to_all.66 = bf16[4,64,2048]{2,1,0:T(8,128)(2,1)} all-to-all(bf16[4,64,2048]{2,1,0:T(8,128)(2,1)} %bitcast.88), channel_id=1, replica_groups=mesh['z'=4,'x'=2,'c'=2,'y'=2] {'x','y'}, dimensions={0} | all-to-all | bytes 2097152 | tf_op jit(solution)/shard_map/all_to_all | solution.py:50
  83.4 16.9 %all_to_all.67 = bf16[8,64,1024]{2,1,0:T(8,128)(2,1)S(1)} all-to-all(bf16[8,64,1024]{2,1,0:T(8,128)(2,1)S(1)} %get-tuple-element.145), channel_id=1, replica_groups=mesh['z'=4,'x'=2,'c'=2,'y'=2] {'x','c','y'}, dimensions={0} | all-to-all | bytes 2097152 | tf_op jit(solution)/shard_map/all_to_all | solution.py:50
  100.4 11.8 %all_to_all.68 = bf16[4,16,1024]{2,1,0:T(8,128)(2,1)S(1)} all-to-all(bf16[4,16,1024]{2,1,0:T(8,128)(2,1)S(1)} %bitcast.97), channel_id=1, replica_groups=mesh['z'=4,'x'=2,'c'=2,'y'=2] {'z'}, dimensions={0} | all-to-all | bytes 262144 | tf_op jit(solution)/shard_map/all_to_all | solution.py:50
  138.2 18.2 %all_to_all.70 = bf16[4,64,2048]{2,1,0:T(8,128)(2,1)} all-to-all(bf16[4,64,2048]{2,1,0:T(8,128)(2,1)S(1)} %bitcast.87), channel_id=1, replica_groups=mesh['z'=4,'x'=2,'c'=2,'y'=2] {'x','y'}, dimensions={0} | all-to-all | bytes 2097152 | tf_op jit(solution)/shard_map/all_to_all | solution.py:50
  170.5 9.9 %collective-permute-done.11.refs_3_ = bf16[128,2048]{1,0:T(8,128)(2,1)S(1)} collective-permute-done((bf16[128,2048]{1,0:T(8,128)(2,1)S(1)}, bf16[128,2048]{1,0:T(8,128)(2,1)S(1)}, u32[]{:S(2)}, u32[]{:S(2)}) %collective-permute-start.11) | collective-permute-done | bytes 524320 | tf_op jit(solution)/shard_map/ppermute | solution.py:46
  184.9 9.3 %collective-permute-done.13.refs_2_ = bf16[128,2048]{1,0:T(8,128)(2,1)S(1)} collective-permute-done((bf16[128,2048]{1,0:T(8,128)(2,1)S(1)}, bf16[128,2048]{1,0:T(8,128)(2,1)S(1)}, u32[]{:S(2)}, u32[]{:S(2)}) %collective-permute-start.13) | collective-permute-done | bytes 524320 | tf_op jit(solution)/shard_map/ppermute | solution.py:46
  270.9 12.0 %feed_up.1 = (bf16[512,2048]{1,0:T(8,128)(2,1)}, bf16[512,2048]{1,0:T(8,128)(2,1)}, f32[512,2048]{1,0:T(8,128)}) custom-call(bf16[128,2048]{1,0:T(8,128)(2,1)S(1)} %copy-done.56, bf16[128,2048]{1,0:T(8,128)(2,1)S(1)} %copy-done.52, bf16[128,2048]{1,0:T(8,128)(2,1)S(1)} %copy-done.50, bf16[64,2048]{1,0:T(8,128)(2,1)S(1)} %copy-done.62, ...), custom_call_target="tpu_custom_call" | custom-call | flops 4294967296 | bytes 12582912 | tf_op jit(solution)/shard_map/feed_up/pallas_call | solution.py:112
  302.3 8.7 %down_grads.1 = bf16[1024,2048]{1,0:T(8,128)(2,1)} custom-call(s32[1]{0:T(128)} %bitcast.24.r, bf16[512,2048]{1,0:T(8,128)(2,1)S(1)} %constant_dynamic-update-slice_fusion.refs_0_.dy, bf16[512,2048]{1,0:T(8,128)(2,1)S(1)} %collective-permute-done.28.refs_1_, bf16[512,2048]{1,0:T(8,128)(2,1)} %get-tuple-element.184.refs_2_, bf16[512,2048]{1,0:T(8,128)(2,1)} %copy-done.77), custom_call_target="tpu_custom_call" | custom-call | flops 4294967296 | bytes 16777216 | tf_op jit(solution)/shard_map/down_grads/pallas_call | solution.py:123
  312.7 12.7 %all-gather.11.cloned.1.call-done.down = bf16[2048,2048]{1,0:T(8,128)(2,1)} async-done(((bf16[256,2048]{1,0:T(8,128)(2,1)}), bf16[2048,2048]{1,0:T(8,128)(2,1)}) %all-gather.11.cloned.1.call-update) | async-done | bytes 8388624 | tf_op jit(solution)/shard_map/all_gather | solution.py:95
  326.9 9.9 %feed_down.1.refs_2_ = bf16[512,2048]{1,0:T(8,128)(2,1)S(1)} custom-call(bf16[512,2048]{1,0:T(8,128)(2,1)S(1)} %copy-done.14, f32[512,2048]{1,0:T(8,128)} %get-tuple-element.177.slope_ref, bf16[2048,2048]{1,0:T(8,128)(2,1)} %all-gather.11.cloned.1.call-done.down), custom_call_target="tpu_custom_call" | custom-call | flops 4294967296 | bytes 25165824 | tf_op jit(solution)/shard_map/feed_down/pallas_call | solution.py:112
  336.9 8.9 %convolution_convert_fusion.2 = bf16[512,2048]{1,0:T(8,128)(2,1)S(1)} fusion(bf16[512,2048]{1,0:T(8,128)(2,1)S(1)} %feed_down.1.refs_2_, bf16[2048,2048]{1,0:T(8,128)(2,1)} %all-gather.9.cloned.1.call-done.refs_5_), kind=kOutput, calls=%fused_computation.5 | convolution fusion | flops 4296015872 | bytes 12582912 | tf_op jit(solution)/shard_map/dot_general | solution.py:26
  358.2 10.9 %collective-permute-done.38.refs_2_ = bf16[128,2048]{1,0:T(8,128)(2,1)S(1)} collective-permute-done((bf16[128,2048]{1,0:T(8,128)(2,1)S(1)}, bf16[128,2048]{1,0:T(8,128)(2,1)S(1)}, u32[]{:S(2)}, u32[]{:S(2)}) %collective-permute-start.38) | collective-permute-done | bytes 524320 | tf_op jit(solution)/shard_map/ppermute | solution.py:46
  375.5 9.2 %convolution_convert_fusion.1 = bf16[512,2048]{1,0:T(8,128)(2,1)} fusion(bf16[512,2048]{1,0:T(8,128)(2,1)S(1)} %copy-done.75, bf16[2048,2048]{1,0:T(8,128)(2,1)} %all-gather.11.cloned.1.call-done.down), kind=kOutput, calls=%fused_computation.4 | convolution fusion | flops 4296015872 | bytes 12582912 | tf_op jit(solution)/shard_map/dot_general | solution.py:26
  390.3 8.8 %up_grads.1 = bf16[1024,2048]{1,0:T(8,128)(2,1)} custom-call(s32[1]{0:T(128)} %bitcast.24.r, bf16[512,2048]{1,0:T(8,128)(2,1)} %get-tuple-element.182.refs_0_, bf16[512,2048]{1,0:T(8,128)(2,1)} %collective-permute-done.34.refs_1_, bf16[512,2048]{1,0:T(8,128)(2,1)} %copy-done.22, bf16[512,2048]{1,0:T(8,128)(2,1)} %copy-done.76), custom_call_target="tpu_custom_call" | custom-call | flops 4294967296 | bytes 16777216 | tf_op jit(solution)/shard_map/up_grads/pallas_call | solution.py:123
  433.1 12.0 %collective-permute-done.49.refs_2_ = bf16[128,2048]{1,0:T(8,128)(2,1)S(1)} collective-permute-done((bf16[128,2048]{1,0:T(8,128)(2,1)S(1)}, bf16[128,2048]{1,0:T(8,128)(2,1)S(1)}, u32[]{:S(2)}, u32[]{:S(2)}) %collective-permute-start.49) | collective-permute-done | bytes 524320 | tf_op jit(solution)/shard_map/ppermute | solution.py:46
  476.3 11.8 %attention_grads.1 = bf16[1024,3072]{1,0:T(8,128)(2,1)} custom-call(s32[1]{0:T(128)} %bitcast.24.r, bf16[512,2048]{1,0:T(8,128)(2,1)} %get-tuple-element.211.refs_0_, bf16[512,2048]{1,0:T(8,128)(2,1)} %collective-permute-done.30.refs_1_, bf16[512,2048]{1,0:T(8,128)(2,1)} %get-tuple-element.213.refs_2_, bf16[512,2048]{1,0:T(8,128)(2,1)} %collective-permute-done.56.refs_3_, ...), custom_call_target="tpu_custom_call" | custom-call | flops 6442450944 | bytes 25165824 | tf_op jit(solution)/shard_map/attention_grads/pallas_call | solution.py:123
  535.6 10.8 %collective-permute-done.60.refs_1_ = bf16[64,4096]{1,0:T(8,128)(2,1)} collective-permute-done((bf16[64,4096]{1,0:T(8,128)(2,1)}, bf16[64,4096]{1,0:T(8,128)(2,1)}, u32[]{:S(2)}, u32[]{:S(2)}) %collective-permute-start.60) | collective-permute-done | bytes 524320 | tf_op jit(solution)/shard_map/ppermute | solution.py:46
  546.9 11.7 %collective-permute-done.62.refs_3_ = bf16[64,4096]{1,0:T(8,128)(2,1)} collective-permute-done((bf16[64,4096]{1,0:T(8,128)(2,1)}, bf16[64,4096]{1,0:T(8,128)(2,1)}, u32[]{:S(2)}, u32[]{:S(2)}) %collective-permute-start.62) | collective-permute-done | bytes 524320 | tf_op jit(solution)/shard_map/ppermute | solution.py:90
  573.9 10.0 %all-to-all-done.9 = bf16[8,80,1024]{2,1,0:T(8,128)(2,1)S(1)} async-done(((bf16[8,80,1024]{2,1,0:T(8,128)(2,1)}), bf16[8,80,1024]{2,1,0:T(8,128)(2,1)S(1)}, u32[]{:S(2)}, u32[]{:S(2)}) %all-to-all-start.9) | async-done | bytes 1310752 | tf_op jit(solution)/shard_map/all_to_all | solution.py:50
  584.9 11.0 %all_to_all.71 = bf16[4,16,1024]{2,1,0:T(8,128)(2,1)S(1)} all-to-all(bf16[4,16,1024]{2,1,0:T(8,128)(2,1)S(1)} %bitcast.99), channel_id=1, replica_groups=mesh['z'=4,'x'=2,'c'=2,'y'=2] {'z'}, dimensions={0} | all-to-all | bytes 262144 | tf_op jit(solution)/shard_map/all_to_all | solution.py:50
  596.0 11.8 %all_to_all.72 = bf16[4,16,1024]{2,1,0:T(8,128)(2,1)S(1)} all-to-all(bf16[4,16,1024]{2,1,0:T(8,128)(2,1)S(1)} %broadcast_in_dim.18), channel_id=1, replica_groups=mesh['z'=4,'x'=2,'c'=2,'y'=2] {'z'}, dimensions={0} | all-to-all | bytes 262144 | tf_op jit(solution)/shard_map/all_to_all | solution.py:50
  607.9 12.0 %all_to_all.73.own_ref = bf16[4,64,1024]{2,1,0:T(8,128)(2,1)S(1)} all-to-all(bf16[4,64,1024]{2,1,0:T(8,128)(2,1)S(1)} %broadcast_in_dim.20), channel_id=1, replica_groups=mesh['z'=4,'x'=2,'c'=2,'y'=2] {'x','y'}, dimensions={0} | all-to-all | bytes 1048576 | tf_op jit(solution)/shard_map/all_to_all | solution.py:50
  (442 shorter events, 368.5 us)
Async XLA Ops:
  7.2 116.0 %all-gather.5.cloned.1.call-start = ((), (), s32[]{:S(2)}) async-start(), calls=%async_computation.16 | async-start | bytes 9437184 | tf_op jit(solution)/shard_map/all_gather | solution.py:95
  27.5 170.0 %all-gather.7.cloned.1.call-start = ((), (), s32[]{:S(2)}) async-start(), calls=%async_computation.17 | async-start | bytes 4718592 | tf_op jit(solution)/shard_map/all_gather | solution.py:95
  65.2 200.7 %all-gather.9.cloned.1.call-start = ((), (), s32[]{:S(2)}) async-start(), calls=%async_computation.18 | async-start | bytes 9437184 | tf_op jit(solution)/shard_map/all_gather | solution.py:95
  80.8 244.6 %all-gather.11.cloned.1.call-start = ((), (), s32[]{:S(2)}) async-start(), calls=%async_computation.19 | async-start | bytes 9437184 | tf_op jit(solution)/shard_map/all_gather | solution.py:95
  156.4 249.9 %reduce-scatter.4.cloned.1.call-start = ((), (), s32[]{:S(2)}) async-start(), calls=%async_computation.20 | async-start | bytes 5242880 | tf_op jit(solution)/shard_map/reduce_scatter | solution.py:99
  263.9 22.4 %collective-permute-start.24 = (bf16[128,2048]{1,0:T(8,128)(2,1)}, bf16[128,2048]{1,0:T(8,128)(2,1)}, u32[]{:S(2)}, u32[]{:S(2)}) collective-permute-start(bf16[128,2048]{1,0:T(8,128)(2,1)} %get-tuple-element.172.refs_3_), channel_id=1, source_target_pairs={{0,1},{1,0},{2,3},{3,2},{4,5},{5,4},{6,7},{7,6},{8,9},{9,8},{10,11... | collective-permute-start | bytes 1572872 | tf_op jit(solution)/shard_map/ppermute | solution.py:46
  263.9 20.1 %collective-permute-start.25 = (bf16[128,2048]{1,0:T(8,128)(2,1)}, bf16[128,2048]{1,0:T(8,128)(2,1)}, u32[]{:S(2)}, u32[]{:S(2)}) collective-permute-start(bf16[128,2048]{1,0:T(8,128)(2,1)} %get-tuple-element.172.refs_3_), channel_id=1, source_target_pairs={{0,4},{4,0},{1,5},{5,1},{2,6},{6,2},{3,7},{7,3},{8,12},{12,8},{9,1... | collective-permute-start | bytes 1572872 | tf_op jit(solution)/shard_map/ppermute | solution.py:46
  295.9 16.5 %collective-permute-start.30 = (bf16[512,2048]{1,0:T(8,128)(2,1)}, bf16[512,2048]{1,0:T(8,128)(2,1)}, u32[]{:S(2)}, u32[]{:S(2)}) collective-permute-start(bf16[512,2048]{1,0:T(8,128)(2,1)} %get-tuple-element.211.refs_0_), channel_id=1, source_target_pairs={{0,2},{2,0},{1,3},{3,1},{4,6},{6,4},{5,7},{7,5},{8,10},{10,8},{9,1... | collective-permute-start | bytes 6291464 | tf_op jit(solution)/shard_map/ppermute | solution.py:46
  296.3 16.0 %collective-permute-start.32 = (bf16[512,2048]{1,0:T(8,128)(2,1)}, bf16[512,2048]{1,0:T(8,128)(2,1)}, u32[]{:S(2)}, u32[]{:S(2)}) collective-permute-start(bf16[512,2048]{1,0:T(8,128)(2,1)} %get-tuple-element.214.refs_4_), channel_id=1, source_target_pairs={{0,2},{2,0},{1,3},{3,1},{4,6},{6,4},{5,7},{7,5},{8,10},{10,8},{9,1... | collective-permute-start | bytes 6291464 | tf_op jit(solution)/shard_map/ppermute | solution.py:46
  296.4 16.0 %collective-permute-start.34 = (bf16[512,2048]{1,0:T(8,128)(2,1)}, bf16[512,2048]{1,0:T(8,128)(2,1)}, u32[]{:S(2)}, u32[]{:S(2)}) collective-permute-start(bf16[512,2048]{1,0:T(8,128)(2,1)} %get-tuple-element.182.refs_0_), channel_id=1, source_target_pairs={{0,2},{2,0},{1,3},{3,1},{4,6},{6,4},{5,7},{7,5},{8,10},{10,8},{9,1... | collective-permute-start | bytes 6291464 | tf_op jit(solution)/shard_map/ppermute | solution.py:46
  312.4 177.3 %reduce-scatter.6.cloned.1.call-start = ((), (), s32[]{:S(2)}) async-start(), calls=%async_computation.21 | async-start | bytes 5242880 | tf_op jit(solution)/shard_map/reduce_scatter | solution.py:99
  349.0 39.9 %collective-permute-start.43 = (bf16[512,2048]{1,0:T(8,128)(2,1)S(1)}, bf16[512,2048]{1,0:T(8,128)(2,1)S(1)}, u32[]{:S(2)}, u32[]{:S(2)}) collective-permute-start(bf16[512,2048]{1,0:T(8,128)(2,1)S(1)} %feed_down.1.refs_2_), channel_id=1, source_target_pairs={{0,2},{2,0},{1,3},{3,1},{4,6},{6,4},{5,7},{7,5},{8,10},{10,8},{9,1... | collective-permute-start | bytes 6291464 | tf_op jit(solution)/shard_map/ppermute | solution.py:46
  455.6 19.6 %collective-permute-start.57 = (bf16[512,2048]{1,0:T(8,128)(2,1)}, bf16[512,2048]{1,0:T(8,128)(2,1)}, u32[]{:S(2)}, u32[]{:S(2)}) collective-permute-start(bf16[512,2048]{1,0:T(8,128)(2,1)} %get-tuple-element.216.refs_6_), channel_id=1, source_target_pairs={{0,2},{2,0},{1,3},{3,1},{4,6},{6,4},{5,7},{7,5},{8,10},{10,8},{9,1... | collective-permute-start | bytes 6291464 | tf_op jit(solution)/shard_map/ppermute | solution.py:46
  467.4 20.6 %collective-permute-start.54 = (bf16[128,2048]{1,0:T(8,128)(2,1)}, bf16[128,2048]{1,0:T(8,128)(2,1)}, u32[]{:S(2)}, u32[]{:S(2)}) collective-permute-start(bf16[128,2048]{1,0:T(8,128)(2,1)} %get-tuple-element.208), channel_id=1, source_target_pairs={{0,4},{4,0},{1,5},{5,1},{2,6},{6,2},{3,7},{7,3},{8,12},{12,8},{9,1... | collective-permute-start | bytes 1572872 | tf_op jit(solution)/shard_map/ppermute | solution.py:46
  469.1 19.0 %all-to-all-start.6 = ((bf16[8,16,1024]{2,1,0:T(8,128)(2,1)}), bf16[8,16,1024]{2,1,0:T(8,128)(2,1)S(1)}, u32[]{:S(2)}, u32[]{:S(2)}) async-start(bf16[8,16,1024]{2,1,0:T(8,128)(2,1)} %bitcast.29), calls=%async_computation.7 | async-start | bytes 524288 | tf_op jit(solution)/shard_map/all_to_all | solution.py:50
  474.3 145.5 %reduce-scatter.8.cloned.1.call-start = ((), (), s32[]{:S(2)}) async-start(), calls=%async_computation.22 | async-start | bytes 7864320 | tf_op jit(solution)/shard_map/reduce_scatter | solution.py:99
  498.9 16.9 %all-to-all-start.7 = ((bf16[4,16,1024]{2,1,0:T(8,128)(2,1)}), bf16[4,16,1024]{2,1,0:T(8,128)(2,1)S(1)}, u32[]{:S(2)}, u32[]{:S(2)}) async-start(bf16[4,16,1024]{2,1,0:T(8,128)(2,1)} %broadcast_in_dim.15), calls=%async_computation.8 | async-start | bytes 262144 | tf_op jit(solution)/shard_map/all_to_all | solution.py:50
  516.9 18.7 %all-to-all-start.8 = ((bf16[8,64,1024]{2,1,0:T(8,128)(2,1)}), bf16[8,64,1024]{2,1,0:T(8,128)(2,1)S(1)}, u32[]{:S(2)}, u32[]{:S(2)}) async-start(bf16[8,64,1024]{2,1,0:T(8,128)(2,1)} %broadcast_in_dim.17), calls=%async_computation.9 | async-start | bytes 2097152 | tf_op jit(solution)/shard_map/all_to_all | solution.py:50
  529.1 17.3 %collective-permute-start.60 = (bf16[64,4096]{1,0:T(8,128)(2,1)}, bf16[64,4096]{1,0:T(8,128)(2,1)}, u32[]{:S(2)}, u32[]{:S(2)}) collective-permute-start(bf16[64,4096]{1,0:T(8,128)(2,1)} %get-tuple-element.227), channel_id=1, source_target_pairs={{0,1},{1,0},{2,3},{3,2},{4,5},{5,4},{6,7},{7,6},{8,9},{9,8},{10,11... | collective-permute-start | bytes 1572872 | tf_op jit(solution)/shard_map/ppermute | solution.py:46
  530.6 16.3 %collective-permute-start.61 = (bf16[64,4096]{1,0:T(8,128)(2,1)}, bf16[64,4096]{1,0:T(8,128)(2,1)}, u32[]{:S(2)}, u32[]{:S(2)}) collective-permute-start(bf16[64,4096]{1,0:T(8,128)(2,1)} %get-tuple-element.228), channel_id=1, source_target_pairs={{0,4},{4,0},{1,5},{5,1},{2,6},{6,2},{3,7},{7,3},{8,12},{12,8},{9,1... | collective-permute-start | bytes 1572872 | tf_op jit(solution)/shard_map/ppermute | solution.py:46
  531.7 26.9 %collective-permute-start.62 = (bf16[64,4096]{1,0:T(8,128)(2,1)}, bf16[64,4096]{1,0:T(8,128)(2,1)}, u32[]{:S(2)}, u32[]{:S(2)}) collective-permute-start(bf16[64,4096]{1,0:T(8,128)(2,1)} %get-tuple-element.229), channel_id=1, source_target_pairs={{0,5},{1,4},{4,1},{5,0},{2,7},{3,6},{6,3},{7,2},{8,13},{9,12},{12,... | collective-permute-start | bytes 1572872 | tf_op jit(solution)/shard_map/ppermute | solution.py:90
  562.9 21.0 %all-to-all-start.9 = ((bf16[8,80,1024]{2,1,0:T(8,128)(2,1)}), bf16[8,80,1024]{2,1,0:T(8,128)(2,1)S(1)}, u32[]{:S(2)}, u32[]{:S(2)}) async-start(bf16[8,80,1024]{2,1,0:T(8,128)(2,1)} %copy-done.24), calls=%async_computation.11 | async-start | bytes 2621440 | tf_op jit(solution)/shard_map/all_to_all | solution.py:50
  619.8 27.6 %collective-permute-start.67 = (bf16[4,64,1024]{2,1,0:T(8,128)(2,1)S(1)}, bf16[4,64,1024]{2,1,0:T(8,128)(2,1)S(1)}, u32[]{:S(2)}, u32[]{:S(2)}) collective-permute-start(bf16[4,64,1024]{2,1,0:T(8,128)(2,1)S(1)} %all_to_all.73.own_ref), channel_id=1, source_target_pairs={{0,2},{2,0},{1,3},{3,1},{4,6},{6,4},{5,7},{7,5},{8,10},{10,8},{9,1... | collective-permute-start | bytes 1572872 | tf_op jit(solution)/shard_map/ppermute | solution.py:46
  623.9 20.0 %collective-permute-start.72 = (bf16[64,3072]{1,0:T(8,128)(2,1)}, bf16[64,3072]{1,0:T(8,128)(2,1)}, u32[]{:S(2)}, u32[]{:S(2)}) collective-permute-start(bf16[64,3072]{1,0:T(8,128)(2,1)} %get-tuple-element.257), channel_id=1, source_target_pairs={{0,5},{1,4},{4,1},{5,0},{2,7},{3,6},{6,3},{7,2},{8,13},{9,12},{12,... | collective-permute-start | bytes 1179656 | tf_op jit(solution)/shard_map/ppermute | solution.py:90
  (138 other events, 1572.2 us)
Sparse Core Ops, SparseCore 0:
  27.6 83.6 all-gather.4
  112.9 47.9 all-gather.6
  162.5 80.7 all-gather.8
  244.7 80.5 all-gather.10
  327.5 75.2 reduce-scatter.3
  406.4 78.0 reduce-scatter.5
  489.9 114.3 reduce-scatter.7

commit v24 on v23

--- a/solution.py
+++ b/solution.py
@@ -644,24 +644,21 @@
 
 
 def finish_wide(parts, rank):
-    rows, total = parts[0].shape
-    width = total // 2
+    rows, width = parts[0].shape
 
     def kernel(r, *refs):
         for k in range(4):
 
             @pl.when(pl.program_id(0) == k)
             def _():
-                refs[4][...] = refs[k][:, :width].astype(F32)
-                refs[5][...] = refs[k][:, width:].astype(F32)
-
-    flat = pl.BlockSpec((rows, width), lambda k, r: (0, k ^ r[0]))
+                refs[4][...] = refs[k][...].astype(F32)
+
     return call(
         kernel,
         (4,),
         [whole(p) for p in parts],
-        [flat, flat],
-        [shape((rows, 4 * width), F32)] * 2,
+        pl.BlockSpec((rows, width), lambda k, r: (0, k ^ r[0])),
+        shape((rows, 4 * width), F32),
         parts,
         "finish_wide",
         rank=rank,
@@ -1003,26 +1000,39 @@
 
         kv_part = kv_part.astype(F32).sum(axis=0).astype(BF)
         kv_sum = spread(kv_part, "z", z_size).reshape(-1, 2 * group)
-        wide_rows = swap_parts(pick_rows([down_rows, up_rows], rank))
         kv_grads = spread(kv_sum, PLANE, 8)
-        kv_grads, wide_rows = lax.optimization_barrier((kv_grads, wide_rows))
         kv_weight_grad, grad_text_w, caption_part = text_back(
             kv_grads, own_text, w_cross, caption, w_text, halves_of(sums, text_width // 4)
         )
         half_context = caption.shape[0] // 2
         caption_part = trade(caption_part, PLANE)
         output = layer_output(after_cross, result, unit, order)
-        down_grad, up_grad = finish_wide(wide_rows, rank)
-        caption_part, output, down_grad, up_grad = lax.optimization_barrier(
-            (caption_part, output, down_grad, up_grad)
-        )
+        caption_part, output, down_rows, up_rows = lax.optimization_barrier(
+            (caption_part, output, down_rows, up_rows)
+        )
+
         caption_part = caption_part.astype(F32).sum(axis=0)
         sums = layer_order(add_z(whole_of(caption_part[half_context:], width)))
         caption_part = caption_part[:half_context].astype(BF).reshape(z_size, -1, text_width // 4)
-        caption_part = trade(caption_part, "z").astype(F32).sum(axis=0).astype(BF)
+        caption_part = trade(caption_part, "z")
+        down_parts = swap_parts(pick_rows([down_rows], rank))
+        caption_part, down_parts, up_rows = lax.optimization_barrier(
+            (caption_part, down_parts, up_rows)
+        )
+
+        caption_part = caption_part.astype(F32).sum(axis=0).astype(BF)
         caption_part = spread(caption_part, "z", z_size).reshape(half_context, -1)
+        up_parts = swap_parts(pick_rows([up_rows], rank))
+        down_grad = finish_wide(down_parts, rank)
+        caption_part, up_parts, down_grad = lax.optimization_barrier(
+            (caption_part, up_parts, down_grad)
+        )
+
         caption_part = spread(caption_part)
-        caption_part, rest_rows = lax.optimization_barrier((caption_part, rest_rows))
+        up_grad = finish_wide(up_parts, rank)
+        caption_part, rest_rows, up_grad = lax.optimization_barrier(
+            (caption_part, rest_rows, up_grad)
+        )
         grad_caption = caption_output(caption_part, swap(caption_part, "c"), core)
         rest_rows = swap_parts(pick_rows([rest_rows], rank))
         qkv_grad, out_grad, grad_cross, cross_out_grad = finish_all(

time: 666 us -> 655 us (0.983)
  blocking collectives: 116 us -> 91.4 us
  starting transfers between devices: 84.9 us -> 104 us
  waiting for transfers between devices: 222 us -> 213 us
    all_to_all x9 -> x7, blocking collectives: 116 us -> 91.4 us  [trade(): return lax.all_to_all(blocks, axes, 0, 0, tiled=True)]
    all_to_all x4 -> x6, waiting for transfers between devices: 18.2 us -> 38.4 us  [trade(): return lax.all_to_all(blocks, axes, 0, 0, tiled=True)]
    ppermute x3 -> x4, waiting for transfers between devices: 22.5 us -> 10.2 us  [swap_parts(): lax.ppermute(parts[3], GROUP, ((0, 3), (1, 2), (2, 1), (3, 0)))]
    ppermute x68 -> x70, waiting for transfers between devices: 160 us -> 148 us  [swap(): return lax.ppermute(values, axis, PAIR)]
    all_to_all x4 -> x6, starting transfers between devices: 17.5 us -> 27.5 us  [trade(): return lax.all_to_all(blocks, axes, 0, 0, tiled=True)]
    ppermute x68 -> x70, starting transfers between devices: 63.5 us -> 65.8 us  [swap(): return lax.ppermute(values, axis, PAIR)]
    pallas_call x10 -> x12, Pallas kernels: 44.1 us -> 43.8 us  [call(): pl.pallas_call(kernel, grid_spec=spec, **options)]
    unnamed x160 -> x156, local copies, waits for them, and re-layouts: 39.9 us -> 39.8 us
  transfers between devices with their start and end apart: 84 -> 89, of which waited for: 46 -> 45; matrix products, arithmetic and copies ran while one was open for 10% -> 10% of each run, Pallas kernels for 17% -> 18%
where the time goes in v24:
time: 655 us; the launch traced here: 647 us
  waiting for transfers between devices  213 us (33%)
  Pallas kernels  119 us (18%)
  starting transfers between devices  104 us (16%)
  blocking collectives  91.4 us (14%)
  local copies, waits for them, and re-layouts  63.6 us (10%)
  matrix products  31.8 us (5%)
  between operations  16.5 us (3%)
  other arithmetic  7.98 us (1%)
    ppermute x70, waiting for transfers between devices, swap(): return lax.ppermute(values, axis, PAIR)  148 us
    all_to_all x7, blocking collectives, trade(): return lax.all_to_all(blocks, axes, 0, 0, tiled=True)  91.4 us
    pallas_call x19, Pallas kernels, call(): pl.pallas_call(kernel, grid=grid, in_specs=in_specs, out_specs=out_specs,...  74.8 us
    ppermute x70, starting transfers between devices, swap(): return lax.ppermute(values, axis, PAIR)  65.8 us
    pallas_call x12, Pallas kernels, call(): pl.pallas_call(kernel, grid_spec=spec, **options)  43.8 us
    unnamed x156, local copies, waits for them, and re-layouts  39.8 us
    all_to_all x6, waiting for transfers between devices, trade(): return lax.all_to_all(blocks, axes, 0, 0, tiled=True)  38.4 us
    dot_general x6, matrix products, dot(): return lax.dot_general(a, b, (dims, ((), ())), preferred_element_type=F32)  31.8 us
  transfers between devices with their start and end apart: 89, of which 45 were waited for; matrix products, arithmetic and copies ran while one was open for 10% of the time, Pallas kernels for 18%

profile of v24, /device:TPU:0, one launch (start us, length us, event | category | flops | bytes accessed | tf_op | source)
XLA Modules:
  0.0 646.9 jit_solution(3616729029968002641)
XLA Ops:
  34.6 8.8 %collective-permute-done.1.refs_2_ = bf16[128,2048]{1,0:T(8,128)(2,1)S(1)} collective-permute-done((bf16[128,2048]{1,0:T(8,128)(2,1)S(1)}, bf16[128,2048]{1,0:T(8,128)(2,1)S(1)}, u32[]{:S(2)}, u32[]{:S(2)}) %collective-permute-start.1) | collective-permute-done | bytes 524320 | tf_op jit(solution)/shard_map/ppermute | solution.py:46
  54.9 10.2 %all_to_all.65 = bf16[4,64,1024]{2,1,0:T(8,128)(2,1)} all-to-all(bf16[4,64,1024]{2,1,0:T(8,128)(2,1)S(1)} %copy.75), channel_id=1, replica_groups=mesh['z'=4,'x'=2,'c'=2,'y'=2] {'x','y'}, dimensions={0} | all-to-all | bytes 1048576 | tf_op jit(solution)/shard_map/all_to_all | solution.py:50
  65.2 15.5 %all_to_all.66 = bf16[4,64,2048]{2,1,0:T(8,128)(2,1)} all-to-all(bf16[4,64,2048]{2,1,0:T(8,128)(2,1)} %bitcast.88), channel_id=1, replica_groups=mesh['z'=4,'x'=2,'c'=2,'y'=2] {'x','y'}, dimensions={0} | all-to-all | bytes 2097152 | tf_op jit(solution)/shard_map/all_to_all | solution.py:50
  83.3 16.9 %all_to_all.67 = bf16[8,64,1024]{2,1,0:T(8,128)(2,1)S(1)} all-to-all(bf16[8,64,1024]{2,1,0:T(8,128)(2,1)S(1)} %get-tuple-element.155), channel_id=1, replica_groups=mesh['z'=4,'x'=2,'c'=2,'y'=2] {'x','c','y'}, dimensions={0} | all-to-all | bytes 2097152 | tf_op jit(solution)/shard_map/all_to_all | solution.py:50
  100.4 11.9 %all_to_all.68 = bf16[4,16,1024]{2,1,0:T(8,128)(2,1)S(1)} all-to-all(bf16[4,16,1024]{2,1,0:T(8,128)(2,1)S(1)} %bitcast.98), channel_id=1, replica_groups=mesh['z'=4,'x'=2,'c'=2,'y'=2] {'z'}, dimensions={0} | all-to-all | bytes 262144 | tf_op jit(solution)/shard_map/all_to_all | solution.py:50
  112.3 8.5 %all_to_all.69 = bf16[4,16,1024]{2,1,0:T(8,128)(2,1)S(1)} all-to-all(bf16[4,16,1024]{2,1,0:T(8,128)(2,1)S(1)} %broadcast_in_dim.12), channel_id=1, replica_groups=mesh['z'=4,'x'=2,'c'=2,'y'=2] {'z'}, dimensions={0} | all-to-all | bytes 262144 | tf_op jit(solution)/shard_map/all_to_all | solution.py:50
  127.2 7.9 %qkv_mm.1 = (bf16[512,2048]{1,0:T(8,128)(2,1)}, bf16[512,1536]{1,0:T(8,128)(2,1)S(1)}) custom-call(bf16[128,2048]{1,0:T(8,128)(2,1)S(1)} %copy-done.52, bf16[128,2048]{1,0:T(8,128)(2,1)S(1)} %copy-done.46, bf16[128,2048]{1,0:T(8,128)(2,1)S(1)} %collective-permute-done.1.refs_2_, bf16[64,2048]{1,0:T(8,128)(2,1)S(1)} %copy-done.56, ...), custom_call_target="tpu_custom_call" | custom-call | flops 3221225472 | bytes 10485760 | tf_op jit(solution)/shard_map/qkv_mm/pallas_call | solution.py:112
  138.2 18.2 %all_to_all.70 = bf16[4,64,2048]{2,1,0:T(8,128)(2,1)} all-to-all(bf16[4,64,2048]{2,1,0:T(8,128)(2,1)S(1)} %bitcast.87), channel_id=1, replica_groups=mesh['z'=4,'x'=2,'c'=2,'y'=2] {'x','y'}, dimensions={0} | all-to-all | bytes 2097152 | tf_op jit(solution)/shard_map/all_to_all | solution.py:50
  170.5 10.0 %collective-permute-done.11.refs_3_ = bf16[128,2048]{1,0:T(8,128)(2,1)S(1)} collective-permute-done((bf16[128,2048]{1,0:T(8,128)(2,1)S(1)}, bf16[128,2048]{1,0:T(8,128)(2,1)S(1)}, u32[]{:S(2)}, u32[]{:S(2)}) %collective-permute-start.11) | collective-permute-done | bytes 524320 | tf_op jit(solution)/shard_map/ppermute | solution.py:46
  185.0 9.3 %collective-permute-done.13.refs_2_ = bf16[128,2048]{1,0:T(8,128)(2,1)S(1)} collective-permute-done((bf16[128,2048]{1,0:T(8,128)(2,1)S(1)}, bf16[128,2048]{1,0:T(8,128)(2,1)S(1)}, u32[]{:S(2)}, u32[]{:S(2)}) %collective-permute-start.13) | collective-permute-done | bytes 524320 | tf_op jit(solution)/shard_map/ppermute | solution.py:46
  270.9 11.9 %feed_up.1 = (bf16[512,2048]{1,0:T(8,128)(2,1)}, bf16[512,2048]{1,0:T(8,128)(2,1)}, f32[512,2048]{1,0:T(8,128)}) custom-call(bf16[128,2048]{1,0:T(8,128)(2,1)S(1)} %copy-done.54, bf16[128,2048]{1,0:T(8,128)(2,1)S(1)} %copy-done.50, bf16[128,2048]{1,0:T(8,128)(2,1)S(1)} %copy-done.48, bf16[64,2048]{1,0:T(8,128)(2,1)S(1)} %copy-done.60, ...), custom_call_target="tpu_custom_call" | custom-call | flops 4294967296 | bytes 12582912 | tf_op jit(solution)/shard_map/feed_up/pallas_call | solution.py:112
  302.3 8.7 %down_grads.1 = bf16[1024,2048]{1,0:T(8,128)(2,1)} custom-call(s32[1]{0:T(128)} %bitcast.24.r, bf16[512,2048]{1,0:T(8,128)(2,1)S(1)} %constant_dynamic-update-slice_fusion.refs_0_.dy, bf16[512,2048]{1,0:T(8,128)(2,1)S(1)} %collective-permute-done.28.refs_1_, bf16[512,2048]{1,0:T(8,128)(2,1)} %get-tuple-element.194.refs_2_, bf16[512,2048]{1,0:T(8,128)(2,1)} %copy-done.75), custom_call_target="tpu_custom_call" | custom-call | flops 4294967296 | bytes 16777216 | tf_op jit(solution)/shard_map/down_grads/pallas_call | solution.py:123
  312.7 12.6 %all-gather.11.cloned.1.call-done.down = bf16[2048,2048]{1,0:T(8,128)(2,1)} async-done(((bf16[256,2048]{1,0:T(8,128)(2,1)}), bf16[2048,2048]{1,0:T(8,128)(2,1)}) %all-gather.11.cloned.1.call-update) | async-done | bytes 8388624 | tf_op jit(solution)/shard_map/all_gather | solution.py:95
  326.9 9.9 %feed_down.1.refs_2_ = bf16[512,2048]{1,0:T(8,128)(2,1)S(1)} custom-call(bf16[512,2048]{1,0:T(8,128)(2,1)S(1)} %copy-done.14, f32[512,2048]{1,0:T(8,128)} %get-tuple-element.187.slope_ref, bf16[2048,2048]{1,0:T(8,128)(2,1)} %all-gather.11.cloned.1.call-done.down), custom_call_target="tpu_custom_call" | custom-call | flops 4294967296 | bytes 25165824 | tf_op jit(solution)/shard_map/feed_down/pallas_call | solution.py:112
  336.9 8.9 %convolution_convert_fusion.2 = bf16[512,2048]{1,0:T(8,128)(2,1)S(1)} fusion(bf16[512,2048]{1,0:T(8,128)(2,1)S(1)} %feed_down.1.refs_2_, bf16[2048,2048]{1,0:T(8,128)(2,1)} %all-gather.9.cloned.1.call-done.refs_5_), kind=kOutput, calls=%fused_computation.5 | convolution fusion | flops 4296015872 | bytes 12582912 | tf_op jit(solution)/shard_map/dot_general | solution.py:26
  358.2 10.9 %collective-permute-done.38.refs_2_ = bf16[128,2048]{1,0:T(8,128)(2,1)S(1)} collective-permute-done((bf16[128,2048]{1,0:T(8,128)(2,1)S(1)}, bf16[128,2048]{1,0:T(8,128)(2,1)S(1)}, u32[]{:S(2)}, u32[]{:S(2)}) %collective-permute-start.38) | collective-permute-done | bytes 524320 | tf_op jit(solution)/shard_map/ppermute | solution.py:46
  375.5 9.2 %convolution_convert_fusion.1 = bf16[512,2048]{1,0:T(8,128)(2,1)} fusion(bf16[512,2048]{1,0:T(8,128)(2,1)S(1)} %copy-done.73, bf16[2048,2048]{1,0:T(8,128)(2,1)} %all-gather.11.cloned.1.call-done.down), kind=kOutput, calls=%fused_computation.4 | convolution fusion | flops 4296015872 | bytes 12582912 | tf_op jit(solution)/shard_map/dot_general | solution.py:26
  390.3 8.8 %up_grads.1 = bf16[1024,2048]{1,0:T(8,128)(2,1)} custom-call(s32[1]{0:T(128)} %bitcast.24.r, bf16[512,2048]{1,0:T(8,128)(2,1)} %get-tuple-element.192.refs_0_, bf16[512,2048]{1,0:T(8,128)(2,1)} %collective-permute-done.34.refs_1_, bf16[512,2048]{1,0:T(8,128)(2,1)} %copy-done.22, bf16[512,2048]{1,0:T(8,128)(2,1)} %copy-done.74), custom_call_target="tpu_custom_call" | custom-call | flops 4294967296 | bytes 16777216 | tf_op jit(solution)/shard_map/up_grads/pallas_call | solution.py:123
  420.2 7.5 %collective-permute-done.47.refs_2_ = bf16[128,2048]{1,0:T(8,128)(2,1)S(1)} collective-permute-done((bf16[128,2048]{1,0:T(8,128)(2,1)S(1)}, bf16[128,2048]{1,0:T(8,128)(2,1)S(1)}, u32[]{:S(2)}, u32[]{:S(2)}) %collective-permute-start.47) | collective-permute-done | bytes 524320 | tf_op jit(solution)/shard_map/ppermute | solution.py:46
  433.1 12.0 %collective-permute-done.49.refs_2_ = bf16[128,2048]{1,0:T(8,128)(2,1)S(1)} collective-permute-done((bf16[128,2048]{1,0:T(8,128)(2,1)S(1)}, bf16[128,2048]{1,0:T(8,128)(2,1)S(1)}, u32[]{:S(2)}, u32[]{:S(2)}) %collective-permute-start.49) | collective-permute-done | bytes 524320 | tf_op jit(solution)/shard_map/ppermute | solution.py:46
  476.3 11.8 %attention_grads.1 = bf16[1024,3072]{1,0:T(8,128)(2,1)} custom-call(s32[1]{0:T(128)} %bitcast.24.r, bf16[512,2048]{1,0:T(8,128)(2,1)} %get-tuple-element.221.refs_0_, bf16[512,2048]{1,0:T(8,128)(2,1)} %collective-permute-done.30.refs_1_, bf16[512,2048]{1,0:T(8,128)(2,1)} %get-tuple-element.223.refs_2_, bf16[512,2048]{1,0:T(8,128)(2,1)} %collective-permute-done.56.refs_3_, ...), custom_call_target="tpu_custom_call" | custom-call | flops 6442450944 | bytes 25165824 | tf_op jit(solution)/shard_map/attention_grads/pallas_call | solution.py:123
  528.3 7.4 %all-to-all-done.8.block = bf16[8,64,1024]{2,1,0:T(8,128)(2,1)} async-done(((bf16[8,64,1024]{2,1,0:T(8,128)(2,1)}), bf16[8,64,1024]{2,1,0:T(8,128)(2,1)}, u32[]{:S(2)}, u32[]{:S(2)}) %all-to-all-start.8) | async-done | bytes 1048608 | tf_op jit(solution)/shard_map/all_to_all | solution.py:50
  549.2 13.8 %all-to-all-done.9 = bf16[8,80,1024]{2,1,0:T(8,128)(2,1)} async-done(((bf16[8,80,1024]{2,1,0:T(8,128)(2,1)}), bf16[8,80,1024]{2,1,0:T(8,128)(2,1)}, u32[]{:S(2)}, u32[]{:S(2)}) %all-to-all-start.9) | async-done | bytes 1310752 | tf_op jit(solution)/shard_map/all_to_all | solution.py:50
  568.4 10.3 %all_to_all.71 = bf16[4,16,1024]{2,1,0:T(8,128)(2,1)S(1)} all-to-all(bf16[4,16,1024]{2,1,0:T(8,128)(2,1)S(1)} %bitcast.99), channel_id=1, replica_groups=mesh['z'=4,'x'=2,'c'=2,'y'=2] {'z'}, dimensions={0} | all-to-all | bytes 262144 | tf_op jit(solution)/shard_map/all_to_all | solution.py:50
  (448 shorter events, 369.5 us)
Async XLA Ops:
  7.2 116.0 %all-gather.5.cloned.1.call-start = ((), (), s32[]{:S(2)}) async-start(), calls=%async_computation.16 | async-start | bytes 9437184 | tf_op jit(solution)/shard_map/all_gather | solution.py:95
  27.5 170.1 %all-gather.7.cloned.1.call-start = ((), (), s32[]{:S(2)}) async-start(), calls=%async_computation.17 | async-start | bytes 4718592 | tf_op jit(solution)/shard_map/all_gather | solution.py:95
  65.2 200.7 %all-gather.9.cloned.1.call-start = ((), (), s32[]{:S(2)}) async-start(), calls=%async_computation.18 | async-start | bytes 9437184 | tf_op jit(solution)/shard_map/all_gather | solution.py:95
  80.7 244.6 %all-gather.11.cloned.1.call-start = ((), (), s32[]{:S(2)}) async-start(), calls=%async_computation.19 | async-start | bytes 9437184 | tf_op jit(solution)/shard_map/all_gather | solution.py:95
  156.4 249.9 %reduce-scatter.4.cloned.1.call-start = ((), (), s32[]{:S(2)}) async-start(), calls=%async_computation.20 | async-start | bytes 5242880 | tf_op jit(solution)/shard_map/reduce_scatter | solution.py:99
  263.9 22.4 %collective-permute-start.24 = (bf16[128,2048]{1,0:T(8,128)(2,1)}, bf16[128,2048]{1,0:T(8,128)(2,1)}, u32[]{:S(2)}, u32[]{:S(2)}) collective-permute-start(bf16[128,2048]{1,0:T(8,128)(2,1)} %get-tuple-element.182.refs_3_), channel_id=1, source_target_pairs={{0,1},{1,0},{2,3},{3,2},{4,5},{5,4},{6,7},{7,6},{8,9},{9,8},{10,11... | collective-permute-start | bytes 1572872 | tf_op jit(solution)/shard_map/ppermute | solution.py:46
  263.9 20.1 %collective-permute-start.25 = (bf16[128,2048]{1,0:T(8,128)(2,1)}, bf16[128,2048]{1,0:T(8,128)(2,1)}, u32[]{:S(2)}, u32[]{:S(2)}) collective-permute-start(bf16[128,2048]{1,0:T(8,128)(2,1)} %get-tuple-element.182.refs_3_), channel_id=1, source_target_pairs={{0,4},{4,0},{1,5},{5,1},{2,6},{6,2},{3,7},{7,3},{8,12},{12,8},{9,1... | collective-permute-start | bytes 1572872 | tf_op jit(solution)/shard_map/ppermute | solution.py:46
  295.8 16.6 %collective-permute-start.30 = (bf16[512,2048]{1,0:T(8,128)(2,1)}, bf16[512,2048]{1,0:T(8,128)(2,1)}, u32[]{:S(2)}, u32[]{:S(2)}) collective-permute-start(bf16[512,2048]{1,0:T(8,128)(2,1)} %get-tuple-element.221.refs_0_), channel_id=1, source_target_pairs={{0,2},{2,0},{1,3},{3,1},{4,6},{6,4},{5,7},{7,5},{8,10},{10,8},{9,1... | collective-permute-start | bytes 6291464 | tf_op jit(solution)/shard_map/ppermute | solution.py:46
  296.3 16.1 %collective-permute-start.32 = (bf16[512,2048]{1,0:T(8,128)(2,1)}, bf16[512,2048]{1,0:T(8,128)(2,1)}, u32[]{:S(2)}, u32[]{:S(2)}) collective-permute-start(bf16[512,2048]{1,0:T(8,128)(2,1)} %get-tuple-element.224.refs_4_), channel_id=1, source_target_pairs={{0,2},{2,0},{1,3},{3,1},{4,6},{6,4},{5,7},{7,5},{8,10},{10,8},{9,1... | collective-permute-start | bytes 6291464 | tf_op jit(solution)/shard_map/ppermute | solution.py:46
  296.4 16.0 %collective-permute-start.34 = (bf16[512,2048]{1,0:T(8,128)(2,1)}, bf16[512,2048]{1,0:T(8,128)(2,1)}, u32[]{:S(2)}, u32[]{:S(2)}) collective-permute-start(bf16[512,2048]{1,0:T(8,128)(2,1)} %get-tuple-element.192.refs_0_), channel_id=1, source_target_pairs={{0,2},{2,0},{1,3},{3,1},{4,6},{6,4},{5,7},{7,5},{8,10},{10,8},{9,1... | collective-permute-start | bytes 6291464 | tf_op jit(solution)/shard_map/ppermute | solution.py:46
  296.9 15.5 %collective-permute-start.31 = (bf16[512,512]{1,0:T(8,128)(2,1)}, bf16[512,512]{1,0:T(8,128)(2,1)}, u32[]{:S(2)}, u32[]{:S(2)}) collective-permute-start(bf16[512,512]{1,0:T(8,128)(2,1)} %self_forward.1.refs_10_), channel_id=1, source_target_pairs={{0,2},{2,0},{1,3},{3,1},{4,6},{6,4},{5,7},{7,5},{8,10},{10,8},{9,1... | collective-permute-start | bytes 1572872 | tf_op jit(solution)/shard_map/ppermute | solution.py:46
  312.5 177.3 %reduce-scatter.6.cloned.1.call-start = ((), (), s32[]{:S(2)}) async-start(), calls=%async_computation.21 | async-start | bytes 5242880 | tf_op jit(solution)/shard_map/reduce_scatter | solution.py:99
  349.0 39.9 %collective-permute-start.43 = (bf16[512,2048]{1,0:T(8,128)(2,1)S(1)}, bf16[512,2048]{1,0:T(8,128)(2,1)S(1)}, u32[]{:S(2)}, u32[]{:S(2)}) collective-permute-start(bf16[512,2048]{1,0:T(8,128)(2,1)S(1)} %feed_down.1.refs_2_), channel_id=1, source_target_pairs={{0,2},{2,0},{1,3},{3,1},{4,6},{6,4},{5,7},{7,5},{8,10},{10,8},{9,1... | collective-permute-start | bytes 6291464 | tf_op jit(solution)/shard_map/ppermute | solution.py:46
  455.6 19.6 %collective-permute-start.57 = (bf16[512,2048]{1,0:T(8,128)(2,1)}, bf16[512,2048]{1,0:T(8,128)(2,1)}, u32[]{:S(2)}, u32[]{:S(2)}) collective-permute-start(bf16[512,2048]{1,0:T(8,128)(2,1)} %get-tuple-element.226.refs_6_), channel_id=1, source_target_pairs={{0,2},{2,0},{1,3},{3,1},{4,6},{6,4},{5,7},{7,5},{8,10},{10,8},{9,1... | collective-permute-start | bytes 6291464 | tf_op jit(solution)/shard_map/ppermute | solution.py:46
  467.5 20.6 %collective-permute-start.54 = (bf16[128,2048]{1,0:T(8,128)(2,1)}, bf16[128,2048]{1,0:T(8,128)(2,1)}, u32[]{:S(2)}, u32[]{:S(2)}) collective-permute-start(bf16[128,2048]{1,0:T(8,128)(2,1)} %get-tuple-element.218), channel_id=1, source_target_pairs={{0,4},{4,0},{1,5},{5,1},{2,6},{6,2},{3,7},{7,3},{8,12},{12,8},{9,1... | collective-permute-start | bytes 1572872 | tf_op jit(solution)/shard_map/ppermute | solution.py:46
  469.1 19.0 %all-to-all-start.6 = ((bf16[8,16,1024]{2,1,0:T(8,128)(2,1)}), bf16[8,16,1024]{2,1,0:T(8,128)(2,1)S(1)}, u32[]{:S(2)}, u32[]{:S(2)}) async-start(bf16[8,16,1024]{2,1,0:T(8,128)(2,1)} %bitcast.29), calls=%async_computation.7 | async-start | bytes 524288 | tf_op jit(solution)/shard_map/all_to_all | solution.py:50
  474.3 134.7 %reduce-scatter.8.cloned.1.call-start = ((), (), s32[]{:S(2)}) async-start(), calls=%async_computation.22 | async-start | bytes 7864320 | tf_op jit(solution)/shard_map/reduce_scatter | solution.py:99
  498.9 16.9 %all-to-all-start.7 = ((bf16[4,16,1024]{2,1,0:T(8,128)(2,1)}), bf16[4,16,1024]{2,1,0:T(8,128)(2,1)S(1)}, u32[]{:S(2)}, u32[]{:S(2)}) async-start(bf16[4,16,1024]{2,1,0:T(8,128)(2,1)} %broadcast_in_dim.13), calls=%async_computation.8 | async-start | bytes 262144 | tf_op jit(solution)/shard_map/all_to_all | solution.py:50
  516.9 18.8 %all-to-all-start.8 = ((bf16[8,64,1024]{2,1,0:T(8,128)(2,1)}), bf16[8,64,1024]{2,1,0:T(8,128)(2,1)}, u32[]{:S(2)}, u32[]{:S(2)}) async-start(bf16[8,64,1024]{2,1,0:T(8,128)(2,1)} %broadcast_in_dim.15), calls=%async_computation.9 | async-start | bytes 2097152 | tf_op jit(solution)/shard_map/all_to_all | solution.py:50
  541.3 21.8 %all-to-all-start.9 = ((bf16[8,80,1024]{2,1,0:T(8,128)(2,1)}), bf16[8,80,1024]{2,1,0:T(8,128)(2,1)}, u32[]{:S(2)}, u32[]{:S(2)}) async-start(bf16[8,80,1024]{2,1,0:T(8,128)(2,1)} %copy-done.24), calls=%async_computation.10 | async-start | bytes 2621440 | tf_op jit(solution)/shard_map/all_to_all | solution.py:50
  579.7 17.1 %collective-permute-start.67 = (bf16[64,2048]{1,0:T(8,128)(2,1)}, bf16[64,2048]{1,0:T(8,128)(2,1)S(1)}, u32[]{:S(2)}, u32[]{:S(2)}) collective-permute-start(bf16[64,2048]{1,0:T(8,128)(2,1)} %get-tuple-element.259), channel_id=1, source_target_pairs={{0,1},{1,0},{2,3},{3,2},{4,5},{5,4},{6,7},{7,6},{8,9},{9,8},{10,11... | collective-permute-start | bytes 786440 | tf_op jit(solution)/shard_map/ppermute | solution.py:46
  581.1 15.8 %collective-permute-start.68 = (bf16[64,2048]{1,0:T(8,128)(2,1)}, bf16[64,2048]{1,0:T(8,128)(2,1)S(1)}, u32[]{:S(2)}, u32[]{:S(2)}) collective-permute-start(bf16[64,2048]{1,0:T(8,128)(2,1)} %get-tuple-element.260), channel_id=1, source_target_pairs={{0,4},{4,0},{1,5},{5,1},{2,6},{6,2},{3,7},{7,3},{8,12},{12,8},{9,1... | collective-permute-start | bytes 786440 | tf_op jit(solution)/shard_map/ppermute | solution.py:46
  609.0 27.6 %collective-permute-start.70 = (bf16[4,64,1024]{2,1,0:T(8,128)(2,1)S(1)}, bf16[4,64,1024]{2,1,0:T(8,128)(2,1)S(1)}, u32[]{:S(2)}, u32[]{:S(2)}) collective-permute-start(bf16[4,64,1024]{2,1,0:T(8,128)(2,1)S(1)} %all-to-all-done.12.own_ref), channel_id=1, source_target_pairs={{0,2},{2,0},{1,3},{3,1},{4,6},{6,4},{5,7},{7,5},{8,10},{10,8},{9,1... | collective-permute-start | bytes 1572872 | tf_op jit(solution)/shard_map/ppermute | solution.py:46
  613.7 19.5 %collective-permute-start.75 = (bf16[64,3072]{1,0:T(8,128)(2,1)}, bf16[64,3072]{1,0:T(8,128)(2,1)}, u32[]{:S(2)}, u32[]{:S(2)}) collective-permute-start(bf16[64,3072]{1,0:T(8,128)(2,1)} %get-tuple-element.277), channel_id=1, source_target_pairs={{0,5},{1,4},{4,1},{5,0},{2,7},{3,6},{6,3},{7,2},{8,13},{9,12},{12,... | collective-permute-start | bytes 1179656 | tf_op jit(solution)/shard_map/ppermute | solution.py:90
  (141 other events, 1610.5 us)
Sparse Core Ops, SparseCore 0:
  27.6 83.6 all-gather.4
  112.9 47.9 all-gather.6
  162.5 80.7 all-gather.8
  244.7 80.5 all-gather.10
  327.5 75.2 reduce-scatter.3
  406.4 78.0 reduce-scatter.5
  489.9 116.4 reduce-scatter.7

commit v25 on v24

--- a/solution.py
+++ b/solution.py
@@ -942,11 +942,7 @@
         )
 
         cross_branch = gather_tokens(cross_branch)
-        activated, cross_own = lax.optimization_barrier((activated, cross_branch[0]))
-        result = mm_t(activated, down).astype(BF)
-        cross_branch, up_part, result = lax.optimization_barrier(
-            ((cross_own,) + cross_branch[1:], up_part, result)
-        )
+        cross_branch, up_part = lax.optimization_barrier((cross_branch, up_part))
         cross_branch, grad_cross_mixed = gather_mm(
             cross_branch, mid, group, group, "cross_out_back"
         )
@@ -959,6 +955,8 @@
             parts, grad_after_cross, after_attn, gain_b
         )
 
+        activated, attn_branch = lax.optimization_barrier((activated, attn_branch))
+        result = mm_t(activated, down).astype(BF)
         attn_branch, result = lax.optimization_barrier((gather_tokens(attn_branch), result))
         result = scatter_first(token_blocks(result))
         attn_branch, grad_self_mixed = gather_mm(attn_branch, first, 3 * group, group, "out_back")
@@ -1035,6 +1033,7 @@
         )
         grad_caption = caption_output(caption_part, swap(caption_part, "c"), core)
         rest_rows = swap_parts(pick_rows([rest_rows], rank))
+        grad_caption, rest_rows = lax.optimization_barrier((grad_caption, rest_rows))
         qkv_grad, out_grad, grad_cross, cross_out_grad = finish_all(
             rest_rows, kv_weight_grad, rank
         )

time: 655 us -> 654 us (level)
    unnamed x156 -> x154, local copies, waits for them, and re-layouts: 39.8 us -> 40.6 us
  transfers between devices with their start and end apart: 89 -> 89, of which waited for: 45 -> 42; matrix products, arithmetic and copies ran while one was open for 10% -> 10% of each run, Pallas kernels for 18% -> 17%
where the time goes in v25:
time: 654 us; the launch traced here: 646 us
  waiting for transfers between devices  212 us (32%)
  Pallas kernels  117 us (18%)
  starting transfers between devices  105 us (16%)
  blocking collectives  91.4 us (14%)
  local copies, waits for them, and re-layouts  64.4 us (10%)
  matrix products  31 us (5%)
  between operations  16.6 us (3%)
  other arithmetic  7.98 us (1%)
    ppermute x70, waiting for transfers between devices, swap(): return lax.ppermute(values, axis, PAIR)  147 us
    all_to_all x7, blocking collectives, trade(): return lax.all_to_all(blocks, axes, 0, 0, tiled=True)  91.4 us
    pallas_call x19, Pallas kernels, call(): pl.pallas_call(kernel, grid=grid, in_specs=in_specs, out_specs=out_specs,...  74.5 us
    ppermute x70, starting transfers between devices, swap(): return lax.ppermute(values, axis, PAIR)  69.9 us
    pallas_call x12, Pallas kernels, call(): pl.pallas_call(kernel, grid_spec=spec, **options)  43 us
    unnamed x154, local copies, waits for them, and re-layouts  40.6 us
    all_to_all x6, waiting for transfers between devices, trade(): return lax.all_to_all(blocks, axes, 0, 0, tiled=True)  39.7 us
    dot_general x6, matrix products, dot(): return lax.dot_general(a, b, (dims, ((), ())), preferred_element_type=F32)  31 us
  transfers between devices with their start and end apart: 89, of which 42 were waited for; matrix products, arithmetic and copies ran while one was open for 10% of the time, Pallas kernels for 17%

profile of v25, /device:TPU:0, one launch (start us, length us, event | category | flops | bytes accessed | tf_op | source)
XLA Modules:
  0.0 645.6 jit_solution(13466322424663281132)
XLA Ops:
  34.6 8.8 %collective-permute-done.1.refs_2_ = bf16[128,2048]{1,0:T(8,128)(2,1)S(1)} collective-permute-done((bf16[128,2048]{1,0:T(8,128)(2,1)S(1)}, bf16[128,2048]{1,0:T(8,128)(2,1)S(1)}, u32[]{:S(2)}, u32[]{:S(2)}) %collective-permute-start.1) | collective-permute-done | bytes 524320 | tf_op jit(solution)/shard_map/ppermute | solution.py:46
  54.9 10.2 %all_to_all.65 = bf16[4,64,1024]{2,1,0:T(8,128)(2,1)} all-to-all(bf16[4,64,1024]{2,1,0:T(8,128)(2,1)S(1)} %copy.75), channel_id=1, replica_groups=mesh['z'=4,'x'=2,'c'=2,'y'=2] {'x','y'}, dimensions={0} | all-to-all | bytes 1048576 | tf_op jit(solution)/shard_map/all_to_all | solution.py:50
  65.2 15.5 %all_to_all.66 = bf16[4,64,2048]{2,1,0:T(8,128)(2,1)} all-to-all(bf16[4,64,2048]{2,1,0:T(8,128)(2,1)} %bitcast.88), channel_id=1, replica_groups=mesh['z'=4,'x'=2,'c'=2,'y'=2] {'x','y'}, dimensions={0} | all-to-all | bytes 2097152 | tf_op jit(solution)/shard_map/all_to_all | solution.py:50
  83.4 16.9 %all_to_all.67 = bf16[8,64,1024]{2,1,0:T(8,128)(2,1)S(1)} all-to-all(bf16[8,64,1024]{2,1,0:T(8,128)(2,1)S(1)} %get-tuple-element.159), channel_id=1, replica_groups=mesh['z'=4,'x'=2,'c'=2,'y'=2] {'x','c','y'}, dimensions={0} | all-to-all | bytes 2097152 | tf_op jit(solution)/shard_map/all_to_all | solution.py:50
  100.4 11.9 %all_to_all.68 = bf16[4,16,1024]{2,1,0:T(8,128)(2,1)S(1)} all-to-all(bf16[4,16,1024]{2,1,0:T(8,128)(2,1)S(1)} %bitcast.98), channel_id=1, replica_groups=mesh['z'=4,'x'=2,'c'=2,'y'=2] {'z'}, dimensions={0} | all-to-all | bytes 262144 | tf_op jit(solution)/shard_map/all_to_all | solution.py:50
  112.3 8.5 %all_to_all.69 = bf16[4,16,1024]{2,1,0:T(8,128)(2,1)S(1)} all-to-all(bf16[4,16,1024]{2,1,0:T(8,128)(2,1)S(1)} %broadcast_in_dim.12), channel_id=1, replica_groups=mesh['z'=4,'x'=2,'c'=2,'y'=2] {'z'}, dimensions={0} | all-to-all | bytes 262144 | tf_op jit(solution)/shard_map/all_to_all | solution.py:50
  127.2 7.9 %qkv_mm.1 = (bf16[512,2048]{1,0:T(8,128)(2,1)}, bf16[512,1536]{1,0:T(8,128)(2,1)S(1)}) custom-call(bf16[128,2048]{1,0:T(8,128)(2,1)S(1)} %copy-done.52, bf16[128,2048]{1,0:T(8,128)(2,1)S(1)} %copy-done.46, bf16[128,2048]{1,0:T(8,128)(2,1)S(1)} %collective-permute-done.1.refs_2_, bf16[64,2048]{1,0:T(8,128)(2,1)S(1)} %copy-done.56, ...), custom_call_target="tpu_custom_call" | custom-call | flops 3221225472 | bytes 10485760 | tf_op jit(solution)/shard_map/qkv_mm/pallas_call | solution.py:112
  138.2 18.2 %all_to_all.70 = bf16[4,64,2048]{2,1,0:T(8,128)(2,1)} all-to-all(bf16[4,64,2048]{2,1,0:T(8,128)(2,1)S(1)} %bitcast.87), channel_id=1, replica_groups=mesh['z'=4,'x'=2,'c'=2,'y'=2] {'x','y'}, dimensions={0} | all-to-all | bytes 2097152 | tf_op jit(solution)/shard_map/all_to_all | solution.py:50
  170.5 9.9 %collective-permute-done.11.refs_3_ = bf16[128,2048]{1,0:T(8,128)(2,1)S(1)} collective-permute-done((bf16[128,2048]{1,0:T(8,128)(2,1)S(1)}, bf16[128,2048]{1,0:T(8,128)(2,1)S(1)}, u32[]{:S(2)}, u32[]{:S(2)}) %collective-permute-start.11) | collective-permute-done | bytes 524320 | tf_op jit(solution)/shard_map/ppermute | solution.py:46
  184.9 9.3 %collective-permute-done.13.refs_2_ = bf16[128,2048]{1,0:T(8,128)(2,1)S(1)} collective-permute-done((bf16[128,2048]{1,0:T(8,128)(2,1)S(1)}, bf16[128,2048]{1,0:T(8,128)(2,1)S(1)}, u32[]{:S(2)}, u32[]{:S(2)}) %collective-permute-start.13) | collective-permute-done | bytes 524320 | tf_op jit(solution)/shard_map/ppermute | solution.py:46
  270.9 12.0 %feed_up.1 = (bf16[512,2048]{1,0:T(8,128)(2,1)}, bf16[512,2048]{1,0:T(8,128)(2,1)}, f32[512,2048]{1,0:T(8,128)}) custom-call(bf16[128,2048]{1,0:T(8,128)(2,1)S(1)} %copy-done.54, bf16[128,2048]{1,0:T(8,128)(2,1)S(1)} %copy-done.50, bf16[128,2048]{1,0:T(8,128)(2,1)S(1)} %copy-done.48, bf16[64,2048]{1,0:T(8,128)(2,1)S(1)} %copy-done.60, ...), custom_call_target="tpu_custom_call" | custom-call | flops 4294967296 | bytes 12582912 | tf_op jit(solution)/shard_map/feed_up/pallas_call | solution.py:112
  302.3 8.8 %down_grads.1 = bf16[1024,2048]{1,0:T(8,128)(2,1)} custom-call(s32[1]{0:T(128)} %bitcast.24.r, bf16[512,2048]{1,0:T(8,128)(2,1)S(1)} %constant_dynamic-update-slice_fusion.refs_0_.dy, bf16[512,2048]{1,0:T(8,128)(2,1)S(1)} %collective-permute-done.28.refs_1_, bf16[512,2048]{1,0:T(8,128)(2,1)} %get-tuple-element.207.refs_2_, bf16[512,2048]{1,0:T(8,128)(2,1)} %copy-done.74), custom_call_target="tpu_custom_call" | custom-call | flops 4294967296 | bytes 16777216 | tf_op jit(solution)/shard_map/down_grads/pallas_call | solution.py:123
  312.7 12.6 %all-gather.11.cloned.1.call-done.down = bf16[2048,2048]{1,0:T(8,128)(2,1)} async-done(((bf16[256,2048]{1,0:T(8,128)(2,1)}), bf16[2048,2048]{1,0:T(8,128)(2,1)}) %all-gather.11.cloned.1.call-update) | async-done | bytes 8388624 | tf_op jit(solution)/shard_map/all_gather | solution.py:95
  326.9 9.9 %feed_down.1.refs_2_ = bf16[512,2048]{1,0:T(8,128)(2,1)S(1)} custom-call(bf16[512,2048]{1,0:T(8,128)(2,1)S(1)} %copy-done.14, f32[512,2048]{1,0:T(8,128)} %get-tuple-element.191.slope_ref, bf16[2048,2048]{1,0:T(8,128)(2,1)} %all-gather.11.cloned.1.call-done.down), custom_call_target="tpu_custom_call" | custom-call | flops 4294967296 | bytes 25165824 | tf_op jit(solution)/shard_map/feed_down/pallas_call | solution.py:112
  336.9 8.9 %convolution_convert_fusion.2 = bf16[512,2048]{1,0:T(8,128)(2,1)S(1)} fusion(bf16[512,2048]{1,0:T(8,128)(2,1)S(1)} %feed_down.1.refs_2_, bf16[2048,2048]{1,0:T(8,128)(2,1)} %all-gather.9.cloned.1.call-done.refs_5_), kind=kOutput, calls=%fused_computation.5 | convolution fusion | flops 4296015872 | bytes 12582912 | tf_op jit(solution)/shard_map/dot_general | solution.py:26
  358.2 10.9 %collective-permute-done.38.refs_2_ = bf16[128,2048]{1,0:T(8,128)(2,1)S(1)} collective-permute-done((bf16[128,2048]{1,0:T(8,128)(2,1)S(1)}, bf16[128,2048]{1,0:T(8,128)(2,1)S(1)}, u32[]{:S(2)}, u32[]{:S(2)}) %collective-permute-start.38) | collective-permute-done | bytes 524320 | tf_op jit(solution)/shard_map/ppermute | solution.py:46
  376.3 9.3 %collective-permute-done.40.refs_2_ = bf16[128,2048]{1,0:T(8,128)(2,1)S(1)} collective-permute-done((bf16[128,2048]{1,0:T(8,128)(2,1)S(1)}, bf16[128,2048]{1,0:T(8,128)(2,1)S(1)}, u32[]{:S(2)}, u32[]{:S(2)}) %collective-permute-start.40) | collective-permute-done | bytes 524320 | tf_op jit(solution)/shard_map/ppermute | solution.py:46
  391.1 8.8 %up_grads.1 = bf16[1024,2048]{1,0:T(8,128)(2,1)} custom-call(s32[1]{0:T(128)} %bitcast.24.r, bf16[512,2048]{1,0:T(8,128)(2,1)} %get-tuple-element.195.refs_0_, bf16[512,2048]{1,0:T(8,128)(2,1)} %collective-permute-done.34.refs_1_, bf16[512,2048]{1,0:T(8,128)(2,1)} %copy-done.22, bf16[512,2048]{1,0:T(8,128)(2,1)} %copy-done.73), custom_call_target="tpu_custom_call" | custom-call | flops 4294967296 | bytes 16777216 | tf_op jit(solution)/shard_map/up_grads/pallas_call | solution.py:123
  433.8 11.9 %collective-permute-done.49.refs_2_ = bf16[128,2048]{1,0:T(8,128)(2,1)S(1)} collective-permute-done((bf16[128,2048]{1,0:T(8,128)(2,1)S(1)}, bf16[128,2048]{1,0:T(8,128)(2,1)S(1)}, u32[]{:S(2)}, u32[]{:S(2)}) %collective-permute-start.49) | collective-permute-done | bytes 524320 | tf_op jit(solution)/shard_map/ppermute | solution.py:46
  447.4 8.4 %convolution_convert_fusion = bf16[512,2048]{1,0:T(8,128)(2,1)S(1)} fusion(bf16[512,2048]{1,0:T(8,128)(2,1)S(1)} %copy-done.72, bf16[2048,2048]{1,0:T(8,128)(2,1)} %all-gather.11.cloned.1.call-done.down), kind=kOutput, calls=%fused_computation.3 | convolution fusion | flops 4296015872 | bytes 12582912 | tf_op jit(solution)/shard_map/dot_general | solution.py:26
  477.9 11.7 %attention_grads.1 = bf16[1024,3072]{1,0:T(8,128)(2,1)} custom-call(s32[1]{0:T(128)} %bitcast.24.r, bf16[512,2048]{1,0:T(8,128)(2,1)} %get-tuple-element.224.refs_0_, bf16[512,2048]{1,0:T(8,128)(2,1)} %collective-permute-done.30.refs_1_, bf16[512,2048]{1,0:T(8,128)(2,1)} %get-tuple-element.226.refs_2_, bf16[512,2048]{1,0:T(8,128)(2,1)} %collective-permute-done.56.refs_3_, ...), custom_call_target="tpu_custom_call" | custom-call | flops 6442450944 | bytes 25165824 | tf_op jit(solution)/shard_map/attention_grads/pallas_call | solution.py:123
  529.4 7.8 %all-to-all-done.8.block = bf16[8,64,1024]{2,1,0:T(8,128)(2,1)} async-done(((bf16[8,64,1024]{2,1,0:T(8,128)(2,1)}), bf16[8,64,1024]{2,1,0:T(8,128)(2,1)}, u32[]{:S(2)}, u32[]{:S(2)}) %all-to-all-start.8) | async-done | bytes 1048608 | tf_op jit(solution)/shard_map/all_to_all | solution.py:50
  550.8 13.8 %all-to-all-done.9 = bf16[8,80,1024]{2,1,0:T(8,128)(2,1)} async-done(((bf16[8,80,1024]{2,1,0:T(8,128)(2,1)}), bf16[8,80,1024]{2,1,0:T(8,128)(2,1)}, u32[]{:S(2)}, u32[]{:S(2)}) %all-to-all-start.9) | async-done | bytes 1310752 | tf_op jit(solution)/shard_map/all_to_all | solution.py:50
  570.0 10.3 %all_to_all.71 = bf16[4,16,1024]{2,1,0:T(8,128)(2,1)S(1)} all-to-all(bf16[4,16,1024]{2,1,0:T(8,128)(2,1)S(1)} %bitcast.99), channel_id=1, replica_groups=mesh['z'=4,'x'=2,'c'=2,'y'=2] {'z'}, dimensions={0} | all-to-all | bytes 262144 | tf_op jit(solution)/shard_map/all_to_all | solution.py:50
  (446 shorter events, 366.9 us)
Async XLA Ops:
  7.2 116.0 %all-gather.5.cloned.1.call-start = ((), (), s32[]{:S(2)}) async-start(), calls=%async_computation.16 | async-start | bytes 9437184 | tf_op jit(solution)/shard_map/all_gather | solution.py:95
  27.5 170.0 %all-gather.7.cloned.1.call-start = ((), (), s32[]{:S(2)}) async-start(), calls=%async_computation.17 | async-start | bytes 4718592 | tf_op jit(solution)/shard_map/all_gather | solution.py:95
  65.2 200.7 %all-gather.9.cloned.1.call-start = ((), (), s32[]{:S(2)}) async-start(), calls=%async_computation.18 | async-start | bytes 9437184 | tf_op jit(solution)/shard_map/all_gather | solution.py:95
  80.7 244.6 %all-gather.11.cloned.1.call-start = ((), (), s32[]{:S(2)}) async-start(), calls=%async_computation.19 | async-start | bytes 9437184 | tf_op jit(solution)/shard_map/all_gather | solution.py:95
  156.4 250.7 %reduce-scatter.4.cloned.1.call-start = ((), (), s32[]{:S(2)}) async-start(), calls=%async_computation.20 | async-start | bytes 5242880 | tf_op jit(solution)/shard_map/reduce_scatter | solution.py:99
  263.8 22.4 %collective-permute-start.24 = (bf16[128,2048]{1,0:T(8,128)(2,1)}, bf16[128,2048]{1,0:T(8,128)(2,1)}, u32[]{:S(2)}, u32[]{:S(2)}) collective-permute-start(bf16[128,2048]{1,0:T(8,128)(2,1)} %get-tuple-element.186.refs_3_), channel_id=1, source_target_pairs={{0,1},{1,0},{2,3},{3,2},{4,5},{5,4},{6,7},{7,6},{8,9},{9,8},{10,11... | collective-permute-start | bytes 1572872 | tf_op jit(solution)/shard_map/ppermute | solution.py:46
  264.0 20.1 %collective-permute-start.25 = (bf16[128,2048]{1,0:T(8,128)(2,1)}, bf16[128,2048]{1,0:T(8,128)(2,1)}, u32[]{:S(2)}, u32[]{:S(2)}) collective-permute-start(bf16[128,2048]{1,0:T(8,128)(2,1)} %get-tuple-element.186.refs_3_), channel_id=1, source_target_pairs={{0,4},{4,0},{1,5},{5,1},{2,6},{6,2},{3,7},{7,3},{8,12},{12,8},{9,1... | collective-permute-start | bytes 1572872 | tf_op jit(solution)/shard_map/ppermute | solution.py:46
  295.8 16.6 %collective-permute-start.30 = (bf16[512,2048]{1,0:T(8,128)(2,1)}, bf16[512,2048]{1,0:T(8,128)(2,1)}, u32[]{:S(2)}, u32[]{:S(2)}) collective-permute-start(bf16[512,2048]{1,0:T(8,128)(2,1)} %get-tuple-element.224.refs_0_), channel_id=1, source_target_pairs={{0,2},{2,0},{1,3},{3,1},{4,6},{6,4},{5,7},{7,5},{8,10},{10,8},{9,1... | collective-permute-start | bytes 6291464 | tf_op jit(solution)/shard_map/ppermute | solution.py:46
  296.3 16.1 %collective-permute-start.32 = (bf16[512,2048]{1,0:T(8,128)(2,1)}, bf16[512,2048]{1,0:T(8,128)(2,1)}, u32[]{:S(2)}, u32[]{:S(2)}) collective-permute-start(bf16[512,2048]{1,0:T(8,128)(2,1)} %get-tuple-element.227.refs_4_), channel_id=1, source_target_pairs={{0,2},{2,0},{1,3},{3,1},{4,6},{6,4},{5,7},{7,5},{8,10},{10,8},{9,1... | collective-permute-start | bytes 6291464 | tf_op jit(solution)/shard_map/ppermute | solution.py:46
  296.4 16.0 %collective-permute-start.34 = (bf16[512,2048]{1,0:T(8,128)(2,1)}, bf16[512,2048]{1,0:T(8,128)(2,1)}, u32[]{:S(2)}, u32[]{:S(2)}) collective-permute-start(bf16[512,2048]{1,0:T(8,128)(2,1)} %get-tuple-element.195.refs_0_), channel_id=1, source_target_pairs={{0,2},{2,0},{1,3},{3,1},{4,6},{6,4},{5,7},{7,5},{8,10},{10,8},{9,1... | collective-permute-start | bytes 6291464 | tf_op jit(solution)/shard_map/ppermute | solution.py:46
  312.5 177.4 %reduce-scatter.6.cloned.1.call-start = ((), (), s32[]{:S(2)}) async-start(), calls=%async_computation.21 | async-start | bytes 5242880 | tf_op jit(solution)/shard_map/reduce_scatter | solution.py:99
  349.0 40.8 %collective-permute-start.43 = (bf16[512,2048]{1,0:T(8,128)(2,1)S(1)}, bf16[512,2048]{1,0:T(8,128)(2,1)S(1)}, u32[]{:S(2)}, u32[]{:S(2)}) collective-permute-start(bf16[512,2048]{1,0:T(8,128)(2,1)S(1)} %feed_down.1.refs_2_), channel_id=1, source_target_pairs={{0,2},{2,0},{1,3},{3,1},{4,6},{6,4},{5,7},{7,5},{8,10},{10,8},{9,1... | collective-permute-start | bytes 6291464 | tf_op jit(solution)/shard_map/ppermute | solution.py:46
  459.3 17.6 %collective-permute-start.57 = (bf16[512,2048]{1,0:T(8,128)(2,1)}, bf16[512,2048]{1,0:T(8,128)(2,1)}, u32[]{:S(2)}, u32[]{:S(2)}) collective-permute-start(bf16[512,2048]{1,0:T(8,128)(2,1)} %get-tuple-element.229.refs_6_), channel_id=1, source_target_pairs={{0,2},{2,0},{1,3},{3,1},{4,6},{6,4},{5,7},{7,5},{8,10},{10,8},{9,1... | collective-permute-start | bytes 6291464 | tf_op jit(solution)/shard_map/ppermute | solution.py:46
  471.1 18.6 %collective-permute-start.54 = (bf16[128,2048]{1,0:T(8,128)(2,1)}, bf16[128,2048]{1,0:T(8,128)(2,1)}, u32[]{:S(2)}, u32[]{:S(2)}) collective-permute-start(bf16[128,2048]{1,0:T(8,128)(2,1)} %get-tuple-element.221), channel_id=1, source_target_pairs={{0,4},{4,0},{1,5},{5,1},{2,6},{6,2},{3,7},{7,3},{8,12},{12,8},{9,1... | collective-permute-start | bytes 1572872 | tf_op jit(solution)/shard_map/ppermute | solution.py:46
  471.1 18.5 %all-to-all-start.6 = ((bf16[8,16,1024]{2,1,0:T(8,128)(2,1)}), bf16[8,16,1024]{2,1,0:T(8,128)(2,1)S(1)}, u32[]{:S(2)}, u32[]{:S(2)}) async-start(bf16[8,16,1024]{2,1,0:T(8,128)(2,1)} %bitcast.29), calls=%async_computation.7 | async-start | bytes 524288 | tf_op jit(solution)/shard_map/all_to_all | solution.py:50
  474.6 136.1 %reduce-scatter.8.cloned.1.call-start = ((), (), s32[]{:S(2)}) async-start(), calls=%async_computation.22 | async-start | bytes 7864320 | tf_op jit(solution)/shard_map/reduce_scatter | solution.py:99
  500.9 16.4 %all-to-all-start.7 = ((bf16[4,16,1024]{2,1,0:T(8,128)(2,1)}), bf16[4,16,1024]{2,1,0:T(8,128)(2,1)S(1)}, u32[]{:S(2)}, u32[]{:S(2)}) async-start(bf16[4,16,1024]{2,1,0:T(8,128)(2,1)} %broadcast_in_dim.13), calls=%async_computation.8 | async-start | bytes 262144 | tf_op jit(solution)/shard_map/all_to_all | solution.py:50
  518.5 18.8 %all-to-all-start.8 = ((bf16[8,64,1024]{2,1,0:T(8,128)(2,1)}), bf16[8,64,1024]{2,1,0:T(8,128)(2,1)}, u32[]{:S(2)}, u32[]{:S(2)}) async-start(bf16[8,64,1024]{2,1,0:T(8,128)(2,1)} %broadcast_in_dim.15), calls=%async_computation.9 | async-start | bytes 2097152 | tf_op jit(solution)/shard_map/all_to_all | solution.py:50
  542.9 21.8 %all-to-all-start.9 = ((bf16[8,80,1024]{2,1,0:T(8,128)(2,1)}), bf16[8,80,1024]{2,1,0:T(8,128)(2,1)}, u32[]{:S(2)}, u32[]{:S(2)}) async-start(bf16[8,80,1024]{2,1,0:T(8,128)(2,1)} %copy-done.24), calls=%async_computation.10 | async-start | bytes 2621440 | tf_op jit(solution)/shard_map/all_to_all | solution.py:50
  580.5 17.3 %collective-permute-start.67 = (bf16[64,2048]{1,0:T(8,128)(2,1)S(1)}, bf16[64,2048]{1,0:T(8,128)(2,1)S(1)}, u32[]{:S(2)}, u32[]{:S(2)}) collective-permute-start(bf16[64,2048]{1,0:T(8,128)(2,1)S(1)} %get-tuple-element.262), channel_id=1, source_target_pairs={{0,1},{1,0},{2,3},{3,2},{4,5},{5,4},{6,7},{7,6},{8,9},{9,8},{10,11... | collective-permute-start | bytes 786440 | tf_op jit(solution)/shard_map/ppermute | solution.py:46
  610.7 17.2 %collective-permute-start.70 = (bf16[4,64,1024]{2,1,0:T(8,128)(2,1)S(1)}, bf16[4,64,1024]{2,1,0:T(8,128)(2,1)S(1)}, u32[]{:S(2)}, u32[]{:S(2)}) collective-permute-start(bf16[4,64,1024]{2,1,0:T(8,128)(2,1)S(1)} %all-to-all-done.12.own_ref), channel_id=1, source_target_pairs={{0,2},{2,0},{1,3},{3,1},{4,6},{6,4},{5,7},{7,5},{8,10},{10,8},{9,1... | collective-permute-start | bytes 1572872 | tf_op jit(solution)/shard_map/ppermute | solution.py:46
  613.3 17.5 %collective-permute-start.71 = (bf16[64,3072]{1,0:T(8,128)(2,1)}, bf16[64,3072]{1,0:T(8,128)(2,1)S(1)}, u32[]{:S(2)}, u32[]{:S(2)}) collective-permute-start(bf16[64,3072]{1,0:T(8,128)(2,1)} %get-tuple-element.278), channel_id=1, source_target_pairs={{0,1},{1,0},{2,3},{3,2},{4,5},{5,4},{6,7},{7,6},{8,9},{9,8},{10,11... | collective-permute-start | bytes 1179656 | tf_op jit(solution)/shard_map/ppermute | solution.py:46
  614.8 16.0 %collective-permute-start.72 = (bf16[64,3072]{1,0:T(8,128)(2,1)}, bf16[64,3072]{1,0:T(8,128)(2,1)S(1)}, u32[]{:S(2)}, u32[]{:S(2)}) collective-permute-start(bf16[64,3072]{1,0:T(8,128)(2,1)} %get-tuple-element.279), channel_id=1, source_target_pairs={{0,4},{4,0},{1,5},{5,1},{2,6},{6,2},{3,7},{7,3},{8,12},{12,8},{9,1... | collective-permute-start | bytes 1179656 | tf_op jit(solution)/shard_map/ppermute | solution.py:46
  615.3 19.5 %collective-permute-start.73 = (bf16[64,3072]{1,0:T(8,128)(2,1)}, bf16[64,3072]{1,0:T(8,128)(2,1)}, u32[]{:S(2)}, u32[]{:S(2)}) collective-permute-start(bf16[64,3072]{1,0:T(8,128)(2,1)} %get-tuple-element.280), channel_id=1, source_target_pairs={{0,5},{1,4},{4,1},{5,0},{2,7},{3,6},{6,3},{7,2},{8,13},{9,12},{12,... | collective-permute-start | bytes 1179656 | tf_op jit(solution)/shard_map/ppermute | solution.py:90
  (140 other events, 1564.2 us)
Sparse Core Ops, SparseCore 0:
  27.6 83.6 all-gather.4
  112.9 47.9 all-gather.6
  162.5 80.7 all-gather.8
  244.7 80.5 all-gather.10
  327.5 75.2 reduce-scatter.3
  407.2 77.0 reduce-scatter.5
  490.1 117.7 reduce-scatter.7

commit v26 on v25

--- a/solution.py
+++ b/solution.py
@@ -59,6 +59,12 @@
     from_x = swap(own, "x")
     from_y = swap(own, "y")
     return own, from_y, from_x, swap(from_x[:half], "y"), swap(from_y[half:], "x")
+
+
+def gather_beside(own, work):
+    half = own.shape[0] // 2
+    from_x, from_y, work = lax.optimization_barrier((swap(own, "x"), swap(own, "y"), work))
+    return (own, from_y, from_x, swap(from_x[:half], "y"), swap(from_y[half:], "x")), work
 
 
 def scatter_first(parts):
@@ -941,8 +947,7 @@
             parts, grad_top, after_cross, gain_c
         )
 
-        cross_branch = gather_tokens(cross_branch)
-        cross_branch, up_part = lax.optimization_barrier((cross_branch, up_part))
+        cross_branch, up_part = gather_beside(cross_branch, up_part)
         cross_branch, grad_cross_mixed = gather_mm(
             cross_branch, mid, group, group, "cross_out_back"
         )
@@ -957,7 +962,8 @@
 
         activated, attn_branch = lax.optimization_barrier((activated, attn_branch))
         result = mm_t(activated, down).astype(BF)
-        attn_branch, result = lax.optimization_barrier((gather_tokens(attn_branch), result))
+        attn_branch, result = gather_beside(attn_branch, result)
+        attn_branch, result = lax.optimization_barrier((attn_branch, result))
         result = scatter_first(token_blocks(result))
         attn_branch, grad_self_mixed = gather_mm(attn_branch, first, 3 * group, group, "out_back")
         grad_projected = self_back(projected, grad_self_mixed, 2 * images)

time: 654 us -> 652 us (level)
  transfers between devices with their start and end apart: 89 -> 89, of which waited for: 42 -> 50; matrix products, arithmetic and copies ran while one was open for 10% -> 10% of each run, Pallas kernels for 17% -> 17%
where the time goes in v26:
time: 652 us; the launch traced here: 644 us
  waiting for transfers between devices  211 us (32%)
  Pallas kernels  116 us (18%)
  starting transfers between devices  108 us (17%)
  blocking collectives  91.4 us (14%)
  local copies, waits for them, and re-layouts  62.3 us (10%)
  matrix products  30.6 us (5%)
  between operations  16.5 us (3%)
  other arithmetic  7.98 us (1%)
    ppermute x70, waiting for transfers between devices, swap(): return lax.ppermute(values, axis, PAIR)  143 us
    all_to_all x7, blocking collectives, trade(): return lax.all_to_all(blocks, axes, 0, 0, tiled=True)  91.4 us
    pallas_call x19, Pallas kernels, call(): pl.pallas_call(kernel, grid=grid, in_specs=in_specs, out_specs=out_specs,...  73.3 us
    ppermute x70, starting transfers between devices, swap(): return lax.ppermute(values, axis, PAIR)  73.1 us
    pallas_call x12, Pallas kernels, call(): pl.pallas_call(kernel, grid_spec=spec, **options)  43 us
    unnamed x154, local copies, waits for them, and re-layouts  39.9 us
    all_to_all x6, waiting for transfers between devices, trade(): return lax.all_to_all(blocks, axes, 0, 0, tiled=True)  39.8 us
    dot_general x6, matrix products, dot(): return lax.dot_general(a, b, (dims, ((), ())), preferred_element_type=F32)  30.6 us
  transfers between devices with their start and end apart: 89, of which 50 were waited for; matrix products, arithmetic and copies ran while one was open for 10% of the time, Pallas kernels for 17%

profile of v26, /device:TPU:0, one launch (start us, length us, event | category | flops | bytes accessed | tf_op | source)
XLA Modules:
  0.0 644.2 jit_solution(13116335943075308052)
XLA Ops:
  34.6 8.8 %collective-permute-done.1.refs_2_ = bf16[128,2048]{1,0:T(8,128)(2,1)S(1)} collective-permute-done((bf16[128,2048]{1,0:T(8,128)(2,1)S(1)}, bf16[128,2048]{1,0:T(8,128)(2,1)S(1)}, u32[]{:S(2)}, u32[]{:S(2)}) %collective-permute-start.1) | collective-permute-done | bytes 524320 | tf_op jit(solution)/shard_map/ppermute | solution.py:46
  54.9 10.2 %all_to_all.65 = bf16[4,64,1024]{2,1,0:T(8,128)(2,1)} all-to-all(bf16[4,64,1024]{2,1,0:T(8,128)(2,1)S(1)} %copy.75), channel_id=1, replica_groups=mesh['z'=4,'x'=2,'c'=2,'y'=2] {'x','y'}, dimensions={0} | all-to-all | bytes 1048576 | tf_op jit(solution)/shard_map/all_to_all | solution.py:50
  65.2 15.5 %all_to_all.66 = bf16[4,64,2048]{2,1,0:T(8,128)(2,1)} all-to-all(bf16[4,64,2048]{2,1,0:T(8,128)(2,1)} %bitcast.88), channel_id=1, replica_groups=mesh['z'=4,'x'=2,'c'=2,'y'=2] {'x','y'}, dimensions={0} | all-to-all | bytes 2097152 | tf_op jit(solution)/shard_map/all_to_all | solution.py:50
  83.4 16.9 %all_to_all.67 = bf16[8,64,1024]{2,1,0:T(8,128)(2,1)S(1)} all-to-all(bf16[8,64,1024]{2,1,0:T(8,128)(2,1)S(1)} %get-tuple-element.159), channel_id=1, replica_groups=mesh['z'=4,'x'=2,'c'=2,'y'=2] {'x','c','y'}, dimensions={0} | all-to-all | bytes 2097152 | tf_op jit(solution)/shard_map/all_to_all | solution.py:50
  100.4 11.9 %all_to_all.68 = bf16[4,16,1024]{2,1,0:T(8,128)(2,1)S(1)} all-to-all(bf16[4,16,1024]{2,1,0:T(8,128)(2,1)S(1)} %bitcast.98), channel_id=1, replica_groups=mesh['z'=4,'x'=2,'c'=2,'y'=2] {'z'}, dimensions={0} | all-to-all | bytes 262144 | tf_op jit(solution)/shard_map/all_to_all | solution.py:50
  112.3 8.5 %all_to_all.69 = bf16[4,16,1024]{2,1,0:T(8,128)(2,1)S(1)} all-to-all(bf16[4,16,1024]{2,1,0:T(8,128)(2,1)S(1)} %broadcast_in_dim.12), channel_id=1, replica_groups=mesh['z'=4,'x'=2,'c'=2,'y'=2] {'z'}, dimensions={0} | all-to-all | bytes 262144 | tf_op jit(solution)/shard_map/all_to_all | solution.py:50
  127.2 7.9 %qkv_mm.1 = (bf16[512,2048]{1,0:T(8,128)(2,1)}, bf16[512,1536]{1,0:T(8,128)(2,1)S(1)}) custom-call(bf16[128,2048]{1,0:T(8,128)(2,1)S(1)} %copy-done.52, bf16[128,2048]{1,0:T(8,128)(2,1)S(1)} %copy-done.46, bf16[128,2048]{1,0:T(8,128)(2,1)S(1)} %collective-permute-done.1.refs_2_, bf16[64,2048]{1,0:T(8,128)(2,1)S(1)} %copy-done.56, ...), custom_call_target="tpu_custom_call" | custom-call | flops 3221225472 | bytes 10485760 | tf_op jit(solution)/shard_map/qkv_mm/pallas_call | solution.py:118
  138.2 18.2 %all_to_all.70 = bf16[4,64,2048]{2,1,0:T(8,128)(2,1)} all-to-all(bf16[4,64,2048]{2,1,0:T(8,128)(2,1)S(1)} %bitcast.87), channel_id=1, replica_groups=mesh['z'=4,'x'=2,'c'=2,'y'=2] {'x','y'}, dimensions={0} | all-to-all | bytes 2097152 | tf_op jit(solution)/shard_map/all_to_all | solution.py:50
  170.5 9.9 %collective-permute-done.11.refs_3_ = bf16[128,2048]{1,0:T(8,128)(2,1)S(1)} collective-permute-done((bf16[128,2048]{1,0:T(8,128)(2,1)S(1)}, bf16[128,2048]{1,0:T(8,128)(2,1)S(1)}, u32[]{:S(2)}, u32[]{:S(2)}) %collective-permute-start.11) | collective-permute-done | bytes 524320 | tf_op jit(solution)/shard_map/ppermute | solution.py:46
  184.9 9.3 %collective-permute-done.13.refs_2_ = bf16[128,2048]{1,0:T(8,128)(2,1)S(1)} collective-permute-done((bf16[128,2048]{1,0:T(8,128)(2,1)S(1)}, bf16[128,2048]{1,0:T(8,128)(2,1)S(1)}, u32[]{:S(2)}, u32[]{:S(2)}) %collective-permute-start.13) | collective-permute-done | bytes 524320 | tf_op jit(solution)/shard_map/ppermute | solution.py:46
  225.7 7.0 %collective-permute-done.19.refs_3_ = bf16[128,2048]{1,0:T(8,128)(2,1)S(1)} collective-permute-done((bf16[128,2048]{1,0:T(8,128)(2,1)S(1)}, bf16[128,2048]{1,0:T(8,128)(2,1)S(1)}, u32[]{:S(2)}, u32[]{:S(2)}) %collective-permute-start.19) | collective-permute-done | bytes 524320 | tf_op jit(solution)/shard_map/ppermute | solution.py:46
  270.9 11.9 %feed_up.1 = (bf16[512,2048]{1,0:T(8,128)(2,1)}, bf16[512,2048]{1,0:T(8,128)(2,1)}, f32[512,2048]{1,0:T(8,128)}) custom-call(bf16[128,2048]{1,0:T(8,128)(2,1)S(1)} %copy-done.54, bf16[128,2048]{1,0:T(8,128)(2,1)S(1)} %copy-done.50, bf16[128,2048]{1,0:T(8,128)(2,1)S(1)} %copy-done.48, bf16[64,2048]{1,0:T(8,128)(2,1)S(1)} %copy-done.60, ...), custom_call_target="tpu_custom_call" | custom-call | flops 4294967296 | bytes 12582912 | tf_op jit(solution)/shard_map/feed_up/pallas_call | solution.py:118
  302.3 8.8 %down_grads.1 = bf16[1024,2048]{1,0:T(8,128)(2,1)} custom-call(s32[1]{0:T(128)} %bitcast.24.r, bf16[512,2048]{1,0:T(8,128)(2,1)S(1)} %constant_dynamic-update-slice_fusion.refs_0_.dy, bf16[512,2048]{1,0:T(8,128)(2,1)S(1)} %collective-permute-done.28.refs_1_, bf16[512,2048]{1,0:T(8,128)(2,1)} %get-tuple-element.204.refs_2_, bf16[512,2048]{1,0:T(8,128)(2,1)} %copy-done.74), custom_call_target="tpu_custom_call" | custom-call | flops 4294967296 | bytes 16777216 | tf_op jit(solution)/shard_map/down_grads/pallas_call | solution.py:129
  312.7 12.7 %all-gather.11.cloned.1.call-done.down = bf16[2048,2048]{1,0:T(8,128)(2,1)} async-done(((bf16[256,2048]{1,0:T(8,128)(2,1)}), bf16[2048,2048]{1,0:T(8,128)(2,1)}) %all-gather.11.cloned.1.call-update) | async-done | bytes 8388624 | tf_op jit(solution)/shard_map/all_gather | solution.py:101
  326.9 9.9 %feed_down.1.refs_2_ = bf16[512,2048]{1,0:T(8,128)(2,1)S(1)} custom-call(bf16[512,2048]{1,0:T(8,128)(2,1)S(1)} %copy-done.14, f32[512,2048]{1,0:T(8,128)} %get-tuple-element.191.slope_ref, bf16[2048,2048]{1,0:T(8,128)(2,1)} %all-gather.11.cloned.1.call-done.down), custom_call_target="tpu_custom_call" | custom-call | flops 4294967296 | bytes 25165824 | tf_op jit(solution)/shard_map/feed_down/pallas_call | solution.py:118
  337.2 8.5 %convolution_convert_fusion.2 = bf16[512,2048]{1,0:T(8,128)(2,1)S(1)} fusion(bf16[512,2048]{1,0:T(8,128)(2,1)S(1)} %feed_down.1.refs_2_, bf16[2048,2048]{1,0:T(8,128)(2,1)} %all-gather.9.cloned.1.call-done.refs_5_), kind=kOutput, calls=%fused_computation.5 | convolution fusion | flops 4296015872 | bytes 12582912 | tf_op jit(solution)/shard_map/dot_general | solution.py:26
  358.2 10.9 %collective-permute-done.38.refs_2_ = bf16[128,2048]{1,0:T(8,128)(2,1)S(1)} collective-permute-done((bf16[128,2048]{1,0:T(8,128)(2,1)S(1)}, bf16[128,2048]{1,0:T(8,128)(2,1)S(1)}, u32[]{:S(2)}, u32[]{:S(2)}) %collective-permute-start.38) | collective-permute-done | bytes 524320 | tf_op jit(solution)/shard_map/ppermute | solution.py:46
  377.6 8.8 %up_grads.1 = bf16[1024,2048]{1,0:T(8,128)(2,1)} custom-call(s32[1]{0:T(128)} %bitcast.24.r, bf16[512,2048]{1,0:T(8,128)(2,1)} %get-tuple-element.195.refs_0_, bf16[512,2048]{1,0:T(8,128)(2,1)} %collective-permute-done.34.refs_1_, bf16[512,2048]{1,0:T(8,128)(2,1)} %copy-done.22, bf16[512,2048]{1,0:T(8,128)(2,1)} %copy-done.73), custom_call_target="tpu_custom_call" | custom-call | flops 4294967296 | bytes 16777216 | tf_op jit(solution)/shard_map/up_grads/pallas_call | solution.py:129
  417.6 10.4 %collective-permute-done.47.refs_2_ = bf16[128,2048]{1,0:T(8,128)(2,1)S(1)} collective-permute-done((bf16[128,2048]{1,0:T(8,128)(2,1)S(1)}, bf16[128,2048]{1,0:T(8,128)(2,1)S(1)}, u32[]{:S(2)}, u32[]{:S(2)}) %collective-permute-start.47) | collective-permute-done | bytes 524320 | tf_op jit(solution)/shard_map/ppermute | solution.py:46
  433.7 8.4 %convolution_convert_fusion = bf16[512,2048]{1,0:T(8,128)(2,1)S(1)} fusion(bf16[512,2048]{1,0:T(8,128)(2,1)S(1)} %copy-done.72, bf16[2048,2048]{1,0:T(8,128)(2,1)} %all-gather.11.cloned.1.call-done.down), kind=kOutput, calls=%fused_computation.3 | convolution fusion | flops 4296015872 | bytes 12582912 | tf_op jit(solution)/shard_map/dot_general | solution.py:26
  476.8 11.7 %attention_grads.1 = bf16[1024,3072]{1,0:T(8,128)(2,1)} custom-call(s32[1]{0:T(128)} %bitcast.24.r, bf16[512,2048]{1,0:T(8,128)(2,1)} %get-tuple-element.224.refs_0_, bf16[512,2048]{1,0:T(8,128)(2,1)} %collective-permute-done.30.refs_1_, bf16[512,2048]{1,0:T(8,128)(2,1)} %get-tuple-element.226.refs_2_, bf16[512,2048]{1,0:T(8,128)(2,1)} %collective-permute-done.56.refs_3_, ...), custom_call_target="tpu_custom_call" | custom-call | flops 6442450944 | bytes 25165824 | tf_op jit(solution)/shard_map/attention_grads/pallas_call | solution.py:129
  528.3 7.4 %all-to-all-done.8.block = bf16[8,64,1024]{2,1,0:T(8,128)(2,1)} async-done(((bf16[8,64,1024]{2,1,0:T(8,128)(2,1)}), bf16[8,64,1024]{2,1,0:T(8,128)(2,1)}, u32[]{:S(2)}, u32[]{:S(2)}) %all-to-all-start.8) | async-done | bytes 1048608 | tf_op jit(solution)/shard_map/all_to_all | solution.py:50
  549.2 13.8 %all-to-all-done.9 = bf16[8,80,1024]{2,1,0:T(8,128)(2,1)} async-done(((bf16[8,80,1024]{2,1,0:T(8,128)(2,1)}), bf16[8,80,1024]{2,1,0:T(8,128)(2,1)}, u32[]{:S(2)}, u32[]{:S(2)}) %all-to-all-start.9) | async-done | bytes 1310752 | tf_op jit(solution)/shard_map/all_to_all | solution.py:50
  568.4 10.3 %all_to_all.71 = bf16[4,16,1024]{2,1,0:T(8,128)(2,1)S(1)} all-to-all(bf16[4,16,1024]{2,1,0:T(8,128)(2,1)S(1)} %bitcast.99), channel_id=1, replica_groups=mesh['z'=4,'x'=2,'c'=2,'y'=2] {'z'}, dimensions={0} | all-to-all | bytes 262144 | tf_op jit(solution)/shard_map/all_to_all | solution.py:50
  (446 shorter events, 370.1 us)
Async XLA Ops:
  7.2 116.0 %all-gather.5.cloned.1.call-start = ((), (), s32[]{:S(2)}) async-start(), calls=%async_computation.16 | async-start | bytes 9437184 | tf_op jit(solution)/shard_map/all_gather | solution.py:101
  27.5 170.0 %all-gather.7.cloned.1.call-start = ((), (), s32[]{:S(2)}) async-start(), calls=%async_computation.17 | async-start | bytes 4718592 | tf_op jit(solution)/shard_map/all_gather | solution.py:101
  65.2 200.7 %all-gather.9.cloned.1.call-start = ((), (), s32[]{:S(2)}) async-start(), calls=%async_computation.18 | async-start | bytes 9437184 | tf_op jit(solution)/shard_map/all_gather | solution.py:101
  80.7 244.6 %all-gather.11.cloned.1.call-start = ((), (), s32[]{:S(2)}) async-start(), calls=%async_computation.19 | async-start | bytes 9437184 | tf_op jit(solution)/shard_map/all_gather | solution.py:101
  156.4 246.5 %reduce-scatter.4.cloned.1.call-start = ((), (), s32[]{:S(2)}) async-start(), calls=%async_computation.20 | async-start | bytes 5242880 | tf_op jit(solution)/shard_map/reduce_scatter | solution.py:105
  263.8 22.4 %collective-permute-start.24 = (bf16[128,2048]{1,0:T(8,128)(2,1)}, bf16[128,2048]{1,0:T(8,128)(2,1)}, u32[]{:S(2)}, u32[]{:S(2)}) collective-permute-start(bf16[128,2048]{1,0:T(8,128)(2,1)} %get-tuple-element.186.refs_3_), channel_id=1, source_target_pairs={{0,1},{1,0},{2,3},{3,2},{4,5},{5,4},{6,7},{7,6},{8,9},{9,8},{10,11... | collective-permute-start | bytes 1572872 | tf_op jit(solution)/shard_map/ppermute | solution.py:46
  264.0 20.1 %collective-permute-start.25 = (bf16[128,2048]{1,0:T(8,128)(2,1)}, bf16[128,2048]{1,0:T(8,128)(2,1)}, u32[]{:S(2)}, u32[]{:S(2)}) collective-permute-start(bf16[128,2048]{1,0:T(8,128)(2,1)} %get-tuple-element.186.refs_3_), channel_id=1, source_target_pairs={{0,4},{4,0},{1,5},{5,1},{2,6},{6,2},{3,7},{7,3},{8,12},{12,8},{9,1... | collective-permute-start | bytes 1572872 | tf_op jit(solution)/shard_map/ppermute | solution.py:46
  295.8 16.6 %collective-permute-start.30 = (bf16[512,2048]{1,0:T(8,128)(2,1)}, bf16[512,2048]{1,0:T(8,128)(2,1)}, u32[]{:S(2)}, u32[]{:S(2)}) collective-permute-start(bf16[512,2048]{1,0:T(8,128)(2,1)} %get-tuple-element.224.refs_0_), channel_id=1, source_target_pairs={{0,2},{2,0},{1,3},{3,1},{4,6},{6,4},{5,7},{7,5},{8,10},{10,8},{9,1... | collective-permute-start | bytes 6291464 | tf_op jit(solution)/shard_map/ppermute | solution.py:46
  296.3 16.1 %collective-permute-start.32 = (bf16[512,2048]{1,0:T(8,128)(2,1)}, bf16[512,2048]{1,0:T(8,128)(2,1)}, u32[]{:S(2)}, u32[]{:S(2)}) collective-permute-start(bf16[512,2048]{1,0:T(8,128)(2,1)} %get-tuple-element.227.refs_4_), channel_id=1, source_target_pairs={{0,2},{2,0},{1,3},{3,1},{4,6},{6,4},{5,7},{7,5},{8,10},{10,8},{9,1... | collective-permute-start | bytes 6291464 | tf_op jit(solution)/shard_map/ppermute | solution.py:46
  296.4 16.0 %collective-permute-start.34 = (bf16[512,2048]{1,0:T(8,128)(2,1)}, bf16[512,2048]{1,0:T(8,128)(2,1)}, u32[]{:S(2)}, u32[]{:S(2)}) collective-permute-start(bf16[512,2048]{1,0:T(8,128)(2,1)} %get-tuple-element.195.refs_0_), channel_id=1, source_target_pairs={{0,2},{2,0},{1,3},{3,1},{4,6},{6,4},{5,7},{7,5},{8,10},{10,8},{9,1... | collective-permute-start | bytes 6291464 | tf_op jit(solution)/shard_map/ppermute | solution.py:46
  312.4 176.1 %reduce-scatter.6.cloned.1.call-start = ((), (), s32[]{:S(2)}) async-start(), calls=%async_computation.21 | async-start | bytes 5242880 | tf_op jit(solution)/shard_map/reduce_scatter | solution.py:105
  336.9 39.5 %collective-permute-start.41 = (bf16[512,2048]{1,0:T(8,128)(2,1)S(1)}, bf16[512,2048]{1,0:T(8,128)(2,1)S(1)}, u32[]{:S(2)}, u32[]{:S(2)}) collective-permute-start(bf16[512,2048]{1,0:T(8,128)(2,1)S(1)} %feed_down.1.refs_2_), channel_id=1, source_target_pairs={{0,2},{2,0},{1,3},{3,1},{4,6},{6,4},{5,7},{7,5},{8,10},{10,8},{9,1... | collective-permute-start | bytes 6291464 | tf_op jit(solution)/shard_map/ppermute | solution.py:46
  455.5 20.2 %collective-permute-start.57 = (bf16[512,2048]{1,0:T(8,128)(2,1)}, bf16[512,2048]{1,0:T(8,128)(2,1)}, u32[]{:S(2)}, u32[]{:S(2)}) collective-permute-start(bf16[512,2048]{1,0:T(8,128)(2,1)} %get-tuple-element.229.refs_6_), channel_id=1, source_target_pairs={{0,2},{2,0},{1,3},{3,1},{4,6},{6,4},{5,7},{7,5},{8,10},{10,8},{9,1... | collective-permute-start | bytes 6291464 | tf_op jit(solution)/shard_map/ppermute | solution.py:46
  467.3 21.2 %collective-permute-start.54 = (bf16[128,2048]{1,0:T(8,128)(2,1)}, bf16[128,2048]{1,0:T(8,128)(2,1)}, u32[]{:S(2)}, u32[]{:S(2)}) collective-permute-start(bf16[128,2048]{1,0:T(8,128)(2,1)} %get-tuple-element.221), channel_id=1, source_target_pairs={{0,4},{4,0},{1,5},{5,1},{2,6},{6,2},{3,7},{7,3},{8,12},{12,8},{9,1... | collective-permute-start | bytes 1572872 | tf_op jit(solution)/shard_map/ppermute | solution.py:46
  468.8 19.7 %all-to-all-start.6 = ((bf16[8,16,1024]{2,1,0:T(8,128)(2,1)}), bf16[8,16,1024]{2,1,0:T(8,128)(2,1)S(1)}, u32[]{:S(2)}, u32[]{:S(2)}) async-start(bf16[8,16,1024]{2,1,0:T(8,128)(2,1)} %bitcast.29), calls=%async_computation.7 | async-start | bytes 524288 | tf_op jit(solution)/shard_map/all_to_all | solution.py:50
  472.9 136.3 %reduce-scatter.8.cloned.1.call-start = ((), (), s32[]{:S(2)}) async-start(), calls=%async_computation.22 | async-start | bytes 7864320 | tf_op jit(solution)/shard_map/reduce_scatter | solution.py:105
  499.6 16.2 %all-to-all-start.7 = ((bf16[4,16,1024]{2,1,0:T(8,128)(2,1)}), bf16[4,16,1024]{2,1,0:T(8,128)(2,1)S(1)}, u32[]{:S(2)}, u32[]{:S(2)}) async-start(bf16[4,16,1024]{2,1,0:T(8,128)(2,1)} %broadcast_in_dim.13), calls=%async_computation.8 | async-start | bytes 262144 | tf_op jit(solution)/shard_map/all_to_all | solution.py:50
  516.9 18.8 %all-to-all-start.8 = ((bf16[8,64,1024]{2,1,0:T(8,128)(2,1)}), bf16[8,64,1024]{2,1,0:T(8,128)(2,1)}, u32[]{:S(2)}, u32[]{:S(2)}) async-start(bf16[8,64,1024]{2,1,0:T(8,128)(2,1)} %broadcast_in_dim.15), calls=%async_computation.9 | async-start | bytes 2097152 | tf_op jit(solution)/shard_map/all_to_all | solution.py:50
  541.3 21.8 %all-to-all-start.9 = ((bf16[8,80,1024]{2,1,0:T(8,128)(2,1)}), bf16[8,80,1024]{2,1,0:T(8,128)(2,1)}, u32[]{:S(2)}, u32[]{:S(2)}) async-start(bf16[8,80,1024]{2,1,0:T(8,128)(2,1)} %copy-done.24), calls=%async_computation.10 | async-start | bytes 2621440 | tf_op jit(solution)/shard_map/all_to_all | solution.py:50
  579.0 17.4 %collective-permute-start.67 = (bf16[64,2048]{1,0:T(8,128)(2,1)S(1)}, bf16[64,2048]{1,0:T(8,128)(2,1)S(1)}, u32[]{:S(2)}, u32[]{:S(2)}) collective-permute-start(bf16[64,2048]{1,0:T(8,128)(2,1)S(1)} %get-tuple-element.262), channel_id=1, source_target_pairs={{0,1},{1,0},{2,3},{3,2},{4,5},{5,4},{6,7},{7,6},{8,9},{9,8},{10,11... | collective-permute-start | bytes 786440 | tf_op jit(solution)/shard_map/ppermute | solution.py:46
  609.3 17.2 %collective-permute-start.70 = (bf16[4,64,1024]{2,1,0:T(8,128)(2,1)S(1)}, bf16[4,64,1024]{2,1,0:T(8,128)(2,1)S(1)}, u32[]{:S(2)}, u32[]{:S(2)}) collective-permute-start(bf16[4,64,1024]{2,1,0:T(8,128)(2,1)S(1)} %all-to-all-done.12.own_ref), channel_id=1, source_target_pairs={{0,2},{2,0},{1,3},{3,1},{4,6},{6,4},{5,7},{7,5},{8,10},{10,8},{9,1... | collective-permute-start | bytes 1572872 | tf_op jit(solution)/shard_map/ppermute | solution.py:46
  611.9 17.5 %collective-permute-start.71 = (bf16[64,3072]{1,0:T(8,128)(2,1)}, bf16[64,3072]{1,0:T(8,128)(2,1)S(1)}, u32[]{:S(2)}, u32[]{:S(2)}) collective-permute-start(bf16[64,3072]{1,0:T(8,128)(2,1)} %get-tuple-element.278), channel_id=1, source_target_pairs={{0,1},{1,0},{2,3},{3,2},{4,5},{5,4},{6,7},{7,6},{8,9},{9,8},{10,11... | collective-permute-start | bytes 1179656 | tf_op jit(solution)/shard_map/ppermute | solution.py:46
  613.4 16.0 %collective-permute-start.72 = (bf16[64,3072]{1,0:T(8,128)(2,1)}, bf16[64,3072]{1,0:T(8,128)(2,1)S(1)}, u32[]{:S(2)}, u32[]{:S(2)}) collective-permute-start(bf16[64,3072]{1,0:T(8,128)(2,1)} %get-tuple-element.279), channel_id=1, source_target_pairs={{0,4},{4,0},{1,5},{5,1},{2,6},{6,2},{3,7},{7,3},{8,12},{12,8},{9,1... | collective-permute-start | bytes 1179656 | tf_op jit(solution)/shard_map/ppermute | solution.py:46
  613.9 19.5 %collective-permute-start.73 = (bf16[64,3072]{1,0:T(8,128)(2,1)}, bf16[64,3072]{1,0:T(8,128)(2,1)}, u32[]{:S(2)}, u32[]{:S(2)}) collective-permute-start(bf16[64,3072]{1,0:T(8,128)(2,1)} %get-tuple-element.280), channel_id=1, source_target_pairs={{0,5},{1,4},{4,1},{5,0},{2,7},{3,6},{6,3},{7,2},{8,13},{9,12},{12,... | collective-permute-start | bytes 1179656 | tf_op jit(solution)/shard_map/ppermute | solution.py:96
  (140 other events, 1566.2 us)
Sparse Core Ops, SparseCore 0:
  27.6 83.6 all-gather.4
  112.9 47.9 all-gather.6
  162.5 80.7 all-gather.8
  244.7 80.5 all-gather.10
  327.5 75.2 reduce-scatter.3
  405.1 80.0 reduce-scatter.5
  488.7 117.6 reduce-scatter.7

commit v27 on v26

--- a/solution.py
+++ b/solution.py
@@ -572,29 +572,25 @@
     )
 
 
-def pick_weights(three, one, rank):
-    rows, width = one.shape[0], one.shape[1] // 4
-
-    def kernel(r, three_ref, one_ref, *outs):
+def pick_weights(three, rank):
+    rows, width = three.shape[1], three.shape[2] // 4
+
+    def kernel(r, three_ref, *outs):
         for k in range(4):
 
             @pl.when(pl.program_id(0) == k)
             def _():
                 for j in range(3):
                     outs[k][:, j * width : (j + 1) * width] = three_ref[j]
-                outs[k][:, 3 * width :] = one_ref[...]
-
-    outs = [shape((rows, 4 * width))] * 4
+
+    outs = [shape((rows, 3 * width))] * 4
     return call(
         kernel,
         (4,),
-        [
-            pl.BlockSpec((3, rows, width), lambda k, r: (0, 0, k ^ r[0])),
-            pl.BlockSpec((rows, width), lambda k, r: (0, k ^ r[0])),
-        ],
+        [pl.BlockSpec((3, rows, width), lambda k, r: (0, 0, k ^ r[0]))],
         [whole(a) for a in outs],
         outs,
-        [three, one],
+        [three],
         "pick_weights",
         rank=rank,
     )
@@ -870,7 +866,7 @@
             return values if inside else layer_order(values)
 
         w_qkv, w_cross = w_qkv.transpose(1, 0, 2), w_cross.transpose(1, 0, 2)
-        first = swap_parts(pick_weights(w_qkv, w_out, rank))
+        first = swap_parts(pick_weights(w_qkv, rank))
         first = gather_rows(place(first, rank))
 
         positions = lax.axis_index("y") * local_rows + jnp.arange(local_rows, dtype=jnp.int32)
@@ -891,7 +887,8 @@
             order,
         )
         attn_in = gather_tokens(attn_in)
-        mid = jnp.concatenate([column_blocks(w_cross[0], 4), column_blocks(w_cross_out, 4)], axis=2)
+        mid = [column_blocks(weight, 4) for weight in (w_out, w_cross[0], w_cross_out)]
+        mid = jnp.concatenate(mid, axis=2)
         up = column_blocks(w_up, 4)
         attn_in, mid, up = lax.optimization_barrier((attn_in, mid, up))
         mid, up = gather_rows(trade(mid)), gather_rows(trade(up))
@@ -910,12 +907,14 @@
         down = column_blocks(w_down, 4)
         self_mixed, down = lax.optimization_barrier((self_mixed, down))
         down = gather_rows(trade(down))
-        parts = mm_scatter(self_mixed, first[:, 3 * group :])
+        parts = mm_scatter(self_mixed, mid[:, :group])
         after_attn, cross_in = add_norm([start_x] + parts, gain_b)
 
-        cross_in, cross_queries = gather_mm(gather_tokens(cross_in), mid, 0, group, "query_mm")
+        cross_in, cross_queries = gather_mm(
+            gather_tokens(cross_in), mid, group, group, "query_mm"
+        )
         cross_mixed = cross_forward(cross_queries, text_kv)
-        parts = mm_scatter(cross_mixed, mid[:, group:])
+        parts = mm_scatter(cross_mixed, mid[:, 2 * group :])
         after_cross, mlp_in = add_norm([after_attn] + parts, gain_c)
 
         mlp_in = gather_tokens(mlp_in)
@@ -949,13 +948,13 @@
 
         cross_branch, up_part = gather_beside(cross_branch, up_part)
         cross_branch, grad_cross_mixed = gather_mm(
-            cross_branch, mid, group, group, "cross_out_back"
+            cross_branch, mid, 2 * group, group, "cross_out_back"
         )
         grad_cq, kv_grad = cross_back(cross_queries, text_kv, grad_cross_mixed)
         up_part, down_rows, kv_grad = lax.optimization_barrier((up_part, down_rows, kv_grad))
         up_rows = scatter_grad(up_part, grad_axes)
         cross_branch, grad_cq_both = both(cross_branch), both(grad_cq)
-        parts = mm_scatter(grad_cq, mid[:, :group])
+        parts = mm_scatter(grad_cq, mid[:, group : 2 * group])
         grad_after_attn, attn_branch, gain_grad_b = norm_back(
             parts, grad_after_cross, after_attn, gain_b
         )
@@ -965,7 +964,7 @@
         attn_branch, result = gather_beside(attn_branch, result)
         attn_branch, result = lax.optimization_barrier((attn_branch, result))
         result = scatter_first(token_blocks(result))
-        attn_branch, grad_self_mixed = gather_mm(attn_branch, first, 3 * group, group, "out_back")
+        attn_branch, grad_self_mixed = gather_mm(attn_branch, mid, 0, group, "out_back")
         grad_projected = self_back(projected, grad_self_mixed, 2 * images)
         kv_part = kv_grad.astype(BF).reshape(2, z_size, -1, 2 * group)
         kv_part = kv_part.transpose(1, 0, 2, 3).reshape(2 * z_size, -1, 2 * group)
@@ -989,7 +988,7 @@
         )
         rest_part, up_rows = lax.optimization_barrier((rest_part, up_rows))
         rest_rows = scatter_grad(rest_part, grad_axes)
-        parts = mm_scatter(grad_projected, first[:, : 3 * group])
+        parts = mm_scatter(grad_projected, first)
         grad_hidden, gain_grad_a, mask_grad = last_back(
             parts,
             grad_after_attn,

time: 652 us -> 651 us (level)
  local copies, waits for them, and re-layouts: 62.3 us -> 49.9 us
  blocking collectives: 91.4 us -> 102 us
    unnamed x154 -> x132, local copies, waits for them, and re-layouts: 39.9 us -> 26 us
    all_to_all x7, blocking collectives: 91.4 us -> 102 us  [trade(): return lax.all_to_all(blocks, axes, 0, 0, tiled=True)]
  transfers between devices with their start and end apart: 89 -> 89, of which waited for: 50 -> 47; matrix products, arithmetic and copies ran while one was open for 10% -> 11% of each run, Pallas kernels for 17% -> 17%
where the time goes in v27:
time: 651 us; the launch traced here: 644 us
  waiting for transfers between devices  208 us (32%)
  Pallas kernels  116 us (18%)
  starting transfers between devices  111 us (17%)
  blocking collectives  102 us (16%)
  local copies, waits for them, and re-layouts  49.9 us (8%)
  matrix products  32.5 us (5%)
  between operations  16.5 us (3%)
  other arithmetic  8.09 us (1%)
    ppermute x70, waiting for transfers between devices, swap(): return lax.ppermute(values, axis, PAIR)  146 us
    all_to_all x7, blocking collectives, trade(): return lax.all_to_all(blocks, axes, 0, 0, tiled=True)  102 us
    ppermute x70, starting transfers between devices, swap(): return lax.ppermute(values, axis, PAIR)  75.9 us
    pallas_call x19, Pallas kernels, call(): pl.pallas_call(kernel, grid=grid, in_specs=in_specs, out_specs=out_specs,...  73 us
    pallas_call x12, Pallas kernels, call(): pl.pallas_call(kernel, grid_spec=spec, **options)  42.7 us
    all_to_all x6, waiting for transfers between devices, trade(): return lax.all_to_all(blocks, axes, 0, 0, tiled=True)  39.7 us
    dot_general x6, matrix products, dot(): return lax.dot_general(a, b, (dims, ((), ())), preferred_element_type=F32)  32.5 us
    all_to_all x6, starting transfers between devices, trade(): return lax.all_to_all(blocks, axes, 0, 0, tiled=True)  26 us
  transfers between devices with their start and end apart: 89, of which 47 were waited for; matrix products, arithmetic and copies ran while one was open for 11% of the time, Pallas kernels for 17%

profile of v27, /device:TPU:0, one launch (start us, length us, event | category | flops | bytes accessed | tf_op | source)
XLA Modules:
  0.0 643.6 jit_solution(996348082709259873)
XLA Ops:
  30.1 8.8 %collective-permute-done.1.refs_2_ = bf16[128,2048]{1,0:T(8,128)(2,1)S(1)} collective-permute-done((bf16[128,2048]{1,0:T(8,128)(2,1)S(1)}, bf16[128,2048]{1,0:T(8,128)(2,1)S(1)}, u32[]{:S(2)}, u32[]{:S(2)}) %collective-permute-start.1) | collective-permute-done | bytes 524320 | tf_op jit(solution)/shard_map/ppermute | solution.py:46
  52.4 12.2 %all_to_all.65 = bf16[4,64,1536]{2,1,0:T(8,128)(2,1)} all-to-all(bf16[4,64,1536]{2,1,0:T(8,128)(2,1)S(1)} %copy.75), channel_id=1, replica_groups=mesh['z'=4,'x'=2,'c'=2,'y'=2] {'x','y'}, dimensions={0} | all-to-all | bytes 1572864 | tf_op jit(solution)/shard_map/all_to_all | solution.py:50
  64.7 15.0 %all_to_all.66 = bf16[4,64,2048]{2,1,0:T(8,128)(2,1)} all-to-all(bf16[4,64,2048]{2,1,0:T(8,128)(2,1)} %bitcast.90), channel_id=1, replica_groups=mesh['z'=4,'x'=2,'c'=2,'y'=2] {'x','y'}, dimensions={0} | all-to-all | bytes 2097152 | tf_op jit(solution)/shard_map/all_to_all | solution.py:50
  82.3 16.9 %all_to_all.67 = bf16[8,64,1024]{2,1,0:T(8,128)(2,1)S(1)} all-to-all(bf16[8,64,1024]{2,1,0:T(8,128)(2,1)S(1)} %get-tuple-element.159), channel_id=1, replica_groups=mesh['z'=4,'x'=2,'c'=2,'y'=2] {'x','c','y'}, dimensions={0} | all-to-all | bytes 2097152 | tf_op jit(solution)/shard_map/all_to_all | solution.py:50
  99.4 15.9 %all_to_all.68 = bf16[4,16,1024]{2,1,0:T(8,128)(2,1)S(1)} all-to-all(bf16[4,16,1024]{2,1,0:T(8,128)(2,1)S(1)} %bitcast.101), channel_id=1, replica_groups=mesh['z'=4,'x'=2,'c'=2,'y'=2] {'z'}, dimensions={0} | all-to-all | bytes 262144 | tf_op jit(solution)/shard_map/all_to_all | solution.py:50
  115.4 12.9 %all_to_all.69 = bf16[4,16,1024]{2,1,0:T(8,128)(2,1)S(1)} all-to-all(bf16[4,16,1024]{2,1,0:T(8,128)(2,1)S(1)} %broadcast_in_dim.12), channel_id=1, replica_groups=mesh['z'=4,'x'=2,'c'=2,'y'=2] {'z'}, dimensions={0} | all-to-all | bytes 262144 | tf_op jit(solution)/shard_map/all_to_all | solution.py:50
  132.8 9.0 %qkv_mm.1 = (bf16[512,2048]{1,0:T(8,128)(2,1)}, bf16[512,1536]{1,0:T(8,128)(2,1)S(1)}) custom-call(bf16[128,2048]{1,0:T(8,128)(2,1)S(1)} %copy-done.45, bf16[128,2048]{1,0:T(8,128)(2,1)S(1)} %copy-done.39, bf16[128,2048]{1,0:T(8,128)(2,1)S(1)} %collective-permute-done.1.refs_2_, bf16[64,2048]{1,0:T(8,128)(2,1)} %collective-permute-done.2.refs_3_, ...), custom_call_target="tpu_custom_call" | custom-call | flops 3221225472 | bytes 10485760 | tf_op jit(solution)/shard_map/qkv_mm/pallas_call | solution.py:118
  144.7 18.2 %all_to_all.70 = bf16[4,64,2048]{2,1,0:T(8,128)(2,1)} all-to-all(bf16[4,64,2048]{2,1,0:T(8,128)(2,1)S(1)} %bitcast.89), channel_id=1, replica_groups=mesh['z'=4,'x'=2,'c'=2,'y'=2] {'x','y'}, dimensions={0} | all-to-all | bytes 2097152 | tf_op jit(solution)/shard_map/all_to_all | solution.py:50
  177.4 10.8 %collective-permute-done.11.refs_3_ = bf16[128,2048]{1,0:T(8,128)(2,1)S(1)} collective-permute-done((bf16[128,2048]{1,0:T(8,128)(2,1)S(1)}, bf16[128,2048]{1,0:T(8,128)(2,1)S(1)}, u32[]{:S(2)}, u32[]{:S(2)}) %collective-permute-start.11) | collective-permute-done | bytes 524320 | tf_op jit(solution)/shard_map/ppermute | solution.py:46
  191.9 9.5 %collective-permute-done.13.refs_2_ = bf16[128,2048]{1,0:T(8,128)(2,1)S(1)} collective-permute-done((bf16[128,2048]{1,0:T(8,128)(2,1)S(1)}, bf16[128,2048]{1,0:T(8,128)(2,1)S(1)}, u32[]{:S(2)}, u32[]{:S(2)}) %collective-permute-start.13) | collective-permute-done | bytes 524320 | tf_op jit(solution)/shard_map/ppermute | solution.py:46
  229.2 7.9 %collective-permute-done.19.refs_3_ = bf16[128,2048]{1,0:T(8,128)(2,1)S(1)} collective-permute-done((bf16[128,2048]{1,0:T(8,128)(2,1)S(1)}, bf16[128,2048]{1,0:T(8,128)(2,1)S(1)}, u32[]{:S(2)}, u32[]{:S(2)}) %collective-permute-start.19) | collective-permute-done | bytes 524320 | tf_op jit(solution)/shard_map/ppermute | solution.py:46
  266.4 8.8 %collective-permute-done.25 = bf16[128,2048]{1,0:T(8,128)(2,1)S(1)} collective-permute-done((bf16[128,2048]{1,0:T(8,128)(2,1)S(1)}, bf16[128,2048]{1,0:T(8,128)(2,1)S(1)}, u32[]{:S(2)}, u32[]{:S(2)}) %collective-permute-start.25) | collective-permute-done | bytes 524320 | tf_op jit(solution)/shard_map/ppermute | solution.py:46
  285.8 11.9 %feed_up.1 = (bf16[512,2048]{1,0:T(8,128)(2,1)}, bf16[512,2048]{1,0:T(8,128)(2,1)}, f32[512,2048]{1,0:T(8,128)}) custom-call(bf16[128,2048]{1,0:T(8,128)(2,1)S(1)} %copy-done.47, bf16[128,2048]{1,0:T(8,128)(2,1)S(1)} %copy-done.43, bf16[128,2048]{1,0:T(8,128)(2,1)S(1)} %copy-done.41, bf16[64,2048]{1,0:T(8,128)(2,1)S(1)} %copy-done.49, ...), custom_call_target="tpu_custom_call" | custom-call | flops 4294967296 | bytes 12582912 | tf_op jit(solution)/shard_map/feed_up/pallas_call | solution.py:118
  308.8 8.6 %down_grads.1 = bf16[1024,2048]{1,0:T(8,128)(2,1)} custom-call(s32[1]{0:T(128)} %bitcast.25.r, bf16[512,2048]{1,0:T(8,128)(2,1)} %constant_dynamic-update-slice_fusion.refs_0_.dy, bf16[512,2048]{1,0:T(8,128)(2,1)S(1)} %collective-permute-done.28.refs_1_, bf16[512,2048]{1,0:T(8,128)(2,1)} %get-tuple-element.204.refs_2_, bf16[512,2048]{1,0:T(8,128)(2,1)} %copy-done.63), custom_call_target="tpu_custom_call" | custom-call | flops 4294967296 | bytes 16777216 | tf_op jit(solution)/shard_map/down_grads/pallas_call | solution.py:129
  324.8 10.7 %feed_down.1.refs_2_ = bf16[512,2048]{1,0:T(8,128)(2,1)S(1)} custom-call(bf16[512,2048]{1,0:T(8,128)(2,1)} %constant_dynamic-update-slice_fusion.refs_0_.dy, f32[512,2048]{1,0:T(8,128)} %get-tuple-element.191.slope_ref, bf16[2048,2048]{1,0:T(8,128)(2,1)} %all-gather.11.cloned.1.call-done.down), custom_call_target="tpu_custom_call" | custom-call | flops 4294967296 | bytes 25165824 | tf_op jit(solution)/shard_map/feed_down/pallas_call | solution.py:118
  335.8 8.6 %convolution_convert_fusion.3 = bf16[512,2048]{1,0:T(8,128)(2,1)S(1)} fusion(bf16[512,2048]{1,0:T(8,128)(2,1)S(1)} %feed_down.1.refs_2_, bf16[2048,2048]{1,0:T(8,128)(2,1)} %all-gather.9.cloned.1.call-done.refs_5_), kind=kOutput, calls=%fused_computation.3 | convolution fusion | flops 4296015872 | bytes 12582912 | tf_op jit(solution)/shard_map/dot_general | solution.py:26
  356.7 10.9 %collective-permute-done.38.refs_2_ = bf16[128,2048]{1,0:T(8,128)(2,1)S(1)} collective-permute-done((bf16[128,2048]{1,0:T(8,128)(2,1)S(1)}, bf16[128,2048]{1,0:T(8,128)(2,1)S(1)}, u32[]{:S(2)}, u32[]{:S(2)}) %collective-permute-start.38) | collective-permute-done | bytes 524320 | tf_op jit(solution)/shard_map/ppermute | solution.py:46
  374.7 8.7 %up_grads.1 = bf16[1024,2048]{1,0:T(8,128)(2,1)} custom-call(s32[1]{0:T(128)} %bitcast.25.r, bf16[512,2048]{1,0:T(8,128)(2,1)} %get-tuple-element.195.refs_0_, bf16[512,2048]{1,0:T(8,128)(2,1)} %collective-permute-done.34.refs_1_, bf16[512,2048]{1,0:T(8,128)(2,1)} %copy-done.22, bf16[512,2048]{1,0:T(8,128)(2,1)} %copy-done.62), custom_call_target="tpu_custom_call" | custom-call | flops 4294967296 | bytes 16777216 | tf_op jit(solution)/shard_map/up_grads/pallas_call | solution.py:129
  417.0 10.3 %collective-permute-done.47.refs_2_ = bf16[128,2048]{1,0:T(8,128)(2,1)S(1)} collective-permute-done((bf16[128,2048]{1,0:T(8,128)(2,1)S(1)}, bf16[128,2048]{1,0:T(8,128)(2,1)S(1)}, u32[]{:S(2)}, u32[]{:S(2)}) %collective-permute-start.47) | collective-permute-done | bytes 524320 | tf_op jit(solution)/shard_map/ppermute | solution.py:46
  433.1 8.5 %convolution_convert_fusion.1 = bf16[512,2048]{1,0:T(8,128)(2,1)S(1)} fusion(bf16[512,2048]{1,0:T(8,128)(2,1)S(1)} %copy-done.61, bf16[2048,2048]{1,0:T(8,128)(2,1)} %all-gather.11.cloned.1.call-done.down), kind=kOutput, calls=%fused_computation.1 | convolution fusion | flops 4296015872 | bytes 12582912 | tf_op jit(solution)/shard_map/dot_general | solution.py:26
  476.2 11.8 %attention_grads.1 = bf16[1024,3072]{1,0:T(8,128)(2,1)} custom-call(s32[1]{0:T(128)} %bitcast.25.r, bf16[512,2048]{1,0:T(8,128)(2,1)} %get-tuple-element.224.refs_0_, bf16[512,2048]{1,0:T(8,128)(2,1)} %collective-permute-done.30.refs_1_, bf16[512,2048]{1,0:T(8,128)(2,1)} %get-tuple-element.226.refs_2_, bf16[512,2048]{1,0:T(8,128)(2,1)} %collective-permute-done.56.refs_3_, ...), custom_call_target="tpu_custom_call" | custom-call | flops 6442450944 | bytes 25165824 | tf_op jit(solution)/shard_map/attention_grads/pallas_call | solution.py:129
  527.8 7.3 %all-to-all-done.8.block = bf16[8,64,1024]{2,1,0:T(8,128)(2,1)} async-done(((bf16[8,64,1024]{2,1,0:T(8,128)(2,1)}), bf16[8,64,1024]{2,1,0:T(8,128)(2,1)}, u32[]{:S(2)}, u32[]{:S(2)}) %all-to-all-start.8) | async-done | bytes 1048608 | tf_op jit(solution)/shard_map/all_to_all | solution.py:50
  548.7 13.8 %all-to-all-done.9 = bf16[8,80,1024]{2,1,0:T(8,128)(2,1)} async-done(((bf16[8,80,1024]{2,1,0:T(8,128)(2,1)}), bf16[8,80,1024]{2,1,0:T(8,128)(2,1)}, u32[]{:S(2)}, u32[]{:S(2)}) %all-to-all-start.9) | async-done | bytes 1310752 | tf_op jit(solution)/shard_map/all_to_all | solution.py:50
  567.8 10.4 %all_to_all.71 = bf16[4,16,1024]{2,1,0:T(8,128)(2,1)S(1)} all-to-all(bf16[4,16,1024]{2,1,0:T(8,128)(2,1)S(1)} %bitcast.102), channel_id=1, replica_groups=mesh['z'=4,'x'=2,'c'=2,'y'=2] {'z'}, dimensions={0} | all-to-all | bytes 262144 | tf_op jit(solution)/shard_map/all_to_all | solution.py:50
  (425 shorter events, 359.6 us)
Async XLA Ops:
  7.2 123.5 %all-gather.5.cloned.1.call-start = ((), (), s32[]{:S(2)}) async-start(), calls=%async_computation.16 | async-start | bytes 7077888 | tf_op jit(solution)/shard_map/all_gather | solution.py:101
  23.6 139.7 %all-gather.7.cloned.1.call-start = ((), (), s32[]{:S(2)}) async-start(), calls=%async_computation.17 | async-start | bytes 7077888 | tf_op jit(solution)/shard_map/all_gather | solution.py:101
  64.6 216.1 %all-gather.9.cloned.1.call-start = ((), (), s32[]{:S(2)}) async-start(), calls=%async_computation.18 | async-start | bytes 9437184 | tf_op jit(solution)/shard_map/all_gather | solution.py:101
  79.7 245.1 %all-gather.11.cloned.1.call-start = ((), (), s32[]{:S(2)}) async-start(), calls=%async_computation.19 | async-start | bytes 9437184 | tf_op jit(solution)/shard_map/all_gather | solution.py:101
  163.0 239.3 %reduce-scatter.4.cloned.1.call-start = ((), (), s32[]{:S(2)}) async-start(), calls=%async_computation.20 | async-start | bytes 5242880 | tf_op jit(solution)/shard_map/reduce_scatter | solution.py:105
  276.0 21.8 %collective-permute-start.26 = (bf16[64,2048]{1,0:T(8,128)(2,1)}, bf16[64,2048]{1,0:T(8,128)(2,1)}, u32[]{:S(2)}, u32[]{:S(2)}) collective-permute-start(bf16[64,2048]{1,0:T(8,128)(2,1)} %slice.347), channel_id=1, source_target_pairs={{0,1},{1,0},{2,3},{3,2},{4,5},{5,4},{6,7},{7,6},{8,9},{9,8},{10,11... | collective-permute-start | bytes 786440 | tf_op jit(solution)/shard_map/ppermute | solution.py:46
  277.8 21.7 %collective-permute-start.27 = (bf16[64,2048]{1,0:T(8,128)(2,1)}, bf16[64,2048]{1,0:T(8,128)(2,1)}, u32[]{:S(2)}, u32[]{:S(2)}) collective-permute-start(bf16[64,2048]{1,0:T(8,128)(2,1)} %slice.348), channel_id=1, source_target_pairs={{0,4},{4,0},{1,5},{5,1},{2,6},{6,2},{3,7},{7,3},{8,12},{12,8},{9,1... | collective-permute-start | bytes 786440 | tf_op jit(solution)/shard_map/ppermute | solution.py:46
  301.7 15.8 %collective-permute-start.30 = (bf16[512,2048]{1,0:T(8,128)(2,1)}, bf16[512,2048]{1,0:T(8,128)(2,1)}, u32[]{:S(2)}, u32[]{:S(2)}) collective-permute-start(bf16[512,2048]{1,0:T(8,128)(2,1)} %get-tuple-element.224.refs_0_), channel_id=1, source_target_pairs={{0,2},{2,0},{1,3},{3,1},{4,6},{6,4},{5,7},{7,5},{8,10},{10,8},{9,1... | collective-permute-start | bytes 6291464 | tf_op jit(solution)/shard_map/ppermute | solution.py:46
  317.5 170.5 %reduce-scatter.6.cloned.1.call-start = ((), (), s32[]{:S(2)}) async-start(), calls=%async_computation.21 | async-start | bytes 5242880 | tf_op jit(solution)/shard_map/reduce_scatter | solution.py:105
  335.5 37.9 %collective-permute-start.41 = (bf16[512,2048]{1,0:T(8,128)(2,1)S(1)}, bf16[512,2048]{1,0:T(8,128)(2,1)S(1)}, u32[]{:S(2)}, u32[]{:S(2)}) collective-permute-start(bf16[512,2048]{1,0:T(8,128)(2,1)S(1)} %feed_down.1.refs_2_), channel_id=1, source_target_pairs={{0,2},{2,0},{1,3},{3,1},{4,6},{6,4},{5,7},{7,5},{8,10},{10,8},{9,1... | collective-permute-start | bytes 6291464 | tf_op jit(solution)/shard_map/ppermute | solution.py:46
  454.6 20.5 %collective-permute-start.57 = (bf16[512,2048]{1,0:T(8,128)(2,1)}, bf16[512,2048]{1,0:T(8,128)(2,1)}, u32[]{:S(2)}, u32[]{:S(2)}) collective-permute-start(bf16[512,2048]{1,0:T(8,128)(2,1)} %get-tuple-element.229.refs_6_), channel_id=1, source_target_pairs={{0,2},{2,0},{1,3},{3,1},{4,6},{6,4},{5,7},{7,5},{8,10},{10,8},{9,1... | collective-permute-start | bytes 6291464 | tf_op jit(solution)/shard_map/ppermute | solution.py:46
  459.3 15.8 %collective-permute-start.56 = (bf16[512,2048]{1,0:T(8,128)(2,1)}, bf16[512,2048]{1,0:T(8,128)(2,1)}, u32[]{:S(2)}, u32[]{:S(2)}) collective-permute-start(bf16[512,2048]{1,0:T(8,128)(2,1)} %get-tuple-element.226.refs_2_), channel_id=1, source_target_pairs={{0,2},{2,0},{1,3},{3,1},{4,6},{6,4},{5,7},{7,5},{8,10},{10,8},{9,1... | collective-permute-start | bytes 6291464 | tf_op jit(solution)/shard_map/ppermute | solution.py:46
  466.4 21.6 %collective-permute-start.54 = (bf16[128,2048]{1,0:T(8,128)(2,1)}, bf16[128,2048]{1,0:T(8,128)(2,1)}, u32[]{:S(2)}, u32[]{:S(2)}) collective-permute-start(bf16[128,2048]{1,0:T(8,128)(2,1)} %get-tuple-element.221), channel_id=1, source_target_pairs={{0,4},{4,0},{1,5},{5,1},{2,6},{6,2},{3,7},{7,3},{8,12},{12,8},{9,1... | collective-permute-start | bytes 1572872 | tf_op jit(solution)/shard_map/ppermute | solution.py:46
  468.2 19.8 %all-to-all-start.6 = ((bf16[8,16,1024]{2,1,0:T(8,128)(2,1)}), bf16[8,16,1024]{2,1,0:T(8,128)(2,1)S(1)}, u32[]{:S(2)}, u32[]{:S(2)}) async-start(bf16[8,16,1024]{2,1,0:T(8,128)(2,1)} %bitcast.30), calls=%async_computation.7 | async-start | bytes 524288 | tf_op jit(solution)/shard_map/all_to_all | solution.py:50
  472.3 136.4 %reduce-scatter.8.cloned.1.call-start = ((), (), s32[]{:S(2)}) async-start(), calls=%async_computation.22 | async-start | bytes 7864320 | tf_op jit(solution)/shard_map/reduce_scatter | solution.py:105
  499.0 16.2 %all-to-all-start.7 = ((bf16[4,16,1024]{2,1,0:T(8,128)(2,1)}), bf16[4,16,1024]{2,1,0:T(8,128)(2,1)S(1)}, u32[]{:S(2)}, u32[]{:S(2)}) async-start(bf16[4,16,1024]{2,1,0:T(8,128)(2,1)} %broadcast_in_dim.13), calls=%async_computation.8 | async-start | bytes 262144 | tf_op jit(solution)/shard_map/all_to_all | solution.py:50
  516.3 18.8 %all-to-all-start.8 = ((bf16[8,64,1024]{2,1,0:T(8,128)(2,1)}), bf16[8,64,1024]{2,1,0:T(8,128)(2,1)}, u32[]{:S(2)}, u32[]{:S(2)}) async-start(bf16[8,64,1024]{2,1,0:T(8,128)(2,1)} %broadcast_in_dim.15), calls=%async_computation.9 | async-start | bytes 2097152 | tf_op jit(solution)/shard_map/all_to_all | solution.py:50
  540.7 21.8 %all-to-all-start.9 = ((bf16[8,80,1024]{2,1,0:T(8,128)(2,1)}), bf16[8,80,1024]{2,1,0:T(8,128)(2,1)}, u32[]{:S(2)}, u32[]{:S(2)}) async-start(bf16[8,80,1024]{2,1,0:T(8,128)(2,1)} %copy-done.24), calls=%async_computation.10 | async-start | bytes 2621440 | tf_op jit(solution)/shard_map/all_to_all | solution.py:50
  578.5 17.4 %collective-permute-start.67 = (bf16[64,2048]{1,0:T(8,128)(2,1)S(1)}, bf16[64,2048]{1,0:T(8,128)(2,1)S(1)}, u32[]{:S(2)}, u32[]{:S(2)}) collective-permute-start(bf16[64,2048]{1,0:T(8,128)(2,1)S(1)} %get-tuple-element.262), channel_id=1, source_target_pairs={{0,1},{1,0},{2,3},{3,2},{4,5},{5,4},{6,7},{7,6},{8,9},{9,8},{10,11... | collective-permute-start | bytes 786440 | tf_op jit(solution)/shard_map/ppermute | solution.py:46
  579.9 16.0 %collective-permute-start.68 = (bf16[64,2048]{1,0:T(8,128)(2,1)S(1)}, bf16[64,2048]{1,0:T(8,128)(2,1)S(1)}, u32[]{:S(2)}, u32[]{:S(2)}) collective-permute-start(bf16[64,2048]{1,0:T(8,128)(2,1)S(1)} %get-tuple-element.263), channel_id=1, source_target_pairs={{0,4},{4,0},{1,5},{5,1},{2,6},{6,2},{3,7},{7,3},{8,12},{12,8},{9,1... | collective-permute-start | bytes 786440 | tf_op jit(solution)/shard_map/ppermute | solution.py:46
  608.7 17.2 %collective-permute-start.70 = (bf16[4,64,1024]{2,1,0:T(8,128)(2,1)S(1)}, bf16[4,64,1024]{2,1,0:T(8,128)(2,1)S(1)}, u32[]{:S(2)}, u32[]{:S(2)}) collective-permute-start(bf16[4,64,1024]{2,1,0:T(8,128)(2,1)S(1)} %all-to-all-done.12.own_ref), channel_id=1, source_target_pairs={{0,2},{2,0},{1,3},{3,1},{4,6},{6,4},{5,7},{7,5},{8,10},{10,8},{9,1... | collective-permute-start | bytes 1572872 | tf_op jit(solution)/shard_map/ppermute | solution.py:46
  611.3 17.5 %collective-permute-start.71 = (bf16[64,3072]{1,0:T(8,128)(2,1)}, bf16[64,3072]{1,0:T(8,128)(2,1)S(1)}, u32[]{:S(2)}, u32[]{:S(2)}) collective-permute-start(bf16[64,3072]{1,0:T(8,128)(2,1)} %get-tuple-element.278), channel_id=1, source_target_pairs={{0,1},{1,0},{2,3},{3,2},{4,5},{5,4},{6,7},{7,6},{8,9},{9,8},{10,11... | collective-permute-start | bytes 1179656 | tf_op jit(solution)/shard_map/ppermute | solution.py:46
  612.8 16.0 %collective-permute-start.72 = (bf16[64,3072]{1,0:T(8,128)(2,1)}, bf16[64,3072]{1,0:T(8,128)(2,1)S(1)}, u32[]{:S(2)}, u32[]{:S(2)}) collective-permute-start(bf16[64,3072]{1,0:T(8,128)(2,1)} %get-tuple-element.279), channel_id=1, source_target_pairs={{0,4},{4,0},{1,5},{5,1},{2,6},{6,2},{3,7},{7,3},{8,12},{12,8},{9,1... | collective-permute-start | bytes 1179656 | tf_op jit(solution)/shard_map/ppermute | solution.py:46
  613.3 19.5 %collective-permute-start.73 = (bf16[64,3072]{1,0:T(8,128)(2,1)}, bf16[64,3072]{1,0:T(8,128)(2,1)}, u32[]{:S(2)}, u32[]{:S(2)}) collective-permute-start(bf16[64,3072]{1,0:T(8,128)(2,1)} %get-tuple-element.280), channel_id=1, source_target_pairs={{0,5},{1,4},{4,1},{5,0},{2,7},{3,6},{6,3},{7,2},{8,13},{9,12},{12,... | collective-permute-start | bytes 1179656 | tf_op jit(solution)/shard_map/ppermute | solution.py:96
  (129 other events, 1715.7 us)
Sparse Core Ops, SparseCore 0:
  23.7 66.1 all-gather.4
  91.5 68.8 all-gather.6
  162.1 80.5 all-gather.8
  244.2 80.5 all-gather.10
  326.9 75.2 reduce-scatter.3
  404.5 80.0 reduce-scatter.5
  488.2 117.6 reduce-scatter.7

commit v28 on v27

--- a/solution.py
+++ b/solution.py
@@ -988,6 +988,8 @@
         )
         rest_part, up_rows = lax.optimization_barrier((rest_part, up_rows))
         rest_rows = scatter_grad(rest_part, grad_axes)
+        kv_part = kv_part.astype(F32).sum(axis=0).astype(BF)
+        kv_part, grad_projected = lax.optimization_barrier((kv_part, grad_projected))
         parts = mm_scatter(grad_projected, first)
         grad_hidden, gain_grad_a, mask_grad = last_back(
             parts,
@@ -1001,7 +1003,6 @@
         sums = jnp.concatenate([gain_grad_a, gain_grad_b, gain_grad_c, mask_grad], axis=0)
 
 
-        kv_part = kv_part.astype(F32).sum(axis=0).astype(BF)
         kv_sum = spread(kv_part, "z", z_size).reshape(-1, 2 * group)
         kv_grads = spread(kv_sum, PLANE, 8)
         kv_weight_grad, grad_text_w, caption_part = text_back(

time: 651 us -> 651 us (level)
  no operation moved by 1% of the time
where the time goes in v28:
time: 651 us; the launch traced here: 644 us
  waiting for transfers between devices  208 us (32%)
  Pallas kernels  116 us (18%)
  starting transfers between devices  111 us (17%)
  blocking collectives  102 us (16%)
  local copies, waits for them, and re-layouts  49.9 us (8%)
  matrix products  32.5 us (5%)
  between operations  16.5 us (3%)
  other arithmetic  8.09 us (1%)
    ppermute x70, waiting for transfers between devices, swap(): return lax.ppermute(values, axis, PAIR)  146 us
    all_to_all x7, blocking collectives, trade(): return lax.all_to_all(blocks, axes, 0, 0, tiled=True)  102 us
    ppermute x70, starting transfers between devices, swap(): return lax.ppermute(values, axis, PAIR)  75.9 us
    pallas_call x19, Pallas kernels, call(): pl.pallas_call(kernel, grid=grid, in_specs=in_specs, out_specs=out_specs,...  73 us
    pallas_call x12, Pallas kernels, call(): pl.pallas_call(kernel, grid_spec=spec, **options)  42.7 us
    all_to_all x6, waiting for transfers between devices, trade(): return lax.all_to_all(blocks, axes, 0, 0, tiled=True)  39.6 us
    dot_general x6, matrix products, dot(): return lax.dot_general(a, b, (dims, ((), ())), preferred_element_type=F32)  32.5 us
    all_to_all x6, starting transfers between devices, trade(): return lax.all_to_all(blocks, axes, 0, 0, tiled=True)  26.1 us
  transfers between devices with their start and end apart: 89, of which 47 were waited for; matrix products, arithmetic and copies ran while one was open for 11% of the time, Pallas kernels for 17%

profile of v28, /device:TPU:0, one launch (start us, length us, event | category | flops | bytes accessed | tf_op | source)
XLA Modules:
  0.0 643.6 jit_solution(20206529395376868)
XLA Ops:
  30.1 8.8 %collective-permute-done.1.refs_2_ = bf16[128,2048]{1,0:T(8,128)(2,1)S(1)} collective-permute-done((bf16[128,2048]{1,0:T(8,128)(2,1)S(1)}, bf16[128,2048]{1,0:T(8,128)(2,1)S(1)}, u32[]{:S(2)}, u32[]{:S(2)}) %collective-permute-start.1) | collective-permute-done | bytes 524320 | tf_op jit(solution)/shard_map/ppermute | solution.py:46
  52.4 12.2 %all_to_all.65 = bf16[4,64,1536]{2,1,0:T(8,128)(2,1)} all-to-all(bf16[4,64,1536]{2,1,0:T(8,128)(2,1)S(1)} %copy.75), channel_id=1, replica_groups=mesh['z'=4,'x'=2,'c'=2,'y'=2] {'x','y'}, dimensions={0} | all-to-all | bytes 1572864 | tf_op jit(solution)/shard_map/all_to_all | solution.py:50
  64.7 15.0 %all_to_all.66 = bf16[4,64,2048]{2,1,0:T(8,128)(2,1)} all-to-all(bf16[4,64,2048]{2,1,0:T(8,128)(2,1)} %bitcast.90), channel_id=1, replica_groups=mesh['z'=4,'x'=2,'c'=2,'y'=2] {'x','y'}, dimensions={0} | all-to-all | bytes 2097152 | tf_op jit(solution)/shard_map/all_to_all | solution.py:50
  82.3 16.9 %all_to_all.67 = bf16[8,64,1024]{2,1,0:T(8,128)(2,1)S(1)} all-to-all(bf16[8,64,1024]{2,1,0:T(8,128)(2,1)S(1)} %get-tuple-element.161), channel_id=1, replica_groups=mesh['z'=4,'x'=2,'c'=2,'y'=2] {'x','c','y'}, dimensions={0} | all-to-all | bytes 2097152 | tf_op jit(solution)/shard_map/all_to_all | solution.py:50
  99.4 15.9 %all_to_all.68 = bf16[4,16,1024]{2,1,0:T(8,128)(2,1)S(1)} all-to-all(bf16[4,16,1024]{2,1,0:T(8,128)(2,1)S(1)} %bitcast.101), channel_id=1, replica_groups=mesh['z'=4,'x'=2,'c'=2,'y'=2] {'z'}, dimensions={0} | all-to-all | bytes 262144 | tf_op jit(solution)/shard_map/all_to_all | solution.py:50
  115.4 12.9 %all_to_all.69 = bf16[4,16,1024]{2,1,0:T(8,128)(2,1)S(1)} all-to-all(bf16[4,16,1024]{2,1,0:T(8,128)(2,1)S(1)} %broadcast_in_dim.12), channel_id=1, replica_groups=mesh['z'=4,'x'=2,'c'=2,'y'=2] {'z'}, dimensions={0} | all-to-all | bytes 262144 | tf_op jit(solution)/shard_map/all_to_all | solution.py:50
  132.8 9.0 %qkv_mm.1 = (bf16[512,2048]{1,0:T(8,128)(2,1)}, bf16[512,1536]{1,0:T(8,128)(2,1)S(1)}) custom-call(bf16[128,2048]{1,0:T(8,128)(2,1)S(1)} %copy-done.45, bf16[128,2048]{1,0:T(8,128)(2,1)S(1)} %copy-done.39, bf16[128,2048]{1,0:T(8,128)(2,1)S(1)} %collective-permute-done.1.refs_2_, bf16[64,2048]{1,0:T(8,128)(2,1)} %collective-permute-done.2.refs_3_, ...), custom_call_target="tpu_custom_call" | custom-call | flops 3221225472 | bytes 10485760 | tf_op jit(solution)/shard_map/qkv_mm/pallas_call | solution.py:118
  144.7 18.2 %all_to_all.70 = bf16[4,64,2048]{2,1,0:T(8,128)(2,1)} all-to-all(bf16[4,64,2048]{2,1,0:T(8,128)(2,1)S(1)} %bitcast.89), channel_id=1, replica_groups=mesh['z'=4,'x'=2,'c'=2,'y'=2] {'x','y'}, dimensions={0} | all-to-all | bytes 2097152 | tf_op jit(solution)/shard_map/all_to_all | solution.py:50
  177.4 10.8 %collective-permute-done.11.refs_3_ = bf16[128,2048]{1,0:T(8,128)(2,1)S(1)} collective-permute-done((bf16[128,2048]{1,0:T(8,128)(2,1)S(1)}, bf16[128,2048]{1,0:T(8,128)(2,1)S(1)}, u32[]{:S(2)}, u32[]{:S(2)}) %collective-permute-start.11) | collective-permute-done | bytes 524320 | tf_op jit(solution)/shard_map/ppermute | solution.py:46
  191.9 9.5 %collective-permute-done.13.refs_2_ = bf16[128,2048]{1,0:T(8,128)(2,1)S(1)} collective-permute-done((bf16[128,2048]{1,0:T(8,128)(2,1)S(1)}, bf16[128,2048]{1,0:T(8,128)(2,1)S(1)}, u32[]{:S(2)}, u32[]{:S(2)}) %collective-permute-start.13) | collective-permute-done | bytes 524320 | tf_op jit(solution)/shard_map/ppermute | solution.py:46
  229.2 7.9 %collective-permute-done.19.refs_3_ = bf16[128,2048]{1,0:T(8,128)(2,1)S(1)} collective-permute-done((bf16[128,2048]{1,0:T(8,128)(2,1)S(1)}, bf16[128,2048]{1,0:T(8,128)(2,1)S(1)}, u32[]{:S(2)}, u32[]{:S(2)}) %collective-permute-start.19) | collective-permute-done | bytes 524320 | tf_op jit(solution)/shard_map/ppermute | solution.py:46
  266.4 8.8 %collective-permute-done.25 = bf16[128,2048]{1,0:T(8,128)(2,1)S(1)} collective-permute-done((bf16[128,2048]{1,0:T(8,128)(2,1)S(1)}, bf16[128,2048]{1,0:T(8,128)(2,1)S(1)}, u32[]{:S(2)}, u32[]{:S(2)}) %collective-permute-start.25) | collective-permute-done | bytes 524320 | tf_op jit(solution)/shard_map/ppermute | solution.py:46
  285.8 11.9 %feed_up.1 = (bf16[512,2048]{1,0:T(8,128)(2,1)}, bf16[512,2048]{1,0:T(8,128)(2,1)}, f32[512,2048]{1,0:T(8,128)}) custom-call(bf16[128,2048]{1,0:T(8,128)(2,1)S(1)} %copy-done.47, bf16[128,2048]{1,0:T(8,128)(2,1)S(1)} %copy-done.43, bf16[128,2048]{1,0:T(8,128)(2,1)S(1)} %copy-done.41, bf16[64,2048]{1,0:T(8,128)(2,1)S(1)} %copy-done.49, ...), custom_call_target="tpu_custom_call" | custom-call | flops 4294967296 | bytes 12582912 | tf_op jit(solution)/shard_map/feed_up/pallas_call | solution.py:118
  308.8 8.6 %down_grads.1 = bf16[1024,2048]{1,0:T(8,128)(2,1)} custom-call(s32[1]{0:T(128)} %bitcast.25.r, bf16[512,2048]{1,0:T(8,128)(2,1)} %constant_dynamic-update-slice_fusion.refs_0_.dy, bf16[512,2048]{1,0:T(8,128)(2,1)S(1)} %collective-permute-done.28.refs_1_, bf16[512,2048]{1,0:T(8,128)(2,1)} %get-tuple-element.206.refs_2_, bf16[512,2048]{1,0:T(8,128)(2,1)} %copy-done.63), custom_call_target="tpu_custom_call" | custom-call | flops 4294967296 | bytes 16777216 | tf_op jit(solution)/shard_map/down_grads/pallas_call | solution.py:129
  324.8 10.7 %feed_down.1.refs_2_ = bf16[512,2048]{1,0:T(8,128)(2,1)S(1)} custom-call(bf16[512,2048]{1,0:T(8,128)(2,1)} %constant_dynamic-update-slice_fusion.refs_0_.dy, f32[512,2048]{1,0:T(8,128)} %get-tuple-element.193.slope_ref, bf16[2048,2048]{1,0:T(8,128)(2,1)} %all-gather.11.cloned.1.call-done.down), custom_call_target="tpu_custom_call" | custom-call | flops 4294967296 | bytes 25165824 | tf_op jit(solution)/shard_map/feed_down/pallas_call | solution.py:118
  335.8 8.6 %convolution_convert_fusion.3 = bf16[512,2048]{1,0:T(8,128)(2,1)S(1)} fusion(bf16[512,2048]{1,0:T(8,128)(2,1)S(1)} %feed_down.1.refs_2_, bf16[2048,2048]{1,0:T(8,128)(2,1)} %all-gather.9.cloned.1.call-done.refs_5_), kind=kOutput, calls=%fused_computation.3 | convolution fusion | flops 4296015872 | bytes 12582912 | tf_op jit(solution)/shard_map/dot_general | solution.py:26
  356.7 10.9 %collective-permute-done.38.refs_2_ = bf16[128,2048]{1,0:T(8,128)(2,1)S(1)} collective-permute-done((bf16[128,2048]{1,0:T(8,128)(2,1)S(1)}, bf16[128,2048]{1,0:T(8,128)(2,1)S(1)}, u32[]{:S(2)}, u32[]{:S(2)}) %collective-permute-start.38) | collective-permute-done | bytes 524320 | tf_op jit(solution)/shard_map/ppermute | solution.py:46
  374.7 8.7 %up_grads.1 = bf16[1024,2048]{1,0:T(8,128)(2,1)} custom-call(s32[1]{0:T(128)} %bitcast.25.r, bf16[512,2048]{1,0:T(8,128)(2,1)} %get-tuple-element.197.refs_0_, bf16[512,2048]{1,0:T(8,128)(2,1)} %collective-permute-done.34.refs_1_, bf16[512,2048]{1,0:T(8,128)(2,1)} %copy-done.22, bf16[512,2048]{1,0:T(8,128)(2,1)} %copy-done.62), custom_call_target="tpu_custom_call" | custom-call | flops 4294967296 | bytes 16777216 | tf_op jit(solution)/shard_map/up_grads/pallas_call | solution.py:129
  417.0 10.3 %collective-permute-done.47.refs_2_ = bf16[128,2048]{1,0:T(8,128)(2,1)S(1)} collective-permute-done((bf16[128,2048]{1,0:T(8,128)(2,1)S(1)}, bf16[128,2048]{1,0:T(8,128)(2,1)S(1)}, u32[]{:S(2)}, u32[]{:S(2)}) %collective-permute-start.47) | collective-permute-done | bytes 524320 | tf_op jit(solution)/shard_map/ppermute | solution.py:46
  433.1 8.5 %convolution_convert_fusion.1 = bf16[512,2048]{1,0:T(8,128)(2,1)S(1)} fusion(bf16[512,2048]{1,0:T(8,128)(2,1)S(1)} %copy-done.61, bf16[2048,2048]{1,0:T(8,128)(2,1)} %all-gather.11.cloned.1.call-done.down), kind=kOutput, calls=%fused_computation.1 | convolution fusion | flops 4296015872 | bytes 12582912 | tf_op jit(solution)/shard_map/dot_general | solution.py:26
  476.2 11.8 %attention_grads.1 = bf16[1024,3072]{1,0:T(8,128)(2,1)} custom-call(s32[1]{0:T(128)} %bitcast.25.r, bf16[512,2048]{1,0:T(8,128)(2,1)} %get-tuple-element.226.refs_0_, bf16[512,2048]{1,0:T(8,128)(2,1)} %collective-permute-done.30.refs_1_, bf16[512,2048]{1,0:T(8,128)(2,1)} %get-tuple-element.228.refs_2_, bf16[512,2048]{1,0:T(8,128)(2,1)} %collective-permute-done.56.refs_3_, ...), custom_call_target="tpu_custom_call" | custom-call | flops 6442450944 | bytes 25165824 | tf_op jit(solution)/shard_map/attention_grads/pallas_call | solution.py:129
  527.8 7.3 %all-to-all-done.8.block = bf16[8,64,1024]{2,1,0:T(8,128)(2,1)} async-done(((bf16[8,64,1024]{2,1,0:T(8,128)(2,1)}), bf16[8,64,1024]{2,1,0:T(8,128)(2,1)}, u32[]{:S(2)}, u32[]{:S(2)}) %all-to-all-start.8) | async-done | bytes 1048608 | tf_op jit(solution)/shard_map/all_to_all | solution.py:50
  548.6 13.8 %all-to-all-done.9 = bf16[8,80,1024]{2,1,0:T(8,128)(2,1)} async-done(((bf16[8,80,1024]{2,1,0:T(8,128)(2,1)}), bf16[8,80,1024]{2,1,0:T(8,128)(2,1)}, u32[]{:S(2)}, u32[]{:S(2)}) %all-to-all-start.9) | async-done | bytes 1310752 | tf_op jit(solution)/shard_map/all_to_all | solution.py:50
  567.8 10.4 %all_to_all.71 = bf16[4,16,1024]{2,1,0:T(8,128)(2,1)S(1)} all-to-all(bf16[4,16,1024]{2,1,0:T(8,128)(2,1)S(1)} %bitcast.102), channel_id=1, replica_groups=mesh['z'=4,'x'=2,'c'=2,'y'=2] {'z'}, dimensions={0} | all-to-all | bytes 262144 | tf_op jit(solution)/shard_map/all_to_all | solution.py:50
  (425 shorter events, 359.5 us)
Async XLA Ops:
  7.2 123.5 %all-gather.5.cloned.1.call-start = ((), (), s32[]{:S(2)}) async-start(), calls=%async_computation.16 | async-start | bytes 7077888 | tf_op jit(solution)/shard_map/all_gather | solution.py:101
  23.6 139.7 %all-gather.7.cloned.1.call-start = ((), (), s32[]{:S(2)}) async-start(), calls=%async_computation.17 | async-start | bytes 7077888 | tf_op jit(solution)/shard_map/all_gather | solution.py:101
  64.6 216.1 %all-gather.9.cloned.1.call-start = ((), (), s32[]{:S(2)}) async-start(), calls=%async_computation.18 | async-start | bytes 9437184 | tf_op jit(solution)/shard_map/all_gather | solution.py:101
  79.7 245.1 %all-gather.11.cloned.1.call-start = ((), (), s32[]{:S(2)}) async-start(), calls=%async_computation.19 | async-start | bytes 9437184 | tf_op jit(solution)/shard_map/all_gather | solution.py:101
  163.0 239.3 %reduce-scatter.4.cloned.1.call-start = ((), (), s32[]{:S(2)}) async-start(), calls=%async_computation.20 | async-start | bytes 5242880 | tf_op jit(solution)/shard_map/reduce_scatter | solution.py:105
  276.0 21.8 %collective-permute-start.26 = (bf16[64,2048]{1,0:T(8,128)(2,1)}, bf16[64,2048]{1,0:T(8,128)(2,1)}, u32[]{:S(2)}, u32[]{:S(2)}) collective-permute-start(bf16[64,2048]{1,0:T(8,128)(2,1)} %slice.347), channel_id=1, source_target_pairs={{0,1},{1,0},{2,3},{3,2},{4,5},{5,4},{6,7},{7,6},{8,9},{9,8},{10,11... | collective-permute-start | bytes 786440 | tf_op jit(solution)/shard_map/ppermute | solution.py:46
  277.8 21.7 %collective-permute-start.27 = (bf16[64,2048]{1,0:T(8,128)(2,1)}, bf16[64,2048]{1,0:T(8,128)(2,1)}, u32[]{:S(2)}, u32[]{:S(2)}) collective-permute-start(bf16[64,2048]{1,0:T(8,128)(2,1)} %slice.348), channel_id=1, source_target_pairs={{0,4},{4,0},{1,5},{5,1},{2,6},{6,2},{3,7},{7,3},{8,12},{12,8},{9,1... | collective-permute-start | bytes 786440 | tf_op jit(solution)/shard_map/ppermute | solution.py:46
  301.7 15.8 %collective-permute-start.30 = (bf16[512,2048]{1,0:T(8,128)(2,1)}, bf16[512,2048]{1,0:T(8,128)(2,1)}, u32[]{:S(2)}, u32[]{:S(2)}) collective-permute-start(bf16[512,2048]{1,0:T(8,128)(2,1)} %get-tuple-element.226.refs_0_), channel_id=1, source_target_pairs={{0,2},{2,0},{1,3},{3,1},{4,6},{6,4},{5,7},{7,5},{8,10},{10,8},{9,1... | collective-permute-start | bytes 6291464 | tf_op jit(solution)/shard_map/ppermute | solution.py:46
  317.5 170.5 %reduce-scatter.6.cloned.1.call-start = ((), (), s32[]{:S(2)}) async-start(), calls=%async_computation.21 | async-start | bytes 5242880 | tf_op jit(solution)/shard_map/reduce_scatter | solution.py:105
  335.5 37.9 %collective-permute-start.41 = (bf16[512,2048]{1,0:T(8,128)(2,1)S(1)}, bf16[512,2048]{1,0:T(8,128)(2,1)S(1)}, u32[]{:S(2)}, u32[]{:S(2)}) collective-permute-start(bf16[512,2048]{1,0:T(8,128)(2,1)S(1)} %feed_down.1.refs_2_), channel_id=1, source_target_pairs={{0,2},{2,0},{1,3},{3,1},{4,6},{6,4},{5,7},{7,5},{8,10},{10,8},{9,1... | collective-permute-start | bytes 6291464 | tf_op jit(solution)/shard_map/ppermute | solution.py:46
  454.6 20.5 %collective-permute-start.57 = (bf16[512,2048]{1,0:T(8,128)(2,1)}, bf16[512,2048]{1,0:T(8,128)(2,1)}, u32[]{:S(2)}, u32[]{:S(2)}) collective-permute-start(bf16[512,2048]{1,0:T(8,128)(2,1)} %get-tuple-element.231.refs_6_), channel_id=1, source_target_pairs={{0,2},{2,0},{1,3},{3,1},{4,6},{6,4},{5,7},{7,5},{8,10},{10,8},{9,1... | collective-permute-start | bytes 6291464 | tf_op jit(solution)/shard_map/ppermute | solution.py:46
  459.3 15.8 %collective-permute-start.56 = (bf16[512,2048]{1,0:T(8,128)(2,1)}, bf16[512,2048]{1,0:T(8,128)(2,1)}, u32[]{:S(2)}, u32[]{:S(2)}) collective-permute-start(bf16[512,2048]{1,0:T(8,128)(2,1)} %get-tuple-element.228.refs_2_), channel_id=1, source_target_pairs={{0,2},{2,0},{1,3},{3,1},{4,6},{6,4},{5,7},{7,5},{8,10},{10,8},{9,1... | collective-permute-start | bytes 6291464 | tf_op jit(solution)/shard_map/ppermute | solution.py:46
  466.4 21.6 %collective-permute-start.54 = (bf16[128,2048]{1,0:T(8,128)(2,1)}, bf16[128,2048]{1,0:T(8,128)(2,1)}, u32[]{:S(2)}, u32[]{:S(2)}) collective-permute-start(bf16[128,2048]{1,0:T(8,128)(2,1)} %get-tuple-element.223), channel_id=1, source_target_pairs={{0,4},{4,0},{1,5},{5,1},{2,6},{6,2},{3,7},{7,3},{8,12},{12,8},{9,1... | collective-permute-start | bytes 1572872 | tf_op jit(solution)/shard_map/ppermute | solution.py:46
  468.2 19.8 %all-to-all-start.6 = ((bf16[8,16,1024]{2,1,0:T(8,128)(2,1)}), bf16[8,16,1024]{2,1,0:T(8,128)(2,1)S(1)}, u32[]{:S(2)}, u32[]{:S(2)}) async-start(bf16[8,16,1024]{2,1,0:T(8,128)(2,1)} %bitcast.30), calls=%async_computation.7 | async-start | bytes 524288 | tf_op jit(solution)/shard_map/all_to_all | solution.py:50
  472.3 136.4 %reduce-scatter.8.cloned.1.call-start = ((), (), s32[]{:S(2)}) async-start(), calls=%async_computation.22 | async-start | bytes 7864320 | tf_op jit(solution)/shard_map/reduce_scatter | solution.py:105
  499.0 16.2 %all-to-all-start.7 = ((bf16[4,16,1024]{2,1,0:T(8,128)(2,1)}), bf16[4,16,1024]{2,1,0:T(8,128)(2,1)S(1)}, u32[]{:S(2)}, u32[]{:S(2)}) async-start(bf16[4,16,1024]{2,1,0:T(8,128)(2,1)} %broadcast_in_dim.13), calls=%async_computation.8 | async-start | bytes 262144 | tf_op jit(solution)/shard_map/all_to_all | solution.py:50
  516.3 18.8 %all-to-all-start.8 = ((bf16[8,64,1024]{2,1,0:T(8,128)(2,1)}), bf16[8,64,1024]{2,1,0:T(8,128)(2,1)}, u32[]{:S(2)}, u32[]{:S(2)}) async-start(bf16[8,64,1024]{2,1,0:T(8,128)(2,1)} %broadcast_in_dim.15), calls=%async_computation.9 | async-start | bytes 2097152 | tf_op jit(solution)/shard_map/all_to_all | solution.py:50
  540.7 21.8 %all-to-all-start.9 = ((bf16[8,80,1024]{2,1,0:T(8,128)(2,1)}), bf16[8,80,1024]{2,1,0:T(8,128)(2,1)}, u32[]{:S(2)}, u32[]{:S(2)}) async-start(bf16[8,80,1024]{2,1,0:T(8,128)(2,1)} %copy-done.24), calls=%async_computation.10 | async-start | bytes 2621440 | tf_op jit(solution)/shard_map/all_to_all | solution.py:50
  578.5 17.4 %collective-permute-start.67 = (bf16[64,2048]{1,0:T(8,128)(2,1)S(1)}, bf16[64,2048]{1,0:T(8,128)(2,1)S(1)}, u32[]{:S(2)}, u32[]{:S(2)}) collective-permute-start(bf16[64,2048]{1,0:T(8,128)(2,1)S(1)} %get-tuple-element.266), channel_id=1, source_target_pairs={{0,1},{1,0},{2,3},{3,2},{4,5},{5,4},{6,7},{7,6},{8,9},{9,8},{10,11... | collective-permute-start | bytes 786440 | tf_op jit(solution)/shard_map/ppermute | solution.py:46
  579.9 16.0 %collective-permute-start.68 = (bf16[64,2048]{1,0:T(8,128)(2,1)S(1)}, bf16[64,2048]{1,0:T(8,128)(2,1)S(1)}, u32[]{:S(2)}, u32[]{:S(2)}) collective-permute-start(bf16[64,2048]{1,0:T(8,128)(2,1)S(1)} %get-tuple-element.267), channel_id=1, source_target_pairs={{0,4},{4,0},{1,5},{5,1},{2,6},{6,2},{3,7},{7,3},{8,12},{12,8},{9,1... | collective-permute-start | bytes 786440 | tf_op jit(solution)/shard_map/ppermute | solution.py:46
  608.7 17.2 %collective-permute-start.70 = (bf16[4,64,1024]{2,1,0:T(8,128)(2,1)S(1)}, bf16[4,64,1024]{2,1,0:T(8,128)(2,1)S(1)}, u32[]{:S(2)}, u32[]{:S(2)}) collective-permute-start(bf16[4,64,1024]{2,1,0:T(8,128)(2,1)S(1)} %all-to-all-done.12.own_ref), channel_id=1, source_target_pairs={{0,2},{2,0},{1,3},{3,1},{4,6},{6,4},{5,7},{7,5},{8,10},{10,8},{9,1... | collective-permute-start | bytes 1572872 | tf_op jit(solution)/shard_map/ppermute | solution.py:46
  611.3 17.5 %collective-permute-start.71 = (bf16[64,3072]{1,0:T(8,128)(2,1)}, bf16[64,3072]{1,0:T(8,128)(2,1)S(1)}, u32[]{:S(2)}, u32[]{:S(2)}) collective-permute-start(bf16[64,3072]{1,0:T(8,128)(2,1)} %get-tuple-element.282), channel_id=1, source_target_pairs={{0,1},{1,0},{2,3},{3,2},{4,5},{5,4},{6,7},{7,6},{8,9},{9,8},{10,11... | collective-permute-start | bytes 1179656 | tf_op jit(solution)/shard_map/ppermute | solution.py:46
  612.8 16.0 %collective-permute-start.72 = (bf16[64,3072]{1,0:T(8,128)(2,1)}, bf16[64,3072]{1,0:T(8,128)(2,1)S(1)}, u32[]{:S(2)}, u32[]{:S(2)}) collective-permute-start(bf16[64,3072]{1,0:T(8,128)(2,1)} %get-tuple-element.283), channel_id=1, source_target_pairs={{0,4},{4,0},{1,5},{5,1},{2,6},{6,2},{3,7},{7,3},{8,12},{12,8},{9,1... | collective-permute-start | bytes 1179656 | tf_op jit(solution)/shard_map/ppermute | solution.py:46
  613.3 19.5 %collective-permute-start.73 = (bf16[64,3072]{1,0:T(8,128)(2,1)}, bf16[64,3072]{1,0:T(8,128)(2,1)}, u32[]{:S(2)}, u32[]{:S(2)}) collective-permute-start(bf16[64,3072]{1,0:T(8,128)(2,1)} %get-tuple-element.284), channel_id=1, source_target_pairs={{0,5},{1,4},{4,1},{5,0},{2,7},{3,6},{6,3},{7,2},{8,13},{9,12},{12,... | collective-permute-start | bytes 1179656 | tf_op jit(solution)/shard_map/ppermute | solution.py:96
  (129 other events, 1715.6 us)
Sparse Core Ops, SparseCore 0:
  23.7 66.1 all-gather.4
  91.5 68.8 all-gather.6
  162.1 80.5 all-gather.8
  244.2 80.5 all-gather.10
  326.9 75.2 reduce-scatter.3
  404.5 80.0 reduce-scatter.5
  488.2 117.6 reduce-scatter.7

commit v29 on v27

--- a/solution.py
+++ b/solution.py
@@ -736,13 +736,12 @@
     )
 
 
-def text_back(blocks, own_text, w_cross, caption, w_text, extra):
+def text_back(blocks, own_text, w_cross, caption, w_text):
     context, rows = own_text.shape
     half, width = context // 2, w_cross.shape[2] // 4
     wide = caption.shape[1] // 4
-    tail = extra.shape[0]
-
-    def kernel(block, own, cross, cap, weight, more, kv_grad, text_grad, out, grads):
+
+    def kernel(block, own, cross, cap, weight, kv_grad, text_grad, out, grads):
         for k in range(8):
             core, group = plane_block(k)
             for j in range(2):
@@ -758,14 +757,13 @@
         part = mm(grad_text, weight[...]).astype(BF)
         for k in range(8):
             core, group = plane_block(k)
-            out[k, :half, :] = part[core * half : (core + 1) * half, group * wide : (group + 1) * wide]
-            out[k, half:, :] = more[...]
-
-    operands = [blocks, own_text, w_cross, caption, w_text, extra]
+            out[k] = part[core * half : (core + 1) * half, group * wide : (group + 1) * wide]
+
+    operands = [blocks, own_text, w_cross, caption, w_text]
     outs = [
         shape((rows, 8 * width), F32),
         shape((rows, 4 * wide), F32),
-        shape((8, half + tail, wide)),
+        shape((8, half, wide)),
     ]
     return call(
         kernel,
@@ -779,8 +777,8 @@
     )
 
 
-def caption_output(own, other, core):
-    count, half, wide = own.shape
+def caption_output(own, other, core, half):
+    count, _, wide = own.shape
 
     def kernel(r, own_ref, other_ref, out):
         block = jnp.where(pl.program_id(0) == r[0], own_ref[0], other_ref[0])
@@ -988,36 +986,24 @@
         )
         rest_part, up_rows = lax.optimization_barrier((rest_part, up_rows))
         rest_rows = scatter_grad(rest_part, grad_axes)
-        parts = mm_scatter(grad_projected, first)
-        grad_hidden, gain_grad_a, mask_grad = last_back(
-            parts,
-            grad_after_attn,
-            start_x,
-            gain_a,
-            masked,
-            unit,
-            order,
-        )
-        sums = jnp.concatenate([gain_grad_a, gain_grad_b, gain_grad_c, mask_grad], axis=0)
-
 
         kv_part = kv_part.astype(F32).sum(axis=0).astype(BF)
         kv_sum = spread(kv_part, "z", z_size).reshape(-1, 2 * group)
+        kv_sum, grad_projected = lax.optimization_barrier((kv_sum, grad_projected))
         kv_grads = spread(kv_sum, PLANE, 8)
+        parts = mm_scatter(grad_projected, first)
         kv_weight_grad, grad_text_w, caption_part = text_back(
-            kv_grads, own_text, w_cross, caption, w_text, halves_of(sums, text_width // 4)
+            kv_grads, own_text, w_cross, caption, w_text
         )
         half_context = caption.shape[0] // 2
         caption_part = trade(caption_part, PLANE)
         output = layer_output(after_cross, result, unit, order)
-        caption_part, output, down_rows, up_rows = lax.optimization_barrier(
-            (caption_part, output, down_rows, up_rows)
-        )
-
-        caption_part = caption_part.astype(F32).sum(axis=0)
-        sums = layer_order(add_z(whole_of(caption_part[half_context:], width)))
-        caption_part = caption_part[:half_context].astype(BF).reshape(z_size, -1, text_width // 4)
-        caption_part = trade(caption_part, "z")
+        caption_part, output, parts, down_rows, up_rows = lax.optimization_barrier(
+            (caption_part, output, parts, down_rows, up_rows)
+        )
+
+        caption_part = caption_part.astype(F32).sum(axis=0).astype(BF)
+        caption_part = trade(caption_part.reshape(z_size, -1, text_width // 4), "z")
         down_parts = swap_parts(pick_rows([down_rows], rank))
         caption_part, down_parts, up_rows = lax.optimization_barrier(
             (caption_part, down_parts, up_rows)
@@ -1025,18 +1011,28 @@
 
         caption_part = caption_part.astype(F32).sum(axis=0).astype(BF)
         caption_part = spread(caption_part, "z", z_size).reshape(half_context, -1)
+        grad_hidden, gain_grad_a, mask_grad = last_back(
+            parts, grad_after_attn, start_x, gain_a, masked, unit, order
+        )
+        sums = jnp.concatenate([gain_grad_a, gain_grad_b, gain_grad_c, mask_grad], axis=0)
         up_parts = swap_parts(pick_rows([up_rows], rank))
         down_grad = finish_wide(down_parts, rank)
-        caption_part, up_parts, down_grad = lax.optimization_barrier(
-            (caption_part, up_parts, down_grad)
-        )
-
+        caption_part, sums, up_parts, down_grad = lax.optimization_barrier(
+            (caption_part, sums, up_parts, down_grad)
+        )
+
+        caption_part = jnp.concatenate([caption_part, halves_of(sums, text_width // 4)], axis=0)
         caption_part = spread(caption_part)
         up_grad = finish_wide(up_parts, rank)
         caption_part, rest_rows, up_grad = lax.optimization_barrier(
             (caption_part, rest_rows, up_grad)
         )
-        grad_caption = caption_output(caption_part, swap(caption_part, "c"), core)
+        caption_far = swap(caption_part, "c")
+        grad_caption = caption_output(caption_part, caption_far, core, half_context)
+        sums = sum(
+            part[:, half_context:].astype(F32).sum(axis=0) for part in (caption_part, caption_far)
+        )
+        sums = layer_order(add_z(whole_of(sums, width)))
         rest_rows = swap_parts(pick_rows([rest_rows], rank))
         grad_caption, rest_rows = lax.optimization_barrier((grad_caption, rest_rows))
         qkv_grad, out_grad, grad_cross, cross_out_grad = finish_all(

time: 651 us -> 670 us (1.029)
  blocking collectives: 102 us -> 124 us
  waiting for transfers between devices: 208 us -> 198 us
    all_to_all x6 -> x5, waiting for transfers between devices: 39.7 us -> 5.37 us  [trade(): return lax.all_to_all(blocks, axes, 0, 0, tiled=True)]
    ppermute x70, waiting for transfers between devices: 146 us -> 169 us  [swap(): return lax.ppermute(values, axis, PAIR)]
    all_to_all x7 -> x8, blocking collectives: 102 us -> 124 us  [trade(): return lax.all_to_all(blocks, axes, 0, 0, tiled=True)]
    all_to_all x6 -> x5, starting transfers between devices: 26 us -> 19.5 us  [trade(): return lax.all_to_all(blocks, axes, 0, 0, tiled=True)]
    unnamed x132 -> x144, local copies, waits for them, and re-layouts: 26 us -> 31 us
  transfers between devices with their start and end apart: 89 -> 88, of which waited for: 47 -> 45; matrix products, arithmetic and copies ran while one was open for 11% -> 11% of each run, Pallas kernels for 17% -> 18%
where the time goes in v29:
time: 670 us; the launch traced here: 662 us
  waiting for transfers between devices  198 us (30%)
  blocking collectives  124 us (19%)
  Pallas kernels  118 us (18%)
  starting transfers between devices  107 us (16%)
  local copies, waits for them, and re-layouts  56.5 us (8%)
  matrix products  32.5 us (5%)
  between operations  16.5 us (2%)
  other arithmetic  9.32 us (1%)
    ppermute x70, waiting for transfers between devices, swap(): return lax.ppermute(values, axis, PAIR)  169 us
    all_to_all x8, blocking collectives, trade(): return lax.all_to_all(blocks, axes, 0, 0, tiled=True)  124 us
    ppermute x70, starting transfers between devices, swap(): return lax.ppermute(values, axis, PAIR)  79.3 us
    pallas_call x19, Pallas kernels, call(): pl.pallas_call(kernel, grid=grid, in_specs=in_specs, out_specs=out_specs,...  71.4 us
    pallas_call x12, Pallas kernels, call(): pl.pallas_call(kernel, grid_spec=spec, **options)  46.6 us
    dot_general x6, matrix products, dot(): return lax.dot_general(a, b, (dims, ((), ())), preferred_element_type=F32)  32.5 us
    unnamed x144, local copies, waits for them, and re-layouts  31 us
    all_to_all x5, starting transfers between devices, trade(): return lax.all_to_all(blocks, axes, 0, 0, tiled=True)  19.5 us
  transfers between devices with their start and end apart: 88, of which 45 were waited for; matrix products, arithmetic and copies ran while one was open for 11% of the time, Pallas kernels for 18%

profile of v29, /device:TPU:0, one launch (start us, length us, event | category | flops | bytes accessed | tf_op | source)
XLA Modules:
  0.0 661.5 jit_solution(10214129208312890885)
XLA Ops:
  30.1 8.8 %collective-permute-done.1.refs_2_ = bf16[128,2048]{1,0:T(8,128)(2,1)S(1)} collective-permute-done((bf16[128,2048]{1,0:T(8,128)(2,1)S(1)}, bf16[128,2048]{1,0:T(8,128)(2,1)S(1)}, u32[]{:S(2)}, u32[]{:S(2)}) %collective-permute-start.1) | collective-permute-done | bytes 524320 | tf_op jit(solution)/shard_map/ppermute | solution.py:46
  52.4 12.2 %all_to_all.65 = bf16[4,64,1536]{2,1,0:T(8,128)(2,1)} all-to-all(bf16[4,64,1536]{2,1,0:T(8,128)(2,1)S(1)} %copy.75), channel_id=1, replica_groups=mesh['z'=4,'x'=2,'c'=2,'y'=2] {'x','y'}, dimensions={0} | all-to-all | bytes 1572864 | tf_op jit(solution)/shard_map/all_to_all | solution.py:50
  64.7 15.0 %all_to_all.66 = bf16[4,64,2048]{2,1,0:T(8,128)(2,1)} all-to-all(bf16[4,64,2048]{2,1,0:T(8,128)(2,1)} %bitcast.90), channel_id=1, replica_groups=mesh['z'=4,'x'=2,'c'=2,'y'=2] {'x','y'}, dimensions={0} | all-to-all | bytes 2097152 | tf_op jit(solution)/shard_map/all_to_all | solution.py:50
  82.3 16.9 %all_to_all.67 = bf16[8,64,1024]{2,1,0:T(8,128)(2,1)S(1)} all-to-all(bf16[8,64,1024]{2,1,0:T(8,128)(2,1)S(1)} %get-tuple-element.165), channel_id=1, replica_groups=mesh['z'=4,'x'=2,'c'=2,'y'=2] {'x','c','y'}, dimensions={0} | all-to-all | bytes 2097152 | tf_op jit(solution)/shard_map/all_to_all | solution.py:50
  99.4 15.9 %all_to_all.68 = bf16[4,16,1024]{2,1,0:T(8,128)(2,1)S(1)} all-to-all(bf16[4,16,1024]{2,1,0:T(8,128)(2,1)S(1)} %bitcast.99), channel_id=1, replica_groups=mesh['z'=4,'x'=2,'c'=2,'y'=2] {'z'}, dimensions={0} | all-to-all | bytes 262144 | tf_op jit(solution)/shard_map/all_to_all | solution.py:50
  115.4 12.9 %all_to_all.69 = bf16[4,16,1024]{2,1,0:T(8,128)(2,1)S(1)} all-to-all(bf16[4,16,1024]{2,1,0:T(8,128)(2,1)S(1)} %broadcast_in_dim.10), channel_id=1, replica_groups=mesh['z'=4,'x'=2,'c'=2,'y'=2] {'z'}, dimensions={0} | all-to-all | bytes 262144 | tf_op jit(solution)/shard_map/all_to_all | solution.py:50
  132.8 9.0 %qkv_mm.1 = (bf16[512,2048]{1,0:T(8,128)(2,1)}, bf16[512,1536]{1,0:T(8,128)(2,1)S(1)}) custom-call(bf16[128,2048]{1,0:T(8,128)(2,1)S(1)} %copy-done.49, bf16[128,2048]{1,0:T(8,128)(2,1)S(1)} %copy-done.43, bf16[128,2048]{1,0:T(8,128)(2,1)S(1)} %collective-permute-done.1.refs_2_, bf16[64,2048]{1,0:T(8,128)(2,1)} %collective-permute-done.2.refs_3_, ...), custom_call_target="tpu_custom_call" | custom-call | flops 3221225472 | bytes 10485760 | tf_op jit(solution)/shard_map/qkv_mm/pallas_call | solution.py:118
  144.7 18.2 %all_to_all.70 = bf16[4,64,2048]{2,1,0:T(8,128)(2,1)} all-to-all(bf16[4,64,2048]{2,1,0:T(8,128)(2,1)S(1)} %bitcast.89), channel_id=1, replica_groups=mesh['z'=4,'x'=2,'c'=2,'y'=2] {'x','y'}, dimensions={0} | all-to-all | bytes 2097152 | tf_op jit(solution)/shard_map/all_to_all | solution.py:50
  177.4 10.8 %collective-permute-done.11.refs_3_ = bf16[128,2048]{1,0:T(8,128)(2,1)S(1)} collective-permute-done((bf16[128,2048]{1,0:T(8,128)(2,1)S(1)}, bf16[128,2048]{1,0:T(8,128)(2,1)S(1)}, u32[]{:S(2)}, u32[]{:S(2)}) %collective-permute-start.11) | collective-permute-done | bytes 524320 | tf_op jit(solution)/shard_map/ppermute | solution.py:46
  191.8 9.4 %collective-permute-done.13.refs_2_ = bf16[128,2048]{1,0:T(8,128)(2,1)S(1)} collective-permute-done((bf16[128,2048]{1,0:T(8,128)(2,1)S(1)}, bf16[128,2048]{1,0:T(8,128)(2,1)S(1)}, u32[]{:S(2)}, u32[]{:S(2)}) %collective-permute-start.13) | collective-permute-done | bytes 524320 | tf_op jit(solution)/shard_map/ppermute | solution.py:46
  266.4 8.8 %collective-permute-done.25 = bf16[128,2048]{1,0:T(8,128)(2,1)S(1)} collective-permute-done((bf16[128,2048]{1,0:T(8,128)(2,1)S(1)}, bf16[128,2048]{1,0:T(8,128)(2,1)S(1)}, u32[]{:S(2)}, u32[]{:S(2)}) %collective-permute-start.25) | collective-permute-done | bytes 524320 | tf_op jit(solution)/shard_map/ppermute | solution.py:46
  285.8 11.9 %feed_up.1 = (bf16[512,2048]{1,0:T(8,128)(2,1)}, bf16[512,2048]{1,0:T(8,128)(2,1)}, f32[512,2048]{1,0:T(8,128)}) custom-call(bf16[128,2048]{1,0:T(8,128)(2,1)S(1)} %copy-done.51, bf16[128,2048]{1,0:T(8,128)(2,1)S(1)} %copy-done.47, bf16[128,2048]{1,0:T(8,128)(2,1)S(1)} %copy-done.45, bf16[64,2048]{1,0:T(8,128)(2,1)S(1)} %copy-done.53, ...), custom_call_target="tpu_custom_call" | custom-call | flops 4294967296 | bytes 12582912 | tf_op jit(solution)/shard_map/feed_up/pallas_call | solution.py:118
  308.8 8.7 %down_grads.1 = bf16[1024,2048]{1,0:T(8,128)(2,1)} custom-call(s32[1]{0:T(128)} %bitcast.25.r, bf16[512,2048]{1,0:T(8,128)(2,1)} %constant_dynamic-update-slice_fusion.refs_0_.dy, bf16[512,2048]{1,0:T(8,128)(2,1)S(1)} %collective-permute-done.28.refs_1_, bf16[512,2048]{1,0:T(8,128)(2,1)} %get-tuple-element.210.refs_2_, bf16[512,2048]{1,0:T(8,128)(2,1)} %copy-done.69), custom_call_target="tpu_custom_call" | custom-call | flops 4294967296 | bytes 16777216 | tf_op jit(solution)/shard_map/down_grads/pallas_call | solution.py:129
  324.8 10.7 %feed_down.1.refs_2_ = bf16[512,2048]{1,0:T(8,128)(2,1)S(1)} custom-call(bf16[512,2048]{1,0:T(8,128)(2,1)} %constant_dynamic-update-slice_fusion.refs_0_.dy, f32[512,2048]{1,0:T(8,128)} %get-tuple-element.197.slope_ref, bf16[2048,2048]{1,0:T(8,128)(2,1)} %all-gather.11.cloned.1.call-done.down), custom_call_target="tpu_custom_call" | custom-call | flops 4294967296 | bytes 25165824 | tf_op jit(solution)/shard_map/feed_down/pallas_call | solution.py:118
  335.8 8.6 %convolution_convert_fusion.3 = bf16[512,2048]{1,0:T(8,128)(2,1)S(1)} fusion(bf16[512,2048]{1,0:T(8,128)(2,1)S(1)} %feed_down.1.refs_2_, bf16[2048,2048]{1,0:T(8,128)(2,1)} %all-gather.9.cloned.1.call-done.refs_5_), kind=kOutput, calls=%fused_computation.3 | convolution fusion | flops 4296015872 | bytes 12582912 | tf_op jit(solution)/shard_map/dot_general | solution.py:26
  356.7 10.9 %collective-permute-done.38.refs_2_ = bf16[128,2048]{1,0:T(8,128)(2,1)S(1)} collective-permute-done((bf16[128,2048]{1,0:T(8,128)(2,1)S(1)}, bf16[128,2048]{1,0:T(8,128)(2,1)S(1)}, u32[]{:S(2)}, u32[]{:S(2)}) %collective-permute-start.38) | collective-permute-done | bytes 524320 | tf_op jit(solution)/shard_map/ppermute | solution.py:46
  374.7 8.7 %up_grads.1 = bf16[1024,2048]{1,0:T(8,128)(2,1)} custom-call(s32[1]{0:T(128)} %bitcast.25.r, bf16[512,2048]{1,0:T(8,128)(2,1)} %get-tuple-element.201.refs_0_, bf16[512,2048]{1,0:T(8,128)(2,1)} %collective-permute-done.34.refs_1_, bf16[512,2048]{1,0:T(8,128)(2,1)} %copy-done.20, bf16[512,2048]{1,0:T(8,128)(2,1)} %copy-done.68), custom_call_target="tpu_custom_call" | custom-call | flops 4294967296 | bytes 16777216 | tf_op jit(solution)/shard_map/up_grads/pallas_call | solution.py:129
  417.0 10.3 %collective-permute-done.47.refs_2_ = bf16[128,2048]{1,0:T(8,128)(2,1)S(1)} collective-permute-done((bf16[128,2048]{1,0:T(8,128)(2,1)S(1)}, bf16[128,2048]{1,0:T(8,128)(2,1)S(1)}, u32[]{:S(2)}, u32[]{:S(2)}) %collective-permute-start.47) | collective-permute-done | bytes 524320 | tf_op jit(solution)/shard_map/ppermute | solution.py:46
  433.1 8.4 %convolution_convert_fusion.1 = bf16[512,2048]{1,0:T(8,128)(2,1)S(1)} fusion(bf16[512,2048]{1,0:T(8,128)(2,1)S(1)} %copy-done.67, bf16[2048,2048]{1,0:T(8,128)(2,1)} %all-gather.11.cloned.1.call-done.down), kind=kOutput, calls=%fused_computation.1 | convolution fusion | flops 4296015872 | bytes 12582912 | tf_op jit(solution)/shard_map/dot_general | solution.py:26
  476.2 11.8 %attention_grads.1 = bf16[1024,3072]{1,0:T(8,128)(2,1)} custom-call(s32[1]{0:T(128)} %bitcast.25.r, bf16[512,2048]{1,0:T(8,128)(2,1)} %get-tuple-element.230.refs_0_, bf16[512,2048]{1,0:T(8,128)(2,1)} %collective-permute-done.30.refs_1_, bf16[512,2048]{1,0:T(8,128)(2,1)} %get-tuple-element.232.refs_2_, bf16[512,2048]{1,0:T(8,128)(2,1)} %collective-permute-done.56.refs_3_, ...), custom_call_target="tpu_custom_call" | custom-call | flops 6442450944 | bytes 25165824 | tf_op jit(solution)/shard_map/attention_grads/pallas_call | solution.py:129
  488.1 16.6 %all_to_all.71 = bf16[4,16,1024]{2,1,0:T(8,128)(2,1)S(1)} all-to-all(bf16[4,16,1024]{2,1,0:T(8,128)(2,1)S(1)} %broadcast_in_dim.11), channel_id=1, replica_groups=mesh['z'=4,'x'=2,'c'=2,'y'=2] {'z'}, dimensions={0} | all-to-all | bytes 262144 | tf_op jit(solution)/shard_map/all_to_all | solution.py:50
  520.8 9.2 %collective-permute-done.60 = bf16[64,2048]{1,0:T(8,128)(2,1)S(1)} collective-permute-done((bf16[64,2048]{1,0:T(8,128)(2,1)S(1)}, bf16[64,2048]{1,0:T(8,128)(2,1)S(1)}, u32[]{:S(2)}, u32[]{:S(2)}) %collective-permute-start.60) | collective-permute-done | bytes 262176 | tf_op jit(solution)/shard_map/ppermute | solution.py:46
  549.1 16.4 %collective-permute-done.63.refs_2_ = bf16[128,2048]{1,0:T(8,128)(2,1)S(1)} collective-permute-done((bf16[128,2048]{1,0:T(8,128)(2,1)S(1)}, bf16[128,2048]{1,0:T(8,128)(2,1)S(1)}, u32[]{:S(2)}, u32[]{:S(2)}) %collective-permute-start.63) | collective-permute-done | bytes 524320 | tf_op jit(solution)/shard_map/ppermute | solution.py:46
  575.0 16.4 %all_to_all.72 = bf16[4,16,1024]{2,1,0:T(8,128)(2,1)} all-to-all(bf16[4,16,1024]{2,1,0:T(8,128)(2,1)} %bitcast.101), channel_id=1, replica_groups=mesh['z'=4,'x'=2,'c'=2,'y'=2] {'z'}, dimensions={0} | all-to-all | bytes 262144 | tf_op jit(solution)/shard_map/all_to_all | solution.py:50
  (439 shorter events, 358.4 us)
Async XLA Ops:
  7.2 123.5 %all-gather.5.cloned.1.call-start = ((), (), s32[]{:S(2)}) async-start(), calls=%async_computation.16 | async-start | bytes 7077888 | tf_op jit(solution)/shard_map/all_gather | solution.py:101
  23.6 139.6 %all-gather.7.cloned.1.call-start = ((), (), s32[]{:S(2)}) async-start(), calls=%async_computation.17 | async-start | bytes 7077888 | tf_op jit(solution)/shard_map/all_gather | solution.py:101
  64.6 216.1 %all-gather.9.cloned.1.call-start = ((), (), s32[]{:S(2)}) async-start(), calls=%async_computation.18 | async-start | bytes 9437184 | tf_op jit(solution)/shard_map/all_gather | solution.py:101
  79.7 245.1 %all-gather.11.cloned.1.call-start = ((), (), s32[]{:S(2)}) async-start(), calls=%async_computation.19 | async-start | bytes 9437184 | tf_op jit(solution)/shard_map/all_gather | solution.py:101
  163.0 239.3 %reduce-scatter.4.cloned.1.call-start = ((), (), s32[]{:S(2)}) async-start(), calls=%async_computation.20 | async-start | bytes 5242880 | tf_op jit(solution)/shard_map/reduce_scatter | solution.py:105
  275.9 21.9 %collective-permute-start.26 = (bf16[64,2048]{1,0:T(8,128)(2,1)}, bf16[64,2048]{1,0:T(8,128)(2,1)}, u32[]{:S(2)}, u32[]{:S(2)}) collective-permute-start(bf16[64,2048]{1,0:T(8,128)(2,1)} %slice.347), channel_id=1, source_target_pairs={{0,1},{1,0},{2,3},{3,2},{4,5},{5,4},{6,7},{7,6},{8,9},{9,8},{10,11... | collective-permute-start | bytes 786440 | tf_op jit(solution)/shard_map/ppermute | solution.py:46
  277.8 21.7 %collective-permute-start.27 = (bf16[64,2048]{1,0:T(8,128)(2,1)}, bf16[64,2048]{1,0:T(8,128)(2,1)}, u32[]{:S(2)}, u32[]{:S(2)}) collective-permute-start(bf16[64,2048]{1,0:T(8,128)(2,1)} %slice.348), channel_id=1, source_target_pairs={{0,4},{4,0},{1,5},{5,1},{2,6},{6,2},{3,7},{7,3},{8,12},{12,8},{9,1... | collective-permute-start | bytes 786440 | tf_op jit(solution)/shard_map/ppermute | solution.py:46
  317.5 170.5 %reduce-scatter.6.cloned.1.call-start = ((), (), s32[]{:S(2)}) async-start(), calls=%async_computation.21 | async-start | bytes 5242880 | tf_op jit(solution)/shard_map/reduce_scatter | solution.py:105
  335.5 37.9 %collective-permute-start.41 = (bf16[512,2048]{1,0:T(8,128)(2,1)S(1)}, bf16[512,2048]{1,0:T(8,128)(2,1)S(1)}, u32[]{:S(2)}, u32[]{:S(2)}) collective-permute-start(bf16[512,2048]{1,0:T(8,128)(2,1)S(1)} %feed_down.1.refs_2_), channel_id=1, source_target_pairs={{0,2},{2,0},{1,3},{3,1},{4,6},{6,4},{5,7},{7,5},{8,10},{10,8},{9,1... | collective-permute-start | bytes 6291464 | tf_op jit(solution)/shard_map/ppermute | solution.py:46
  454.9 20.2 %collective-permute-start.57 = (bf16[512,2048]{1,0:T(8,128)(2,1)}, bf16[512,2048]{1,0:T(8,128)(2,1)}, u32[]{:S(2)}, u32[]{:S(2)}) collective-permute-start(bf16[512,2048]{1,0:T(8,128)(2,1)} %get-tuple-element.235.refs_6_), channel_id=1, source_target_pairs={{0,2},{2,0},{1,3},{3,1},{4,6},{6,4},{5,7},{7,5},{8,10},{10,8},{9,1... | collective-permute-start | bytes 6291464 | tf_op jit(solution)/shard_map/ppermute | solution.py:46
  466.7 21.3 %collective-permute-start.54 = (bf16[128,2048]{1,0:T(8,128)(2,1)}, bf16[128,2048]{1,0:T(8,128)(2,1)}, u32[]{:S(2)}, u32[]{:S(2)}) collective-permute-start(bf16[128,2048]{1,0:T(8,128)(2,1)} %get-tuple-element.227), channel_id=1, source_target_pairs={{0,4},{4,0},{1,5},{5,1},{2,6},{6,2},{3,7},{7,3},{8,12},{12,8},{9,1... | collective-permute-start | bytes 1572872 | tf_op jit(solution)/shard_map/ppermute | solution.py:46
  468.2 19.8 %all-to-all-start.6 = ((bf16[8,16,1024]{2,1,0:T(8,128)(2,1)}), bf16[8,16,1024]{2,1,0:T(8,128)(2,1)S(1)}, u32[]{:S(2)}, u32[]{:S(2)}) async-start(bf16[8,16,1024]{2,1,0:T(8,128)(2,1)} %bitcast.30), calls=%async_computation.7 | async-start | bytes 524288 | tf_op jit(solution)/shard_map/all_to_all | solution.py:50
  472.3 153.0 %reduce-scatter.8.cloned.1.call-start = ((), (), s32[]{:S(2)}) async-start(), calls=%async_computation.22 | async-start | bytes 7864320 | tf_op jit(solution)/shard_map/reduce_scatter | solution.py:105
  505.8 25.2 %all-to-all-start.8 = ((bf16[8,64,1024]{2,1,0:T(8,128)(2,1)}), bf16[8,64,1024]{2,1,0:T(8,128)(2,1)}, u32[]{:S(2)}, u32[]{:S(2)}) async-start(bf16[8,64,1024]{2,1,0:T(8,128)(2,1)} %broadcast_in_dim.12), calls=%async_computation.9 | async-start | bytes 2097152 | tf_op jit(solution)/shard_map/all_to_all | solution.py:50
  535.6 30.9 %all-to-all-start.9 = ((bf16[8,64,1024]{2,1,0:T(8,128)(2,1)}), bf16[8,64,1024]{2,1,0:T(8,128)(2,1)}, u32[]{:S(2)}, u32[]{:S(2)}) async-start(bf16[8,64,1024]{2,1,0:T(8,128)(2,1)} %copy-done.28), calls=%async_computation.10 | async-start | bytes 2097152 | tf_op jit(solution)/shard_map/all_to_all | solution.py:50
  540.0 25.5 %collective-permute-start.63 = (bf16[128,2048]{1,0:T(8,128)(2,1)S(1)}, bf16[128,2048]{1,0:T(8,128)(2,1)S(1)}, u32[]{:S(2)}, u32[]{:S(2)}) collective-permute-start(bf16[128,2048]{1,0:T(8,128)(2,1)S(1)} %pad_maximum_fusion.12), channel_id=1, source_target_pairs={{0,1},{1,0},{2,3},{3,2},{4,5},{5,4},{6,7},{7,6},{8,9},{9,8},{10,11... | collective-permute-start | bytes 1572872 | tf_op jit(solution)/shard_map/ppermute | solution.py:46
  543.0 22.7 %collective-permute-start.61 = (bf16[128,2048]{1,0:T(8,128)(2,1)S(1)}, bf16[128,2048]{1,0:T(8,128)(2,1)S(1)}, u32[]{:S(2)}, u32[]{:S(2)}) collective-permute-start(bf16[128,2048]{1,0:T(8,128)(2,1)S(1)} %pad_maximum_fusion.11), channel_id=1, source_target_pairs={{0,4},{4,0},{1,5},{5,1},{2,6},{6,2},{3,7},{7,3},{8,12},{12,8},{9,1... | collective-permute-start | bytes 1572872 | tf_op jit(solution)/shard_map/ppermute | solution.py:46
  569.4 22.0 %collective-permute-start.64 = (bf16[64,2048]{1,0:T(8,128)(2,1)}, bf16[64,2048]{1,0:T(8,128)(2,1)S(1)}, u32[]{:S(2)}, u32[]{:S(2)}) collective-permute-start(bf16[64,2048]{1,0:T(8,128)(2,1)} %get-tuple-element.262), channel_id=1, source_target_pairs={{0,1},{1,0},{2,3},{3,2},{4,5},{5,4},{6,7},{7,6},{8,9},{9,8},{10,11... | collective-permute-start | bytes 786440 | tf_op jit(solution)/shard_map/ppermute | solution.py:46
  570.9 21.2 %collective-permute-start.65 = (bf16[64,2048]{1,0:T(8,128)(2,1)}, bf16[64,2048]{1,0:T(8,128)(2,1)}, u32[]{:S(2)}, u32[]{:S(2)}) collective-permute-start(bf16[64,2048]{1,0:T(8,128)(2,1)} %get-tuple-element.263), channel_id=1, source_target_pairs={{0,4},{4,0},{1,5},{5,1},{2,6},{6,2},{3,7},{7,3},{8,12},{12,8},{9,1... | collective-permute-start | bytes 786440 | tf_op jit(solution)/shard_map/ppermute | solution.py:46
  571.4 20.7 %collective-permute-start.66 = (bf16[64,2048]{1,0:T(8,128)(2,1)}, bf16[64,2048]{1,0:T(8,128)(2,1)}, u32[]{:S(2)}, u32[]{:S(2)}) collective-permute-start(bf16[64,2048]{1,0:T(8,128)(2,1)} %get-tuple-element.264), channel_id=1, source_target_pairs={{0,5},{1,4},{4,1},{5,0},{2,7},{3,6},{6,3},{7,2},{8,13},{9,12},{12,... | collective-permute-start | bytes 786440 | tf_op jit(solution)/shard_map/ppermute | solution.py:96
  594.4 19.1 %collective-permute-start.67 = (bf16[64,2048]{1,0:T(8,128)(2,1)}, bf16[64,2048]{1,0:T(8,128)(2,1)}, u32[]{:S(2)}, u32[]{:S(2)}) collective-permute-start(bf16[64,2048]{1,0:T(8,128)(2,1)} %get-tuple-element.273), channel_id=1, source_target_pairs={{0,1},{1,0},{2,3},{3,2},{4,5},{5,4},{6,7},{7,6},{8,9},{9,8},{10,11... | collective-permute-start | bytes 786440 | tf_op jit(solution)/shard_map/ppermute | solution.py:46
  595.8 17.7 %collective-permute-start.68 = (bf16[64,2048]{1,0:T(8,128)(2,1)}, bf16[64,2048]{1,0:T(8,128)(2,1)}, u32[]{:S(2)}, u32[]{:S(2)}) collective-permute-start(bf16[64,2048]{1,0:T(8,128)(2,1)} %get-tuple-element.274), channel_id=1, source_target_pairs={{0,4},{4,0},{1,5},{5,1},{2,6},{6,2},{3,7},{7,3},{8,12},{12,8},{9,1... | collective-permute-start | bytes 786440 | tf_op jit(solution)/shard_map/ppermute | solution.py:46
  596.5 17.1 %collective-permute-start.69 = (bf16[64,2048]{1,0:T(8,128)(2,1)}, bf16[64,2048]{1,0:T(8,128)(2,1)}, u32[]{:S(2)}, u32[]{:S(2)}) collective-permute-start(bf16[64,2048]{1,0:T(8,128)(2,1)} %get-tuple-element.275), channel_id=1, source_target_pairs={{0,5},{1,4},{4,1},{5,0},{2,7},{3,6},{6,3},{7,2},{8,13},{9,12},{12,... | collective-permute-start | bytes 786440 | tf_op jit(solution)/shard_map/ppermute | solution.py:96
  629.9 19.4 %collective-permute-start.73 = (bf16[64,3072]{1,0:T(8,128)(2,1)}, bf16[64,3072]{1,0:T(8,128)(2,1)}, u32[]{:S(2)}, u32[]{:S(2)}) collective-permute-start(bf16[64,3072]{1,0:T(8,128)(2,1)} %get-tuple-element.292), channel_id=1, source_target_pairs={{0,5},{1,4},{4,1},{5,0},{2,7},{3,6},{6,3},{7,2},{8,13},{9,12},{12,... | collective-permute-start | bytes 1179656 | tf_op jit(solution)/shard_map/ppermute | solution.py:96
  (134 other events, 1716.3 us)
Sparse Core Ops, SparseCore 0:
  23.7 66.1 all-gather.4
  91.5 68.8 all-gather.6
  162.1 80.5 all-gather.8
  244.2 80.5 all-gather.10
  326.9 75.2 reduce-scatter.3
  404.5 80.0 reduce-scatter.5
  488.2 114.9 reduce-scatter.7

commit v30 on v27

--- a/solution.py
+++ b/solution.py
@@ -667,39 +667,61 @@
     )
 
 
-def finish_all(parts, text_grad, rank):
+def finish_attention(parts, rank):
     rows, total = parts[0].shape
-    width = total // 6
+    width = total // 4
 
     def kernel(r, *refs):
-        key, value, three, out, cross, cross_out = refs[4:]
+        three, out = refs[4:]
         for k in range(4):
 
             @pl.when(pl.program_id(0) == k)
             def _():
-                def part(j):
-                    return refs[k][:, j * width : (j + 1) * width].astype(F32)
-
                 for j in range(3):
-                    three[j] = part(j)
-                out[...] = part(3)
-                cross[0] = part(4)
-                cross_out[...] = part(5)
-
-        cross[1] = key[...]
-        cross[2] = value[...]
-
-    wide = pl.BlockSpec((3, rows, width), lambda k, r: (0, 0, k ^ r[0]))
+                    three[j] = refs[k][:, j * width : (j + 1) * width].astype(F32)
+                out[...] = refs[k][:, 3 * width :].astype(F32)
+
+    return call(
+        kernel,
+        (4,),
+        [whole(p) for p in parts],
+        [
+            pl.BlockSpec((3, rows, width), lambda k, r: (0, 0, k ^ r[0])),
+            pl.BlockSpec((rows, width), lambda k, r: (0, k ^ r[0])),
+        ],
+        [shape((3, rows, 4 * width), F32), shape((rows, 4 * width), F32)],
+        parts,
+        "finish_attention",
+        rank=rank,
+    )
+
+
+def finish_cross(parts, text_grad, rank):
+    rows, total = parts[0].shape
+    width = total // 2
+
+    def kernel(r, *refs):
+        key, value, three, out = refs[4:]
+        for k in range(4):
+
+            @pl.when(pl.program_id(0) == k)
+            def _():
+                three[0] = refs[k][:, :width].astype(F32)
+                out[...] = refs[k][:, width:].astype(F32)
+
+        three[1] = key[...]
+        three[2] = value[...]
+
     flat = pl.BlockSpec((rows, width), lambda k, r: (0, k ^ r[0]))
     return call(
         kernel,
         (4,),
         [whole(p) for p in parts]
         + [flat, pl.BlockSpec((rows, width), lambda k, r: (0, 4 + (k ^ r[0])))],
-        [wide, flat, wide, flat],
-        [shape((3, rows, 4 * width), F32), shape((rows, 4 * width), F32)] * 2,
+        [pl.BlockSpec((3, rows, width), lambda k, r: (0, 0, k ^ r[0])), flat],
+        [shape((3, rows, 4 * width), F32), shape((rows, 4 * width), F32)],
         [*parts, text_grad, text_grad],
-        "finish_all",
+        "finish_cross",
         rank=rank,
     )
 
@@ -973,21 +995,19 @@
         )
         kv_part = trade(kv_part, DATA)
         result = scatter_second(result)
-        rest_part = grad_products(
-            [
-                (early[0], both(grad_projected)),
-                (both(attn_branch), early[1]),
-                (early[2], grad_cq_both),
-                (cross_branch, early[3]),
-            ],
+        attn_part = grad_products(
+            [(early[0], both(grad_projected)), (both(attn_branch), early[1])],
             "attention_grads",
             *halves,
         )
-        grad_projected, result, kv_part, rest_part = lax.optimization_barrier(
-            (grad_projected, result, kv_part, rest_part)
-        )
-        rest_part, up_rows = lax.optimization_barrier((rest_part, up_rows))
-        rest_rows = scatter_grad(rest_part, grad_axes)
+        grad_projected, result, kv_part, attn_part, cross_branch = lax.optimization_barrier(
+            (grad_projected, result, kv_part, attn_part, cross_branch)
+        )
+        attn_part, up_rows = lax.optimization_barrier((attn_part, up_rows))
+        attn_rows = scatter_grad(attn_part, grad_axes)
+        cross_part = grad_products(
+            [(early[2], grad_cq_both), (cross_branch, early[3])], "cross_grads", *halves
+        )
         parts = mm_scatter(grad_projected, first)
         grad_hidden, gain_grad_a, mask_grad = last_back(
             parts,
@@ -1010,9 +1030,10 @@
         half_context = caption.shape[0] // 2
         caption_part = trade(caption_part, PLANE)
         output = layer_output(after_cross, result, unit, order)
-        caption_part, output, down_rows, up_rows = lax.optimization_barrier(
-            (caption_part, output, down_rows, up_rows)
-        )
+        caption_part, output, down_rows, up_rows, attn_rows, cross_part = lax.optimization_barrier(
+            (caption_part, output, down_rows, up_rows, attn_rows, cross_part)
+        )
+        cross_rows = scatter_grad(cross_part, grad_axes)
 
         caption_part = caption_part.astype(F32).sum(axis=0)
         sums = layer_order(add_z(whole_of(caption_part[half_context:], width)))
@@ -1033,15 +1054,17 @@
 
         caption_part = spread(caption_part)
         up_grad = finish_wide(up_parts, rank)
-        caption_part, rest_rows, up_grad = lax.optimization_barrier(
-            (caption_part, rest_rows, up_grad)
+        attn_parts = swap_parts(pick_rows([attn_rows], rank))
+        caption_part, cross_rows, up_grad, attn_parts = lax.optimization_barrier(
+            (caption_part, cross_rows, up_grad, attn_parts)
         )
         grad_caption = caption_output(caption_part, swap(caption_part, "c"), core)
-        rest_rows = swap_parts(pick_rows([rest_rows], rank))
-        grad_caption, rest_rows = lax.optimization_barrier((grad_caption, rest_rows))
-        qkv_grad, out_grad, grad_cross, cross_out_grad = finish_all(
-            rest_rows, kv_weight_grad, rank
-        )
+        qkv_grad, out_grad = finish_attention(attn_parts, rank)
+        cross_rows = swap_parts(pick_rows([cross_rows], rank))
+        grad_caption, qkv_grad, out_grad, cross_rows = lax.optimization_barrier(
+            (grad_caption, qkv_grad, out_grad, cross_rows)
+        )
+        grad_cross, cross_out_grad = finish_cross(cross_rows, kv_weight_grad, rank)
         return (
             outer(output).reshape(hidden.shape),
             outer(grad_hidden).reshape(hidden.shape),

time: 651 us -> 663 us (1.018)
  waiting for transfers between devices: 208 us -> 221 us
    ppermute x70 -> x72, waiting for transfers between devices: 146 us -> 160 us  [swap(): return lax.ppermute(values, axis, PAIR)]
    all_to_all x6, waiting for transfers between devices: 39.7 us -> 27.5 us  [trade(): return lax.all_to_all(blocks, axes, 0, 0, tiled=True)]
    reduce_scatter x3 -> x4, waiting for transfers between devices: 4.46 us -> 12.7 us  [scatter_grad(): summed = lax.psum_scatter(partial, axes, scatter_dimension=0, tiled=True)]
    ppermute x70 -> x72, starting transfers between devices: 75.9 us -> 79.5 us  [swap(): return lax.ppermute(values, axis, PAIR)]
    pallas_call x12 -> x15, Pallas kernels: 42.7 us -> 45.4 us  [call(): pl.pallas_call(kernel, grid_spec=spec, **options)]
  transfers between devices with their start and end apart: 89 -> 93, of which waited for: 47 -> 50; matrix products, arithmetic and copies ran while one was open for 11% -> 10% of each run, Pallas kernels for 17% -> 17%
where the time goes in v30:
time: 663 us; the launch traced here: 655 us
  waiting for transfers between devices  221 us (33%)
  Pallas kernels  118 us (18%)
  starting transfers between devices  108 us (16%)
  blocking collectives  106 us (16%)
  local copies, waits for them, and re-layouts  45.8 us (7%)
  matrix products  32.6 us (5%)
  between operations  16.5 us (2%)
  other arithmetic  8.14 us (1%)
    ppermute x72, waiting for transfers between devices, swap(): return lax.ppermute(values, axis, PAIR)  160 us
    all_to_all x7, blocking collectives, trade(): return lax.all_to_all(blocks, axes, 0, 0, tiled=True)  106 us
    ppermute x72, starting transfers between devices, swap(): return lax.ppermute(values, axis, PAIR)  79.5 us
    pallas_call x19, Pallas kernels, call(): pl.pallas_call(kernel, grid=grid, in_specs=in_specs, out_specs=out_specs,...  72.7 us
    pallas_call x15, Pallas kernels, call(): pl.pallas_call(kernel, grid_spec=spec, **options)  45.4 us
    dot_general x6, matrix products, dot(): return lax.dot_general(a, b, (dims, ((), ())), preferred_element_type=F32)  32.6 us
    all_to_all x6, waiting for transfers between devices, trade(): return lax.all_to_all(blocks, axes, 0, 0, tiled=True)  27.5 us
    unnamed x132, local copies, waits for them, and re-layouts  23.5 us
  transfers between devices with their start and end apart: 93, of which 50 were waited for; matrix products, arithmetic and copies ran while one was open for 10% of the time, Pallas kernels for 17%

profile of v30, /device:TPU:0, one launch (start us, length us, event | category | flops | bytes accessed | tf_op | source)
XLA Modules:
  0.0 655.4 jit_solution(7770956444723342540)
XLA Ops:
  31.0 9.6 %collective-permute-done.1.refs_2_ = bf16[128,2048]{1,0:T(8,128)(2,1)S(1)} collective-permute-done((bf16[128,2048]{1,0:T(8,128)(2,1)S(1)}, bf16[128,2048]{1,0:T(8,128)(2,1)S(1)}, u32[]{:S(2)}, u32[]{:S(2)}) %collective-permute-start.1) | collective-permute-done | bytes 524320 | tf_op jit(solution)/shard_map/ppermute | solution.py:46
  53.1 12.2 %all_to_all.65 = bf16[4,64,1536]{2,1,0:T(8,128)(2,1)} all-to-all(bf16[4,64,1536]{2,1,0:T(8,128)(2,1)S(1)} %copy.75), channel_id=1, replica_groups=mesh['z'=4,'x'=2,'c'=2,'y'=2] {'x','y'}, dimensions={0} | all-to-all | bytes 1572864 | tf_op jit(solution)/shard_map/all_to_all | solution.py:50
  65.3 15.0 %all_to_all.66 = bf16[4,64,2048]{2,1,0:T(8,128)(2,1)} all-to-all(bf16[4,64,2048]{2,1,0:T(8,128)(2,1)} %bitcast.92), channel_id=1, replica_groups=mesh['z'=4,'x'=2,'c'=2,'y'=2] {'x','y'}, dimensions={0} | all-to-all | bytes 2097152 | tf_op jit(solution)/shard_map/all_to_all | solution.py:50
  81.7 16.9 %all_to_all.67 = bf16[8,64,1024]{2,1,0:T(8,128)(2,1)S(1)} all-to-all(bf16[8,64,1024]{2,1,0:T(8,128)(2,1)S(1)} %get-tuple-element.173), channel_id=1, replica_groups=mesh['z'=4,'x'=2,'c'=2,'y'=2] {'x','c','y'}, dimensions={0} | all-to-all | bytes 2097152 | tf_op jit(solution)/shard_map/all_to_all | solution.py:50
  98.8 16.5 %all_to_all.68 = bf16[4,16,1024]{2,1,0:T(8,128)(2,1)S(1)} all-to-all(bf16[4,16,1024]{2,1,0:T(8,128)(2,1)S(1)} %bitcast.103), channel_id=1, replica_groups=mesh['z'=4,'x'=2,'c'=2,'y'=2] {'z'}, dimensions={0} | all-to-all | bytes 262144 | tf_op jit(solution)/shard_map/all_to_all | solution.py:50
  115.4 12.9 %all_to_all.69 = bf16[4,16,1024]{2,1,0:T(8,128)(2,1)S(1)} all-to-all(bf16[4,16,1024]{2,1,0:T(8,128)(2,1)S(1)} %broadcast_in_dim.12), channel_id=1, replica_groups=mesh['z'=4,'x'=2,'c'=2,'y'=2] {'z'}, dimensions={0} | all-to-all | bytes 262144 | tf_op jit(solution)/shard_map/all_to_all | solution.py:50
  132.6 7.9 %qkv_mm.1 = (bf16[512,2048]{1,0:T(8,128)(2,1)}, bf16[512,1536]{1,0:T(8,128)(2,1)S(1)}) custom-call(bf16[128,2048]{1,0:T(8,128)(2,1)S(1)} %copy-done.41, bf16[128,2048]{1,0:T(8,128)(2,1)S(1)} %collective-permute-done.refs_1_, bf16[128,2048]{1,0:T(8,128)(2,1)S(1)} %collective-permute-done.1.refs_2_, bf16[64,2048]{1,0:T(8,128)(2,1)S(1)} %copy-done.45, ...), custom_call_target="tpu_custom_call" | custom-call | flops 3221225472 | bytes 10485760 | tf_op jit(solution)/shard_map/qkv_mm/pallas_call | solution.py:118
  143.5 18.2 %all_to_all.70 = bf16[4,64,2048]{2,1,0:T(8,128)(2,1)} all-to-all(bf16[4,64,2048]{2,1,0:T(8,128)(2,1)S(1)} %bitcast.91), channel_id=1, replica_groups=mesh['z'=4,'x'=2,'c'=2,'y'=2] {'x','y'}, dimensions={0} | all-to-all | bytes 2097152 | tf_op jit(solution)/shard_map/all_to_all | solution.py:50
  176.2 10.9 %collective-permute-done.11.refs_3_ = bf16[128,2048]{1,0:T(8,128)(2,1)S(1)} collective-permute-done((bf16[128,2048]{1,0:T(8,128)(2,1)S(1)}, bf16[128,2048]{1,0:T(8,128)(2,1)S(1)}, u32[]{:S(2)}, u32[]{:S(2)}) %collective-permute-start.11) | collective-permute-done | bytes 524320 | tf_op jit(solution)/shard_map/ppermute | solution.py:46
  190.6 10.1 %collective-permute-done.13.refs_2_ = bf16[128,2048]{1,0:T(8,128)(2,1)S(1)} collective-permute-done((bf16[128,2048]{1,0:T(8,128)(2,1)S(1)}, bf16[128,2048]{1,0:T(8,128)(2,1)S(1)}, u32[]{:S(2)}, u32[]{:S(2)}) %collective-permute-start.13) | collective-permute-done | bytes 524320 | tf_op jit(solution)/shard_map/ppermute | solution.py:46
  245.1 10.0 %collective-permute-done.21.refs_2_ = bf16[128,2048]{1,0:T(8,128)(2,1)S(1)} collective-permute-done((bf16[128,2048]{1,0:T(8,128)(2,1)S(1)}, bf16[128,2048]{1,0:T(8,128)(2,1)S(1)}, u32[]{:S(2)}, u32[]{:S(2)}) %collective-permute-start.21) | collective-permute-done | bytes 524320 | tf_op jit(solution)/shard_map/ppermute | solution.py:46
  267.6 8.9 %collective-permute-done.25 = bf16[128,2048]{1,0:T(8,128)(2,1)S(1)} collective-permute-done((bf16[128,2048]{1,0:T(8,128)(2,1)S(1)}, bf16[128,2048]{1,0:T(8,128)(2,1)S(1)}, u32[]{:S(2)}, u32[]{:S(2)}) %collective-permute-start.25) | collective-permute-done | bytes 524320 | tf_op jit(solution)/shard_map/ppermute | solution.py:46
  286.0 11.9 %feed_up.1 = (bf16[512,2048]{1,0:T(8,128)(2,1)}, bf16[512,2048]{1,0:T(8,128)(2,1)}, f32[512,2048]{1,0:T(8,128)}) custom-call(bf16[128,2048]{1,0:T(8,128)(2,1)S(1)} %copy-done.43, bf16[128,2048]{1,0:T(8,128)(2,1)S(1)} %copy-done.39, bf16[128,2048]{1,0:T(8,128)(2,1)S(1)} %collective-permute-done.21.refs_2_, bf16[64,2048]{1,0:T(8,128)(2,1)S(1)} %copy-done.49, ...), custom_call_target="tpu_custom_call" | custom-call | flops 4294967296 | bytes 12582912 | tf_op jit(solution)/shard_map/feed_up/pallas_call | solution.py:118
  309.0 8.7 %down_grads.1 = bf16[1024,2048]{1,0:T(8,128)(2,1)} custom-call(s32[1]{0:T(128)} %bitcast.25.r, bf16[512,2048]{1,0:T(8,128)(2,1)} %constant_dynamic-update-slice_fusion.refs_0_.dy, bf16[512,2048]{1,0:T(8,128)(2,1)S(1)} %collective-permute-done.28.refs_1_, bf16[512,2048]{1,0:T(8,128)(2,1)} %get-tuple-element.218.refs_2_, bf16[512,2048]{1,0:T(8,128)(2,1)} %copy-done.63), custom_call_target="tpu_custom_call" | custom-call | flops 4294967296 | bytes 16777216 | tf_op jit(solution)/shard_map/down_grads/pallas_call | solution.py:129
  324.8 10.7 %feed_down.1.refs_2_ = bf16[512,2048]{1,0:T(8,128)(2,1)S(1)} custom-call(bf16[512,2048]{1,0:T(8,128)(2,1)} %constant_dynamic-update-slice_fusion.refs_0_.dy, f32[512,2048]{1,0:T(8,128)} %get-tuple-element.205.slope_ref, bf16[2048,2048]{1,0:T(8,128)(2,1)} %all-gather.11.cloned.1.call-done.down), custom_call_target="tpu_custom_call" | custom-call | flops 4294967296 | bytes 25165824 | tf_op jit(solution)/shard_map/feed_down/pallas_call | solution.py:118
  335.8 8.6 %convolution_convert_fusion.3 = bf16[512,2048]{1,0:T(8,128)(2,1)S(1)} fusion(bf16[512,2048]{1,0:T(8,128)(2,1)S(1)} %feed_down.1.refs_2_, bf16[2048,2048]{1,0:T(8,128)(2,1)} %all-gather.9.cloned.1.call-done.refs_5_), kind=kOutput, calls=%fused_computation.3 | convolution fusion | flops 4296015872 | bytes 12582912 | tf_op jit(solution)/shard_map/dot_general | solution.py:26
  356.7 10.9 %collective-permute-done.38.refs_2_ = bf16[128,2048]{1,0:T(8,128)(2,1)S(1)} collective-permute-done((bf16[128,2048]{1,0:T(8,128)(2,1)S(1)}, bf16[128,2048]{1,0:T(8,128)(2,1)S(1)}, u32[]{:S(2)}, u32[]{:S(2)}) %collective-permute-start.38) | collective-permute-done | bytes 524320 | tf_op jit(solution)/shard_map/ppermute | solution.py:46
  374.7 8.7 %up_grads.1 = bf16[1024,2048]{1,0:T(8,128)(2,1)} custom-call(s32[1]{0:T(128)} %bitcast.25.r, bf16[512,2048]{1,0:T(8,128)(2,1)} %get-tuple-element.209.refs_0_, bf16[512,2048]{1,0:T(8,128)(2,1)} %collective-permute-done.34.refs_1_, bf16[512,2048]{1,0:T(8,128)(2,1)} %copy-done.21, bf16[512,2048]{1,0:T(8,128)(2,1)} %copy-done.62), custom_call_target="tpu_custom_call" | custom-call | flops 4294967296 | bytes 16777216 | tf_op jit(solution)/shard_map/up_grads/pallas_call | solution.py:129
  417.0 10.3 %collective-permute-done.47.refs_2_ = bf16[128,2048]{1,0:T(8,128)(2,1)S(1)} collective-permute-done((bf16[128,2048]{1,0:T(8,128)(2,1)S(1)}, bf16[128,2048]{1,0:T(8,128)(2,1)S(1)}, u32[]{:S(2)}, u32[]{:S(2)}) %collective-permute-start.47) | collective-permute-done | bytes 524320 | tf_op jit(solution)/shard_map/ppermute | solution.py:46
  433.1 8.5 %convolution_convert_fusion.1 = bf16[512,2048]{1,0:T(8,128)(2,1)S(1)} fusion(bf16[512,2048]{1,0:T(8,128)(2,1)S(1)} %copy-done.61, bf16[2048,2048]{1,0:T(8,128)(2,1)} %all-gather.11.cloned.1.call-done.down), kind=kOutput, calls=%fused_computation.1 | convolution fusion | flops 4296015872 | bytes 12582912 | tf_op jit(solution)/shard_map/dot_general | solution.py:26
  473.9 8.2 %attention_grads.1 = bf16[1024,2048]{1,0:T(8,128)(2,1)} custom-call(s32[1]{0:T(128)} %bitcast.25.r, bf16[512,2048]{1,0:T(8,128)(2,1)} %get-tuple-element.238.refs_0_, bf16[512,2048]{1,0:T(8,128)(2,1)} %collective-permute-done.30.refs_1_, bf16[512,2048]{1,0:T(8,128)(2,1)} %get-tuple-element.240.refs_2_, bf16[512,2048]{1,0:T(8,128)(2,1)} %collective-permute-done.56.refs_3_, ...), custom_call_target="tpu_custom_call" | custom-call | flops 4294967296 | bytes 16777216 | tf_op jit(solution)/shard_map/attention_grads/pallas_call | solution.py:129
  559.4 8.3 %reduce-scatter.9.cloned.1.call-done = bf16[256,2048]{1,0:T(8,128)(2,1)} async-done(((bf16[1024,2048]{1,0:T(8,128)(2,1)}), bf16[256,2048]{1,0:T(8,128)(2,1)}) %reduce-scatter.9.cloned.1.call-update) | async-done | bytes 1048592 | tf_op jit(solution)/shard_map/reduce_scatter | solution.py:105
  573.1 14.1 %all_to_all.71 = bf16[4,16,1024]{2,1,0:T(8,128)(2,1)S(1)} all-to-all(bf16[4,16,1024]{2,1,0:T(8,128)(2,1)S(1)} %bitcast.104), channel_id=1, replica_groups=mesh['z'=4,'x'=2,'c'=2,'y'=2] {'z'}, dimensions={0} | all-to-all | bytes 262144 | tf_op jit(solution)/shard_map/all_to_all | solution.py:50
  597.6 8.5 %all-to-all-done.11 = bf16[4,16,1024]{2,1,0:T(8,128)(2,1)S(1)} async-done(((bf16[4,16,1024]{2,1,0:T(8,128)(2,1)}), bf16[4,16,1024]{2,1,0:T(8,128)(2,1)S(1)}, u32[]{:S(2)}, u32[]{:S(2)}) %all-to-all-start.11) | async-done | bytes 131104 | tf_op jit(solution)/shard_map/all_to_all | solution.py:50
  (437 shorter events, 372.4 us)
Async XLA Ops:
  7.2 123.5 %all-gather.5.cloned.1.call-start = ((), (), s32[]{:S(2)}) async-start(), calls=%async_computation.17 | async-start | bytes 7077888 | tf_op jit(solution)/shard_map/all_gather | solution.py:101
  23.6 138.5 %all-gather.7.cloned.1.call-start = ((), (), s32[]{:S(2)}) async-start(), calls=%async_computation.18 | async-start | bytes 7077888 | tf_op jit(solution)/shard_map/all_gather | solution.py:101
  65.2 216.7 %all-gather.9.cloned.1.call-start = ((), (), s32[]{:S(2)}) async-start(), calls=%async_computation.19 | async-start | bytes 9437184 | tf_op jit(solution)/shard_map/all_gather | solution.py:101
  80.3 244.4 %all-gather.11.cloned.1.call-start = ((), (), s32[]{:S(2)}) async-start(), calls=%async_computation.20 | async-start | bytes 9437184 | tf_op jit(solution)/shard_map/all_gather | solution.py:101
  161.8 240.5 %reduce-scatter.5.cloned.1.call-start = ((), (), s32[]{:S(2)}) async-start(), calls=%async_computation.21 | async-start | bytes 5242880 | tf_op jit(solution)/shard_map/reduce_scatter | solution.py:105
  277.2 20.8 %collective-permute-start.26 = (bf16[64,2048]{1,0:T(8,128)(2,1)}, bf16[64,2048]{1,0:T(8,128)(2,1)}, u32[]{:S(2)}, u32[]{:S(2)}) collective-permute-start(bf16[64,2048]{1,0:T(8,128)(2,1)} %slice.347), channel_id=1, source_target_pairs={{0,1},{1,0},{2,3},{3,2},{4,5},{5,4},{6,7},{7,6},{8,9},{9,8},{10,11... | collective-permute-start | bytes 786440 | tf_op jit(solution)/shard_map/ppermute | solution.py:46
  278.5 21.2 %collective-permute-start.27 = (bf16[64,2048]{1,0:T(8,128)(2,1)}, bf16[64,2048]{1,0:T(8,128)(2,1)}, u32[]{:S(2)}, u32[]{:S(2)}) collective-permute-start(bf16[64,2048]{1,0:T(8,128)(2,1)} %slice.348), channel_id=1, source_target_pairs={{0,4},{4,0},{1,5},{5,1},{2,6},{6,2},{3,7},{7,3},{8,12},{12,8},{9,1... | collective-permute-start | bytes 786440 | tf_op jit(solution)/shard_map/ppermute | solution.py:46
  318.4 168.1 %reduce-scatter.7.cloned.1.call-start = ((), (), s32[]{:S(2)}) async-start(), calls=%async_computation.22 | async-start | bytes 5242880 | tf_op jit(solution)/shard_map/reduce_scatter | solution.py:105
  335.5 37.9 %collective-permute-start.41 = (bf16[512,2048]{1,0:T(8,128)(2,1)S(1)}, bf16[512,2048]{1,0:T(8,128)(2,1)S(1)}, u32[]{:S(2)}, u32[]{:S(2)}) collective-permute-start(bf16[512,2048]{1,0:T(8,128)(2,1)S(1)} %feed_down.1.refs_2_), channel_id=1, source_target_pairs={{0,2},{2,0},{1,3},{3,1},{4,6},{6,4},{5,7},{7,5},{8,10},{10,8},{9,1... | collective-permute-start | bytes 6291464 | tf_op jit(solution)/shard_map/ppermute | solution.py:46
  455.0 27.1 %collective-permute-start.58 = (bf16[512,2048]{1,0:T(8,128)(2,1)}, bf16[512,2048]{1,0:T(8,128)(2,1)}, u32[]{:S(2)}, u32[]{:S(2)}) collective-permute-start(bf16[512,2048]{1,0:T(8,128)(2,1)} %get-tuple-element.263.refs_2_), channel_id=1, source_target_pairs={{0,2},{2,0},{1,3},{3,1},{4,6},{6,4},{5,7},{7,5},{8,10},{10,8},{9,1... | collective-permute-start | bytes 6291464 | tf_op jit(solution)/shard_map/ppermute | solution.py:46
  466.3 20.2 %collective-permute-start.54 = (bf16[128,2048]{1,0:T(8,128)(2,1)}, bf16[128,2048]{1,0:T(8,128)(2,1)}, u32[]{:S(2)}, u32[]{:S(2)}) collective-permute-start(bf16[128,2048]{1,0:T(8,128)(2,1)} %get-tuple-element.235), channel_id=1, source_target_pairs={{0,4},{4,0},{1,5},{5,1},{2,6},{6,2},{3,7},{7,3},{8,12},{12,8},{9,1... | collective-permute-start | bytes 1572872 | tf_op jit(solution)/shard_map/ppermute | solution.py:46
  467.8 18.7 %collective-permute-start.55 = (bf16[128,2048]{1,0:T(8,128)(2,1)}, bf16[128,2048]{1,0:T(8,128)(2,1)}, u32[]{:S(2)}, u32[]{:S(2)}) collective-permute-start(bf16[128,2048]{1,0:T(8,128)(2,1)} %get-tuple-element.236), channel_id=1, source_target_pairs={{0,1},{1,0},{2,3},{3,2},{4,5},{5,4},{6,7},{7,6},{8,9},{9,8},{10,11... | collective-permute-start | bytes 1572872 | tf_op jit(solution)/shard_map/ppermute | solution.py:46
  473.8 93.8 %reduce-scatter.9.cloned.1.call-start = ((), (), s32[]{:S(2)}) async-start(), calls=%async_computation.23 | async-start | bytes 5242880 | tf_op jit(solution)/shard_map/reduce_scatter | solution.py:105
  512.5 19.6 %all-to-all-start.8 = ((bf16[8,64,1024]{2,1,0:T(8,128)(2,1)}), bf16[8,64,1024]{2,1,0:T(8,128)(2,1)}, u32[]{:S(2)}, u32[]{:S(2)}) async-start(bf16[8,64,1024]{2,1,0:T(8,128)(2,1)} %broadcast_in_dim.15), calls=%async_computation.9 | async-start | bytes 2097152 | tf_op jit(solution)/shard_map/all_to_all | solution.py:50
  537.7 21.8 %all-to-all-start.9 = ((bf16[8,80,1024]{2,1,0:T(8,128)(2,1)}), bf16[8,80,1024]{2,1,0:T(8,128)(2,1)}, u32[]{:S(2)}, u32[]{:S(2)}) async-start(bf16[8,80,1024]{2,1,0:T(8,128)(2,1)} %copy-done.22), calls=%async_computation.10 | async-start | bytes 2621440 | tf_op jit(solution)/shard_map/all_to_all | solution.py:50
  542.1 83.1 %reduce-scatter.11.cloned.1.call-start = ((), (), s32[]{:S(2)}) async-start(), calls=%async_computation.24 | async-start | bytes 2621440 | tf_op jit(solution)/shard_map/reduce_scatter | solution.py:105
  567.9 19.2 %collective-permute-start.64 = (bf16[64,2048]{1,0:T(8,128)(2,1)S(1)}, bf16[64,2048]{1,0:T(8,128)(2,1)S(1)}, u32[]{:S(2)}, u32[]{:S(2)}) collective-permute-start(bf16[64,2048]{1,0:T(8,128)(2,1)S(1)} %get-tuple-element.272), channel_id=1, source_target_pairs={{0,1},{1,0},{2,3},{3,2},{4,5},{5,4},{6,7},{7,6},{8,9},{9,8},{10,11... | collective-permute-start | bytes 786440 | tf_op jit(solution)/shard_map/ppermute | solution.py:46
  569.5 17.7 %collective-permute-start.65 = (bf16[64,2048]{1,0:T(8,128)(2,1)S(1)}, bf16[64,2048]{1,0:T(8,128)(2,1)S(1)}, u32[]{:S(2)}, u32[]{:S(2)}) collective-permute-start(bf16[64,2048]{1,0:T(8,128)(2,1)S(1)} %get-tuple-element.273), channel_id=1, source_target_pairs={{0,4},{4,0},{1,5},{5,1},{2,6},{6,2},{3,7},{7,3},{8,12},{12,8},{9,1... | collective-permute-start | bytes 786440 | tf_op jit(solution)/shard_map/ppermute | solution.py:46
  588.2 17.9 %collective-permute-start.67 = (bf16[64,2048]{1,0:T(8,128)(2,1)}, bf16[64,2048]{1,0:T(8,128)(2,1)S(1)}, u32[]{:S(2)}, u32[]{:S(2)}) collective-permute-start(bf16[64,2048]{1,0:T(8,128)(2,1)} %get-tuple-element.279), channel_id=1, source_target_pairs={{0,1},{1,0},{2,3},{3,2},{4,5},{5,4},{6,7},{7,6},{8,9},{9,8},{10,11... | collective-permute-start | bytes 786440 | tf_op jit(solution)/shard_map/ppermute | solution.py:46
  607.0 18.2 %all-to-all-start.12 = ((bf16[4,64,1024]{2,1,0:T(8,128)(2,1)}), bf16[4,64,1024]{2,1,0:T(8,128)(2,1)S(1)}, u32[]{:S(2)}, u32[]{:S(2)}) async-start(bf16[4,64,1024]{2,1,0:T(8,128)(2,1)} %broadcast_in_dim.17), calls=%async_computation.15 | async-start | bytes 1048576 | tf_op jit(solution)/shard_map/all_to_all | solution.py:50
  625.2 17.9 %collective-permute-start.73 = (bf16[4,64,1024]{2,1,0:T(8,128)(2,1)S(1)}, bf16[4,64,1024]{2,1,0:T(8,128)(2,1)S(1)}, u32[]{:S(2)}, u32[]{:S(2)}) collective-permute-start(bf16[4,64,1024]{2,1,0:T(8,128)(2,1)S(1)} %all-to-all-done.12.own_ref), channel_id=1, source_target_pairs={{0,2},{2,0},{1,3},{3,1},{4,6},{6,4},{5,7},{7,5},{8,10},{10,8},{9,1... | collective-permute-start | bytes 1572872 | tf_op jit(solution)/shard_map/ppermute | solution.py:46
  626.4 19.6 %collective-permute-start.74 = (bf16[64,1024]{1,0:T(8,128)(2,1)S(1)}, bf16[64,1024]{1,0:T(8,128)(2,1)S(1)}, u32[]{:S(2)}, u32[]{:S(2)}) collective-permute-start(bf16[64,1024]{1,0:T(8,128)(2,1)S(1)} %get-tuple-element.306), channel_id=1, source_target_pairs={{0,1},{1,0},{2,3},{3,2},{4,5},{5,4},{6,7},{7,6},{8,9},{9,8},{10,11... | collective-permute-start | bytes 393224 | tf_op jit(solution)/shard_map/ppermute | solution.py:46
  627.0 19.0 %collective-permute-start.75 = (bf16[64,1024]{1,0:T(8,128)(2,1)S(1)}, bf16[64,1024]{1,0:T(8,128)(2,1)S(1)}, u32[]{:S(2)}, u32[]{:S(2)}) collective-permute-start(bf16[64,1024]{1,0:T(8,128)(2,1)S(1)} %get-tuple-element.307), channel_id=1, source_target_pairs={{0,4},{4,0},{1,5},{5,1},{2,6},{6,2},{3,7},{7,3},{8,12},{12,8},{9,1... | collective-permute-start | bytes 393224 | tf_op jit(solution)/shard_map/ppermute | solution.py:46
  627.3 18.8 %collective-permute-start.76 = (bf16[64,1024]{1,0:T(8,128)(2,1)S(1)}, bf16[64,1024]{1,0:T(8,128)(2,1)S(1)}, u32[]{:S(2)}, u32[]{:S(2)}) collective-permute-start(bf16[64,1024]{1,0:T(8,128)(2,1)S(1)} %get-tuple-element.308), channel_id=1, source_target_pairs={{0,5},{1,4},{4,1},{5,0},{2,7},{3,6},{6,3},{7,2},{8,13},{9,12},{12,... | collective-permute-start | bytes 393224 | tf_op jit(solution)/shard_map/ppermute | solution.py:96
  (133 other events, 1529.3 us)
Sparse Core Ops, SparseCore 0:
  23.7 66.1 all-gather.4
  91.5 68.8 all-gather.6
  162.1 80.5 all-gather.8
  244.2 80.5 all-gather.10
  326.9 75.2 reduce-scatter.4
  404.5 79.2 reduce-scatter.6
  486.7 80.9 reduce-scatter.8
  570.1 48.3 reduce-scatter.10

commit v31 on v27

--- a/solution.py
+++ b/solution.py
@@ -1033,9 +1033,7 @@
 
         caption_part = spread(caption_part)
         up_grad = finish_wide(up_parts, rank)
-        caption_part, rest_rows, up_grad = lax.optimization_barrier(
-            (caption_part, rest_rows, up_grad)
-        )
+        rest_rows, up_grad = lax.optimization_barrier((rest_rows, up_grad))
         grad_caption = caption_output(caption_part, swap(caption_part, "c"), core)
         rest_rows = swap_parts(pick_rows([rest_rows], rank))
         grad_caption, rest_rows = lax.optimization_barrier((grad_caption, rest_rows))

time: 651 us -> 653 us (level)
  blocking collectives: 102 us -> 114 us
    all_to_all x7 -> x8, blocking collectives: 102 us -> 114 us  [trade(): return lax.all_to_all(blocks, axes, 0, 0, tiled=True)]
    all_to_all x6 -> x5, waiting for transfers between devices: 39.7 us -> 33.3 us  [trade(): return lax.all_to_all(blocks, axes, 0, 0, tiled=True)]
    all_to_all x6 -> x5, starting transfers between devices: 26 us -> 22.4 us  [trade(): return lax.all_to_all(blocks, axes, 0, 0, tiled=True)]
  transfers between devices with their start and end apart: 89 -> 88, of which waited for: 47 -> 47; matrix products, arithmetic and copies ran while one was open for 11% -> 11% of each run, Pallas kernels for 17% -> 17%
where the time goes in v31:
time: 653 us; the launch traced here: 645 us
  waiting for transfers between devices  202 us (31%)
  Pallas kernels  116 us (18%)
  blocking collectives  114 us (17%)
  starting transfers between devices  108 us (17%)
  local copies, waits for them, and re-layouts  49.1 us (8%)
  matrix products  32.5 us (5%)
  between operations  16.5 us (3%)
  other arithmetic  8.09 us (1%)
    ppermute x70, waiting for transfers between devices, swap(): return lax.ppermute(values, axis, PAIR)  145 us
    all_to_all x8, blocking collectives, trade(): return lax.all_to_all(blocks, axes, 0, 0, tiled=True)  114 us
    ppermute x70, starting transfers between devices, swap(): return lax.ppermute(values, axis, PAIR)  75.5 us
    pallas_call x19, Pallas kernels, call(): pl.pallas_call(kernel, grid=grid, in_specs=in_specs, out_specs=out_specs,...  73 us
    pallas_call x12, Pallas kernels, call(): pl.pallas_call(kernel, grid_spec=spec, **options)  42.7 us
    all_to_all x5, waiting for transfers between devices, trade(): return lax.all_to_all(blocks, axes, 0, 0, tiled=True)  33.3 us
    dot_general x6, matrix products, dot(): return lax.dot_general(a, b, (dims, ((), ())), preferred_element_type=F32)  32.5 us
    unnamed x132, local copies, waits for them, and re-layouts  26 us
  transfers between devices with their start and end apart: 88, of which 47 were waited for; matrix products, arithmetic and copies ran while one was open for 11% of the time, Pallas kernels for 17%

profile of v31, /device:TPU:0, one launch (start us, length us, event | category | flops | bytes accessed | tf_op | source)
XLA Modules:
  0.0 644.9 jit_solution(13529138397834112136)
XLA Ops:
  30.1 8.8 %collective-permute-done.1.refs_2_ = bf16[128,2048]{1,0:T(8,128)(2,1)S(1)} collective-permute-done((bf16[128,2048]{1,0:T(8,128)(2,1)S(1)}, bf16[128,2048]{1,0:T(8,128)(2,1)S(1)}, u32[]{:S(2)}, u32[]{:S(2)}) %collective-permute-start.1) | collective-permute-done | bytes 524320 | tf_op jit(solution)/shard_map/ppermute | solution.py:46
  52.4 12.2 %all_to_all.65 = bf16[4,64,1536]{2,1,0:T(8,128)(2,1)} all-to-all(bf16[4,64,1536]{2,1,0:T(8,128)(2,1)S(1)} %copy.75), channel_id=1, replica_groups=mesh['z'=4,'x'=2,'c'=2,'y'=2] {'x','y'}, dimensions={0} | all-to-all | bytes 1572864 | tf_op jit(solution)/shard_map/all_to_all | solution.py:50
  64.7 15.0 %all_to_all.66 = bf16[4,64,2048]{2,1,0:T(8,128)(2,1)} all-to-all(bf16[4,64,2048]{2,1,0:T(8,128)(2,1)} %bitcast.90), channel_id=1, replica_groups=mesh['z'=4,'x'=2,'c'=2,'y'=2] {'x','y'}, dimensions={0} | all-to-all | bytes 2097152 | tf_op jit(solution)/shard_map/all_to_all | solution.py:50
  82.3 16.9 %all_to_all.67 = bf16[8,64,1024]{2,1,0:T(8,128)(2,1)S(1)} all-to-all(bf16[8,64,1024]{2,1,0:T(8,128)(2,1)S(1)} %get-tuple-element.158), channel_id=1, replica_groups=mesh['z'=4,'x'=2,'c'=2,'y'=2] {'x','c','y'}, dimensions={0} | all-to-all | bytes 2097152 | tf_op jit(solution)/shard_map/all_to_all | solution.py:50
  99.4 15.9 %all_to_all.68 = bf16[4,16,1024]{2,1,0:T(8,128)(2,1)S(1)} all-to-all(bf16[4,16,1024]{2,1,0:T(8,128)(2,1)S(1)} %bitcast.101), channel_id=1, replica_groups=mesh['z'=4,'x'=2,'c'=2,'y'=2] {'z'}, dimensions={0} | all-to-all | bytes 262144 | tf_op jit(solution)/shard_map/all_to_all | solution.py:50
  115.4 12.9 %all_to_all.69 = bf16[4,16,1024]{2,1,0:T(8,128)(2,1)S(1)} all-to-all(bf16[4,16,1024]{2,1,0:T(8,128)(2,1)S(1)} %broadcast_in_dim.12), channel_id=1, replica_groups=mesh['z'=4,'x'=2,'c'=2,'y'=2] {'z'}, dimensions={0} | all-to-all | bytes 262144 | tf_op jit(solution)/shard_map/all_to_all | solution.py:50
  132.8 9.0 %qkv_mm.1 = (bf16[512,2048]{1,0:T(8,128)(2,1)}, bf16[512,1536]{1,0:T(8,128)(2,1)S(1)}) custom-call(bf16[128,2048]{1,0:T(8,128)(2,1)S(1)} %copy-done.45, bf16[128,2048]{1,0:T(8,128)(2,1)S(1)} %copy-done.39, bf16[128,2048]{1,0:T(8,128)(2,1)S(1)} %collective-permute-done.1.refs_2_, bf16[64,2048]{1,0:T(8,128)(2,1)} %collective-permute-done.2.refs_3_, ...), custom_call_target="tpu_custom_call" | custom-call | flops 3221225472 | bytes 10485760 | tf_op jit(solution)/shard_map/qkv_mm/pallas_call | solution.py:118
  144.7 18.2 %all_to_all.70 = bf16[4,64,2048]{2,1,0:T(8,128)(2,1)} all-to-all(bf16[4,64,2048]{2,1,0:T(8,128)(2,1)S(1)} %bitcast.89), channel_id=1, replica_groups=mesh['z'=4,'x'=2,'c'=2,'y'=2] {'x','y'}, dimensions={0} | all-to-all | bytes 2097152 | tf_op jit(solution)/shard_map/all_to_all | solution.py:50
  177.4 10.8 %collective-permute-done.11.refs_3_ = bf16[128,2048]{1,0:T(8,128)(2,1)S(1)} collective-permute-done((bf16[128,2048]{1,0:T(8,128)(2,1)S(1)}, bf16[128,2048]{1,0:T(8,128)(2,1)S(1)}, u32[]{:S(2)}, u32[]{:S(2)}) %collective-permute-start.11) | collective-permute-done | bytes 524320 | tf_op jit(solution)/shard_map/ppermute | solution.py:46
  191.9 9.5 %collective-permute-done.13.refs_2_ = bf16[128,2048]{1,0:T(8,128)(2,1)S(1)} collective-permute-done((bf16[128,2048]{1,0:T(8,128)(2,1)S(1)}, bf16[128,2048]{1,0:T(8,128)(2,1)S(1)}, u32[]{:S(2)}, u32[]{:S(2)}) %collective-permute-start.13) | collective-permute-done | bytes 524320 | tf_op jit(solution)/shard_map/ppermute | solution.py:46
  229.2 7.9 %collective-permute-done.19.refs_3_ = bf16[128,2048]{1,0:T(8,128)(2,1)S(1)} collective-permute-done((bf16[128,2048]{1,0:T(8,128)(2,1)S(1)}, bf16[128,2048]{1,0:T(8,128)(2,1)S(1)}, u32[]{:S(2)}, u32[]{:S(2)}) %collective-permute-start.19) | collective-permute-done | bytes 524320 | tf_op jit(solution)/shard_map/ppermute | solution.py:46
  266.4 8.8 %collective-permute-done.25 = bf16[128,2048]{1,0:T(8,128)(2,1)S(1)} collective-permute-done((bf16[128,2048]{1,0:T(8,128)(2,1)S(1)}, bf16[128,2048]{1,0:T(8,128)(2,1)S(1)}, u32[]{:S(2)}, u32[]{:S(2)}) %collective-permute-start.25) | collective-permute-done | bytes 524320 | tf_op jit(solution)/shard_map/ppermute | solution.py:46
  285.8 11.9 %feed_up.1 = (bf16[512,2048]{1,0:T(8,128)(2,1)}, bf16[512,2048]{1,0:T(8,128)(2,1)}, f32[512,2048]{1,0:T(8,128)}) custom-call(bf16[128,2048]{1,0:T(8,128)(2,1)S(1)} %copy-done.47, bf16[128,2048]{1,0:T(8,128)(2,1)S(1)} %copy-done.43, bf16[128,2048]{1,0:T(8,128)(2,1)S(1)} %copy-done.41, bf16[64,2048]{1,0:T(8,128)(2,1)S(1)} %copy-done.49, ...), custom_call_target="tpu_custom_call" | custom-call | flops 4294967296 | bytes 12582912 | tf_op jit(solution)/shard_map/feed_up/pallas_call | solution.py:118
  308.8 8.7 %down_grads.1 = bf16[1024,2048]{1,0:T(8,128)(2,1)} custom-call(s32[1]{0:T(128)} %bitcast.25.r, bf16[512,2048]{1,0:T(8,128)(2,1)} %constant_dynamic-update-slice_fusion.refs_0_.dy, bf16[512,2048]{1,0:T(8,128)(2,1)S(1)} %collective-permute-done.28.refs_1_, bf16[512,2048]{1,0:T(8,128)(2,1)} %get-tuple-element.203.refs_2_, bf16[512,2048]{1,0:T(8,128)(2,1)} %copy-done.63), custom_call_target="tpu_custom_call" | custom-call | flops 4294967296 | bytes 16777216 | tf_op jit(solution)/shard_map/down_grads/pallas_call | solution.py:129
  324.8 10.7 %feed_down.1.refs_2_ = bf16[512,2048]{1,0:T(8,128)(2,1)S(1)} custom-call(bf16[512,2048]{1,0:T(8,128)(2,1)} %constant_dynamic-update-slice_fusion.refs_0_.dy, f32[512,2048]{1,0:T(8,128)} %get-tuple-element.190.slope_ref, bf16[2048,2048]{1,0:T(8,128)(2,1)} %all-gather.11.cloned.1.call-done.down), custom_call_target="tpu_custom_call" | custom-call | flops 4294967296 | bytes 25165824 | tf_op jit(solution)/shard_map/feed_down/pallas_call | solution.py:118
  335.8 8.6 %convolution_convert_fusion.3 = bf16[512,2048]{1,0:T(8,128)(2,1)S(1)} fusion(bf16[512,2048]{1,0:T(8,128)(2,1)S(1)} %feed_down.1.refs_2_, bf16[2048,2048]{1,0:T(8,128)(2,1)} %all-gather.9.cloned.1.call-done.refs_5_), kind=kOutput, calls=%fused_computation.3 | convolution fusion | flops 4296015872 | bytes 12582912 | tf_op jit(solution)/shard_map/dot_general | solution.py:26
  356.7 10.9 %collective-permute-done.38.refs_2_ = bf16[128,2048]{1,0:T(8,128)(2,1)S(1)} collective-permute-done((bf16[128,2048]{1,0:T(8,128)(2,1)S(1)}, bf16[128,2048]{1,0:T(8,128)(2,1)S(1)}, u32[]{:S(2)}, u32[]{:S(2)}) %collective-permute-start.38) | collective-permute-done | bytes 524320 | tf_op jit(solution)/shard_map/ppermute | solution.py:46
  374.7 8.7 %up_grads.1 = bf16[1024,2048]{1,0:T(8,128)(2,1)} custom-call(s32[1]{0:T(128)} %bitcast.25.r, bf16[512,2048]{1,0:T(8,128)(2,1)} %get-tuple-element.194.refs_0_, bf16[512,2048]{1,0:T(8,128)(2,1)} %collective-permute-done.34.refs_1_, bf16[512,2048]{1,0:T(8,128)(2,1)} %copy-done.22, bf16[512,2048]{1,0:T(8,128)(2,1)} %copy-done.62), custom_call_target="tpu_custom_call" | custom-call | flops 4294967296 | bytes 16777216 | tf_op jit(solution)/shard_map/up_grads/pallas_call | solution.py:129
  417.0 10.3 %collective-permute-done.47.refs_2_ = bf16[128,2048]{1,0:T(8,128)(2,1)S(1)} collective-permute-done((bf16[128,2048]{1,0:T(8,128)(2,1)S(1)}, bf16[128,2048]{1,0:T(8,128)(2,1)S(1)}, u32[]{:S(2)}, u32[]{:S(2)}) %collective-permute-start.47) | collective-permute-done | bytes 524320 | tf_op jit(solution)/shard_map/ppermute | solution.py:46
  433.1 8.4 %convolution_convert_fusion.1 = bf16[512,2048]{1,0:T(8,128)(2,1)S(1)} fusion(bf16[512,2048]{1,0:T(8,128)(2,1)S(1)} %copy-done.61, bf16[2048,2048]{1,0:T(8,128)(2,1)} %all-gather.11.cloned.1.call-done.down), kind=kOutput, calls=%fused_computation.1 | convolution fusion | flops 4296015872 | bytes 12582912 | tf_op jit(solution)/shard_map/dot_general | solution.py:26
  476.2 11.8 %attention_grads.1 = bf16[1024,3072]{1,0:T(8,128)(2,1)} custom-call(s32[1]{0:T(128)} %bitcast.25.r, bf16[512,2048]{1,0:T(8,128)(2,1)} %get-tuple-element.223.refs_0_, bf16[512,2048]{1,0:T(8,128)(2,1)} %collective-permute-done.30.refs_1_, bf16[512,2048]{1,0:T(8,128)(2,1)} %get-tuple-element.225.refs_2_, bf16[512,2048]{1,0:T(8,128)(2,1)} %collective-permute-done.56.refs_3_, ...), custom_call_target="tpu_custom_call" | custom-call | flops 6442450944 | bytes 25165824 | tf_op jit(solution)/shard_map/attention_grads/pallas_call | solution.py:129
  548.6 13.8 %all-to-all-done.9 = bf16[8,80,1024]{2,1,0:T(8,128)(2,1)} async-done(((bf16[8,80,1024]{2,1,0:T(8,128)(2,1)}), bf16[8,80,1024]{2,1,0:T(8,128)(2,1)}, u32[]{:S(2)}, u32[]{:S(2)}) %all-to-all-start.9) | async-done | bytes 1310752 | tf_op jit(solution)/shard_map/all_to_all | solution.py:50
  567.8 10.4 %all_to_all.71 = bf16[4,16,1024]{2,1,0:T(8,128)(2,1)S(1)} all-to-all(bf16[4,16,1024]{2,1,0:T(8,128)(2,1)S(1)} %bitcast.102), channel_id=1, replica_groups=mesh['z'=4,'x'=2,'c'=2,'y'=2] {'z'}, dimensions={0} | all-to-all | bytes 262144 | tf_op jit(solution)/shard_map/all_to_all | solution.py:50
  595.9 12.2 %all_to_all.72.own_ref = bf16[4,64,1024]{2,1,0:T(8,128)(2,1)S(1)} all-to-all(bf16[4,64,1024]{2,1,0:T(8,128)(2,1)S(1)} %broadcast_in_dim.17), channel_id=1, replica_groups=mesh['z'=4,'x'=2,'c'=2,'y'=2] {'x','y'}, dimensions={0} | all-to-all | bytes 1048576 | tf_op jit(solution)/shard_map/all_to_all | solution.py:50
  (424 shorter events, 355.9 us)
Async XLA Ops:
  7.2 123.5 %all-gather.5.cloned.1.call-start = ((), (), s32[]{:S(2)}) async-start(), calls=%async_computation.16 | async-start | bytes 7077888 | tf_op jit(solution)/shard_map/all_gather | solution.py:101
  23.6 139.6 %all-gather.7.cloned.1.call-start = ((), (), s32[]{:S(2)}) async-start(), calls=%async_computation.17 | async-start | bytes 7077888 | tf_op jit(solution)/shard_map/all_gather | solution.py:101
  64.6 216.2 %all-gather.9.cloned.1.call-start = ((), (), s32[]{:S(2)}) async-start(), calls=%async_computation.18 | async-start | bytes 9437184 | tf_op jit(solution)/shard_map/all_gather | solution.py:101
  79.7 245.1 %all-gather.11.cloned.1.call-start = ((), (), s32[]{:S(2)}) async-start(), calls=%async_computation.19 | async-start | bytes 9437184 | tf_op jit(solution)/shard_map/all_gather | solution.py:101
  163.0 239.3 %reduce-scatter.4.cloned.1.call-start = ((), (), s32[]{:S(2)}) async-start(), calls=%async_computation.20 | async-start | bytes 5242880 | tf_op jit(solution)/shard_map/reduce_scatter | solution.py:105
  276.0 21.8 %collective-permute-start.26 = (bf16[64,2048]{1,0:T(8,128)(2,1)}, bf16[64,2048]{1,0:T(8,128)(2,1)}, u32[]{:S(2)}, u32[]{:S(2)}) collective-permute-start(bf16[64,2048]{1,0:T(8,128)(2,1)} %slice.347), channel_id=1, source_target_pairs={{0,1},{1,0},{2,3},{3,2},{4,5},{5,4},{6,7},{7,6},{8,9},{9,8},{10,11... | collective-permute-start | bytes 786440 | tf_op jit(solution)/shard_map/ppermute | solution.py:46
  277.8 21.7 %collective-permute-start.27 = (bf16[64,2048]{1,0:T(8,128)(2,1)}, bf16[64,2048]{1,0:T(8,128)(2,1)}, u32[]{:S(2)}, u32[]{:S(2)}) collective-permute-start(bf16[64,2048]{1,0:T(8,128)(2,1)} %slice.348), channel_id=1, source_target_pairs={{0,4},{4,0},{1,5},{5,1},{2,6},{6,2},{3,7},{7,3},{8,12},{12,8},{9,1... | collective-permute-start | bytes 786440 | tf_op jit(solution)/shard_map/ppermute | solution.py:46
  301.6 15.8 %collective-permute-start.30 = (bf16[512,2048]{1,0:T(8,128)(2,1)}, bf16[512,2048]{1,0:T(8,128)(2,1)}, u32[]{:S(2)}, u32[]{:S(2)}) collective-permute-start(bf16[512,2048]{1,0:T(8,128)(2,1)} %get-tuple-element.223.refs_0_), channel_id=1, source_target_pairs={{0,2},{2,0},{1,3},{3,1},{4,6},{6,4},{5,7},{7,5},{8,10},{10,8},{9,1... | collective-permute-start | bytes 6291464 | tf_op jit(solution)/shard_map/ppermute | solution.py:46
  301.7 15.8 %collective-permute-start.32 = (bf16[512,2048]{1,0:T(8,128)(2,1)}, bf16[512,2048]{1,0:T(8,128)(2,1)}, u32[]{:S(2)}, u32[]{:S(2)}) collective-permute-start(bf16[512,2048]{1,0:T(8,128)(2,1)} %get-tuple-element.226.refs_4_), channel_id=1, source_target_pairs={{0,2},{2,0},{1,3},{3,1},{4,6},{6,4},{5,7},{7,5},{8,10},{10,8},{9,1... | collective-permute-start | bytes 6291464 | tf_op jit(solution)/shard_map/ppermute | solution.py:46
  317.5 170.5 %reduce-scatter.6.cloned.1.call-start = ((), (), s32[]{:S(2)}) async-start(), calls=%async_computation.21 | async-start | bytes 5242880 | tf_op jit(solution)/shard_map/reduce_scatter | solution.py:105
  335.5 37.9 %collective-permute-start.41 = (bf16[512,2048]{1,0:T(8,128)(2,1)S(1)}, bf16[512,2048]{1,0:T(8,128)(2,1)S(1)}, u32[]{:S(2)}, u32[]{:S(2)}) collective-permute-start(bf16[512,2048]{1,0:T(8,128)(2,1)S(1)} %feed_down.1.refs_2_), channel_id=1, source_target_pairs={{0,2},{2,0},{1,3},{3,1},{4,6},{6,4},{5,7},{7,5},{8,10},{10,8},{9,1... | collective-permute-start | bytes 6291464 | tf_op jit(solution)/shard_map/ppermute | solution.py:46
  454.9 20.2 %collective-permute-start.57 = (bf16[512,2048]{1,0:T(8,128)(2,1)}, bf16[512,2048]{1,0:T(8,128)(2,1)}, u32[]{:S(2)}, u32[]{:S(2)}) collective-permute-start(bf16[512,2048]{1,0:T(8,128)(2,1)} %get-tuple-element.228.refs_6_), channel_id=1, source_target_pairs={{0,2},{2,0},{1,3},{3,1},{4,6},{6,4},{5,7},{7,5},{8,10},{10,8},{9,1... | collective-permute-start | bytes 6291464 | tf_op jit(solution)/shard_map/ppermute | solution.py:46
  466.7 21.3 %collective-permute-start.54 = (bf16[128,2048]{1,0:T(8,128)(2,1)}, bf16[128,2048]{1,0:T(8,128)(2,1)}, u32[]{:S(2)}, u32[]{:S(2)}) collective-permute-start(bf16[128,2048]{1,0:T(8,128)(2,1)} %get-tuple-element.220), channel_id=1, source_target_pairs={{0,4},{4,0},{1,5},{5,1},{2,6},{6,2},{3,7},{7,3},{8,12},{12,8},{9,1... | collective-permute-start | bytes 1572872 | tf_op jit(solution)/shard_map/ppermute | solution.py:46
  468.2 19.8 %all-to-all-start.6 = ((bf16[8,16,1024]{2,1,0:T(8,128)(2,1)}), bf16[8,16,1024]{2,1,0:T(8,128)(2,1)S(1)}, u32[]{:S(2)}, u32[]{:S(2)}) async-start(bf16[8,16,1024]{2,1,0:T(8,128)(2,1)} %bitcast.30), calls=%async_computation.7 | async-start | bytes 524288 | tf_op jit(solution)/shard_map/all_to_all | solution.py:50
  472.3 137.7 %reduce-scatter.8.cloned.1.call-start = ((), (), s32[]{:S(2)}) async-start(), calls=%async_computation.22 | async-start | bytes 7864320 | tf_op jit(solution)/shard_map/reduce_scatter | solution.py:105
  499.0 16.2 %all-to-all-start.7 = ((bf16[4,16,1024]{2,1,0:T(8,128)(2,1)}), bf16[4,16,1024]{2,1,0:T(8,128)(2,1)S(1)}, u32[]{:S(2)}, u32[]{:S(2)}) async-start(bf16[4,16,1024]{2,1,0:T(8,128)(2,1)} %broadcast_in_dim.13), calls=%async_computation.8 | async-start | bytes 262144 | tf_op jit(solution)/shard_map/all_to_all | solution.py:50
  516.3 18.8 %all-to-all-start.8 = ((bf16[8,64,1024]{2,1,0:T(8,128)(2,1)}), bf16[8,64,1024]{2,1,0:T(8,128)(2,1)}, u32[]{:S(2)}, u32[]{:S(2)}) async-start(bf16[8,64,1024]{2,1,0:T(8,128)(2,1)} %broadcast_in_dim.15), calls=%async_computation.9 | async-start | bytes 2097152 | tf_op jit(solution)/shard_map/all_to_all | solution.py:50
  540.7 21.8 %all-to-all-start.9 = ((bf16[8,80,1024]{2,1,0:T(8,128)(2,1)}), bf16[8,80,1024]{2,1,0:T(8,128)(2,1)}, u32[]{:S(2)}, u32[]{:S(2)}) async-start(bf16[8,80,1024]{2,1,0:T(8,128)(2,1)} %copy-done.24), calls=%async_computation.10 | async-start | bytes 2621440 | tf_op jit(solution)/shard_map/all_to_all | solution.py:50
  578.4 17.4 %collective-permute-start.67 = (bf16[64,2048]{1,0:T(8,128)(2,1)S(1)}, bf16[64,2048]{1,0:T(8,128)(2,1)S(1)}, u32[]{:S(2)}, u32[]{:S(2)}) collective-permute-start(bf16[64,2048]{1,0:T(8,128)(2,1)S(1)} %get-tuple-element.261), channel_id=1, source_target_pairs={{0,1},{1,0},{2,3},{3,2},{4,5},{5,4},{6,7},{7,6},{8,9},{9,8},{10,11... | collective-permute-start | bytes 786440 | tf_op jit(solution)/shard_map/ppermute | solution.py:46
  579.8 16.0 %collective-permute-start.68 = (bf16[64,2048]{1,0:T(8,128)(2,1)S(1)}, bf16[64,2048]{1,0:T(8,128)(2,1)S(1)}, u32[]{:S(2)}, u32[]{:S(2)}) collective-permute-start(bf16[64,2048]{1,0:T(8,128)(2,1)S(1)} %get-tuple-element.262), channel_id=1, source_target_pairs={{0,4},{4,0},{1,5},{5,1},{2,6},{6,2},{3,7},{7,3},{8,12},{12,8},{9,1... | collective-permute-start | bytes 786440 | tf_op jit(solution)/shard_map/ppermute | solution.py:46
  608.1 19.0 %collective-permute-start.70 = (bf16[4,64,1024]{2,1,0:T(8,128)(2,1)S(1)}, bf16[4,64,1024]{2,1,0:T(8,128)(2,1)S(1)}, u32[]{:S(2)}, u32[]{:S(2)}) collective-permute-start(bf16[4,64,1024]{2,1,0:T(8,128)(2,1)S(1)} %all_to_all.72.own_ref), channel_id=1, source_target_pairs={{0,2},{2,0},{1,3},{3,1},{4,6},{6,4},{5,7},{7,5},{8,10},{10,8},{9,1... | collective-permute-start | bytes 1572872 | tf_op jit(solution)/shard_map/ppermute | solution.py:46
  612.6 17.5 %collective-permute-start.71 = (bf16[64,3072]{1,0:T(8,128)(2,1)}, bf16[64,3072]{1,0:T(8,128)(2,1)S(1)}, u32[]{:S(2)}, u32[]{:S(2)}) collective-permute-start(bf16[64,3072]{1,0:T(8,128)(2,1)} %get-tuple-element.276), channel_id=1, source_target_pairs={{0,1},{1,0},{2,3},{3,2},{4,5},{5,4},{6,7},{7,6},{8,9},{9,8},{10,11... | collective-permute-start | bytes 1179656 | tf_op jit(solution)/shard_map/ppermute | solution.py:46
  613.5 16.6 %collective-permute-start.72 = (bf16[64,3072]{1,0:T(8,128)(2,1)}, bf16[64,3072]{1,0:T(8,128)(2,1)S(1)}, u32[]{:S(2)}, u32[]{:S(2)}) collective-permute-start(bf16[64,3072]{1,0:T(8,128)(2,1)} %get-tuple-element.277), channel_id=1, source_target_pairs={{0,4},{4,0},{1,5},{5,1},{2,6},{6,2},{3,7},{7,3},{8,12},{12,8},{9,1... | collective-permute-start | bytes 1179656 | tf_op jit(solution)/shard_map/ppermute | solution.py:46
  614.1 20.0 %collective-permute-start.73 = (bf16[64,3072]{1,0:T(8,128)(2,1)}, bf16[64,3072]{1,0:T(8,128)(2,1)}, u32[]{:S(2)}, u32[]{:S(2)}) collective-permute-start(bf16[64,3072]{1,0:T(8,128)(2,1)} %get-tuple-element.278), channel_id=1, source_target_pairs={{0,5},{1,4},{4,1},{5,0},{2,7},{3,6},{6,3},{7,2},{8,13},{9,12},{12,... | collective-permute-start | bytes 1179656 | tf_op jit(solution)/shard_map/ppermute | solution.py:96
  (128 other events, 1703.3 us)
Sparse Core Ops, SparseCore 0:
  23.7 66.1 all-gather.4
  91.5 68.8 all-gather.6
  162.1 80.5 all-gather.8
  244.2 80.5 all-gather.10
  326.9 75.2 reduce-scatter.3
  404.5 80.0 reduce-scatter.5
  488.2 117.6 reduce-scatter.7

commit v32 on v31

--- a/solution.py
+++ b/solution.py
@@ -1033,10 +1033,11 @@
 
         caption_part = spread(caption_part)
         up_grad = finish_wide(up_parts, rank)
-        rest_rows, up_grad = lax.optimization_barrier((rest_rows, up_grad))
         grad_caption = caption_output(caption_part, swap(caption_part, "c"), core)
         rest_rows = swap_parts(pick_rows([rest_rows], rank))
-        grad_caption, rest_rows = lax.optimization_barrier((grad_caption, rest_rows))
+        grad_caption, up_grad, rest_rows = lax.optimization_barrier(
+            (grad_caption, up_grad, rest_rows)
+        )
         qkv_grad, out_grad, grad_cross, cross_out_grad = finish_all(
             rest_rows, kv_weight_grad, rank
         )

time: 653 us -> 650 us (level)
    unnamed x132 -> x136, local copies, waits for them, and re-layouts: 26 us -> 27.7 us
  transfers between devices with their start and end apart: 88 -> 88, of which waited for: 47 -> 46; matrix products, arithmetic and copies ran while one was open for 11% -> 11% of each run, Pallas kernels for 17% -> 17%
where the time goes in v32:
time: 650 us; the launch traced here: 642 us
  waiting for transfers between devices  197 us (30%)
  Pallas kernels  115 us (18%)
  blocking collectives  113 us (17%)
  starting transfers between devices  109 us (17%)
  local copies, waits for them, and re-layouts  50.8 us (8%)
  matrix products  32.5 us (5%)
  between operations  16.5 us (3%)
  other arithmetic  8.09 us (1%)
    ppermute x70, waiting for transfers between devices, swap(): return lax.ppermute(values, axis, PAIR)  146 us
    all_to_all x8, blocking collectives, trade(): return lax.all_to_all(blocks, axes, 0, 0, tiled=True)  113 us
    ppermute x70, starting transfers between devices, swap(): return lax.ppermute(values, axis, PAIR)  75.3 us
    pallas_call x19, Pallas kernels, call(): pl.pallas_call(kernel, grid=grid, in_specs=in_specs, out_specs=out_specs,...  73 us
    pallas_call x12, Pallas kernels, call(): pl.pallas_call(kernel, grid_spec=spec, **options)  42.4 us
    all_to_all x5, waiting for transfers between devices, trade(): return lax.all_to_all(blocks, axes, 0, 0, tiled=True)  33 us
    dot_general x6, matrix products, dot(): return lax.dot_general(a, b, (dims, ((), ())), preferred_element_type=F32)  32.5 us
    unnamed x136, local copies, waits for them, and re-layouts  27.7 us
  transfers between devices with their start and end apart: 88, of which 46 were waited for; matrix products, arithmetic and copies ran while one was open for 11% of the time, Pallas kernels for 17%

profile of v32, /device:TPU:0, one launch (start us, length us, event | category | flops | bytes accessed | tf_op | source)
XLA Modules:
  0.0 642.5 jit_solution(14586484729756589765)
XLA Ops:
  30.1 8.8 %collective-permute-done.1.refs_2_ = bf16[128,2048]{1,0:T(8,128)(2,1)S(1)} collective-permute-done((bf16[128,2048]{1,0:T(8,128)(2,1)S(1)}, bf16[128,2048]{1,0:T(8,128)(2,1)S(1)}, u32[]{:S(2)}, u32[]{:S(2)}) %collective-permute-start.1) | collective-permute-done | bytes 524320 | tf_op jit(solution)/shard_map/ppermute | solution.py:46
  52.4 12.2 %all_to_all.65 = bf16[4,64,1536]{2,1,0:T(8,128)(2,1)} all-to-all(bf16[4,64,1536]{2,1,0:T(8,128)(2,1)S(1)} %copy.75), channel_id=1, replica_groups=mesh['z'=4,'x'=2,'c'=2,'y'=2] {'x','y'}, dimensions={0} | all-to-all | bytes 1572864 | tf_op jit(solution)/shard_map/all_to_all | solution.py:50
  64.7 15.0 %all_to_all.66 = bf16[4,64,2048]{2,1,0:T(8,128)(2,1)} all-to-all(bf16[4,64,2048]{2,1,0:T(8,128)(2,1)} %bitcast.90), channel_id=1, replica_groups=mesh['z'=4,'x'=2,'c'=2,'y'=2] {'x','y'}, dimensions={0} | all-to-all | bytes 2097152 | tf_op jit(solution)/shard_map/all_to_all | solution.py:50
  82.3 16.9 %all_to_all.67 = bf16[8,64,1024]{2,1,0:T(8,128)(2,1)S(1)} all-to-all(bf16[8,64,1024]{2,1,0:T(8,128)(2,1)S(1)} %get-tuple-element.157), channel_id=1, replica_groups=mesh['z'=4,'x'=2,'c'=2,'y'=2] {'x','c','y'}, dimensions={0} | all-to-all | bytes 2097152 | tf_op jit(solution)/shard_map/all_to_all | solution.py:50
  99.4 15.9 %all_to_all.68 = bf16[4,16,1024]{2,1,0:T(8,128)(2,1)S(1)} all-to-all(bf16[4,16,1024]{2,1,0:T(8,128)(2,1)S(1)} %bitcast.101), channel_id=1, replica_groups=mesh['z'=4,'x'=2,'c'=2,'y'=2] {'z'}, dimensions={0} | all-to-all | bytes 262144 | tf_op jit(solution)/shard_map/all_to_all | solution.py:50
  115.4 12.9 %all_to_all.69 = bf16[4,16,1024]{2,1,0:T(8,128)(2,1)S(1)} all-to-all(bf16[4,16,1024]{2,1,0:T(8,128)(2,1)S(1)} %broadcast_in_dim.12), channel_id=1, replica_groups=mesh['z'=4,'x'=2,'c'=2,'y'=2] {'z'}, dimensions={0} | all-to-all | bytes 262144 | tf_op jit(solution)/shard_map/all_to_all | solution.py:50
  132.8 9.0 %qkv_mm.1 = (bf16[512,2048]{1,0:T(8,128)(2,1)}, bf16[512,1536]{1,0:T(8,128)(2,1)S(1)}) custom-call(bf16[128,2048]{1,0:T(8,128)(2,1)S(1)} %copy-done.47, bf16[128,2048]{1,0:T(8,128)(2,1)S(1)} %copy-done.41, bf16[128,2048]{1,0:T(8,128)(2,1)S(1)} %collective-permute-done.1.refs_2_, bf16[64,2048]{1,0:T(8,128)(2,1)} %collective-permute-done.2.refs_3_, ...), custom_call_target="tpu_custom_call" | custom-call | flops 3221225472 | bytes 10485760 | tf_op jit(solution)/shard_map/qkv_mm/pallas_call | solution.py:118
  144.7 18.2 %all_to_all.70 = bf16[4,64,2048]{2,1,0:T(8,128)(2,1)} all-to-all(bf16[4,64,2048]{2,1,0:T(8,128)(2,1)S(1)} %bitcast.89), channel_id=1, replica_groups=mesh['z'=4,'x'=2,'c'=2,'y'=2] {'x','y'}, dimensions={0} | all-to-all | bytes 2097152 | tf_op jit(solution)/shard_map/all_to_all | solution.py:50
  177.4 10.8 %collective-permute-done.11.refs_3_ = bf16[128,2048]{1,0:T(8,128)(2,1)S(1)} collective-permute-done((bf16[128,2048]{1,0:T(8,128)(2,1)S(1)}, bf16[128,2048]{1,0:T(8,128)(2,1)S(1)}, u32[]{:S(2)}, u32[]{:S(2)}) %collective-permute-start.11) | collective-permute-done | bytes 524320 | tf_op jit(solution)/shard_map/ppermute | solution.py:46
  191.9 9.5 %collective-permute-done.13.refs_2_ = bf16[128,2048]{1,0:T(8,128)(2,1)S(1)} collective-permute-done((bf16[128,2048]{1,0:T(8,128)(2,1)S(1)}, bf16[128,2048]{1,0:T(8,128)(2,1)S(1)}, u32[]{:S(2)}, u32[]{:S(2)}) %collective-permute-start.13) | collective-permute-done | bytes 524320 | tf_op jit(solution)/shard_map/ppermute | solution.py:46
  229.2 7.9 %collective-permute-done.19.refs_3_ = bf16[128,2048]{1,0:T(8,128)(2,1)S(1)} collective-permute-done((bf16[128,2048]{1,0:T(8,128)(2,1)S(1)}, bf16[128,2048]{1,0:T(8,128)(2,1)S(1)}, u32[]{:S(2)}, u32[]{:S(2)}) %collective-permute-start.19) | collective-permute-done | bytes 524320 | tf_op jit(solution)/shard_map/ppermute | solution.py:46
  266.4 8.8 %collective-permute-done.25 = bf16[128,2048]{1,0:T(8,128)(2,1)S(1)} collective-permute-done((bf16[128,2048]{1,0:T(8,128)(2,1)S(1)}, bf16[128,2048]{1,0:T(8,128)(2,1)S(1)}, u32[]{:S(2)}, u32[]{:S(2)}) %collective-permute-start.25) | collective-permute-done | bytes 524320 | tf_op jit(solution)/shard_map/ppermute | solution.py:46
  285.8 11.9 %feed_up.1 = (bf16[512,2048]{1,0:T(8,128)(2,1)}, bf16[512,2048]{1,0:T(8,128)(2,1)}, f32[512,2048]{1,0:T(8,128)}) custom-call(bf16[128,2048]{1,0:T(8,128)(2,1)S(1)} %copy-done.49, bf16[128,2048]{1,0:T(8,128)(2,1)S(1)} %copy-done.45, bf16[128,2048]{1,0:T(8,128)(2,1)S(1)} %copy-done.43, bf16[64,2048]{1,0:T(8,128)(2,1)S(1)} %copy-done.51, ...), custom_call_target="tpu_custom_call" | custom-call | flops 4294967296 | bytes 12582912 | tf_op jit(solution)/shard_map/feed_up/pallas_call | solution.py:118
  308.8 8.6 %down_grads.1 = bf16[1024,2048]{1,0:T(8,128)(2,1)} custom-call(s32[1]{0:T(128)} %bitcast.25.r, bf16[512,2048]{1,0:T(8,128)(2,1)} %constant_dynamic-update-slice_fusion.refs_0_.dy, bf16[512,2048]{1,0:T(8,128)(2,1)S(1)} %collective-permute-done.28.refs_1_, bf16[512,2048]{1,0:T(8,128)(2,1)} %get-tuple-element.202.refs_2_, bf16[512,2048]{1,0:T(8,128)(2,1)} %copy-done.65), custom_call_target="tpu_custom_call" | custom-call | flops 4294967296 | bytes 16777216 | tf_op jit(solution)/shard_map/down_grads/pallas_call | solution.py:129
  324.8 10.7 %feed_down.1.refs_2_ = bf16[512,2048]{1,0:T(8,128)(2,1)S(1)} custom-call(bf16[512,2048]{1,0:T(8,128)(2,1)} %constant_dynamic-update-slice_fusion.refs_0_.dy, f32[512,2048]{1,0:T(8,128)} %get-tuple-element.189.slope_ref, bf16[2048,2048]{1,0:T(8,128)(2,1)} %all-gather.11.cloned.1.call-done.down), custom_call_target="tpu_custom_call" | custom-call | flops 4294967296 | bytes 25165824 | tf_op jit(solution)/shard_map/feed_down/pallas_call | solution.py:118
  335.8 8.6 %convolution_convert_fusion.3 = bf16[512,2048]{1,0:T(8,128)(2,1)S(1)} fusion(bf16[512,2048]{1,0:T(8,128)(2,1)S(1)} %feed_down.1.refs_2_, bf16[2048,2048]{1,0:T(8,128)(2,1)} %all-gather.9.cloned.1.call-done.refs_5_), kind=kOutput, calls=%fused_computation.3 | convolution fusion | flops 4296015872 | bytes 12582912 | tf_op jit(solution)/shard_map/dot_general | solution.py:26
  356.7 10.9 %collective-permute-done.38.refs_2_ = bf16[128,2048]{1,0:T(8,128)(2,1)S(1)} collective-permute-done((bf16[128,2048]{1,0:T(8,128)(2,1)S(1)}, bf16[128,2048]{1,0:T(8,128)(2,1)S(1)}, u32[]{:S(2)}, u32[]{:S(2)}) %collective-permute-start.38) | collective-permute-done | bytes 524320 | tf_op jit(solution)/shard_map/ppermute | solution.py:46
  374.7 8.7 %up_grads.1 = bf16[1024,2048]{1,0:T(8,128)(2,1)} custom-call(s32[1]{0:T(128)} %bitcast.25.r, bf16[512,2048]{1,0:T(8,128)(2,1)} %get-tuple-element.193.refs_0_, bf16[512,2048]{1,0:T(8,128)(2,1)} %collective-permute-done.34.refs_1_, bf16[512,2048]{1,0:T(8,128)(2,1)} %copy-done.22, bf16[512,2048]{1,0:T(8,128)(2,1)} %copy-done.64), custom_call_target="tpu_custom_call" | custom-call | flops 4294967296 | bytes 16777216 | tf_op jit(solution)/shard_map/up_grads/pallas_call | solution.py:129
  417.0 10.3 %collective-permute-done.47.refs_2_ = bf16[128,2048]{1,0:T(8,128)(2,1)S(1)} collective-permute-done((bf16[128,2048]{1,0:T(8,128)(2,1)S(1)}, bf16[128,2048]{1,0:T(8,128)(2,1)S(1)}, u32[]{:S(2)}, u32[]{:S(2)}) %collective-permute-start.47) | collective-permute-done | bytes 524320 | tf_op jit(solution)/shard_map/ppermute | solution.py:46
  433.1 8.5 %convolution_convert_fusion.1 = bf16[512,2048]{1,0:T(8,128)(2,1)S(1)} fusion(bf16[512,2048]{1,0:T(8,128)(2,1)S(1)} %copy-done.63, bf16[2048,2048]{1,0:T(8,128)(2,1)} %all-gather.11.cloned.1.call-done.down), kind=kOutput, calls=%fused_computation.1 | convolution fusion | flops 4296015872 | bytes 12582912 | tf_op jit(solution)/shard_map/dot_general | solution.py:26
  476.2 11.8 %attention_grads.1 = bf16[1024,3072]{1,0:T(8,128)(2,1)} custom-call(s32[1]{0:T(128)} %bitcast.25.r, bf16[512,2048]{1,0:T(8,128)(2,1)} %get-tuple-element.222.refs_0_, bf16[512,2048]{1,0:T(8,128)(2,1)} %collective-permute-done.30.refs_1_, bf16[512,2048]{1,0:T(8,128)(2,1)} %get-tuple-element.224.refs_2_, bf16[512,2048]{1,0:T(8,128)(2,1)} %collective-permute-done.56.refs_3_, ...), custom_call_target="tpu_custom_call" | custom-call | flops 6442450944 | bytes 25165824 | tf_op jit(solution)/shard_map/attention_grads/pallas_call | solution.py:129
  548.7 13.8 %all-to-all-done.9 = bf16[8,80,1024]{2,1,0:T(8,128)(2,1)} async-done(((bf16[8,80,1024]{2,1,0:T(8,128)(2,1)}), bf16[8,80,1024]{2,1,0:T(8,128)(2,1)}, u32[]{:S(2)}, u32[]{:S(2)}) %all-to-all-start.9) | async-done | bytes 1310752 | tf_op jit(solution)/shard_map/all_to_all | solution.py:50
  567.8 10.4 %all_to_all.71 = bf16[4,16,1024]{2,1,0:T(8,128)(2,1)S(1)} all-to-all(bf16[4,16,1024]{2,1,0:T(8,128)(2,1)S(1)} %bitcast.102), channel_id=1, replica_groups=mesh['z'=4,'x'=2,'c'=2,'y'=2] {'z'}, dimensions={0} | all-to-all | bytes 262144 | tf_op jit(solution)/shard_map/all_to_all | solution.py:50
  597.0 11.7 %all_to_all.72.own_ref = bf16[4,64,1024]{2,1,0:T(8,128)(2,1)S(1)} all-to-all(bf16[4,64,1024]{2,1,0:T(8,128)(2,1)S(1)} %broadcast_in_dim.17), channel_id=1, replica_groups=mesh['z'=4,'x'=2,'c'=2,'y'=2] {'x','y'}, dimensions={0} | all-to-all | bytes 1048576 | tf_op jit(solution)/shard_map/all_to_all | solution.py:50
  (428 shorter events, 354.1 us)
Async XLA Ops:
  7.2 123.5 %all-gather.5.cloned.1.call-start = ((), (), s32[]{:S(2)}) async-start(), calls=%async_computation.16 | async-start | bytes 7077888 | tf_op jit(solution)/shard_map/all_gather | solution.py:101
  23.6 139.7 %all-gather.7.cloned.1.call-start = ((), (), s32[]{:S(2)}) async-start(), calls=%async_computation.17 | async-start | bytes 7077888 | tf_op jit(solution)/shard_map/all_gather | solution.py:101
  64.6 216.1 %all-gather.9.cloned.1.call-start = ((), (), s32[]{:S(2)}) async-start(), calls=%async_computation.18 | async-start | bytes 9437184 | tf_op jit(solution)/shard_map/all_gather | solution.py:101
  79.7 245.1 %all-gather.11.cloned.1.call-start = ((), (), s32[]{:S(2)}) async-start(), calls=%async_computation.19 | async-start | bytes 9437184 | tf_op jit(solution)/shard_map/all_gather | solution.py:101
  163.0 239.3 %reduce-scatter.4.cloned.1.call-start = ((), (), s32[]{:S(2)}) async-start(), calls=%async_computation.20 | async-start | bytes 5242880 | tf_op jit(solution)/shard_map/reduce_scatter | solution.py:105
  276.0 21.8 %collective-permute-start.26 = (bf16[64,2048]{1,0:T(8,128)(2,1)}, bf16[64,2048]{1,0:T(8,128)(2,1)}, u32[]{:S(2)}, u32[]{:S(2)}) collective-permute-start(bf16[64,2048]{1,0:T(8,128)(2,1)} %slice.347), channel_id=1, source_target_pairs={{0,1},{1,0},{2,3},{3,2},{4,5},{5,4},{6,7},{7,6},{8,9},{9,8},{10,11... | collective-permute-start | bytes 786440 | tf_op jit(solution)/shard_map/ppermute | solution.py:46
  277.8 21.7 %collective-permute-start.27 = (bf16[64,2048]{1,0:T(8,128)(2,1)}, bf16[64,2048]{1,0:T(8,128)(2,1)}, u32[]{:S(2)}, u32[]{:S(2)}) collective-permute-start(bf16[64,2048]{1,0:T(8,128)(2,1)} %slice.348), channel_id=1, source_target_pairs={{0,4},{4,0},{1,5},{5,1},{2,6},{6,2},{3,7},{7,3},{8,12},{12,8},{9,1... | collective-permute-start | bytes 786440 | tf_op jit(solution)/shard_map/ppermute | solution.py:46
  301.7 15.8 %collective-permute-start.30 = (bf16[512,2048]{1,0:T(8,128)(2,1)}, bf16[512,2048]{1,0:T(8,128)(2,1)}, u32[]{:S(2)}, u32[]{:S(2)}) collective-permute-start(bf16[512,2048]{1,0:T(8,128)(2,1)} %get-tuple-element.222.refs_0_), channel_id=1, source_target_pairs={{0,2},{2,0},{1,3},{3,1},{4,6},{6,4},{5,7},{7,5},{8,10},{10,8},{9,1... | collective-permute-start | bytes 6291464 | tf_op jit(solution)/shard_map/ppermute | solution.py:46
  301.7 15.8 %collective-permute-start.32 = (bf16[512,2048]{1,0:T(8,128)(2,1)}, bf16[512,2048]{1,0:T(8,128)(2,1)}, u32[]{:S(2)}, u32[]{:S(2)}) collective-permute-start(bf16[512,2048]{1,0:T(8,128)(2,1)} %get-tuple-element.225.refs_4_), channel_id=1, source_target_pairs={{0,2},{2,0},{1,3},{3,1},{4,6},{6,4},{5,7},{7,5},{8,10},{10,8},{9,1... | collective-permute-start | bytes 6291464 | tf_op jit(solution)/shard_map/ppermute | solution.py:46
  317.5 170.5 %reduce-scatter.6.cloned.1.call-start = ((), (), s32[]{:S(2)}) async-start(), calls=%async_computation.21 | async-start | bytes 5242880 | tf_op jit(solution)/shard_map/reduce_scatter | solution.py:105
  335.5 37.9 %collective-permute-start.41 = (bf16[512,2048]{1,0:T(8,128)(2,1)S(1)}, bf16[512,2048]{1,0:T(8,128)(2,1)S(1)}, u32[]{:S(2)}, u32[]{:S(2)}) collective-permute-start(bf16[512,2048]{1,0:T(8,128)(2,1)S(1)} %feed_down.1.refs_2_), channel_id=1, source_target_pairs={{0,2},{2,0},{1,3},{3,1},{4,6},{6,4},{5,7},{7,5},{8,10},{10,8},{9,1... | collective-permute-start | bytes 6291464 | tf_op jit(solution)/shard_map/ppermute | solution.py:46
  454.6 20.5 %collective-permute-start.57 = (bf16[512,2048]{1,0:T(8,128)(2,1)}, bf16[512,2048]{1,0:T(8,128)(2,1)}, u32[]{:S(2)}, u32[]{:S(2)}) collective-permute-start(bf16[512,2048]{1,0:T(8,128)(2,1)} %get-tuple-element.227.refs_6_), channel_id=1, source_target_pairs={{0,2},{2,0},{1,3},{3,1},{4,6},{6,4},{5,7},{7,5},{8,10},{10,8},{9,1... | collective-permute-start | bytes 6291464 | tf_op jit(solution)/shard_map/ppermute | solution.py:46
  459.3 15.8 %collective-permute-start.56 = (bf16[512,2048]{1,0:T(8,128)(2,1)}, bf16[512,2048]{1,0:T(8,128)(2,1)}, u32[]{:S(2)}, u32[]{:S(2)}) collective-permute-start(bf16[512,2048]{1,0:T(8,128)(2,1)} %get-tuple-element.224.refs_2_), channel_id=1, source_target_pairs={{0,2},{2,0},{1,3},{3,1},{4,6},{6,4},{5,7},{7,5},{8,10},{10,8},{9,1... | collective-permute-start | bytes 6291464 | tf_op jit(solution)/shard_map/ppermute | solution.py:46
  466.4 21.6 %collective-permute-start.54 = (bf16[128,2048]{1,0:T(8,128)(2,1)}, bf16[128,2048]{1,0:T(8,128)(2,1)}, u32[]{:S(2)}, u32[]{:S(2)}) collective-permute-start(bf16[128,2048]{1,0:T(8,128)(2,1)} %get-tuple-element.219), channel_id=1, source_target_pairs={{0,4},{4,0},{1,5},{5,1},{2,6},{6,2},{3,7},{7,3},{8,12},{12,8},{9,1... | collective-permute-start | bytes 1572872 | tf_op jit(solution)/shard_map/ppermute | solution.py:46
  468.2 19.8 %all-to-all-start.6 = ((bf16[8,16,1024]{2,1,0:T(8,128)(2,1)}), bf16[8,16,1024]{2,1,0:T(8,128)(2,1)S(1)}, u32[]{:S(2)}, u32[]{:S(2)}) async-start(bf16[8,16,1024]{2,1,0:T(8,128)(2,1)} %bitcast.30), calls=%async_computation.7 | async-start | bytes 524288 | tf_op jit(solution)/shard_map/all_to_all | solution.py:50
  472.3 136.3 %reduce-scatter.8.cloned.1.call-start = ((), (), s32[]{:S(2)}) async-start(), calls=%async_computation.22 | async-start | bytes 7864320 | tf_op jit(solution)/shard_map/reduce_scatter | solution.py:105
  499.0 16.2 %all-to-all-start.7 = ((bf16[4,16,1024]{2,1,0:T(8,128)(2,1)}), bf16[4,16,1024]{2,1,0:T(8,128)(2,1)S(1)}, u32[]{:S(2)}, u32[]{:S(2)}) async-start(bf16[4,16,1024]{2,1,0:T(8,128)(2,1)} %broadcast_in_dim.13), calls=%async_computation.8 | async-start | bytes 262144 | tf_op jit(solution)/shard_map/all_to_all | solution.py:50
  516.3 18.8 %all-to-all-start.8 = ((bf16[8,64,1024]{2,1,0:T(8,128)(2,1)}), bf16[8,64,1024]{2,1,0:T(8,128)(2,1)}, u32[]{:S(2)}, u32[]{:S(2)}) async-start(bf16[8,64,1024]{2,1,0:T(8,128)(2,1)} %broadcast_in_dim.15), calls=%async_computation.9 | async-start | bytes 2097152 | tf_op jit(solution)/shard_map/all_to_all | solution.py:50
  540.7 21.8 %all-to-all-start.9 = ((bf16[8,80,1024]{2,1,0:T(8,128)(2,1)}), bf16[8,80,1024]{2,1,0:T(8,128)(2,1)}, u32[]{:S(2)}, u32[]{:S(2)}) async-start(bf16[8,80,1024]{2,1,0:T(8,128)(2,1)} %copy-done.24), calls=%async_computation.10 | async-start | bytes 2621440 | tf_op jit(solution)/shard_map/all_to_all | solution.py:50
  579.2 17.0 %collective-permute-start.67 = (bf16[64,2048]{1,0:T(8,128)(2,1)}, bf16[64,2048]{1,0:T(8,128)(2,1)S(1)}, u32[]{:S(2)}, u32[]{:S(2)}) collective-permute-start(bf16[64,2048]{1,0:T(8,128)(2,1)} %get-tuple-element.260), channel_id=1, source_target_pairs={{0,1},{1,0},{2,3},{3,2},{4,5},{5,4},{6,7},{7,6},{8,9},{9,8},{10,11... | collective-permute-start | bytes 786440 | tf_op jit(solution)/shard_map/ppermute | solution.py:46
  608.6 20.6 %collective-permute-start.70 = (bf16[4,64,1024]{2,1,0:T(8,128)(2,1)S(1)}, bf16[4,64,1024]{2,1,0:T(8,128)(2,1)S(1)}, u32[]{:S(2)}, u32[]{:S(2)}) collective-permute-start(bf16[4,64,1024]{2,1,0:T(8,128)(2,1)S(1)} %all_to_all.72.own_ref), channel_id=1, source_target_pairs={{0,2},{2,0},{1,3},{3,1},{4,6},{6,4},{5,7},{7,5},{8,10},{10,8},{9,1... | collective-permute-start | bytes 1572872 | tf_op jit(solution)/shard_map/ppermute | solution.py:46
  611.3 20.9 %collective-permute-start.71 = (bf16[64,3072]{1,0:T(8,128)(2,1)}, bf16[64,3072]{1,0:T(8,128)(2,1)S(1)}, u32[]{:S(2)}, u32[]{:S(2)}) collective-permute-start(bf16[64,3072]{1,0:T(8,128)(2,1)} %get-tuple-element.274), channel_id=1, source_target_pairs={{0,1},{1,0},{2,3},{3,2},{4,5},{5,4},{6,7},{7,6},{8,9},{9,8},{10,11... | collective-permute-start | bytes 1179656 | tf_op jit(solution)/shard_map/ppermute | solution.py:46
  612.2 20.0 %collective-permute-start.72 = (bf16[64,3072]{1,0:T(8,128)(2,1)}, bf16[64,3072]{1,0:T(8,128)(2,1)S(1)}, u32[]{:S(2)}, u32[]{:S(2)}) collective-permute-start(bf16[64,3072]{1,0:T(8,128)(2,1)} %get-tuple-element.275), channel_id=1, source_target_pairs={{0,4},{4,0},{1,5},{5,1},{2,6},{6,2},{3,7},{7,3},{8,12},{12,8},{9,1... | collective-permute-start | bytes 1179656 | tf_op jit(solution)/shard_map/ppermute | solution.py:46
  612.7 19.9 %collective-permute-start.73 = (bf16[64,3072]{1,0:T(8,128)(2,1)}, bf16[64,3072]{1,0:T(8,128)(2,1)S(1)}, u32[]{:S(2)}, u32[]{:S(2)}) collective-permute-start(bf16[64,3072]{1,0:T(8,128)(2,1)} %get-tuple-element.276), channel_id=1, source_target_pairs={{0,5},{1,4},{4,1},{5,0},{2,7},{3,6},{6,3},{7,2},{8,13},{9,12},{12,... | collective-permute-start | bytes 1179656 | tf_op jit(solution)/shard_map/ppermute | solution.py:96
  (130 other events, 1687.9 us)
Sparse Core Ops, SparseCore 0:
  23.7 66.1 all-gather.4
  91.5 68.8 all-gather.6
  162.1 80.5 all-gather.8
  244.2 80.5 all-gather.10
  326.9 75.2 reduce-scatter.3
  404.5 80.0 reduce-scatter.5
  488.2 117.6 reduce-scatter.7
